TPU v7x, 32 devices: a whole 2x2x4 slice. The times are simulated.
32 devices in a mesh: grp: 2 (over x), tile: 8 (over z, y), lev: 2 (over core).
Axes of the slice: x: 2, y: 2, z: 4, core: 2. Of those that a mesh axis runs over, the one named last changes fastest.
Arguments:
- perturb: bfloat16 [32, 80, 2048], P('lev', 'grp', 'tile'), may hold values from -0.625 to 0.625
- control: float32 [32, 80, 2048], P('lev', 'grp', 'tile'), may hold values from -6 to 6
- level_loc: float32 [32, 32], P('lev'), may hold values from 0 to 1
- static_control: float32 [32, 8192], P('lev', 'tile'), may hold values from -6 to 6
- filter_diag: float32 [8192], P('tile'), may hold values from 0.5 to 2
- filter_off: float32 [8192], P('tile'), may hold values from 0.2 to 0.6
- send_src: int32 [8, 8, 128], P('tile'), may hold values from 0 to 255
- send_wt: float32 [8, 8, 128], P('tile'), may hold values from 0.2 to 1
- counts: int32 [8, 8], P('tile'), may hold values from 1 to 128, as said below
- recv_tgt: int32 [8, 8, 128], P('tile'), may hold values from 0 to 1023
- obs_weight: float32 [32, 8192], P('lev', 'tile'), may hold values from 0.2 to 2
- innovation: float32 [32, 8192], P('lev', 'tile'), may hold values from -6 to 6
Outputs:
- increment: float32 [32, 8192], P('lev', 'tile')
- grad_static: float32 [32, 8192], P('lev', 'tile')
- grad_ens: float32 [32, 80, 2048], P('lev', 'grp', 'tile')
Inputs may be any that keep to these rules, and one draw needn't show every extreme that they name: Slot j from band s to tile d is the same intersection in send_src[s, d, j], send_wt[s, d, j] and recv_tgt[d, s, j]; only slots below counts[s, d] are live. One tile receives 128 live slots from every band.
All inputs are finite; a program needn't handle non-finite values.
Results may differ from a plain program's by a relative error of at most 0.0003.
Values may be sent and summed in bfloat16 or wider, within the bound.
No kernel may reach another device: no remote copies, remote signals or barrier semaphores. Data moves between devices by JAX's collectives and lax.ppermute only.
A program may use at most 64 MiB of HBM per device.

v0:
```python
import jax
import jax.numpy as jnp
from jax import lax
from jax.sharding import PartitionSpec as P


def extended(shard, sides, width):
    for axis, dim in sides:
        size, length = (lax.axis_size(axis), shard.shape[dim])
        up = [(i, (i + 1) % size) for i in range(size - 1)]
        down = [(j, i) for i, j in up]
        last = lax.slice_in_dim(shard, length - width, length, axis=dim)
        first = lax.slice_in_dim(shard, 0, width, axis=dim)
        before = lax.ppermute(last, axis, up)
        after = lax.ppermute(first, axis, down)
        shard = jnp.concatenate([before, shard, after], axis=dim)
    return shard


def body(
    perturb,
    control,
    level_loc,
    static_control,
    filter_diag,
    filter_off,
    send_src,
    send_wt,
    counts,
    recv_tgt,
    obs_weight,
    innovation,
):
    highest = lax.Precision.HIGHEST
    band_cols = control.shape[2]
    tile_cols = static_control.shape[1]
    loc_block = level_loc
    localized = jnp.einsum(
        "kl,lmc->kmc",
        loc_block,
        lax.all_gather(control, "lev", axis=0, tiled=True),
        precision=highest,
    )
    band_sum = jnp.sum(perturb.astype(jnp.float32) * localized, axis=1)
    source = send_src[0]
    target = recv_tgt[0]
    slot_index = lax.broadcasted_iota(jnp.int32, source.shape, 1)
    factor = jnp.where(slot_index < counts[0][:, None], send_wt[0], jnp.zeros_like(send_wt[0]))

    def neighbours(values):
        padded = extended(values, (("tile", 1),), 1)
        return (padded[:, :-2], padded[:, 2:])

    arrived = lax.all_to_all(
        jnp.take(band_sum, source, axis=1) * factor, "tile", split_axis=1, concat_axis=1, tiled=True
    )
    height = arrived.shape[0]
    remapped = lax.psum(
        jnp.zeros((height, tile_cols), jnp.float32)
        .at[:, target.reshape(-1)]
        .add(arrived.reshape(height, -1)),
        "grp",
    )
    left_side, right_side = neighbours(static_control)
    increment = remapped + filter_diag * static_control + filter_off * (left_side + right_side)
    misfit = obs_weight * (increment - innovation)
    left_side, right_side = neighbours(filter_off * misfit)
    grad_static = static_control + filter_diag * misfit + left_side + right_side
    returned = lax.all_to_all(
        jnp.take(misfit, target, axis=1), "tile", split_axis=1, concat_axis=1, tiled=True
    )
    height = returned.shape[0]
    band_grad = (
        jnp.zeros((height, band_cols), jnp.float32)
        .at[:, source.reshape(-1)]
        .add((returned * factor).reshape(height, -1))
    )
    weighted = perturb.astype(jnp.float32) * band_grad[:, None, :]
    loc_block = level_loc
    grad_ens = control + lax.psum_scatter(
        jnp.einsum("kl,kmc->lmc", loc_block, weighted, precision=highest),
        "lev",
        scatter_dimension=0,
        tiled=True,
    )
    return (increment, grad_static, grad_ens)


def solution(mesh):
    return jax.shard_map(
        body,
        mesh=mesh,
        in_specs=(
            P("lev", "grp", "tile"),
            P("lev", "grp", "tile"),
            P("lev", None),
            P("lev", "tile"),
            P("tile"),
            P("tile"),
            P("tile", None, None),
            P("tile", None, None),
            P("tile", None),
            P("tile", None, None),
            P("lev", "tile"),
            P("lev", "tile"),
        ),
        out_specs=(P("lev", "tile"), P("lev", "tile"), P("lev", "grp", "tile")),
        check_vma=False,
    )
```

profile of v0, /device:TPU:0, one launch (start us, length us, event | category | flops | bytes accessed | tf_op | source)
XLA Modules:
  0.0 110.8 jit_solution(4907814162196248426)
XLA Ops:
  7.2 0.0 copy-start
  7.2 0.0 all-gather.2.cloned.1.call-start
  7.3 2.2 %copy.82 = f32[16,40,256]{2,0,1:T(8,128)} copy(f32[16,40,256]{2,1,0:T(8,128)} %param.13) | data formatting | bytes 1310720 | tf_op args[1]
  9.5 0.0 all-gather.2.cloned.1.call-update
  9.5 0.1 fusion.20
  9.6 4.9 %collective-permute-start = (f32[16,1]{1,0:T(8,128)S(1)}, f32[16,1]{1,0:T(8,128)S(1)}, u32[]{:S(2)}, u32[]{:S(2)}) collective-permute-start(f32[16,1]{1,0:T(8,128)S(1)} %get-tuple-element.20), channel_id=1, source_target_pairs={{0,2},{2,4},{4,6},{6,8},{8,10},{10,12},{12,14},{1,3},{3,5},{5,7},{... | collective-permute-start | bytes 200 | tf_op jit(solution)/shard_map/ppermute | solution.py:14
  14.4 1.3 %collective-permute-start.1 = (f32[16,1]{1,0:T(8,128)S(1)}, f32[16,1]{1,0:T(8,128)S(1)}, u32[]{:S(2)}, u32[]{:S(2)}) collective-permute-start(f32[16,1]{1,0:T(8,128)S(1)} %get-tuple-element.21), channel_id=1, source_target_pairs={{2,0},{4,2},{6,4},{8,6},{10,8},{12,10},{14,12},{3,1},{5,3},{7,5},{... | collective-permute-start | bytes 200 | tf_op jit(solution)/shard_map/ppermute | solution.py:15
  15.8 0.1 select_bitcast_fusion.1
  15.9 6.4 %all-gather.2.cloned.1.call-done = f32[32,40,256]{2,0,1:T(8,128)} async-done(((f32[16,40,256]{2,0,1:T(8,128)}), f32[32,40,256]{2,0,1:T(8,128)}) %all-gather.2.cloned.1.call-update) | async-done | bytes 1310736 | tf_op jit(solution)/shard_map/all_gather | solution.py:41
  22.4 2.1 %fusion = f32[16,256]{1,0:T(8,128)S(1)} fusion(f32[32,40,256]{2,0,1:T(8,128)} %all-gather.2.cloned.1.call-done, bf16[16,40,256]{2,1,0:T(8,128)(2,1)S(1)} %copy-done.2, f32[16,32]{1,0:T(8,128)S(1)} %copy-done), kind=kOutput, calls=%fused_computation.6 | convolution fusion | flops 63401984 | bytes 1656832 | tf_op jit(solution)/shard_map/kl,lmc->kmc/dot_general | solution.py:38
  24.4 0.1 copy.83
  24.5 2.8 %gather_fusion = f32[1024,16]{1,0:T(8,128)S(1)} fusion(f32[16,256]{0,1:T(8,128)S(1)} %copy.83, s32[1024]{0:T(1024)S(1)} %fusion.15), kind=kCustom, calls=%fused_computation | custom fusion | bytes 135168 | tf_op jit(solution)/shard_map/jit(_take)/gather | solution.py:55
  27.4 0.0 copy-start.4
  27.4 0.0 copy-start.5
  27.4 0.0 copy-start.8
  27.4 0.0 copy-start.9
  27.4 0.2 copy.84
  27.6 0.7 multiply_bitcast_fusion
  28.2 5.8 %all-to-all-start = ((f32[16,8,128]{2,0,1:T(8,128)}), f32[16,8,128]{2,0,1:T(8,128)S(1)}, u32[]{:S(2)}, u32[]{:S(2)}) async-start(f32[16,8,128]{2,0,1:T(8,128)} %multiply_bitcast_fusion), calls=%async_computation | async-start | bytes 131072 | tf_op jit(solution)/shard_map/all_to_all | solution.py:54
  34.0 0.0 all-reduce.2.cloned.1.call-start
  34.1 6.8 %all-to-all-done = f32[16,8,128]{2,0,1:T(8,128)S(1)} async-done(((f32[16,8,128]{2,0,1:T(8,128)}), f32[16,8,128]{2,0,1:T(8,128)S(1)}, u32[]{:S(2)}, u32[]{:S(2)}) %all-to-all-start) | async-done | bytes 65568 | tf_op jit(solution)/shard_map/all_to_all | solution.py:54
  40.9 0.2 copy.86
  41.1 6.2 %scatter_custom_fusion = f32[16,1024]{0,1:T(8,128)S(1)} fusion(s32[1024]{0:T(1024)S(1)} %bitcast.60, f32[1024,16]{1,0:T(8,128)S(1)} %copy.86, f32[]{:T(128)} %constant.12.clone.1), kind=kCustom, calls=%fused_computation.10 | custom fusion | flops 16384 | bytes 65540 | tf_op jit(solution)/shard_map/scatter-add | solution.py:61
  47.3 0.8 copy.87
  48.1 0.0 all-reduce.2.cloned.1.call-update
  48.1 0.0 collective-permute-done
  48.1 18.4 %all-reduce.2.cloned.1.call-done = f32[16,1024]{1,0:T(8,128)} async-done(((f32[16,1024]{1,0:T(8,128)}), f32[16,1024]{1,0:T(8,128)}) %all-reduce.2.cloned.1.call-update) | async-done | bytes 65552 | tf_op jit(solution)/shard_map/psum | solution.py:58
  66.5 1.6 %broadcast_multiply_fusion = (f32[16,1024]{1,0:T(8,128)S(1)}, f32[16,1024]{1,0:T(8,128)S(1)}, f32[16,1024]{1,0:T(8,128)}) fusion(f32[1024]{0:T(1024)S(1)} %copy-done.9, f32[16,1024]{1,0:T(8,128)S(1)} %copy-done.4, f32[16,1024]{1,0:T(8,128)S(1)} %copy-done.5, f32[16,1]{1,0:T(8,128)S(1)} %collective-permute-done.1, f32[16,1024]{1,0:T(8,128)S(1)} %copy-done.3, ...), kind=kLoop, calls=%fused_computation.29 | loop fusion | flops 163840 | bytes 467072 | tf_op jit(solution)/shard_map/mul | solution.py:67
  68.1 0.2 copy.88
  68.3 2.8 %gather_fusion.1 = f32[1024,16]{1,0:T(8,128)S(1)} fusion(f32[16,1024]{0,1:T(8,128)S(1)} %copy.88, s32[1024]{0:T(1024)S(1)} %fusion.17), kind=kCustom, calls=%fused_computation.1 | custom fusion | bytes 135168 | tf_op jit(solution)/shard_map/jit(_take)/gather | solution.py:70
  71.1 0.2 copy.89
  71.3 0.6 select_bitcast_fusion
  71.9 5.5 %all-to-all-start.1 = ((f32[16,8,128]{2,0,1:T(8,128)}), f32[16,8,128]{2,0,1:T(8,128)S(1)}, u32[]{:S(2)}, u32[]{:S(2)}) async-start(f32[16,8,128]{2,0,1:T(8,128)} %select_bitcast_fusion), calls=%async_computation.1 | async-start | bytes 131072 | tf_op jit(solution)/shard_map/all_to_all | solution.py:69
  77.5 0.0 reduce-scatter.2.cloned.1.call-start
  77.5 6.8 %all-to-all-done.1 = f32[16,8,128]{2,0,1:T(8,128)S(1)} async-done(((f32[16,8,128]{2,0,1:T(8,128)}), f32[16,8,128]{2,0,1:T(8,128)S(1)}, u32[]{:S(2)}, u32[]{:S(2)}) %all-to-all-start.1) | async-done | bytes 65568 | tf_op jit(solution)/shard_map/all_to_all | solution.py:69
  84.4 0.2 copy.91
  84.6 6.1 %scatter_custom_fusion.1 = f32[16,256]{0,1:T(8,128)S(1)} fusion(s32[1024]{0:T(1024)S(1)} %bitcast.59, f32[1024,16]{1,0:T(8,128)S(1)} %copy.91, f32[]{:T(128)} %constant.12.clone.1), kind=kCustom, calls=%fused_computation.26 | custom fusion | flops 16384 | bytes 16388 | tf_op jit(solution)/shard_map/scatter-add | solution.py:76
  90.6 0.1 copy.92
  90.7 2.3 %convolution_bitcast_fusion = f32[32,40,256]{2,0,1:T(8,128)} fusion(f32[16,256]{1,0:T(8,128)S(1)} %copy.92, bf16[16,40,256]{2,1,0:T(8,128)(2,1)S(1)} %copy-done.2, f32[16,32]{1,0:T(8,128)S(1)} %copy-done), kind=kOutput, calls=%fused_computation.4 | convolution fusion | flops 63242240 | bytes 1656832 | tf_op jit(solution)/shard_map/kl,kmc->lmc/dot_general | solution.py:81
  93.0 0.0 reduce-scatter.2.cloned.1.call-update
  93.0 0.1 fusion.19
  93.1 2.3 %collective-permute-start.2 = (f32[16,1]{1,0:T(8,128)S(1)}, f32[16,1]{1,0:T(8,128)S(1)}, u32[]{:S(2)}, u32[]{:S(2)}) collective-permute-start(f32[16,1]{1,0:T(8,128)S(1)} %get-tuple-element.18), channel_id=1, source_target_pairs={{0,2},{2,4},{4,6},{6,8},{8,10},{10,12},{12,14},{1,3},{3,5},{5,7},{... | collective-permute-start | bytes 200 | tf_op jit(solution)/shard_map/ppermute | solution.py:14
  95.4 1.3 %collective-permute-start.3 = (f32[16,1]{1,0:T(8,128)S(1)}, f32[16,1]{1,0:T(8,128)S(1)}, u32[]{:S(2)}, u32[]{:S(2)}) collective-permute-start(f32[16,1]{1,0:T(8,128)S(1)} %get-tuple-element.19), channel_id=1, source_target_pairs={{2,0},{4,2},{6,4},{8,6},{10,8},{12,10},{14,12},{3,1},{5,3},{7,5},{... | collective-permute-start | bytes 200 | tf_op jit(solution)/shard_map/ppermute | solution.py:15
  96.7 0.0 collective-permute-done.2
  96.8 4.2 %collective-permute-done.3 = f32[16,1]{1,0:T(8,128)S(1)} collective-permute-done((f32[16,1]{1,0:T(8,128)S(1)}, f32[16,1]{1,0:T(8,128)S(1)}, u32[]{:S(2)}, u32[]{:S(2)}) %collective-permute-start.3) | collective-permute-done | bytes 96 | tf_op jit(solution)/shard_map/ppermute | solution.py:15
  101.0 0.7 fusion.5
  101.7 1.3 %copy_add_fusion = f32[16,40,256]{2,0,1:T(8,128)S(1)} fusion(f32[16,40,256]{2,0,1:T(8,128)} %reduce-scatter.2.cloned.1.call-done, f32[16,40,256]{2,1,0:T(8,128)S(1)} %copy-done.1), kind=kLoop, calls=%fused_computation.46 | loop fusion | flops 163840 | bytes 1966080 | tf_op jit(solution)/shard_map/add | solution.py:80
  103.0 1.2 %copy.94 = f32[16,40,256]{2,1,0:T(8,128)} copy(f32[16,40,256]{2,0,1:T(8,128)S(1)} %copy_add_fusion) | data formatting | bytes 1310720
  (29 shorter events, 0.1 us)
Async XLA Ops:
  7.2 15.2 %copy-start = (f32[16,32]{1,0:T(8,128)S(1)}, f32[16,32]{1,0:T(8,128)}, u32[]{:S(2)}) copy-start(f32[16,32]{1,0:T(8,128)} %param.14) | copy-start | bytes 6148
  7.2 2.3 %copy-start.3 = (f32[16,1024]{1,0:T(8,128)S(1)}, f32[16,1024]{1,0:T(8,128)}, u32[]{:S(2)}) copy-start(f32[16,1024]{1,0:T(8,128)} %param.15) | copy-start | bytes 196612
  7.2 8.6 %copy-start.7 = (s32[1,8,128]{2,1,0:T(8,128)S(1)}, s32[1,8,128]{2,1,0:T(8,128)}, u32[]{:S(2)}) copy-start(s32[1,8,128]{2,1,0:T(8,128)} %param.18) | copy-start | bytes 12292
  7.2 8.6 %copy-start.6 = (s32[1,8,128]{2,1,0:T(8,128)S(1)}, s32[1,8,128]{2,1,0:T(8,128)}, u32[]{:S(2)}) copy-start(s32[1,8,128]{2,1,0:T(8,128)} %param.21) | copy-start | bytes 12292
  7.2 8.6 %copy-start.11 = (s32[1,8]{1,0:T(1,128)S(1)}, s32[1,8]{1,0:T(1,128)}, u32[]{:S(2)}) copy-start(s32[1,8]{1,0:T(1,128)} %param.20) | copy-start | bytes 100
  7.2 8.6 %copy-start.10 = (f32[1,8,128]{2,1,0:T(8,128)S(1)}, f32[1,8,128]{2,1,0:T(8,128)}, u32[]{:S(2)}) copy-start(f32[1,8,128]{2,1,0:T(8,128)} %param.19) | copy-start | bytes 12292
  7.2 15.1 %copy-start.2 = (bf16[16,40,256]{2,1,0:T(8,128)(2,1)S(1)}, bf16[16,40,256]{2,1,0:T(8,128)(2,1)}, u32[]{:S(2)}) copy-start(bf16[16,40,256]{2,1,0:T(8,128)(2,1)} %param.12) | copy-start | bytes 983044
  7.2 15.1 %all-gather.2.cloned.1.call-start = ((), (), s32[]{:S(2)}) async-start(), calls=%async_computation.3 | async-start | bytes 1966080 | tf_op jit(solution)/shard_map/all_gather | solution.py:41
  9.6 38.5 %collective-permute-start = (f32[16,1]{1,0:T(8,128)S(1)}, f32[16,1]{1,0:T(8,128)S(1)}, u32[]{:S(2)}, u32[]{:S(2)}) collective-permute-start(f32[16,1]{1,0:T(8,128)S(1)} %get-tuple-element.20), channel_id=1, source_target_pairs={{0,2},{2,4},{4,6},{6,8},{8,10},{10,12},{12,14},{1,3},{3,5},{5,7},{... | collective-permute-start | bytes 200 | tf_op jit(solution)/shard_map/ppermute | solution.py:14
  14.4 33.7 %collective-permute-start.1 = (f32[16,1]{1,0:T(8,128)S(1)}, f32[16,1]{1,0:T(8,128)S(1)}, u32[]{:S(2)}, u32[]{:S(2)}) collective-permute-start(f32[16,1]{1,0:T(8,128)S(1)} %get-tuple-element.21), channel_id=1, source_target_pairs={{2,0},{4,2},{6,4},{8,6},{10,8},{12,10},{14,12},{3,1},{5,3},{7,5},{... | collective-permute-start | bytes 200 | tf_op jit(solution)/shard_map/ppermute | solution.py:15
  27.4 39.1 %copy-start.4 = (f32[16,1024]{1,0:T(8,128)S(1)}, f32[16,1024]{1,0:T(8,128)}, u32[]{:S(2)}) copy-start(f32[16,1024]{1,0:T(8,128)} %param.22) | copy-start | bytes 196612
  27.4 39.1 %copy-start.5 = (f32[16,1024]{1,0:T(8,128)S(1)}, f32[16,1024]{1,0:T(8,128)}, u32[]{:S(2)}) copy-start(f32[16,1024]{1,0:T(8,128)} %param.23) | copy-start | bytes 196612
  27.4 39.1 %copy-start.8 = (f32[1024]{0:T(1024)S(1)}, f32[1024]{0:T(1024)}, u32[]{:S(2)}) copy-start(f32[1024]{0:T(1024)} %param.16) | copy-start | bytes 12292
  27.4 39.1 %copy-start.9 = (f32[1024]{0:T(1024)S(1)}, f32[1024]{0:T(1024)}, u32[]{:S(2)}) copy-start(f32[1024]{0:T(1024)} %param.17) | copy-start | bytes 12292
  28.2 12.7 %all-to-all-start = ((f32[16,8,128]{2,0,1:T(8,128)}), f32[16,8,128]{2,0,1:T(8,128)S(1)}, u32[]{:S(2)}, u32[]{:S(2)}) async-start(f32[16,8,128]{2,0,1:T(8,128)} %multiply_bitcast_fusion), calls=%async_computation | async-start | bytes 131072 | tf_op jit(solution)/shard_map/all_to_all | solution.py:54
  34.0 32.5 %all-reduce.2.cloned.1.call-start = ((), (), s32[]{:S(2)}) async-start(), calls=%async_computation.4 | async-start | bytes 131072 | tf_op jit(solution)/shard_map/psum | solution.py:58
  71.9 12.4 %all-to-all-start.1 = ((f32[16,8,128]{2,0,1:T(8,128)}), f32[16,8,128]{2,0,1:T(8,128)S(1)}, u32[]{:S(2)}, u32[]{:S(2)}) async-start(f32[16,8,128]{2,0,1:T(8,128)} %select_bitcast_fusion), calls=%async_computation.1 | async-start | bytes 131072 | tf_op jit(solution)/shard_map/all_to_all | solution.py:69
  77.5 24.2 %reduce-scatter.2.cloned.1.call-start = ((), (), s32[]{:S(2)}) async-start(), calls=%async_computation.5 | async-start | bytes 1966080 | tf_op jit(solution)/shard_map/reduce_scatter | solution.py:80
  90.7 11.0 %copy-start.1 = (f32[16,40,256]{2,1,0:T(8,128)S(1)}, f32[16,40,256]{2,1,0:T(8,128)}, u32[]{:S(2)}) copy-start(f32[16,40,256]{2,1,0:T(8,128)} %param.13) | copy-start | bytes 1966084
  93.1 3.6 %collective-permute-start.2 = (f32[16,1]{1,0:T(8,128)S(1)}, f32[16,1]{1,0:T(8,128)S(1)}, u32[]{:S(2)}, u32[]{:S(2)}) collective-permute-start(f32[16,1]{1,0:T(8,128)S(1)} %get-tuple-element.18), channel_id=1, source_target_pairs={{0,2},{2,4},{4,6},{6,8},{8,10},{10,12},{12,14},{1,3},{3,5},{5,7},{... | collective-permute-start | bytes 200 | tf_op jit(solution)/shard_map/ppermute | solution.py:14
  95.4 5.5 %collective-permute-start.3 = (f32[16,1]{1,0:T(8,128)S(1)}, f32[16,1]{1,0:T(8,128)S(1)}, u32[]{:S(2)}, u32[]{:S(2)}) collective-permute-start(f32[16,1]{1,0:T(8,128)S(1)} %get-tuple-element.19), channel_id=1, source_target_pairs={{2,0},{4,2},{6,4},{8,6},{10,8},{12,10},{14,12},{3,1},{5,3},{7,5},{... | collective-permute-start | bytes 200 | tf_op jit(solution)/shard_map/ppermute | solution.py:15
Sparse Core Ops, SparseCore 0:
  10.2 12.1 all-gather.1
  48.2 18.2 all-reduce.1
  93.2 5.3 reduce-scatter.1
where the time goes:
time: 111 us
  waiting for transfers between devices  42.8 us (39%)
  starting transfers between devices  21.1 us (19%)
  other arithmetic  17.3 us (16%)
  between operations  14 us (13%)
  local copies, waits for them, and re-layouts  11.1 us (10%)
  matrix products  4.4 us (4%)
    psum x1, waiting for transfers between devices, body(): lax.psum(jnp.zeros((height, tile_cols), jnp.float32).at[:, target.reshape...  18.4 us
    ppermute x2, starting transfers between devices, extended(): before = lax.ppermute(last, axis, up)  7.14 us
    all_to_all x1, waiting for transfers between devices, body(): lax.all_to_all(jnp.take(misfit, target, axis=1), 'tile', split_axis=1, co...  6.85 us
    all_to_all x1, waiting for transfers between devices, body(): lax.all_to_all(jnp.take(band_sum, source, axis=1) * factor, 'tile', split...  6.84 us
    all_gather x1, waiting for transfers between devices, body(): lax.all_gather(control, 'lev', axis=0, tiled=True)  6.45 us
    scatter-add x1, other arithmetic, body(): remapped = lax.psum(jnp.zeros((height, tile_cols), jnp.float32).at[:, tar...  6.15 us
    scatter-add x1, other arithmetic, body(): band_grad = jnp.zeros((height, band_cols), jnp.float32).at[:, source.resh...  6.06 us
    all_to_all x1, starting transfers between devices, body(): lax.all_to_all(jnp.take(band_sum, source, axis=1) * factor, 'tile', split...  5.77 us
  transfers between devices with their start and end apart: 9, of which 5 were waited for; matrix products, arithmetic and copies ran while one was open for 13% of the time, Pallas kernels for 0%

commit v1 on v0

v1 whole, which is shorter than its diff:
```python
import functools

import jax
import jax.numpy as jnp
from jax import lax
from jax.experimental import pallas as pl
from jax.experimental.pallas import tpu as pltpu
from jax.sharding import PartitionSpec as P

F32 = jnp.float32
BF16 = jnp.bfloat16
SUB = 8
EXTRA = 8
VMEM = pl.BlockSpec(memory_space=pltpu.VMEM)
SMEM = pl.BlockSpec(memory_space=pltpu.SMEM)
PARAMS = pltpu.CompilerParams(vmem_limit_bytes=40 * 1024 * 1024)


def halves(values):
    high = values.astype(BF16)
    low = (values - high.astype(F32)).astype(BF16)
    return high, low


def product(a, b, dims=((1,), (0,))):
    return lax.dot_general(a, b, (dims, ((), ())), preferred_element_type=F32)


def select(values, chosen, dims=((1,), (0,))):
    rows = values.shape[0]
    both = product(jnp.concatenate(halves(values), axis=0), chosen, dims)
    return both[:rows] + both[rows:]


def spread(matrix, first, second):
    rows, cols = matrix.shape
    row = lax.broadcasted_iota(jnp.int32, (rows * SUB, rows), 0) // SUB
    left = (row == lax.broadcasted_iota(jnp.int32, (rows * SUB, rows), 1) ).astype(F32)
    col = lax.broadcasted_iota(jnp.int32, (cols, cols * SUB), 1) // SUB
    turned = (col + second) % cols
    right = (turned == lax.broadcasted_iota(jnp.int32, (cols, cols * SUB), 0)).astype(BF16)
    out = []
    same = (
        lax.broadcasted_iota(jnp.int32, (rows * SUB, cols * SUB), 0) % SUB
        == lax.broadcasted_iota(jnp.int32, (rows * SUB, cols * SUB), 1) % SUB
    )
    for part in halves(matrix):
        wide = product(part, right)
        tall = product(left.astype(BF16), wide.astype(BF16))
        out.append(jnp.where(same, tall, 0.0).astype(BF16))
    return out


def mix(weights, values):
    high, low = halves(values)
    return product(weights[0], high) + (product(weights[0], low) + product(weights[1], high))


def one_hot(index, size):
    rows = lax.broadcasted_iota(jnp.int32, (size, index.shape[1]), 0)
    return jnp.where(rows == index, 1.0, 0.0).astype(BF16)


def column_as_row(column, lane, offset):
    n = column.shape[0]
    place = lax.broadcasted_iota(jnp.int32, (n, 128), 1) == lax.broadcasted_iota(jnp.int32, (n, 128), 0) + offset
    return jnp.sum(jnp.where(place, column, 0.0), axis=0, keepdims=True)


def row_as_column(row, n, offset):
    place = lax.broadcasted_iota(jnp.int32, (n, 128), 1) == lax.broadcasted_iota(jnp.int32, (n, 128), 0) + offset
    return jnp.sum(jnp.where(place, row, 0.0), axis=1, keepdims=True)


def edge_rows(values):
    n = values.shape[0]
    row = column_as_row(values[:, -1:], None, 0) + column_as_row(values[:, :1], None, n)
    return jnp.broadcast_to(row, (EXTRA, 128))


def factor_of(counts_ref, weight_ref, d):
    slot = lax.broadcasted_iota(jnp.int32, (1, weight_ref.shape[2]), 1)
    return jnp.where(slot < counts_ref[0, d], weight_ref[0, pl.ds(d, 1), :], 0.0)


def loop(n, step, init):
    return lax.fori_loop(0, n, step, init, unroll=n if n <= 8 else 1)


def band_kernel(lev_ref, counts_ref, perturb_ref, own_ref, other_ref, loc_ref, static_ref, src_ref, weight_ref, out_ref, acc_ref):
    levels, members, cols = perturb_ref.shape
    weights = spread(loc_ref[...], 0, lev_ref[0] * levels)
    total = jnp.zeros((levels, SUB, cols), F32)
    perturb = perturb_ref[...].astype(F32)
    for m in range(0, members, SUB):
        tile = jnp.concatenate([own_ref[:, m : m + SUB, :], other_ref[:, m : m + SUB, :]], axis=0)
        localized = mix(weights, tile.reshape(2 * levels * SUB, cols)).reshape(levels, SUB, cols)
        total = total + perturb[:, m : m + SUB, :] * localized
    band_sum = jnp.sum(total, axis=1)
    acc_ref[...] = jnp.concatenate(halves(band_sum), axis=0)
    n = src_ref.shape[1]
    edges = edge_rows(static_ref[...])

    def step(d, carry):
        chosen = one_hot(src_ref[0, pl.ds(d, 1), :], cols)
        both = product(acc_ref[...], chosen)
        payload = (both[:levels] + both[levels:]) * factor_of(counts_ref, weight_ref, d)
        for g in range(out_ref.shape[0]):
            out_ref[g, d, :levels, :] = payload
            out_ref[g, d, levels:, :] = edges
        return carry

    loop(n, step, 0)


def tile_kernel(pos_ref, arrived_ref, tgt_ref, static_ref, diag_ref, off_ref, obs_ref, innov_ref,
                increment_ref, partial_ref, out_ref):
    levels, cols = static_ref.shape
    groups, n = arrived_ref.shape[:2]
    me = pos_ref[0]

    def step(s, total):
        values = sum(arrived_ref[g, s, :levels, :] for g in range(groups))
        chosen = one_hot(tgt_ref[0, pl.ds(s, 1), :], cols)
        return total + select(values, chosen, ((1,), (1,)))

    remapped = loop(n, step, jnp.zeros((levels, cols), F32))
    before = arrived_ref[0, jnp.maximum(me - 1, 0), levels : levels + 1, :]
    after = arrived_ref[0, jnp.minimum(me + 1, n - 1), levels : levels + 1, :]
    before = jnp.where(me > 0, row_as_column(before, levels, 0), 0.0)
    after = jnp.where(me < n - 1, row_as_column(after, levels, levels), 0.0)
    static = static_ref[...]
    lane = lax.broadcasted_iota(jnp.int32, (levels, cols), 1)
    left = jnp.where(lane == 0, before, pltpu.roll(static, 1, 1))
    right = jnp.where(lane == cols - 1, after, pltpu.roll(static, cols - 1, 1))
    increment = remapped + diag_ref[...] * static + off_ref[...] * (left + right)
    increment_ref[...] = increment
    misfit = obs_ref[...] * (increment - innov_ref[...])
    coupled = off_ref[...] * misfit
    left = jnp.where(lane == 0, 0.0, pltpu.roll(coupled, 1, 1))
    right = jnp.where(lane == cols - 1, 0.0, pltpu.roll(coupled, cols - 1, 1))
    partial_ref[...] = static + diag_ref[...] * misfit + left + right
    edges = edge_rows(coupled)
    both = jnp.concatenate(halves(misfit), axis=0)

    def give(s, carry):
        chosen = one_hot(tgt_ref[0, pl.ds(s, 1), :], cols)
        picked = product(both, chosen)
        out_ref[s, :levels, :] = picked[:levels] + picked[levels:]
        out_ref[s, levels:, :] = edges
        return carry

    loop(n, give, 0)


def adjoint_kernel(pos_ref, counts_ref, returned_ref, src_ref, weight_ref, partial_ref, loc_ref, grad_ref, out_ref):
    levels, cols = partial_ref.shape
    n = returned_ref.shape[0]
    band = out_ref.shape[1] - 128
    me = pos_ref[0]

    def step(d, total):
        values = returned_ref[d, :levels, :] * factor_of(counts_ref, weight_ref, d)
        return total + select(values, one_hot(src_ref[0, pl.ds(d, 1), :], band), ((1,), (1,)))

    out_ref[:, :band] = loop(n, step, jnp.zeros((levels, band), F32))
    out_ref[:, band:] = jnp.concatenate([loc_ref[...], jnp.zeros((levels, 128 - loc_ref.shape[1]), F32)], axis=1)
    before = returned_ref[jnp.maximum(me - 1, 0), levels : levels + 1, :]
    after = returned_ref[jnp.minimum(me + 1, n - 1), levels : levels + 1, :]
    before = jnp.where(me > 0, row_as_column(before, levels, 0), 0.0)
    after = jnp.where(me < n - 1, row_as_column(after, levels, levels), 0.0)
    lane = lax.broadcasted_iota(jnp.int32, (levels, cols), 1)
    grad_ref[...] = partial_ref[...] + (jnp.where(lane == 0, before, 0.0) + jnp.where(lane == cols - 1, after, 0.0))


def ens_kernel(lev_ref, perturb_ref, other_ref, control_ref, mine_ref, theirs_ref, out_ref):
    levels, members, cols = perturb_ref.shape
    mine, theirs = mine_ref[...], theirs_ref[...]
    loc = jnp.concatenate([mine[:, cols : cols + 2 * levels], theirs[:, cols : cols + 2 * levels]], axis=0)
    full = loc.shape[0]
    l_row = lax.broadcasted_iota(jnp.int32, (levels * SUB, full), 0) // SUB + lev_ref[0] * levels
    pick_l = (l_row == lax.broadcasted_iota(jnp.int32, (levels * SUB, full), 1)).astype(BF16)
    k_col = lax.broadcasted_iota(jnp.int32, (full, full * SUB), 1) // SUB
    pick_k = (k_col == lax.broadcasted_iota(jnp.int32, (full, full * SUB), 0)).astype(BF16)
    same = (
        lax.broadcasted_iota(jnp.int32, (levels * SUB, full * SUB), 0) % SUB
        == lax.broadcasted_iota(jnp.int32, (levels * SUB, full * SUB), 1) % SUB
    )
    weights = []
    for part in halves(loc):
        tall = product(pick_l, part, ((1,), (1,)))
        wide = product(tall.astype(BF16), pick_k)
        weights.append(jnp.where(same, wide, 0.0).astype(BF16))
    perturb = perturb_ref[...].astype(F32)
    other = other_ref[...].astype(F32)
    grad = jnp.concatenate([mine[:, :cols], theirs[:, :cols]], axis=0)[:, None, :]
    for m in range(0, members, SUB):
        tile = jnp.concatenate([perturb[:, m : m + SUB, :], other[:, m : m + SUB, :]], axis=0) * grad
        mixed = mix(weights, tile.reshape(full * SUB, cols)).reshape(levels, SUB, cols)
        out_ref[:, m : m + SUB, :] = control_ref[:, m : m + SUB, :] + mixed


def call(kernel, out_shape, spaces, scratch=()):
    return pl.pallas_call(
        kernel,
        out_shape=out_shape,
        in_specs=spaces,
        out_specs=jax.tree.map(lambda _: VMEM, out_shape),
        scratch_shapes=scratch,
        compiler_params=PARAMS,
    )


def body(
    perturb,
    control,
    level_loc,
    static_control,
    filter_diag,
    filter_off,
    send_src,
    send_wt,
    counts,
    recv_tgt,
    obs_weight,
    innovation,
):
    levels, members, band_cols = control.shape
    tile_cols = static_control.shape[1]
    n = lax.axis_size("tile")
    groups = lax.axis_size("grp")
    cap = send_src.shape[2]
    shape = jax.ShapeDtypeStruct
    swap = [(0, 1), (1, 0)]
    lev = lax.axis_index("lev").astype(jnp.int32).reshape(1)
    pos = lax.axis_index("tile").astype(jnp.int32).reshape(1)
    other_control = lax.ppermute(control, "lev", swap)
    other_perturb = lax.ppermute(perturb, "lev", swap)
    payload = call(
        band_kernel,
        shape((groups, n, levels + EXTRA, cap), F32),
        [SMEM, SMEM] + [VMEM] * 7,
        [pltpu.VMEM((2 * levels, band_cols), BF16)],
    )(lev, counts, perturb, control, other_control, level_loc, static_control, send_src, send_wt)
    arrived = lax.all_to_all(
        payload.reshape(groups * n, levels + EXTRA, cap), ("grp", "tile"), split_axis=0, concat_axis=0, tiled=True
    ).reshape(groups, n, levels + EXTRA, cap)
    flat = shape((levels, tile_cols), F32)
    increment, partial, giving = call(
        tile_kernel, (flat, flat, shape((n, levels + EXTRA, cap), F32)), [SMEM] + [VMEM] * 7
    )(pos, arrived, recv_tgt, static_control, filter_diag.reshape(1, -1), filter_off.reshape(1, -1), obs_weight, innovation)
    returned = lax.all_to_all(giving, "tile", split_axis=0, concat_axis=0, tiled=True)
    grad_static, mine = call(
        adjoint_kernel, (flat, shape((levels, band_cols + 128), F32)), [SMEM, SMEM] + [VMEM] * 5
    )(pos, counts, returned, send_src, send_wt, partial, level_loc)
    theirs = lax.ppermute(mine, "lev", swap)
    grad_ens = call(ens_kernel, shape(control.shape, F32), [SMEM] + [VMEM] * 5)(
        lev, perturb, other_perturb, control, mine, theirs
    )
    return (increment, grad_static, grad_ens)


def solution(mesh):
    return jax.shard_map(
        body,
        mesh=mesh,
        in_specs=(
            P("lev", "grp", "tile"),
            P("lev", "grp", "tile"),
            P("lev", None),
            P("lev", "tile"),
            P("tile"),
            P("tile"),
            P("tile", None, None),
            P("tile", None, None),
            P("tile", None),
            P("tile", None, None),
            P("lev", "tile"),
            P("lev", "tile"),
        ),
        out_specs=(P("lev", "tile"), P("lev", "tile"), P("lev", "grp", "tile")),
        check_vma=False,
    )
```

time: 111 us -> 43.2 us (0.39)
  waiting for transfers between devices: 42.8 us -> 11.7 us
  other arithmetic: 17.3 us -> 0 us
  between operations: 14 us -> 0.74 us
  starting transfers between devices: 21.1 us -> 8.96 us
  blocking collectives: 0 us -> 10.4 us
  local copies, waits for them, and re-layouts: 11.1 us -> 4.33 us
  Pallas kernels: 0 us -> 6.54 us
  matrix products: 4.4 us -> 0 us
    psum x1 -> x0, waiting for transfers between devices: 18.4 us -> none  [body(): lax.psum(jnp.zeros((height, tile_cols), jnp.float32).at[:, target.reshape...]
    scatter-add x2 -> x0, other arithmetic: 12.2 us -> none  [the longest x1 6.15 us: body(): remapped = lax.psum(jnp.zeros((height, tile_cols), jnp.float32).at[:, tar...]
    all_to_all x0 -> x1, blocking collectives: none -> 10.4 us  [body(): lax.all_to_all(giving, 'tile', split_axis=0, concat_axis=0, tiled=True)]
    ppermute x4 -> x3, starting transfers between devices: 9.73 us -> 0.59 us  [the longest x1 0.52 us: body(): other_control = lax.ppermute(control, 'lev', swap)]
    pallas_call x0 -> x4, Pallas kernels: none -> 6.54 us  [the longest x1 2.24 us: body(): call(band_kernel, shape((groups, n, levels + EXTRA, cap), F32), [SMEM, SM...]
    all_gather x1 -> x0, waiting for transfers between devices: 6.45 us -> none  [body(): lax.all_gather(control, 'lev', axis=0, tiled=True)]
    gather x4 -> x0, local copies, waits for them, and re-layouts: 5.96 us -> none  [the longest x2 2.98 us: body(): jnp.take(misfit, target, axis=1)]
    all_to_all x2 -> x1, waiting for transfers between devices: 13.7 us -> 8.59 us  [body(): lax.all_to_all(payload.reshape(groups * n, levels + EXTRA, cap), ('grp',...]
  transfers between devices with their start and end apart: 9 -> 4, of which waited for: 5 -> 3; matrix products, arithmetic and copies ran while one was open for 13% -> 0% of each run, Pallas kernels for 0% -> 7%
where the time goes in v1:
time: 43.2 us; the launch traced here: 42.7 us
  waiting for transfers between devices  11.7 us (27%)
  blocking collectives  10.4 us (24%)
  starting transfers between devices  8.96 us (21%)
  Pallas kernels  6.54 us (15%)
  local copies, waits for them, and re-layouts  4.33 us (10%)
  between operations  0.74 us (2%)
    all_to_all x1, blocking collectives, body(): lax.all_to_all(giving, 'tile', split_axis=0, concat_axis=0, tiled=True)  10.4 us
    all_to_all x1, waiting for transfers between devices, body(): lax.all_to_all(payload.reshape(groups * n, levels + EXTRA, cap), ('grp',...  8.59 us
    all_to_all x1, starting transfers between devices, body(): lax.all_to_all(payload.reshape(groups * n, levels + EXTRA, cap), ('grp',...  8.36 us
    unnamed x34, local copies, waits for them, and re-layouts  4.33 us
    pallas_call x1, Pallas kernels, body(): call(band_kernel, shape((groups, n, levels + EXTRA, cap), F32), [SMEM, SM...  2.24 us
    ppermute x1, waiting for transfers between devices, body(): other_control = lax.ppermute(control, 'lev', swap)  1.93 us
    pallas_call x1, Pallas kernels, body(): call(ens_kernel, shape(control.shape, F32), [SMEM] + [VMEM] * 5)  1.51 us
    pallas_call x1, Pallas kernels, body(): call(tile_kernel, (flat, flat, shape((n, levels + EXTRA, cap), F32)), [SM...  1.43 us
  transfers between devices with their start and end apart: 4, of which 3 were waited for; matrix products, arithmetic and copies ran while one was open for 0% of the time, Pallas kernels for 7%

profile of v1, /device:TPU:0, one launch (start us, length us, event | category | flops | bytes accessed | tf_op | source)
XLA Modules:
  0.0 42.7 jit_solution(2750918196214618663)
XLA Ops:
  0.6 0.0 copy-start.10
  0.6 0.5 %collective-permute-start = (f32[16,40,256]{2,1,0:T(8,128)}, f32[16,40,256]{2,1,0:T(8,128)S(1)}, u32[]{:S(2)}, u32[]{:S(2)}) collective-permute-start(f32[16,40,256]{2,1,0:T(8,128)} %control_ref.1), channel_id=1, source_target_pairs={{0,1},{1,0},{2,3},{3,2},{4,5},{5,4},{6,7},{7,6},{8,9},{9,8},{10,11... | collective-permute-start | bytes 1966088 | tf_op jit(solution)/shard_map/ppermute | solution.py:237
  1.2 0.0 copy-start.16
  1.2 1.9 %collective-permute-done.other_ref = f32[16,40,256]{2,1,0:T(8,128)S(1)} collective-permute-done((f32[16,40,256]{2,1,0:T(8,128)}, f32[16,40,256]{2,1,0:T(8,128)S(1)}, u32[]{:S(2)}, u32[]{:S(2)}) %collective-permute-start) | collective-permute-done | bytes 655392 | tf_op jit(solution)/shard_map/ppermute | solution.py:237
  3.1 0.0 copy-done.10
  3.1 0.0 copy-done.16
  3.1 0.0 copy-start
  3.1 1.1 %copy-done = f32[16,40,256]{2,1,0:T(8,128)S(1)} copy-done((f32[16,40,256]{2,1,0:T(8,128)S(1)}, f32[16,40,256]{2,1,0:T(8,128)}, u32[]{:S(2)}) %copy-start) | copy-done | bytes 655384
  4.2 0.0 copy-start.2
  4.2 1.0 %copy-done.2 = bf16[16,40,256]{2,1,0:T(8,128)(2,1)S(1)} copy-done((bf16[16,40,256]{2,1,0:T(8,128)(2,1)S(1)}, bf16[16,40,256]{2,1,0:T(8,128)(2,1)}, u32[]{:S(2)}) %copy-start.2) | copy-done | bytes 327704
  5.2 0.0 copy-start.4
  5.2 0.8 %copy-done.4 = f32[16,1024]{1,0:T(8,128)S(1)} copy-done((f32[16,1024]{1,0:T(8,128)S(1)}, f32[16,1024]{1,0:T(8,128)}, u32[]{:S(2)}) %copy-start.4) | copy-done | bytes 65560
  6.0 0.0 copy-start.8
  6.0 0.7 %copy-done.8 = f32[16,32]{1,0:T(8,128)S(1)} copy-done((f32[16,32]{1,0:T(8,128)S(1)}, f32[16,32]{1,0:T(8,128)}, u32[]{:S(2)}) %copy-start.8) | copy-done | bytes 2072
  6.7 0.0 copy-start.11
  6.7 0.7 %copy-done.11 = f32[1,8,128]{2,1,0:T(8,128)S(1)} copy-done((f32[1,8,128]{2,1,0:T(8,128)S(1)}, f32[1,8,128]{2,1,0:T(8,128)}, u32[]{:S(2)}) %copy-start.11) | copy-done | bytes 4120
  7.4 0.0 copy-start.3
  7.4 0.0 copy-start.5
  7.4 0.0 copy-start.6
  7.4 0.0 copy-start.7
  7.4 0.0 copy-start.13
  7.4 0.0 copy-start.14
  7.4 0.0 copy-start.15
  7.4 2.2 %shard_map.139 = f32[2,8,24,128]{3,2,1,0:T(8,128)} custom-call(s32[1]{0:T(128)} %bitcast.1.lev_ref, s32[1,8]{1,0:T(1,128)S(1)} %copy-done.16, bf16[16,40,256]{2,1,0:T(8,128)(2,1)S(1)} %copy-done.2, f32[16,40,256]{2,1,0:T(8,128)S(1)} %copy-done, f32[16,40,256]{2,1,0:T(8,128)S(1)} %collective-permute-done.other_ref, f32[16,32]{1,0:T(8,128)S(1)} %copy-done.8, ...), custom_call_target="tpu_custom_call" | custom-call | tf_op jit(solution)/shard_map/pallas_call | solution.py:239
  9.7 0.0 copy-start.1
  9.7 8.4 %all-to-all-start = ((f32[16,24,128]{2,1,0:T(8,128)}), f32[16,24,128]{2,1,0:T(8,128)S(1)}, u32[]{:S(2)}, u32[]{:S(2)}) async-start(f32[16,24,128]{2,1,0:T(8,128)} %bitcast.2), calls=%async_computation | async-start | bytes 393216 | tf_op jit(solution)/shard_map/all_to_all | solution.py:245
  18.0 0.0 copy-done.3
  18.1 0.1 collective-permute-start.1
  18.1 8.6 %all-to-all-done = f32[16,24,128]{2,1,0:T(8,128)S(1)} async-done(((f32[16,24,128]{2,1,0:T(8,128)}), f32[16,24,128]{2,1,0:T(8,128)S(1)}, u32[]{:S(2)}, u32[]{:S(2)}) %all-to-all-start) | async-done | bytes 196640 | tf_op jit(solution)/shard_map/all_to_all | solution.py:245
  26.7 0.0 copy-done.5
  26.7 0.0 copy-done.6
  26.7 0.0 copy-done.7
  26.7 0.0 copy-done.13
  26.7 0.0 copy-done.14
  26.8 0.0 copy-done.15
  26.8 1.4 %shard_map.140 = (f32[16,1024]{1,0:T(8,128)}, f32[16,1024]{1,0:T(8,128)S(1)}, f32[8,24,128]{2,1,0:T(8,128)S(1)}) custom-call(s32[1]{0:T(128)} %bitcast.pos_ref, f32[2,8,24,128]{3,2,1,0:T(8,128)S(1)} %bitcast.6, s32[1,8,128]{2,1,0:T(8,128)S(1)} %copy-done.13, f32[16,1024]{1,0:T(8,128)S(1)} %copy-done.5, f32[1,1024]{1,0:T(1,128)S(1)} %bitcast.7, ...), custom_call_target="tpu_custom_call" | custom-call | tf_op jit(solution)/shard_map/pallas_call | solution.py:249
  28.2 0.0 copy-start.9
  28.2 0.0 copy-start.12
  28.2 10.4 %all_to_all.10.returned_ref = f32[8,24,128]{2,1,0:T(8,128)S(1)} all-to-all(f32[8,24,128]{2,1,0:T(8,128)S(1)} %get-tuple-element.9), channel_id=1, replica_groups=mesh['grp'=2,'tile'=8,'lev'=2] {'tile'}, dimensions={0} | all-to-all | bytes 196608 | tf_op jit(solution)/shard_map/all_to_all | solution.py:252
  38.6 0.0 copy-done.9
  38.6 0.0 copy-done.12
  38.6 1.4 %shard_map.141 = (f32[16,1024]{1,0:T(8,128)}, f32[16,384]{1,0:T(8,128)S(1)}) custom-call(s32[1]{0:T(128)} %bitcast.pos_ref, s32[1,8]{1,0:T(1,128)S(1)} %copy-done.16, f32[8,24,128]{2,1,0:T(8,128)S(1)} %all_to_all.10.returned_ref, s32[1,8,128]{2,1,0:T(8,128)S(1)} %copy-done.10, f32[1,8,128]{2,1,0:T(8,128)S(1)} %copy-done.12, ...), custom_call_target="tpu_custom_call" | custom-call | tf_op jit(solution)/shard_map/pallas_call | solution.py:253
  40.0 0.0 collective-permute-start.2
  40.0 0.0 collective-permute-done.1.other_ref
  40.0 1.2 %collective-permute-done.2.theirs_ref = f32[16,384]{1,0:T(8,128)S(1)} collective-permute-done((f32[16,384]{1,0:T(8,128)S(1)}, f32[16,384]{1,0:T(8,128)S(1)}, u32[]{:S(2)}, u32[]{:S(2)}) %collective-permute-start.2) | collective-permute-done | bytes 24608 | tf_op jit(solution)/shard_map/ppermute | solution.py:256
  41.2 0.0 copy-done.1
  41.2 1.5 %shard_map.142 = f32[16,40,256]{2,1,0:T(8,128)} custom-call(s32[1]{0:T(128)} %bitcast.1.lev_ref, bf16[16,40,256]{2,1,0:T(8,128)(2,1)S(1)} %copy-done.3, bf16[16,40,256]{2,1,0:T(8,128)(2,1)S(1)} %collective-permute-done.1.other_ref, f32[16,40,256]{2,1,0:T(8,128)S(1)} %copy-done.1, f32[16,384]{1,0:T(8,128)S(1)} %get-tuple-element.12.mine_ref, ...), custom_call_target="tpu_custom_call" | custom-call | tf_op jit(solution)/shard_map/pallas_call | solution.py:257
Async XLA Ops:
  0.6 2.5 %copy-start.10 = (s32[1,8,128]{2,1,0:T(8,128)S(1)}, s32[1,8,128]{2,1,0:T(8,128)}, u32[]{:S(2)}) copy-start(s32[1,8,128]{2,1,0:T(8,128)} %src_ref.3) | copy-start | bytes 12292
  0.6 2.5 %collective-permute-start = (f32[16,40,256]{2,1,0:T(8,128)}, f32[16,40,256]{2,1,0:T(8,128)S(1)}, u32[]{:S(2)}, u32[]{:S(2)}) collective-permute-start(f32[16,40,256]{2,1,0:T(8,128)} %control_ref.1), channel_id=1, source_target_pairs={{0,1},{1,0},{2,3},{3,2},{4,5},{5,4},{6,7},{7,6},{8,9},{9,8},{10,11... | collective-permute-start | bytes 1966088 | tf_op jit(solution)/shard_map/ppermute | solution.py:237
  1.2 1.9 %copy-start.16 = (s32[1,8]{1,0:T(1,128)S(1)}, s32[1,8]{1,0:T(1,128)}, u32[]{:S(2)}) copy-start(s32[1,8]{1,0:T(1,128)} %counts_ref.3) | copy-start | bytes 100
  3.1 1.1 %copy-start = (f32[16,40,256]{2,1,0:T(8,128)S(1)}, f32[16,40,256]{2,1,0:T(8,128)}, u32[]{:S(2)}) copy-start(f32[16,40,256]{2,1,0:T(8,128)} %control_ref.1) | copy-start | bytes 1966084
  4.2 1.0 %copy-start.2 = (bf16[16,40,256]{2,1,0:T(8,128)(2,1)S(1)}, bf16[16,40,256]{2,1,0:T(8,128)(2,1)}, u32[]{:S(2)}) copy-start(bf16[16,40,256]{2,1,0:T(8,128)(2,1)} %perturb_ref.3) | copy-start | bytes 983044
  5.2 0.8 %copy-start.4 = (f32[16,1024]{1,0:T(8,128)S(1)}, f32[16,1024]{1,0:T(8,128)}, u32[]{:S(2)}) copy-start(f32[16,1024]{1,0:T(8,128)} %static_ref.3) | copy-start | bytes 196612
  6.0 0.7 %copy-start.8 = (f32[16,32]{1,0:T(8,128)S(1)}, f32[16,32]{1,0:T(8,128)}, u32[]{:S(2)}) copy-start(f32[16,32]{1,0:T(8,128)} %loc_ref.3) | copy-start | bytes 6148
  6.7 0.7 %copy-start.11 = (f32[1,8,128]{2,1,0:T(8,128)S(1)}, f32[1,8,128]{2,1,0:T(8,128)}, u32[]{:S(2)}) copy-start(f32[1,8,128]{2,1,0:T(8,128)} %weight_ref.3) | copy-start | bytes 12292
  7.4 10.7 %copy-start.3 = (bf16[16,40,256]{2,1,0:T(8,128)(2,1)S(1)}, bf16[16,40,256]{2,1,0:T(8,128)(2,1)}, u32[]{:S(2)}) copy-start(bf16[16,40,256]{2,1,0:T(8,128)(2,1)} %perturb_ref.3) | copy-start | bytes 983044
  7.4 19.3 %copy-start.5 = (f32[16,1024]{1,0:T(8,128)S(1)}, f32[16,1024]{1,0:T(8,128)}, u32[]{:S(2)}) copy-start(f32[16,1024]{1,0:T(8,128)} %static_ref.3) | copy-start | bytes 196612
  7.4 19.3 %copy-start.6 = (f32[16,1024]{1,0:T(8,128)S(1)}, f32[16,1024]{1,0:T(8,128)}, u32[]{:S(2)}) copy-start(f32[16,1024]{1,0:T(8,128)} %obs_ref.1) | copy-start | bytes 196612
  7.4 19.3 %copy-start.7 = (f32[16,1024]{1,0:T(8,128)S(1)}, f32[16,1024]{1,0:T(8,128)}, u32[]{:S(2)}) copy-start(f32[16,1024]{1,0:T(8,128)} %innov_ref.1) | copy-start | bytes 196612
  7.4 19.3 %copy-start.13 = (s32[1,8,128]{2,1,0:T(8,128)S(1)}, s32[1,8,128]{2,1,0:T(8,128)}, u32[]{:S(2)}) copy-start(s32[1,8,128]{2,1,0:T(8,128)} %tgt_ref.1) | copy-start | bytes 12292
  7.4 19.3 %copy-start.14 = (f32[1024]{0:T(1024)S(1)}, f32[1024]{0:T(1024)}, u32[]{:S(2)}) copy-start(f32[1024]{0:T(1024)} %param.16) | copy-start | bytes 12292
  7.4 19.3 %copy-start.15 = (f32[1024]{0:T(1024)S(1)}, f32[1024]{0:T(1024)}, u32[]{:S(2)}) copy-start(f32[1024]{0:T(1024)} %param.17) | copy-start | bytes 12292
  9.7 31.5 %copy-start.1 = (f32[16,40,256]{2,1,0:T(8,128)S(1)}, f32[16,40,256]{2,1,0:T(8,128)}, u32[]{:S(2)}) copy-start(f32[16,40,256]{2,1,0:T(8,128)} %control_ref.1) | copy-start | bytes 1966084
  9.7 17.1 %all-to-all-start = ((f32[16,24,128]{2,1,0:T(8,128)}), f32[16,24,128]{2,1,0:T(8,128)S(1)}, u32[]{:S(2)}, u32[]{:S(2)}) async-start(f32[16,24,128]{2,1,0:T(8,128)} %bitcast.2), calls=%async_computation | async-start | bytes 393216 | tf_op jit(solution)/shard_map/all_to_all | solution.py:245
  18.1 21.9 %collective-permute-start.1 = (bf16[16,40,256]{2,1,0:T(8,128)(2,1)S(1)}, bf16[16,40,256]{2,1,0:T(8,128)(2,1)S(1)}, u32[]{:S(2)}, u32[]{:S(2)}) collective-permute-start(bf16[16,40,256]{2,1,0:T(8,128)(2,1)S(1)} %copy-done.3), channel_id=1, source_target_pairs={{0,1},{1,0},{2,3},{3,2},{4,5},{5,4},{6,7},{7,6},{8,9},{9,8},{10,11... | collective-permute-start | bytes 983048 | tf_op jit(solution)/shard_map/ppermute | solution.py:238
  28.2 10.4 %copy-start.9 = (f32[16,32]{1,0:T(8,128)S(1)}, f32[16,32]{1,0:T(8,128)}, u32[]{:S(2)}) copy-start(f32[16,32]{1,0:T(8,128)} %loc_ref.3) | copy-start | bytes 6148
  28.2 10.4 %copy-start.12 = (f32[1,8,128]{2,1,0:T(8,128)S(1)}, f32[1,8,128]{2,1,0:T(8,128)}, u32[]{:S(2)}) copy-start(f32[1,8,128]{2,1,0:T(8,128)} %weight_ref.3) | copy-start | bytes 12292
  40.0 1.2 %collective-permute-start.2 = (f32[16,384]{1,0:T(8,128)S(1)}, f32[16,384]{1,0:T(8,128)S(1)}, u32[]{:S(2)}, u32[]{:S(2)}) collective-permute-start(f32[16,384]{1,0:T(8,128)S(1)} %get-tuple-element.12.mine_ref), channel_id=1, source_target_pairs={{0,1},{1,0},{2,3},{3,2},{4,5},{5,4},{6,7},{7,6},{8,9},{9,8},{10,11... | collective-permute-start | bytes 73736 | tf_op jit(solution)/shard_map/ppermute | solution.py:256

commit v2 on v1

--- a/solution.py
+++ b/solution.py
@@ -12,8 +12,9 @@
 SUB = 8
 EXTRA = 8
 VMEM = pl.BlockSpec(memory_space=pltpu.VMEM)
+HBM = pl.BlockSpec(memory_space=pltpu.HBM)
 SMEM = pl.BlockSpec(memory_space=pltpu.SMEM)
-PARAMS = pltpu.CompilerParams(vmem_limit_bytes=40 * 1024 * 1024)
+MIB = 1024 * 1024
 
 
 def halves(values):
@@ -32,22 +33,20 @@
     return both[:rows] + both[rows:]
 
 
-def spread(matrix, first, second):
+def spread(matrix, start, count):
     rows, cols = matrix.shape
-    row = lax.broadcasted_iota(jnp.int32, (rows * SUB, rows), 0) // SUB
-    left = (row == lax.broadcasted_iota(jnp.int32, (rows * SUB, rows), 1) ).astype(F32)
-    col = lax.broadcasted_iota(jnp.int32, (cols, cols * SUB), 1) // SUB
-    turned = (col + second) % cols
-    right = (turned == lax.broadcasted_iota(jnp.int32, (cols, cols * SUB), 0)).astype(BF16)
+
+    def iota(shape, axis):
+        return lax.broadcasted_iota(jnp.int32, shape, axis)
+
+    shape = (rows * SUB, count * SUB)
+    tall = (iota((rows * SUB, rows), 0) // SUB == iota((rows * SUB, rows), 1)).astype(BF16)
+    wide = (iota((cols, count * SUB), 1) // SUB + start == iota((cols, count * SUB), 0)).astype(BF16)
+    same = iota(shape, 0) % SUB == iota(shape, 1) % SUB
     out = []
-    same = (
-        lax.broadcasted_iota(jnp.int32, (rows * SUB, cols * SUB), 0) % SUB
-        == lax.broadcasted_iota(jnp.int32, (rows * SUB, cols * SUB), 1) % SUB
-    )
     for part in halves(matrix):
-        wide = product(part, right)
-        tall = product(left.astype(BF16), wide.astype(BF16))
-        out.append(jnp.where(same, tall, 0.0).astype(BF16))
+        filled = product(tall, product(part, wide).astype(BF16))
+        out.append(jnp.where(same, filled, 0.0).astype(BF16))
     return out
 
 
@@ -87,16 +86,34 @@
     return lax.fori_loop(0, n, step, init, unroll=n if n <= 8 else 1)
 
 
-def band_kernel(lev_ref, counts_ref, perturb_ref, own_ref, other_ref, loc_ref, static_ref, src_ref, weight_ref, out_ref, acc_ref):
+def own_kernel(lev_ref, perturb_hbm, control_hbm, loc_hbm, part_ref, perturb_ref, control_ref, loc_ref, sems):
+    staged = [(loc_hbm, loc_ref), (control_hbm, control_ref), (perturb_hbm, perturb_ref)]
+    copies = [pltpu.make_async_copy(source, target, sems.at[i]) for i, (source, target) in enumerate(staged)]
+    for copy in copies:
+        copy.start()
+    levels = perturb_ref.shape[0]
+    copies[0].wait()
+    weights = spread(loc_ref[...], lev_ref[0] * levels, levels)
+    copies[1].wait()
+    copies[2].wait()
+    part_ref[...] = mixed_sum(weights, perturb_ref, control_ref)
+
+
+def mixed_sum(weights, perturb_ref, control_ref):
     levels, members, cols = perturb_ref.shape
-    weights = spread(loc_ref[...], 0, lev_ref[0] * levels)
+    perturb = perturb_ref[...].astype(F32)
     total = jnp.zeros((levels, SUB, cols), F32)
-    perturb = perturb_ref[...].astype(F32)
     for m in range(0, members, SUB):
-        tile = jnp.concatenate([own_ref[:, m : m + SUB, :], other_ref[:, m : m + SUB, :]], axis=0)
-        localized = mix(weights, tile.reshape(2 * levels * SUB, cols)).reshape(levels, SUB, cols)
-        total = total + perturb[:, m : m + SUB, :] * localized
-    band_sum = jnp.sum(total, axis=1)
+        tile = control_ref[:, m : m + SUB, :].reshape(levels * SUB, cols)
+        total = total + perturb[:, m : m + SUB, :] * mix(weights, tile).reshape(levels, SUB, cols)
+    return jnp.sum(total, axis=1)
+
+
+def band_kernel(lev_ref, counts_ref, perturb_ref, other_ref, part_ref, loc_ref, static_ref, src_ref, weight_ref,
+                out_ref, acc_ref):
+    levels, members, cols = perturb_ref.shape
+    weights = spread(loc_ref[...], (1 - lev_ref[0]) * levels, levels)
+    band_sum = part_ref[...] + mixed_sum(weights, perturb_ref, other_ref)
     acc_ref[...] = jnp.concatenate(halves(band_sum), axis=0)
     n = src_ref.shape[1]
     edges = edge_rows(static_ref[...])
@@ -200,14 +217,14 @@
         out_ref[:, m : m + SUB, :] = control_ref[:, m : m + SUB, :] + mixed
 
 
-def call(kernel, out_shape, spaces, scratch=()):
+def call(kernel, out_shape, spaces, scratch=(), limit=40 * MIB):
     return pl.pallas_call(
         kernel,
         out_shape=out_shape,
         in_specs=spaces,
         out_specs=jax.tree.map(lambda _: VMEM, out_shape),
         scratch_shapes=scratch,
-        compiler_params=PARAMS,
+        compiler_params=pltpu.CompilerParams(vmem_limit_bytes=limit),
     )
 
 
@@ -236,12 +253,19 @@
     pos = lax.axis_index("tile").astype(jnp.int32).reshape(1)
     other_control = lax.ppermute(control, "lev", swap)
     other_perturb = lax.ppermute(perturb, "lev", swap)
+    part = call(
+        own_kernel,
+        shape((levels, band_cols), F32),
+        [SMEM] + [HBM] * 3,
+        [pltpu.VMEM(a.shape, a.dtype) for a in (perturb, control, level_loc)] + [pltpu.SemaphoreType.DMA((3,))],
+        limit=58 * MIB,
+    )(lev, perturb, control, level_loc)
     payload = call(
         band_kernel,
         shape((groups, n, levels + EXTRA, cap), F32),
-        [SMEM, SMEM] + [VMEM] * 7,
+        [SMEM] * 2 + [VMEM] * 7,
         [pltpu.VMEM((2 * levels, band_cols), BF16)],
-    )(lev, counts, perturb, control, other_control, level_loc, static_control, send_src, send_wt)
+    )(lev, counts, perturb, other_control, part, level_loc, static_control, send_src, send_wt)
     arrived = lax.all_to_all(
         payload.reshape(groups * n, levels + EXTRA, cap), ("grp", "tile"), split_axis=0, concat_axis=0, tiled=True
     ).reshape(groups, n, levels + EXTRA, cap)

time: 43.2 us -> 39.7 us (0.919)
  local copies, waits for them, and re-layouts: 4.33 us -> 0.76 us
  Pallas kernels: 6.54 us -> 8.75 us
  waiting for transfers between devices: 11.7 us -> 9.95 us
    unnamed x34 -> x26, local copies, waits for them, and re-layouts: 4.33 us -> 0.76 us
    pallas_call x1 -> x2, Pallas kernels: 2.24 us -> 4.46 us  [the longest x1 2.3 us: body(): call(own_kernel, shape((levels, band_cols), F32), [SMEM] + [HBM] * 3, [pl...]
    ppermute x1, waiting for transfers between devices: 1.93 us -> 0.01 us  [body(): other_control = lax.ppermute(control, 'lev', swap)]
  transfers between devices with their start and end apart: 4 -> 4, of which waited for: 3 -> 2; matrix products, arithmetic and copies ran while one was open for 0% -> 0% of each run, Pallas kernels for 7% -> 13%
where the time goes in v2:
time: 39.7 us; the launch traced here: 39.3 us
  blocking collectives  10.3 us (26%)
  waiting for transfers between devices  9.95 us (25%)
  starting transfers between devices  8.81 us (22%)
  Pallas kernels  8.75 us (22%)
  between operations  0.77 us (2%)
  local copies, waits for them, and re-layouts  0.76 us (2%)
    all_to_all x1, blocking collectives, body(): lax.all_to_all(giving, 'tile', split_axis=0, concat_axis=0, tiled=True)  10.3 us
    all_to_all x1, waiting for transfers between devices, body(): lax.all_to_all(payload.reshape(groups * n, levels + EXTRA, cap), ('grp',...  8.76 us
    all_to_all x1, starting transfers between devices, body(): lax.all_to_all(payload.reshape(groups * n, levels + EXTRA, cap), ('grp',...  8.04 us
    pallas_call x1, Pallas kernels, body(): call(own_kernel, shape((levels, band_cols), F32), [SMEM] + [HBM] * 3, [pl...  2.3 us
    pallas_call x1, Pallas kernels, body(): call(band_kernel, shape((groups, n, levels + EXTRA, cap), F32), [SMEM] *...  2.16 us
    pallas_call x1, Pallas kernels, body(): call(ens_kernel, shape(control.shape, F32), [SMEM] + [VMEM] * 5)  1.51 us
    pallas_call x1, Pallas kernels, body(): call(tile_kernel, (flat, flat, shape((n, levels + EXTRA, cap), F32)), [SM...  1.43 us
    pallas_call x1, Pallas kernels, body(): call(adjoint_kernel, (flat, shape((levels, band_cols + 128), F32)), [SMEM...  1.36 us
  transfers between devices with their start and end apart: 4, of which 2 were waited for; matrix products, arithmetic and copies ran while one was open for 0% of the time, Pallas kernels for 13%

profile of v2, /device:TPU:0, one launch (start us, length us, event | category | flops | bytes accessed | tf_op | source)
XLA Modules:
  0.0 39.3 jit_solution(17562802906975438679)
XLA Ops:
  0.6 0.5 %collective-permute-start = (f32[16,40,256]{2,1,0:T(8,128)}, f32[16,40,256]{2,1,0:T(8,128)S(1)}, u32[]{:S(2)}, u32[]{:S(2)}) collective-permute-start(f32[16,40,256]{2,1,0:T(8,128)} %control_ref.1), channel_id=1, source_target_pairs={{0,1},{1,0},{2,3},{3,2},{4,5},{5,4},{6,7},{7,6},{8,9},{9,8},{10,11... | collective-permute-start | bytes 1966088 | tf_op jit(solution)/shard_map/ppermute | solution.py:254
  1.1 0.0 copy-start
  1.2 0.0 copy-start.2
  1.2 0.0 copy-start.3
  1.2 0.0 copy-start.7
  1.2 0.0 copy-start.8
  1.2 0.0 copy-start.12
  1.2 2.3 %shard_map.139.part_ref = f32[16,256]{1,0:T(8,128)} custom-call(s32[1]{0:T(128)} %bitcast.1.lev_ref, bf16[16,40,256]{2,1,0:T(8,128)(2,1)} %perturb_ref.3, f32[16,40,256]{2,1,0:T(8,128)} %control_ref.1, f32[16,32]{1,0:T(8,128)} %loc_ref.3), custom_call_target="tpu_custom_call" | custom-call | tf_op jit(solution)/shard_map/pallas_call | solution.py:256
  3.5 0.0 collective-permute-done.other_ref
  3.5 0.0 copy-done
  3.5 0.0 copy-done.2
  3.5 0.0 copy-done.3
  3.5 0.0 copy-done.7
  3.5 0.0 copy-done.8
  3.6 0.0 copy-done.12
  3.6 0.0 copy-start.4
  3.6 0.7 %copy-done.4 = f32[16,256]{1,0:T(8,128)S(1)} copy-done((f32[16,256]{1,0:T(8,128)S(1)}, f32[16,256]{1,0:T(8,128)}, u32[]{:S(2)}) %copy-start.4) | copy-done | bytes 16408
  4.3 0.0 copy-start.5
  4.3 0.0 copy-start.6
  4.3 0.0 copy-start.9
  4.3 0.0 copy-start.10
  4.3 0.0 copy-start.11
  4.3 2.2 %shard_map.140 = f32[2,8,24,128]{3,2,1,0:T(8,128)} custom-call(s32[1]{0:T(128)} %bitcast.1.lev_ref, s32[1,8]{1,0:T(1,128)S(1)} %copy-done.12, bf16[16,40,256]{2,1,0:T(8,128)(2,1)S(1)} %copy-done, f32[16,40,256]{2,1,0:T(8,128)S(1)} %collective-permute-done.other_ref, f32[16,256]{1,0:T(8,128)S(1)} %copy-done.4, f32[16,32]{1,0:T(8,128)S(1)} %copy-done.3, ...), custom_call_target="tpu_custom_call" | custom-call | tf_op jit(solution)/shard_map/pallas_call | solution.py:263
  6.5 0.0 copy-start.1
  6.5 8.0 %all-to-all-start = ((f32[16,24,128]{2,1,0:T(8,128)}), f32[16,24,128]{2,1,0:T(8,128)S(1)}, u32[]{:S(2)}, u32[]{:S(2)}) async-start(f32[16,24,128]{2,1,0:T(8,128)} %bitcast.2), calls=%async_computation | async-start | bytes 393216 | tf_op jit(solution)/shard_map/all_to_all | solution.py:269
  14.5 0.2 collective-permute-start.1
  14.8 8.8 %all-to-all-done = f32[16,24,128]{2,1,0:T(8,128)S(1)} async-done(((f32[16,24,128]{2,1,0:T(8,128)}), f32[16,24,128]{2,1,0:T(8,128)S(1)}, u32[]{:S(2)}, u32[]{:S(2)}) %all-to-all-start) | async-done | bytes 196640 | tf_op jit(solution)/shard_map/all_to_all | solution.py:269
  23.5 0.0 copy-done.5
  23.5 0.0 copy-done.6
  23.5 0.0 copy-done.9
  23.5 0.0 copy-done.10
  23.5 0.0 copy-done.11
  23.5 1.4 %shard_map.141 = (f32[16,1024]{1,0:T(8,128)}, f32[16,1024]{1,0:T(8,128)S(1)}, f32[8,24,128]{2,1,0:T(8,128)S(1)}) custom-call(s32[1]{0:T(128)} %bitcast.pos_ref, f32[2,8,24,128]{3,2,1,0:T(8,128)S(1)} %bitcast.6, s32[1,8,128]{2,1,0:T(8,128)S(1)} %copy-done.9, f32[16,1024]{1,0:T(8,128)S(1)} %copy-done.2, f32[1,1024]{1,0:T(1,128)S(1)} %bitcast.7, ...), custom_call_target="tpu_custom_call" | custom-call | tf_op jit(solution)/shard_map/pallas_call | solution.py:273
  25.0 10.3 %all_to_all.10.returned_ref = f32[8,24,128]{2,1,0:T(8,128)S(1)} all-to-all(f32[8,24,128]{2,1,0:T(8,128)S(1)} %get-tuple-element.9), channel_id=1, replica_groups=mesh['grp'=2,'tile'=8,'lev'=2] {'tile'}, dimensions={0} | all-to-all | bytes 196608 | tf_op jit(solution)/shard_map/all_to_all | solution.py:276
  35.3 1.4 %shard_map.142 = (f32[16,1024]{1,0:T(8,128)}, f32[16,384]{1,0:T(8,128)S(1)}) custom-call(s32[1]{0:T(128)} %bitcast.pos_ref, s32[1,8]{1,0:T(1,128)S(1)} %copy-done.12, f32[8,24,128]{2,1,0:T(8,128)S(1)} %all_to_all.10.returned_ref, s32[1,8,128]{2,1,0:T(8,128)S(1)} %copy-done.7, f32[1,8,128]{2,1,0:T(8,128)S(1)} %copy-done.8, ...), custom_call_target="tpu_custom_call" | custom-call | tf_op jit(solution)/shard_map/pallas_call | solution.py:277
  36.6 0.0 collective-permute-start.2
  36.6 0.0 collective-permute-done.1.other_ref
  36.6 1.2 %collective-permute-done.2.theirs_ref = f32[16,384]{1,0:T(8,128)S(1)} collective-permute-done((f32[16,384]{1,0:T(8,128)S(1)}, f32[16,384]{1,0:T(8,128)S(1)}, u32[]{:S(2)}, u32[]{:S(2)}) %collective-permute-start.2) | collective-permute-done | bytes 24608 | tf_op jit(solution)/shard_map/ppermute | solution.py:280
  37.8 0.0 copy-done.1
  37.8 1.5 %shard_map.143 = f32[16,40,256]{2,1,0:T(8,128)} custom-call(s32[1]{0:T(128)} %bitcast.1.lev_ref, bf16[16,40,256]{2,1,0:T(8,128)(2,1)S(1)} %copy-done, bf16[16,40,256]{2,1,0:T(8,128)(2,1)S(1)} %collective-permute-done.1.other_ref, f32[16,40,256]{2,1,0:T(8,128)S(1)} %copy-done.1, f32[16,384]{1,0:T(8,128)S(1)} %get-tuple-element.12.mine_ref, ...), custom_call_target="tpu_custom_call" | custom-call | tf_op jit(solution)/shard_map/pallas_call | solution.py:281
Async XLA Ops:
  0.6 2.9 %collective-permute-start = (f32[16,40,256]{2,1,0:T(8,128)}, f32[16,40,256]{2,1,0:T(8,128)S(1)}, u32[]{:S(2)}, u32[]{:S(2)}) collective-permute-start(f32[16,40,256]{2,1,0:T(8,128)} %control_ref.1), channel_id=1, source_target_pairs={{0,1},{1,0},{2,3},{3,2},{4,5},{5,4},{6,7},{7,6},{8,9},{9,8},{10,11... | collective-permute-start | bytes 1966088 | tf_op jit(solution)/shard_map/ppermute | solution.py:254
  1.1 2.4 %copy-start = (bf16[16,40,256]{2,1,0:T(8,128)(2,1)S(1)}, bf16[16,40,256]{2,1,0:T(8,128)(2,1)}, u32[]{:S(2)}) copy-start(bf16[16,40,256]{2,1,0:T(8,128)(2,1)} %perturb_ref.3) | copy-start | bytes 983044
  1.2 2.4 %copy-start.2 = (f32[16,1024]{1,0:T(8,128)S(1)}, f32[16,1024]{1,0:T(8,128)}, u32[]{:S(2)}) copy-start(f32[16,1024]{1,0:T(8,128)} %static_ref.3) | copy-start | bytes 196612
  1.2 2.4 %copy-start.3 = (f32[16,32]{1,0:T(8,128)S(1)}, f32[16,32]{1,0:T(8,128)}, u32[]{:S(2)}) copy-start(f32[16,32]{1,0:T(8,128)} %loc_ref.3) | copy-start | bytes 6148
  1.2 2.4 %copy-start.7 = (s32[1,8,128]{2,1,0:T(8,128)S(1)}, s32[1,8,128]{2,1,0:T(8,128)}, u32[]{:S(2)}) copy-start(s32[1,8,128]{2,1,0:T(8,128)} %src_ref.3) | copy-start | bytes 12292
  1.2 2.4 %copy-start.8 = (f32[1,8,128]{2,1,0:T(8,128)S(1)}, f32[1,8,128]{2,1,0:T(8,128)}, u32[]{:S(2)}) copy-start(f32[1,8,128]{2,1,0:T(8,128)} %weight_ref.3) | copy-start | bytes 12292
  1.2 2.4 %copy-start.12 = (s32[1,8]{1,0:T(1,128)S(1)}, s32[1,8]{1,0:T(1,128)}, u32[]{:S(2)}) copy-start(s32[1,8]{1,0:T(1,128)} %counts_ref.3) | copy-start | bytes 100
  3.6 0.7 %copy-start.4 = (f32[16,256]{1,0:T(8,128)S(1)}, f32[16,256]{1,0:T(8,128)}, u32[]{:S(2)}) copy-start(f32[16,256]{1,0:T(8,128)} %shard_map.139.part_ref) | copy-start | bytes 49156
  4.3 19.2 %copy-start.5 = (f32[16,1024]{1,0:T(8,128)S(1)}, f32[16,1024]{1,0:T(8,128)}, u32[]{:S(2)}) copy-start(f32[16,1024]{1,0:T(8,128)} %obs_ref.1) | copy-start | bytes 196612
  4.3 19.2 %copy-start.6 = (f32[16,1024]{1,0:T(8,128)S(1)}, f32[16,1024]{1,0:T(8,128)}, u32[]{:S(2)}) copy-start(f32[16,1024]{1,0:T(8,128)} %innov_ref.1) | copy-start | bytes 196612
  4.3 19.2 %copy-start.9 = (s32[1,8,128]{2,1,0:T(8,128)S(1)}, s32[1,8,128]{2,1,0:T(8,128)}, u32[]{:S(2)}) copy-start(s32[1,8,128]{2,1,0:T(8,128)} %tgt_ref.1) | copy-start | bytes 12292
  4.3 19.2 %copy-start.10 = (f32[1024]{0:T(1024)S(1)}, f32[1024]{0:T(1024)}, u32[]{:S(2)}) copy-start(f32[1024]{0:T(1024)} %param.16) | copy-start | bytes 12292
  4.3 19.2 %copy-start.11 = (f32[1024]{0:T(1024)S(1)}, f32[1024]{0:T(1024)}, u32[]{:S(2)}) copy-start(f32[1024]{0:T(1024)} %param.17) | copy-start | bytes 12292
  6.5 31.4 %copy-start.1 = (f32[16,40,256]{2,1,0:T(8,128)S(1)}, f32[16,40,256]{2,1,0:T(8,128)}, u32[]{:S(2)}) copy-start(f32[16,40,256]{2,1,0:T(8,128)} %control_ref.1) | copy-start | bytes 1966084
  6.5 17.1 %all-to-all-start = ((f32[16,24,128]{2,1,0:T(8,128)}), f32[16,24,128]{2,1,0:T(8,128)S(1)}, u32[]{:S(2)}, u32[]{:S(2)}) async-start(f32[16,24,128]{2,1,0:T(8,128)} %bitcast.2), calls=%async_computation | async-start | bytes 393216 | tf_op jit(solution)/shard_map/all_to_all | solution.py:269
  14.5 22.1 %collective-permute-start.1 = (bf16[16,40,256]{2,1,0:T(8,128)(2,1)S(1)}, bf16[16,40,256]{2,1,0:T(8,128)(2,1)S(1)}, u32[]{:S(2)}, u32[]{:S(2)}) collective-permute-start(bf16[16,40,256]{2,1,0:T(8,128)(2,1)S(1)} %copy-done), channel_id=1, source_target_pairs={{0,1},{1,0},{2,3},{3,2},{4,5},{5,4},{6,7},{7,6},{8,9},{9,8},{10,11... | collective-permute-start | bytes 983048 | tf_op jit(solution)/shard_map/ppermute | solution.py:255
  36.6 1.2 %collective-permute-start.2 = (f32[16,384]{1,0:T(8,128)S(1)}, f32[16,384]{1,0:T(8,128)S(1)}, u32[]{:S(2)}, u32[]{:S(2)}) collective-permute-start(f32[16,384]{1,0:T(8,128)S(1)} %get-tuple-element.12.mine_ref), channel_id=1, source_target_pairs={{0,1},{1,0},{2,3},{3,2},{4,5},{5,4},{6,7},{7,6},{8,9},{9,8},{10,11... | collective-permute-start | bytes 73736 | tf_op jit(solution)/shard_map/ppermute | solution.py:280

commit v3 on v2

--- a/solution.py
+++ b/solution.py
@@ -215,6 +215,152 @@
         tile = jnp.concatenate([perturb[:, m : m + SUB, :], other[:, m : m + SUB, :]], axis=0) * grad
         mixed = mix(weights, tile.reshape(full * SUB, cols)).reshape(levels, SUB, cols)
         out_ref[:, m : m + SUB, :] = control_ref[:, m : m + SUB, :] + mixed
+
+
+class Rows:
+    def __init__(self, levels, band, n, cap):
+        self.sums = [slice(i * levels, (i + 1) * levels) for i in range(band // cap)]
+        at = band // cap * levels
+        self.first = at
+        self.weight = slice(at, at + levels)
+        self.base = slice(at + levels, at + 2 * levels)
+        at += 2 * levels
+        self.src, self.factor, self.tgt, self.edge = at, at + n, at + 2 * n, at + 3 * n
+        self.total = at + 3 * n + EXTRA
+
+
+def static_kernel(counts_ref, static_ref, diag_ref, off_ref, obs_ref, innov_ref, src_ref, weight_ref, tgt_ref, out_ref):
+    levels, cols = static_ref.shape
+    n, _, cap = out_ref.shape
+    rows = Rows(levels, 0, n, cap)
+    static, off, obs = static_ref[...], off_ref[...], obs_ref[...]
+    lane = lax.broadcasted_iota(jnp.int32, (levels, cols), 1)
+    left = jnp.where(lane == 0, 0.0, pltpu.roll(static, 1, 1))
+    right = jnp.where(lane == cols - 1, 0.0, pltpu.roll(static, cols - 1, 1))
+    base = diag_ref[...] * static + off * (left + right) - innov_ref[...]
+    coupled = off * obs
+    ends = [v[:, i] for v in (static, coupled, base) for i in (slice(cols - 1, cols), slice(0, 1))]
+    edge = sum(column_as_row(end, None, i * levels) for i, end in enumerate(ends))
+    place = lax.broadcasted_iota(jnp.int32, (1, cap), 1)
+    edge = edge + jnp.where(place == 6 * levels, off[:, cols - 1 :], 0.0)
+    edge = edge + jnp.where(place == 6 * levels + 1, off[:, :1], 0.0)
+    edge = jnp.broadcast_to(edge, (EXTRA, cap))
+    both = jnp.concatenate(halves(jnp.concatenate([obs, base], axis=0)), axis=0)
+    src = src_ref[0].astype(F32)
+    tgt = tgt_ref[0].astype(F32)
+    factor = jnp.concatenate([factor_of(counts_ref, weight_ref, d) for d in range(n)], axis=0)
+    for q in range(n):
+        picked = product(both, one_hot(tgt_ref[0, q : q + 1, :], cols))
+        out_ref[q, : 2 * levels, :] = picked[: 2 * levels] + picked[2 * levels :]
+        out_ref[q, rows.src : rows.src + n, :] = src
+        out_ref[q, rows.factor : rows.factor + n, :] = factor
+        out_ref[q, rows.tgt : rows.tgt + n, :] = tgt
+        out_ref[q, rows.edge :, :] = edge
+
+
+def sum_kernel(lev_ref, perturb_ref, other_ref, part_ref, loc_ref, out_ref):
+    levels = perturb_ref.shape[0]
+    weights = spread(loc_ref[...], (1 - lev_ref[0]) * levels, levels)
+    out_ref[...] = part_ref[...] + mixed_sum(weights, perturb_ref, other_ref)
+
+
+def payload_kernel(*refs):
+    *sums, rest_ref, out_ref = refs
+    total = sum(ref[...] for ref in sums)
+    levels, band = total.shape
+    n, _, cap = out_ref.shape
+    rows = Rows(levels, band, n, cap)
+    for q in range(n):
+        for i, place in enumerate(rows.sums):
+            out_ref[q, place, :] = total[:, i * cap : (i + 1) * cap]
+        out_ref[q, rows.first :, :] = rest_ref[q]
+
+
+def shared_kernel(cols, pos_ref, arrived_ref, loc_ref, out_ref, slots_ref):
+    levels = loc_ref.shape[0]
+    n, _, cap = arrived_ref.shape
+    band = out_ref.shape[1] - 128
+    rows = Rows(levels, band, n, cap)
+    me = pos_ref[0]
+    column = lax.broadcasted_iota(jnp.int32, (band, cap), 0).astype(F32)
+
+    def chosen(s, d):
+        return jnp.where(column == arrived_ref[s, rows.src + d : rows.src + d + 1, :], 1.0, 0.0).astype(BF16)
+
+    for s in range(n):
+        sums = jnp.concatenate([arrived_ref[s, place, :] for place in rows.sums], axis=1)
+        both = jnp.concatenate(halves(sums), axis=0)
+        for d in range(n):
+            picked = product(both, chosen(s, d))
+            values = (picked[:levels] + picked[levels:]) * arrived_ref[s, rows.factor + d : rows.factor + d + 1, :]
+            slots_ref[d, :, s * cap : (s + 1) * cap] = jnp.concatenate(halves(values), axis=0)
+    own = jnp.concatenate([arrived_ref[d, pl.ds(rows.tgt + me, 1), :] for d in range(n)], axis=0)
+    turned = own.T
+    last = cols - 1.0
+    total = jnp.zeros((levels, band), F32)
+    for d in range(n):
+        same = [
+            jnp.where(turned[:, d : d + 1] == arrived_ref[d, rows.tgt + s : rows.tgt + s + 1, :], 1.0, 0.0).astype(BF16)
+            for s in range(n)
+        ]
+        met = product(slots_ref[d], jnp.concatenate(same, axis=1), ((1,), (1,)))
+        value = met[:levels] + met[levels:] + arrived_ref[d, rows.base, :]
+        edge = arrived_ref[d, rows.edge : rows.edge + 1, :]
+        if d > 0:
+            before = row_as_column(arrived_ref[d - 1, rows.edge : rows.edge + 1, :], levels, 0)
+            near = jnp.where(own[d : d + 1] == 0.0, edge[:, 6 * levels + 1 : 6 * levels + 2], 0.0)
+            value = value + before * near
+        if d < n - 1:
+            after = row_as_column(arrived_ref[d + 1, rows.edge : rows.edge + 1, :], levels, levels)
+            near = jnp.where(own[d : d + 1] == last, edge[:, 6 * levels : 6 * levels + 1], 0.0)
+            value = value + after * near
+        misfit = arrived_ref[d, rows.weight, :] * value
+        given = misfit * arrived_ref[me, rows.factor + d : rows.factor + d + 1, :]
+        total = total + select(given, chosen(me, d), ((1,), (1,)))
+    out_ref[:, :band] = total
+    out_ref[:, band:] = jnp.concatenate([loc_ref[...], jnp.zeros((levels, 128 - loc_ref.shape[1]), F32)], axis=1)
+
+
+def outputs_kernel(pos_ref, arrived_ref, slots_ref, tgt_ref, static_ref, diag_ref, off_ref, obs_ref, innov_ref,
+                   increment_ref, grad_ref):
+    levels, cols = static_ref.shape
+    n, _, cap = arrived_ref.shape
+    edge_at = arrived_ref.shape[1] - EXTRA
+    tgt_at = edge_at - n
+    me = pos_ref[0]
+    remapped = jnp.zeros((2 * levels, cols), F32)
+    for s in range(n):
+        remapped = remapped + product(
+            slots_ref[me, :, s * cap : (s + 1) * cap], one_hot(tgt_ref[0, s : s + 1, :], cols), ((1,), (1,))
+        )
+    remapped = remapped[:levels] + remapped[levels:]
+    static, off = static_ref[...], off_ref[...]
+    lane = lax.broadcasted_iota(jnp.int32, (levels, cols), 1)
+
+    def beside(there, exists, column, own_end, side):
+        edge = arrived_ref[there, edge_at : edge_at + 1, :]
+        static_end, coupling, base = (row_as_column(edge, levels, (2 * i + side) * levels) for i in range(3))
+        values = slots_ref[there, :levels, :].astype(F32) + slots_ref[there, levels:, :].astype(F32)
+        landed = [
+            jnp.where(arrived_ref[there, tgt_at + s : tgt_at + s + 1, :] == column, values[:, s * cap : (s + 1) * cap], 0.0)
+            for s in range(n)
+        ]
+        remap_end = jnp.sum(sum(landed), axis=1, keepdims=True)
+        off_end = edge[:, 6 * levels + side : 6 * levels + side + 1]
+        coupled = coupling * (remap_end + base + off_end * own_end)
+        return jnp.where(exists, static_end, 0.0), jnp.where(exists, coupled, 0.0)
+
+    before, coupled_before = beside(jnp.maximum(me - 1, 0), me > 0, cols - 1.0, static[:, :1], 0)
+    after, coupled_after = beside(jnp.minimum(me + 1, n - 1), me < n - 1, 0.0, static[:, cols - 1 :], 1)
+    left = jnp.where(lane == 0, before, pltpu.roll(static, 1, 1))
+    right = jnp.where(lane == cols - 1, after, pltpu.roll(static, cols - 1, 1))
+    increment = remapped + diag_ref[...] * static + off * (left + right)
+    increment_ref[...] = increment
+    misfit = obs_ref[...] * (increment - innov_ref[...])
+    coupled = off * misfit
+    left = jnp.where(lane == 0, coupled_before, pltpu.roll(coupled, 1, 1))
+    right = jnp.where(lane == cols - 1, coupled_after, pltpu.roll(coupled, cols - 1, 1))
+    grad_ref[...] = static + diag_ref[...] * misfit + left + right
 
 
 def call(kernel, out_shape, spaces, scratch=(), limit=40 * MIB):
@@ -260,23 +406,46 @@
         [pltpu.VMEM(a.shape, a.dtype) for a in (perturb, control, level_loc)] + [pltpu.SemaphoreType.DMA((3,))],
         limit=58 * MIB,
     )(lev, perturb, control, level_loc)
-    payload = call(
-        band_kernel,
-        shape((groups, n, levels + EXTRA, cap), F32),
-        [SMEM] * 2 + [VMEM] * 7,
-        [pltpu.VMEM((2 * levels, band_cols), BF16)],
-    )(lev, counts, perturb, other_control, part, level_loc, static_control, send_src, send_wt)
-    arrived = lax.all_to_all(
-        payload.reshape(groups * n, levels + EXTRA, cap), ("grp", "tile"), split_axis=0, concat_axis=0, tiled=True
-    ).reshape(groups, n, levels + EXTRA, cap)
     flat = shape((levels, tile_cols), F32)
-    increment, partial, giving = call(
-        tile_kernel, (flat, flat, shape((n, levels + EXTRA, cap), F32)), [SMEM] + [VMEM] * 7
-    )(pos, arrived, recv_tgt, static_control, filter_diag.reshape(1, -1), filter_off.reshape(1, -1), obs_weight, innovation)
-    returned = lax.all_to_all(giving, "tile", split_axis=0, concat_axis=0, tiled=True)
-    grad_static, mine = call(
-        adjoint_kernel, (flat, shape((levels, band_cols + 128), F32)), [SMEM, SMEM] + [VMEM] * 5
-    )(pos, counts, returned, send_src, send_wt, partial, level_loc)
+    mine_shape = shape((levels, band_cols + 128), F32)
+    diag, off = filter_diag.reshape(1, -1), filter_off.reshape(1, -1)
+    if n * cap <= tile_cols:
+        rows = Rows(levels, band_cols, n, cap)
+        rest = call(static_kernel, shape((n, rows.total - rows.first, cap), F32), [SMEM] + [VMEM] * 8)(
+            counts, static_control, diag, off, obs_weight, innovation, send_src, send_wt, recv_tgt
+        )
+        sums = [
+            call(sum_kernel, shape((levels, band_cols), F32), [SMEM] + [VMEM] * 4)(
+                lev, perturb, other_control, part, level_loc
+            )
+        ]
+        for k in range(1, groups):
+            sums.append(lax.ppermute(sums[0], "grp", [(g, (g + k) % groups) for g in range(groups)]))
+        payload = call(payload_kernel, shape((n, rows.total, cap), F32), [VMEM] * (groups + 1))(*sums, rest)
+        arrived = lax.all_to_all(payload, "tile", split_axis=0, concat_axis=0, tiled=True)
+        mine, slots = call(
+            functools.partial(shared_kernel, tile_cols), (mine_shape, shape((n, 2 * levels, n * cap), BF16)), [SMEM] + [VMEM] * 2
+        )(pos, arrived, level_loc)
+        increment, grad_static = call(outputs_kernel, (flat, flat), [SMEM] + [VMEM] * 8)(
+            pos, arrived, slots, recv_tgt, static_control, diag, off, obs_weight, innovation
+        )
+    else:
+        payload = call(
+            band_kernel,
+            shape((groups, n, levels + EXTRA, cap), F32),
+            [SMEM] * 2 + [VMEM] * 7,
+            [pltpu.VMEM((2 * levels, band_cols), BF16)],
+        )(lev, counts, perturb, other_control, part, level_loc, static_control, send_src, send_wt)
+        arrived = lax.all_to_all(
+            payload.reshape(groups * n, levels + EXTRA, cap), ("grp", "tile"), split_axis=0, concat_axis=0, tiled=True
+        ).reshape(groups, n, levels + EXTRA, cap)
+        increment, partial, giving = call(
+            tile_kernel, (flat, flat, shape((n, levels + EXTRA, cap), F32)), [SMEM] + [VMEM] * 7
+        )(pos, arrived, recv_tgt, static_control, diag, off, obs_weight, innovation)
+        returned = lax.all_to_all(giving, "tile", split_axis=0, concat_axis=0, tiled=True)
+        grad_static, mine = call(adjoint_kernel, (flat, mine_shape), [SMEM, SMEM] + [VMEM] * 5)(
+            pos, counts, returned, send_src, send_wt, partial, level_loc
+        )
     theirs = lax.ppermute(mine, "lev", swap)
     grad_ens = call(ens_kernel, shape(control.shape, F32), [SMEM] + [VMEM] * 5)(
         lev, perturb, other_perturb, control, mine, theirs

time: 39.7 us -> 33.7 us (0.85)
  blocking collectives: 10.3 us -> 0 us
  waiting for transfers between devices: 9.95 us -> 11.6 us
  Pallas kernels: 8.75 us -> 10.1 us
  local copies, waits for them, and re-layouts: 0.76 us -> 1.39 us
  starting transfers between devices: 8.81 us -> 9.43 us
    all_to_all x1 -> x0, blocking collectives: 10.3 us -> none  [body(): lax.all_to_all(giving, 'tile', split_axis=0, concat_axis=0, tiled=True)]
    all_to_all x1, waiting for transfers between devices: 8.76 us -> 11.6 us  [body(): lax.all_to_all(payload, 'tile', split_axis=0, concat_axis=0, tiled=True)]
    ppermute x0 -> x1, starting transfers between devices: none -> 2.59 us  [body(): lax.ppermute(sums[0], 'grp', [(g, (g + k) % groups) for g in range(groups)])]
    all_to_all x1, starting transfers between devices: 8.04 us -> 6.32 us  [body(): lax.all_to_all(payload, 'tile', split_axis=0, concat_axis=0, tiled=True)]
    pallas_call x3 -> x5, Pallas kernels: 4.94 us -> 6.32 us  [the longest x1 2.25 us: body(): call(functools.partial(shared_kernel, tile_cols), (mine_shape, shape((n,...]
    ppermute x1, waiting for transfers between devices: 1.19 us -> 0.01 us  [body(): theirs = lax.ppermute(mine, 'lev', swap)]
    unnamed x26, local copies, waits for them, and re-layouts: 0.76 us -> 1.39 us
  transfers between devices with their start and end apart: 4 -> 5, of which waited for: 2 -> 1; matrix products, arithmetic and copies ran while one was open for 0% -> 0% of each run, Pallas kernels for 13% -> 21%
where the time goes in v3:
time: 33.7 us; the launch traced here: 33.4 us
  waiting for transfers between devices  11.6 us (34%)
  Pallas kernels  10.1 us (30%)
  starting transfers between devices  9.43 us (28%)
  local copies, waits for them, and re-layouts  1.39 us (4%)
  between operations  0.79 us (2%)
    all_to_all x1, waiting for transfers between devices, body(): lax.all_to_all(payload, 'tile', split_axis=0, concat_axis=0, tiled=True)  11.6 us
    all_to_all x1, starting transfers between devices, body(): lax.all_to_all(payload, 'tile', split_axis=0, concat_axis=0, tiled=True)  6.32 us
    ppermute x1, starting transfers between devices, body(): lax.ppermute(sums[0], 'grp', [(g, (g + k) % groups) for g in range(groups)])  2.59 us
    pallas_call x1, Pallas kernels, body(): call(own_kernel, shape((levels, band_cols), F32), [SMEM] + [HBM] * 3, [pl...  2.3 us
    pallas_call x1, Pallas kernels, body(): call(functools.partial(shared_kernel, tile_cols), (mine_shape, shape((n,...  2.25 us
    pallas_call x1, Pallas kernels, body(): call(outputs_kernel, (flat, flat), [SMEM] + [VMEM] * 8)  1.52 us
    pallas_call x1, Pallas kernels, body(): call(ens_kernel, shape(control.shape, F32), [SMEM] + [VMEM] * 5)  1.52 us
    unnamed x26, local copies, waits for them, and re-layouts  1.39 us
  transfers between devices with their start and end apart: 5, of which 1 were waited for; matrix products, arithmetic and copies ran while one was open for 0% of the time, Pallas kernels for 21%

profile of v3, /device:TPU:0, one launch (start us, length us, event | category | flops | bytes accessed | tf_op | source)
XLA Modules:
  0.0 33.4 jit_solution(4542242392278590026)
XLA Ops:
  0.6 0.5 %collective-permute-start = (f32[16,40,256]{2,1,0:T(8,128)}, f32[16,40,256]{2,1,0:T(8,128)S(1)}, u32[]{:S(2)}, u32[]{:S(2)}) collective-permute-start(f32[16,40,256]{2,1,0:T(8,128)} %control_ref.1), channel_id=1, source_target_pairs={{0,1},{1,0},{2,3},{3,2},{4,5},{5,4},{6,7},{7,6},{8,9},{9,8},{10,11... | collective-permute-start | bytes 1966088 | tf_op jit(solution)/shard_map/ppermute | solution.py:400
  1.1 0.0 copy-start
  1.1 0.0 copy-start.5
  1.2 2.3 %shard_map.139.part_ref = f32[16,256]{1,0:T(8,128)} custom-call(s32[1]{0:T(128)} %bitcast.1.lev_ref, bf16[16,40,256]{2,1,0:T(8,128)(2,1)} %perturb_ref.3, f32[16,40,256]{2,1,0:T(8,128)} %control_ref.1, f32[16,32]{1,0:T(8,128)} %loc_ref.3), custom_call_target="tpu_custom_call" | custom-call | tf_op jit(solution)/shard_map/pallas_call | solution.py:402
  3.5 0.0 copy-start.2
  3.5 0.0 copy-start.3
  3.5 0.0 copy-start.4
  3.5 0.0 collective-permute-done.other_ref
  3.5 0.0 copy-done
  3.5 0.0 copy-done.5
  3.5 0.0 copy-start.6
  3.5 0.7 %copy-done.6 = f32[16,256]{1,0:T(8,128)S(1)} copy-done((f32[16,256]{1,0:T(8,128)S(1)}, f32[16,256]{1,0:T(8,128)}, u32[]{:S(2)}) %copy-start.6) | copy-done | bytes 16408
  4.3 0.0 copy-start.7
  4.3 0.0 copy-start.8
  4.3 0.0 copy-start.9
  4.3 0.0 copy-start.10
  4.3 0.0 copy-start.11
  4.3 0.7 %shard_map.140.refs_0_ = f32[16,256]{1,0:T(8,128)S(1)} custom-call(s32[1]{0:T(128)} %bitcast.1.lev_ref, bf16[16,40,256]{2,1,0:T(8,128)(2,1)S(1)} %copy-done, f32[16,40,256]{2,1,0:T(8,128)S(1)} %collective-permute-done.other_ref, f32[16,256]{1,0:T(8,128)S(1)} %copy-done.6, f32[16,32]{1,0:T(8,128)S(1)} %copy-done.5), custom_call_target="tpu_custom_call" | custom-call | tf_op jit(solution)/shard_map/pallas_call | solution.py:418
  5.0 2.6 %collective-permute-start.1 = (f32[16,256]{1,0:T(8,128)S(1)}, f32[16,256]{1,0:T(8,128)S(1)}, u32[]{:S(2)}, u32[]{:S(2)}) collective-permute-start(f32[16,256]{1,0:T(8,128)S(1)} %shard_map.140.refs_0_), channel_id=1, source_target_pairs={{0,16},{16,0},{1,17},{17,1},{2,18},{18,2},{3,19},{19,3},{4,20},{20... | collective-permute-start | bytes 49160 | tf_op jit(solution)/shard_map/ppermute | solution.py:423
  7.6 0.0 copy-start.12
  7.6 0.0 copy-done.2
  7.6 0.0 copy-done.3
  7.6 0.0 copy-done.4
  7.6 0.0 copy-done.7
  7.6 0.0 copy-done.8
  7.6 0.0 copy-done.9
  7.6 0.0 copy-done.10
  7.6 0.0 copy-done.11
  7.6 0.6 %copy-done.12 = s32[1,8]{1,0:T(1,128)S(1)} copy-done((s32[1,8]{1,0:T(1,128)S(1)}, s32[1,8]{1,0:T(1,128)}, u32[]{:S(2)}) %copy-start.12) | copy-done | bytes 56
  8.2 1.1 %shard_map.141.refs_2_ = f32[8,64,128]{2,1,0:T(8,128)S(1)} custom-call(s32[1,8]{1,0:T(1,128)S(1)} %copy-done.12, f32[16,1024]{1,0:T(8,128)S(1)} %copy-done.2, f32[1,1024]{1,0:T(1,128)S(1)} %bitcast.4, f32[1,1024]{1,0:T(1,128)S(1)} %bitcast.6, f32[16,1024]{1,0:T(8,128)S(1)} %copy-done.3, f32[16,1024]{1,0:T(8,128)S(1)} %copy-done.4, ...), custom_call_target="tpu_custom_call" | custom-call | tf_op jit(solution)/shard_map/pallas_call | solution.py:414
  9.3 0.0 collective-permute-done.1.refs_1_
  9.3 0.8 %shard_map.142 = f32[8,96,128]{2,1,0:T(8,128)} custom-call(f32[16,256]{1,0:T(8,128)S(1)} %shard_map.140.refs_0_, f32[16,256]{1,0:T(8,128)S(1)} %collective-permute-done.1.refs_1_, f32[8,64,128]{2,1,0:T(8,128)S(1)} %shard_map.141.refs_2_), custom_call_target="tpu_custom_call" | custom-call | tf_op jit(solution)/shard_map/pallas_call | solution.py:424
  10.1 6.3 %all-to-all-start = ((f32[8,96,128]{2,1,0:T(8,128)}), f32[8,96,128]{2,1,0:T(8,128)S(1)}, u32[]{:S(2)}, u32[]{:S(2)}) async-start(f32[8,96,128]{2,1,0:T(8,128)} %shard_map.142), calls=%async_computation | async-start | bytes 786432 | tf_op jit(solution)/shard_map/all_to_all | solution.py:425
  16.4 0.0 collective-permute-start.2
  16.5 11.6 %all-to-all-done.arrived_ref = f32[8,96,128]{2,1,0:T(8,128)S(1)} async-done(((f32[8,96,128]{2,1,0:T(8,128)}), f32[8,96,128]{2,1,0:T(8,128)S(1)}, u32[]{:S(2)}, u32[]{:S(2)}) %all-to-all-start) | async-done | bytes 393248 | tf_op jit(solution)/shard_map/all_to_all | solution.py:425
  28.0 2.3 %shard_map.143 = (f32[16,384]{1,0:T(8,128)S(1)}, bf16[8,32,1024]{2,1,0:T(8,128)(2,1)S(1)}) custom-call(s32[1]{0:T(128)} %bitcast.pos_ref, f32[8,96,128]{2,1,0:T(8,128)S(1)} %all-to-all-done.arrived_ref, f32[16,32]{1,0:T(8,128)S(1)} %copy-done.5), custom_call_target="tpu_custom_call" | custom-call | tf_op jit(solution)/shard_map/pallas_call | solution.py:426
  30.3 0.0 copy-start.1
  30.3 0.0 collective-permute-start.3
  30.3 1.5 %shard_map.144 = (f32[16,1024]{1,0:T(8,128)}, f32[16,1024]{1,0:T(8,128)}) custom-call(s32[1]{0:T(128)} %bitcast.pos_ref, f32[8,96,128]{2,1,0:T(8,128)S(1)} %all-to-all-done.arrived_ref, bf16[8,32,1024]{2,1,0:T(8,128)(2,1)S(1)} %get-tuple-element.7.slots_ref, s32[1,8,128]{2,1,0:T(8,128)S(1)} %copy-done.9, f32[16,1024]{1,0:T(8,128)S(1)} %copy-done.2, ...), custom_call_target="tpu_custom_call" | custom-call | tf_op jit(solution)/shard_map/pallas_call | solution.py:429
  31.8 0.0 collective-permute-done.2.other_ref
  31.8 0.0 collective-permute-done.3.theirs_ref
  31.8 0.0 copy-done.1
  31.8 1.5 %shard_map.145 = f32[16,40,256]{2,1,0:T(8,128)} custom-call(s32[1]{0:T(128)} %bitcast.1.lev_ref, bf16[16,40,256]{2,1,0:T(8,128)(2,1)S(1)} %copy-done, bf16[16,40,256]{2,1,0:T(8,128)(2,1)S(1)} %collective-permute-done.2.other_ref, f32[16,40,256]{2,1,0:T(8,128)S(1)} %copy-done.1, f32[16,384]{1,0:T(8,128)S(1)} %get-tuple-element.10.mine_ref, ...), custom_call_target="tpu_custom_call" | custom-call | tf_op jit(solution)/shard_map/pallas_call | solution.py:450
Async XLA Ops:
  0.6 2.9 %collective-permute-start = (f32[16,40,256]{2,1,0:T(8,128)}, f32[16,40,256]{2,1,0:T(8,128)S(1)}, u32[]{:S(2)}, u32[]{:S(2)}) collective-permute-start(f32[16,40,256]{2,1,0:T(8,128)} %control_ref.1), channel_id=1, source_target_pairs={{0,1},{1,0},{2,3},{3,2},{4,5},{5,4},{6,7},{7,6},{8,9},{9,8},{10,11... | collective-permute-start | bytes 1966088 | tf_op jit(solution)/shard_map/ppermute | solution.py:400
  1.1 2.4 %copy-start = (bf16[16,40,256]{2,1,0:T(8,128)(2,1)S(1)}, bf16[16,40,256]{2,1,0:T(8,128)(2,1)}, u32[]{:S(2)}) copy-start(bf16[16,40,256]{2,1,0:T(8,128)(2,1)} %perturb_ref.3) | copy-start | bytes 983044
  1.1 2.4 %copy-start.5 = (f32[16,32]{1,0:T(8,128)S(1)}, f32[16,32]{1,0:T(8,128)}, u32[]{:S(2)}) copy-start(f32[16,32]{1,0:T(8,128)} %loc_ref.3) | copy-start | bytes 6148
  3.5 4.1 %copy-start.2 = (f32[16,1024]{1,0:T(8,128)S(1)}, f32[16,1024]{1,0:T(8,128)}, u32[]{:S(2)}) copy-start(f32[16,1024]{1,0:T(8,128)} %static_ref.3) | copy-start | bytes 196612
  3.5 4.1 %copy-start.3 = (f32[16,1024]{1,0:T(8,128)S(1)}, f32[16,1024]{1,0:T(8,128)}, u32[]{:S(2)}) copy-start(f32[16,1024]{1,0:T(8,128)} %obs_ref.3) | copy-start | bytes 196612
  3.5 4.1 %copy-start.4 = (f32[16,1024]{1,0:T(8,128)S(1)}, f32[16,1024]{1,0:T(8,128)}, u32[]{:S(2)}) copy-start(f32[16,1024]{1,0:T(8,128)} %innov_ref.3) | copy-start | bytes 196612
  3.5 0.8 %copy-start.6 = (f32[16,256]{1,0:T(8,128)S(1)}, f32[16,256]{1,0:T(8,128)}, u32[]{:S(2)}) copy-start(f32[16,256]{1,0:T(8,128)} %shard_map.139.part_ref) | copy-start | bytes 49156
  4.3 3.3 %copy-start.7 = (f32[1024]{0:T(1024)S(1)}, f32[1024]{0:T(1024)}, u32[]{:S(2)}) copy-start(f32[1024]{0:T(1024)} %param.16) | copy-start | bytes 12292
  4.3 3.3 %copy-start.8 = (f32[1024]{0:T(1024)S(1)}, f32[1024]{0:T(1024)}, u32[]{:S(2)}) copy-start(f32[1024]{0:T(1024)} %param.17) | copy-start | bytes 12292
  4.3 3.3 %copy-start.9 = (s32[1,8,128]{2,1,0:T(8,128)S(1)}, s32[1,8,128]{2,1,0:T(8,128)}, u32[]{:S(2)}) copy-start(s32[1,8,128]{2,1,0:T(8,128)} %tgt_ref.3) | copy-start | bytes 12292
  4.3 3.3 %copy-start.10 = (s32[1,8,128]{2,1,0:T(8,128)S(1)}, s32[1,8,128]{2,1,0:T(8,128)}, u32[]{:S(2)}) copy-start(s32[1,8,128]{2,1,0:T(8,128)} %src_ref.1) | copy-start | bytes 12292
  4.3 3.3 %copy-start.11 = (f32[1,8,128]{2,1,0:T(8,128)S(1)}, f32[1,8,128]{2,1,0:T(8,128)}, u32[]{:S(2)}) copy-start(f32[1,8,128]{2,1,0:T(8,128)} %weight_ref.1) | copy-start | bytes 12292
  5.0 4.4 %collective-permute-start.1 = (f32[16,256]{1,0:T(8,128)S(1)}, f32[16,256]{1,0:T(8,128)S(1)}, u32[]{:S(2)}, u32[]{:S(2)}) collective-permute-start(f32[16,256]{1,0:T(8,128)S(1)} %shard_map.140.refs_0_), channel_id=1, source_target_pairs={{0,16},{16,0},{1,17},{17,1},{2,18},{18,2},{3,19},{19,3},{4,20},{20... | collective-permute-start | bytes 49160 | tf_op jit(solution)/shard_map/ppermute | solution.py:423
  7.6 0.7 %copy-start.12 = (s32[1,8]{1,0:T(1,128)S(1)}, s32[1,8]{1,0:T(1,128)}, u32[]{:S(2)}) copy-start(s32[1,8]{1,0:T(1,128)} %counts_ref.1) | copy-start | bytes 100
  10.1 17.9 %all-to-all-start = ((f32[8,96,128]{2,1,0:T(8,128)}), f32[8,96,128]{2,1,0:T(8,128)S(1)}, u32[]{:S(2)}, u32[]{:S(2)}) async-start(f32[8,96,128]{2,1,0:T(8,128)} %shard_map.142), calls=%async_computation | async-start | bytes 786432 | tf_op jit(solution)/shard_map/all_to_all | solution.py:425
  16.4 15.4 %collective-permute-start.2 = (bf16[16,40,256]{2,1,0:T(8,128)(2,1)S(1)}, bf16[16,40,256]{2,1,0:T(8,128)(2,1)S(1)}, u32[]{:S(2)}, u32[]{:S(2)}) collective-permute-start(bf16[16,40,256]{2,1,0:T(8,128)(2,1)S(1)} %copy-done), channel_id=1, source_target_pairs={{0,1},{1,0},{2,3},{3,2},{4,5},{5,4},{6,7},{7,6},{8,9},{9,8},{10,11... | collective-permute-start | bytes 983048 | tf_op jit(solution)/shard_map/ppermute | solution.py:401
  30.3 1.5 %copy-start.1 = (f32[16,40,256]{2,1,0:T(8,128)S(1)}, f32[16,40,256]{2,1,0:T(8,128)}, u32[]{:S(2)}) copy-start(f32[16,40,256]{2,1,0:T(8,128)} %control_ref.1) | copy-start | bytes 1966084
  30.3 1.5 %collective-permute-start.3 = (f32[16,384]{1,0:T(8,128)S(1)}, f32[16,384]{1,0:T(8,128)S(1)}, u32[]{:S(2)}, u32[]{:S(2)}) collective-permute-start(f32[16,384]{1,0:T(8,128)S(1)} %get-tuple-element.10.mine_ref), channel_id=1, source_target_pairs={{0,1},{1,0},{2,3},{3,2},{4,5},{5,4},{6,7},{7,6},{8,9},{9,8},{10,11... | collective-permute-start | bytes 73736 | tf_op jit(solution)/shard_map/ppermute | solution.py:449

commit v4 on v3

--- a/solution.py
+++ b/solution.py
@@ -218,21 +218,21 @@
 
 
 class Rows:
-    def __init__(self, levels, band, n, cap):
-        self.sums = [slice(i * levels, (i + 1) * levels) for i in range(band // cap)]
-        at = band // cap * levels
-        self.first = at
-        self.weight = slice(at, at + levels)
-        self.base = slice(at + levels, at + 2 * levels)
-        at += 2 * levels
+    def __init__(self, levels, n):
+        self.weight = slice(0, levels)
+        self.base = slice(levels, 2 * levels)
+        at = 2 * levels
         self.src, self.factor, self.tgt, self.edge = at, at + n, at + 2 * n, at + 3 * n
         self.total = at + 3 * n + EXTRA
 
 
-def static_kernel(counts_ref, static_ref, diag_ref, off_ref, obs_ref, innov_ref, src_ref, weight_ref, tgt_ref, out_ref):
+def static_kernel(pos_ref, counts_ref, static_ref, diag_ref, off_ref, obs_ref, innov_ref, src_ref, weight_ref, tgt_ref,
+                  *out_refs):
     levels, cols = static_ref.shape
-    n, _, cap = out_ref.shape
-    rows = Rows(levels, 0, n, cap)
+    n = len(out_refs)
+    cap = src_ref.shape[2]
+    rows = Rows(levels, n)
+    me = pos_ref[0]
     static, off, obs = static_ref[...], off_ref[...], obs_ref[...]
     lane = lax.broadcasted_iota(jnp.int32, (levels, cols), 1)
     left = jnp.where(lane == 0, 0.0, pltpu.roll(static, 1, 1))
@@ -246,16 +246,17 @@
     edge = edge + jnp.where(place == 6 * levels + 1, off[:, :1], 0.0)
     edge = jnp.broadcast_to(edge, (EXTRA, cap))
     both = jnp.concatenate(halves(jnp.concatenate([obs, base], axis=0)), axis=0)
-    src = src_ref[0].astype(F32)
-    tgt = tgt_ref[0].astype(F32)
-    factor = jnp.concatenate([factor_of(counts_ref, weight_ref, d) for d in range(n)], axis=0)
-    for q in range(n):
-        picked = product(both, one_hot(tgt_ref[0, q : q + 1, :], cols))
-        out_ref[q, : 2 * levels, :] = picked[: 2 * levels] + picked[2 * levels :]
-        out_ref[q, rows.src : rows.src + n, :] = src
-        out_ref[q, rows.factor : rows.factor + n, :] = factor
-        out_ref[q, rows.tgt : rows.tgt + n, :] = tgt
-        out_ref[q, rows.edge :, :] = edge
+    tgts = [tgt_ref[0, pl.ds(me ^ r, 1), :] for r in range(n)]
+    src = jnp.concatenate([src_ref[0, pl.ds(me ^ r, 1), :] for r in range(n)], axis=0).astype(F32)
+    tgt = jnp.concatenate(tgts, axis=0).astype(F32)
+    factor = jnp.concatenate([factor_of(counts_ref, weight_ref, me ^ r) for r in range(n)], axis=0)
+    for r, out_ref in enumerate(out_refs):
+        picked = product(both, one_hot(tgts[r], cols))
+        out_ref[: 2 * levels, :] = picked[: 2 * levels] + picked[2 * levels :]
+        out_ref[rows.src : rows.src + n, :] = src
+        out_ref[rows.factor : rows.factor + n, :] = factor
+        out_ref[rows.tgt : rows.tgt + n, :] = tgt
+        out_ref[rows.edge :, :] = edge
 
 
 def sum_kernel(lev_ref, perturb_ref, other_ref, part_ref, loc_ref, out_ref):
@@ -264,85 +265,98 @@
     out_ref[...] = part_ref[...] + mixed_sum(weights, perturb_ref, other_ref)
 
 
-def payload_kernel(*refs):
-    *sums, rest_ref, out_ref = refs
+def blocks_kernel(groups, *refs):
+    sums = refs[:groups]
+    count = (len(refs) - groups - 1) // 2
+    rests = refs[groups : groups + count]
+    total_ref = refs[groups + count]
+    out_refs = refs[groups + count + 1 :]
     total = sum(ref[...] for ref in sums)
-    levels, band = total.shape
-    n, _, cap = out_ref.shape
-    rows = Rows(levels, band, n, cap)
-    for q in range(n):
-        for i, place in enumerate(rows.sums):
-            out_ref[q, place, :] = total[:, i * cap : (i + 1) * cap]
-        out_ref[q, rows.first :, :] = rest_ref[q]
-
-
-def shared_kernel(cols, pos_ref, arrived_ref, loc_ref, out_ref, slots_ref):
-    levels = loc_ref.shape[0]
-    n, _, cap = arrived_ref.shape
+    cap = total_ref.shape[1]
+    total = jnp.concatenate([total[:, at : at + cap] for at in range(0, total.shape[1], cap)], axis=0)
+    total_ref[...] = total
+    for rest_ref, out_ref in zip(rests, out_refs):
+        out_ref[: total.shape[0], :] = total
+        out_ref[total.shape[0] :, :] = rest_ref[...]
+
+
+def shared_kernel(n, levels, cols, pos_ref, loc_ref, *refs):
+    sums_refs, rest_refs = refs[:n], refs[n : 2 * n]
+    out_ref, slots_ref, tables_ref = refs[2 * n :]
+    cap = slots_ref.shape[2] // n
     band = out_ref.shape[1] - 128
-    rows = Rows(levels, band, n, cap)
+    rows = Rows(levels, n)
+    parts = band // cap
     me = pos_ref[0]
+    heads = [ref.shape[0] - rows.total for ref in rest_refs]
+
+    def rest(r, at, size):
+        return rest_refs[r][heads[r] + at : heads[r] + at + size, :]
+
+    def row(r, at):
+        return rest(r, at, 1)
+
     column = lax.broadcasted_iota(jnp.int32, (band, cap), 0).astype(F32)
 
     def chosen(s, d):
-        return jnp.where(column == arrived_ref[s, rows.src + d : rows.src + d + 1, :], 1.0, 0.0).astype(BF16)
-
+        return jnp.where(column == row(s, rows.src + (s ^ d)), 1.0, 0.0).astype(BF16)
+
+    for r in range(n):
+        tables_ref[me ^ r] = rest(r, rows.tgt, n + EXTRA)
     for s in range(n):
-        sums = jnp.concatenate([arrived_ref[s, place, :] for place in rows.sums], axis=1)
+        sums = jnp.concatenate([sums_refs[s][i * levels : (i + 1) * levels, :] for i in range(parts)], axis=1)
         both = jnp.concatenate(halves(sums), axis=0)
         for d in range(n):
             picked = product(both, chosen(s, d))
-            values = (picked[:levels] + picked[levels:]) * arrived_ref[s, rows.factor + d : rows.factor + d + 1, :]
+            values = (picked[:levels] + picked[levels:]) * row(s, rows.factor + (s ^ d))
             slots_ref[d, :, s * cap : (s + 1) * cap] = jnp.concatenate(halves(values), axis=0)
-    own = jnp.concatenate([arrived_ref[d, pl.ds(rows.tgt + me, 1), :] for d in range(n)], axis=0)
+    own = jnp.concatenate([row(d, rows.tgt + d) for d in range(n)], axis=0)
     turned = own.T
     last = cols - 1.0
     total = jnp.zeros((levels, band), F32)
     for d in range(n):
         same = [
-            jnp.where(turned[:, d : d + 1] == arrived_ref[d, rows.tgt + s : rows.tgt + s + 1, :], 1.0, 0.0).astype(BF16)
-            for s in range(n)
+            jnp.where(turned[:, d : d + 1] == row(d, rows.tgt + (s ^ d)), 1.0, 0.0).astype(BF16) for s in range(n)
         ]
         met = product(slots_ref[d], jnp.concatenate(same, axis=1), ((1,), (1,)))
-        value = met[:levels] + met[levels:] + arrived_ref[d, rows.base, :]
-        edge = arrived_ref[d, rows.edge : rows.edge + 1, :]
-        if d > 0:
-            before = row_as_column(arrived_ref[d - 1, rows.edge : rows.edge + 1, :], levels, 0)
-            near = jnp.where(own[d : d + 1] == 0.0, edge[:, 6 * levels + 1 : 6 * levels + 2], 0.0)
-            value = value + before * near
-        if d < n - 1:
-            after = row_as_column(arrived_ref[d + 1, rows.edge : rows.edge + 1, :], levels, levels)
-            near = jnp.where(own[d : d + 1] == last, edge[:, 6 * levels : 6 * levels + 1], 0.0)
-            value = value + after * near
-        misfit = arrived_ref[d, rows.weight, :] * value
-        given = misfit * arrived_ref[me, rows.factor + d : rows.factor + d + 1, :]
-        total = total + select(given, chosen(me, d), ((1,), (1,)))
+        value = met[:levels] + met[levels:] + rest(d, levels, levels)
+        edge = row(d, rows.edge)
+        there = me ^ d
+        before = tables_ref[jnp.maximum(there - 1, 0), n : n + 1, :]
+        near = jnp.where((own[d : d + 1] == 0.0) & (there > 0), edge[:, 6 * levels + 1 : 6 * levels + 2], 0.0)
+        value = value + row_as_column(before, levels, 0) * near
+        after = tables_ref[jnp.minimum(there + 1, n - 1), n : n + 1, :]
+        near = jnp.where((own[d : d + 1] == last) & (there < n - 1), edge[:, 6 * levels : 6 * levels + 1], 0.0)
+        value = value + row_as_column(after, levels, levels) * near
+        misfit = rest(d, 0, levels) * value
+        given = misfit * row(0, rows.factor + d)
+        total = total + select(given, chosen(0, d), ((1,), (1,)))
     out_ref[:, :band] = total
     out_ref[:, band:] = jnp.concatenate([loc_ref[...], jnp.zeros((levels, 128 - loc_ref.shape[1]), F32)], axis=1)
 
 
-def outputs_kernel(pos_ref, arrived_ref, slots_ref, tgt_ref, static_ref, diag_ref, off_ref, obs_ref, innov_ref,
+def outputs_kernel(pos_ref, slots_ref, tables_ref, static_ref, diag_ref, off_ref, obs_ref, innov_ref,
                    increment_ref, grad_ref):
     levels, cols = static_ref.shape
-    n, _, cap = arrived_ref.shape
-    edge_at = arrived_ref.shape[1] - EXTRA
-    tgt_at = edge_at - n
+    n = tables_ref.shape[0]
+    cap = tables_ref.shape[2]
     me = pos_ref[0]
+    row = lax.broadcasted_iota(jnp.int32, (cols, cap), 0).astype(F32)
     remapped = jnp.zeros((2 * levels, cols), F32)
     for s in range(n):
-        remapped = remapped + product(
-            slots_ref[me, :, s * cap : (s + 1) * cap], one_hot(tgt_ref[0, s : s + 1, :], cols), ((1,), (1,))
-        )
+        landing = jnp.where(row == tables_ref[me, s : s + 1, :], 1.0, 0.0).astype(BF16)
+        remapped = remapped + product(slots_ref[0, :, s * cap : (s + 1) * cap], landing, ((1,), (1,)))
     remapped = remapped[:levels] + remapped[levels:]
     static, off = static_ref[...], off_ref[...]
     lane = lax.broadcasted_iota(jnp.int32, (levels, cols), 1)
 
     def beside(there, exists, column, own_end, side):
-        edge = arrived_ref[there, edge_at : edge_at + 1, :]
+        edge = tables_ref[there, n : n + 1, :]
         static_end, coupling, base = (row_as_column(edge, levels, (2 * i + side) * levels) for i in range(3))
-        values = slots_ref[there, :levels, :].astype(F32) + slots_ref[there, levels:, :].astype(F32)
+        far = me ^ there
+        values = slots_ref[far, :levels, :].astype(F32) + slots_ref[far, levels:, :].astype(F32)
         landed = [
-            jnp.where(arrived_ref[there, tgt_at + s : tgt_at + s + 1, :] == column, values[:, s * cap : (s + 1) * cap], 0.0)
+            jnp.where(tables_ref[there, pl.ds(s ^ far, 1), :] == column, values[:, s * cap : (s + 1) * cap], 0.0)
             for s in range(n)
         ]
         remap_end = jnp.sum(sum(landed), axis=1, keepdims=True)
@@ -409,10 +423,11 @@
     flat = shape((levels, tile_cols), F32)
     mine_shape = shape((levels, band_cols + 128), F32)
     diag, off = filter_diag.reshape(1, -1), filter_off.reshape(1, -1)
-    if n * cap <= tile_cols:
-        rows = Rows(levels, band_cols, n, cap)
-        rest = call(static_kernel, shape((n, rows.total - rows.first, cap), F32), [SMEM] + [VMEM] * 8)(
-            counts, static_control, diag, off, obs_weight, innovation, send_src, send_wt, recv_tgt
+    if n * cap <= tile_cols and n & (n - 1) == 0:
+        rows = Rows(levels, n)
+        stacked = band_cols // cap * levels
+        rests = call(static_kernel, [shape((rows.total, cap), F32)] * n, [SMEM] * 2 + [VMEM] * 8)(
+            pos, counts, static_control, diag, off, obs_weight, innovation, send_src, send_wt, recv_tgt
         )
         sums = [
             call(sum_kernel, shape((levels, band_cols), F32), [SMEM] + [VMEM] * 4)(
@@ -421,13 +436,22 @@
         ]
         for k in range(1, groups):
             sums.append(lax.ppermute(sums[0], "grp", [(g, (g + k) % groups) for g in range(groups)]))
-        payload = call(payload_kernel, shape((n, rows.total, cap), F32), [VMEM] * (groups + 1))(*sums, rest)
-        arrived = lax.all_to_all(payload, "tile", split_axis=0, concat_axis=0, tiled=True)
-        mine, slots = call(
-            functools.partial(shared_kernel, tile_cols), (mine_shape, shape((n, 2 * levels, n * cap), BF16)), [SMEM] + [VMEM] * 2
-        )(pos, arrived, level_loc)
-        increment, grad_static = call(outputs_kernel, (flat, flat), [SMEM] + [VMEM] * 8)(
-            pos, arrived, slots, recv_tgt, static_control, diag, off, obs_weight, innovation
+        total, *blocks = call(
+            functools.partial(blocks_kernel, groups),
+            [shape((stacked, cap), F32)] + [shape((stacked + rows.total, cap), F32)] * (n - 1),
+            [VMEM] * (groups + n - 1),
+        )(*sums, *rests[1:])
+        arrived = {}
+        for r in reversed(range(1, n)):
+            arrived[r] = lax.ppermute(blocks[r - 1], "tile", [(i, i ^ r) for i in range(n)])
+        arrived = [arrived[r] for r in range(1, n)]
+        mine, slots, tables = call(
+            functools.partial(shared_kernel, n, levels, tile_cols),
+            (mine_shape, shape((n, 2 * levels, n * cap), BF16), shape((n, n + EXTRA, cap), F32)),
+            [SMEM] + [VMEM] * (2 * n + 1),
+        )(pos, level_loc, total, *arrived, rests[0], *arrived)
+        increment, grad_static = call(outputs_kernel, (flat, flat), [SMEM] + [VMEM] * 7)(
+            pos, slots, tables, static_control, diag, off, obs_weight, innovation
         )
     else:
         payload = call(

time: 33.7 us -> 33.8 us (level)
  starting transfers between devices: 9.43 us -> 15.5 us
  waiting for transfers between devices: 11.6 us -> 6.38 us
  Pallas kernels: 10.1 us -> 9.42 us
    ppermute x0 -> x7, starting transfers between devices: none -> 11.9 us  [body(): lax.ppermute(blocks[r - 1], 'tile', [(i, i ^ r) for i in range(n)])]
    all_to_all x1 -> x0, waiting for transfers between devices: 11.6 us -> none  [body(): lax.all_to_all(payload, 'tile', split_axis=0, concat_axis=0, tiled=True)]
    ppermute x0 -> x7, waiting for transfers between devices: none -> 6.37 us  [body(): lax.ppermute(blocks[r - 1], 'tile', [(i, i ^ r) for i in range(n)])]
    all_to_all x1 -> x0, starting transfers between devices: 6.32 us -> none  [body(): lax.all_to_all(payload, 'tile', split_axis=0, concat_axis=0, tiled=True)]
    pallas_call x4, Pallas kernels: 5.65 us -> 4.93 us  [the longest x1 2.26 us: body(): call(functools.partial(shared_kernel, n, levels, tile_cols), (mine_shape,...]
    ppermute x1, starting transfers between devices: 2.59 us -> 2.97 us  [body(): lax.ppermute(sums[0], 'grp', [(g, (g + k) % groups) for g in range(groups)])]
  transfers between devices with their start and end apart: 5 -> 11, of which waited for: 1 -> 3; matrix products, arithmetic and copies ran while one was open for 0% -> 0% of each run, Pallas kernels for 21% -> 24%
where the time goes in v4:
time: 33.8 us; the launch traced here: 33.5 us
  starting transfers between devices  15.5 us (46%)
  Pallas kernels  9.42 us (28%)
  waiting for transfers between devices  6.38 us (19%)
  local copies, waits for them, and re-layouts  1.43 us (4%)
  between operations  0.78 us (2%)
    ppermute x7, starting transfers between devices, body(): lax.ppermute(blocks[r - 1], 'tile', [(i, i ^ r) for i in range(n)])  11.9 us
    ppermute x7, waiting for transfers between devices, body(): lax.ppermute(blocks[r - 1], 'tile', [(i, i ^ r) for i in range(n)])  6.37 us
    ppermute x1, starting transfers between devices, body(): lax.ppermute(sums[0], 'grp', [(g, (g + k) % groups) for g in range(groups)])  2.97 us
    pallas_call x1, Pallas kernels, body(): call(own_kernel, shape((levels, band_cols), F32), [SMEM] + [HBM] * 3, [pl...  2.3 us
    pallas_call x1, Pallas kernels, body(): call(functools.partial(shared_kernel, n, levels, tile_cols), (mine_shape,...  2.26 us
    pallas_call x1, Pallas kernels, body(): call(outputs_kernel, (flat, flat), [SMEM] + [VMEM] * 7)  1.53 us
    pallas_call x1, Pallas kernels, body(): call(ens_kernel, shape(control.shape, F32), [SMEM] + [VMEM] * 5)  1.52 us
    unnamed x26, local copies, waits for them, and re-layouts  1.43 us
  transfers between devices with their start and end apart: 11, of which 3 were waited for; matrix products, arithmetic and copies ran while one was open for 0% of the time, Pallas kernels for 24%

profile of v4, /device:TPU:0, one launch (start us, length us, event | category | flops | bytes accessed | tf_op | source)
XLA Modules:
  0.0 33.5 jit_solution(15536742191521393675)
XLA Ops:
  0.6 0.5 %collective-permute-start = (f32[16,40,256]{2,1,0:T(8,128)}, f32[16,40,256]{2,1,0:T(8,128)S(1)}, u32[]{:S(2)}, u32[]{:S(2)}) collective-permute-start(f32[16,40,256]{2,1,0:T(8,128)} %control_ref.1), channel_id=1, source_target_pairs={{0,1},{1,0},{2,3},{3,2},{4,5},{5,4},{6,7},{7,6},{8,9},{9,8},{10,11... | collective-permute-start | bytes 1966088 | tf_op jit(solution)/shard_map/ppermute | solution.py:414
  1.1 0.1 collective-permute-start.9
  1.2 0.0 copy-start
  1.2 0.0 copy-start.5
  1.2 2.3 %shard_map.139.part_ref = f32[16,256]{1,0:T(8,128)} custom-call(s32[1]{0:T(128)} %bitcast.1.lev_ref, bf16[16,40,256]{2,1,0:T(8,128)(2,1)} %perturb_ref.3, f32[16,40,256]{2,1,0:T(8,128)} %control_ref.1, f32[16,32]{1,0:T(8,128)} %loc_ref.3), custom_call_target="tpu_custom_call" | custom-call | tf_op jit(solution)/shard_map/pallas_call | solution.py:416
  3.5 0.0 copy-start.2
  3.6 0.0 copy-start.3
  3.6 0.0 copy-start.4
  3.6 0.0 collective-permute-done.other_ref
  3.6 0.0 copy-done
  3.6 0.0 copy-done.5
  3.6 0.0 copy-start.6
  3.6 0.7 %copy-done.6 = f32[16,256]{1,0:T(8,128)S(1)} copy-done((f32[16,256]{1,0:T(8,128)S(1)}, f32[16,256]{1,0:T(8,128)}, u32[]{:S(2)}) %copy-start.6) | copy-done | bytes 16408
  4.4 0.0 copy-start.9
  4.4 0.7 %shard_map.140.refs_0_ = f32[16,256]{1,0:T(8,128)S(1)} custom-call(s32[1]{0:T(128)} %bitcast.1.lev_ref, bf16[16,40,256]{2,1,0:T(8,128)(2,1)S(1)} %copy-done, f32[16,40,256]{2,1,0:T(8,128)S(1)} %collective-permute-done.other_ref, f32[16,256]{1,0:T(8,128)S(1)} %copy-done.6, f32[16,32]{1,0:T(8,128)S(1)} %copy-done.5), custom_call_target="tpu_custom_call" | custom-call | tf_op jit(solution)/shard_map/pallas_call | solution.py:433
  5.1 3.0 %collective-permute-start.1 = (f32[16,256]{1,0:T(8,128)S(1)}, f32[16,256]{1,0:T(8,128)S(1)}, u32[]{:S(2)}, u32[]{:S(2)}) collective-permute-start(f32[16,256]{1,0:T(8,128)S(1)} %shard_map.140.refs_0_), channel_id=1, source_target_pairs={{0,16},{16,0},{1,17},{17,1},{2,18},{18,2},{3,19},{19,3},{4,20},{20... | collective-permute-start | bytes 49160 | tf_op jit(solution)/shard_map/ppermute | solution.py:438
  8.0 0.0 copy-done.2
  8.0 0.0 copy-done.3
  8.0 0.0 copy-done.4
  8.1 0.0 copy-done.9
  8.1 0.0 copy-done.10
  8.1 0.0 copy-done.11
  8.1 0.6 %copy-done.8 = f32[1024]{0:T(1024)S(1)} copy-done((f32[1024]{0:T(1024)S(1)}, f32[1024]{0:T(1024)}, u32[]{:S(2)}) %copy-start.8) | copy-done | bytes 4120
  8.7 0.0 copy-done.7
  8.7 0.0 copy-done.12
  8.7 1.1 %shard_map.141 = (f32[64,128]{1,0:T(8,128)S(1)}, f32[64,128]{1,0:T(8,128)S(1)}, f32[64,128]{1,0:T(8,128)S(1)}, f32[64,128]{1,0:T(8,128)S(1)}, f32[64,128]{1,0:T(...) custom-call(s32[1]{0:T(128)} %bitcast.pos_ref, s32[1,8]{1,0:T(1,128)S(1)} %copy-done.12, ...), custom_call_target="tpu_custom_call" | custom-call | tf_op jit(solution)/shard_map/pallas_call | solution.py:429
  9.8 0.0 collective-permute-done.1.refs_1_
  9.9 2.0 %collective-permute-start.2 = (f32[96,128]{1,0:T(8,128)S(1)}, f32[96,128]{1,0:T(8,128)S(1)}, u32[]{:S(2)}, u32[]{:S(2)}) collective-permute-start(f32[96,128]{1,0:T(8,128)S(1)} %get-tuple-element.32), channel_id=1, source_target_pairs={{0,2},{2,0},{4,6},{6,4},{8,10},{10,8},{12,14},{14,12},{1,3},{3,1},... | collective-permute-start | bytes 147464 | tf_op jit(solution)/shard_map/ppermute | solution.py:446
  11.9 1.6 %collective-permute-start.3 = (f32[96,128]{1,0:T(8,128)S(1)}, f32[96,128]{1,0:T(8,128)S(1)}, u32[]{:S(2)}, u32[]{:S(2)}) collective-permute-start(f32[96,128]{1,0:T(8,128)S(1)} %get-tuple-element.33), channel_id=1, source_target_pairs={{0,4},{2,6},{4,0},{6,2},{8,12},{10,14},{12,8},{14,10},{1,5},{3,7},... | collective-permute-start | bytes 147464 | tf_op jit(solution)/shard_map/ppermute | solution.py:446
  13.5 0.0 collective-permute-start.4
  13.5 3.0 %collective-permute-start.5 = (f32[96,128]{1,0:T(8,128)S(1)}, f32[96,128]{1,0:T(8,128)S(1)}, u32[]{:S(2)}, u32[]{:S(2)}) collective-permute-start(f32[96,128]{1,0:T(8,128)S(1)} %get-tuple-element.35), channel_id=1, source_target_pairs={{0,8},{2,10},{4,12},{6,14},{8,0},{10,2},{12,4},{14,6},{1,9},{3,11}... | collective-permute-start | bytes 147464 | tf_op jit(solution)/shard_map/ppermute | solution.py:446
  16.5 0.0 collective-permute-done.2.refs_1_.refs_9_
  16.5 1.5 %collective-permute-start.6 = (f32[96,128]{1,0:T(8,128)S(1)}, f32[96,128]{1,0:T(8,128)S(1)}, u32[]{:S(2)}, u32[]{:S(2)}) collective-permute-start(f32[96,128]{1,0:T(8,128)S(1)} %get-tuple-element.36), channel_id=1, source_target_pairs={{0,10},{2,8},{4,14},{6,12},{8,2},{10,0},{12,6},{14,4},{1,11},{3,9}... | collective-permute-start | bytes 147464 | tf_op jit(solution)/shard_map/ppermute | solution.py:446
  18.0 0.0 collective-permute-done.3.refs_2_.refs_10_
  18.0 3.3 %collective-permute-start.7 = (f32[96,128]{1,0:T(8,128)S(1)}, f32[96,128]{1,0:T(8,128)S(1)}, u32[]{:S(2)}, u32[]{:S(2)}) collective-permute-start(f32[96,128]{1,0:T(8,128)S(1)} %get-tuple-element.37), channel_id=1, source_target_pairs={{0,12},{2,14},{4,8},{6,10},{8,4},{10,6},{12,0},{14,2},{1,13},{3,15... | collective-permute-start | bytes 147464 | tf_op jit(solution)/shard_map/ppermute | solution.py:446
  21.4 0.0 collective-permute-done.4.refs_3_.refs_11_
  21.4 0.4 %collective-permute-start.8 = (f32[96,128]{1,0:T(8,128)S(1)}, f32[96,128]{1,0:T(8,128)S(1)}, u32[]{:S(2)}, u32[]{:S(2)}) collective-permute-start(f32[96,128]{1,0:T(8,128)S(1)} %get-tuple-element.38), channel_id=1, source_target_pairs={{0,14},{2,12},{4,10},{6,8},{8,6},{10,4},{12,2},{14,0},{1,15},{3,13... | collective-permute-start | bytes 147464 | tf_op jit(solution)/shard_map/ppermute | solution.py:446
  21.8 0.0 collective-permute-done.5.refs_4_.refs_12_
  21.8 2.5 %collective-permute-done.6.refs_5_.refs_13_ = f32[96,128]{1,0:T(8,128)S(1)} collective-permute-done((f32[96,128]{1,0:T(8,128)S(1)}, f32[96,128]{1,0:T(8,128)S(1)}, u32[]{:S(2)}, u32[]{:S(2)}) %collective-permute-start.6) | collective-permute-done | bytes 49184 | tf_op jit(solution)/shard_map/ppermute | solution.py:446
  24.3 0.2 collective-permute-done.7.refs_6_.refs_14_
  24.6 3.6 %collective-permute-done.8.refs_7_.refs_15_ = f32[96,128]{1,0:T(8,128)S(1)} collective-permute-done((f32[96,128]{1,0:T(8,128)S(1)}, f32[96,128]{1,0:T(8,128)S(1)}, u32[]{:S(2)}, u32[]{:S(2)}) %collective-permute-start.8) | collective-permute-done | bytes 49184 | tf_op jit(solution)/shard_map/ppermute | solution.py:446
  28.2 2.3 %shard_map.143 = (f32[16,384]{1,0:T(8,128)S(1)}, bf16[8,32,1024]{2,1,0:T(8,128)(2,1)S(1)}, f32[8,16,128]{2,1,0:T(8,128)S(1)}) custom-call(s32[1]{0:T(128)} %bitcast.pos_ref, f32[16,32]{1,0:T(8,128)S(1)} %copy-done.5, f32[32,128]{1,0:T(8,128)S(1)} %get-tuple-element.31.refs_0_, f32[96,128]{1,0:T(8,128)S(1)} %collective-permute-done.2.refs_1_.refs_9_, ...), custom_call_target="tpu_custom_call" | custom-call | tf_op jit(solution)/shard_map/pallas_call | solution.py:448
  30.4 0.0 collective-permute-start.10
  30.4 1.5 %shard_map.144 = (f32[16,1024]{1,0:T(8,128)}, f32[16,1024]{1,0:T(8,128)}) custom-call(s32[1]{0:T(128)} %bitcast.pos_ref, bf16[8,32,1024]{2,1,0:T(8,128)(2,1)S(1)} %get-tuple-element.40.slots_ref, f32[8,16,128]{2,1,0:T(8,128)S(1)} %get-tuple-element.41.tables_ref, f32[16,1024]{1,0:T(8,128)S(1)} %copy-done.2, f32[1,1024]{1,0:T(1,128)S(1)} %bitcast.5, ...), custom_call_target="tpu_custom_call" | custom-call | tf_op jit(solution)/shard_map/pallas_call | solution.py:453
  31.9 0.0 collective-permute-done.9.other_ref
  31.9 0.0 collective-permute-done.10.theirs_ref
  31.9 0.0 copy-done.1
  32.0 1.5 %shard_map.145 = f32[16,40,256]{2,1,0:T(8,128)} custom-call(s32[1]{0:T(128)} %bitcast.1.lev_ref, bf16[16,40,256]{2,1,0:T(8,128)(2,1)S(1)} %copy-done, bf16[16,40,256]{2,1,0:T(8,128)(2,1)S(1)} %collective-permute-done.9.other_ref, f32[16,40,256]{2,1,0:T(8,128)S(1)} %copy-done.1, f32[16,384]{1,0:T(8,128)S(1)} %get-tuple-element.44.mine_ref, ...), custom_call_target="tpu_custom_call" | custom-call | tf_op jit(solution)/shard_map/pallas_call | solution.py:474
  (7 shorter events, 0.0 us)
Async XLA Ops:
  0.6 3.0 %collective-permute-start = (f32[16,40,256]{2,1,0:T(8,128)}, f32[16,40,256]{2,1,0:T(8,128)S(1)}, u32[]{:S(2)}, u32[]{:S(2)}) collective-permute-start(f32[16,40,256]{2,1,0:T(8,128)} %control_ref.1), channel_id=1, source_target_pairs={{0,1},{1,0},{2,3},{3,2},{4,5},{5,4},{6,7},{7,6},{8,9},{9,8},{10,11... | collective-permute-start | bytes 1966088 | tf_op jit(solution)/shard_map/ppermute | solution.py:414
  1.1 30.8 %collective-permute-start.9 = (bf16[16,40,256]{2,1,0:T(8,128)(2,1)}, bf16[16,40,256]{2,1,0:T(8,128)(2,1)S(1)}, u32[]{:S(2)}, u32[]{:S(2)}) collective-permute-start(bf16[16,40,256]{2,1,0:T(8,128)(2,1)} %perturb_ref.3), channel_id=1, source_target_pairs={{0,1},{1,0},{2,3},{3,2},{4,5},{5,4},{6,7},{7,6},{8,9},{9,8},{10,11... | collective-permute-start | bytes 983048 | tf_op jit(solution)/shard_map/ppermute | solution.py:415
  1.2 2.4 %copy-start = (bf16[16,40,256]{2,1,0:T(8,128)(2,1)S(1)}, bf16[16,40,256]{2,1,0:T(8,128)(2,1)}, u32[]{:S(2)}) copy-start(bf16[16,40,256]{2,1,0:T(8,128)(2,1)} %perturb_ref.3) | copy-start | bytes 983044
  1.2 2.4 %copy-start.5 = (f32[16,32]{1,0:T(8,128)S(1)}, f32[16,32]{1,0:T(8,128)}, u32[]{:S(2)}) copy-start(f32[16,32]{1,0:T(8,128)} %loc_ref.3) | copy-start | bytes 6148
  3.5 4.5 %copy-start.2 = (f32[16,1024]{1,0:T(8,128)S(1)}, f32[16,1024]{1,0:T(8,128)}, u32[]{:S(2)}) copy-start(f32[16,1024]{1,0:T(8,128)} %static_ref.3) | copy-start | bytes 196612
  3.6 4.5 %copy-start.3 = (f32[16,1024]{1,0:T(8,128)S(1)}, f32[16,1024]{1,0:T(8,128)}, u32[]{:S(2)}) copy-start(f32[16,1024]{1,0:T(8,128)} %obs_ref.3) | copy-start | bytes 196612
  3.6 4.5 %copy-start.4 = (f32[16,1024]{1,0:T(8,128)S(1)}, f32[16,1024]{1,0:T(8,128)}, u32[]{:S(2)}) copy-start(f32[16,1024]{1,0:T(8,128)} %innov_ref.3) | copy-start | bytes 196612
  3.6 0.8 %copy-start.6 = (f32[16,256]{1,0:T(8,128)S(1)}, f32[16,256]{1,0:T(8,128)}, u32[]{:S(2)}) copy-start(f32[16,256]{1,0:T(8,128)} %shard_map.139.part_ref) | copy-start | bytes 49156
  4.4 3.7 %copy-start.9 = (s32[1,8,128]{2,1,0:T(8,128)S(1)}, s32[1,8,128]{2,1,0:T(8,128)}, u32[]{:S(2)}) copy-start(s32[1,8,128]{2,1,0:T(8,128)} %src_ref.1) | copy-start | bytes 12292
  4.4 3.7 %copy-start.10 = (f32[1,8,128]{2,1,0:T(8,128)S(1)}, f32[1,8,128]{2,1,0:T(8,128)}, u32[]{:S(2)}) copy-start(f32[1,8,128]{2,1,0:T(8,128)} %weight_ref.1) | copy-start | bytes 12292
  4.4 3.7 %copy-start.11 = (s32[1,8,128]{2,1,0:T(8,128)S(1)}, s32[1,8,128]{2,1,0:T(8,128)}, u32[]{:S(2)}) copy-start(s32[1,8,128]{2,1,0:T(8,128)} %tgt_ref.1) | copy-start | bytes 12292
  5.1 4.8 %collective-permute-start.1 = (f32[16,256]{1,0:T(8,128)S(1)}, f32[16,256]{1,0:T(8,128)S(1)}, u32[]{:S(2)}, u32[]{:S(2)}) collective-permute-start(f32[16,256]{1,0:T(8,128)S(1)} %shard_map.140.refs_0_), channel_id=1, source_target_pairs={{0,16},{16,0},{1,17},{17,1},{2,18},{18,2},{3,19},{19,3},{4,20},{20... | collective-permute-start | bytes 49160 | tf_op jit(solution)/shard_map/ppermute | solution.py:438
  8.0 0.7 %copy-start.8 = (f32[1024]{0:T(1024)S(1)}, f32[1024]{0:T(1024)}, u32[]{:S(2)}) copy-start(f32[1024]{0:T(1024)} %param.17) | copy-start | bytes 12292
  8.0 0.7 %copy-start.7 = (f32[1024]{0:T(1024)S(1)}, f32[1024]{0:T(1024)}, u32[]{:S(2)}) copy-start(f32[1024]{0:T(1024)} %param.16) | copy-start | bytes 12292
  8.0 0.7 %copy-start.12 = (s32[1,8]{1,0:T(1,128)S(1)}, s32[1,8]{1,0:T(1,128)}, u32[]{:S(2)}) copy-start(s32[1,8]{1,0:T(1,128)} %counts_ref.1) | copy-start | bytes 100
  9.9 6.6 %collective-permute-start.2 = (f32[96,128]{1,0:T(8,128)S(1)}, f32[96,128]{1,0:T(8,128)S(1)}, u32[]{:S(2)}, u32[]{:S(2)}) collective-permute-start(f32[96,128]{1,0:T(8,128)S(1)} %get-tuple-element.32), channel_id=1, source_target_pairs={{0,2},{2,0},{4,6},{6,4},{8,10},{10,8},{12,14},{14,12},{1,3},{3,1},... | collective-permute-start | bytes 147464 | tf_op jit(solution)/shard_map/ppermute | solution.py:446
  11.9 6.1 %collective-permute-start.3 = (f32[96,128]{1,0:T(8,128)S(1)}, f32[96,128]{1,0:T(8,128)S(1)}, u32[]{:S(2)}, u32[]{:S(2)}) collective-permute-start(f32[96,128]{1,0:T(8,128)S(1)} %get-tuple-element.33), channel_id=1, source_target_pairs={{0,4},{2,6},{4,0},{6,2},{8,12},{10,14},{12,8},{14,10},{1,5},{3,7},... | collective-permute-start | bytes 147464 | tf_op jit(solution)/shard_map/ppermute | solution.py:446
  13.5 7.9 %collective-permute-start.4 = (f32[96,128]{1,0:T(8,128)S(1)}, f32[96,128]{1,0:T(8,128)S(1)}, u32[]{:S(2)}, u32[]{:S(2)}) collective-permute-start(f32[96,128]{1,0:T(8,128)S(1)} %get-tuple-element.34), channel_id=1, source_target_pairs={{0,6},{2,4},{4,2},{6,0},{8,14},{10,12},{12,10},{14,8},{1,7},{3,5},... | collective-permute-start | bytes 147464 | tf_op jit(solution)/shard_map/ppermute | solution.py:446
  13.5 8.3 %collective-permute-start.5 = (f32[96,128]{1,0:T(8,128)S(1)}, f32[96,128]{1,0:T(8,128)S(1)}, u32[]{:S(2)}, u32[]{:S(2)}) collective-permute-start(f32[96,128]{1,0:T(8,128)S(1)} %get-tuple-element.35), channel_id=1, source_target_pairs={{0,8},{2,10},{4,12},{6,14},{8,0},{10,2},{12,4},{14,6},{1,9},{3,11}... | collective-permute-start | bytes 147464 | tf_op jit(solution)/shard_map/ppermute | solution.py:446
  16.5 7.9 %collective-permute-start.6 = (f32[96,128]{1,0:T(8,128)S(1)}, f32[96,128]{1,0:T(8,128)S(1)}, u32[]{:S(2)}, u32[]{:S(2)}) collective-permute-start(f32[96,128]{1,0:T(8,128)S(1)} %get-tuple-element.36), channel_id=1, source_target_pairs={{0,10},{2,8},{4,14},{6,12},{8,2},{10,0},{12,6},{14,4},{1,11},{3,9}... | collective-permute-start | bytes 147464 | tf_op jit(solution)/shard_map/ppermute | solution.py:446
  18.0 6.6 %collective-permute-start.7 = (f32[96,128]{1,0:T(8,128)S(1)}, f32[96,128]{1,0:T(8,128)S(1)}, u32[]{:S(2)}, u32[]{:S(2)}) collective-permute-start(f32[96,128]{1,0:T(8,128)S(1)} %get-tuple-element.37), channel_id=1, source_target_pairs={{0,12},{2,14},{4,8},{6,10},{8,4},{10,6},{12,0},{14,2},{1,13},{3,15... | collective-permute-start | bytes 147464 | tf_op jit(solution)/shard_map/ppermute | solution.py:446
  21.4 6.8 %collective-permute-start.8 = (f32[96,128]{1,0:T(8,128)S(1)}, f32[96,128]{1,0:T(8,128)S(1)}, u32[]{:S(2)}, u32[]{:S(2)}) collective-permute-start(f32[96,128]{1,0:T(8,128)S(1)} %get-tuple-element.38), channel_id=1, source_target_pairs={{0,14},{2,12},{4,10},{6,8},{8,6},{10,4},{12,2},{14,0},{1,15},{3,13... | collective-permute-start | bytes 147464 | tf_op jit(solution)/shard_map/ppermute | solution.py:446
  28.2 3.8 %copy-start.1 = (f32[16,40,256]{2,1,0:T(8,128)S(1)}, f32[16,40,256]{2,1,0:T(8,128)}, u32[]{:S(2)}) copy-start(f32[16,40,256]{2,1,0:T(8,128)} %control_ref.1) | copy-start | bytes 1966084
  30.4 1.5 %collective-permute-start.10 = (f32[16,384]{1,0:T(8,128)S(1)}, f32[16,384]{1,0:T(8,128)S(1)}, u32[]{:S(2)}, u32[]{:S(2)}) collective-permute-start(f32[16,384]{1,0:T(8,128)S(1)} %get-tuple-element.44.mine_ref), channel_id=1, source_target_pairs={{0,1},{1,0},{2,3},{3,2},{4,5},{5,4},{6,7},{7,6},{8,9},{9,8},{10,11... | collective-permute-start | bytes 73736 | tf_op jit(solution)/shard_map/ppermute | solution.py:473

commit v5 on v4

--- a/solution.py
+++ b/solution.py
@@ -222,11 +222,11 @@
         self.weight = slice(0, levels)
         self.base = slice(levels, 2 * levels)
         at = 2 * levels
-        self.src, self.factor, self.tgt, self.edge = at, at + n, at + 2 * n, at + 3 * n
-        self.total = at + 3 * n + EXTRA
-
-
-def static_kernel(pos_ref, counts_ref, static_ref, diag_ref, off_ref, obs_ref, innov_ref, src_ref, weight_ref, tgt_ref,
+        self.factor, self.index, self.edge = at, at + n, at + 2 * n
+        self.total = at + 2 * n + EXTRA
+
+
+def static_kernel(band, pos_ref, counts_ref, static_ref, diag_ref, off_ref, obs_ref, innov_ref, src_ref, weight_ref, tgt_ref,
                   *out_refs):
     levels, cols = static_ref.shape
     n = len(out_refs)
@@ -248,14 +248,13 @@
     both = jnp.concatenate(halves(jnp.concatenate([obs, base], axis=0)), axis=0)
     tgts = [tgt_ref[0, pl.ds(me ^ r, 1), :] for r in range(n)]
     src = jnp.concatenate([src_ref[0, pl.ds(me ^ r, 1), :] for r in range(n)], axis=0).astype(F32)
-    tgt = jnp.concatenate(tgts, axis=0).astype(F32)
+    index = jnp.concatenate(tgts, axis=0).astype(F32) * float(band) + src
     factor = jnp.concatenate([factor_of(counts_ref, weight_ref, me ^ r) for r in range(n)], axis=0)
     for r, out_ref in enumerate(out_refs):
         picked = product(both, one_hot(tgts[r], cols))
         out_ref[: 2 * levels, :] = picked[: 2 * levels] + picked[2 * levels :]
-        out_ref[rows.src : rows.src + n, :] = src
         out_ref[rows.factor : rows.factor + n, :] = factor
-        out_ref[rows.tgt : rows.tgt + n, :] = tgt
+        out_ref[rows.index : rows.index + n, :] = index
         out_ref[rows.edge :, :] = edge
 
 
@@ -280,9 +279,12 @@
         out_ref[total.shape[0] :, :] = rest_ref[...]
 
 
-def shared_kernel(n, levels, cols, pos_ref, loc_ref, *refs):
-    sums_refs, rest_refs = refs[:n], refs[n : 2 * n]
-    out_ref, slots_ref, tables_ref = refs[2 * n :]
+def shared_kernel(order, levels, cols, pos_ref, loc_ref, total_ref, rest_ref, *refs):
+    n = len(order) + 1
+    blocks = dict(zip(order, refs))
+    sums_refs = [total_ref] + [blocks[r] for r in range(1, n)]
+    rest_refs = [rest_ref] + [blocks[r] for r in range(1, n)]
+    out_ref, slots_ref, tables_ref = refs[n - 1 :]
     cap = slots_ref.shape[2] // n
     band = out_ref.shape[1] - 128
     rows = Rows(levels, n)
@@ -297,12 +299,17 @@
         return rest(r, at, 1)
 
     column = lax.broadcasted_iota(jnp.int32, (band, cap), 0).astype(F32)
+    src, tgt = [], []
+    for r in range(n):
+        words = rest(r, rows.index, n)
+        tgt.append(jnp.floor((words + 0.5) * (1.0 / band)))
+        src.append(words - tgt[r] * float(band))
+        tables_ref[me ^ r, :n, :] = tgt[r]
+        tables_ref[me ^ r, n:, :] = rest(r, rows.edge, EXTRA)
 
     def chosen(s, d):
-        return jnp.where(column == row(s, rows.src + (s ^ d)), 1.0, 0.0).astype(BF16)
-
-    for r in range(n):
-        tables_ref[me ^ r] = rest(r, rows.tgt, n + EXTRA)
+        return jnp.where(column == src[s][s ^ d : (s ^ d) + 1], 1.0, 0.0).astype(BF16)
+
     for s in range(n):
         sums = jnp.concatenate([sums_refs[s][i * levels : (i + 1) * levels, :] for i in range(parts)], axis=1)
         both = jnp.concatenate(halves(sums), axis=0)
@@ -310,13 +317,13 @@
             picked = product(both, chosen(s, d))
             values = (picked[:levels] + picked[levels:]) * row(s, rows.factor + (s ^ d))
             slots_ref[d, :, s * cap : (s + 1) * cap] = jnp.concatenate(halves(values), axis=0)
-    own = jnp.concatenate([row(d, rows.tgt + d) for d in range(n)], axis=0)
+    own = jnp.concatenate([tgt[d][d : d + 1] for d in range(n)], axis=0)
     turned = own.T
     last = cols - 1.0
     total = jnp.zeros((levels, band), F32)
     for d in range(n):
         same = [
-            jnp.where(turned[:, d : d + 1] == row(d, rows.tgt + (s ^ d)), 1.0, 0.0).astype(BF16) for s in range(n)
+            jnp.where(turned[:, d : d + 1] == tgt[d][s ^ d : (s ^ d) + 1], 1.0, 0.0).astype(BF16) for s in range(n)
         ]
         met = product(slots_ref[d], jnp.concatenate(same, axis=1), ((1,), (1,)))
         value = met[:levels] + met[levels:] + rest(d, levels, levels)
@@ -423,10 +430,10 @@
     flat = shape((levels, tile_cols), F32)
     mine_shape = shape((levels, band_cols + 128), F32)
     diag, off = filter_diag.reshape(1, -1), filter_off.reshape(1, -1)
-    if n * cap <= tile_cols and n & (n - 1) == 0:
+    if n * cap <= tile_cols and n & (n - 1) == 0 and band_cols * tile_cols <= 2**20:
         rows = Rows(levels, n)
         stacked = band_cols // cap * levels
-        rests = call(static_kernel, [shape((rows.total, cap), F32)] * n, [SMEM] * 2 + [VMEM] * 8)(
+        rests = call(functools.partial(static_kernel, band_cols), [shape((rows.total, cap), F32)] * n, [SMEM] * 2 + [VMEM] * 8)(
             pos, counts, static_control, diag, off, obs_weight, innovation, send_src, send_wt, recv_tgt
         )
         sums = [
@@ -434,6 +441,7 @@
                 lev, perturb, other_control, part, level_loc
             )
         ]
+        sums[0], other_perturb = lax.optimization_barrier((sums[0], other_perturb))
         for k in range(1, groups):
             sums.append(lax.ppermute(sums[0], "grp", [(g, (g + k) % groups) for g in range(groups)]))
         total, *blocks = call(
@@ -441,15 +449,13 @@
             [shape((stacked, cap), F32)] + [shape((stacked + rows.total, cap), F32)] * (n - 1),
             [VMEM] * (groups + n - 1),
         )(*sums, *rests[1:])
-        arrived = {}
-        for r in reversed(range(1, n)):
-            arrived[r] = lax.ppermute(blocks[r - 1], "tile", [(i, i ^ r) for i in range(n)])
-        arrived = [arrived[r] for r in range(1, n)]
+        order = [*range(n // 2, n), *range(1, n // 2)]
+        arrived = [lax.ppermute(blocks[r - 1], "tile", [(i, i ^ r) for i in range(n)]) for r in order]
         mine, slots, tables = call(
-            functools.partial(shared_kernel, n, levels, tile_cols),
+            functools.partial(shared_kernel, order, levels, tile_cols),
             (mine_shape, shape((n, 2 * levels, n * cap), BF16), shape((n, n + EXTRA, cap), F32)),
-            [SMEM] + [VMEM] * (2 * n + 1),
-        )(pos, level_loc, total, *arrived, rests[0], *arrived)
+            [SMEM] + [VMEM] * (n + 2),
+        )(pos, level_loc, total, rests[0], *arrived)
         increment, grad_static = call(outputs_kernel, (flat, flat), [SMEM] + [VMEM] * 7)(
             pos, slots, tables, static_control, diag, off, obs_weight, innovation
         )

time: 33.8 us -> 31.1 us (0.920)
  waiting for transfers between devices: 6.38 us -> 4.93 us
  starting transfers between devices: 15.5 us -> 14.2 us
    ppermute x7, waiting for transfers between devices: 6.37 us -> 4.92 us  [body(): lax.ppermute(blocks[r - 1], 'tile', [(i, i ^ r) for i in range(n)])]
    ppermute x7, starting transfers between devices: 11.9 us -> 10.6 us  [body(): lax.ppermute(blocks[r - 1], 'tile', [(i, i ^ r) for i in range(n)])]
  transfers between devices with their start and end apart: 11 -> 11, of which waited for: 3 -> 3; matrix products, arithmetic and copies ran while one was open for 0% -> 0% of each run, Pallas kernels for 24% -> 18%
where the time goes in v5:
time: 31.1 us; the launch traced here: 30.8 us
  starting transfers between devices  14.2 us (46%)
  Pallas kernels  9.42 us (30%)
  waiting for transfers between devices  4.93 us (16%)
  local copies, waits for them, and re-layouts  1.44 us (5%)
  between operations  0.8 us (3%)
    ppermute x7, starting transfers between devices, body(): lax.ppermute(blocks[r - 1], 'tile', [(i, i ^ r) for i in range(n)])  10.6 us
    ppermute x7, waiting for transfers between devices, body(): lax.ppermute(blocks[r - 1], 'tile', [(i, i ^ r) for i in range(n)])  4.92 us
    ppermute x1, starting transfers between devices, body(): lax.ppermute(sums[0], 'grp', [(g, (g + k) % groups) for g in range(groups)])  2.97 us
    pallas_call x1, Pallas kernels, body(): call(own_kernel, shape((levels, band_cols), F32), [SMEM] + [HBM] * 3, [pl...  2.3 us
    pallas_call x1, Pallas kernels, body(): call(functools.partial(shared_kernel, order, levels, tile_cols), (mine_sh...  2.27 us
    pallas_call x1, Pallas kernels, body(): call(outputs_kernel, (flat, flat), [SMEM] + [VMEM] * 7)  1.53 us
    pallas_call x1, Pallas kernels, body(): call(ens_kernel, shape(control.shape, F32), [SMEM] + [VMEM] * 5)  1.52 us
    unnamed x26, local copies, waits for them, and re-layouts  1.44 us
  transfers between devices with their start and end apart: 11, of which 3 were waited for; matrix products, arithmetic and copies ran while one was open for 0% of the time, Pallas kernels for 18%

profile of v5, /device:TPU:0, one launch (start us, length us, event | category | flops | bytes accessed | tf_op | source)
XLA Modules:
  0.0 30.8 jit_solution(1758986027535905135)
XLA Ops:
  0.6 0.5 %collective-permute-start = (f32[16,40,256]{2,1,0:T(8,128)}, f32[16,40,256]{2,1,0:T(8,128)S(1)}, u32[]{:S(2)}, u32[]{:S(2)}) collective-permute-start(f32[16,40,256]{2,1,0:T(8,128)} %control_ref.1), channel_id=1, source_target_pairs={{0,1},{1,0},{2,3},{3,2},{4,5},{5,4},{6,7},{7,6},{8,9},{9,8},{10,11... | collective-permute-start | bytes 1966088 | tf_op jit(solution)/shard_map/ppermute | solution.py:421
  1.1 0.1 collective-permute-start.1
  1.2 0.0 copy-start
  1.2 0.0 copy-start.5
  1.2 2.3 %shard_map.139.part_ref = f32[16,256]{1,0:T(8,128)} custom-call(s32[1]{0:T(128)} %bitcast.1.lev_ref, bf16[16,40,256]{2,1,0:T(8,128)(2,1)} %perturb_ref.3, f32[16,40,256]{2,1,0:T(8,128)} %control_ref.1, f32[16,32]{1,0:T(8,128)} %loc_ref.3), custom_call_target="tpu_custom_call" | custom-call | tf_op jit(solution)/shard_map/pallas_call | solution.py:423
  3.5 0.0 copy-start.2
  3.6 0.0 copy-start.3
  3.6 0.0 copy-start.4
  3.6 0.0 collective-permute-done.other_ref
  3.6 0.0 copy-done
  3.6 0.0 copy-done.5
  3.6 0.0 copy-start.6
  3.6 0.7 %copy-done.6 = f32[16,256]{1,0:T(8,128)S(1)} copy-done((f32[16,256]{1,0:T(8,128)S(1)}, f32[16,256]{1,0:T(8,128)}, u32[]{:S(2)}) %copy-start.6) | copy-done | bytes 16408
  4.4 0.7 %shard_map.140.refs_0_ = f32[16,256]{1,0:T(8,128)S(1)} custom-call(s32[1]{0:T(128)} %bitcast.1.lev_ref, bf16[16,40,256]{2,1,0:T(8,128)(2,1)S(1)} %copy-done, f32[16,40,256]{2,1,0:T(8,128)S(1)} %collective-permute-done.other_ref, f32[16,256]{1,0:T(8,128)S(1)} %copy-done.6, f32[16,32]{1,0:T(8,128)S(1)} %copy-done.5), custom_call_target="tpu_custom_call" | custom-call | tf_op jit(solution)/shard_map/pallas_call | solution.py:440
  5.1 0.0 collective-permute-done.1.other_ref
  5.1 3.0 %collective-permute-start.2 = (f32[16,256]{1,0:T(8,128)S(1)}, f32[16,256]{1,0:T(8,128)S(1)}, u32[]{:S(2)}, u32[]{:S(2)}) collective-permute-start(f32[16,256]{1,0:T(8,128)S(1)} %shard_map.140.refs_0_), channel_id=1, source_target_pairs={{0,16},{16,0},{1,17},{17,1},{2,18},{18,2},{3,19},{19,3},{4,20},{20... | collective-permute-start | bytes 49160 | tf_op jit(solution)/shard_map/ppermute | solution.py:446
  8.0 0.0 copy-done.2
  8.0 0.0 copy-done.3
  8.1 0.0 copy-done.4
  8.1 0.0 copy-done.9
  8.1 0.0 copy-done.10
  8.1 0.0 copy-done.11
  8.1 0.6 %copy-done.8 = f32[1024]{0:T(1024)S(1)} copy-done((f32[1024]{0:T(1024)S(1)}, f32[1024]{0:T(1024)}, u32[]{:S(2)}) %copy-start.8) | copy-done | bytes 4120
  8.7 0.0 copy-done.7
  8.7 0.0 copy-done.12
  8.7 1.1 %shard_map.141 = (f32[56,128]{1,0:T(8,128)S(1)}, f32[56,128]{1,0:T(8,128)S(1)}, f32[56,128]{1,0:T(8,128)S(1)}, f32[56,128]{1,0:T(8,128)S(1)}, f32[56,128]{1,0:T(...) custom-call(s32[1]{0:T(128)} %bitcast.pos_ref, s32[1,8]{1,0:T(1,128)S(1)} %copy-done.12, ...), custom_call_target="tpu_custom_call" | custom-call | tf_op jit(solution)/shard_map/pallas_call | solution.py:436
  9.8 0.0 collective-permute-done.2.refs_1_
  9.9 0.0 copy-start.1
  9.9 3.1 %collective-permute-start.3 = (f32[88,128]{1,0:T(8,128)S(1)}, f32[88,128]{1,0:T(8,128)S(1)}, u32[]{:S(2)}, u32[]{:S(2)}) collective-permute-start(f32[88,128]{1,0:T(8,128)S(1)} %get-tuple-element.36), channel_id=1, source_target_pairs={{0,8},{2,10},{4,12},{6,14},{8,0},{10,2},{12,4},{14,6},{1,9},{3,11}... | collective-permute-start | bytes 135176 | tf_op jit(solution)/shard_map/ppermute | solution.py:453
  13.0 1.3 %collective-permute-start.4 = (f32[88,128]{1,0:T(8,128)S(1)}, f32[88,128]{1,0:T(8,128)S(1)}, u32[]{:S(2)}, u32[]{:S(2)}) collective-permute-start(f32[88,128]{1,0:T(8,128)S(1)} %get-tuple-element.37), channel_id=1, source_target_pairs={{0,10},{2,8},{4,14},{6,12},{8,2},{10,0},{12,6},{14,4},{1,11},{3,9}... | collective-permute-start | bytes 135176 | tf_op jit(solution)/shard_map/ppermute | solution.py:453
  14.3 3.6 %collective-permute-start.5 = (f32[88,128]{1,0:T(8,128)S(1)}, f32[88,128]{1,0:T(8,128)S(1)}, u32[]{:S(2)}, u32[]{:S(2)}) collective-permute-start(f32[88,128]{1,0:T(8,128)S(1)} %get-tuple-element.38), channel_id=1, source_target_pairs={{0,12},{2,14},{4,8},{6,10},{8,4},{10,6},{12,0},{14,2},{1,13},{3,15... | collective-permute-start | bytes 135176 | tf_op jit(solution)/shard_map/ppermute | solution.py:453
  17.9 0.0 collective-permute-start.6
  17.9 1.7 %collective-permute-start.7 = (f32[88,128]{1,0:T(8,128)S(1)}, f32[88,128]{1,0:T(8,128)S(1)}, u32[]{:S(2)}, u32[]{:S(2)}) collective-permute-start(f32[88,128]{1,0:T(8,128)S(1)} %get-tuple-element.40), channel_id=1, source_target_pairs={{0,2},{2,0},{4,6},{6,4},{8,10},{10,8},{12,14},{14,12},{1,3},{3,1},... | collective-permute-start | bytes 135176 | tf_op jit(solution)/shard_map/ppermute | solution.py:453
  19.6 0.0 collective-permute-done.3.refs_0_
  19.6 0.0 collective-permute-start.8
  19.6 0.9 %collective-permute-done.4.refs_1_ = f32[88,128]{1,0:T(8,128)S(1)} collective-permute-done((f32[88,128]{1,0:T(8,128)S(1)}, f32[88,128]{1,0:T(8,128)S(1)}, u32[]{:S(2)}, u32[]{:S(2)}) %collective-permute-start.4) | collective-permute-done | bytes 45088 | tf_op jit(solution)/shard_map/ppermute | solution.py:453
  20.5 1.0 %collective-permute-start.9 = (f32[88,128]{1,0:T(8,128)S(1)}, f32[88,128]{1,0:T(8,128)S(1)}, u32[]{:S(2)}, u32[]{:S(2)}) collective-permute-start(f32[88,128]{1,0:T(8,128)S(1)} %get-tuple-element.42), channel_id=1, source_target_pairs={{0,6},{2,4},{4,2},{6,0},{8,14},{10,12},{12,10},{14,8},{1,7},{3,5},... | collective-permute-start | bytes 135176 | tf_op jit(solution)/shard_map/ppermute | solution.py:453
  21.5 0.0 collective-permute-done.5.refs_2_
  21.5 3.4 %collective-permute-done.6.refs_3_ = f32[88,128]{1,0:T(8,128)S(1)} collective-permute-done((f32[88,128]{1,0:T(8,128)S(1)}, f32[88,128]{1,0:T(8,128)S(1)}, u32[]{:S(2)}, u32[]{:S(2)}) %collective-permute-start.6) | collective-permute-done | bytes 45088 | tf_op jit(solution)/shard_map/ppermute | solution.py:453
  24.9 0.0 collective-permute-done.7.refs_4_
  24.9 0.0 collective-permute-done.8.refs_5_
  24.9 0.6 %collective-permute-done.9.refs_6_ = f32[88,128]{1,0:T(8,128)S(1)} collective-permute-done((f32[88,128]{1,0:T(8,128)S(1)}, f32[88,128]{1,0:T(8,128)S(1)}, u32[]{:S(2)}, u32[]{:S(2)}) %collective-permute-start.9) | collective-permute-done | bytes 45088 | tf_op jit(solution)/shard_map/ppermute | solution.py:453
  25.4 2.3 %shard_map.143 = (f32[16,384]{1,0:T(8,128)S(1)}, bf16[8,32,1024]{2,1,0:T(8,128)(2,1)S(1)}, f32[8,16,128]{2,1,0:T(8,128)S(1)}) custom-call(s32[1]{0:T(128)} %bitcast.pos_ref, f32[16,32]{1,0:T(8,128)S(1)} %copy-done.5, f32[32,128]{1,0:T(8,128)S(1)} %get-tuple-element.34.total_ref, f32[56,128]{1,0:T(8,128)S(1)} %get-tuple-element.35.rest_ref, ...), custom_call_target="tpu_custom_call" | custom-call | tf_op jit(solution)/shard_map/pallas_call | solution.py:454
  27.7 0.0 collective-permute-start.10
  27.7 1.5 %shard_map.144 = (f32[16,1024]{1,0:T(8,128)}, f32[16,1024]{1,0:T(8,128)}) custom-call(s32[1]{0:T(128)} %bitcast.pos_ref, bf16[8,32,1024]{2,1,0:T(8,128)(2,1)S(1)} %get-tuple-element.43.slots_ref, f32[8,16,128]{2,1,0:T(8,128)S(1)} %get-tuple-element.44.tables_ref, f32[16,1024]{1,0:T(8,128)S(1)} %copy-done.2, f32[1,1024]{1,0:T(1,128)S(1)} %bitcast.5, ...), custom_call_target="tpu_custom_call" | custom-call | tf_op jit(solution)/shard_map/pallas_call | solution.py:459
  29.2 0.0 collective-permute-done.10.theirs_ref
  29.3 0.0 copy-done.1
  29.3 1.5 %shard_map.145 = f32[16,40,256]{2,1,0:T(8,128)} custom-call(s32[1]{0:T(128)} %bitcast.1.lev_ref, bf16[16,40,256]{2,1,0:T(8,128)(2,1)S(1)} %copy-done, bf16[16,40,256]{2,1,0:T(8,128)(2,1)S(1)} %collective-permute-done.1.other_ref, f32[16,40,256]{2,1,0:T(8,128)S(1)} %copy-done.1, f32[16,384]{1,0:T(8,128)S(1)} %get-tuple-element.48.mine_ref, ...), custom_call_target="tpu_custom_call" | custom-call | tf_op jit(solution)/shard_map/pallas_call | solution.py:480
  (7 shorter events, 0.0 us)
Async XLA Ops:
  0.6 3.0 %collective-permute-start = (f32[16,40,256]{2,1,0:T(8,128)}, f32[16,40,256]{2,1,0:T(8,128)S(1)}, u32[]{:S(2)}, u32[]{:S(2)}) collective-permute-start(f32[16,40,256]{2,1,0:T(8,128)} %control_ref.1), channel_id=1, source_target_pairs={{0,1},{1,0},{2,3},{3,2},{4,5},{5,4},{6,7},{7,6},{8,9},{9,8},{10,11... | collective-permute-start | bytes 1966088 | tf_op jit(solution)/shard_map/ppermute | solution.py:421
  1.1 3.9 %collective-permute-start.1 = (bf16[16,40,256]{2,1,0:T(8,128)(2,1)}, bf16[16,40,256]{2,1,0:T(8,128)(2,1)S(1)}, u32[]{:S(2)}, u32[]{:S(2)}) collective-permute-start(bf16[16,40,256]{2,1,0:T(8,128)(2,1)} %perturb_ref.3), channel_id=1, source_target_pairs={{0,1},{1,0},{2,3},{3,2},{4,5},{5,4},{6,7},{7,6},{8,9},{9,8},{10,11... | collective-permute-start | bytes 983048 | tf_op jit(solution)/shard_map/ppermute | solution.py:422
  1.2 2.4 %copy-start = (bf16[16,40,256]{2,1,0:T(8,128)(2,1)S(1)}, bf16[16,40,256]{2,1,0:T(8,128)(2,1)}, u32[]{:S(2)}) copy-start(bf16[16,40,256]{2,1,0:T(8,128)(2,1)} %perturb_ref.3) | copy-start | bytes 983044
  1.2 2.4 %copy-start.5 = (f32[16,32]{1,0:T(8,128)S(1)}, f32[16,32]{1,0:T(8,128)}, u32[]{:S(2)}) copy-start(f32[16,32]{1,0:T(8,128)} %loc_ref.3) | copy-start | bytes 6148
  3.5 4.5 %copy-start.2 = (f32[16,1024]{1,0:T(8,128)S(1)}, f32[16,1024]{1,0:T(8,128)}, u32[]{:S(2)}) copy-start(f32[16,1024]{1,0:T(8,128)} %static_ref.3) | copy-start | bytes 196612
  3.6 4.5 %copy-start.3 = (f32[16,1024]{1,0:T(8,128)S(1)}, f32[16,1024]{1,0:T(8,128)}, u32[]{:S(2)}) copy-start(f32[16,1024]{1,0:T(8,128)} %obs_ref.3) | copy-start | bytes 196612
  3.6 4.5 %copy-start.4 = (f32[16,1024]{1,0:T(8,128)S(1)}, f32[16,1024]{1,0:T(8,128)}, u32[]{:S(2)}) copy-start(f32[16,1024]{1,0:T(8,128)} %innov_ref.3) | copy-start | bytes 196612
  3.6 0.8 %copy-start.6 = (f32[16,256]{1,0:T(8,128)S(1)}, f32[16,256]{1,0:T(8,128)}, u32[]{:S(2)}) copy-start(f32[16,256]{1,0:T(8,128)} %shard_map.139.part_ref) | copy-start | bytes 49156
  4.4 3.7 %copy-start.9 = (s32[1,8,128]{2,1,0:T(8,128)S(1)}, s32[1,8,128]{2,1,0:T(8,128)}, u32[]{:S(2)}) copy-start(s32[1,8,128]{2,1,0:T(8,128)} %src_ref.1) | copy-start | bytes 12292
  4.4 3.7 %copy-start.10 = (f32[1,8,128]{2,1,0:T(8,128)S(1)}, f32[1,8,128]{2,1,0:T(8,128)}, u32[]{:S(2)}) copy-start(f32[1,8,128]{2,1,0:T(8,128)} %weight_ref.1) | copy-start | bytes 12292
  4.4 3.7 %copy-start.11 = (s32[1,8,128]{2,1,0:T(8,128)S(1)}, s32[1,8,128]{2,1,0:T(8,128)}, u32[]{:S(2)}) copy-start(s32[1,8,128]{2,1,0:T(8,128)} %tgt_ref.1) | copy-start | bytes 12292
  5.1 4.8 %collective-permute-start.2 = (f32[16,256]{1,0:T(8,128)S(1)}, f32[16,256]{1,0:T(8,128)S(1)}, u32[]{:S(2)}, u32[]{:S(2)}) collective-permute-start(f32[16,256]{1,0:T(8,128)S(1)} %shard_map.140.refs_0_), channel_id=1, source_target_pairs={{0,16},{16,0},{1,17},{17,1},{2,18},{18,2},{3,19},{19,3},{4,20},{20... | collective-permute-start | bytes 49160 | tf_op jit(solution)/shard_map/ppermute | solution.py:446
  8.0 0.7 %copy-start.8 = (f32[1024]{0:T(1024)S(1)}, f32[1024]{0:T(1024)}, u32[]{:S(2)}) copy-start(f32[1024]{0:T(1024)} %param.17) | copy-start | bytes 12292
  8.0 0.7 %copy-start.7 = (f32[1024]{0:T(1024)S(1)}, f32[1024]{0:T(1024)}, u32[]{:S(2)}) copy-start(f32[1024]{0:T(1024)} %param.16) | copy-start | bytes 12292
  8.0 0.7 %copy-start.12 = (s32[1,8]{1,0:T(1,128)S(1)}, s32[1,8]{1,0:T(1,128)}, u32[]{:S(2)}) copy-start(s32[1,8]{1,0:T(1,128)} %counts_ref.1) | copy-start | bytes 100
  9.9 19.4 %copy-start.1 = (f32[16,40,256]{2,1,0:T(8,128)S(1)}, f32[16,40,256]{2,1,0:T(8,128)}, u32[]{:S(2)}) copy-start(f32[16,40,256]{2,1,0:T(8,128)} %control_ref.1) | copy-start | bytes 1966084
  9.9 9.7 %collective-permute-start.3 = (f32[88,128]{1,0:T(8,128)S(1)}, f32[88,128]{1,0:T(8,128)S(1)}, u32[]{:S(2)}, u32[]{:S(2)}) collective-permute-start(f32[88,128]{1,0:T(8,128)S(1)} %get-tuple-element.36), channel_id=1, source_target_pairs={{0,8},{2,10},{4,12},{6,14},{8,0},{10,2},{12,4},{14,6},{1,9},{3,11}... | collective-permute-start | bytes 135176 | tf_op jit(solution)/shard_map/ppermute | solution.py:453
  13.0 7.5 %collective-permute-start.4 = (f32[88,128]{1,0:T(8,128)S(1)}, f32[88,128]{1,0:T(8,128)S(1)}, u32[]{:S(2)}, u32[]{:S(2)}) collective-permute-start(f32[88,128]{1,0:T(8,128)S(1)} %get-tuple-element.37), channel_id=1, source_target_pairs={{0,10},{2,8},{4,14},{6,12},{8,2},{10,0},{12,6},{14,4},{1,11},{3,9}... | collective-permute-start | bytes 135176 | tf_op jit(solution)/shard_map/ppermute | solution.py:453
  14.3 7.2 %collective-permute-start.5 = (f32[88,128]{1,0:T(8,128)S(1)}, f32[88,128]{1,0:T(8,128)S(1)}, u32[]{:S(2)}, u32[]{:S(2)}) collective-permute-start(f32[88,128]{1,0:T(8,128)S(1)} %get-tuple-element.38), channel_id=1, source_target_pairs={{0,12},{2,14},{4,8},{6,10},{8,4},{10,6},{12,0},{14,2},{1,13},{3,15... | collective-permute-start | bytes 135176 | tf_op jit(solution)/shard_map/ppermute | solution.py:453
  17.9 7.0 %collective-permute-start.6 = (f32[88,128]{1,0:T(8,128)S(1)}, f32[88,128]{1,0:T(8,128)S(1)}, u32[]{:S(2)}, u32[]{:S(2)}) collective-permute-start(f32[88,128]{1,0:T(8,128)S(1)} %get-tuple-element.39), channel_id=1, source_target_pairs={{0,14},{2,12},{4,10},{6,8},{8,6},{10,4},{12,2},{14,0},{1,15},{3,13... | collective-permute-start | bytes 135176 | tf_op jit(solution)/shard_map/ppermute | solution.py:453
  17.9 7.0 %collective-permute-start.7 = (f32[88,128]{1,0:T(8,128)S(1)}, f32[88,128]{1,0:T(8,128)S(1)}, u32[]{:S(2)}, u32[]{:S(2)}) collective-permute-start(f32[88,128]{1,0:T(8,128)S(1)} %get-tuple-element.40), channel_id=1, source_target_pairs={{0,2},{2,0},{4,6},{6,4},{8,10},{10,8},{12,14},{14,12},{1,3},{3,1},... | collective-permute-start | bytes 135176 | tf_op jit(solution)/shard_map/ppermute | solution.py:453
  19.6 5.3 %collective-permute-start.8 = (f32[88,128]{1,0:T(8,128)S(1)}, f32[88,128]{1,0:T(8,128)S(1)}, u32[]{:S(2)}, u32[]{:S(2)}) collective-permute-start(f32[88,128]{1,0:T(8,128)S(1)} %get-tuple-element.41), channel_id=1, source_target_pairs={{0,4},{2,6},{4,0},{6,2},{8,12},{10,14},{12,8},{14,10},{1,5},{3,7},... | collective-permute-start | bytes 135176 | tf_op jit(solution)/shard_map/ppermute | solution.py:453
  20.5 4.9 %collective-permute-start.9 = (f32[88,128]{1,0:T(8,128)S(1)}, f32[88,128]{1,0:T(8,128)S(1)}, u32[]{:S(2)}, u32[]{:S(2)}) collective-permute-start(f32[88,128]{1,0:T(8,128)S(1)} %get-tuple-element.42), channel_id=1, source_target_pairs={{0,6},{2,4},{4,2},{6,0},{8,14},{10,12},{12,10},{14,8},{1,7},{3,5},... | collective-permute-start | bytes 135176 | tf_op jit(solution)/shard_map/ppermute | solution.py:453
  27.7 1.5 %collective-permute-start.10 = (f32[16,384]{1,0:T(8,128)S(1)}, f32[16,384]{1,0:T(8,128)S(1)}, u32[]{:S(2)}, u32[]{:S(2)}) collective-permute-start(f32[16,384]{1,0:T(8,128)S(1)} %get-tuple-element.48.mine_ref), channel_id=1, source_target_pairs={{0,1},{1,0},{2,3},{3,2},{4,5},{5,4},{6,7},{7,6},{8,9},{9,8},{10,11... | collective-permute-start | bytes 73736 | tf_op jit(solution)/shard_map/ppermute | solution.py:479

commit v6 on v5

--- a/solution.py
+++ b/solution.py
@@ -279,70 +279,98 @@
         out_ref[total.shape[0] :, :] = rest_ref[...]
 
 
-def shared_kernel(order, levels, cols, pos_ref, loc_ref, total_ref, rest_ref, *refs):
-    n = len(order) + 1
-    blocks = dict(zip(order, refs))
-    sums_refs = [total_ref] + [blocks[r] for r in range(1, n)]
-    rest_refs = [rest_ref] + [blocks[r] for r in range(1, n)]
-    out_ref, slots_ref, tables_ref = refs[n - 1 :]
-    cap = slots_ref.shape[2] // n
-    band = out_ref.shape[1] - 128
-    rows = Rows(levels, n)
-    parts = band // cap
+class Block:
+    def __init__(self, refs, n, levels, band):
+        cap = refs[0].shape[1]
+        self.levels, self.parts, self.cap = levels, band // cap, cap
+        self.sums_ref, self.rest_ref = refs[0], refs[-1]
+        self.head = 0 if len(refs) == 2 else self.parts * levels
+        self.rows = Rows(levels, n)
+        words = self.rest(self.rows.index, n)
+        self.tgt = jnp.floor((words + 0.5) * (1.0 / band))
+        self.src = words - self.tgt * float(band)
+        self.factor = self.rest(self.rows.factor, n)
+
+    def rest(self, at, size):
+        return self.rest_ref[self.head + at : self.head + at + size, :]
+
+    def sums(self):
+        parts = [self.sums_ref[i * self.levels : (i + 1) * self.levels, :] for i in range(self.parts)]
+        return jnp.concatenate(halves(jnp.concatenate(parts, axis=1)), axis=0)
+
+
+def line(table, i):
+    return table[i : i + 1]
+
+
+def pick_source(block, r):
+    band = block.parts * block.cap
+    column = lax.broadcasted_iota(jnp.int32, (band, block.cap), 0).astype(F32)
+    return jnp.where(column == line(block.src, r), 1.0, 0.0).astype(BF16)
+
+
+def fill_slots(bands, blocks, n, slots_ref):
+    for i, s in enumerate(bands):
+        block = blocks[s]
+        both = block.sums()
+        for d in range(n):
+            picked = product(both, pick_source(block, s ^ d))
+            values = (picked[: block.levels] + picked[block.levels :]) * line(block.factor, s ^ d)
+            slots_ref[d, :, i * block.cap : (i + 1) * block.cap] = jnp.concatenate(halves(values), axis=0)
+
+
+def met_at(d, block, bands, slots_ref):
+    own = jnp.broadcast_to(line(block.tgt, d), (block.cap, block.cap)).T
+    same = [jnp.where(own == line(block.tgt, s ^ d), 1.0, 0.0).astype(BF16) for s in bands]
+    met = product(slots_ref[d], jnp.concatenate(same, axis=1), ((1,), (1,)))
+    return met[: block.levels] + met[block.levels :]
+
+
+def open_blocks(order, counts, refs, n, levels, band):
+    blocks = {}
+    for r, count in zip(order, counts):
+        blocks[r] = Block(refs[:count], n, levels, band)
+        refs = refs[count:]
+    return blocks, refs
+
+
+def early_kernel(n, levels, band, first, counts, *refs):
+    blocks, (slots_ref, met_ref) = open_blocks(first, counts, refs, n, levels, band)
+    fill_slots(first, blocks, n, slots_ref)
+    for i, d in enumerate(first):
+        met_ref[i] = met_at(d, blocks[d], first, slots_ref)
+
+
+def shared_kernel(n, cols, first, second, counts, pos_ref, loc_ref, slots_ref, met_ref, *refs):
+    levels = loc_ref.shape[0]
+    band = refs[-3].shape[1] - 128
+    blocks, (out_ref, late_ref, tables_ref) = open_blocks(first + second, counts, refs, n, levels, band)
     me = pos_ref[0]
-    heads = [ref.shape[0] - rows.total for ref in rest_refs]
-
-    def rest(r, at, size):
-        return rest_refs[r][heads[r] + at : heads[r] + at + size, :]
-
-    def row(r, at):
-        return rest(r, at, 1)
-
-    column = lax.broadcasted_iota(jnp.int32, (band, cap), 0).astype(F32)
-    src, tgt = [], []
-    for r in range(n):
-        words = rest(r, rows.index, n)
-        tgt.append(jnp.floor((words + 0.5) * (1.0 / band)))
-        src.append(words - tgt[r] * float(band))
-        tables_ref[me ^ r, :n, :] = tgt[r]
-        tables_ref[me ^ r, n:, :] = rest(r, rows.edge, EXTRA)
-
-    def chosen(s, d):
-        return jnp.where(column == src[s][s ^ d : (s ^ d) + 1], 1.0, 0.0).astype(BF16)
-
-    for s in range(n):
-        sums = jnp.concatenate([sums_refs[s][i * levels : (i + 1) * levels, :] for i in range(parts)], axis=1)
-        both = jnp.concatenate(halves(sums), axis=0)
-        for d in range(n):
-            picked = product(both, chosen(s, d))
-            values = (picked[:levels] + picked[levels:]) * row(s, rows.factor + (s ^ d))
-            slots_ref[d, :, s * cap : (s + 1) * cap] = jnp.concatenate(halves(values), axis=0)
-    own = jnp.concatenate([tgt[d][d : d + 1] for d in range(n)], axis=0)
-    turned = own.T
+    for r, block in blocks.items():
+        tables_ref[me ^ r, :n, :] = block.tgt
+        tables_ref[me ^ r, n:, :] = block.rest(block.rows.edge, EXTRA)
+    fill_slots(second, blocks, n, late_ref)
     last = cols - 1.0
     total = jnp.zeros((levels, band), F32)
-    for d in range(n):
-        same = [
-            jnp.where(turned[:, d : d + 1] == tgt[d][s ^ d : (s ^ d) + 1], 1.0, 0.0).astype(BF16) for s in range(n)
-        ]
-        met = product(slots_ref[d], jnp.concatenate(same, axis=1), ((1,), (1,)))
-        value = met[:levels] + met[levels:] + rest(d, levels, levels)
-        edge = row(d, rows.edge)
+    for d, block in blocks.items():
+        value = met_at(d, block, second, late_ref) + block.rest(levels, levels)
+        value = value + (met_ref[first.index(d)] if d in first else met_at(d, block, first, slots_ref))
+        edge = block.rest(block.rows.edge, 1)
+        own = line(block.tgt, d)
         there = me ^ d
         before = tables_ref[jnp.maximum(there - 1, 0), n : n + 1, :]
-        near = jnp.where((own[d : d + 1] == 0.0) & (there > 0), edge[:, 6 * levels + 1 : 6 * levels + 2], 0.0)
+        near = jnp.where((own == 0.0) & (there > 0), edge[:, 6 * levels + 1 : 6 * levels + 2], 0.0)
         value = value + row_as_column(before, levels, 0) * near
         after = tables_ref[jnp.minimum(there + 1, n - 1), n : n + 1, :]
-        near = jnp.where((own[d : d + 1] == last) & (there < n - 1), edge[:, 6 * levels : 6 * levels + 1], 0.0)
+        near = jnp.where((own == last) & (there < n - 1), edge[:, 6 * levels : 6 * levels + 1], 0.0)
         value = value + row_as_column(after, levels, levels) * near
-        misfit = rest(d, 0, levels) * value
-        given = misfit * row(0, rows.factor + d)
-        total = total + select(given, chosen(0, d), ((1,), (1,)))
+        given = block.rest(0, levels) * value * line(blocks[0].factor, d)
+        total = total + select(given, pick_source(blocks[0], d), ((1,), (1,)))
     out_ref[:, :band] = total
     out_ref[:, band:] = jnp.concatenate([loc_ref[...], jnp.zeros((levels, 128 - loc_ref.shape[1]), F32)], axis=1)
 
 
-def outputs_kernel(pos_ref, slots_ref, tables_ref, static_ref, diag_ref, off_ref, obs_ref, innov_ref,
+def outputs_kernel(first, second, pos_ref, early_ref, late_ref, tables_ref, static_ref, diag_ref, off_ref, obs_ref, innov_ref,
                    increment_ref, grad_ref):
     levels, cols = static_ref.shape
     n = tables_ref.shape[0]
@@ -350,9 +378,11 @@
     me = pos_ref[0]
     row = lax.broadcasted_iota(jnp.int32, (cols, cap), 0).astype(F32)
     remapped = jnp.zeros((2 * levels, cols), F32)
-    for s in range(n):
+    given = [(s, ref, slice(i * cap, (i + 1) * cap)) for bands, ref in ((first, early_ref), (second, late_ref))
+             for i, s in enumerate(bands)]
+    for s, ref, place in given:
         landing = jnp.where(row == tables_ref[me, s : s + 1, :], 1.0, 0.0).astype(BF16)
-        remapped = remapped + product(slots_ref[0, :, s * cap : (s + 1) * cap], landing, ((1,), (1,)))
+        remapped = remapped + product(ref[0, :, place], landing, ((1,), (1,)))
     remapped = remapped[:levels] + remapped[levels:]
     static, off = static_ref[...], off_ref[...]
     lane = lax.broadcasted_iota(jnp.int32, (levels, cols), 1)
@@ -361,11 +391,10 @@
         edge = tables_ref[there, n : n + 1, :]
         static_end, coupling, base = (row_as_column(edge, levels, (2 * i + side) * levels) for i in range(3))
         far = me ^ there
-        values = slots_ref[far, :levels, :].astype(F32) + slots_ref[far, levels:, :].astype(F32)
-        landed = [
-            jnp.where(tables_ref[there, pl.ds(s ^ far, 1), :] == column, values[:, s * cap : (s + 1) * cap], 0.0)
-            for s in range(n)
-        ]
+        landed = []
+        for s, ref, place in given:
+            values = ref[far, :levels, place].astype(F32) + ref[far, levels:, place].astype(F32)
+            landed.append(jnp.where(tables_ref[there, pl.ds(s ^ far, 1), :] == column, values, 0.0))
         remap_end = jnp.sum(sum(landed), axis=1, keepdims=True)
         off_end = edge[:, 6 * levels + side : 6 * levels + side + 1]
         coupled = coupling * (remap_end + base + off_end * own_end)
@@ -444,20 +473,41 @@
         sums[0], other_perturb = lax.optimization_barrier((sums[0], other_perturb))
         for k in range(1, groups):
             sums.append(lax.ppermute(sums[0], "grp", [(g, (g + k) % groups) for g in range(groups)]))
+        far, near = list(range(n // 2, n)), list(range(1, n // 2))
+        ahead = far[len(far) // 2 :]
+        whole = [r for r in far + near if r not in ahead]
+
+        def to(r, block):
+            return lax.ppermute(block, "tile", [(i, i ^ r) for i in range(n)])
+
+        static_parts = {r: to(r, rests[r]) for r in ahead}
         total, *blocks = call(
             functools.partial(blocks_kernel, groups),
-            [shape((stacked, cap), F32)] + [shape((stacked + rows.total, cap), F32)] * (n - 1),
-            [VMEM] * (groups + n - 1),
-        )(*sums, *rests[1:])
-        order = [*range(n // 2, n), *range(1, n // 2)]
-        arrived = [lax.ppermute(blocks[r - 1], "tile", [(i, i ^ r) for i in range(n)]) for r in order]
-        mine, slots, tables = call(
-            functools.partial(shared_kernel, order, levels, tile_cols),
-            (mine_shape, shape((n, 2 * levels, n * cap), BF16), shape((n, n + EXTRA, cap), F32)),
-            [SMEM] + [VMEM] * (n + 2),
-        )(pos, level_loc, total, rests[0], *arrived)
-        increment, grad_static = call(outputs_kernel, (flat, flat), [SMEM] + [VMEM] * 7)(
-            pos, slots, tables, static_control, diag, off, obs_weight, innovation
+            [shape((stacked, cap), F32)] + [shape((stacked + rows.total, cap), F32)] * len(whole),
+            [VMEM] * (groups + len(whole)),
+        )(*sums, *[rests[r] for r in whole])
+        blocks = dict(zip(whole, blocks))
+        arrived = {r: (to(r, total), static_parts[r]) if r in ahead else (to(r, blocks[r]),) for r in far + near}
+        arrived[0] = (total, rests[0])
+        first, second = [0] + far, near
+
+        def taken(order):
+            return tuple(len(arrived[r]) for r in order), [ref for r in order for ref in arrived[r]]
+
+        counts_first, refs_first = taken(first)
+        slots, met = call(
+            functools.partial(early_kernel, n, levels, band_cols, first, counts_first),
+            (shape((n, 2 * levels, len(first) * cap), BF16), shape((len(first), levels, cap), F32)),
+            [VMEM] * len(refs_first),
+        )(*refs_first)
+        counts_all, refs_all = taken(first + second)
+        mine, late, tables = call(
+            functools.partial(shared_kernel, n, tile_cols, first, second, counts_all),
+            (mine_shape, shape((n, 2 * levels, len(second) * cap), BF16), shape((n, n + EXTRA, cap), F32)),
+            [SMEM] + [VMEM] * (3 + len(refs_all)),
+        )(pos, level_loc, slots, met, *refs_all)
+        increment, grad_static = call(functools.partial(outputs_kernel, first, second), (flat, flat), [SMEM] + [VMEM] * 8)(
+            pos, slots, late, tables, static_control, diag, off, obs_weight, innovation
         )
     else:
         payload = call(

time: 31.1 us -> 34.2 us (1.100)
  starting transfers between devices: 14.2 us -> 19.6 us
  waiting for transfers between devices: 4.93 us -> 2.59 us
    ppermute x7 -> x9, starting transfers between devices: 10.6 us -> 16 us  [to(): return lax.ppermute(block, 'tile', [(i, i ^ r) for i in range(n)])]
    ppermute x7 -> x9, waiting for transfers between devices: 4.92 us -> 2.58 us  [to(): return lax.ppermute(block, 'tile', [(i, i ^ r) for i in range(n)])]
    pallas_call x2 -> x3, Pallas kernels: 3.8 us -> 3.8 us  [the longest x1 1.53 us: body(): call(functools.partial(outputs_kernel, first, second), (flat, flat), [SME...]
  transfers between devices with their start and end apart: 11 -> 13, of which waited for: 3 -> 2; matrix products, arithmetic and copies ran while one was open for 0% -> 0% of each run, Pallas kernels for 18% -> 19%
where the time goes in v6:
time: 34.2 us; the launch traced here: 33.8 us
  starting transfers between devices  19.6 us (57%)
  Pallas kernels  9.41 us (28%)
  waiting for transfers between devices  2.59 us (8%)
  local copies, waits for them, and re-layouts  1.43 us (4%)
  between operations  0.79 us (2%)
    ppermute x9, starting transfers between devices, to(): return lax.ppermute(block, 'tile', [(i, i ^ r) for i in range(n)])  16 us
    ppermute x1, starting transfers between devices, body(): lax.ppermute(sums[0], 'grp', [(g, (g + k) % groups) for g in range(groups)])  2.97 us
    ppermute x9, waiting for transfers between devices, to(): return lax.ppermute(block, 'tile', [(i, i ^ r) for i in range(n)])  2.58 us
    pallas_call x1, Pallas kernels, body(): call(own_kernel, shape((levels, band_cols), F32), [SMEM] + [HBM] * 3, [pl...  2.3 us
    pallas_call x1, Pallas kernels, body(): call(functools.partial(outputs_kernel, first, second), (flat, flat), [SME...  1.53 us
    pallas_call x1, Pallas kernels, body(): call(ens_kernel, shape(control.shape, F32), [SMEM] + [VMEM] * 5)  1.52 us
    pallas_call x1, Pallas kernels, body(): call(functools.partial(shared_kernel, n, tile_cols, first, second, counts...  1.51 us
    unnamed x26, local copies, waits for them, and re-layouts  1.43 us
  transfers between devices with their start and end apart: 13, of which 2 were waited for; matrix products, arithmetic and copies ran while one was open for 0% of the time, Pallas kernels for 19%

profile of v6, /device:TPU:0, one launch (start us, length us, event | category | flops | bytes accessed | tf_op | source)
XLA Modules:
  0.0 33.8 jit_solution(12636065620880744256)
XLA Ops:
  0.6 0.5 %collective-permute-start = (f32[16,40,256]{2,1,0:T(8,128)}, f32[16,40,256]{2,1,0:T(8,128)S(1)}, u32[]{:S(2)}, u32[]{:S(2)}) collective-permute-start(f32[16,40,256]{2,1,0:T(8,128)} %control_ref.1), channel_id=1, source_target_pairs={{0,1},{1,0},{2,3},{3,2},{4,5},{5,4},{6,7},{7,6},{8,9},{9,8},{10,11... | collective-permute-start | bytes 1966088 | tf_op jit(solution)/shard_map/ppermute | solution.py:450
  1.1 0.1 collective-permute-start.1
  1.2 2.3 %shard_map.139.part_ref = f32[16,256]{1,0:T(8,128)} custom-call(s32[1]{0:T(128)} %bitcast.1.lev_ref, bf16[16,40,256]{2,1,0:T(8,128)(2,1)} %perturb_ref.3, f32[16,40,256]{2,1,0:T(8,128)} %control_ref.1, f32[16,32]{1,0:T(8,128)} %loc_ref.3), custom_call_target="tpu_custom_call" | custom-call | tf_op jit(solution)/shard_map/pallas_call | solution.py:452
  3.5 0.0 copy-start.2
  3.6 0.0 copy-start.3
  3.6 0.0 copy-start.4
  3.6 0.0 collective-permute-done.other_ref
  3.6 0.0 copy-done
  3.6 0.0 copy-start.6
  3.6 0.7 %copy-done.6 = f32[16,256]{1,0:T(8,128)S(1)} copy-done((f32[16,256]{1,0:T(8,128)S(1)}, f32[16,256]{1,0:T(8,128)}, u32[]{:S(2)}) %copy-start.6) | copy-done | bytes 16408
  4.4 0.7 %shard_map.140.refs_0_ = f32[16,256]{1,0:T(8,128)S(1)} custom-call(s32[1]{0:T(128)} %bitcast.1.lev_ref, bf16[16,40,256]{2,1,0:T(8,128)(2,1)S(1)} %copy-done, f32[16,40,256]{2,1,0:T(8,128)S(1)} %collective-permute-done.other_ref, f32[16,256]{1,0:T(8,128)S(1)} %copy-done.6, f32[16,32]{1,0:T(8,128)S(1)} %copy-done.5), custom_call_target="tpu_custom_call" | custom-call | tf_op jit(solution)/shard_map/pallas_call | solution.py:469
  5.1 0.0 collective-permute-done.1.other_ref
  5.1 3.0 %collective-permute-start.2 = (f32[16,256]{1,0:T(8,128)S(1)}, f32[16,256]{1,0:T(8,128)S(1)}, u32[]{:S(2)}, u32[]{:S(2)}) collective-permute-start(f32[16,256]{1,0:T(8,128)S(1)} %shard_map.140.refs_0_), channel_id=1, source_target_pairs={{0,16},{16,0},{1,17},{17,1},{2,18},{18,2},{3,19},{19,3},{4,20},{20... | collective-permute-start | bytes 49160 | tf_op jit(solution)/shard_map/ppermute | solution.py:475
  8.0 0.0 copy-done.3
  8.1 0.0 copy-done.4
  8.1 0.0 copy-done.9
  8.1 0.0 copy-done.10
  8.1 0.0 copy-done.11
  8.1 0.6 %copy-done.8 = f32[1024]{0:T(1024)S(1)} copy-done((f32[1024]{0:T(1024)S(1)}, f32[1024]{0:T(1024)}, u32[]{:S(2)}) %copy-start.8) | copy-done | bytes 4120
  8.7 0.0 copy-done.7
  8.7 0.0 copy-done.12
  8.7 1.1 %shard_map.141 = (f32[56,128]{1,0:T(8,128)S(1)}, f32[56,128]{1,0:T(8,128)S(1)}, f32[56,128]{1,0:T(8,128)S(1)}, f32[56,128]{1,0:T(8,128)S(1)}, f32[56,128]{1,0:T(...) custom-call(s32[1]{0:T(128)} %bitcast.pos_ref, s32[1,8]{1,0:T(1,128)S(1)} %copy-done.12, ...), custom_call_target="tpu_custom_call" | custom-call | tf_op jit(solution)/shard_map/pallas_call | solution.py:465
  9.8 3.7 %collective-permute-start.6 = (f32[56,128]{1,0:T(8,128)S(1)}, f32[56,128]{1,0:T(8,128)S(1)}, u32[]{:S(2)}, u32[]{:S(2)}) collective-permute-start(f32[56,128]{1,0:T(8,128)S(1)} %get-tuple-element.36), channel_id=1, source_target_pairs={{0,12},{2,14},{4,8},{6,10},{8,4},{10,6},{12,0},{14,2},{1,13},{3,15... | collective-permute-start | bytes 86024 | tf_op jit(solution)/shard_map/ppermute | solution.py:481
  13.5 1.2 %collective-permute-start.8 = (f32[56,128]{1,0:T(8,128)S(1)}, f32[56,128]{1,0:T(8,128)S(1)}, u32[]{:S(2)}, u32[]{:S(2)}) collective-permute-start(f32[56,128]{1,0:T(8,128)S(1)} %get-tuple-element.37), channel_id=1, source_target_pairs={{0,14},{2,12},{4,10},{6,8},{8,6},{10,4},{12,2},{14,0},{1,15},{3,13... | collective-permute-start | bytes 86024 | tf_op jit(solution)/shard_map/ppermute | solution.py:481
  14.7 0.0 collective-permute-done.2.refs_1_
  14.7 3.6 %collective-permute-start.7 = (f32[32,128]{1,0:T(8,128)S(1)}, f32[32,128]{1,0:T(8,128)S(1)}, u32[]{:S(2)}, u32[]{:S(2)}) collective-permute-start(f32[32,128]{1,0:T(8,128)S(1)} %get-tuple-element.32.refs_0_), channel_id=1, source_target_pairs={{0,14},{2,12},{4,10},{6,8},{8,6},{10,4},{12,2},{14,0},{1,15},{3,13... | collective-permute-start | bytes 49160 | tf_op jit(solution)/shard_map/ppermute | solution.py:481
  18.3 0.2 collective-permute-start.5
  18.6 0.0 collective-permute-start.3
  18.6 0.0 collective-permute-done.6.refs_5_
  18.6 3.9 %collective-permute-start.4 = (f32[88,128]{1,0:T(8,128)S(1)}, f32[88,128]{1,0:T(8,128)S(1)}, u32[]{:S(2)}, u32[]{:S(2)}) collective-permute-start(f32[88,128]{1,0:T(8,128)S(1)} %get-tuple-element.35), channel_id=1, source_target_pairs={{0,10},{2,8},{4,14},{6,12},{8,2},{10,0},{12,6},{14,4},{1,11},{3,9}... | collective-permute-start | bytes 135176 | tf_op jit(solution)/shard_map/ppermute | solution.py:481
  22.4 0.0 collective-permute-done.8.refs_7_
  22.4 0.5 %collective-permute-start.9 = (f32[88,128]{1,0:T(8,128)S(1)}, f32[88,128]{1,0:T(8,128)S(1)}, u32[]{:S(2)}, u32[]{:S(2)}) collective-permute-start(f32[88,128]{1,0:T(8,128)S(1)} %get-tuple-element.40), channel_id=1, source_target_pairs={{0,2},{2,0},{4,6},{6,4},{8,10},{10,8},{12,14},{14,12},{1,3},{3,1},... | collective-permute-start | bytes 135176 | tf_op jit(solution)/shard_map/ppermute | solution.py:481
  22.9 0.0 collective-permute-done.7.refs_6_
  23.0 1.4 %collective-permute-start.10 = (f32[88,128]{1,0:T(8,128)S(1)}, f32[88,128]{1,0:T(8,128)S(1)}, u32[]{:S(2)}, u32[]{:S(2)}) collective-permute-start(f32[88,128]{1,0:T(8,128)S(1)} %get-tuple-element.41), channel_id=1, source_target_pairs={{0,4},{2,6},{4,0},{6,2},{8,12},{10,14},{12,8},{14,10},{1,5},{3,7},... | collective-permute-start | bytes 135176 | tf_op jit(solution)/shard_map/ppermute | solution.py:481
  24.3 0.0 collective-permute-done.5.refs_4_
  24.3 1.6 %collective-permute-start.11 = (f32[88,128]{1,0:T(8,128)S(1)}, f32[88,128]{1,0:T(8,128)S(1)}, u32[]{:S(2)}, u32[]{:S(2)}) collective-permute-start(f32[88,128]{1,0:T(8,128)S(1)} %get-tuple-element.42), channel_id=1, source_target_pairs={{0,6},{2,4},{4,2},{6,0},{8,14},{10,12},{12,10},{14,8},{1,7},{3,5},... | collective-permute-start | bytes 135176 | tf_op jit(solution)/shard_map/ppermute | solution.py:481
  25.9 0.0 collective-permute-done.3.refs_2_
  25.9 0.3 collective-permute-done.4.refs_3_
  26.2 0.8 %shard_map.143 = (bf16[8,32,640]{2,1,0:T(8,128)(2,1)S(1)}, f32[5,16,128]{2,1,0:T(8,128)S(1)}) custom-call(f32[32,128]{1,0:T(8,128)S(1)} %get-tuple-element.32.refs_0_, f32[56,128]{1,0:T(8,128)S(1)} %get-tuple-element.33.refs_1_, f32[88,128]{1,0:T(8,128)S(1)} %collective-permute-done.3.refs_2_, f32[88,128]{1,0:T(8,128)S(1)} %collective-permute-done.4.refs_3_, ...), custom_call_target="tpu_custom_call" | custom-call | tf_op jit(solution)/shard_map/pallas_call | solution.py:498
  26.9 0.0 collective-permute-done.9.refs_8_
  27.0 0.0 collective-permute-done.10.refs_9_
  27.0 2.3 %collective-permute-done.11.refs_10_ = f32[88,128]{1,0:T(8,128)S(1)} collective-permute-done((f32[88,128]{1,0:T(8,128)S(1)}, f32[88,128]{1,0:T(8,128)S(1)}, u32[]{:S(2)}, u32[]{:S(2)}) %collective-permute-start.11) | collective-permute-done | bytes 45088 | tf_op jit(solution)/shard_map/ppermute | solution.py:481
  29.3 1.5 %shard_map.144 = (f32[16,384]{1,0:T(8,128)S(1)}, bf16[8,32,384]{2,1,0:T(8,128)(2,1)S(1)}, f32[8,16,128]{2,1,0:T(8,128)S(1)}) custom-call(s32[1]{0:T(128)} %bitcast.pos_ref, f32[16,32]{1,0:T(8,128)S(1)} %copy-done.5, bf16[8,32,640]{2,1,0:T(8,128)(2,1)S(1)} %get-tuple-element.38.slots_ref.early_ref, f32[5,16,128]{2,1,0:T(8,128)S(1)} %get-tuple-element.39.met_ref, ...), custom_call_target="tpu_custom_call" | custom-call | tf_op jit(solution)/shard_map/pallas_call | solution.py:504
  30.8 0.0 collective-permute-start.12
  30.8 1.5 %shard_map.145 = (f32[16,1024]{1,0:T(8,128)}, f32[16,1024]{1,0:T(8,128)}) custom-call(s32[1]{0:T(128)} %bitcast.pos_ref, bf16[8,32,640]{2,1,0:T(8,128)(2,1)S(1)} %get-tuple-element.38.slots_ref.early_ref, bf16[8,32,384]{2,1,0:T(8,128)(2,1)S(1)} %get-tuple-element.43.late_ref, f32[8,16,128]{2,1,0:T(8,128)S(1)} %get-tuple-element.44.tables_ref, ...), custom_call_target="tpu_custom_call" | custom-call | tf_op jit(solution)/shard_map/pallas_call | solution.py:509
  32.3 0.0 collective-permute-done.12.theirs_ref
  32.3 0.0 copy-done.1
  32.3 1.5 %shard_map.146 = f32[16,40,256]{2,1,0:T(8,128)} custom-call(s32[1]{0:T(128)} %bitcast.1.lev_ref, bf16[16,40,256]{2,1,0:T(8,128)(2,1)S(1)} %copy-done, bf16[16,40,256]{2,1,0:T(8,128)(2,1)S(1)} %collective-permute-done.1.other_ref, f32[16,40,256]{2,1,0:T(8,128)S(1)} %copy-done.1, f32[16,384]{1,0:T(8,128)S(1)} %get-tuple-element.48.mine_ref, ...), custom_call_target="tpu_custom_call" | custom-call | tf_op jit(solution)/shard_map/pallas_call | solution.py:530
  (12 shorter events, 0.0 us)
Async XLA Ops:
  0.6 3.0 %collective-permute-start = (f32[16,40,256]{2,1,0:T(8,128)}, f32[16,40,256]{2,1,0:T(8,128)S(1)}, u32[]{:S(2)}, u32[]{:S(2)}) collective-permute-start(f32[16,40,256]{2,1,0:T(8,128)} %control_ref.1), channel_id=1, source_target_pairs={{0,1},{1,0},{2,3},{3,2},{4,5},{5,4},{6,7},{7,6},{8,9},{9,8},{10,11... | collective-permute-start | bytes 1966088 | tf_op jit(solution)/shard_map/ppermute | solution.py:450
  1.1 3.9 %collective-permute-start.1 = (bf16[16,40,256]{2,1,0:T(8,128)(2,1)}, bf16[16,40,256]{2,1,0:T(8,128)(2,1)S(1)}, u32[]{:S(2)}, u32[]{:S(2)}) collective-permute-start(bf16[16,40,256]{2,1,0:T(8,128)(2,1)} %perturb_ref.3), channel_id=1, source_target_pairs={{0,1},{1,0},{2,3},{3,2},{4,5},{5,4},{6,7},{7,6},{8,9},{9,8},{10,11... | collective-permute-start | bytes 983048 | tf_op jit(solution)/shard_map/ppermute | solution.py:451
  1.2 2.4 %copy-start = (bf16[16,40,256]{2,1,0:T(8,128)(2,1)S(1)}, bf16[16,40,256]{2,1,0:T(8,128)(2,1)}, u32[]{:S(2)}) copy-start(bf16[16,40,256]{2,1,0:T(8,128)(2,1)} %perturb_ref.3) | copy-start | bytes 983044
  1.2 2.4 %copy-start.5 = (f32[16,32]{1,0:T(8,128)S(1)}, f32[16,32]{1,0:T(8,128)}, u32[]{:S(2)}) copy-start(f32[16,32]{1,0:T(8,128)} %loc_ref.3) | copy-start | bytes 6148
  3.5 4.5 %copy-start.2 = (f32[16,1024]{1,0:T(8,128)S(1)}, f32[16,1024]{1,0:T(8,128)}, u32[]{:S(2)}) copy-start(f32[16,1024]{1,0:T(8,128)} %static_ref.3) | copy-start | bytes 196612
  3.6 4.5 %copy-start.3 = (f32[16,1024]{1,0:T(8,128)S(1)}, f32[16,1024]{1,0:T(8,128)}, u32[]{:S(2)}) copy-start(f32[16,1024]{1,0:T(8,128)} %obs_ref.3) | copy-start | bytes 196612
  3.6 4.5 %copy-start.4 = (f32[16,1024]{1,0:T(8,128)S(1)}, f32[16,1024]{1,0:T(8,128)}, u32[]{:S(2)}) copy-start(f32[16,1024]{1,0:T(8,128)} %innov_ref.3) | copy-start | bytes 196612
  3.6 0.8 %copy-start.6 = (f32[16,256]{1,0:T(8,128)S(1)}, f32[16,256]{1,0:T(8,128)}, u32[]{:S(2)}) copy-start(f32[16,256]{1,0:T(8,128)} %shard_map.139.part_ref) | copy-start | bytes 49156
  4.4 3.7 %copy-start.9 = (s32[1,8,128]{2,1,0:T(8,128)S(1)}, s32[1,8,128]{2,1,0:T(8,128)}, u32[]{:S(2)}) copy-start(s32[1,8,128]{2,1,0:T(8,128)} %src_ref.1) | copy-start | bytes 12292
  4.4 3.7 %copy-start.10 = (f32[1,8,128]{2,1,0:T(8,128)S(1)}, f32[1,8,128]{2,1,0:T(8,128)}, u32[]{:S(2)}) copy-start(f32[1,8,128]{2,1,0:T(8,128)} %weight_ref.1) | copy-start | bytes 12292
  4.4 3.7 %copy-start.11 = (s32[1,8,128]{2,1,0:T(8,128)S(1)}, s32[1,8,128]{2,1,0:T(8,128)}, u32[]{:S(2)}) copy-start(s32[1,8,128]{2,1,0:T(8,128)} %tgt_ref.1) | copy-start | bytes 12292
  5.1 9.6 %collective-permute-start.2 = (f32[16,256]{1,0:T(8,128)S(1)}, f32[16,256]{1,0:T(8,128)S(1)}, u32[]{:S(2)}, u32[]{:S(2)}) collective-permute-start(f32[16,256]{1,0:T(8,128)S(1)} %shard_map.140.refs_0_), channel_id=1, source_target_pairs={{0,16},{16,0},{1,17},{17,1},{2,18},{18,2},{3,19},{19,3},{4,20},{20... | collective-permute-start | bytes 49160 | tf_op jit(solution)/shard_map/ppermute | solution.py:475
  8.0 0.7 %copy-start.8 = (f32[1024]{0:T(1024)S(1)}, f32[1024]{0:T(1024)}, u32[]{:S(2)}) copy-start(f32[1024]{0:T(1024)} %param.17) | copy-start | bytes 12292
  8.0 0.7 %copy-start.7 = (f32[1024]{0:T(1024)S(1)}, f32[1024]{0:T(1024)}, u32[]{:S(2)}) copy-start(f32[1024]{0:T(1024)} %param.16) | copy-start | bytes 12292
  8.0 0.7 %copy-start.12 = (s32[1,8]{1,0:T(1,128)S(1)}, s32[1,8]{1,0:T(1,128)}, u32[]{:S(2)}) copy-start(s32[1,8]{1,0:T(1,128)} %counts_ref.1) | copy-start | bytes 100
  9.8 8.7 %collective-permute-start.6 = (f32[56,128]{1,0:T(8,128)S(1)}, f32[56,128]{1,0:T(8,128)S(1)}, u32[]{:S(2)}, u32[]{:S(2)}) collective-permute-start(f32[56,128]{1,0:T(8,128)S(1)} %get-tuple-element.36), channel_id=1, source_target_pairs={{0,12},{2,14},{4,8},{6,10},{8,4},{10,6},{12,0},{14,2},{1,13},{3,15... | collective-permute-start | bytes 86024 | tf_op jit(solution)/shard_map/ppermute | solution.py:481
  13.5 8.9 %collective-permute-start.8 = (f32[56,128]{1,0:T(8,128)S(1)}, f32[56,128]{1,0:T(8,128)S(1)}, u32[]{:S(2)}, u32[]{:S(2)}) collective-permute-start(f32[56,128]{1,0:T(8,128)S(1)} %get-tuple-element.37), channel_id=1, source_target_pairs={{0,14},{2,12},{4,10},{6,8},{8,6},{10,4},{12,2},{14,0},{1,15},{3,13... | collective-permute-start | bytes 86024 | tf_op jit(solution)/shard_map/ppermute | solution.py:481
  14.7 8.2 %collective-permute-start.7 = (f32[32,128]{1,0:T(8,128)S(1)}, f32[32,128]{1,0:T(8,128)S(1)}, u32[]{:S(2)}, u32[]{:S(2)}) collective-permute-start(f32[32,128]{1,0:T(8,128)S(1)} %get-tuple-element.32.refs_0_), channel_id=1, source_target_pairs={{0,14},{2,12},{4,10},{6,8},{8,6},{10,4},{12,2},{14,0},{1,15},{3,13... | collective-permute-start | bytes 49160 | tf_op jit(solution)/shard_map/ppermute | solution.py:481
  18.3 6.0 %collective-permute-start.5 = (f32[32,128]{1,0:T(8,128)S(1)}, f32[32,128]{1,0:T(8,128)S(1)}, u32[]{:S(2)}, u32[]{:S(2)}) collective-permute-start(f32[32,128]{1,0:T(8,128)S(1)} %get-tuple-element.32.refs_0_), channel_id=1, source_target_pairs={{0,12},{2,14},{4,8},{6,10},{8,4},{10,6},{12,0},{14,2},{1,13},{3,15... | collective-permute-start | bytes 49160 | tf_op jit(solution)/shard_map/ppermute | solution.py:481
  18.6 7.4 %collective-permute-start.3 = (f32[88,128]{1,0:T(8,128)S(1)}, f32[88,128]{1,0:T(8,128)S(1)}, u32[]{:S(2)}, u32[]{:S(2)}) collective-permute-start(f32[88,128]{1,0:T(8,128)S(1)} %get-tuple-element.34), channel_id=1, source_target_pairs={{0,8},{2,10},{4,12},{6,14},{8,0},{10,2},{12,4},{14,6},{1,9},{3,11}... | collective-permute-start | bytes 135176 | tf_op jit(solution)/shard_map/ppermute | solution.py:481
  18.6 7.6 %collective-permute-start.4 = (f32[88,128]{1,0:T(8,128)S(1)}, f32[88,128]{1,0:T(8,128)S(1)}, u32[]{:S(2)}, u32[]{:S(2)}) collective-permute-start(f32[88,128]{1,0:T(8,128)S(1)} %get-tuple-element.35), channel_id=1, source_target_pairs={{0,10},{2,8},{4,14},{6,12},{8,2},{10,0},{12,6},{14,4},{1,11},{3,9}... | collective-permute-start | bytes 135176 | tf_op jit(solution)/shard_map/ppermute | solution.py:481
  22.4 4.5 %collective-permute-start.9 = (f32[88,128]{1,0:T(8,128)S(1)}, f32[88,128]{1,0:T(8,128)S(1)}, u32[]{:S(2)}, u32[]{:S(2)}) collective-permute-start(f32[88,128]{1,0:T(8,128)S(1)} %get-tuple-element.40), channel_id=1, source_target_pairs={{0,2},{2,0},{4,6},{6,4},{8,10},{10,8},{12,14},{14,12},{1,3},{3,1},... | collective-permute-start | bytes 135176 | tf_op jit(solution)/shard_map/ppermute | solution.py:481
  23.0 4.0 %collective-permute-start.10 = (f32[88,128]{1,0:T(8,128)S(1)}, f32[88,128]{1,0:T(8,128)S(1)}, u32[]{:S(2)}, u32[]{:S(2)}) collective-permute-start(f32[88,128]{1,0:T(8,128)S(1)} %get-tuple-element.41), channel_id=1, source_target_pairs={{0,4},{2,6},{4,0},{6,2},{8,12},{10,14},{12,8},{14,10},{1,5},{3,7},... | collective-permute-start | bytes 135176 | tf_op jit(solution)/shard_map/ppermute | solution.py:481
  24.3 4.9 %collective-permute-start.11 = (f32[88,128]{1,0:T(8,128)S(1)}, f32[88,128]{1,0:T(8,128)S(1)}, u32[]{:S(2)}, u32[]{:S(2)}) collective-permute-start(f32[88,128]{1,0:T(8,128)S(1)} %get-tuple-element.42), channel_id=1, source_target_pairs={{0,6},{2,4},{4,2},{6,0},{8,14},{10,12},{12,10},{14,8},{1,7},{3,5},... | collective-permute-start | bytes 135176 | tf_op jit(solution)/shard_map/ppermute | solution.py:481
  29.3 3.1 %copy-start.1 = (f32[16,40,256]{2,1,0:T(8,128)S(1)}, f32[16,40,256]{2,1,0:T(8,128)}, u32[]{:S(2)}) copy-start(f32[16,40,256]{2,1,0:T(8,128)} %control_ref.1) | copy-start | bytes 1966084
  30.8 1.5 %collective-permute-start.12 = (f32[16,384]{1,0:T(8,128)S(1)}, f32[16,384]{1,0:T(8,128)S(1)}, u32[]{:S(2)}, u32[]{:S(2)}) collective-permute-start(f32[16,384]{1,0:T(8,128)S(1)} %get-tuple-element.48.mine_ref), channel_id=1, source_target_pairs={{0,1},{1,0},{2,3},{3,2},{4,5},{5,4},{6,7},{7,6},{8,9},{9,8},{10,11... | collective-permute-start | bytes 73736 | tf_op jit(solution)/shard_map/ppermute | solution.py:529

commit v7 on v6

--- a/solution.py
+++ b/solution.py
@@ -217,6 +217,15 @@
         out_ref[:, m : m + SUB, :] = control_ref[:, m : m + SUB, :] + mixed
 
 
+def relabel(r, n, lev):
+    high, low = n // 2, n // 4
+    if low == 0:
+        return r
+    both = high | low
+    turned = (r & ~both) | ((r & low) << 1) | ((r & high) >> 1)
+    return r + (turned - r) * lev
+
+
 class Rows:
     def __init__(self, levels, n):
         self.weight = slice(0, levels)
@@ -226,13 +235,13 @@
         self.total = at + 2 * n + EXTRA
 
 
-def static_kernel(band, pos_ref, counts_ref, static_ref, diag_ref, off_ref, obs_ref, innov_ref, src_ref, weight_ref, tgt_ref,
+def static_kernel(band, pos_ref, lev_ref, counts_ref, static_ref, diag_ref, off_ref, obs_ref, innov_ref, src_ref, weight_ref, tgt_ref,
                   *out_refs):
     levels, cols = static_ref.shape
     n = len(out_refs)
     cap = src_ref.shape[2]
     rows = Rows(levels, n)
-    me = pos_ref[0]
+    peers = [pos_ref[0] ^ relabel(r, n, lev_ref[0]) for r in range(n)]
     static, off, obs = static_ref[...], off_ref[...], obs_ref[...]
     lane = lax.broadcasted_iota(jnp.int32, (levels, cols), 1)
     left = jnp.where(lane == 0, 0.0, pltpu.roll(static, 1, 1))
@@ -246,10 +255,10 @@
     edge = edge + jnp.where(place == 6 * levels + 1, off[:, :1], 0.0)
     edge = jnp.broadcast_to(edge, (EXTRA, cap))
     both = jnp.concatenate(halves(jnp.concatenate([obs, base], axis=0)), axis=0)
-    tgts = [tgt_ref[0, pl.ds(me ^ r, 1), :] for r in range(n)]
-    src = jnp.concatenate([src_ref[0, pl.ds(me ^ r, 1), :] for r in range(n)], axis=0).astype(F32)
+    tgts = [tgt_ref[0, pl.ds(peer, 1), :] for peer in peers]
+    src = jnp.concatenate([src_ref[0, pl.ds(peer, 1), :] for peer in peers], axis=0).astype(F32)
     index = jnp.concatenate(tgts, axis=0).astype(F32) * float(band) + src
-    factor = jnp.concatenate([factor_of(counts_ref, weight_ref, me ^ r) for r in range(n)], axis=0)
+    factor = jnp.concatenate([factor_of(counts_ref, weight_ref, peer) for peer in peers], axis=0)
     for r, out_ref in enumerate(out_refs):
         picked = product(both, one_hot(tgts[r], cols))
         out_ref[: 2 * levels, :] = picked[: 2 * levels] + picked[2 * levels :]
@@ -341,14 +350,15 @@
         met_ref[i] = met_at(d, blocks[d], first, slots_ref)
 
 
-def shared_kernel(n, cols, first, second, counts, pos_ref, loc_ref, slots_ref, met_ref, *refs):
+def shared_kernel(n, cols, first, second, counts, pos_ref, lev_ref, loc_ref, slots_ref, met_ref, *refs):
     levels = loc_ref.shape[0]
     band = refs[-3].shape[1] - 128
     blocks, (out_ref, late_ref, tables_ref) = open_blocks(first + second, counts, refs, n, levels, band)
     me = pos_ref[0]
     for r, block in blocks.items():
-        tables_ref[me ^ r, :n, :] = block.tgt
-        tables_ref[me ^ r, n:, :] = block.rest(block.rows.edge, EXTRA)
+        there = me ^ relabel(r, n, lev_ref[0])
+        tables_ref[there, :n, :] = block.tgt
+        tables_ref[there, n:, :] = block.rest(block.rows.edge, EXTRA)
     fill_slots(second, blocks, n, late_ref)
     last = cols - 1.0
     total = jnp.zeros((levels, band), F32)
@@ -357,7 +367,7 @@
         value = value + (met_ref[first.index(d)] if d in first else met_at(d, block, first, slots_ref))
         edge = block.rest(block.rows.edge, 1)
         own = line(block.tgt, d)
-        there = me ^ d
+        there = me ^ relabel(d, n, lev_ref[0])
         before = tables_ref[jnp.maximum(there - 1, 0), n : n + 1, :]
         near = jnp.where((own == 0.0) & (there > 0), edge[:, 6 * levels + 1 : 6 * levels + 2], 0.0)
         value = value + row_as_column(before, levels, 0) * near
@@ -370,7 +380,7 @@
     out_ref[:, band:] = jnp.concatenate([loc_ref[...], jnp.zeros((levels, 128 - loc_ref.shape[1]), F32)], axis=1)
 
 
-def outputs_kernel(first, second, pos_ref, early_ref, late_ref, tables_ref, static_ref, diag_ref, off_ref, obs_ref, innov_ref,
+def outputs_kernel(first, second, pos_ref, lev_ref, early_ref, late_ref, tables_ref, static_ref, diag_ref, off_ref, obs_ref, innov_ref,
                    increment_ref, grad_ref):
     levels, cols = static_ref.shape
     n = tables_ref.shape[0]
@@ -390,7 +400,7 @@
     def beside(there, exists, column, own_end, side):
         edge = tables_ref[there, n : n + 1, :]
         static_end, coupling, base = (row_as_column(edge, levels, (2 * i + side) * levels) for i in range(3))
-        far = me ^ there
+        far = relabel(me ^ there, n, lev_ref[0])
         landed = []
         for s, ref, place in given:
             values = ref[far, :levels, place].astype(F32) + ref[far, levels:, place].astype(F32)
@@ -459,11 +469,11 @@
     flat = shape((levels, tile_cols), F32)
     mine_shape = shape((levels, band_cols + 128), F32)
     diag, off = filter_diag.reshape(1, -1), filter_off.reshape(1, -1)
-    if n * cap <= tile_cols and n & (n - 1) == 0 and band_cols * tile_cols <= 2**20:
+    if n * cap <= tile_cols and n >= 4 and lax.axis_size("lev") == 2 and n & (n - 1) == 0 and band_cols * tile_cols <= 2**20:
         rows = Rows(levels, n)
         stacked = band_cols // cap * levels
-        rests = call(functools.partial(static_kernel, band_cols), [shape((rows.total, cap), F32)] * n, [SMEM] * 2 + [VMEM] * 8)(
-            pos, counts, static_control, diag, off, obs_weight, innovation, send_src, send_wt, recv_tgt
+        rests = call(functools.partial(static_kernel, band_cols), [shape((rows.total, cap), F32)] * n, [SMEM] * 3 + [VMEM] * 8)(
+            pos, lev, counts, static_control, diag, off, obs_weight, innovation, send_src, send_wt, recv_tgt
         )
         sums = [
             call(sum_kernel, shape((levels, band_cols), F32), [SMEM] + [VMEM] * 4)(
@@ -473,23 +483,20 @@
         sums[0], other_perturb = lax.optimization_barrier((sums[0], other_perturb))
         for k in range(1, groups):
             sums.append(lax.ppermute(sums[0], "grp", [(g, (g + k) % groups) for g in range(groups)]))
-        far, near = list(range(n // 2, n)), list(range(1, n // 2))
-        ahead = far[len(far) // 2 :]
-        whole = [r for r in far + near if r not in ahead]
-
-        def to(r, block):
-            return lax.ppermute(block, "tile", [(i, i ^ r) for i in range(n)])
-
-        static_parts = {r: to(r, rests[r]) for r in ahead}
         total, *blocks = call(
             functools.partial(blocks_kernel, groups),
-            [shape((stacked, cap), F32)] + [shape((stacked + rows.total, cap), F32)] * len(whole),
-            [VMEM] * (groups + len(whole)),
-        )(*sums, *[rests[r] for r in whole])
-        blocks = dict(zip(whole, blocks))
-        arrived = {r: (to(r, total), static_parts[r]) if r in ahead else (to(r, blocks[r]),) for r in far + near}
-        arrived[0] = (total, rests[0])
-        first, second = [0] + far, near
+            [shape((stacked, cap), F32)] + [shape((stacked + rows.total, cap), F32)] * (n - 1),
+            [VMEM] * (groups + n - 1),
+        )(*sums, *rests[1:])
+        first = sorted(range(n // 2, n), key=lambda r: (relabel(r, n, 1) != r, r))
+        first = first[: n // 4 // 2] + first[n // 4 :] + first[n // 4 // 2 : n // 4]
+        second = [*range(2, n // 2), *range(1, min(2, n // 2))]
+        levs = lax.axis_size("lev")
+        arrived = {0: (total, rests[0])}
+        for r in first + second:
+            pairs = [(i * levs + v, (i ^ relabel(r, n, v)) * levs + v) for i in range(n) for v in range(levs)]
+            arrived[r] = (lax.ppermute(blocks[r - 1], ("tile", "lev"), pairs),)
+        first = [0] + first
 
         def taken(order):
             return tuple(len(arrived[r]) for r in order), [ref for r in order for ref in arrived[r]]
@@ -504,10 +511,10 @@
         mine, late, tables = call(
             functools.partial(shared_kernel, n, tile_cols, first, second, counts_all),
             (mine_shape, shape((n, 2 * levels, len(second) * cap), BF16), shape((n, n + EXTRA, cap), F32)),
-            [SMEM] + [VMEM] * (3 + len(refs_all)),
-        )(pos, level_loc, slots, met, *refs_all)
-        increment, grad_static = call(functools.partial(outputs_kernel, first, second), (flat, flat), [SMEM] + [VMEM] * 8)(
-            pos, slots, late, tables, static_control, diag, off, obs_weight, innovation
+            [SMEM] * 2 + [VMEM] * (3 + len(refs_all)),
+        )(pos, lev, level_loc, slots, met, *refs_all)
+        increment, grad_static = call(functools.partial(outputs_kernel, first, second), (flat, flat), [SMEM] * 2 + [VMEM] * 8)(
+            pos, lev, slots, late, tables, static_control, diag, off, obs_weight, innovation
         )
     else:
         payload = call(

time: 34.2 us -> 30.3 us (0.89)
  starting transfers between devices: 19.6 us -> 15 us
  waiting for transfers between devices: 2.59 us -> 3.29 us
    ppermute x9 -> x7, starting transfers between devices: 16 us -> 11.5 us  [body(): arrived[r] = (lax.ppermute(blocks[r - 1], ('tile', 'lev'), pairs),)]
    ppermute x9 -> x7, waiting for transfers between devices: 2.58 us -> 3.28 us  [body(): arrived[r] = (lax.ppermute(blocks[r - 1], ('tile', 'lev'), pairs),)]
  transfers between devices with their start and end apart: 13 -> 11, of which waited for: 2 -> 2; matrix products, arithmetic and copies ran while one was open for 0% -> 0% of each run, Pallas kernels for 19% -> 21%
where the time goes in v7:
time: 30.3 us; the launch traced here: 30 us
  starting transfers between devices  15 us (50%)
  Pallas kernels  9.41 us (31%)
  waiting for transfers between devices  3.29 us (11%)
  local copies, waits for them, and re-layouts  1.44 us (5%)
  between operations  0.83 us (3%)
    ppermute x7, starting transfers between devices, body(): arrived[r] = (lax.ppermute(blocks[r - 1], ('tile', 'lev'), pairs),)  11.5 us
    ppermute x7, waiting for transfers between devices, body(): arrived[r] = (lax.ppermute(blocks[r - 1], ('tile', 'lev'), pairs),)  3.28 us
    ppermute x1, starting transfers between devices, body(): lax.ppermute(sums[0], 'grp', [(g, (g + k) % groups) for g in range(groups)])  2.97 us
    pallas_call x1, Pallas kernels, body(): call(own_kernel, shape((levels, band_cols), F32), [SMEM] + [HBM] * 3, [pl...  2.3 us
    pallas_call x1, Pallas kernels, body(): call(functools.partial(outputs_kernel, first, second), (flat, flat), [SME...  1.53 us
    pallas_call x1, Pallas kernels, body(): call(functools.partial(shared_kernel, n, tile_cols, first, second, counts...  1.52 us
    pallas_call x1, Pallas kernels, body(): call(ens_kernel, shape(control.shape, F32), [SMEM] + [VMEM] * 5)  1.51 us
    unnamed x26, local copies, waits for them, and re-layouts  1.44 us
  transfers between devices with their start and end apart: 11, of which 2 were waited for; matrix products, arithmetic and copies ran while one was open for 0% of the time, Pallas kernels for 21%

profile of v7, /device:TPU:0, one launch (start us, length us, event | category | flops | bytes accessed | tf_op | source)
XLA Modules:
  0.0 30.0 jit_solution(12272710223125639146)
XLA Ops:
  0.6 0.5 %collective-permute-start = (f32[16,40,256]{2,1,0:T(8,128)}, f32[16,40,256]{2,1,0:T(8,128)S(1)}, u32[]{:S(2)}, u32[]{:S(2)}) collective-permute-start(f32[16,40,256]{2,1,0:T(8,128)} %control_ref.1), channel_id=1, source_target_pairs={{0,1},{1,0},{2,3},{3,2},{4,5},{5,4},{6,7},{7,6},{8,9},{9,8},{10,11... | collective-permute-start | bytes 1966088 | tf_op jit(solution)/shard_map/ppermute | solution.py:460
  1.1 0.1 collective-permute-start.1
  1.2 0.0 copy-start
  1.2 2.3 %shard_map.139.part_ref = f32[16,256]{1,0:T(8,128)} custom-call(s32[1]{0:T(128)} %bitcast.1.lev_ref, bf16[16,40,256]{2,1,0:T(8,128)(2,1)} %perturb_ref.3, f32[16,40,256]{2,1,0:T(8,128)} %control_ref.1, f32[16,32]{1,0:T(8,128)} %loc_ref.3), custom_call_target="tpu_custom_call" | custom-call | tf_op jit(solution)/shard_map/pallas_call | solution.py:462
  3.5 0.0 copy-start.2
  3.6 0.0 copy-start.3
  3.6 0.0 copy-start.4
  3.6 0.0 collective-permute-done.other_ref
  3.6 0.0 copy-done
  3.6 0.0 copy-done.5
  3.6 0.0 copy-start.6
  3.6 0.7 %copy-done.6 = f32[16,256]{1,0:T(8,128)S(1)} copy-done((f32[16,256]{1,0:T(8,128)S(1)}, f32[16,256]{1,0:T(8,128)}, u32[]{:S(2)}) %copy-start.6) | copy-done | bytes 16408
  4.4 0.7 %shard_map.140.refs_0_ = f32[16,256]{1,0:T(8,128)S(1)} custom-call(s32[1]{0:T(128)} %bitcast.1.lev_ref, bf16[16,40,256]{2,1,0:T(8,128)(2,1)S(1)} %copy-done, f32[16,40,256]{2,1,0:T(8,128)S(1)} %collective-permute-done.other_ref, f32[16,256]{1,0:T(8,128)S(1)} %copy-done.6, f32[16,32]{1,0:T(8,128)S(1)} %copy-done.5), custom_call_target="tpu_custom_call" | custom-call | tf_op jit(solution)/shard_map/pallas_call | solution.py:479
  5.1 0.0 collective-permute-done.1.other_ref
  5.1 3.0 %collective-permute-start.2 = (f32[16,256]{1,0:T(8,128)S(1)}, f32[16,256]{1,0:T(8,128)S(1)}, u32[]{:S(2)}, u32[]{:S(2)}) collective-permute-start(f32[16,256]{1,0:T(8,128)S(1)} %shard_map.140.refs_0_), channel_id=1, source_target_pairs={{0,16},{16,0},{1,17},{17,1},{2,18},{18,2},{3,19},{19,3},{4,20},{20... | collective-permute-start | bytes 49160 | tf_op jit(solution)/shard_map/ppermute | solution.py:485
  8.0 0.0 copy-done.2
  8.0 0.0 copy-done.3
  8.1 0.0 copy-done.4
  8.1 0.0 copy-done.9
  8.1 0.0 copy-done.10
  8.1 0.0 copy-done.11
  8.1 0.6 %copy-done.8 = f32[1024]{0:T(1024)S(1)} copy-done((f32[1024]{0:T(1024)S(1)}, f32[1024]{0:T(1024)}, u32[]{:S(2)}) %copy-start.8) | copy-done | bytes 4120
  8.7 0.0 copy-done.7
  8.7 0.0 copy-done.12
  8.7 1.1 %shard_map.141 = (f32[56,128]{1,0:T(8,128)S(1)}, f32[56,128]{1,0:T(8,128)S(1)}, f32[56,128]{1,0:T(8,128)S(1)}, f32[56,128]{1,0:T(8,128)S(1)}, f32[56,128]{1,0:T(...) custom-call(s32[1]{0:T(128)} %bitcast.pos_ref, s32[1]{0:T(128)} %bitcast.1.lev_ref, ...), custom_call_target="tpu_custom_call" | custom-call | tf_op jit(solution)/shard_map/pallas_call | solution.py:475
  9.8 0.0 collective-permute-done.2.refs_1_
  9.9 4.1 %collective-permute-start.3 = (f32[88,128]{1,0:T(8,128)S(1)}, f32[88,128]{1,0:T(8,128)S(1)}, u32[]{:S(2)}, u32[]{:S(2)}) collective-permute-start(f32[88,128]{1,0:T(8,128)S(1)} %get-tuple-element.38), channel_id=1, source_target_pairs={{0,12},{1,13},{2,14},{3,15},{4,8},{5,9},{6,10},{7,11},{8,4},{9,5},... | collective-permute-start | bytes 135176 | tf_op jit(solution)/shard_map/ppermute | solution.py:498
  14.0 0.0 collective-permute-start.4
  14.0 3.9 %collective-permute-start.5 = (f32[88,128]{1,0:T(8,128)S(1)}, f32[88,128]{1,0:T(8,128)S(1)}, u32[]{:S(2)}, u32[]{:S(2)}) collective-permute-start(f32[88,128]{1,0:T(8,128)S(1)} %get-tuple-element.40), channel_id=1, source_target_pairs={{0,10},{1,7},{2,8},{3,5},{4,14},{5,3},{6,12},{7,1},{8,2},{9,15},{1... | collective-permute-start | bytes 135176 | tf_op jit(solution)/shard_map/ppermute | solution.py:498
  17.9 0.0 collective-permute-start.6
  17.9 0.6 %collective-permute-start.7 = (f32[88,128]{1,0:T(8,128)S(1)}, f32[88,128]{1,0:T(8,128)S(1)}, u32[]{:S(2)}, u32[]{:S(2)}) collective-permute-start(f32[88,128]{1,0:T(8,128)S(1)} %get-tuple-element.44), channel_id=1, source_target_pairs={{0,4},{1,9},{2,6},{3,11},{4,0},{5,13},{6,2},{7,15},{8,12},{9,1},{1... | collective-permute-start | bytes 135176 | tf_op jit(solution)/shard_map/ppermute | solution.py:498
  18.4 0.0 collective-permute-done.3.refs_2_
  18.4 2.6 %collective-permute-start.8 = (f32[88,128]{1,0:T(8,128)S(1)}, f32[88,128]{1,0:T(8,128)S(1)}, u32[]{:S(2)}, u32[]{:S(2)}) collective-permute-start(f32[88,128]{1,0:T(8,128)S(1)} %get-tuple-element.45), channel_id=1, source_target_pairs={{0,6},{1,11},{2,4},{3,9},{4,2},{5,15},{6,0},{7,13},{8,14},{9,3},{1... | collective-permute-start | bytes 135176 | tf_op jit(solution)/shard_map/ppermute | solution.py:498
  21.0 0.0 collective-permute-done.4.refs_3_
  21.0 0.3 %collective-permute-start.9 = (f32[88,128]{1,0:T(8,128)S(1)}, f32[88,128]{1,0:T(8,128)S(1)}, u32[]{:S(2)}, u32[]{:S(2)}) collective-permute-start(f32[88,128]{1,0:T(8,128)S(1)} %get-tuple-element.46), channel_id=1, source_target_pairs={{0,2},{1,3},{2,0},{3,1},{4,6},{5,7},{6,4},{7,5},{8,10},{9,11},{10,... | collective-permute-start | bytes 135176 | tf_op jit(solution)/shard_map/ppermute | solution.py:498
  21.4 1.3 %collective-permute-done.5.refs_4_ = f32[88,128]{1,0:T(8,128)S(1)} collective-permute-done((f32[88,128]{1,0:T(8,128)S(1)}, f32[88,128]{1,0:T(8,128)S(1)}, u32[]{:S(2)}, u32[]{:S(2)}) %collective-permute-start.5) | collective-permute-done | bytes 45088 | tf_op jit(solution)/shard_map/ppermute | solution.py:498
  22.7 1.9 %collective-permute-done.6.refs_5_ = f32[88,128]{1,0:T(8,128)S(1)} collective-permute-done((f32[88,128]{1,0:T(8,128)S(1)}, f32[88,128]{1,0:T(8,128)S(1)}, u32[]{:S(2)}, u32[]{:S(2)}) %collective-permute-start.6) | collective-permute-done | bytes 45088 | tf_op jit(solution)/shard_map/ppermute | solution.py:498
  24.6 0.7 %shard_map.143 = (bf16[8,32,640]{2,1,0:T(8,128)(2,1)S(1)}, f32[5,16,128]{2,1,0:T(8,128)S(1)}) custom-call(f32[32,128]{1,0:T(8,128)S(1)} %get-tuple-element.36.refs_0_, f32[56,128]{1,0:T(8,128)S(1)} %get-tuple-element.37.refs_1_, f32[88,128]{1,0:T(8,128)S(1)} %collective-permute-done.3.refs_2_, f32[88,128]{1,0:T(8,128)S(1)} %collective-permute-done.4.refs_3_, ...), custom_call_target="tpu_custom_call" | custom-call | tf_op jit(solution)/shard_map/pallas_call | solution.py:505
  25.4 0.0 collective-permute-done.7.refs_6_
  25.4 0.0 collective-permute-done.8.refs_7_
  25.4 0.0 collective-permute-done.9.refs_8_
  25.4 0.0 copy-start.1
  25.4 1.5 %shard_map.144 = (f32[16,384]{1,0:T(8,128)S(1)}, bf16[8,32,384]{2,1,0:T(8,128)(2,1)S(1)}, f32[8,16,128]{2,1,0:T(8,128)S(1)}) custom-call(s32[1]{0:T(128)} %bitcast.pos_ref, s32[1]{0:T(128)} %bitcast.1.lev_ref, f32[16,32]{1,0:T(8,128)S(1)} %copy-done.5, bf16[8,32,640]{2,1,0:T(8,128)(2,1)S(1)} %get-tuple-element.42.slots_ref.early_ref, ...), custom_call_target="tpu_custom_call" | custom-call | tf_op jit(solution)/shard_map/pallas_call | solution.py:511
  26.9 0.0 collective-permute-start.10
  26.9 1.5 %shard_map.145 = (f32[16,1024]{1,0:T(8,128)}, f32[16,1024]{1,0:T(8,128)}) custom-call(s32[1]{0:T(128)} %bitcast.pos_ref, s32[1]{0:T(128)} %bitcast.1.lev_ref, bf16[8,32,640]{2,1,0:T(8,128)(2,1)S(1)} %get-tuple-element.42.slots_ref.early_ref, bf16[8,32,384]{2,1,0:T(8,128)(2,1)S(1)} %get-tuple-element.47.late_ref, ...), custom_call_target="tpu_custom_call" | custom-call | tf_op jit(solution)/shard_map/pallas_call | solution.py:516
  28.5 0.0 collective-permute-done.10.theirs_ref
  28.5 0.0 copy-done.1
  28.5 1.5 %shard_map.146 = f32[16,40,256]{2,1,0:T(8,128)} custom-call(s32[1]{0:T(128)} %bitcast.1.lev_ref, bf16[16,40,256]{2,1,0:T(8,128)(2,1)S(1)} %copy-done, bf16[16,40,256]{2,1,0:T(8,128)(2,1)S(1)} %collective-permute-done.1.other_ref, f32[16,40,256]{2,1,0:T(8,128)S(1)} %copy-done.1, f32[16,384]{1,0:T(8,128)S(1)} %get-tuple-element.52.mine_ref, ...), custom_call_target="tpu_custom_call" | custom-call | tf_op jit(solution)/shard_map/pallas_call | solution.py:537
  (8 shorter events, 0.0 us)
Async XLA Ops:
  0.6 3.0 %collective-permute-start = (f32[16,40,256]{2,1,0:T(8,128)}, f32[16,40,256]{2,1,0:T(8,128)S(1)}, u32[]{:S(2)}, u32[]{:S(2)}) collective-permute-start(f32[16,40,256]{2,1,0:T(8,128)} %control_ref.1), channel_id=1, source_target_pairs={{0,1},{1,0},{2,3},{3,2},{4,5},{5,4},{6,7},{7,6},{8,9},{9,8},{10,11... | collective-permute-start | bytes 1966088 | tf_op jit(solution)/shard_map/ppermute | solution.py:460
  1.1 3.9 %collective-permute-start.1 = (bf16[16,40,256]{2,1,0:T(8,128)(2,1)}, bf16[16,40,256]{2,1,0:T(8,128)(2,1)S(1)}, u32[]{:S(2)}, u32[]{:S(2)}) collective-permute-start(bf16[16,40,256]{2,1,0:T(8,128)(2,1)} %perturb_ref.3), channel_id=1, source_target_pairs={{0,1},{1,0},{2,3},{3,2},{4,5},{5,4},{6,7},{7,6},{8,9},{9,8},{10,11... | collective-permute-start | bytes 983048 | tf_op jit(solution)/shard_map/ppermute | solution.py:461
  1.2 2.4 %copy-start = (bf16[16,40,256]{2,1,0:T(8,128)(2,1)S(1)}, bf16[16,40,256]{2,1,0:T(8,128)(2,1)}, u32[]{:S(2)}) copy-start(bf16[16,40,256]{2,1,0:T(8,128)(2,1)} %perturb_ref.3) | copy-start | bytes 983044
  1.2 2.4 %copy-start.5 = (f32[16,32]{1,0:T(8,128)S(1)}, f32[16,32]{1,0:T(8,128)}, u32[]{:S(2)}) copy-start(f32[16,32]{1,0:T(8,128)} %loc_ref.3) | copy-start | bytes 6148
  3.5 4.5 %copy-start.2 = (f32[16,1024]{1,0:T(8,128)S(1)}, f32[16,1024]{1,0:T(8,128)}, u32[]{:S(2)}) copy-start(f32[16,1024]{1,0:T(8,128)} %static_ref.3) | copy-start | bytes 196612
  3.6 4.5 %copy-start.3 = (f32[16,1024]{1,0:T(8,128)S(1)}, f32[16,1024]{1,0:T(8,128)}, u32[]{:S(2)}) copy-start(f32[16,1024]{1,0:T(8,128)} %obs_ref.3) | copy-start | bytes 196612
  3.6 4.5 %copy-start.4 = (f32[16,1024]{1,0:T(8,128)S(1)}, f32[16,1024]{1,0:T(8,128)}, u32[]{:S(2)}) copy-start(f32[16,1024]{1,0:T(8,128)} %innov_ref.3) | copy-start | bytes 196612
  3.6 0.8 %copy-start.6 = (f32[16,256]{1,0:T(8,128)S(1)}, f32[16,256]{1,0:T(8,128)}, u32[]{:S(2)}) copy-start(f32[16,256]{1,0:T(8,128)} %shard_map.139.part_ref) | copy-start | bytes 49156
  4.4 3.7 %copy-start.9 = (s32[1,8,128]{2,1,0:T(8,128)S(1)}, s32[1,8,128]{2,1,0:T(8,128)}, u32[]{:S(2)}) copy-start(s32[1,8,128]{2,1,0:T(8,128)} %src_ref.1) | copy-start | bytes 12292
  4.4 3.7 %copy-start.10 = (f32[1,8,128]{2,1,0:T(8,128)S(1)}, f32[1,8,128]{2,1,0:T(8,128)}, u32[]{:S(2)}) copy-start(f32[1,8,128]{2,1,0:T(8,128)} %weight_ref.1) | copy-start | bytes 12292
  4.4 3.7 %copy-start.11 = (s32[1,8,128]{2,1,0:T(8,128)S(1)}, s32[1,8,128]{2,1,0:T(8,128)}, u32[]{:S(2)}) copy-start(s32[1,8,128]{2,1,0:T(8,128)} %tgt_ref.1) | copy-start | bytes 12292
  5.1 4.8 %collective-permute-start.2 = (f32[16,256]{1,0:T(8,128)S(1)}, f32[16,256]{1,0:T(8,128)S(1)}, u32[]{:S(2)}, u32[]{:S(2)}) collective-permute-start(f32[16,256]{1,0:T(8,128)S(1)} %shard_map.140.refs_0_), channel_id=1, source_target_pairs={{0,16},{16,0},{1,17},{17,1},{2,18},{18,2},{3,19},{19,3},{4,20},{20... | collective-permute-start | bytes 49160 | tf_op jit(solution)/shard_map/ppermute | solution.py:485
  8.0 0.7 %copy-start.8 = (f32[1024]{0:T(1024)S(1)}, f32[1024]{0:T(1024)}, u32[]{:S(2)}) copy-start(f32[1024]{0:T(1024)} %param.17) | copy-start | bytes 12292
  8.0 0.7 %copy-start.7 = (f32[1024]{0:T(1024)S(1)}, f32[1024]{0:T(1024)}, u32[]{:S(2)}) copy-start(f32[1024]{0:T(1024)} %param.16) | copy-start | bytes 12292
  8.0 0.7 %copy-start.12 = (s32[1,8]{1,0:T(1,128)S(1)}, s32[1,8]{1,0:T(1,128)}, u32[]{:S(2)}) copy-start(s32[1,8]{1,0:T(1,128)} %counts_ref.1) | copy-start | bytes 100
  9.9 8.5 %collective-permute-start.3 = (f32[88,128]{1,0:T(8,128)S(1)}, f32[88,128]{1,0:T(8,128)S(1)}, u32[]{:S(2)}, u32[]{:S(2)}) collective-permute-start(f32[88,128]{1,0:T(8,128)S(1)} %get-tuple-element.38), channel_id=1, source_target_pairs={{0,12},{1,13},{2,14},{3,15},{4,8},{5,9},{6,10},{7,11},{8,4},{9,5},... | collective-permute-start | bytes 135176 | tf_op jit(solution)/shard_map/ppermute | solution.py:498
  14.0 7.1 %collective-permute-start.4 = (f32[88,128]{1,0:T(8,128)S(1)}, f32[88,128]{1,0:T(8,128)S(1)}, u32[]{:S(2)}, u32[]{:S(2)}) collective-permute-start(f32[88,128]{1,0:T(8,128)S(1)} %get-tuple-element.39), channel_id=1, source_target_pairs={{0,8},{1,5},{2,10},{3,7},{4,12},{5,1},{6,14},{7,3},{8,0},{9,13},{1... | collective-permute-start | bytes 135176 | tf_op jit(solution)/shard_map/ppermute | solution.py:498
  14.0 8.7 %collective-permute-start.5 = (f32[88,128]{1,0:T(8,128)S(1)}, f32[88,128]{1,0:T(8,128)S(1)}, u32[]{:S(2)}, u32[]{:S(2)}) collective-permute-start(f32[88,128]{1,0:T(8,128)S(1)} %get-tuple-element.40), channel_id=1, source_target_pairs={{0,10},{1,7},{2,8},{3,5},{4,14},{5,3},{6,12},{7,1},{8,2},{9,15},{1... | collective-permute-start | bytes 135176 | tf_op jit(solution)/shard_map/ppermute | solution.py:498
  17.9 6.7 %collective-permute-start.6 = (f32[88,128]{1,0:T(8,128)S(1)}, f32[88,128]{1,0:T(8,128)S(1)}, u32[]{:S(2)}, u32[]{:S(2)}) collective-permute-start(f32[88,128]{1,0:T(8,128)S(1)} %get-tuple-element.41), channel_id=1, source_target_pairs={{0,14},{1,15},{2,12},{3,13},{4,10},{5,11},{6,8},{7,9},{8,6},{9,7},... | collective-permute-start | bytes 135176 | tf_op jit(solution)/shard_map/ppermute | solution.py:498
  17.9 7.5 %collective-permute-start.7 = (f32[88,128]{1,0:T(8,128)S(1)}, f32[88,128]{1,0:T(8,128)S(1)}, u32[]{:S(2)}, u32[]{:S(2)}) collective-permute-start(f32[88,128]{1,0:T(8,128)S(1)} %get-tuple-element.44), channel_id=1, source_target_pairs={{0,4},{1,9},{2,6},{3,11},{4,0},{5,13},{6,2},{7,15},{8,12},{9,1},{1... | collective-permute-start | bytes 135176 | tf_op jit(solution)/shard_map/ppermute | solution.py:498
  18.4 7.0 %collective-permute-start.8 = (f32[88,128]{1,0:T(8,128)S(1)}, f32[88,128]{1,0:T(8,128)S(1)}, u32[]{:S(2)}, u32[]{:S(2)}) collective-permute-start(f32[88,128]{1,0:T(8,128)S(1)} %get-tuple-element.45), channel_id=1, source_target_pairs={{0,6},{1,11},{2,4},{3,9},{4,2},{5,15},{6,0},{7,13},{8,14},{9,3},{1... | collective-permute-start | bytes 135176 | tf_op jit(solution)/shard_map/ppermute | solution.py:498
  21.0 4.4 %collective-permute-start.9 = (f32[88,128]{1,0:T(8,128)S(1)}, f32[88,128]{1,0:T(8,128)S(1)}, u32[]{:S(2)}, u32[]{:S(2)}) collective-permute-start(f32[88,128]{1,0:T(8,128)S(1)} %get-tuple-element.46), channel_id=1, source_target_pairs={{0,2},{1,3},{2,0},{3,1},{4,6},{5,7},{6,4},{7,5},{8,10},{9,11},{10,... | collective-permute-start | bytes 135176 | tf_op jit(solution)/shard_map/ppermute | solution.py:498
  25.4 3.1 %copy-start.1 = (f32[16,40,256]{2,1,0:T(8,128)S(1)}, f32[16,40,256]{2,1,0:T(8,128)}, u32[]{:S(2)}) copy-start(f32[16,40,256]{2,1,0:T(8,128)} %control_ref.1) | copy-start | bytes 1966084
  26.9 1.5 %collective-permute-start.10 = (f32[16,384]{1,0:T(8,128)S(1)}, f32[16,384]{1,0:T(8,128)S(1)}, u32[]{:S(2)}, u32[]{:S(2)}) collective-permute-start(f32[16,384]{1,0:T(8,128)S(1)} %get-tuple-element.52.mine_ref), channel_id=1, source_target_pairs={{0,1},{1,0},{2,3},{3,2},{4,5},{5,4},{6,7},{7,6},{8,9},{9,8},{10,11... | collective-permute-start | bytes 73736 | tf_op jit(solution)/shard_map/ppermute | solution.py:536

commit v8 on v7

--- a/solution.py
+++ b/solution.py
@@ -87,23 +87,26 @@
 
 
 def own_kernel(lev_ref, perturb_hbm, control_hbm, loc_hbm, part_ref, perturb_ref, control_ref, loc_ref, sems):
-    staged = [(loc_hbm, loc_ref), (control_hbm, control_ref), (perturb_hbm, perturb_ref)]
+    levels, members, _ = perturb_ref.shape
+    tiles = [slice(m, m + SUB) for m in range(0, members, SUB)]
+    staged = [(loc_hbm, loc_ref), (perturb_hbm, perturb_ref)]
+    staged += [(control_hbm.at[:, tile, :], control_ref.at[:, tile, :]) for tile in tiles]
     copies = [pltpu.make_async_copy(source, target, sems.at[i]) for i, (source, target) in enumerate(staged)]
     for copy in copies:
         copy.start()
-    levels = perturb_ref.shape[0]
     copies[0].wait()
     weights = spread(loc_ref[...], lev_ref[0] * levels, levels)
     copies[1].wait()
-    copies[2].wait()
-    part_ref[...] = mixed_sum(weights, perturb_ref, control_ref)
-
-
-def mixed_sum(weights, perturb_ref, control_ref):
+    part_ref[...] = mixed_sum(weights, perturb_ref, control_ref, [copy.wait for copy in copies[2:]])
+
+
+def mixed_sum(weights, perturb_ref, control_ref, waits=()):
     levels, members, cols = perturb_ref.shape
     perturb = perturb_ref[...].astype(F32)
     total = jnp.zeros((levels, SUB, cols), F32)
-    for m in range(0, members, SUB):
+    for i, m in enumerate(range(0, members, SUB)):
+        if waits:
+            waits[i]()
         tile = control_ref[:, m : m + SUB, :].reshape(levels * SUB, cols)
         total = total + perturb[:, m : m + SUB, :] * mix(weights, tile).reshape(levels, SUB, cols)
     return jnp.sum(total, axis=1)
@@ -190,7 +193,7 @@
     grad_ref[...] = partial_ref[...] + (jnp.where(lane == 0, before, 0.0) + jnp.where(lane == cols - 1, after, 0.0))
 
 
-def ens_kernel(lev_ref, perturb_ref, other_ref, control_ref, mine_ref, theirs_ref, out_ref):
+def ens_kernel(lev_ref, perturb_ref, other_ref, control_ref, mine_ref, theirs_ref, out_hbm, out_ref, sems):
     levels, members, cols = perturb_ref.shape
     mine, theirs = mine_ref[...], theirs_ref[...]
     loc = jnp.concatenate([mine[:, cols : cols + 2 * levels], theirs[:, cols : cols + 2 * levels]], axis=0)
@@ -211,10 +214,16 @@
     perturb = perturb_ref[...].astype(F32)
     other = other_ref[...].astype(F32)
     grad = jnp.concatenate([mine[:, :cols], theirs[:, :cols]], axis=0)[:, None, :]
-    for m in range(0, members, SUB):
+    copies = []
+    for i, m in enumerate(range(0, members, SUB)):
         tile = jnp.concatenate([perturb[:, m : m + SUB, :], other[:, m : m + SUB, :]], axis=0) * grad
         mixed = mix(weights, tile.reshape(full * SUB, cols)).reshape(levels, SUB, cols)
-        out_ref[:, m : m + SUB, :] = control_ref[:, m : m + SUB, :] + mixed
+        place = (slice(None), slice(m, m + SUB), slice(None))
+        out_ref[place] = control_ref[place] + mixed
+        copies.append(pltpu.make_async_copy(out_ref.at[place], out_hbm.at[place], sems.at[i]))
+        copies[-1].start()
+    for copy in copies:
+        copy.wait()
 
 
 def relabel(r, n, lev):
@@ -335,36 +344,70 @@
     return met[: block.levels] + met[block.levels :]
 
 
-def open_blocks(order, counts, refs, n, levels, band):
-    blocks = {}
-    for r, count in zip(order, counts):
-        blocks[r] = Block(refs[:count], n, levels, band)
-        refs = refs[count:]
-    return blocks, refs
-
-
-def early_kernel(n, levels, band, first, counts, *refs):
-    blocks, (slots_ref, met_ref) = open_blocks(first, counts, refs, n, levels, band)
-    fill_slots(first, blocks, n, slots_ref)
-    for i, d in enumerate(first):
-        met_ref[i] = met_at(d, blocks[d], first, slots_ref)
-
-
-def shared_kernel(n, cols, first, second, counts, pos_ref, lev_ref, loc_ref, slots_ref, met_ref, *refs):
+def land(table, bands, slots_ref, cols):
+    cap = table.shape[1]
+    row = lax.broadcasted_iota(jnp.int32, (cols, cap), 0).astype(F32)
+    total = 0.0
+    for i, s in enumerate(bands):
+        landing = jnp.where(row == line(table, s), 1.0, 0.0).astype(BF16)
+        total = total + product(slots_ref[0, :, i * cap : (i + 1) * cap], landing, ((1,), (1,)))
+    levels = total.shape[0] // 2
+    return total[:levels] + total[levels:]
+
+
+def open_blocks(labels, refs, n, levels, band):
+    blocks = {0: Block(refs[:2], n, levels, band)}
+    refs = refs[2:]
+    for i, r in enumerate(labels[1:]):
+        blocks[r] = Block(refs[i : i + 1], n, levels, band)
+    return blocks, refs[len(labels) - 1 :]
+
+
+def stage_kernel(n, levels, band, cols, stages, *refs):
+    known = sum(stages[:-1], [])
+    blocks, refs = open_blocks(known + stages[-1], refs, n, levels, band)
+    old, refs = refs[: len(stages) - 1], refs[len(stages) - 1 :]
+    if known:
+        met_old, remap_old, slots_ref, met_ref, remap_ref = refs
+    else:
+        slots_ref, met_ref, remap_ref, pick_ref = refs
+        for d in range(n):
+            pick_ref[d] = pick_source(blocks[0], d)
+    fill_slots(stages[-1], blocks, n, slots_ref)
+    for i, (d, block) in enumerate(blocks.items()):
+        met = met_at(d, block, stages[-1], slots_ref)
+        if d in known:
+            met = met + met_old[i]
+        else:
+            for bands, ref in zip(stages, old):
+                met = met + met_at(d, block, bands, ref)
+        met_ref[i] = met
+    landed = land(blocks[0].tgt, stages[-1], slots_ref, cols)
+    remap_ref[...] = landed + remap_old[...] if known else landed
+
+
+def shared_kernel(n, cols, stages, pos_ref, lev_ref, loc_ref, *refs):
     levels = loc_ref.shape[0]
     band = refs[-3].shape[1] - 128
-    blocks, (out_ref, late_ref, tables_ref) = open_blocks(first + second, counts, refs, n, levels, band)
+    known = sum(stages[:-1], [])
+    blocks, refs = open_blocks(known + stages[-1], refs, n, levels, band)
+    old, refs = refs[: len(stages) - 1], refs[len(stages) - 1 :]
+    met_old, pick_ref, out_ref, slots_ref, tables_ref = refs
     me = pos_ref[0]
     for r, block in blocks.items():
         there = me ^ relabel(r, n, lev_ref[0])
         tables_ref[there, :n, :] = block.tgt
         tables_ref[there, n:, :] = block.rest(block.rows.edge, EXTRA)
-    fill_slots(second, blocks, n, late_ref)
+    fill_slots(stages[-1], blocks, n, slots_ref)
     last = cols - 1.0
     total = jnp.zeros((levels, band), F32)
-    for d, block in blocks.items():
-        value = met_at(d, block, second, late_ref) + block.rest(levels, levels)
-        value = value + (met_ref[first.index(d)] if d in first else met_at(d, block, first, slots_ref))
+    for i, (d, block) in enumerate(blocks.items()):
+        value = met_at(d, block, stages[-1], slots_ref) + block.rest(levels, levels)
+        if d in known:
+            value = value + met_old[i]
+        else:
+            for bands, ref in zip(stages, old):
+                value = value + met_at(d, block, bands, ref)
         edge = block.rest(block.rows.edge, 1)
         own = line(block.tgt, d)
         there = me ^ relabel(d, n, lev_ref[0])
@@ -375,25 +418,22 @@
         near = jnp.where((own == last) & (there < n - 1), edge[:, 6 * levels : 6 * levels + 1], 0.0)
         value = value + row_as_column(after, levels, levels) * near
         given = block.rest(0, levels) * value * line(blocks[0].factor, d)
-        total = total + select(given, pick_source(blocks[0], d), ((1,), (1,)))
+        total = total + select(given, pick_ref[d], ((1,), (1,)))
     out_ref[:, :band] = total
     out_ref[:, band:] = jnp.concatenate([loc_ref[...], jnp.zeros((levels, 128 - loc_ref.shape[1]), F32)], axis=1)
 
 
-def outputs_kernel(first, second, pos_ref, lev_ref, early_ref, late_ref, tables_ref, static_ref, diag_ref, off_ref, obs_ref, innov_ref,
-                   increment_ref, grad_ref):
+def outputs_kernel(stages, pos_ref, lev_ref, *refs):
+    slots_refs, refs = refs[: len(stages)], refs[len(stages) :]
+    remap_ref, tables_ref, static_ref, diag_ref, off_ref, obs_ref, innov_ref, increment_ref, grad_ref = refs
     levels, cols = static_ref.shape
     n = tables_ref.shape[0]
     cap = tables_ref.shape[2]
     me = pos_ref[0]
-    row = lax.broadcasted_iota(jnp.int32, (cols, cap), 0).astype(F32)
-    remapped = jnp.zeros((2 * levels, cols), F32)
-    given = [(s, ref, slice(i * cap, (i + 1) * cap)) for bands, ref in ((first, early_ref), (second, late_ref))
-             for i, s in enumerate(bands)]
-    for s, ref, place in given:
-        landing = jnp.where(row == tables_ref[me, s : s + 1, :], 1.0, 0.0).astype(BF16)
-        remapped = remapped + product(ref[0, :, place], landing, ((1,), (1,)))
-    remapped = remapped[:levels] + remapped[levels:]
+    given = [
+        (s, ref, slice(i * cap, (i + 1) * cap)) for bands, ref in zip(stages, slots_refs) for i, s in enumerate(bands)
+    ]
+    remapped = remap_ref[...] + land(tables_ref[me, :n, :], stages[-1], slots_refs[-1], cols)
     static, off = static_ref[...], off_ref[...]
     lane = lax.broadcasted_iota(jnp.int32, (levels, cols), 1)
 
@@ -423,12 +463,12 @@
     grad_ref[...] = static + diag_ref[...] * misfit + left + right
 
 
-def call(kernel, out_shape, spaces, scratch=(), limit=40 * MIB):
+def call(kernel, out_shape, spaces, scratch=(), limit=40 * MIB, out=VMEM):
     return pl.pallas_call(
         kernel,
         out_shape=out_shape,
         in_specs=spaces,
-        out_specs=jax.tree.map(lambda _: VMEM, out_shape),
+        out_specs=jax.tree.map(lambda _: out, out_shape),
         scratch_shapes=scratch,
         compiler_params=pltpu.CompilerParams(vmem_limit_bytes=limit),
     )
@@ -463,13 +503,13 @@
         own_kernel,
         shape((levels, band_cols), F32),
         [SMEM] + [HBM] * 3,
-        [pltpu.VMEM(a.shape, a.dtype) for a in (perturb, control, level_loc)] + [pltpu.SemaphoreType.DMA((3,))],
+        [pltpu.VMEM(a.shape, a.dtype) for a in (perturb, control, level_loc)] + [pltpu.SemaphoreType.DMA((2 + members // SUB,))],
         limit=58 * MIB,
     )(lev, perturb, control, level_loc)
     flat = shape((levels, tile_cols), F32)
     mine_shape = shape((levels, band_cols + 128), F32)
     diag, off = filter_diag.reshape(1, -1), filter_off.reshape(1, -1)
-    if n * cap <= tile_cols and n >= 4 and lax.axis_size("lev") == 2 and n & (n - 1) == 0 and band_cols * tile_cols <= 2**20:
+    if n * cap <= tile_cols and n >= 8 and lax.axis_size("lev") == 2 and n & (n - 1) == 0 and band_cols * tile_cols <= 2**20:
         rows = Rows(levels, n)
         stacked = band_cols // cap * levels
         rests = call(functools.partial(static_kernel, band_cols), [shape((rows.total, cap), F32)] * n, [SMEM] * 3 + [VMEM] * 8)(
@@ -488,34 +528,42 @@
             [shape((stacked, cap), F32)] + [shape((stacked + rows.total, cap), F32)] * (n - 1),
             [VMEM] * (groups + n - 1),
         )(*sums, *rests[1:])
-        first = sorted(range(n // 2, n), key=lambda r: (relabel(r, n, 1) != r, r))
-        first = first[: n // 4 // 2] + first[n // 4 :] + first[n // 4 // 2 : n // 4]
-        second = [*range(2, n // 2), *range(1, min(2, n // 2))]
+        far = sorted(range(n // 2, n), key=lambda r: (relabel(r, n, 1) != r, r))
+        far = far[: n // 4 // 2] + far[n // 4 :] + far[n // 4 // 2 : n // 4]
+        stages = [[0] + far, list(range(2, n // 2)), [1]]
         levs = lax.axis_size("lev")
-        arrived = {0: (total, rests[0])}
-        for r in first + second:
+        arrived = {0: [total, rests[0]]}
+        for r in sum(stages, [])[1:]:
             pairs = [(i * levs + v, (i ^ relabel(r, n, v)) * levs + v) for i in range(n) for v in range(levs)]
-            arrived[r] = (lax.ppermute(blocks[r - 1], ("tile", "lev"), pairs),)
-        first = [0] + first
-
-        def taken(order):
-            return tuple(len(arrived[r]) for r in order), [ref for r in order for ref in arrived[r]]
-
-        counts_first, refs_first = taken(first)
-        slots, met = call(
-            functools.partial(early_kernel, n, levels, band_cols, first, counts_first),
-            (shape((n, 2 * levels, len(first) * cap), BF16), shape((len(first), levels, cap), F32)),
-            [VMEM] * len(refs_first),
-        )(*refs_first)
-        counts_all, refs_all = taken(first + second)
-        mine, late, tables = call(
-            functools.partial(shared_kernel, n, tile_cols, first, second, counts_all),
-            (mine_shape, shape((n, 2 * levels, len(second) * cap), BF16), shape((n, n + EXTRA, cap), F32)),
-            [SMEM] * 2 + [VMEM] * (3 + len(refs_all)),
-        )(pos, lev, level_loc, slots, met, *refs_all)
-        increment, grad_static = call(functools.partial(outputs_kernel, first, second), (flat, flat), [SMEM] * 2 + [VMEM] * 8)(
-            pos, lev, slots, late, tables, static_control, diag, off, obs_weight, innovation
-        )
+            arrived[r] = [lax.ppermute(blocks[r - 1], ("tile", "lev"), pairs)]
+        slots, carried, picks = [], [], []
+        for count in range(1, len(stages)):
+            labels = sum(stages[:count], [])
+            refs = [ref for r in labels for ref in arrived[r]]
+            outs = [
+                shape((n, 2 * levels, len(stages[count - 1]) * cap), BF16),
+                shape((len(labels), levels, cap), F32),
+                flat,
+            ] + [shape((n, band_cols, cap), BF16)] * (count == 1)
+            new, *carried = call(
+                functools.partial(stage_kernel, n, levels, band_cols, tile_cols, stages[:count]),
+                outs,
+                [VMEM] * (len(refs) + len(slots) + len(carried)),
+            )(*refs, *slots, *carried)
+            slots.append(new)
+            picks += carried[2:]
+            carried = carried[:2]
+        met, remap = carried
+        refs = [ref for r in sum(stages, []) for ref in arrived[r]] + slots + [met] + picks
+        mine, new, tables = call(
+            functools.partial(shared_kernel, n, tile_cols, stages),
+            (mine_shape, shape((n, 2 * levels, len(stages[-1]) * cap), BF16), shape((n, n + EXTRA, cap), F32)),
+            [SMEM] * 2 + [VMEM] * (1 + len(refs)),
+        )(pos, lev, level_loc, *refs)
+        slots.append(new)
+        increment, grad_static = call(
+            functools.partial(outputs_kernel, stages), (flat, flat), [SMEM] * 2 + [VMEM] * (len(slots) + 7)
+        )(pos, lev, *slots, remap, tables, static_control, diag, off, obs_weight, innovation)
     else:
         payload = call(
             band_kernel,
@@ -534,7 +582,13 @@
             pos, counts, returned, send_src, send_wt, partial, level_loc
         )
     theirs = lax.ppermute(mine, "lev", swap)
-    grad_ens = call(ens_kernel, shape(control.shape, F32), [SMEM] + [VMEM] * 5)(
+    grad_ens = call(
+        ens_kernel,
+        shape(control.shape, F32),
+        [SMEM] + [VMEM] * 5,
+        [pltpu.VMEM(control.shape, F32), pltpu.SemaphoreType.DMA((members // SUB,))],
+        out=HBM,
+    )(
         lev, perturb, other_perturb, control, mine, theirs
     )
     return (increment, grad_static, grad_ens)

time: 30.3 us -> 30.9 us (1.020)
  Pallas kernels: 9.41 us -> 9.86 us
    pallas_call x1, Pallas kernels: 2.3 us -> 2.93 us  [body(): call(own_kernel, shape((levels, band_cols), F32), [SMEM] + [HBM] * 3, [pl...]
    pallas_call x4 -> x5, Pallas kernels: 5.3 us -> 5.11 us  [the longest x2 1.87 us: body(): call(functools.partial(stage_kernel, n, levels, band_cols, tile_cols, sta...]
  transfers between devices with their start and end apart: 11 -> 11, of which waited for: 2 -> 3; matrix products, arithmetic and copies ran while one was open for 0% -> 0% of each run, Pallas kernels for 21% -> 25%
where the time goes in v8:
time: 30.9 us; the launch traced here: 30.6 us
  starting transfers between devices  15 us (49%)
  Pallas kernels  9.86 us (32%)
  waiting for transfers between devices  3.51 us (11%)
  local copies, waits for them, and re-layouts  1.43 us (5%)
  between operations  0.8 us (3%)
    ppermute x7, starting transfers between devices, body(): arrived[r] = [lax.ppermute(blocks[r - 1], ('tile', 'lev'), pairs)]  11.5 us
    ppermute x7, waiting for transfers between devices, body(): arrived[r] = [lax.ppermute(blocks[r - 1], ('tile', 'lev'), pairs)]  3.26 us
    ppermute x1, starting transfers between devices, body(): lax.ppermute(sums[0], 'grp', [(g, (g + k) % groups) for g in range(groups)])  2.98 us
    pallas_call x1, Pallas kernels, body(): call(own_kernel, shape((levels, band_cols), F32), [SMEM] + [HBM] * 3, [pl...  2.93 us
    pallas_call x2, Pallas kernels, body(): call(functools.partial(stage_kernel, n, levels, band_cols, tile_cols, sta...  1.87 us
    unnamed x26, local copies, waits for them, and re-layouts  1.43 us
    pallas_call x1, Pallas kernels, body(): call(ens_kernel, shape(control.shape, F32), [SMEM] + [VMEM] * 5, [pltpu.V...  1.4 us
    pallas_call x1, Pallas kernels, body(): call(functools.partial(static_kernel, band_cols), [shape((rows.total, cap...  1.11 us
  transfers between devices with their start and end apart: 11, of which 3 were waited for; matrix products, arithmetic and copies ran while one was open for 0% of the time, Pallas kernels for 25%

profile of v8, /device:TPU:0, one launch (start us, length us, event | category | flops | bytes accessed | tf_op | source)
XLA Modules:
  0.0 30.6 jit_solution(650266608196772792)
XLA Ops:
  0.6 0.5 %collective-permute-start = (f32[16,40,256]{2,1,0:T(8,128)}, f32[16,40,256]{2,1,0:T(8,128)S(1)}, u32[]{:S(2)}, u32[]{:S(2)}) collective-permute-start(f32[16,40,256]{2,1,0:T(8,128)} %control_ref.1), channel_id=1, source_target_pairs={{0,1},{1,0},{2,3},{3,2},{4,5},{5,4},{6,7},{7,6},{8,9},{9,8},{10,11... | collective-permute-start | bytes 1966088 | tf_op jit(solution)/shard_map/ppermute | solution.py:500
  1.1 0.1 collective-permute-start.1
  1.2 0.0 copy-start
  1.2 2.9 %shard_map.139.part_ref = f32[16,256]{1,0:T(8,128)} custom-call(s32[1]{0:T(128)} %bitcast.1.lev_ref, bf16[16,40,256]{2,1,0:T(8,128)(2,1)} %perturb_ref.3, f32[16,40,256]{2,1,0:T(8,128)} %control_ref.1, f32[16,32]{1,0:T(8,128)} %loc_ref.3), custom_call_target="tpu_custom_call" | custom-call | tf_op jit(solution)/shard_map/pallas_call | solution.py:502
  4.2 0.0 copy-start.2
  4.2 0.0 copy-start.3
  4.2 0.0 copy-start.4
  4.2 0.0 collective-permute-done.other_ref
  4.2 0.0 copy-done
  4.2 0.0 copy-done.5
  4.2 0.0 copy-start.6
  4.3 0.7 %copy-done.6 = f32[16,256]{1,0:T(8,128)S(1)} copy-done((f32[16,256]{1,0:T(8,128)S(1)}, f32[16,256]{1,0:T(8,128)}, u32[]{:S(2)}) %copy-start.6) | copy-done | bytes 16408
  5.0 0.7 %shard_map.140.refs_0_ = f32[16,256]{1,0:T(8,128)S(1)} custom-call(s32[1]{0:T(128)} %bitcast.1.lev_ref, bf16[16,40,256]{2,1,0:T(8,128)(2,1)S(1)} %copy-done, f32[16,40,256]{2,1,0:T(8,128)S(1)} %collective-permute-done.other_ref, f32[16,256]{1,0:T(8,128)S(1)} %copy-done.6, f32[16,32]{1,0:T(8,128)S(1)} %copy-done.5), custom_call_target="tpu_custom_call" | custom-call | tf_op jit(solution)/shard_map/pallas_call | solution.py:519
  5.7 0.0 collective-permute-done.1.other_ref
  5.7 3.0 %collective-permute-start.2 = (f32[16,256]{1,0:T(8,128)S(1)}, f32[16,256]{1,0:T(8,128)S(1)}, u32[]{:S(2)}, u32[]{:S(2)}) collective-permute-start(f32[16,256]{1,0:T(8,128)S(1)} %shard_map.140.refs_0_), channel_id=1, source_target_pairs={{0,16},{16,0},{1,17},{17,1},{2,18},{18,2},{3,19},{19,3},{4,20},{20... | collective-permute-start | bytes 49160 | tf_op jit(solution)/shard_map/ppermute | solution.py:525
  8.7 0.0 copy-done.2
  8.7 0.0 copy-done.3
  8.7 0.0 copy-done.4
  8.7 0.0 copy-done.9
  8.7 0.0 copy-done.10
  8.7 0.0 copy-done.11
  8.7 0.6 %copy-done.8 = f32[1024]{0:T(1024)S(1)} copy-done((f32[1024]{0:T(1024)S(1)}, f32[1024]{0:T(1024)}, u32[]{:S(2)}) %copy-start.8) | copy-done | bytes 4120
  9.4 0.0 copy-done.7
  9.4 0.0 copy-done.12
  9.4 1.1 %shard_map.141 = (f32[56,128]{1,0:T(8,128)S(1)}, f32[56,128]{1,0:T(8,128)S(1)}, f32[56,128]{1,0:T(8,128)S(1)}, f32[56,128]{1,0:T(8,128)S(1)}, f32[56,128]{1,0:T(...) custom-call(s32[1]{0:T(128)} %bitcast.pos_ref, s32[1]{0:T(128)} %bitcast.1.lev_ref, ...), custom_call_target="tpu_custom_call" | custom-call | tf_op jit(solution)/shard_map/pallas_call | solution.py:515
  10.5 0.0 collective-permute-done.2.refs_1_
  10.5 4.1 %collective-permute-start.3 = (f32[88,128]{1,0:T(8,128)S(1)}, f32[88,128]{1,0:T(8,128)S(1)}, u32[]{:S(2)}, u32[]{:S(2)}) collective-permute-start(f32[88,128]{1,0:T(8,128)S(1)} %get-tuple-element.43), channel_id=1, source_target_pairs={{0,12},{1,13},{2,14},{3,15},{4,8},{5,9},{6,10},{7,11},{8,4},{9,5},... | collective-permute-start | bytes 135176 | tf_op jit(solution)/shard_map/ppermute | solution.py:538
  14.6 0.0 collective-permute-start.4
  14.6 3.9 %collective-permute-start.5 = (f32[88,128]{1,0:T(8,128)S(1)}, f32[88,128]{1,0:T(8,128)S(1)}, u32[]{:S(2)}, u32[]{:S(2)}) collective-permute-start(f32[88,128]{1,0:T(8,128)S(1)} %get-tuple-element.45), channel_id=1, source_target_pairs={{0,10},{1,7},{2,8},{3,5},{4,14},{5,3},{6,12},{7,1},{8,2},{9,15},{1... | collective-permute-start | bytes 135176 | tf_op jit(solution)/shard_map/ppermute | solution.py:538
  18.5 0.0 collective-permute-start.6
  18.5 0.6 %collective-permute-start.7 = (f32[88,128]{1,0:T(8,128)S(1)}, f32[88,128]{1,0:T(8,128)S(1)}, u32[]{:S(2)}, u32[]{:S(2)}) collective-permute-start(f32[88,128]{1,0:T(8,128)S(1)} %get-tuple-element.48), channel_id=1, source_target_pairs={{0,4},{1,9},{2,6},{3,11},{4,0},{5,13},{6,2},{7,15},{8,12},{9,1},{1... | collective-permute-start | bytes 135176 | tf_op jit(solution)/shard_map/ppermute | solution.py:538
  19.1 0.0 collective-permute-done.3.refs_2_
  19.1 2.6 %collective-permute-start.8 = (f32[88,128]{1,0:T(8,128)S(1)}, f32[88,128]{1,0:T(8,128)S(1)}, u32[]{:S(2)}, u32[]{:S(2)}) collective-permute-start(f32[88,128]{1,0:T(8,128)S(1)} %get-tuple-element.49), channel_id=1, source_target_pairs={{0,6},{1,11},{2,4},{3,9},{4,2},{5,15},{6,0},{7,13},{8,14},{9,3},{1... | collective-permute-start | bytes 135176 | tf_op jit(solution)/shard_map/ppermute | solution.py:538
  21.7 0.0 collective-permute-done.4.refs_3_
  21.7 0.4 %collective-permute-start.9 = (f32[88,128]{1,0:T(8,128)S(1)}, f32[88,128]{1,0:T(8,128)S(1)}, u32[]{:S(2)}, u32[]{:S(2)}) collective-permute-start(f32[88,128]{1,0:T(8,128)S(1)} %get-tuple-element.53), channel_id=1, source_target_pairs={{0,2},{1,3},{2,0},{3,1},{4,6},{5,7},{6,4},{7,5},{8,10},{9,11},{10,... | collective-permute-start | bytes 135176 | tf_op jit(solution)/shard_map/ppermute | solution.py:538
  22.0 1.3 %collective-permute-done.5.refs_4_ = f32[88,128]{1,0:T(8,128)S(1)} collective-permute-done((f32[88,128]{1,0:T(8,128)S(1)}, f32[88,128]{1,0:T(8,128)S(1)}, u32[]{:S(2)}, u32[]{:S(2)}) %collective-permute-start.5) | collective-permute-done | bytes 45088 | tf_op jit(solution)/shard_map/ppermute | solution.py:538
  23.4 1.9 %collective-permute-done.6.refs_5_ = f32[88,128]{1,0:T(8,128)S(1)} collective-permute-done((f32[88,128]{1,0:T(8,128)S(1)}, f32[88,128]{1,0:T(8,128)S(1)}, u32[]{:S(2)}, u32[]{:S(2)}) %collective-permute-start.6) | collective-permute-done | bytes 45088 | tf_op jit(solution)/shard_map/ppermute | solution.py:538
  25.2 1.1 %shard_map.143 = (bf16[8,32,640]{2,1,0:T(8,128)(2,1)S(1)}, f32[5,16,128]{2,1,0:T(8,128)S(1)}, f32[16,1024]{1,0:T(8,128)S(1)}, bf16[8,256,128]{2,1,0:T(8,128)(2,1)S(1)}) custom-call(f32[32,128]{1,0:T(8,128)S(1)} %get-tuple-element.41.refs_0_, f32[56,128]{1,0:T(8,128)S(1)} %get-tuple-element.42.refs_1_, f32[88,128]{1,0:T(8,128)S(1)} %collective-permute-done.3.refs_2_, ...), custom_call_target="tpu_custom_call" | custom-call | tf_op jit(solution)/shard_map/pallas_call | solution.py:548
  26.4 0.0 collective-permute-done.7.refs_6_
  26.4 0.0 collective-permute-done.8.refs_7_
  26.4 0.8 %shard_map.144 = (bf16[8,32,256]{2,1,0:T(8,128)(2,1)S(1)}, f32[7,16,128]{2,1,0:T(8,128)S(1)}, f32[16,1024]{1,0:T(8,128)S(1)}) custom-call(f32[32,128]{1,0:T(8,128)S(1)} %get-tuple-element.41.refs_0_, f32[56,128]{1,0:T(8,128)S(1)} %get-tuple-element.42.refs_1_, f32[88,128]{1,0:T(8,128)S(1)} %collective-permute-done.3.refs_2_, ...), custom_call_target="tpu_custom_call" | custom-call | tf_op jit(solution)/shard_map/pallas_call | solution.py:548
  27.1 0.0 collective-permute-done.9.refs_8_
  27.1 0.9 %shard_map.145 = (f32[16,384]{1,0:T(8,128)S(1)}, bf16[8,32,128]{2,1,0:T(8,128)(2,1)S(1)}, f32[8,16,128]{2,1,0:T(8,128)S(1)}) custom-call(s32[1]{0:T(128)} %bitcast.pos_ref, s32[1]{0:T(128)} %bitcast.1.lev_ref, f32[16,32]{1,0:T(8,128)S(1)} %copy-done.5, f32[32,128]{1,0:T(8,128)S(1)} %get-tuple-element.41.refs_0_, f32[56,128]{1,0:T(8,128)S(1)} %get-tuple-element.42.refs_1_, ...), custom_call_target="tpu_custom_call" | custom-call | tf_op jit(solution)/shard_map/pallas_call | solution.py:558
  28.0 0.0 collective-permute-start.10
  28.0 1.0 %shard_map.146 = (f32[16,1024]{1,0:T(8,128)}, f32[16,1024]{1,0:T(8,128)}) custom-call(s32[1]{0:T(128)} %bitcast.pos_ref, s32[1]{0:T(128)} %bitcast.1.lev_ref, bf16[8,32,640]{2,1,0:T(8,128)(2,1)S(1)} %get-tuple-element.47.refs_8_.refs_9_.refs_0_, bf16[8,32,256]{2,1,0:T(8,128)(2,1)S(1)} %get-tuple-element.52.refs_10_.refs_1_, ...), custom_call_target="tpu_custom_call" | custom-call | tf_op jit(solution)/shard_map/pallas_call | solution.py:564
  29.0 0.2 collective-permute-done.10.theirs_ref
  29.2 0.0 copy-done.1
  29.2 1.4 %shard_map.147 = f32[16,40,256]{2,1,0:T(8,128)} custom-call(s32[1]{0:T(128)} %bitcast.1.lev_ref, bf16[16,40,256]{2,1,0:T(8,128)(2,1)S(1)} %copy-done, bf16[16,40,256]{2,1,0:T(8,128)(2,1)S(1)} %collective-permute-done.1.other_ref, f32[16,40,256]{2,1,0:T(8,128)S(1)} %copy-done.1, f32[16,384]{1,0:T(8,128)S(1)} %get-tuple-element.62.mine_ref, ...), custom_call_target="tpu_custom_call" | custom-call | tf_op jit(solution)/shard_map/pallas_call | solution.py:585
  (9 shorter events, 0.0 us)
Async XLA Ops:
  0.6 3.6 %collective-permute-start = (f32[16,40,256]{2,1,0:T(8,128)}, f32[16,40,256]{2,1,0:T(8,128)S(1)}, u32[]{:S(2)}, u32[]{:S(2)}) collective-permute-start(f32[16,40,256]{2,1,0:T(8,128)} %control_ref.1), channel_id=1, source_target_pairs={{0,1},{1,0},{2,3},{3,2},{4,5},{5,4},{6,7},{7,6},{8,9},{9,8},{10,11... | collective-permute-start | bytes 1966088 | tf_op jit(solution)/shard_map/ppermute | solution.py:500
  1.1 4.5 %collective-permute-start.1 = (bf16[16,40,256]{2,1,0:T(8,128)(2,1)}, bf16[16,40,256]{2,1,0:T(8,128)(2,1)S(1)}, u32[]{:S(2)}, u32[]{:S(2)}) collective-permute-start(bf16[16,40,256]{2,1,0:T(8,128)(2,1)} %perturb_ref.3), channel_id=1, source_target_pairs={{0,1},{1,0},{2,3},{3,2},{4,5},{5,4},{6,7},{7,6},{8,9},{9,8},{10,11... | collective-permute-start | bytes 983048 | tf_op jit(solution)/shard_map/ppermute | solution.py:501
  1.2 3.0 %copy-start = (bf16[16,40,256]{2,1,0:T(8,128)(2,1)S(1)}, bf16[16,40,256]{2,1,0:T(8,128)(2,1)}, u32[]{:S(2)}) copy-start(bf16[16,40,256]{2,1,0:T(8,128)(2,1)} %perturb_ref.3) | copy-start | bytes 983044
  1.2 3.0 %copy-start.5 = (f32[16,32]{1,0:T(8,128)S(1)}, f32[16,32]{1,0:T(8,128)}, u32[]{:S(2)}) copy-start(f32[16,32]{1,0:T(8,128)} %loc_ref.3) | copy-start | bytes 6148
  4.2 4.5 %copy-start.2 = (f32[16,1024]{1,0:T(8,128)S(1)}, f32[16,1024]{1,0:T(8,128)}, u32[]{:S(2)}) copy-start(f32[16,1024]{1,0:T(8,128)} %refs_5_.1) | copy-start | bytes 196612
  4.2 4.5 %copy-start.3 = (f32[16,1024]{1,0:T(8,128)S(1)}, f32[16,1024]{1,0:T(8,128)}, u32[]{:S(2)}) copy-start(f32[16,1024]{1,0:T(8,128)} %refs_8_.1) | copy-start | bytes 196612
  4.2 4.5 %copy-start.4 = (f32[16,1024]{1,0:T(8,128)S(1)}, f32[16,1024]{1,0:T(8,128)}, u32[]{:S(2)}) copy-start(f32[16,1024]{1,0:T(8,128)} %refs_9_.1) | copy-start | bytes 196612
  4.2 0.8 %copy-start.6 = (f32[16,256]{1,0:T(8,128)S(1)}, f32[16,256]{1,0:T(8,128)}, u32[]{:S(2)}) copy-start(f32[16,256]{1,0:T(8,128)} %shard_map.139.part_ref) | copy-start | bytes 49156
  5.0 3.7 %copy-start.9 = (s32[1,8,128]{2,1,0:T(8,128)S(1)}, s32[1,8,128]{2,1,0:T(8,128)}, u32[]{:S(2)}) copy-start(s32[1,8,128]{2,1,0:T(8,128)} %src_ref.1) | copy-start | bytes 12292
  5.0 3.7 %copy-start.10 = (f32[1,8,128]{2,1,0:T(8,128)S(1)}, f32[1,8,128]{2,1,0:T(8,128)}, u32[]{:S(2)}) copy-start(f32[1,8,128]{2,1,0:T(8,128)} %weight_ref.1) | copy-start | bytes 12292
  5.0 3.7 %copy-start.11 = (s32[1,8,128]{2,1,0:T(8,128)S(1)}, s32[1,8,128]{2,1,0:T(8,128)}, u32[]{:S(2)}) copy-start(s32[1,8,128]{2,1,0:T(8,128)} %tgt_ref.1) | copy-start | bytes 12292
  5.7 4.8 %collective-permute-start.2 = (f32[16,256]{1,0:T(8,128)S(1)}, f32[16,256]{1,0:T(8,128)S(1)}, u32[]{:S(2)}, u32[]{:S(2)}) collective-permute-start(f32[16,256]{1,0:T(8,128)S(1)} %shard_map.140.refs_0_), channel_id=1, source_target_pairs={{0,16},{16,0},{1,17},{17,1},{2,18},{18,2},{3,19},{19,3},{4,20},{20... | collective-permute-start | bytes 49160 | tf_op jit(solution)/shard_map/ppermute | solution.py:525
  8.7 0.7 %copy-start.8 = (f32[1024]{0:T(1024)S(1)}, f32[1024]{0:T(1024)}, u32[]{:S(2)}) copy-start(f32[1024]{0:T(1024)} %param.17) | copy-start | bytes 12292
  8.7 0.7 %copy-start.7 = (f32[1024]{0:T(1024)S(1)}, f32[1024]{0:T(1024)}, u32[]{:S(2)}) copy-start(f32[1024]{0:T(1024)} %param.16) | copy-start | bytes 12292
  8.7 0.7 %copy-start.12 = (s32[1,8]{1,0:T(1,128)S(1)}, s32[1,8]{1,0:T(1,128)}, u32[]{:S(2)}) copy-start(s32[1,8]{1,0:T(1,128)} %counts_ref.1) | copy-start | bytes 100
  10.5 8.5 %collective-permute-start.3 = (f32[88,128]{1,0:T(8,128)S(1)}, f32[88,128]{1,0:T(8,128)S(1)}, u32[]{:S(2)}, u32[]{:S(2)}) collective-permute-start(f32[88,128]{1,0:T(8,128)S(1)} %get-tuple-element.43), channel_id=1, source_target_pairs={{0,12},{1,13},{2,14},{3,15},{4,8},{5,9},{6,10},{7,11},{8,4},{9,5},... | collective-permute-start | bytes 135176 | tf_op jit(solution)/shard_map/ppermute | solution.py:538
  14.6 7.0 %collective-permute-start.4 = (f32[88,128]{1,0:T(8,128)S(1)}, f32[88,128]{1,0:T(8,128)S(1)}, u32[]{:S(2)}, u32[]{:S(2)}) collective-permute-start(f32[88,128]{1,0:T(8,128)S(1)} %get-tuple-element.44), channel_id=1, source_target_pairs={{0,8},{1,5},{2,10},{3,7},{4,12},{5,1},{6,14},{7,3},{8,0},{9,13},{1... | collective-permute-start | bytes 135176 | tf_op jit(solution)/shard_map/ppermute | solution.py:538
  14.6 8.7 %collective-permute-start.5 = (f32[88,128]{1,0:T(8,128)S(1)}, f32[88,128]{1,0:T(8,128)S(1)}, u32[]{:S(2)}, u32[]{:S(2)}) collective-permute-start(f32[88,128]{1,0:T(8,128)S(1)} %get-tuple-element.45), channel_id=1, source_target_pairs={{0,10},{1,7},{2,8},{3,5},{4,14},{5,3},{6,12},{7,1},{8,2},{9,15},{1... | collective-permute-start | bytes 135176 | tf_op jit(solution)/shard_map/ppermute | solution.py:538
  18.5 6.7 %collective-permute-start.6 = (f32[88,128]{1,0:T(8,128)S(1)}, f32[88,128]{1,0:T(8,128)S(1)}, u32[]{:S(2)}, u32[]{:S(2)}) collective-permute-start(f32[88,128]{1,0:T(8,128)S(1)} %get-tuple-element.46), channel_id=1, source_target_pairs={{0,14},{1,15},{2,12},{3,13},{4,10},{5,11},{6,8},{7,9},{8,6},{9,7},... | collective-permute-start | bytes 135176 | tf_op jit(solution)/shard_map/ppermute | solution.py:538
  18.5 7.9 %collective-permute-start.7 = (f32[88,128]{1,0:T(8,128)S(1)}, f32[88,128]{1,0:T(8,128)S(1)}, u32[]{:S(2)}, u32[]{:S(2)}) collective-permute-start(f32[88,128]{1,0:T(8,128)S(1)} %get-tuple-element.48), channel_id=1, source_target_pairs={{0,4},{1,9},{2,6},{3,11},{4,0},{5,13},{6,2},{7,15},{8,12},{9,1},{1... | collective-permute-start | bytes 135176 | tf_op jit(solution)/shard_map/ppermute | solution.py:538
  19.1 7.3 %collective-permute-start.8 = (f32[88,128]{1,0:T(8,128)S(1)}, f32[88,128]{1,0:T(8,128)S(1)}, u32[]{:S(2)}, u32[]{:S(2)}) collective-permute-start(f32[88,128]{1,0:T(8,128)S(1)} %get-tuple-element.49), channel_id=1, source_target_pairs={{0,6},{1,11},{2,4},{3,9},{4,2},{5,15},{6,0},{7,13},{8,14},{9,3},{1... | collective-permute-start | bytes 135176 | tf_op jit(solution)/shard_map/ppermute | solution.py:538
  21.7 5.5 %collective-permute-start.9 = (f32[88,128]{1,0:T(8,128)S(1)}, f32[88,128]{1,0:T(8,128)S(1)}, u32[]{:S(2)}, u32[]{:S(2)}) collective-permute-start(f32[88,128]{1,0:T(8,128)S(1)} %get-tuple-element.53), channel_id=1, source_target_pairs={{0,2},{1,3},{2,0},{3,1},{4,6},{5,7},{6,4},{7,5},{8,10},{9,11},{10,... | collective-permute-start | bytes 135176 | tf_op jit(solution)/shard_map/ppermute | solution.py:538
  28.0 1.2 %copy-start.1 = (f32[16,40,256]{2,1,0:T(8,128)S(1)}, f32[16,40,256]{2,1,0:T(8,128)}, u32[]{:S(2)}) copy-start(f32[16,40,256]{2,1,0:T(8,128)} %control_ref.1) | copy-start | bytes 1966084
  28.0 1.2 %collective-permute-start.10 = (f32[16,384]{1,0:T(8,128)S(1)}, f32[16,384]{1,0:T(8,128)S(1)}, u32[]{:S(2)}, u32[]{:S(2)}) collective-permute-start(f32[16,384]{1,0:T(8,128)S(1)} %get-tuple-element.62.mine_ref), channel_id=1, source_target_pairs={{0,1},{1,0},{2,3},{3,2},{4,5},{5,4},{6,7},{7,6},{8,9},{9,8},{10,11... | collective-permute-start | bytes 73736 | tf_op jit(solution)/shard_map/ppermute | solution.py:584

commit v9 on v8

--- a/solution.py
+++ b/solution.py
@@ -52,7 +52,9 @@
 
 def mix(weights, values):
     high, low = halves(values)
-    return product(weights[0], high) + (product(weights[0], low) + product(weights[1], high))
+    rows = weights[0].shape[0]
+    both = product(jnp.concatenate(weights, axis=0), high)
+    return both[:rows] + (product(weights[0], low) + both[rows:])
 
 
 def one_hot(index, size):
@@ -87,26 +89,23 @@
 
 
 def own_kernel(lev_ref, perturb_hbm, control_hbm, loc_hbm, part_ref, perturb_ref, control_ref, loc_ref, sems):
-    levels, members, _ = perturb_ref.shape
-    tiles = [slice(m, m + SUB) for m in range(0, members, SUB)]
-    staged = [(loc_hbm, loc_ref), (perturb_hbm, perturb_ref)]
-    staged += [(control_hbm.at[:, tile, :], control_ref.at[:, tile, :]) for tile in tiles]
+    staged = [(loc_hbm, loc_ref), (control_hbm, control_ref), (perturb_hbm, perturb_ref)]
     copies = [pltpu.make_async_copy(source, target, sems.at[i]) for i, (source, target) in enumerate(staged)]
     for copy in copies:
         copy.start()
+    levels = perturb_ref.shape[0]
     copies[0].wait()
     weights = spread(loc_ref[...], lev_ref[0] * levels, levels)
     copies[1].wait()
-    part_ref[...] = mixed_sum(weights, perturb_ref, control_ref, [copy.wait for copy in copies[2:]])
-
-
-def mixed_sum(weights, perturb_ref, control_ref, waits=()):
+    copies[2].wait()
+    part_ref[...] = mixed_sum(weights, perturb_ref, control_ref)
+
+
+def mixed_sum(weights, perturb_ref, control_ref):
     levels, members, cols = perturb_ref.shape
     perturb = perturb_ref[...].astype(F32)
     total = jnp.zeros((levels, SUB, cols), F32)
-    for i, m in enumerate(range(0, members, SUB)):
-        if waits:
-            waits[i]()
+    for m in range(0, members, SUB):
         tile = control_ref[:, m : m + SUB, :].reshape(levels * SUB, cols)
         total = total + perturb[:, m : m + SUB, :] * mix(weights, tile).reshape(levels, SUB, cols)
     return jnp.sum(total, axis=1)
@@ -276,10 +275,14 @@
         out_ref[rows.edge :, :] = edge
 
 
-def sum_kernel(lev_ref, perturb_ref, other_ref, part_ref, loc_ref, out_ref):
+def other_kernel(lev_ref, perturb_ref, other_ref, loc_ref, out_ref):
     levels = perturb_ref.shape[0]
     weights = spread(loc_ref[...], (1 - lev_ref[0]) * levels, levels)
-    out_ref[...] = part_ref[...] + mixed_sum(weights, perturb_ref, other_ref)
+    out_ref[...] = mixed_sum(weights, perturb_ref, other_ref)
+
+
+def add_kernel(a_ref, b_ref, out_ref):
+    out_ref[...] = a_ref[...] + b_ref[...]
 
 
 def blocks_kernel(groups, *refs):
@@ -503,7 +506,7 @@
         own_kernel,
         shape((levels, band_cols), F32),
         [SMEM] + [HBM] * 3,
-        [pltpu.VMEM(a.shape, a.dtype) for a in (perturb, control, level_loc)] + [pltpu.SemaphoreType.DMA((2 + members // SUB,))],
+        [pltpu.VMEM(a.shape, a.dtype) for a in (perturb, control, level_loc)] + [pltpu.SemaphoreType.DMA((3,))],
         limit=58 * MIB,
     )(lev, perturb, control, level_loc)
     flat = shape((levels, tile_cols), F32)
@@ -515,11 +518,10 @@
         rests = call(functools.partial(static_kernel, band_cols), [shape((rows.total, cap), F32)] * n, [SMEM] * 3 + [VMEM] * 8)(
             pos, lev, counts, static_control, diag, off, obs_weight, innovation, send_src, send_wt, recv_tgt
         )
-        sums = [
-            call(sum_kernel, shape((levels, band_cols), F32), [SMEM] + [VMEM] * 4)(
-                lev, perturb, other_control, part, level_loc
-            )
-        ]
+        other_part = call(other_kernel, shape((levels, band_cols), F32), [SMEM] + [VMEM] * 3)(
+            lev, perturb, other_control, level_loc
+        )
+        sums = [call(add_kernel, shape((levels, band_cols), F32), [VMEM] * 2)(part, other_part)]
         sums[0], other_perturb = lax.optimization_barrier((sums[0], other_perturb))
         for k in range(1, groups):
             sums.append(lax.ppermute(sums[0], "grp", [(g, (g + k) % groups) for g in range(groups)]))
@@ -528,9 +530,10 @@
             [shape((stacked, cap), F32)] + [shape((stacked + rows.total, cap), F32)] * (n - 1),
             [VMEM] * (groups + n - 1),
         )(*sums, *rests[1:])
-        far = sorted(range(n // 2, n), key=lambda r: (relabel(r, n, 1) != r, r))
-        far = far[: n // 4 // 2] + far[n // 4 :] + far[n // 4 // 2 : n // 4]
-        stages = [[0] + far, list(range(2, n // 2)), [1]]
+        low, high = n // 4, n // 2
+        both_far = [high + low + i for i in range(low)]
+        mixed = [r for i in reversed(range(low)) for r in (high + i, low + i)]
+        stages = [[0] + both_far + mixed[:low], mixed[low:], list(range(1, low))]
         levs = lax.axis_size("lev")
         arrived = {0: [total, rests[0]]}
         for r in sum(stages, [])[1:]:

time: 30.9 us -> 29 us (0.939)
  waiting for transfers between devices: 3.51 us -> 1.61 us
  starting transfers between devices: 15 us -> 16.4 us
  local copies, waits for them, and re-layouts: 1.43 us -> 0.7 us
  Pallas kernels: 9.86 us -> 9.27 us
    ppermute x7, waiting for transfers between devices: 3.26 us -> 1.35 us  [body(): arrived[r] = [lax.ppermute(blocks[r - 1], ('tile', 'lev'), pairs)]]
    ppermute x7, starting transfers between devices: 11.5 us -> 12.8 us  [body(): arrived[r] = [lax.ppermute(blocks[r - 1], ('tile', 'lev'), pairs)]]
    unnamed x26, local copies, waits for them, and re-layouts: 1.43 us -> 0.7 us
    pallas_call x1, Pallas kernels: 2.93 us -> 2.3 us  [body(): call(own_kernel, shape((levels, band_cols), F32), [SMEM] + [HBM] * 3, [pl...]
    pallas_call x1 -> x2, Pallas kernels: 0.68 us -> 0.69 us  [the longest x1 0.68 us: body(): call(other_kernel, shape((levels, band_cols), F32), [SMEM] + [VMEM] * 3)]
  transfers between devices with their start and end apart: 11 -> 11, of which waited for: 3 -> 3; matrix products, arithmetic and copies ran while one was open for 0% -> 0% of each run, Pallas kernels for 25% -> 24%
where the time goes in v9:
time: 29 us; the launch traced here: 28.8 us
  starting transfers between devices  16.4 us (57%)
  Pallas kernels  9.27 us (32%)
  waiting for transfers between devices  1.61 us (6%)
  between operations  0.83 us (3%)
  local copies, waits for them, and re-layouts  0.7 us (2%)
    ppermute x7, starting transfers between devices, body(): arrived[r] = [lax.ppermute(blocks[r - 1], ('tile', 'lev'), pairs)]  12.8 us
    ppermute x1, starting transfers between devices, body(): lax.ppermute(sums[0], 'grp', [(g, (g + k) % groups) for g in range(groups)])  2.98 us
    pallas_call x1, Pallas kernels, body(): call(own_kernel, shape((levels, band_cols), F32), [SMEM] + [HBM] * 3, [pl...  2.3 us
    pallas_call x2, Pallas kernels, body(): call(functools.partial(stage_kernel, n, levels, band_cols, tile_cols, sta...  1.9 us
    pallas_call x1, Pallas kernels, body(): call(ens_kernel, shape(control.shape, F32), [SMEM] + [VMEM] * 5, [pltpu.V...  1.41 us
    ppermute x7, waiting for transfers between devices, body(): arrived[r] = [lax.ppermute(blocks[r - 1], ('tile', 'lev'), pairs)]  1.35 us
    pallas_call x1, Pallas kernels, body(): call(functools.partial(static_kernel, band_cols), [shape((rows.total, cap...  1.1 us
    pallas_call x1, Pallas kernels, body(): call(functools.partial(outputs_kernel, stages), (flat, flat), [SMEM] * 2...  0.96 us
  transfers between devices with their start and end apart: 11, of which 3 were waited for; matrix products, arithmetic and copies ran while one was open for 0% of the time, Pallas kernels for 24%

profile of v9, /device:TPU:0, one launch (start us, length us, event | category | flops | bytes accessed | tf_op | source)
XLA Modules:
  0.0 28.8 jit_solution(5711102111675604975)
XLA Ops:
  0.6 0.5 %collective-permute-start = (f32[16,40,256]{2,1,0:T(8,128)}, f32[16,40,256]{2,1,0:T(8,128)S(1)}, u32[]{:S(2)}, u32[]{:S(2)}) collective-permute-start(f32[16,40,256]{2,1,0:T(8,128)} %control_ref.1), channel_id=1, source_target_pairs={{0,1},{1,0},{2,3},{3,2},{4,5},{5,4},{6,7},{7,6},{8,9},{9,8},{10,11... | collective-permute-start | bytes 1966088 | tf_op jit(solution)/shard_map/ppermute | solution.py:503
  1.1 0.1 collective-permute-start.1
  1.2 2.3 %shard_map.139.a_ref = f32[16,256]{1,0:T(8,128)} custom-call(s32[1]{0:T(128)} %bitcast.1.lev_ref, bf16[16,40,256]{2,1,0:T(8,128)(2,1)} %perturb_ref.3, f32[16,40,256]{2,1,0:T(8,128)} %control_ref.1, f32[16,32]{1,0:T(8,128)} %loc_ref.3), custom_call_target="tpu_custom_call" | custom-call | tf_op jit(solution)/shard_map/pallas_call | solution.py:505
  3.5 0.0 copy-start.6
  3.6 0.0 collective-permute-done.other_ref
  3.6 0.0 copy-done
  3.6 0.0 copy-done.5
  3.6 0.0 copy-start.2
  3.6 0.0 copy-start.3
  3.6 0.0 copy-start.4
  3.6 0.7 %shard_map.140.b_ref = f32[16,256]{1,0:T(8,128)S(1)} custom-call(s32[1]{0:T(128)} %bitcast.1.lev_ref, bf16[16,40,256]{2,1,0:T(8,128)(2,1)S(1)} %copy-done, f32[16,40,256]{2,1,0:T(8,128)S(1)} %collective-permute-done.other_ref, f32[16,32]{1,0:T(8,128)S(1)} %copy-done.5), custom_call_target="tpu_custom_call" | custom-call | tf_op jit(solution)/shard_map/pallas_call | solution.py:521
  4.3 0.0 copy-done.6
  4.3 0.0 copy-start.9
  4.3 0.0 copy-start.10
  4.3 0.0 copy-start.11
  4.4 0.0 collective-permute-done.1.other_ref
  4.4 3.0 %collective-permute-start.2 = (f32[16,256]{1,0:T(8,128)S(1)}, f32[16,256]{1,0:T(8,128)S(1)}, u32[]{:S(2)}, u32[]{:S(2)}) collective-permute-start(f32[16,256]{1,0:T(8,128)S(1)} %shard_map.141.refs_0_), channel_id=1, source_target_pairs={{0,16},{16,0},{1,17},{17,1},{2,18},{18,2},{3,19},{19,3},{4,20},{20... | collective-permute-start | bytes 49160 | tf_op jit(solution)/shard_map/ppermute | solution.py:527
  7.4 0.0 copy-done.2
  7.4 0.0 copy-done.3
  7.4 0.0 copy-done.4
  7.4 0.0 copy-done.9
  7.4 0.0 copy-done.10
  7.4 0.6 %copy-done.8 = f32[1024]{0:T(1024)S(1)} copy-done((f32[1024]{0:T(1024)S(1)}, f32[1024]{0:T(1024)}, u32[]{:S(2)}) %copy-start.8) | copy-done | bytes 4120
  8.1 0.0 copy-done.7
  8.1 1.1 %shard_map.142 = (f32[56,128]{1,0:T(8,128)S(1)}, f32[56,128]{1,0:T(8,128)S(1)}, f32[56,128]{1,0:T(8,128)S(1)}, f32[56,128]{1,0:T(8,128)S(1)}, f32[56,128]{1,0:T(...) custom-call(s32[1]{0:T(128)} %bitcast.pos_ref, s32[1]{0:T(128)} %bitcast.1.lev_ref, ...), custom_call_target="tpu_custom_call" | custom-call | tf_op jit(solution)/shard_map/pallas_call | solution.py:518
  9.2 0.0 collective-permute-done.2.refs_1_
  9.2 4.1 %collective-permute-start.3 = (f32[88,128]{1,0:T(8,128)S(1)}, f32[88,128]{1,0:T(8,128)S(1)}, u32[]{:S(2)}, u32[]{:S(2)}) collective-permute-start(f32[88,128]{1,0:T(8,128)S(1)} %get-tuple-element.43), channel_id=1, source_target_pairs={{0,12},{1,13},{2,14},{3,15},{4,8},{5,9},{6,10},{7,11},{8,4},{9,5},... | collective-permute-start | bytes 135176 | tf_op jit(solution)/shard_map/ppermute | solution.py:541
  13.3 1.2 %collective-permute-start.4 = (f32[88,128]{1,0:T(8,128)S(1)}, f32[88,128]{1,0:T(8,128)S(1)}, u32[]{:S(2)}, u32[]{:S(2)}) collective-permute-start(f32[88,128]{1,0:T(8,128)S(1)} %get-tuple-element.44), channel_id=1, source_target_pairs={{0,14},{1,15},{2,12},{3,13},{4,10},{5,11},{6,8},{7,9},{8,6},{9,7},... | collective-permute-start | bytes 135176 | tf_op jit(solution)/shard_map/ppermute | solution.py:541
  14.5 0.7 %collective-permute-start.5 = (f32[88,128]{1,0:T(8,128)S(1)}, f32[88,128]{1,0:T(8,128)S(1)}, u32[]{:S(2)}, u32[]{:S(2)}) collective-permute-start(f32[88,128]{1,0:T(8,128)S(1)} %get-tuple-element.45), channel_id=1, source_target_pairs={{0,10},{1,7},{2,8},{3,5},{4,14},{5,3},{6,12},{7,1},{8,2},{9,15},{1... | collective-permute-start | bytes 135176 | tf_op jit(solution)/shard_map/ppermute | solution.py:541
  15.2 4.3 %collective-permute-start.6 = (f32[88,128]{1,0:T(8,128)S(1)}, f32[88,128]{1,0:T(8,128)S(1)}, u32[]{:S(2)}, u32[]{:S(2)}) collective-permute-start(f32[88,128]{1,0:T(8,128)S(1)} %get-tuple-element.46), channel_id=1, source_target_pairs={{0,6},{1,11},{2,4},{3,9},{4,2},{5,15},{6,0},{7,13},{8,14},{9,3},{1... | collective-permute-start | bytes 135176 | tf_op jit(solution)/shard_map/ppermute | solution.py:541
  19.5 0.0 collective-permute-start.7
  19.5 0.0 collective-permute-done.3.refs_2_
  19.6 0.8 %collective-permute-start.8 = (f32[88,128]{1,0:T(8,128)S(1)}, f32[88,128]{1,0:T(8,128)S(1)}, u32[]{:S(2)}, u32[]{:S(2)}) collective-permute-start(f32[88,128]{1,0:T(8,128)S(1)} %get-tuple-element.49), channel_id=1, source_target_pairs={{0,4},{1,9},{2,6},{3,11},{4,0},{5,13},{6,2},{7,15},{8,12},{9,1},{1... | collective-permute-start | bytes 135176 | tf_op jit(solution)/shard_map/ppermute | solution.py:541
  20.3 0.0 collective-permute-done.4.refs_3_
  20.3 1.7 %collective-permute-start.9 = (f32[88,128]{1,0:T(8,128)S(1)}, f32[88,128]{1,0:T(8,128)S(1)}, u32[]{:S(2)}, u32[]{:S(2)}) collective-permute-start(f32[88,128]{1,0:T(8,128)S(1)} %get-tuple-element.53), channel_id=1, source_target_pairs={{0,2},{1,3},{2,0},{3,1},{4,6},{5,7},{6,4},{7,5},{8,10},{9,11},{10,... | collective-permute-start | bytes 135176 | tf_op jit(solution)/shard_map/ppermute | solution.py:541
  22.0 0.0 collective-permute-done.5.refs_4_
  22.0 0.4 %collective-permute-done.6.refs_5_ = f32[88,128]{1,0:T(8,128)S(1)} collective-permute-done((f32[88,128]{1,0:T(8,128)S(1)}, f32[88,128]{1,0:T(8,128)S(1)}, u32[]{:S(2)}, u32[]{:S(2)}) %collective-permute-start.6) | collective-permute-done | bytes 45088 | tf_op jit(solution)/shard_map/ppermute | solution.py:541
  22.5 1.1 %shard_map.144 = (bf16[8,32,640]{2,1,0:T(8,128)(2,1)S(1)}, f32[5,16,128]{2,1,0:T(8,128)S(1)}, f32[16,1024]{1,0:T(8,128)S(1)}, bf16[8,256,128]{2,1,0:T(8,128)(2,1)S(1)}) custom-call(f32[32,128]{1,0:T(8,128)S(1)} %get-tuple-element.41.refs_0_, f32[56,128]{1,0:T(8,128)S(1)} %get-tuple-element.42.refs_1_, f32[88,128]{1,0:T(8,128)S(1)} %collective-permute-done.3.refs_2_, ...), custom_call_target="tpu_custom_call" | custom-call | tf_op jit(solution)/shard_map/pallas_call | solution.py:551
  23.6 0.9 %collective-permute-done.7.refs_6_ = f32[88,128]{1,0:T(8,128)S(1)} collective-permute-done((f32[88,128]{1,0:T(8,128)S(1)}, f32[88,128]{1,0:T(8,128)S(1)}, u32[]{:S(2)}, u32[]{:S(2)}) %collective-permute-start.7) | collective-permute-done | bytes 45088 | tf_op jit(solution)/shard_map/ppermute | solution.py:541
  24.5 0.0 collective-permute-done.8.refs_7_
  24.5 0.8 %shard_map.145 = (bf16[8,32,256]{2,1,0:T(8,128)(2,1)S(1)}, f32[7,16,128]{2,1,0:T(8,128)S(1)}, f32[16,1024]{1,0:T(8,128)S(1)}) custom-call(f32[32,128]{1,0:T(8,128)S(1)} %get-tuple-element.41.refs_0_, f32[56,128]{1,0:T(8,128)S(1)} %get-tuple-element.42.refs_1_, f32[88,128]{1,0:T(8,128)S(1)} %collective-permute-done.3.refs_2_, ...), custom_call_target="tpu_custom_call" | custom-call | tf_op jit(solution)/shard_map/pallas_call | solution.py:551
  25.3 0.0 collective-permute-done.9.refs_8_
  25.3 0.9 %shard_map.146 = (f32[16,384]{1,0:T(8,128)S(1)}, bf16[8,32,128]{2,1,0:T(8,128)(2,1)S(1)}, f32[8,16,128]{2,1,0:T(8,128)S(1)}) custom-call(s32[1]{0:T(128)} %bitcast.pos_ref, s32[1]{0:T(128)} %bitcast.1.lev_ref, f32[16,32]{1,0:T(8,128)S(1)} %copy-done.5, f32[32,128]{1,0:T(8,128)S(1)} %get-tuple-element.41.refs_0_, f32[56,128]{1,0:T(8,128)S(1)} %get-tuple-element.42.refs_1_, ...), custom_call_target="tpu_custom_call" | custom-call | tf_op jit(solution)/shard_map/pallas_call | solution.py:561
  26.2 0.0 collective-permute-start.10
  26.2 1.0 %shard_map.147 = (f32[16,1024]{1,0:T(8,128)}, f32[16,1024]{1,0:T(8,128)}) custom-call(s32[1]{0:T(128)} %bitcast.pos_ref, s32[1]{0:T(128)} %bitcast.1.lev_ref, bf16[8,32,640]{2,1,0:T(8,128)(2,1)S(1)} %get-tuple-element.47.refs_8_.refs_9_.refs_0_, bf16[8,32,256]{2,1,0:T(8,128)(2,1)S(1)} %get-tuple-element.52.refs_10_.refs_1_, ...), custom_call_target="tpu_custom_call" | custom-call | tf_op jit(solution)/shard_map/pallas_call | solution.py:567
  27.1 0.2 collective-permute-done.10.theirs_ref
  27.4 0.0 copy-done.1
  27.4 1.4 %shard_map.148 = f32[16,40,256]{2,1,0:T(8,128)} custom-call(s32[1]{0:T(128)} %bitcast.1.lev_ref, bf16[16,40,256]{2,1,0:T(8,128)(2,1)S(1)} %copy-done, bf16[16,40,256]{2,1,0:T(8,128)(2,1)S(1)} %collective-permute-done.1.other_ref, f32[16,40,256]{2,1,0:T(8,128)S(1)} %copy-done.1, f32[16,384]{1,0:T(8,128)S(1)} %get-tuple-element.62.mine_ref, ...), custom_call_target="tpu_custom_call" | custom-call | tf_op jit(solution)/shard_map/pallas_call | solution.py:588
  (10 shorter events, 0.0 us)
Async XLA Ops:
  0.6 2.9 %collective-permute-start = (f32[16,40,256]{2,1,0:T(8,128)}, f32[16,40,256]{2,1,0:T(8,128)S(1)}, u32[]{:S(2)}, u32[]{:S(2)}) collective-permute-start(f32[16,40,256]{2,1,0:T(8,128)} %control_ref.1), channel_id=1, source_target_pairs={{0,1},{1,0},{2,3},{3,2},{4,5},{5,4},{6,7},{7,6},{8,9},{9,8},{10,11... | collective-permute-start | bytes 1966088 | tf_op jit(solution)/shard_map/ppermute | solution.py:503
  1.1 3.2 %collective-permute-start.1 = (bf16[16,40,256]{2,1,0:T(8,128)(2,1)}, bf16[16,40,256]{2,1,0:T(8,128)(2,1)S(1)}, u32[]{:S(2)}, u32[]{:S(2)}) collective-permute-start(bf16[16,40,256]{2,1,0:T(8,128)(2,1)} %perturb_ref.3), channel_id=1, source_target_pairs={{0,1},{1,0},{2,3},{3,2},{4,5},{5,4},{6,7},{7,6},{8,9},{9,8},{10,11... | collective-permute-start | bytes 983048 | tf_op jit(solution)/shard_map/ppermute | solution.py:504
  1.2 2.3 %copy-start = (bf16[16,40,256]{2,1,0:T(8,128)(2,1)S(1)}, bf16[16,40,256]{2,1,0:T(8,128)(2,1)}, u32[]{:S(2)}) copy-start(bf16[16,40,256]{2,1,0:T(8,128)(2,1)} %perturb_ref.3) | copy-start | bytes 983044
  1.2 2.3 %copy-start.5 = (f32[16,32]{1,0:T(8,128)S(1)}, f32[16,32]{1,0:T(8,128)}, u32[]{:S(2)}) copy-start(f32[16,32]{1,0:T(8,128)} %loc_ref.3) | copy-start | bytes 6148
  3.5 0.8 %copy-start.6 = (f32[16,256]{1,0:T(8,128)S(1)}, f32[16,256]{1,0:T(8,128)}, u32[]{:S(2)}) copy-start(f32[16,256]{1,0:T(8,128)} %shard_map.139.a_ref) | copy-start | bytes 49156
  3.6 3.8 %copy-start.2 = (f32[16,1024]{1,0:T(8,128)S(1)}, f32[16,1024]{1,0:T(8,128)}, u32[]{:S(2)}) copy-start(f32[16,1024]{1,0:T(8,128)} %refs_5_.1) | copy-start | bytes 196612
  3.6 3.8 %copy-start.3 = (f32[16,1024]{1,0:T(8,128)S(1)}, f32[16,1024]{1,0:T(8,128)}, u32[]{:S(2)}) copy-start(f32[16,1024]{1,0:T(8,128)} %refs_8_.1) | copy-start | bytes 196612
  3.6 3.8 %copy-start.4 = (f32[16,1024]{1,0:T(8,128)S(1)}, f32[16,1024]{1,0:T(8,128)}, u32[]{:S(2)}) copy-start(f32[16,1024]{1,0:T(8,128)} %refs_9_.1) | copy-start | bytes 196612
  4.3 3.1 %copy-start.9 = (s32[1,8,128]{2,1,0:T(8,128)S(1)}, s32[1,8,128]{2,1,0:T(8,128)}, u32[]{:S(2)}) copy-start(s32[1,8,128]{2,1,0:T(8,128)} %src_ref.1) | copy-start | bytes 12292
  4.3 3.1 %copy-start.10 = (f32[1,8,128]{2,1,0:T(8,128)S(1)}, f32[1,8,128]{2,1,0:T(8,128)}, u32[]{:S(2)}) copy-start(f32[1,8,128]{2,1,0:T(8,128)} %weight_ref.1) | copy-start | bytes 12292
  4.3 3.1 %copy-start.11 = (s32[1,8,128]{2,1,0:T(8,128)S(1)}, s32[1,8,128]{2,1,0:T(8,128)}, u32[]{:S(2)}) copy-start(s32[1,8,128]{2,1,0:T(8,128)} %tgt_ref.1) | copy-start | bytes 12292
  4.4 4.8 %collective-permute-start.2 = (f32[16,256]{1,0:T(8,128)S(1)}, f32[16,256]{1,0:T(8,128)S(1)}, u32[]{:S(2)}, u32[]{:S(2)}) collective-permute-start(f32[16,256]{1,0:T(8,128)S(1)} %shard_map.141.refs_0_), channel_id=1, source_target_pairs={{0,16},{16,0},{1,17},{17,1},{2,18},{18,2},{3,19},{19,3},{4,20},{20... | collective-permute-start | bytes 49160 | tf_op jit(solution)/shard_map/ppermute | solution.py:527
  7.4 0.7 %copy-start.8 = (f32[1024]{0:T(1024)S(1)}, f32[1024]{0:T(1024)}, u32[]{:S(2)}) copy-start(f32[1024]{0:T(1024)} %param.17) | copy-start | bytes 12292
  7.4 0.7 %copy-start.7 = (f32[1024]{0:T(1024)S(1)}, f32[1024]{0:T(1024)}, u32[]{:S(2)}) copy-start(f32[1024]{0:T(1024)} %param.16) | copy-start | bytes 12292
  7.4 0.7 %copy-start.12 = (s32[1,8]{1,0:T(1,128)S(1)}, s32[1,8]{1,0:T(1,128)}, u32[]{:S(2)}) copy-start(s32[1,8]{1,0:T(1,128)} %counts_ref.1) | copy-start | bytes 100
  9.2 10.3 %collective-permute-start.3 = (f32[88,128]{1,0:T(8,128)S(1)}, f32[88,128]{1,0:T(8,128)S(1)}, u32[]{:S(2)}, u32[]{:S(2)}) collective-permute-start(f32[88,128]{1,0:T(8,128)S(1)} %get-tuple-element.43), channel_id=1, source_target_pairs={{0,12},{1,13},{2,14},{3,15},{4,8},{5,9},{6,10},{7,11},{8,4},{9,5},... | collective-permute-start | bytes 135176 | tf_op jit(solution)/shard_map/ppermute | solution.py:541
  13.3 7.0 %collective-permute-start.4 = (f32[88,128]{1,0:T(8,128)S(1)}, f32[88,128]{1,0:T(8,128)S(1)}, u32[]{:S(2)}, u32[]{:S(2)}) collective-permute-start(f32[88,128]{1,0:T(8,128)S(1)} %get-tuple-element.44), channel_id=1, source_target_pairs={{0,14},{1,15},{2,12},{3,13},{4,10},{5,11},{6,8},{7,9},{8,6},{9,7},... | collective-permute-start | bytes 135176 | tf_op jit(solution)/shard_map/ppermute | solution.py:541
  14.5 7.5 %collective-permute-start.5 = (f32[88,128]{1,0:T(8,128)S(1)}, f32[88,128]{1,0:T(8,128)S(1)}, u32[]{:S(2)}, u32[]{:S(2)}) collective-permute-start(f32[88,128]{1,0:T(8,128)S(1)} %get-tuple-element.45), channel_id=1, source_target_pairs={{0,10},{1,7},{2,8},{3,5},{4,14},{5,3},{6,12},{7,1},{8,2},{9,15},{1... | collective-permute-start | bytes 135176 | tf_op jit(solution)/shard_map/ppermute | solution.py:541
  15.2 7.3 %collective-permute-start.6 = (f32[88,128]{1,0:T(8,128)S(1)}, f32[88,128]{1,0:T(8,128)S(1)}, u32[]{:S(2)}, u32[]{:S(2)}) collective-permute-start(f32[88,128]{1,0:T(8,128)S(1)} %get-tuple-element.46), channel_id=1, source_target_pairs={{0,6},{1,11},{2,4},{3,9},{4,2},{5,15},{6,0},{7,13},{8,14},{9,3},{1... | collective-permute-start | bytes 135176 | tf_op jit(solution)/shard_map/ppermute | solution.py:541
  19.5 4.9 %collective-permute-start.7 = (f32[88,128]{1,0:T(8,128)S(1)}, f32[88,128]{1,0:T(8,128)S(1)}, u32[]{:S(2)}, u32[]{:S(2)}) collective-permute-start(f32[88,128]{1,0:T(8,128)S(1)} %get-tuple-element.48), channel_id=1, source_target_pairs={{0,8},{1,5},{2,10},{3,7},{4,12},{5,1},{6,14},{7,3},{8,0},{9,13},{1... | collective-permute-start | bytes 135176 | tf_op jit(solution)/shard_map/ppermute | solution.py:541
  19.6 4.9 %collective-permute-start.8 = (f32[88,128]{1,0:T(8,128)S(1)}, f32[88,128]{1,0:T(8,128)S(1)}, u32[]{:S(2)}, u32[]{:S(2)}) collective-permute-start(f32[88,128]{1,0:T(8,128)S(1)} %get-tuple-element.49), channel_id=1, source_target_pairs={{0,4},{1,9},{2,6},{3,11},{4,0},{5,13},{6,2},{7,15},{8,12},{9,1},{1... | collective-permute-start | bytes 135176 | tf_op jit(solution)/shard_map/ppermute | solution.py:541
  20.3 4.9 %collective-permute-start.9 = (f32[88,128]{1,0:T(8,128)S(1)}, f32[88,128]{1,0:T(8,128)S(1)}, u32[]{:S(2)}, u32[]{:S(2)}) collective-permute-start(f32[88,128]{1,0:T(8,128)S(1)} %get-tuple-element.53), channel_id=1, source_target_pairs={{0,2},{1,3},{2,0},{3,1},{4,6},{5,7},{6,4},{7,5},{8,10},{9,11},{10,... | collective-permute-start | bytes 135176 | tf_op jit(solution)/shard_map/ppermute | solution.py:541
  26.2 1.2 %copy-start.1 = (f32[16,40,256]{2,1,0:T(8,128)S(1)}, f32[16,40,256]{2,1,0:T(8,128)}, u32[]{:S(2)}) copy-start(f32[16,40,256]{2,1,0:T(8,128)} %control_ref.1) | copy-start | bytes 1966084
  26.2 1.2 %collective-permute-start.10 = (f32[16,384]{1,0:T(8,128)S(1)}, f32[16,384]{1,0:T(8,128)S(1)}, u32[]{:S(2)}, u32[]{:S(2)}) collective-permute-start(f32[16,384]{1,0:T(8,128)S(1)} %get-tuple-element.62.mine_ref), channel_id=1, source_target_pairs={{0,1},{1,0},{2,3},{3,2},{4,5},{5,4},{6,7},{7,6},{8,9},{9,8},{10,11... | collective-permute-start | bytes 73736 | tf_op jit(solution)/shard_map/ppermute | solution.py:587

commit v10 on v9

--- a/solution.py
+++ b/solution.py
@@ -192,34 +192,49 @@
     grad_ref[...] = partial_ref[...] + (jnp.where(lane == 0, before, 0.0) + jnp.where(lane == cols - 1, after, 0.0))
 
 
-def ens_kernel(lev_ref, perturb_ref, other_ref, control_ref, mine_ref, theirs_ref, out_hbm, out_ref, sems):
-    levels, members, cols = perturb_ref.shape
-    mine, theirs = mine_ref[...], theirs_ref[...]
-    loc = jnp.concatenate([mine[:, cols : cols + 2 * levels], theirs[:, cols : cols + 2 * levels]], axis=0)
+def ens_weights(loc, start, count):
     full = loc.shape[0]
-    l_row = lax.broadcasted_iota(jnp.int32, (levels * SUB, full), 0) // SUB + lev_ref[0] * levels
-    pick_l = (l_row == lax.broadcasted_iota(jnp.int32, (levels * SUB, full), 1)).astype(BF16)
-    k_col = lax.broadcasted_iota(jnp.int32, (full, full * SUB), 1) // SUB
-    pick_k = (k_col == lax.broadcasted_iota(jnp.int32, (full, full * SUB), 0)).astype(BF16)
-    same = (
-        lax.broadcasted_iota(jnp.int32, (levels * SUB, full * SUB), 0) % SUB
-        == lax.broadcasted_iota(jnp.int32, (levels * SUB, full * SUB), 1) % SUB
-    )
+
+    def iota(shape, axis):
+        return lax.broadcasted_iota(jnp.int32, shape, axis)
+
+    shape = (count * SUB, full * SUB)
+    pick_l = (iota((count * SUB, loc.shape[1]), 0) // SUB + start == iota((count * SUB, loc.shape[1]), 1)).astype(BF16)
+    pick_k = (iota((full, full * SUB), 1) // SUB == iota((full, full * SUB), 0)).astype(BF16)
+    same = iota(shape, 0) % SUB == iota(shape, 1) % SUB
     weights = []
     for part in halves(loc):
-        tall = product(pick_l, part, ((1,), (1,)))
-        wide = product(tall.astype(BF16), pick_k)
+        wide = product(product(pick_l, part, ((1,), (1,))).astype(BF16), pick_k)
         weights.append(jnp.where(same, wide, 0.0).astype(BF16))
+    return weights
+
+
+def ens_tiles(lev_ref, perturb_ref, band_ref, before_ref):
+    levels, members, cols = perturb_ref.shape
+    band = band_ref[...]
+    weights = ens_weights(band[:, cols : cols + 2 * levels], lev_ref[0] * levels, levels)
+    grad = band[:, :cols][:, None, :]
     perturb = perturb_ref[...].astype(F32)
-    other = other_ref[...].astype(F32)
-    grad = jnp.concatenate([mine[:, :cols], theirs[:, :cols]], axis=0)[:, None, :]
-    copies = []
-    for i, m in enumerate(range(0, members, SUB)):
-        tile = jnp.concatenate([perturb[:, m : m + SUB, :], other[:, m : m + SUB, :]], axis=0) * grad
-        mixed = mix(weights, tile.reshape(full * SUB, cols)).reshape(levels, SUB, cols)
+    for m in range(0, members, SUB):
         place = (slice(None), slice(m, m + SUB), slice(None))
-        out_ref[place] = control_ref[place] + mixed
-        copies.append(pltpu.make_async_copy(out_ref.at[place], out_hbm.at[place], sems.at[i]))
+        tile = (perturb[place] * grad).reshape(levels * SUB, cols)
+        yield place, before_ref[place] + mix(weights, tile).reshape(levels, SUB, cols)
+
+
+def ens_own_kernel(lev_ref, perturb_ref, mine_ref, control_ref, out_ref):
+    for place, values in ens_tiles(lev_ref, perturb_ref, mine_ref, control_ref):
+        out_ref[place] = values
+
+
+def ens_kernel(lev_ref, perturb_ref, theirs_ref, own_ref, *refs):
+    count = (len(refs) - 3) // 2
+    flats, (out_hbm, *flat_hbms), (out_ref, sems) = refs[:count], refs[count : 2 * count + 1], refs[2 * count + 1 :]
+    copies = [pltpu.make_async_copy(a, b, sems.at[i]) for i, (a, b) in enumerate(zip(flats, flat_hbms))]
+    for copy in copies:
+        copy.start()
+    for place, values in ens_tiles(lev_ref, perturb_ref, theirs_ref, own_ref):
+        out_ref[place] = values
+        copies.append(pltpu.make_async_copy(out_ref.at[place], out_hbm.at[place], sems.at[len(copies)]))
         copies[-1].start()
     for copy in copies:
         copy.wait()
@@ -501,7 +516,6 @@
     lev = lax.axis_index("lev").astype(jnp.int32).reshape(1)
     pos = lax.axis_index("tile").astype(jnp.int32).reshape(1)
     other_control = lax.ppermute(control, "lev", swap)
-    other_perturb = lax.ppermute(perturb, "lev", swap)
     part = call(
         own_kernel,
         shape((levels, band_cols), F32),
@@ -522,7 +536,7 @@
             lev, perturb, other_control, level_loc
         )
         sums = [call(add_kernel, shape((levels, band_cols), F32), [VMEM] * 2)(part, other_part)]
-        sums[0], other_perturb = lax.optimization_barrier((sums[0], other_perturb))
+        sums[0], other_perturb = lax.optimization_barrier((sums[0], lax.ppermute(perturb, "lev", swap)))
         for k in range(1, groups):
             sums.append(lax.ppermute(sums[0], "grp", [(g, (g + k) % groups) for g in range(groups)]))
         total, *blocks = call(
@@ -532,7 +546,7 @@
         )(*sums, *rests[1:])
         low, high = n // 4, n // 2
         both_far = [high + low + i for i in range(low)]
-        mixed = [r for i in reversed(range(low)) for r in (high + i, low + i)]
+        mixed = [high + i for i in reversed(range(low))] + [low + i for i in reversed(range(low))]
         stages = [[0] + both_far + mixed[:low], mixed[low:], list(range(1, low))]
         levs = lax.axis_size("lev")
         arrived = {0: [total, rests[0]]}
@@ -568,6 +582,7 @@
             functools.partial(outputs_kernel, stages), (flat, flat), [SMEM] * 2 + [VMEM] * (len(slots) + 7)
         )(pos, lev, *slots, remap, tables, static_control, diag, off, obs_weight, innovation)
     else:
+        other_perturb = lax.ppermute(perturb, "lev", swap)
         payload = call(
             band_kernel,
             shape((groups, n, levels + EXTRA, cap), F32),
@@ -585,15 +600,14 @@
             pos, counts, returned, send_src, send_wt, partial, level_loc
         )
     theirs = lax.ppermute(mine, "lev", swap)
-    grad_ens = call(
+    own = call(ens_own_kernel, shape(control.shape, F32), [SMEM] + [VMEM] * 3)(lev, perturb, mine, control)
+    grad_ens, increment, grad_static = call(
         ens_kernel,
-        shape(control.shape, F32),
+        (shape(control.shape, F32), flat, flat),
         [SMEM] + [VMEM] * 5,
-        [pltpu.VMEM(control.shape, F32), pltpu.SemaphoreType.DMA((members // SUB,))],
+        [pltpu.VMEM(control.shape, F32), pltpu.SemaphoreType.DMA((2 + members // SUB,))],
         out=HBM,
-    )(
-        lev, perturb, other_perturb, control, mine, theirs
-    )
+    )(lev, other_perturb, theirs, own, increment, grad_static)
     return (increment, grad_static, grad_ens)
 
 

time: 29 us -> 28.4 us (0.979)
  waiting for transfers between devices: 1.61 us -> 0.48 us
    ppermute x7, waiting for transfers between devices: 1.35 us -> 0.47 us  [body(): arrived[r] = [lax.ppermute(blocks[r - 1], ('tile', 'lev'), pairs)]]
    pallas_call x1 -> x2, Pallas kernels: 1.41 us -> 2.3 us  [the longest x1 1.51 us: body(): call(ens_kernel, (shape(control.shape, F32), flat, flat), [SMEM] + [VMEM]...]
    pallas_call x1, Pallas kernels: 0.96 us -> 0.32 us  [body(): call(functools.partial(outputs_kernel, stages), (flat, flat), [SMEM] * 2...]
  transfers between devices with their start and end apart: 11 -> 11, of which waited for: 3 -> 1; matrix products, arithmetic and copies ran while one was open for 0% -> 0% of each run, Pallas kernels for 24% -> 25%
where the time goes in v10:
time: 28.4 us; the launch traced here: 28.1 us
  starting transfers between devices  16.4 us (58%)
  Pallas kernels  9.5 us (33%)
  local copies, waits for them, and re-layouts  0.92 us (3%)
  between operations  0.85 us (3%)
  waiting for transfers between devices  0.48 us (2%)
    ppermute x7, starting transfers between devices, body(): arrived[r] = [lax.ppermute(blocks[r - 1], ('tile', 'lev'), pairs)]  12.8 us
    ppermute x1, starting transfers between devices, body(): lax.ppermute(sums[0], 'grp', [(g, (g + k) % groups) for g in range(groups)])  2.98 us
    pallas_call x1, Pallas kernels, body(): call(own_kernel, shape((levels, band_cols), F32), [SMEM] + [HBM] * 3, [pl...  2.3 us
    pallas_call x2, Pallas kernels, body(): call(functools.partial(stage_kernel, n, levels, band_cols, tile_cols, sta...  1.9 us
    pallas_call x1, Pallas kernels, body(): call(ens_kernel, (shape(control.shape, F32), flat, flat), [SMEM] + [VMEM]...  1.51 us
    pallas_call x1, Pallas kernels, body(): call(functools.partial(static_kernel, band_cols), [shape((rows.total, cap...  1.1 us
    unnamed x26, local copies, waits for them, and re-layouts  0.92 us
    pallas_call x1, Pallas kernels, body(): call(functools.partial(shared_kernel, n, tile_cols, stages), (mine_shape,...  0.86 us
  transfers between devices with their start and end apart: 11, of which 1 were waited for; matrix products, arithmetic and copies ran while one was open for 0% of the time, Pallas kernels for 25%

profile of v10, /device:TPU:0, one launch (start us, length us, event | category | flops | bytes accessed | tf_op | source)
XLA Modules:
  0.0 28.1 jit_solution(11551591352373357620)
XLA Ops:
  0.6 0.5 %collective-permute-start = (f32[16,40,256]{2,1,0:T(8,128)}, f32[16,40,256]{2,1,0:T(8,128)S(1)}, u32[]{:S(2)}, u32[]{:S(2)}) collective-permute-start(f32[16,40,256]{2,1,0:T(8,128)} %control_ref.1), channel_id=1, source_target_pairs={{0,1},{1,0},{2,3},{3,2},{4,5},{5,4},{6,7},{7,6},{8,9},{9,8},{10,11... | collective-permute-start | bytes 1966088 | tf_op jit(solution)/shard_map/ppermute | solution.py:518
  1.1 0.1 collective-permute-start.1
  1.2 2.3 %shard_map.139.a_ref = f32[16,256]{1,0:T(8,128)} custom-call(s32[1]{0:T(128)} %bitcast.lev_ref, bf16[16,40,256]{2,1,0:T(8,128)(2,1)} %perturb_ref.3, f32[16,40,256]{2,1,0:T(8,128)} %control_ref.1, f32[16,32]{1,0:T(8,128)} %loc_ref.3), custom_call_target="tpu_custom_call" | custom-call | tf_op jit(solution)/shard_map/pallas_call | solution.py:519
  3.5 0.0 copy-start.6
  3.6 0.0 collective-permute-done.other_ref
  3.6 0.0 copy-done
  3.6 0.0 copy-done.5
  3.6 0.0 copy-start.2
  3.6 0.0 copy-start.3
  3.6 0.0 copy-start.4
  3.6 0.7 %shard_map.140.b_ref = f32[16,256]{1,0:T(8,128)S(1)} custom-call(s32[1]{0:T(128)} %bitcast.lev_ref, bf16[16,40,256]{2,1,0:T(8,128)(2,1)S(1)} %copy-done, f32[16,40,256]{2,1,0:T(8,128)S(1)} %collective-permute-done.other_ref, f32[16,32]{1,0:T(8,128)S(1)} %copy-done.5), custom_call_target="tpu_custom_call" | custom-call | tf_op jit(solution)/shard_map/pallas_call | solution.py:535
  4.3 0.0 copy-done.6
  4.3 0.0 copy-start.9
  4.3 0.0 copy-start.10
  4.3 0.0 copy-start.11
  4.4 0.0 collective-permute-done.1.perturb_ref
  4.4 3.0 %collective-permute-start.2 = (f32[16,256]{1,0:T(8,128)S(1)}, f32[16,256]{1,0:T(8,128)S(1)}, u32[]{:S(2)}, u32[]{:S(2)}) collective-permute-start(f32[16,256]{1,0:T(8,128)S(1)} %shard_map.141.refs_0_), channel_id=1, source_target_pairs={{0,16},{16,0},{1,17},{17,1},{2,18},{18,2},{3,19},{19,3},{4,20},{20... | collective-permute-start | bytes 49160 | tf_op jit(solution)/shard_map/ppermute | solution.py:541
  7.4 0.0 copy-done.2
  7.4 0.0 copy-done.3
  7.4 0.0 copy-done.4
  7.4 0.0 copy-done.9
  7.4 0.6 %copy-done.8 = f32[1024]{0:T(1024)S(1)} copy-done((f32[1024]{0:T(1024)S(1)}, f32[1024]{0:T(1024)}, u32[]{:S(2)}) %copy-start.8) | copy-done | bytes 4120
  8.1 0.0 copy-done.7
  8.1 1.1 %shard_map.142 = (f32[56,128]{1,0:T(8,128)S(1)}, f32[56,128]{1,0:T(8,128)S(1)}, f32[56,128]{1,0:T(8,128)S(1)}, f32[56,128]{1,0:T(8,128)S(1)}, f32[56,128]{1,0:T(...) custom-call(s32[1]{0:T(128)} %bitcast.1.pos_ref, s32[1]{0:T(128)} %bitcast.lev_ref, ...), custom_call_target="tpu_custom_call" | custom-call | tf_op jit(solution)/shard_map/pallas_call | solution.py:532
  9.2 0.0 collective-permute-done.2.refs_1_
  9.2 4.1 %collective-permute-start.3 = (f32[88,128]{1,0:T(8,128)S(1)}, f32[88,128]{1,0:T(8,128)S(1)}, u32[]{:S(2)}, u32[]{:S(2)}) collective-permute-start(f32[88,128]{1,0:T(8,128)S(1)} %get-tuple-element.47), channel_id=1, source_target_pairs={{0,12},{1,13},{2,14},{3,15},{4,8},{5,9},{6,10},{7,11},{8,4},{9,5},... | collective-permute-start | bytes 135176 | tf_op jit(solution)/shard_map/ppermute | solution.py:555
  13.3 1.2 %collective-permute-start.4 = (f32[88,128]{1,0:T(8,128)S(1)}, f32[88,128]{1,0:T(8,128)S(1)}, u32[]{:S(2)}, u32[]{:S(2)}) collective-permute-start(f32[88,128]{1,0:T(8,128)S(1)} %get-tuple-element.48), channel_id=1, source_target_pairs={{0,14},{1,15},{2,12},{3,13},{4,10},{5,11},{6,8},{7,9},{8,6},{9,7},... | collective-permute-start | bytes 135176 | tf_op jit(solution)/shard_map/ppermute | solution.py:555
  14.5 0.7 %collective-permute-start.5 = (f32[88,128]{1,0:T(8,128)S(1)}, f32[88,128]{1,0:T(8,128)S(1)}, u32[]{:S(2)}, u32[]{:S(2)}) collective-permute-start(f32[88,128]{1,0:T(8,128)S(1)} %get-tuple-element.49), channel_id=1, source_target_pairs={{0,10},{1,7},{2,8},{3,5},{4,14},{5,3},{6,12},{7,1},{8,2},{9,15},{1... | collective-permute-start | bytes 135176 | tf_op jit(solution)/shard_map/ppermute | solution.py:555
  15.2 2.0 %collective-permute-start.6 = (f32[88,128]{1,0:T(8,128)S(1)}, f32[88,128]{1,0:T(8,128)S(1)}, u32[]{:S(2)}, u32[]{:S(2)}) collective-permute-start(f32[88,128]{1,0:T(8,128)S(1)} %get-tuple-element.50), channel_id=1, source_target_pairs={{0,8},{1,5},{2,10},{3,7},{4,12},{5,1},{6,14},{7,3},{8,0},{9,13},{1... | collective-permute-start | bytes 135176 | tf_op jit(solution)/shard_map/ppermute | solution.py:555
  17.2 2.3 %collective-permute-start.7 = (f32[88,128]{1,0:T(8,128)S(1)}, f32[88,128]{1,0:T(8,128)S(1)}, u32[]{:S(2)}, u32[]{:S(2)}) collective-permute-start(f32[88,128]{1,0:T(8,128)S(1)} %get-tuple-element.51), channel_id=1, source_target_pairs={{0,6},{1,11},{2,4},{3,9},{4,2},{5,15},{6,0},{7,13},{8,14},{9,3},{1... | collective-permute-start | bytes 135176 | tf_op jit(solution)/shard_map/ppermute | solution.py:555
  19.5 0.0 collective-permute-done.3.refs_2_
  19.6 0.8 %collective-permute-start.8 = (f32[88,128]{1,0:T(8,128)S(1)}, f32[88,128]{1,0:T(8,128)S(1)}, u32[]{:S(2)}, u32[]{:S(2)}) collective-permute-start(f32[88,128]{1,0:T(8,128)S(1)} %get-tuple-element.52), channel_id=1, source_target_pairs={{0,4},{1,9},{2,6},{3,11},{4,0},{5,13},{6,2},{7,15},{8,12},{9,1},{1... | collective-permute-start | bytes 135176 | tf_op jit(solution)/shard_map/ppermute | solution.py:555
  20.4 0.0 collective-permute-done.4.refs_3_
  20.4 1.7 %collective-permute-start.9 = (f32[88,128]{1,0:T(8,128)S(1)}, f32[88,128]{1,0:T(8,128)S(1)}, u32[]{:S(2)}, u32[]{:S(2)}) collective-permute-start(f32[88,128]{1,0:T(8,128)S(1)} %get-tuple-element.53), channel_id=1, source_target_pairs={{0,2},{1,3},{2,0},{3,1},{4,6},{5,7},{6,4},{7,5},{8,10},{9,11},{10,... | collective-permute-start | bytes 135176 | tf_op jit(solution)/shard_map/ppermute | solution.py:555
  22.0 0.0 collective-permute-done.5.refs_4_
  22.0 0.0 collective-permute-done.6.refs_5_
  22.0 1.1 %shard_map.144 = (bf16[8,32,640]{2,1,0:T(8,128)(2,1)S(1)}, f32[5,16,128]{2,1,0:T(8,128)S(1)}, f32[16,1024]{1,0:T(8,128)S(1)}, bf16[8,256,128]{2,1,0:T(8,128)(2,1)S(1)}) custom-call(f32[32,128]{1,0:T(8,128)S(1)} %get-tuple-element.45.refs_0_, f32[56,128]{1,0:T(8,128)S(1)} %get-tuple-element.46.refs_1_, f32[88,128]{1,0:T(8,128)S(1)} %collective-permute-done.3.refs_2_, ...), custom_call_target="tpu_custom_call" | custom-call | tf_op jit(solution)/shard_map/pallas_call | solution.py:565
  23.2 0.0 collective-permute-done.7.refs_6_
  23.2 0.4 %collective-permute-done.8.refs_7_ = f32[88,128]{1,0:T(8,128)S(1)} collective-permute-done((f32[88,128]{1,0:T(8,128)S(1)}, f32[88,128]{1,0:T(8,128)S(1)}, u32[]{:S(2)}, u32[]{:S(2)}) %collective-permute-start.8) | collective-permute-done | bytes 45088 | tf_op jit(solution)/shard_map/ppermute | solution.py:555
  23.6 0.8 %shard_map.145 = (bf16[8,32,256]{2,1,0:T(8,128)(2,1)S(1)}, f32[7,16,128]{2,1,0:T(8,128)S(1)}, f32[16,1024]{1,0:T(8,128)S(1)}) custom-call(f32[32,128]{1,0:T(8,128)S(1)} %get-tuple-element.45.refs_0_, f32[56,128]{1,0:T(8,128)S(1)} %get-tuple-element.46.refs_1_, f32[88,128]{1,0:T(8,128)S(1)} %collective-permute-done.3.refs_2_, ...), custom_call_target="tpu_custom_call" | custom-call | tf_op jit(solution)/shard_map/pallas_call | solution.py:565
  24.4 0.0 collective-permute-done.9.refs_8_
  24.4 0.9 %shard_map.146 = (f32[16,384]{1,0:T(8,128)S(1)}, bf16[8,32,128]{2,1,0:T(8,128)(2,1)S(1)}, f32[8,16,128]{2,1,0:T(8,128)S(1)}) custom-call(s32[1]{0:T(128)} %bitcast.1.pos_ref, s32[1]{0:T(128)} %bitcast.lev_ref, f32[16,32]{1,0:T(8,128)S(1)} %copy-done.5, f32[32,128]{1,0:T(8,128)S(1)} %get-tuple-element.45.refs_0_, f32[56,128]{1,0:T(8,128)S(1)} %get-tuple-element.46.refs_1_, ...), custom_call_target="tpu_custom_call" | custom-call | tf_op jit(solution)/shard_map/pallas_call | solution.py:575
  25.3 0.0 collective-permute-start.10
  25.3 0.2 copy-done.1
  25.5 0.8 %shard_map.147.own_ref = f32[16,40,256]{2,1,0:T(8,128)S(1)} custom-call(s32[1]{0:T(128)} %bitcast.lev_ref, bf16[16,40,256]{2,1,0:T(8,128)(2,1)S(1)} %copy-done, f32[16,384]{1,0:T(8,128)S(1)} %get-tuple-element.60.mine_ref, f32[16,40,256]{2,1,0:T(8,128)S(1)} %copy-done.1), custom_call_target="tpu_custom_call" | custom-call | tf_op jit(solution)/shard_map/pallas_call | solution.py:603
  26.3 0.3 %shard_map.148 = (f32[16,1024]{1,0:T(8,128)S(1)}, f32[16,1024]{1,0:T(8,128)S(1)}) custom-call(s32[1]{0:T(128)} %bitcast.1.pos_ref, s32[1]{0:T(128)} %bitcast.lev_ref, bf16[8,32,640]{2,1,0:T(8,128)(2,1)S(1)} %get-tuple-element.54.refs_8_.refs_9_.refs_0_, bf16[8,32,256]{2,1,0:T(8,128)(2,1)S(1)} %get-tuple-element.57.refs_10_.refs_1_, ...), custom_call_target="tpu_custom_call" | custom-call | tf_op jit(solution)/shard_map/pallas_call | solution.py:581
  26.6 0.0 collective-permute-done.10.theirs_ref
  26.6 1.5 %shard_map.149 = (f32[16,40,256]{2,1,0:T(8,128)}, f32[16,1024]{1,0:T(8,128)}, f32[16,1024]{1,0:T(8,128)}) custom-call(s32[1]{0:T(128)} %bitcast.lev_ref, bf16[16,40,256]{2,1,0:T(8,128)(2,1)S(1)} %collective-permute-done.1.perturb_ref, f32[16,384]{1,0:T(8,128)S(1)} %collective-permute-done.10.theirs_ref, f32[16,40,256]{2,1,0:T(8,128)S(1)} %shard_map.147.own_ref, ...), custom_call_target="tpu_custom_call" | custom-call | tf_op jit(solution)/shard_map/pallas_call | solution.py:604
  (11 shorter events, 0.1 us)
Async XLA Ops:
  0.6 2.9 %collective-permute-start = (f32[16,40,256]{2,1,0:T(8,128)}, f32[16,40,256]{2,1,0:T(8,128)S(1)}, u32[]{:S(2)}, u32[]{:S(2)}) collective-permute-start(f32[16,40,256]{2,1,0:T(8,128)} %control_ref.1), channel_id=1, source_target_pairs={{0,1},{1,0},{2,3},{3,2},{4,5},{5,4},{6,7},{7,6},{8,9},{9,8},{10,11... | collective-permute-start | bytes 1966088 | tf_op jit(solution)/shard_map/ppermute | solution.py:518
  1.1 3.2 %collective-permute-start.1 = (bf16[16,40,256]{2,1,0:T(8,128)(2,1)}, bf16[16,40,256]{2,1,0:T(8,128)(2,1)S(1)}, u32[]{:S(2)}, u32[]{:S(2)}) collective-permute-start(bf16[16,40,256]{2,1,0:T(8,128)(2,1)} %perturb_ref.3), channel_id=1, source_target_pairs={{0,1},{1,0},{2,3},{3,2},{4,5},{5,4},{6,7},{7,6},{8,9},{9,8},{10,11... | collective-permute-start | bytes 983048 | tf_op jit(solution)/shard_map/ppermute | solution.py:539
  1.2 2.3 %copy-start = (bf16[16,40,256]{2,1,0:T(8,128)(2,1)S(1)}, bf16[16,40,256]{2,1,0:T(8,128)(2,1)}, u32[]{:S(2)}) copy-start(bf16[16,40,256]{2,1,0:T(8,128)(2,1)} %perturb_ref.3) | copy-start | bytes 983044
  1.2 2.3 %copy-start.5 = (f32[16,32]{1,0:T(8,128)S(1)}, f32[16,32]{1,0:T(8,128)}, u32[]{:S(2)}) copy-start(f32[16,32]{1,0:T(8,128)} %loc_ref.3) | copy-start | bytes 6148
  3.5 0.8 %copy-start.6 = (f32[16,256]{1,0:T(8,128)S(1)}, f32[16,256]{1,0:T(8,128)}, u32[]{:S(2)}) copy-start(f32[16,256]{1,0:T(8,128)} %shard_map.139.a_ref) | copy-start | bytes 49156
  3.6 3.8 %copy-start.2 = (f32[16,1024]{1,0:T(8,128)S(1)}, f32[16,1024]{1,0:T(8,128)}, u32[]{:S(2)}) copy-start(f32[16,1024]{1,0:T(8,128)} %refs_5_.1) | copy-start | bytes 196612
  3.6 3.8 %copy-start.3 = (f32[16,1024]{1,0:T(8,128)S(1)}, f32[16,1024]{1,0:T(8,128)}, u32[]{:S(2)}) copy-start(f32[16,1024]{1,0:T(8,128)} %refs_8_.1) | copy-start | bytes 196612
  3.6 3.8 %copy-start.4 = (f32[16,1024]{1,0:T(8,128)S(1)}, f32[16,1024]{1,0:T(8,128)}, u32[]{:S(2)}) copy-start(f32[16,1024]{1,0:T(8,128)} %refs_9_.1) | copy-start | bytes 196612
  4.3 3.1 %copy-start.9 = (s32[1,8,128]{2,1,0:T(8,128)S(1)}, s32[1,8,128]{2,1,0:T(8,128)}, u32[]{:S(2)}) copy-start(s32[1,8,128]{2,1,0:T(8,128)} %src_ref.1) | copy-start | bytes 12292
  4.3 3.1 %copy-start.10 = (f32[1,8,128]{2,1,0:T(8,128)S(1)}, f32[1,8,128]{2,1,0:T(8,128)}, u32[]{:S(2)}) copy-start(f32[1,8,128]{2,1,0:T(8,128)} %weight_ref.1) | copy-start | bytes 12292
  4.3 3.1 %copy-start.11 = (s32[1,8,128]{2,1,0:T(8,128)S(1)}, s32[1,8,128]{2,1,0:T(8,128)}, u32[]{:S(2)}) copy-start(s32[1,8,128]{2,1,0:T(8,128)} %tgt_ref.1) | copy-start | bytes 12292
  4.4 4.8 %collective-permute-start.2 = (f32[16,256]{1,0:T(8,128)S(1)}, f32[16,256]{1,0:T(8,128)S(1)}, u32[]{:S(2)}, u32[]{:S(2)}) collective-permute-start(f32[16,256]{1,0:T(8,128)S(1)} %shard_map.141.refs_0_), channel_id=1, source_target_pairs={{0,16},{16,0},{1,17},{17,1},{2,18},{18,2},{3,19},{19,3},{4,20},{20... | collective-permute-start | bytes 49160 | tf_op jit(solution)/shard_map/ppermute | solution.py:541
  7.4 0.7 %copy-start.8 = (f32[1024]{0:T(1024)S(1)}, f32[1024]{0:T(1024)}, u32[]{:S(2)}) copy-start(f32[1024]{0:T(1024)} %param.17) | copy-start | bytes 12292
  7.4 0.7 %copy-start.7 = (f32[1024]{0:T(1024)S(1)}, f32[1024]{0:T(1024)}, u32[]{:S(2)}) copy-start(f32[1024]{0:T(1024)} %param.16) | copy-start | bytes 12292
  7.4 0.7 %copy-start.12 = (s32[1,8]{1,0:T(1,128)S(1)}, s32[1,8]{1,0:T(1,128)}, u32[]{:S(2)}) copy-start(s32[1,8]{1,0:T(1,128)} %counts_ref.1) | copy-start | bytes 100
  9.2 10.3 %collective-permute-start.3 = (f32[88,128]{1,0:T(8,128)S(1)}, f32[88,128]{1,0:T(8,128)S(1)}, u32[]{:S(2)}, u32[]{:S(2)}) collective-permute-start(f32[88,128]{1,0:T(8,128)S(1)} %get-tuple-element.47), channel_id=1, source_target_pairs={{0,12},{1,13},{2,14},{3,15},{4,8},{5,9},{6,10},{7,11},{8,4},{9,5},... | collective-permute-start | bytes 135176 | tf_op jit(solution)/shard_map/ppermute | solution.py:555
  13.3 7.1 %collective-permute-start.4 = (f32[88,128]{1,0:T(8,128)S(1)}, f32[88,128]{1,0:T(8,128)S(1)}, u32[]{:S(2)}, u32[]{:S(2)}) collective-permute-start(f32[88,128]{1,0:T(8,128)S(1)} %get-tuple-element.48), channel_id=1, source_target_pairs={{0,14},{1,15},{2,12},{3,13},{4,10},{5,11},{6,8},{7,9},{8,6},{9,7},... | collective-permute-start | bytes 135176 | tf_op jit(solution)/shard_map/ppermute | solution.py:555
  14.5 7.6 %collective-permute-start.5 = (f32[88,128]{1,0:T(8,128)S(1)}, f32[88,128]{1,0:T(8,128)S(1)}, u32[]{:S(2)}, u32[]{:S(2)}) collective-permute-start(f32[88,128]{1,0:T(8,128)S(1)} %get-tuple-element.49), channel_id=1, source_target_pairs={{0,10},{1,7},{2,8},{3,5},{4,14},{5,3},{6,12},{7,1},{8,2},{9,15},{1... | collective-permute-start | bytes 135176 | tf_op jit(solution)/shard_map/ppermute | solution.py:555
  15.2 6.8 %collective-permute-start.6 = (f32[88,128]{1,0:T(8,128)S(1)}, f32[88,128]{1,0:T(8,128)S(1)}, u32[]{:S(2)}, u32[]{:S(2)}) collective-permute-start(f32[88,128]{1,0:T(8,128)S(1)} %get-tuple-element.50), channel_id=1, source_target_pairs={{0,8},{1,5},{2,10},{3,7},{4,12},{5,1},{6,14},{7,3},{8,0},{9,13},{1... | collective-permute-start | bytes 135176 | tf_op jit(solution)/shard_map/ppermute | solution.py:555
  17.2 6.0 %collective-permute-start.7 = (f32[88,128]{1,0:T(8,128)S(1)}, f32[88,128]{1,0:T(8,128)S(1)}, u32[]{:S(2)}, u32[]{:S(2)}) collective-permute-start(f32[88,128]{1,0:T(8,128)S(1)} %get-tuple-element.51), channel_id=1, source_target_pairs={{0,6},{1,11},{2,4},{3,9},{4,2},{5,15},{6,0},{7,13},{8,14},{9,3},{1... | collective-permute-start | bytes 135176 | tf_op jit(solution)/shard_map/ppermute | solution.py:555
  19.6 4.0 %collective-permute-start.8 = (f32[88,128]{1,0:T(8,128)S(1)}, f32[88,128]{1,0:T(8,128)S(1)}, u32[]{:S(2)}, u32[]{:S(2)}) collective-permute-start(f32[88,128]{1,0:T(8,128)S(1)} %get-tuple-element.52), channel_id=1, source_target_pairs={{0,4},{1,9},{2,6},{3,11},{4,0},{5,13},{6,2},{7,15},{8,12},{9,1},{1... | collective-permute-start | bytes 135176 | tf_op jit(solution)/shard_map/ppermute | solution.py:555
  20.4 4.0 %collective-permute-start.9 = (f32[88,128]{1,0:T(8,128)S(1)}, f32[88,128]{1,0:T(8,128)S(1)}, u32[]{:S(2)}, u32[]{:S(2)}) collective-permute-start(f32[88,128]{1,0:T(8,128)S(1)} %get-tuple-element.53), channel_id=1, source_target_pairs={{0,2},{1,3},{2,0},{3,1},{4,6},{5,7},{6,4},{7,5},{8,10},{9,11},{10,... | collective-permute-start | bytes 135176 | tf_op jit(solution)/shard_map/ppermute | solution.py:555
  24.4 1.1 %copy-start.1 = (f32[16,40,256]{2,1,0:T(8,128)S(1)}, f32[16,40,256]{2,1,0:T(8,128)}, u32[]{:S(2)}) copy-start(f32[16,40,256]{2,1,0:T(8,128)} %control_ref.1) | copy-start | bytes 1966084
  25.3 1.3 %collective-permute-start.10 = (f32[16,384]{1,0:T(8,128)S(1)}, f32[16,384]{1,0:T(8,128)S(1)}, u32[]{:S(2)}, u32[]{:S(2)}) collective-permute-start(f32[16,384]{1,0:T(8,128)S(1)} %get-tuple-element.60.mine_ref), channel_id=1, source_target_pairs={{0,1},{1,0},{2,3},{3,2},{4,5},{5,4},{6,7},{7,6},{8,9},{9,8},{10,11... | collective-permute-start | bytes 73736 | tf_op jit(solution)/shard_map/ppermute | solution.py:602

commit v11 on v10

--- a/solution.py
+++ b/solution.py
@@ -172,18 +172,16 @@
     loop(n, give, 0)
 
 
-def adjoint_kernel(pos_ref, counts_ref, returned_ref, src_ref, weight_ref, partial_ref, loc_ref, grad_ref, out_ref):
+def adjoint_kernel(band, pos_ref, counts_ref, returned_ref, src_ref, weight_ref, partial_ref, mix_ref, grad_ref, out_ref):
     levels, cols = partial_ref.shape
     n = returned_ref.shape[0]
-    band = out_ref.shape[1] - 128
     me = pos_ref[0]
 
     def step(d, total):
         values = returned_ref[d, :levels, :] * factor_of(counts_ref, weight_ref, d)
         return total + select(values, one_hot(src_ref[0, pl.ds(d, 1), :], band), ((1,), (1,)))
 
-    out_ref[:, :band] = loop(n, step, jnp.zeros((levels, band), F32))
-    out_ref[:, band:] = jnp.concatenate([loc_ref[...], jnp.zeros((levels, 128 - loc_ref.shape[1]), F32)], axis=1)
+    out_ref[...] = band_rows(loop(n, step, jnp.zeros((levels, band), F32)), mix_ref[...])
     before = returned_ref[jnp.maximum(me - 1, 0), levels : levels + 1, :]
     after = returned_ref[jnp.minimum(me + 1, n - 1), levels : levels + 1, :]
     before = jnp.where(me > 0, row_as_column(before, levels, 0), 0.0)
@@ -209,11 +207,23 @@
     return weights
 
 
-def ens_tiles(lev_ref, perturb_ref, band_ref, before_ref):
+def mix_kernel(lev_ref, loc_ref, own_ref, given_ref):
+    levels = loc_ref.shape[0]
+    own_ref[0], own_ref[1] = ens_weights(loc_ref[...], lev_ref[0] * levels, levels)
+    high, low = ens_weights(loc_ref[...], (1 - lev_ref[0]) * levels, levels)
+    given_ref[...] = high.astype(F32) + low.astype(F32)
+
+
+def band_rows(band, weights):
+    width = weights.shape[1]
+    return jnp.concatenate([band[:, at : at + width] for at in range(0, band.shape[1], width)] + [weights], axis=0)
+
+
+def ens_tiles(perturb_ref, rows_ref, weights, before_ref):
     levels, members, cols = perturb_ref.shape
-    band = band_ref[...]
-    weights = ens_weights(band[:, cols : cols + 2 * levels], lev_ref[0] * levels, levels)
-    grad = band[:, :cols][:, None, :]
+    width = rows_ref.shape[1]
+    parts = [rows_ref[i * levels : (i + 1) * levels, :] for i in range(cols // width)]
+    grad = jnp.concatenate(parts, axis=1)[:, None, :]
     perturb = perturb_ref[...].astype(F32)
     for m in range(0, members, SUB):
         place = (slice(None), slice(m, m + SUB), slice(None))
@@ -221,18 +231,19 @@
         yield place, before_ref[place] + mix(weights, tile).reshape(levels, SUB, cols)
 
 
-def ens_own_kernel(lev_ref, perturb_ref, mine_ref, control_ref, out_ref):
-    for place, values in ens_tiles(lev_ref, perturb_ref, mine_ref, control_ref):
+def ens_own_kernel(perturb_ref, mine_ref, weights_ref, control_ref, out_ref):
+    for place, values in ens_tiles(perturb_ref, mine_ref, (weights_ref[0], weights_ref[1]), control_ref):
         out_ref[place] = values
 
 
-def ens_kernel(lev_ref, perturb_ref, theirs_ref, own_ref, *refs):
+def ens_kernel(perturb_ref, theirs_ref, own_ref, *refs):
     count = (len(refs) - 3) // 2
     flats, (out_hbm, *flat_hbms), (out_ref, sems) = refs[:count], refs[count : 2 * count + 1], refs[2 * count + 1 :]
     copies = [pltpu.make_async_copy(a, b, sems.at[i]) for i, (a, b) in enumerate(zip(flats, flat_hbms))]
     for copy in copies:
         copy.start()
-    for place, values in ens_tiles(lev_ref, perturb_ref, theirs_ref, own_ref):
+    weights = halves(theirs_ref[theirs_ref.shape[0] - theirs_ref.shape[1] :, :])
+    for place, values in ens_tiles(perturb_ref, theirs_ref, weights, own_ref):
         out_ref[place] = values
         copies.append(pltpu.make_async_copy(out_ref.at[place], out_hbm.at[place], sems.at[len(copies)]))
         copies[-1].start()
@@ -381,16 +392,17 @@
     return blocks, refs[len(labels) - 1 :]
 
 
-def stage_kernel(n, levels, band, cols, stages, *refs):
+def stage_kernel(n, levels, band, cols, stages, lev_ref, loc_ref, *refs):
     known = sum(stages[:-1], [])
     blocks, refs = open_blocks(known + stages[-1], refs, n, levels, band)
     old, refs = refs[: len(stages) - 1], refs[len(stages) - 1 :]
     if known:
         met_old, remap_old, slots_ref, met_ref, remap_ref = refs
     else:
-        slots_ref, met_ref, remap_ref, pick_ref = refs
+        slots_ref, met_ref, remap_ref, pick_ref, own_ref, given_ref = refs
         for d in range(n):
             pick_ref[d] = pick_source(blocks[0], d)
+        mix_kernel(lev_ref, loc_ref, own_ref, given_ref)
     fill_slots(stages[-1], blocks, n, slots_ref)
     for i, (d, block) in enumerate(blocks.items()):
         met = met_at(d, block, stages[-1], slots_ref)
@@ -404,9 +416,7 @@
     remap_ref[...] = landed + remap_old[...] if known else landed
 
 
-def shared_kernel(n, cols, stages, pos_ref, lev_ref, loc_ref, *refs):
-    levels = loc_ref.shape[0]
-    band = refs[-3].shape[1] - 128
+def shared_kernel(n, levels, band, cols, stages, pos_ref, lev_ref, mix_ref, *refs):
     known = sum(stages[:-1], [])
     blocks, refs = open_blocks(known + stages[-1], refs, n, levels, band)
     old, refs = refs[: len(stages) - 1], refs[len(stages) - 1 :]
@@ -437,8 +447,7 @@
         value = value + row_as_column(after, levels, levels) * near
         given = block.rest(0, levels) * value * line(blocks[0].factor, d)
         total = total + select(given, pick_ref[d], ((1,), (1,)))
-    out_ref[:, :band] = total
-    out_ref[:, band:] = jnp.concatenate([loc_ref[...], jnp.zeros((levels, 128 - loc_ref.shape[1]), F32)], axis=1)
+    out_ref[...] = band_rows(total, mix_ref[...])
 
 
 def outputs_kernel(stages, pos_ref, lev_ref, *refs):
@@ -524,7 +533,9 @@
         limit=58 * MIB,
     )(lev, perturb, control, level_loc)
     flat = shape((levels, tile_cols), F32)
-    mine_shape = shape((levels, band_cols + 128), F32)
+    width = levels * SUB
+    mine_shape = shape((band_cols // width * levels + width, width), F32)
+    mix_shapes = [shape((2, width, width), BF16), shape((width, width), F32)]
     diag, off = filter_diag.reshape(1, -1), filter_off.reshape(1, -1)
     if n * cap <= tile_cols and n >= 8 and lax.axis_size("lev") == 2 and n & (n - 1) == 0 and band_cols * tile_cols <= 2**20:
         rows = Rows(levels, n)
@@ -547,13 +558,13 @@
         low, high = n // 4, n // 2
         both_far = [high + low + i for i in range(low)]
         mixed = [high + i for i in reversed(range(low))] + [low + i for i in reversed(range(low))]
-        stages = [[0] + both_far + mixed[:low], mixed[low:], list(range(1, low))]
+        stages = [[0] + both_far + mixed[: low // 2], mixed[low // 2 :], list(range(1, low))]
         levs = lax.axis_size("lev")
         arrived = {0: [total, rests[0]]}
         for r in sum(stages, [])[1:]:
             pairs = [(i * levs + v, (i ^ relabel(r, n, v)) * levs + v) for i in range(n) for v in range(levs)]
             arrived[r] = [lax.ppermute(blocks[r - 1], ("tile", "lev"), pairs)]
-        slots, carried, picks = [], [], []
+        slots, carried, made = [], [], []
         for count in range(1, len(stages)):
             labels = sum(stages[:count], [])
             refs = [ref for r in labels for ref in arrived[r]]
@@ -561,22 +572,23 @@
                 shape((n, 2 * levels, len(stages[count - 1]) * cap), BF16),
                 shape((len(labels), levels, cap), F32),
                 flat,
-            ] + [shape((n, band_cols, cap), BF16)] * (count == 1)
+            ] + [shape((n, band_cols, cap), BF16), *mix_shapes] * (count == 1)
             new, *carried = call(
                 functools.partial(stage_kernel, n, levels, band_cols, tile_cols, stages[:count]),
                 outs,
-                [VMEM] * (len(refs) + len(slots) + len(carried)),
-            )(*refs, *slots, *carried)
+                [SMEM] + [VMEM] * (1 + len(refs) + len(slots) + len(carried)),
+            )(lev, level_loc, *refs, *slots, *carried)
             slots.append(new)
-            picks += carried[2:]
+            made += carried[2:]
             carried = carried[:2]
         met, remap = carried
-        refs = [ref for r in sum(stages, []) for ref in arrived[r]] + slots + [met] + picks
+        picks, own_mix, given_mix = made
+        refs = [ref for r in sum(stages, []) for ref in arrived[r]] + slots + [met, picks]
         mine, new, tables = call(
-            functools.partial(shared_kernel, n, tile_cols, stages),
+            functools.partial(shared_kernel, n, levels, band_cols, tile_cols, stages),
             (mine_shape, shape((n, 2 * levels, len(stages[-1]) * cap), BF16), shape((n, n + EXTRA, cap), F32)),
             [SMEM] * 2 + [VMEM] * (1 + len(refs)),
-        )(pos, lev, level_loc, *refs)
+        )(pos, lev, given_mix, *refs)
         slots.append(new)
         increment, grad_static = call(
             functools.partial(outputs_kernel, stages), (flat, flat), [SMEM] * 2 + [VMEM] * (len(slots) + 7)
@@ -596,18 +608,19 @@
             tile_kernel, (flat, flat, shape((n, levels + EXTRA, cap), F32)), [SMEM] + [VMEM] * 7
         )(pos, arrived, recv_tgt, static_control, diag, off, obs_weight, innovation)
         returned = lax.all_to_all(giving, "tile", split_axis=0, concat_axis=0, tiled=True)
-        grad_static, mine = call(adjoint_kernel, (flat, mine_shape), [SMEM, SMEM] + [VMEM] * 5)(
-            pos, counts, returned, send_src, send_wt, partial, level_loc
-        )
+        own_mix, given_mix = call(mix_kernel, mix_shapes, [SMEM, VMEM])(lev, level_loc)
+        grad_static, mine = call(
+            functools.partial(adjoint_kernel, band_cols), (flat, mine_shape), [SMEM, SMEM] + [VMEM] * 5
+        )(pos, counts, returned, send_src, send_wt, partial, given_mix)
     theirs = lax.ppermute(mine, "lev", swap)
-    own = call(ens_own_kernel, shape(control.shape, F32), [SMEM] + [VMEM] * 3)(lev, perturb, mine, control)
+    own = call(ens_own_kernel, shape(control.shape, F32), [VMEM] * 4)(perturb, mine, own_mix, control)
     grad_ens, increment, grad_static = call(
         ens_kernel,
         (shape(control.shape, F32), flat, flat),
-        [SMEM] + [VMEM] * 5,
+        [VMEM] * 5,
         [pltpu.VMEM(control.shape, F32), pltpu.SemaphoreType.DMA((2 + members // SUB,))],
         out=HBM,
-    )(lev, other_perturb, theirs, own, increment, grad_static)
+    )(other_perturb, theirs, own, increment, grad_static)
     return (increment, grad_static, grad_ens)
 
 

time: 28.4 us -> 28.2 us (level)
  Pallas kernels: 9.5 us -> 9.03 us
    pallas_call x3, Pallas kernels: 3.16 us -> 2.48 us  [the longest x1 1.18 us: body(): call(ens_kernel, (shape(control.shape, F32), flat, flat), [VMEM] * 5, [pl...]
    ppermute x1, waiting for transfers between devices: 0.01 us -> 0.31 us  [body(): theirs = lax.ppermute(mine, 'lev', swap)]
  transfers between devices with their start and end apart: 11 -> 11, of which waited for: 1 -> 2; matrix products, arithmetic and copies ran while one was open for 0% -> 0% of each run, Pallas kernels for 25% -> 25%
where the time goes in v11:
time: 28.2 us; the launch traced here: 27.9 us
  starting transfers between devices  16.4 us (58%)
  Pallas kernels  9.03 us (32%)
  local copies, waits for them, and re-layouts  0.93 us (3%)
  between operations  0.86 us (3%)
  waiting for transfers between devices  0.74 us (3%)
    ppermute x7, starting transfers between devices, body(): arrived[r] = [lax.ppermute(blocks[r - 1], ('tile', 'lev'), pairs)]  12.8 us
    ppermute x1, starting transfers between devices, body(): lax.ppermute(sums[0], 'grp', [(g, (g + k) % groups) for g in range(groups)])  2.98 us
    pallas_call x1, Pallas kernels, body(): call(own_kernel, shape((levels, band_cols), F32), [SMEM] + [HBM] * 3, [pl...  2.3 us
    pallas_call x2, Pallas kernels, body(): call(functools.partial(stage_kernel, n, levels, band_cols, tile_cols, sta...  2.11 us
    pallas_call x1, Pallas kernels, body(): call(ens_kernel, (shape(control.shape, F32), flat, flat), [VMEM] * 5, [pl...  1.18 us
    pallas_call x1, Pallas kernels, body(): call(functools.partial(static_kernel, band_cols), [shape((rows.total, cap...  1.1 us
    unnamed x26, local copies, waits for them, and re-layouts  0.93 us
    pallas_call x1, Pallas kernels, body(): call(functools.partial(shared_kernel, n, levels, band_cols, tile_cols, st...  0.88 us
  transfers between devices with their start and end apart: 11, of which 2 were waited for; matrix products, arithmetic and copies ran while one was open for 0% of the time, Pallas kernels for 25%

profile of v11, /device:TPU:0, one launch (start us, length us, event | category | flops | bytes accessed | tf_op | source)
XLA Modules:
  0.0 27.9 jit_solution(15967104411297260046)
XLA Ops:
  0.6 0.5 %collective-permute-start = (f32[16,40,256]{2,1,0:T(8,128)}, f32[16,40,256]{2,1,0:T(8,128)S(1)}, u32[]{:S(2)}, u32[]{:S(2)}) collective-permute-start(f32[16,40,256]{2,1,0:T(8,128)} %control_ref.1), channel_id=1, source_target_pairs={{0,1},{1,0},{2,3},{3,2},{4,5},{5,4},{6,7},{7,6},{8,9},{9,8},{10,11... | collective-permute-start | bytes 1966088 | tf_op jit(solution)/shard_map/ppermute | solution.py:527
  1.1 0.1 collective-permute-start.1
  1.2 2.3 %shard_map.139.a_ref = f32[16,256]{1,0:T(8,128)} custom-call(s32[1]{0:T(128)} %bitcast.lev_ref, bf16[16,40,256]{2,1,0:T(8,128)(2,1)} %perturb_ref.3, f32[16,40,256]{2,1,0:T(8,128)} %control_ref.1, f32[16,32]{1,0:T(8,128)} %loc_ref.5), custom_call_target="tpu_custom_call" | custom-call | tf_op jit(solution)/shard_map/pallas_call | solution.py:528
  3.5 0.0 copy-start.6
  3.6 0.0 collective-permute-done.other_ref
  3.6 0.0 copy-start.2
  3.6 0.0 copy-start.3
  3.6 0.0 copy-start.4
  3.6 0.7 %shard_map.140.b_ref = f32[16,256]{1,0:T(8,128)S(1)} custom-call(s32[1]{0:T(128)} %bitcast.lev_ref, bf16[16,40,256]{2,1,0:T(8,128)(2,1)S(1)} %copy-done, f32[16,40,256]{2,1,0:T(8,128)S(1)} %collective-permute-done.other_ref, f32[16,32]{1,0:T(8,128)S(1)} %copy-done.5), custom_call_target="tpu_custom_call" | custom-call | tf_op jit(solution)/shard_map/pallas_call | solution.py:546
  4.3 0.0 copy-start.9
  4.3 0.0 copy-start.10
  4.3 0.0 copy-start.11
  4.4 0.0 collective-permute-done.1.perturb_ref
  4.4 3.0 %collective-permute-start.2 = (f32[16,256]{1,0:T(8,128)S(1)}, f32[16,256]{1,0:T(8,128)S(1)}, u32[]{:S(2)}, u32[]{:S(2)}) collective-permute-start(f32[16,256]{1,0:T(8,128)S(1)} %shard_map.141.refs_0_), channel_id=1, source_target_pairs={{0,16},{16,0},{1,17},{17,1},{2,18},{18,2},{3,19},{19,3},{4,20},{20... | collective-permute-start | bytes 49160 | tf_op jit(solution)/shard_map/ppermute | solution.py:552
  7.4 0.0 copy-done.3
  7.4 0.0 copy-done.4
  7.4 0.0 copy-done.9
  7.4 0.0 copy-done.10
  7.4 0.0 copy-done.11
  7.4 0.6 %copy-done.8 = f32[1024]{0:T(1024)S(1)} copy-done((f32[1024]{0:T(1024)S(1)}, f32[1024]{0:T(1024)}, u32[]{:S(2)}) %copy-start.8) | copy-done | bytes 4120
  8.1 0.0 copy-done.7
  8.1 0.0 copy-done.12
  8.1 1.1 %shard_map.142 = (f32[56,128]{1,0:T(8,128)S(1)}, f32[56,128]{1,0:T(8,128)S(1)}, f32[56,128]{1,0:T(8,128)S(1)}, f32[56,128]{1,0:T(8,128)S(1)}, f32[56,128]{1,0:T(...) custom-call(s32[1]{0:T(128)} %bitcast.1.pos_ref, s32[1]{0:T(128)} %bitcast.lev_ref, ...), custom_call_target="tpu_custom_call" | custom-call | tf_op jit(solution)/shard_map/pallas_call | solution.py:543
  9.2 0.0 collective-permute-done.2.refs_1_
  9.2 4.1 %collective-permute-start.3 = (f32[88,128]{1,0:T(8,128)S(1)}, f32[88,128]{1,0:T(8,128)S(1)}, u32[]{:S(2)}, u32[]{:S(2)}) collective-permute-start(f32[88,128]{1,0:T(8,128)S(1)} %get-tuple-element.49), channel_id=1, source_target_pairs={{0,12},{1,13},{2,14},{3,15},{4,8},{5,9},{6,10},{7,11},{8,4},{9,5},... | collective-permute-start | bytes 135176 | tf_op jit(solution)/shard_map/ppermute | solution.py:566
  13.3 1.2 %collective-permute-start.4 = (f32[88,128]{1,0:T(8,128)S(1)}, f32[88,128]{1,0:T(8,128)S(1)}, u32[]{:S(2)}, u32[]{:S(2)}) collective-permute-start(f32[88,128]{1,0:T(8,128)S(1)} %get-tuple-element.50), channel_id=1, source_target_pairs={{0,14},{1,15},{2,12},{3,13},{4,10},{5,11},{6,8},{7,9},{8,6},{9,7},... | collective-permute-start | bytes 135176 | tf_op jit(solution)/shard_map/ppermute | solution.py:566
  14.5 0.7 %collective-permute-start.5 = (f32[88,128]{1,0:T(8,128)S(1)}, f32[88,128]{1,0:T(8,128)S(1)}, u32[]{:S(2)}, u32[]{:S(2)}) collective-permute-start(f32[88,128]{1,0:T(8,128)S(1)} %get-tuple-element.51), channel_id=1, source_target_pairs={{0,10},{1,7},{2,8},{3,5},{4,14},{5,3},{6,12},{7,1},{8,2},{9,15},{1... | collective-permute-start | bytes 135176 | tf_op jit(solution)/shard_map/ppermute | solution.py:566
  15.2 2.0 %collective-permute-start.6 = (f32[88,128]{1,0:T(8,128)S(1)}, f32[88,128]{1,0:T(8,128)S(1)}, u32[]{:S(2)}, u32[]{:S(2)}) collective-permute-start(f32[88,128]{1,0:T(8,128)S(1)} %get-tuple-element.53), channel_id=1, source_target_pairs={{0,8},{1,5},{2,10},{3,7},{4,12},{5,1},{6,14},{7,3},{8,0},{9,13},{1... | collective-permute-start | bytes 135176 | tf_op jit(solution)/shard_map/ppermute | solution.py:566
  17.2 2.3 %collective-permute-start.7 = (f32[88,128]{1,0:T(8,128)S(1)}, f32[88,128]{1,0:T(8,128)S(1)}, u32[]{:S(2)}, u32[]{:S(2)}) collective-permute-start(f32[88,128]{1,0:T(8,128)S(1)} %get-tuple-element.54), channel_id=1, source_target_pairs={{0,6},{1,11},{2,4},{3,9},{4,2},{5,15},{6,0},{7,13},{8,14},{9,3},{1... | collective-permute-start | bytes 135176 | tf_op jit(solution)/shard_map/ppermute | solution.py:566
  19.5 0.0 collective-permute-done.3.refs_2_
  19.6 0.8 %collective-permute-start.8 = (f32[88,128]{1,0:T(8,128)S(1)}, f32[88,128]{1,0:T(8,128)S(1)}, u32[]{:S(2)}, u32[]{:S(2)}) collective-permute-start(f32[88,128]{1,0:T(8,128)S(1)} %get-tuple-element.55), channel_id=1, source_target_pairs={{0,4},{1,9},{2,6},{3,11},{4,0},{5,13},{6,2},{7,15},{8,12},{9,1},{1... | collective-permute-start | bytes 135176 | tf_op jit(solution)/shard_map/ppermute | solution.py:566
  20.4 0.0 collective-permute-done.4.refs_3_
  20.4 1.7 %collective-permute-start.9 = (f32[88,128]{1,0:T(8,128)S(1)}, f32[88,128]{1,0:T(8,128)S(1)}, u32[]{:S(2)}, u32[]{:S(2)}) collective-permute-start(f32[88,128]{1,0:T(8,128)S(1)} %get-tuple-element.56), channel_id=1, source_target_pairs={{0,2},{1,3},{2,0},{3,1},{4,6},{5,7},{6,4},{7,5},{8,10},{9,11},{10,... | collective-permute-start | bytes 135176 | tf_op jit(solution)/shard_map/ppermute | solution.py:566
  22.0 0.0 collective-permute-done.5.refs_4_
  22.0 1.1 %shard_map.144 = (bf16[8,32,512]{2,1,0:T(8,128)(2,1)S(1)}, f32[4,16,128]{2,1,0:T(8,128)S(1)}, f32[16,1024]{1,0:T(8,128)S(1)}, bf16[8,256,128]{2,1,0:T(8,128)(2,1...) custom-call(s32[1]{0:T(128)} %bitcast.lev_ref, f32[16,32]{1,0:T(8,128)S(1)} %copy-done.5, ...), custom_call_target="tpu_custom_call" | custom-call | tf_op jit(solution)/shard_map/pallas_call | solution.py:576
  23.2 0.0 collective-permute-done.6.refs_5_
  23.2 0.0 collective-permute-done.7.refs_6_
  23.2 0.4 %collective-permute-done.8.refs_7_ = f32[88,128]{1,0:T(8,128)S(1)} collective-permute-done((f32[88,128]{1,0:T(8,128)S(1)}, f32[88,128]{1,0:T(8,128)S(1)}, u32[]{:S(2)}, u32[]{:S(2)}) %collective-permute-start.8) | collective-permute-done | bytes 45088 | tf_op jit(solution)/shard_map/ppermute | solution.py:566
  23.6 1.0 %shard_map.145 = (bf16[8,32,384]{2,1,0:T(8,128)(2,1)S(1)}, f32[7,16,128]{2,1,0:T(8,128)S(1)}, f32[16,1024]{1,0:T(8,128)S(1)}) custom-call(s32[1]{0:T(128)} %bitcast.lev_ref, f32[16,32]{1,0:T(8,128)S(1)} %copy-done.5, f32[32,128]{1,0:T(8,128)S(1)} %get-tuple-element.47.refs_0_, f32[56,128]{1,0:T(8,128)S(1)} %get-tuple-element.48.refs_1_, ...), custom_call_target="tpu_custom_call" | custom-call | tf_op jit(solution)/shard_map/pallas_call | solution.py:576
  24.6 0.0 collective-permute-done.9.refs_8_
  24.6 0.0 copy-start.1
  24.6 0.9 %shard_map.146 = (f32[160,128]{1,0:T(8,128)S(1)}, bf16[8,32,128]{2,1,0:T(8,128)(2,1)S(1)}, f32[8,16,128]{2,1,0:T(8,128)S(1)}) custom-call(s32[1]{0:T(128)} %bitcast.1.pos_ref, s32[1]{0:T(128)} %bitcast.lev_ref, f32[128,128]{1,0:T(8,128)S(1)} %get-tuple-element.52.mix_ref, f32[32,128]{1,0:T(8,128)S(1)} %get-tuple-element.47.refs_0_, ...), custom_call_target="tpu_custom_call" | custom-call | tf_op jit(solution)/shard_map/pallas_call | solution.py:587
  25.5 0.0 collective-permute-start.10
  25.5 0.2 copy-done.1
  25.7 0.4 %shard_map.147.own_ref = f32[16,40,256]{2,1,0:T(8,128)S(1)} custom-call(bf16[16,40,256]{2,1,0:T(8,128)(2,1)S(1)} %copy-done, f32[160,128]{1,0:T(8,128)S(1)} %get-tuple-element.63.mine_ref, bf16[2,128,128]{2,1,0:T(8,128)(2,1)S(1)} %get-tuple-element.64.weights_ref, f32[16,40,256]{2,1,0:T(8,128)S(1)} %copy-done.1), custom_call_target="tpu_custom_call" | custom-call | tf_op jit(solution)/shard_map/pallas_call | solution.py:616
  26.1 0.3 %shard_map.148 = (f32[16,1024]{1,0:T(8,128)S(1)}, f32[16,1024]{1,0:T(8,128)S(1)}) custom-call(s32[1]{0:T(128)} %bitcast.1.pos_ref, s32[1]{0:T(128)} %bitcast.lev_ref, bf16[8,32,512]{2,1,0:T(8,128)(2,1)S(1)} %get-tuple-element.57.refs_8_.refs_9_.refs_0_, bf16[8,32,384]{2,1,0:T(8,128)(2,1)S(1)} %get-tuple-element.60.refs_10_.refs_1_, ...), custom_call_target="tpu_custom_call" | custom-call | tf_op jit(solution)/shard_map/pallas_call | solution.py:593
  26.5 0.3 %collective-permute-done.10.theirs_ref = f32[160,128]{1,0:T(8,128)S(1)} collective-permute-done((f32[160,128]{1,0:T(8,128)S(1)}, f32[160,128]{1,0:T(8,128)S(1)}, u32[]{:S(2)}, u32[]{:S(2)}) %collective-permute-start.10) | collective-permute-done | bytes 81952 | tf_op jit(solution)/shard_map/ppermute | solution.py:615
  26.8 1.2 %shard_map.149 = (f32[16,40,256]{2,1,0:T(8,128)}, f32[16,1024]{1,0:T(8,128)}, f32[16,1024]{1,0:T(8,128)}) custom-call(bf16[16,40,256]{2,1,0:T(8,128)(2,1)S(1)} %collective-permute-done.1.perturb_ref, f32[160,128]{1,0:T(8,128)S(1)} %collective-permute-done.10.theirs_ref, f32[16,40,256]{2,1,0:T(8,128)S(1)} %shard_map.147.own_ref, ...), custom_call_target="tpu_custom_call" | custom-call | tf_op jit(solution)/shard_map/pallas_call | solution.py:617
  (11 shorter events, 0.1 us)
Async XLA Ops:
  0.6 2.9 %collective-permute-start = (f32[16,40,256]{2,1,0:T(8,128)}, f32[16,40,256]{2,1,0:T(8,128)S(1)}, u32[]{:S(2)}, u32[]{:S(2)}) collective-permute-start(f32[16,40,256]{2,1,0:T(8,128)} %control_ref.1), channel_id=1, source_target_pairs={{0,1},{1,0},{2,3},{3,2},{4,5},{5,4},{6,7},{7,6},{8,9},{9,8},{10,11... | collective-permute-start | bytes 1966088 | tf_op jit(solution)/shard_map/ppermute | solution.py:527
  1.1 3.2 %collective-permute-start.1 = (bf16[16,40,256]{2,1,0:T(8,128)(2,1)}, bf16[16,40,256]{2,1,0:T(8,128)(2,1)S(1)}, u32[]{:S(2)}, u32[]{:S(2)}) collective-permute-start(bf16[16,40,256]{2,1,0:T(8,128)(2,1)} %perturb_ref.3), channel_id=1, source_target_pairs={{0,1},{1,0},{2,3},{3,2},{4,5},{5,4},{6,7},{7,6},{8,9},{9,8},{10,11... | collective-permute-start | bytes 983048 | tf_op jit(solution)/shard_map/ppermute | solution.py:550
  1.2 2.3 %copy-start = (bf16[16,40,256]{2,1,0:T(8,128)(2,1)S(1)}, bf16[16,40,256]{2,1,0:T(8,128)(2,1)}, u32[]{:S(2)}) copy-start(bf16[16,40,256]{2,1,0:T(8,128)(2,1)} %perturb_ref.3) | copy-start | bytes 983044
  1.2 2.3 %copy-start.5 = (f32[16,32]{1,0:T(8,128)S(1)}, f32[16,32]{1,0:T(8,128)}, u32[]{:S(2)}) copy-start(f32[16,32]{1,0:T(8,128)} %loc_ref.5) | copy-start | bytes 6148
  3.5 0.8 %copy-start.6 = (f32[16,256]{1,0:T(8,128)S(1)}, f32[16,256]{1,0:T(8,128)}, u32[]{:S(2)}) copy-start(f32[16,256]{1,0:T(8,128)} %shard_map.139.a_ref) | copy-start | bytes 49156
  3.6 3.8 %copy-start.2 = (f32[16,1024]{1,0:T(8,128)S(1)}, f32[16,1024]{1,0:T(8,128)}, u32[]{:S(2)}) copy-start(f32[16,1024]{1,0:T(8,128)} %refs_5_.1) | copy-start | bytes 196612
  3.6 3.8 %copy-start.3 = (f32[16,1024]{1,0:T(8,128)S(1)}, f32[16,1024]{1,0:T(8,128)}, u32[]{:S(2)}) copy-start(f32[16,1024]{1,0:T(8,128)} %refs_8_.1) | copy-start | bytes 196612
  3.6 3.8 %copy-start.4 = (f32[16,1024]{1,0:T(8,128)S(1)}, f32[16,1024]{1,0:T(8,128)}, u32[]{:S(2)}) copy-start(f32[16,1024]{1,0:T(8,128)} %refs_9_.1) | copy-start | bytes 196612
  4.3 3.1 %copy-start.9 = (s32[1,8,128]{2,1,0:T(8,128)S(1)}, s32[1,8,128]{2,1,0:T(8,128)}, u32[]{:S(2)}) copy-start(s32[1,8,128]{2,1,0:T(8,128)} %src_ref.1) | copy-start | bytes 12292
  4.3 3.1 %copy-start.10 = (f32[1,8,128]{2,1,0:T(8,128)S(1)}, f32[1,8,128]{2,1,0:T(8,128)}, u32[]{:S(2)}) copy-start(f32[1,8,128]{2,1,0:T(8,128)} %weight_ref.1) | copy-start | bytes 12292
  4.3 3.1 %copy-start.11 = (s32[1,8,128]{2,1,0:T(8,128)S(1)}, s32[1,8,128]{2,1,0:T(8,128)}, u32[]{:S(2)}) copy-start(s32[1,8,128]{2,1,0:T(8,128)} %tgt_ref.1) | copy-start | bytes 12292
  4.4 4.8 %collective-permute-start.2 = (f32[16,256]{1,0:T(8,128)S(1)}, f32[16,256]{1,0:T(8,128)S(1)}, u32[]{:S(2)}, u32[]{:S(2)}) collective-permute-start(f32[16,256]{1,0:T(8,128)S(1)} %shard_map.141.refs_0_), channel_id=1, source_target_pairs={{0,16},{16,0},{1,17},{17,1},{2,18},{18,2},{3,19},{19,3},{4,20},{20... | collective-permute-start | bytes 49160 | tf_op jit(solution)/shard_map/ppermute | solution.py:552
  7.4 0.7 %copy-start.8 = (f32[1024]{0:T(1024)S(1)}, f32[1024]{0:T(1024)}, u32[]{:S(2)}) copy-start(f32[1024]{0:T(1024)} %param.17) | copy-start | bytes 12292
  7.4 0.7 %copy-start.7 = (f32[1024]{0:T(1024)S(1)}, f32[1024]{0:T(1024)}, u32[]{:S(2)}) copy-start(f32[1024]{0:T(1024)} %param.16) | copy-start | bytes 12292
  7.4 0.7 %copy-start.12 = (s32[1,8]{1,0:T(1,128)S(1)}, s32[1,8]{1,0:T(1,128)}, u32[]{:S(2)}) copy-start(s32[1,8]{1,0:T(1,128)} %counts_ref.1) | copy-start | bytes 100
  9.2 10.3 %collective-permute-start.3 = (f32[88,128]{1,0:T(8,128)S(1)}, f32[88,128]{1,0:T(8,128)S(1)}, u32[]{:S(2)}, u32[]{:S(2)}) collective-permute-start(f32[88,128]{1,0:T(8,128)S(1)} %get-tuple-element.49), channel_id=1, source_target_pairs={{0,12},{1,13},{2,14},{3,15},{4,8},{5,9},{6,10},{7,11},{8,4},{9,5},... | collective-permute-start | bytes 135176 | tf_op jit(solution)/shard_map/ppermute | solution.py:566
  13.3 7.1 %collective-permute-start.4 = (f32[88,128]{1,0:T(8,128)S(1)}, f32[88,128]{1,0:T(8,128)S(1)}, u32[]{:S(2)}, u32[]{:S(2)}) collective-permute-start(f32[88,128]{1,0:T(8,128)S(1)} %get-tuple-element.50), channel_id=1, source_target_pairs={{0,14},{1,15},{2,12},{3,13},{4,10},{5,11},{6,8},{7,9},{8,6},{9,7},... | collective-permute-start | bytes 135176 | tf_op jit(solution)/shard_map/ppermute | solution.py:566
  14.5 7.6 %collective-permute-start.5 = (f32[88,128]{1,0:T(8,128)S(1)}, f32[88,128]{1,0:T(8,128)S(1)}, u32[]{:S(2)}, u32[]{:S(2)}) collective-permute-start(f32[88,128]{1,0:T(8,128)S(1)} %get-tuple-element.51), channel_id=1, source_target_pairs={{0,10},{1,7},{2,8},{3,5},{4,14},{5,3},{6,12},{7,1},{8,2},{9,15},{1... | collective-permute-start | bytes 135176 | tf_op jit(solution)/shard_map/ppermute | solution.py:566
  15.2 8.0 %collective-permute-start.6 = (f32[88,128]{1,0:T(8,128)S(1)}, f32[88,128]{1,0:T(8,128)S(1)}, u32[]{:S(2)}, u32[]{:S(2)}) collective-permute-start(f32[88,128]{1,0:T(8,128)S(1)} %get-tuple-element.53), channel_id=1, source_target_pairs={{0,8},{1,5},{2,10},{3,7},{4,12},{5,1},{6,14},{7,3},{8,0},{9,13},{1... | collective-permute-start | bytes 135176 | tf_op jit(solution)/shard_map/ppermute | solution.py:566
  17.2 6.0 %collective-permute-start.7 = (f32[88,128]{1,0:T(8,128)S(1)}, f32[88,128]{1,0:T(8,128)S(1)}, u32[]{:S(2)}, u32[]{:S(2)}) collective-permute-start(f32[88,128]{1,0:T(8,128)S(1)} %get-tuple-element.54), channel_id=1, source_target_pairs={{0,6},{1,11},{2,4},{3,9},{4,2},{5,15},{6,0},{7,13},{8,14},{9,3},{1... | collective-permute-start | bytes 135176 | tf_op jit(solution)/shard_map/ppermute | solution.py:566
  19.6 4.0 %collective-permute-start.8 = (f32[88,128]{1,0:T(8,128)S(1)}, f32[88,128]{1,0:T(8,128)S(1)}, u32[]{:S(2)}, u32[]{:S(2)}) collective-permute-start(f32[88,128]{1,0:T(8,128)S(1)} %get-tuple-element.55), channel_id=1, source_target_pairs={{0,4},{1,9},{2,6},{3,11},{4,0},{5,13},{6,2},{7,15},{8,12},{9,1},{1... | collective-permute-start | bytes 135176 | tf_op jit(solution)/shard_map/ppermute | solution.py:566
  20.4 4.2 %collective-permute-start.9 = (f32[88,128]{1,0:T(8,128)S(1)}, f32[88,128]{1,0:T(8,128)S(1)}, u32[]{:S(2)}, u32[]{:S(2)}) collective-permute-start(f32[88,128]{1,0:T(8,128)S(1)} %get-tuple-element.56), channel_id=1, source_target_pairs={{0,2},{1,3},{2,0},{3,1},{4,6},{5,7},{6,4},{7,5},{8,10},{9,11},{10,... | collective-permute-start | bytes 135176 | tf_op jit(solution)/shard_map/ppermute | solution.py:566
  24.6 1.1 %copy-start.1 = (f32[16,40,256]{2,1,0:T(8,128)S(1)}, f32[16,40,256]{2,1,0:T(8,128)}, u32[]{:S(2)}) copy-start(f32[16,40,256]{2,1,0:T(8,128)} %control_ref.1) | copy-start | bytes 1966084
  25.5 1.3 %collective-permute-start.10 = (f32[160,128]{1,0:T(8,128)S(1)}, f32[160,128]{1,0:T(8,128)S(1)}, u32[]{:S(2)}, u32[]{:S(2)}) collective-permute-start(f32[160,128]{1,0:T(8,128)S(1)} %get-tuple-element.63.mine_ref), channel_id=1, source_target_pairs={{0,1},{1,0},{2,3},{3,2},{4,5},{5,4},{6,7},{7,6},{8,9},{9,8},{10,11... | collective-permute-start | bytes 245768 | tf_op jit(solution)/shard_map/ppermute | solution.py:615

commit v12 on v11

--- a/solution.py
+++ b/solution.py
@@ -33,21 +33,23 @@
     return both[:rows] + both[rows:]
 
 
-def spread(matrix, start, count):
-    rows, cols = matrix.shape
-
-    def iota(shape, axis):
-        return lax.broadcasted_iota(jnp.int32, shape, axis)
-
-    shape = (rows * SUB, count * SUB)
-    tall = (iota((rows * SUB, rows), 0) // SUB == iota((rows * SUB, rows), 1)).astype(BF16)
-    wide = (iota((cols, count * SUB), 1) // SUB + start == iota((cols, count * SUB), 0)).astype(BF16)
-    same = iota(shape, 0) % SUB == iota(shape, 1) % SUB
-    out = []
-    for part in halves(matrix):
-        filled = product(tall, product(part, wide).astype(BF16))
-        out.append(jnp.where(same, filled, 0.0).astype(BF16))
-    return out
+def iota(shape, axis):
+    return lax.broadcasted_iota(jnp.int32, shape, axis)
+
+
+def wide_rows(matrix, start, count):
+    cols = matrix.shape[1]
+    shape = (cols, count * SUB)
+    place = (iota(shape, 1) // SUB + start) % cols
+    pick = (place == iota(shape, 0)).astype(BF16)
+    high, low = halves(matrix)
+    return product(high, pick) + product(low, pick)
+
+
+def spread(wide):
+    rows, cols = wide.shape
+    tall = jnp.broadcast_to(wide[:, None, :], (rows, SUB, cols)).reshape(rows * SUB, cols)
+    return jnp.where(iota(tall.shape, 0) % SUB == iota(tall.shape, 1) % SUB, tall, 0.0)
 
 
 def mix(weights, values):
@@ -88,35 +90,29 @@
     return lax.fori_loop(0, n, step, init, unroll=n if n <= 8 else 1)
 
 
-def own_kernel(lev_ref, perturb_hbm, control_hbm, loc_hbm, part_ref, perturb_ref, control_ref, loc_ref, sems):
-    staged = [(loc_hbm, loc_ref), (control_hbm, control_ref), (perturb_hbm, perturb_ref)]
-    copies = [pltpu.make_async_copy(source, target, sems.at[i]) for i, (source, target) in enumerate(staged)]
-    for copy in copies:
-        copy.start()
-    levels = perturb_ref.shape[0]
-    copies[0].wait()
-    weights = spread(loc_ref[...], lev_ref[0] * levels, levels)
-    copies[1].wait()
-    copies[2].wait()
-    part_ref[...] = mixed_sum(weights, perturb_ref, control_ref)
-
-
-def mixed_sum(weights, perturb_ref, control_ref):
+def mix_kernel(lev_ref, loc_ref, mix_ref, own_ref, given_ref):
+    levels = loc_ref.shape[0]
+    start = lev_ref[0] * levels
+    loc = loc_ref[...]
+    mix_ref[0], mix_ref[1] = halves(spread(wide_rows(loc, start, 2 * levels)))
+    own_ref[0], own_ref[1] = halves(spread(wide_rows(loc, start, levels)).T)
+    given_ref[...] = wide_rows(loc, levels - start, levels)
+
+
+def sum_kernel(perturb_ref, control_ref, other_ref, mix_ref, out_ref):
     levels, members, cols = perturb_ref.shape
     perturb = perturb_ref[...].astype(F32)
     total = jnp.zeros((levels, SUB, cols), F32)
     for m in range(0, members, SUB):
-        tile = control_ref[:, m : m + SUB, :].reshape(levels * SUB, cols)
-        total = total + perturb[:, m : m + SUB, :] * mix(weights, tile).reshape(levels, SUB, cols)
-    return jnp.sum(total, axis=1)
-
-
-def band_kernel(lev_ref, counts_ref, perturb_ref, other_ref, part_ref, loc_ref, static_ref, src_ref, weight_ref,
-                out_ref, acc_ref):
-    levels, members, cols = perturb_ref.shape
-    weights = spread(loc_ref[...], (1 - lev_ref[0]) * levels, levels)
-    band_sum = part_ref[...] + mixed_sum(weights, perturb_ref, other_ref)
-    acc_ref[...] = jnp.concatenate(halves(band_sum), axis=0)
+        tile = jnp.concatenate([control_ref[:, m : m + SUB, :], other_ref[:, m : m + SUB, :]], axis=0)
+        mixed = mix((mix_ref[0], mix_ref[1]), tile.reshape(2 * levels * SUB, cols))
+        total = total + perturb[:, m : m + SUB, :] * mixed.reshape(levels, SUB, cols)
+    out_ref[...] = jnp.sum(total, axis=1)
+
+
+def band_kernel(counts_ref, sum_ref, static_ref, src_ref, weight_ref, out_ref, acc_ref):
+    levels, cols = sum_ref.shape
+    acc_ref[...] = jnp.concatenate(halves(sum_ref[...]), axis=0)
     n = src_ref.shape[1]
     edges = edge_rows(static_ref[...])
 
@@ -190,30 +186,6 @@
     grad_ref[...] = partial_ref[...] + (jnp.where(lane == 0, before, 0.0) + jnp.where(lane == cols - 1, after, 0.0))
 
 
-def ens_weights(loc, start, count):
-    full = loc.shape[0]
-
-    def iota(shape, axis):
-        return lax.broadcasted_iota(jnp.int32, shape, axis)
-
-    shape = (count * SUB, full * SUB)
-    pick_l = (iota((count * SUB, loc.shape[1]), 0) // SUB + start == iota((count * SUB, loc.shape[1]), 1)).astype(BF16)
-    pick_k = (iota((full, full * SUB), 1) // SUB == iota((full, full * SUB), 0)).astype(BF16)
-    same = iota(shape, 0) % SUB == iota(shape, 1) % SUB
-    weights = []
-    for part in halves(loc):
-        wide = product(product(pick_l, part, ((1,), (1,))).astype(BF16), pick_k)
-        weights.append(jnp.where(same, wide, 0.0).astype(BF16))
-    return weights
-
-
-def mix_kernel(lev_ref, loc_ref, own_ref, given_ref):
-    levels = loc_ref.shape[0]
-    own_ref[0], own_ref[1] = ens_weights(loc_ref[...], lev_ref[0] * levels, levels)
-    high, low = ens_weights(loc_ref[...], (1 - lev_ref[0]) * levels, levels)
-    given_ref[...] = high.astype(F32) + low.astype(F32)
-
-
 def band_rows(band, weights):
     width = weights.shape[1]
     return jnp.concatenate([band[:, at : at + width] for at in range(0, band.shape[1], width)] + [weights], axis=0)
@@ -242,7 +214,8 @@
     copies = [pltpu.make_async_copy(a, b, sems.at[i]) for i, (a, b) in enumerate(zip(flats, flat_hbms))]
     for copy in copies:
         copy.start()
-    weights = halves(theirs_ref[theirs_ref.shape[0] - theirs_ref.shape[1] :, :])
+    levels = perturb_ref.shape[0]
+    weights = halves(spread(theirs_ref[theirs_ref.shape[0] - levels :, :]).T)
     for place, values in ens_tiles(perturb_ref, theirs_ref, weights, own_ref):
         out_ref[place] = values
         copies.append(pltpu.make_async_copy(out_ref.at[place], out_hbm.at[place], sems.at[len(copies)]))
@@ -301,16 +274,6 @@
         out_ref[rows.edge :, :] = edge
 
 
-def other_kernel(lev_ref, perturb_ref, other_ref, loc_ref, out_ref):
-    levels = perturb_ref.shape[0]
-    weights = spread(loc_ref[...], (1 - lev_ref[0]) * levels, levels)
-    out_ref[...] = mixed_sum(weights, perturb_ref, other_ref)
-
-
-def add_kernel(a_ref, b_ref, out_ref):
-    out_ref[...] = a_ref[...] + b_ref[...]
-
-
 def blocks_kernel(groups, *refs):
     sums = refs[:groups]
     count = (len(refs) - groups - 1) // 2
@@ -392,17 +355,16 @@
     return blocks, refs[len(labels) - 1 :]
 
 
-def stage_kernel(n, levels, band, cols, stages, lev_ref, loc_ref, *refs):
+def stage_kernel(n, levels, band, cols, stages, *refs):
     known = sum(stages[:-1], [])
     blocks, refs = open_blocks(known + stages[-1], refs, n, levels, band)
     old, refs = refs[: len(stages) - 1], refs[len(stages) - 1 :]
     if known:
         met_old, remap_old, slots_ref, met_ref, remap_ref = refs
     else:
-        slots_ref, met_ref, remap_ref, pick_ref, own_ref, given_ref = refs
+        slots_ref, met_ref, remap_ref, pick_ref = refs
         for d in range(n):
             pick_ref[d] = pick_source(blocks[0], d)
-        mix_kernel(lev_ref, loc_ref, own_ref, given_ref)
     fill_slots(stages[-1], blocks, n, slots_ref)
     for i, (d, block) in enumerate(blocks.items()):
         met = met_at(d, block, stages[-1], slots_ref)
@@ -490,14 +452,15 @@
     grad_ref[...] = static + diag_ref[...] * misfit + left + right
 
 
-def call(kernel, out_shape, spaces, scratch=(), limit=40 * MIB, out=VMEM):
+def call(kernel, out_shape, spaces, scratch=(), out=VMEM, cost=None):
     return pl.pallas_call(
         kernel,
         out_shape=out_shape,
         in_specs=spaces,
         out_specs=jax.tree.map(lambda _: out, out_shape),
         scratch_shapes=scratch,
-        compiler_params=pltpu.CompilerParams(vmem_limit_bytes=limit),
+        cost_estimate=cost,
+        compiler_params=pltpu.CompilerParams(vmem_limit_bytes=40 * MIB),
     )
 
 
@@ -525,17 +488,16 @@
     lev = lax.axis_index("lev").astype(jnp.int32).reshape(1)
     pos = lax.axis_index("tile").astype(jnp.int32).reshape(1)
     other_control = lax.ppermute(control, "lev", swap)
-    part = call(
-        own_kernel,
-        shape((levels, band_cols), F32),
-        [SMEM] + [HBM] * 3,
-        [pltpu.VMEM(a.shape, a.dtype) for a in (perturb, control, level_loc)] + [pltpu.SemaphoreType.DMA((3,))],
-        limit=58 * MIB,
-    )(lev, perturb, control, level_loc)
+    width = levels * SUB
+    level_mix, own_mix, given_mix = call(
+        mix_kernel,
+        (shape((2, width, 2 * width), BF16), shape((2, width, width), BF16), shape((levels, width), F32)),
+        [SMEM, VMEM],
+        cost=pl.CostEstimate(flops=10**9, bytes_accessed=0, transcendentals=0),
+    )(lev, level_loc)
+    own_sum = call(sum_kernel, shape((levels, band_cols), F32), [VMEM] * 4)(perturb, control, other_control, level_mix)
     flat = shape((levels, tile_cols), F32)
-    width = levels * SUB
-    mine_shape = shape((band_cols // width * levels + width, width), F32)
-    mix_shapes = [shape((2, width, width), BF16), shape((width, width), F32)]
+    mine_shape = shape((band_cols // width * levels + levels, width), F32)
     diag, off = filter_diag.reshape(1, -1), filter_off.reshape(1, -1)
     if n * cap <= tile_cols and n >= 8 and lax.axis_size("lev") == 2 and n & (n - 1) == 0 and band_cols * tile_cols <= 2**20:
         rows = Rows(levels, n)
@@ -543,10 +505,7 @@
         rests = call(functools.partial(static_kernel, band_cols), [shape((rows.total, cap), F32)] * n, [SMEM] * 3 + [VMEM] * 8)(
             pos, lev, counts, static_control, diag, off, obs_weight, innovation, send_src, send_wt, recv_tgt
         )
-        other_part = call(other_kernel, shape((levels, band_cols), F32), [SMEM] + [VMEM] * 3)(
-            lev, perturb, other_control, level_loc
-        )
-        sums = [call(add_kernel, shape((levels, band_cols), F32), [VMEM] * 2)(part, other_part)]
+        sums = [own_sum]
         sums[0], other_perturb = lax.optimization_barrier((sums[0], lax.ppermute(perturb, "lev", swap)))
         for k in range(1, groups):
             sums.append(lax.ppermute(sums[0], "grp", [(g, (g + k) % groups) for g in range(groups)]))
@@ -564,7 +523,7 @@
         for r in sum(stages, [])[1:]:
             pairs = [(i * levs + v, (i ^ relabel(r, n, v)) * levs + v) for i in range(n) for v in range(levs)]
             arrived[r] = [lax.ppermute(blocks[r - 1], ("tile", "lev"), pairs)]
-        slots, carried, made = [], [], []
+        slots, carried, picks = [], [], []
         for count in range(1, len(stages)):
             labels = sum(stages[:count], [])
             refs = [ref for r in labels for ref in arrived[r]]
@@ -572,18 +531,17 @@
                 shape((n, 2 * levels, len(stages[count - 1]) * cap), BF16),
                 shape((len(labels), levels, cap), F32),
                 flat,
-            ] + [shape((n, band_cols, cap), BF16), *mix_shapes] * (count == 1)
+            ] + [shape((n, band_cols, cap), BF16)] * (count == 1)
             new, *carried = call(
                 functools.partial(stage_kernel, n, levels, band_cols, tile_cols, stages[:count]),
                 outs,
-                [SMEM] + [VMEM] * (1 + len(refs) + len(slots) + len(carried)),
-            )(lev, level_loc, *refs, *slots, *carried)
+                [VMEM] * (len(refs) + len(slots) + len(carried)),
+            )(*refs, *slots, *carried)
             slots.append(new)
-            made += carried[2:]
+            picks += carried[2:]
             carried = carried[:2]
         met, remap = carried
-        picks, own_mix, given_mix = made
-        refs = [ref for r in sum(stages, []) for ref in arrived[r]] + slots + [met, picks]
+        refs = [ref for r in sum(stages, []) for ref in arrived[r]] + slots + [met] + picks
         mine, new, tables = call(
             functools.partial(shared_kernel, n, levels, band_cols, tile_cols, stages),
             (mine_shape, shape((n, 2 * levels, len(stages[-1]) * cap), BF16), shape((n, n + EXTRA, cap), F32)),
@@ -598,9 +556,9 @@
         payload = call(
             band_kernel,
             shape((groups, n, levels + EXTRA, cap), F32),
-            [SMEM] * 2 + [VMEM] * 7,
+            [SMEM] + [VMEM] * 4,
             [pltpu.VMEM((2 * levels, band_cols), BF16)],
-        )(lev, counts, perturb, other_control, part, level_loc, static_control, send_src, send_wt)
+        )(counts, own_sum, static_control, send_src, send_wt)
         arrived = lax.all_to_all(
             payload.reshape(groups * n, levels + EXTRA, cap), ("grp", "tile"), split_axis=0, concat_axis=0, tiled=True
         ).reshape(groups, n, levels + EXTRA, cap)
@@ -608,7 +566,6 @@
             tile_kernel, (flat, flat, shape((n, levels + EXTRA, cap), F32)), [SMEM] + [VMEM] * 7
         )(pos, arrived, recv_tgt, static_control, diag, off, obs_weight, innovation)
         returned = lax.all_to_all(giving, "tile", split_axis=0, concat_axis=0, tiled=True)
-        own_mix, given_mix = call(mix_kernel, mix_shapes, [SMEM, VMEM])(lev, level_loc)
         grad_static, mine = call(
             functools.partial(adjoint_kernel, band_cols), (flat, mine_shape), [SMEM, SMEM] + [VMEM] * 5
         )(pos, counts, returned, send_src, send_wt, partial, given_mix)

time: 28.2 us -> 27.4 us (0.972)
  Pallas kernels: 9.03 us -> 6.66 us
  waiting for transfers between devices: 0.74 us -> 2 us
  local copies, waits for them, and re-layouts: 0.93 us -> 1.39 us
    pallas_call x3 -> x2, Pallas kernels: 2.99 us -> 0.73 us  [the longest x1 0.49 us: body(): call(sum_kernel, shape((levels, band_cols), F32), [VMEM] * 4)]
    ppermute x1, waiting for transfers between devices: 0.01 us -> 0.9 us  [body(): other_control = lax.ppermute(control, 'lev', swap)]
    unnamed x26 -> x24, local copies, waits for them, and re-layouts: 0.93 us -> 1.39 us
  transfers between devices with their start and end apart: 11 -> 11, of which waited for: 2 -> 4; matrix products, arithmetic and copies ran while one was open for 0% -> 0% of each run, Pallas kernels for 25% -> 17%
where the time goes in v12:
time: 27.4 us; the launch traced here: 27.2 us
  starting transfers between devices  16.4 us (60%)
  Pallas kernels  6.66 us (24%)
  waiting for transfers between devices  2 us (7%)
  local copies, waits for them, and re-layouts  1.39 us (5%)
  between operations  0.78 us (3%)
    ppermute x7, starting transfers between devices, body(): arrived[r] = [lax.ppermute(blocks[r - 1], ('tile', 'lev'), pairs)]  12.8 us
    ppermute x1, starting transfers between devices, body(): lax.ppermute(sums[0], 'grp', [(g, (g + k) % groups) for g in range(groups)])  2.97 us
    pallas_call x2, Pallas kernels, body(): call(functools.partial(stage_kernel, n, levels, band_cols, tile_cols, sta...  1.9 us
    unnamed x24, local copies, waits for them, and re-layouts  1.39 us
    pallas_call x1, Pallas kernels, body(): call(ens_kernel, (shape(control.shape, F32), flat, flat), [VMEM] * 5, [pl...  1.24 us
    pallas_call x1, Pallas kernels, body(): call(functools.partial(static_kernel, band_cols), [shape((rows.total, cap...  1.11 us
    ppermute x1, waiting for transfers between devices, body(): other_control = lax.ppermute(control, 'lev', swap)  0.9 us
    pallas_call x1, Pallas kernels, body(): call(functools.partial(shared_kernel, n, levels, band_cols, tile_cols, st...  0.88 us
  transfers between devices with their start and end apart: 11, of which 4 were waited for; matrix products, arithmetic and copies ran while one was open for 0% of the time, Pallas kernels for 17%

profile of v12, /device:TPU:0, one launch (start us, length us, event | category | flops | bytes accessed | tf_op | source)
XLA Modules:
  0.0 27.2 jit_solution(519119820153532422)
XLA Ops:
  0.6 0.5 %collective-permute-start = (f32[16,40,256]{2,1,0:T(8,128)}, f32[16,40,256]{2,1,0:T(8,128)S(1)}, u32[]{:S(2)}, u32[]{:S(2)}) collective-permute-start(f32[16,40,256]{2,1,0:T(8,128)} %control_ref.3), channel_id=1, source_target_pairs={{0,1},{1,0},{2,3},{3,2},{4,5},{5,4},{6,7},{7,6},{8,9},{9,8},{10,11... | collective-permute-start | bytes 1966088 | tf_op jit(solution)/shard_map/ppermute | solution.py:490
  1.1 0.1 collective-permute-start.1
  1.2 0.0 copy-start.11
  1.2 0.7 %copy-done.11 = f32[16,32]{1,0:T(8,128)S(1)} copy-done((f32[16,32]{1,0:T(8,128)S(1)}, f32[16,32]{1,0:T(8,128)}, u32[]{:S(2)}) %copy-start.11) | copy-done | bytes 2072
  1.9 0.0 copy-start
  1.9 0.2 shard_map.139
  2.2 0.9 %collective-permute-done.other_ref = f32[16,40,256]{2,1,0:T(8,128)S(1)} collective-permute-done((f32[16,40,256]{2,1,0:T(8,128)}, f32[16,40,256]{2,1,0:T(8,128)S(1)}, u32[]{:S(2)}, u32[]{:S(2)}) %collective-permute-start) | collective-permute-done | bytes 655392 | tf_op jit(solution)/shard_map/ppermute | solution.py:490
  3.1 0.0 copy-done
  3.1 0.0 copy-done.1
  3.1 0.0 copy-start.7
  3.1 0.0 copy-start.8
  3.1 0.0 copy-start.9
  3.1 0.5 %shard_map.140.refs_0_ = f32[16,256]{1,0:T(8,128)S(1)} custom-call(bf16[16,40,256]{2,1,0:T(8,128)(2,1)S(1)} %copy-done.1, f32[16,40,256]{2,1,0:T(8,128)S(1)} %copy-done, f32[16,40,256]{2,1,0:T(8,128)S(1)} %collective-permute-done.other_ref, bf16[2,128,256]{2,1,0:T(8,128)(2,1)S(1)} %get-tuple-element.39.mix_ref), custom_call_target="tpu_custom_call" | custom-call | tf_op jit(solution)/shard_map/pallas_call | solution.py:498
  3.6 0.0 collective-permute-done.1.perturb_ref
  3.7 3.0 %collective-permute-start.2 = (f32[16,256]{1,0:T(8,128)S(1)}, f32[16,256]{1,0:T(8,128)S(1)}, u32[]{:S(2)}, u32[]{:S(2)}) collective-permute-start(f32[16,256]{1,0:T(8,128)S(1)} %shard_map.140.refs_0_), channel_id=1, source_target_pairs={{0,16},{16,0},{1,17},{17,1},{2,18},{18,2},{3,19},{19,3},{4,20},{20... | collective-permute-start | bytes 49160 | tf_op jit(solution)/shard_map/ppermute | solution.py:511
  6.6 0.0 copy-done.2
  6.6 0.0 copy-done.3
  6.6 0.0 copy-done.4
  6.7 0.0 copy-done.7
  6.7 0.0 copy-done.8
  6.7 0.0 copy-done.9
  6.7 0.6 %copy-done.6 = f32[1024]{0:T(1024)S(1)} copy-done((f32[1024]{0:T(1024)S(1)}, f32[1024]{0:T(1024)}, u32[]{:S(2)}) %copy-start.6) | copy-done | bytes 4120
  7.3 0.0 copy-done.5
  7.3 0.0 copy-done.10
  7.3 1.1 %shard_map.141 = (f32[56,128]{1,0:T(8,128)S(1)}, f32[56,128]{1,0:T(8,128)S(1)}, f32[56,128]{1,0:T(8,128)S(1)}, f32[56,128]{1,0:T(8,128)S(1)}, f32[56,128]{1,0:T(...) custom-call(s32[1]{0:T(128)} %bitcast.1.pos_ref, s32[1]{0:T(128)} %bitcast.lev_ref, ...), custom_call_target="tpu_custom_call" | custom-call | tf_op jit(solution)/shard_map/pallas_call | solution.py:505
  8.4 0.0 collective-permute-done.2.refs_1_
  8.5 4.1 %collective-permute-start.3 = (f32[88,128]{1,0:T(8,128)S(1)}, f32[88,128]{1,0:T(8,128)S(1)}, u32[]{:S(2)}, u32[]{:S(2)}) collective-permute-start(f32[88,128]{1,0:T(8,128)S(1)} %get-tuple-element.52), channel_id=1, source_target_pairs={{0,12},{1,13},{2,14},{3,15},{4,8},{5,9},{6,10},{7,11},{8,4},{9,5},... | collective-permute-start | bytes 135176 | tf_op jit(solution)/shard_map/ppermute | solution.py:525
  12.6 1.2 %collective-permute-start.4 = (f32[88,128]{1,0:T(8,128)S(1)}, f32[88,128]{1,0:T(8,128)S(1)}, u32[]{:S(2)}, u32[]{:S(2)}) collective-permute-start(f32[88,128]{1,0:T(8,128)S(1)} %get-tuple-element.53), channel_id=1, source_target_pairs={{0,14},{1,15},{2,12},{3,13},{4,10},{5,11},{6,8},{7,9},{8,6},{9,7},... | collective-permute-start | bytes 135176 | tf_op jit(solution)/shard_map/ppermute | solution.py:525
  13.7 0.7 %collective-permute-start.5 = (f32[88,128]{1,0:T(8,128)S(1)}, f32[88,128]{1,0:T(8,128)S(1)}, u32[]{:S(2)}, u32[]{:S(2)}) collective-permute-start(f32[88,128]{1,0:T(8,128)S(1)} %get-tuple-element.54), channel_id=1, source_target_pairs={{0,10},{1,7},{2,8},{3,5},{4,14},{5,3},{6,12},{7,1},{8,2},{9,15},{1... | collective-permute-start | bytes 135176 | tf_op jit(solution)/shard_map/ppermute | solution.py:525
  14.5 2.0 %collective-permute-start.6 = (f32[88,128]{1,0:T(8,128)S(1)}, f32[88,128]{1,0:T(8,128)S(1)}, u32[]{:S(2)}, u32[]{:S(2)}) collective-permute-start(f32[88,128]{1,0:T(8,128)S(1)} %get-tuple-element.55), channel_id=1, source_target_pairs={{0,8},{1,5},{2,10},{3,7},{4,12},{5,1},{6,14},{7,3},{8,0},{9,13},{1... | collective-permute-start | bytes 135176 | tf_op jit(solution)/shard_map/ppermute | solution.py:525
  16.5 2.3 %collective-permute-start.7 = (f32[88,128]{1,0:T(8,128)S(1)}, f32[88,128]{1,0:T(8,128)S(1)}, u32[]{:S(2)}, u32[]{:S(2)}) collective-permute-start(f32[88,128]{1,0:T(8,128)S(1)} %get-tuple-element.56), channel_id=1, source_target_pairs={{0,6},{1,11},{2,4},{3,9},{4,2},{5,15},{6,0},{7,13},{8,14},{9,3},{1... | collective-permute-start | bytes 135176 | tf_op jit(solution)/shard_map/ppermute | solution.py:525
  18.8 0.0 collective-permute-done.3.refs_2_
  18.8 0.8 %collective-permute-start.8 = (f32[88,128]{1,0:T(8,128)S(1)}, f32[88,128]{1,0:T(8,128)S(1)}, u32[]{:S(2)}, u32[]{:S(2)}) collective-permute-start(f32[88,128]{1,0:T(8,128)S(1)} %get-tuple-element.57), channel_id=1, source_target_pairs={{0,4},{1,9},{2,6},{3,11},{4,0},{5,13},{6,2},{7,15},{8,12},{9,1},{1... | collective-permute-start | bytes 135176 | tf_op jit(solution)/shard_map/ppermute | solution.py:525
  19.6 0.0 collective-permute-done.4.refs_3_
  19.6 1.7 %collective-permute-start.9 = (f32[88,128]{1,0:T(8,128)S(1)}, f32[88,128]{1,0:T(8,128)S(1)}, u32[]{:S(2)}, u32[]{:S(2)}) collective-permute-start(f32[88,128]{1,0:T(8,128)S(1)} %get-tuple-element.58), channel_id=1, source_target_pairs={{0,2},{1,3},{2,0},{3,1},{4,6},{5,7},{6,4},{7,5},{8,10},{9,11},{10,... | collective-permute-start | bytes 135176 | tf_op jit(solution)/shard_map/ppermute | solution.py:525
  21.3 0.0 collective-permute-done.5.refs_4_
  21.3 0.9 %shard_map.143 = (bf16[8,32,512]{2,1,0:T(8,128)(2,1)S(1)}, f32[4,16,128]{2,1,0:T(8,128)S(1)}, f32[16,1024]{1,0:T(8,128)S(1)}, bf16[8,256,128]{2,1,0:T(8,128)(2,1)S(1)}) custom-call(f32[32,128]{1,0:T(8,128)S(1)} %get-tuple-element.50.refs_0_, f32[56,128]{1,0:T(8,128)S(1)} %get-tuple-element.51.refs_1_, f32[88,128]{1,0:T(8,128)S(1)} %collective-permute-done.3.refs_2_, ...), custom_call_target="tpu_custom_call" | custom-call | tf_op jit(solution)/shard_map/pallas_call | solution.py:535
  22.2 0.0 collective-permute-done.6.refs_5_
  22.2 0.1 collective-permute-done.7.refs_6_
  22.3 0.6 %collective-permute-done.8.refs_7_ = f32[88,128]{1,0:T(8,128)S(1)} collective-permute-done((f32[88,128]{1,0:T(8,128)S(1)}, f32[88,128]{1,0:T(8,128)S(1)}, u32[]{:S(2)}, u32[]{:S(2)}) %collective-permute-start.8) | collective-permute-done | bytes 45088 | tf_op jit(solution)/shard_map/ppermute | solution.py:525
  22.9 1.0 %shard_map.144 = (bf16[8,32,384]{2,1,0:T(8,128)(2,1)S(1)}, f32[7,16,128]{2,1,0:T(8,128)S(1)}, f32[16,1024]{1,0:T(8,128)S(1)}) custom-call(f32[32,128]{1,0:T(8,128)S(1)} %get-tuple-element.50.refs_0_, f32[56,128]{1,0:T(8,128)S(1)} %get-tuple-element.51.refs_1_, f32[88,128]{1,0:T(8,128)S(1)} %collective-permute-done.3.refs_2_, ...), custom_call_target="tpu_custom_call" | custom-call | tf_op jit(solution)/shard_map/pallas_call | solution.py:535
  23.8 0.0 collective-permute-done.9.refs_8_
  23.8 0.9 %shard_map.145 = (f32[48,128]{1,0:T(8,128)S(1)}, bf16[8,32,128]{2,1,0:T(8,128)(2,1)S(1)}, f32[8,16,128]{2,1,0:T(8,128)S(1)}) custom-call(s32[1]{0:T(128)} %bitcast.1.pos_ref, s32[1]{0:T(128)} %bitcast.lev_ref, f32[16,128]{1,0:T(8,128)S(1)} %get-tuple-element.41.mix_ref, f32[32,128]{1,0:T(8,128)S(1)} %get-tuple-element.50.refs_0_, ...), custom_call_target="tpu_custom_call" | custom-call | tf_op jit(solution)/shard_map/pallas_call | solution.py:545
  24.7 0.0 collective-permute-start.10
  24.7 0.4 %shard_map.146.own_ref = f32[16,40,256]{2,1,0:T(8,128)S(1)} custom-call(bf16[16,40,256]{2,1,0:T(8,128)(2,1)S(1)} %copy-done.1, f32[48,128]{1,0:T(8,128)S(1)} %get-tuple-element.65.mine_ref, bf16[2,128,128]{2,1,0:T(8,128)(2,1)S(1)} %get-tuple-element.66.weights_ref, f32[16,40,256]{2,1,0:T(8,128)S(1)} %copy-done), custom_call_target="tpu_custom_call" | custom-call | tf_op jit(solution)/shard_map/pallas_call | solution.py:573
  25.2 0.3 %shard_map.147 = (f32[16,1024]{1,0:T(8,128)S(1)}, f32[16,1024]{1,0:T(8,128)S(1)}) custom-call(s32[1]{0:T(128)} %bitcast.1.pos_ref, s32[1]{0:T(128)} %bitcast.lev_ref, bf16[8,32,512]{2,1,0:T(8,128)(2,1)S(1)} %get-tuple-element.59.refs_8_.refs_9_.refs_0_, bf16[8,32,384]{2,1,0:T(8,128)(2,1)S(1)} %get-tuple-element.62.refs_10_.refs_1_, ...), custom_call_target="tpu_custom_call" | custom-call | tf_op jit(solution)/shard_map/pallas_call | solution.py:551
  25.5 0.4 %collective-permute-done.10.theirs_ref = f32[48,128]{1,0:T(8,128)S(1)} collective-permute-done((f32[48,128]{1,0:T(8,128)S(1)}, f32[48,128]{1,0:T(8,128)S(1)}, u32[]{:S(2)}, u32[]{:S(2)}) %collective-permute-start.10) | collective-permute-done | bytes 24608 | tf_op jit(solution)/shard_map/ppermute | solution.py:572
  25.9 1.2 %shard_map.148 = (f32[16,40,256]{2,1,0:T(8,128)}, f32[16,1024]{1,0:T(8,128)}, f32[16,1024]{1,0:T(8,128)}) custom-call(bf16[16,40,256]{2,1,0:T(8,128)(2,1)S(1)} %collective-permute-done.1.perturb_ref, f32[48,128]{1,0:T(8,128)S(1)} %collective-permute-done.10.theirs_ref, f32[16,40,256]{2,1,0:T(8,128)S(1)} %shard_map.146.own_ref, ...), custom_call_target="tpu_custom_call" | custom-call | tf_op jit(solution)/shard_map/pallas_call | solution.py:574
  (8 shorter events, 0.0 us)
Async XLA Ops:
  0.6 2.5 %collective-permute-start = (f32[16,40,256]{2,1,0:T(8,128)}, f32[16,40,256]{2,1,0:T(8,128)S(1)}, u32[]{:S(2)}, u32[]{:S(2)}) collective-permute-start(f32[16,40,256]{2,1,0:T(8,128)} %control_ref.3), channel_id=1, source_target_pairs={{0,1},{1,0},{2,3},{3,2},{4,5},{5,4},{6,7},{7,6},{8,9},{9,8},{10,11... | collective-permute-start | bytes 1966088 | tf_op jit(solution)/shard_map/ppermute | solution.py:490
  1.1 2.5 %collective-permute-start.1 = (bf16[16,40,256]{2,1,0:T(8,128)(2,1)}, bf16[16,40,256]{2,1,0:T(8,128)(2,1)S(1)}, u32[]{:S(2)}, u32[]{:S(2)}) collective-permute-start(bf16[16,40,256]{2,1,0:T(8,128)(2,1)} %perturb_ref.3), channel_id=1, source_target_pairs={{0,1},{1,0},{2,3},{3,2},{4,5},{5,4},{6,7},{7,6},{8,9},{9,8},{10,11... | collective-permute-start | bytes 983048 | tf_op jit(solution)/shard_map/ppermute | solution.py:509
  1.2 0.7 %copy-start.11 = (f32[16,32]{1,0:T(8,128)S(1)}, f32[16,32]{1,0:T(8,128)}, u32[]{:S(2)}) copy-start(f32[16,32]{1,0:T(8,128)} %loc_ref.1) | copy-start | bytes 6148
  1.9 1.2 %copy-start = (f32[16,40,256]{2,1,0:T(8,128)S(1)}, f32[16,40,256]{2,1,0:T(8,128)}, u32[]{:S(2)}) copy-start(f32[16,40,256]{2,1,0:T(8,128)} %control_ref.3) | copy-start | bytes 1966084
  1.9 1.2 %copy-start.1 = (bf16[16,40,256]{2,1,0:T(8,128)(2,1)S(1)}, bf16[16,40,256]{2,1,0:T(8,128)(2,1)}, u32[]{:S(2)}) copy-start(bf16[16,40,256]{2,1,0:T(8,128)(2,1)} %perturb_ref.3) | copy-start | bytes 983044
  3.1 3.5 %copy-start.2 = (f32[16,1024]{1,0:T(8,128)S(1)}, f32[16,1024]{1,0:T(8,128)}, u32[]{:S(2)}) copy-start(f32[16,1024]{1,0:T(8,128)} %refs_5_.1) | copy-start | bytes 196612
  3.1 3.5 %copy-start.3 = (f32[16,1024]{1,0:T(8,128)S(1)}, f32[16,1024]{1,0:T(8,128)}, u32[]{:S(2)}) copy-start(f32[16,1024]{1,0:T(8,128)} %refs_8_.1) | copy-start | bytes 196612
  3.1 3.5 %copy-start.4 = (f32[16,1024]{1,0:T(8,128)S(1)}, f32[16,1024]{1,0:T(8,128)}, u32[]{:S(2)}) copy-start(f32[16,1024]{1,0:T(8,128)} %refs_9_.1) | copy-start | bytes 196612
  3.1 3.5 %copy-start.7 = (s32[1,8,128]{2,1,0:T(8,128)S(1)}, s32[1,8,128]{2,1,0:T(8,128)}, u32[]{:S(2)}) copy-start(s32[1,8,128]{2,1,0:T(8,128)} %src_ref.1) | copy-start | bytes 12292
  3.1 3.5 %copy-start.8 = (f32[1,8,128]{2,1,0:T(8,128)S(1)}, f32[1,8,128]{2,1,0:T(8,128)}, u32[]{:S(2)}) copy-start(f32[1,8,128]{2,1,0:T(8,128)} %weight_ref.1) | copy-start | bytes 12292
  3.1 3.5 %copy-start.9 = (s32[1,8,128]{2,1,0:T(8,128)S(1)}, s32[1,8,128]{2,1,0:T(8,128)}, u32[]{:S(2)}) copy-start(s32[1,8,128]{2,1,0:T(8,128)} %tgt_ref.1) | copy-start | bytes 12292
  3.7 4.8 %collective-permute-start.2 = (f32[16,256]{1,0:T(8,128)S(1)}, f32[16,256]{1,0:T(8,128)S(1)}, u32[]{:S(2)}, u32[]{:S(2)}) collective-permute-start(f32[16,256]{1,0:T(8,128)S(1)} %shard_map.140.refs_0_), channel_id=1, source_target_pairs={{0,16},{16,0},{1,17},{17,1},{2,18},{18,2},{3,19},{19,3},{4,20},{20... | collective-permute-start | bytes 49160 | tf_op jit(solution)/shard_map/ppermute | solution.py:511
  6.6 0.7 %copy-start.6 = (f32[1024]{0:T(1024)S(1)}, f32[1024]{0:T(1024)}, u32[]{:S(2)}) copy-start(f32[1024]{0:T(1024)} %param.17) | copy-start | bytes 12292
  6.6 0.7 %copy-start.5 = (f32[1024]{0:T(1024)S(1)}, f32[1024]{0:T(1024)}, u32[]{:S(2)}) copy-start(f32[1024]{0:T(1024)} %param.16) | copy-start | bytes 12292
  6.6 0.7 %copy-start.10 = (s32[1,8]{1,0:T(1,128)S(1)}, s32[1,8]{1,0:T(1,128)}, u32[]{:S(2)}) copy-start(s32[1,8]{1,0:T(1,128)} %counts_ref.1) | copy-start | bytes 100
  8.5 10.3 %collective-permute-start.3 = (f32[88,128]{1,0:T(8,128)S(1)}, f32[88,128]{1,0:T(8,128)S(1)}, u32[]{:S(2)}, u32[]{:S(2)}) collective-permute-start(f32[88,128]{1,0:T(8,128)S(1)} %get-tuple-element.52), channel_id=1, source_target_pairs={{0,12},{1,13},{2,14},{3,15},{4,8},{5,9},{6,10},{7,11},{8,4},{9,5},... | collective-permute-start | bytes 135176 | tf_op jit(solution)/shard_map/ppermute | solution.py:525
  12.6 7.1 %collective-permute-start.4 = (f32[88,128]{1,0:T(8,128)S(1)}, f32[88,128]{1,0:T(8,128)S(1)}, u32[]{:S(2)}, u32[]{:S(2)}) collective-permute-start(f32[88,128]{1,0:T(8,128)S(1)} %get-tuple-element.53), channel_id=1, source_target_pairs={{0,14},{1,15},{2,12},{3,13},{4,10},{5,11},{6,8},{7,9},{8,6},{9,7},... | collective-permute-start | bytes 135176 | tf_op jit(solution)/shard_map/ppermute | solution.py:525
  13.7 7.6 %collective-permute-start.5 = (f32[88,128]{1,0:T(8,128)S(1)}, f32[88,128]{1,0:T(8,128)S(1)}, u32[]{:S(2)}, u32[]{:S(2)}) collective-permute-start(f32[88,128]{1,0:T(8,128)S(1)} %get-tuple-element.54), channel_id=1, source_target_pairs={{0,10},{1,7},{2,8},{3,5},{4,14},{5,3},{6,12},{7,1},{8,2},{9,15},{1... | collective-permute-start | bytes 135176 | tf_op jit(solution)/shard_map/ppermute | solution.py:525
  14.5 7.7 %collective-permute-start.6 = (f32[88,128]{1,0:T(8,128)S(1)}, f32[88,128]{1,0:T(8,128)S(1)}, u32[]{:S(2)}, u32[]{:S(2)}) collective-permute-start(f32[88,128]{1,0:T(8,128)S(1)} %get-tuple-element.55), channel_id=1, source_target_pairs={{0,8},{1,5},{2,10},{3,7},{4,12},{5,1},{6,14},{7,3},{8,0},{9,13},{1... | collective-permute-start | bytes 135176 | tf_op jit(solution)/shard_map/ppermute | solution.py:525
  16.5 5.8 %collective-permute-start.7 = (f32[88,128]{1,0:T(8,128)S(1)}, f32[88,128]{1,0:T(8,128)S(1)}, u32[]{:S(2)}, u32[]{:S(2)}) collective-permute-start(f32[88,128]{1,0:T(8,128)S(1)} %get-tuple-element.56), channel_id=1, source_target_pairs={{0,6},{1,11},{2,4},{3,9},{4,2},{5,15},{6,0},{7,13},{8,14},{9,3},{1... | collective-permute-start | bytes 135176 | tf_op jit(solution)/shard_map/ppermute | solution.py:525
  18.8 4.0 %collective-permute-start.8 = (f32[88,128]{1,0:T(8,128)S(1)}, f32[88,128]{1,0:T(8,128)S(1)}, u32[]{:S(2)}, u32[]{:S(2)}) collective-permute-start(f32[88,128]{1,0:T(8,128)S(1)} %get-tuple-element.57), channel_id=1, source_target_pairs={{0,4},{1,9},{2,6},{3,11},{4,0},{5,13},{6,2},{7,15},{8,12},{9,1},{1... | collective-permute-start | bytes 135176 | tf_op jit(solution)/shard_map/ppermute | solution.py:525
  19.6 4.2 %collective-permute-start.9 = (f32[88,128]{1,0:T(8,128)S(1)}, f32[88,128]{1,0:T(8,128)S(1)}, u32[]{:S(2)}, u32[]{:S(2)}) collective-permute-start(f32[88,128]{1,0:T(8,128)S(1)} %get-tuple-element.58), channel_id=1, source_target_pairs={{0,2},{1,3},{2,0},{3,1},{4,6},{5,7},{6,4},{7,5},{8,10},{9,11},{10,... | collective-permute-start | bytes 135176 | tf_op jit(solution)/shard_map/ppermute | solution.py:525
  24.7 1.2 %collective-permute-start.10 = (f32[48,128]{1,0:T(8,128)S(1)}, f32[48,128]{1,0:T(8,128)S(1)}, u32[]{:S(2)}, u32[]{:S(2)}) collective-permute-start(f32[48,128]{1,0:T(8,128)S(1)} %get-tuple-element.65.mine_ref), channel_id=1, source_target_pairs={{0,1},{1,0},{2,3},{3,2},{4,5},{5,4},{6,7},{7,6},{8,9},{9,8},{10,11... | collective-permute-start | bytes 73736 | tf_op jit(solution)/shard_map/ppermute | solution.py:572

commit v13 on v12

--- a/solution.py
+++ b/solution.py
@@ -90,29 +90,35 @@
     return lax.fori_loop(0, n, step, init, unroll=n if n <= 8 else 1)
 
 
-def mix_kernel(lev_ref, loc_ref, mix_ref, own_ref, given_ref):
+def mix_kernel(lev_ref, loc_ref, other_ref, sums_ref, ens_ref):
     levels = loc_ref.shape[0]
     start = lev_ref[0] * levels
-    loc = loc_ref[...]
-    mix_ref[0], mix_ref[1] = halves(spread(wide_rows(loc, start, 2 * levels)))
-    own_ref[0], own_ref[1] = halves(spread(wide_rows(loc, start, levels)).T)
-    given_ref[...] = wide_rows(loc, levels - start, levels)
-
-
-def sum_kernel(perturb_ref, control_ref, other_ref, mix_ref, out_ref):
+    locs = loc_ref[...], other_ref[...]
+    sums_ref[...] = jnp.concatenate(
+        [term for both in zip(*(halves(spread(wide_rows(loc, start, 2 * levels))) for loc in locs)) for term in both]
+    )
+    for i, loc in enumerate(locs):
+        ens_ref[2 * i], ens_ref[2 * i + 1] = halves(spread(wide_rows(loc, start, levels)).T)
+
+
+def sum_kernel(perturb_ref, other_perturb_ref, control_ref, other_ref, mix_ref, out_ref):
     levels, members, cols = perturb_ref.shape
-    perturb = perturb_ref[...].astype(F32)
-    total = jnp.zeros((levels, SUB, cols), F32)
+    perturb = jnp.concatenate([perturb_ref[...].astype(F32), other_perturb_ref[...].astype(F32)], axis=0)
+    total = jnp.zeros((2 * levels, SUB, cols), F32)
+    rows = mix_ref.shape[0] // 2
     for m in range(0, members, SUB):
         tile = jnp.concatenate([control_ref[:, m : m + SUB, :], other_ref[:, m : m + SUB, :]], axis=0)
-        mixed = mix((mix_ref[0], mix_ref[1]), tile.reshape(2 * levels * SUB, cols))
-        total = total + perturb[:, m : m + SUB, :] * mixed.reshape(levels, SUB, cols)
-    out_ref[...] = jnp.sum(total, axis=1)
+        high, low = halves(tile.reshape(2 * levels * SUB, cols))
+        both = product(mix_ref[...], high)
+        mixed = both[:rows] + (product(mix_ref[:rows, :], low) + both[rows:])
+        total = total + perturb[:, m : m + SUB, :] * mixed.reshape(2 * levels, SUB, cols)
+    out_ref[: 2 * levels, :] = jnp.sum(total, axis=1)
+    out_ref[2 * levels :, :] = jnp.zeros((SUB, cols), F32)
 
 
 def band_kernel(counts_ref, sum_ref, static_ref, src_ref, weight_ref, out_ref, acc_ref):
-    levels, cols = sum_ref.shape
-    acc_ref[...] = jnp.concatenate(halves(sum_ref[...]), axis=0)
+    levels, cols = static_ref.shape[0], sum_ref.shape[1]
+    acc_ref[...] = jnp.concatenate(halves(sum_ref[:levels, :]), axis=0)
     n = src_ref.shape[1]
     edges = edge_rows(static_ref[...])
 
@@ -168,7 +174,7 @@
     loop(n, give, 0)
 
 
-def adjoint_kernel(band, pos_ref, counts_ref, returned_ref, src_ref, weight_ref, partial_ref, mix_ref, grad_ref, out_ref):
+def adjoint_kernel(band, pos_ref, counts_ref, returned_ref, src_ref, weight_ref, partial_ref, grad_ref, out_ref):
     levels, cols = partial_ref.shape
     n = returned_ref.shape[0]
     me = pos_ref[0]
@@ -177,7 +183,7 @@
         values = returned_ref[d, :levels, :] * factor_of(counts_ref, weight_ref, d)
         return total + select(values, one_hot(src_ref[0, pl.ds(d, 1), :], band), ((1,), (1,)))
 
-    out_ref[...] = band_rows(loop(n, step, jnp.zeros((levels, band), F32)), mix_ref[...])
+    out_ref[...] = stack(loop(n, step, jnp.zeros((levels, band), F32)), out_ref.shape[1])
     before = returned_ref[jnp.maximum(me - 1, 0), levels : levels + 1, :]
     after = returned_ref[jnp.minimum(me + 1, n - 1), levels : levels + 1, :]
     before = jnp.where(me > 0, row_as_column(before, levels, 0), 0.0)
@@ -186,9 +192,8 @@
     grad_ref[...] = partial_ref[...] + (jnp.where(lane == 0, before, 0.0) + jnp.where(lane == cols - 1, after, 0.0))
 
 
-def band_rows(band, weights):
-    width = weights.shape[1]
-    return jnp.concatenate([band[:, at : at + width] for at in range(0, band.shape[1], width)] + [weights], axis=0)
+def stack(values, width):
+    return jnp.concatenate([values[:, at : at + width] for at in range(0, values.shape[1], width)], axis=0)
 
 
 def ens_tiles(perturb_ref, rows_ref, weights, before_ref):
@@ -208,15 +213,13 @@
         out_ref[place] = values
 
 
-def ens_kernel(perturb_ref, theirs_ref, own_ref, *refs):
+def ens_kernel(perturb_ref, theirs_ref, weights_ref, own_ref, *refs):
     count = (len(refs) - 3) // 2
     flats, (out_hbm, *flat_hbms), (out_ref, sems) = refs[:count], refs[count : 2 * count + 1], refs[2 * count + 1 :]
     copies = [pltpu.make_async_copy(a, b, sems.at[i]) for i, (a, b) in enumerate(zip(flats, flat_hbms))]
     for copy in copies:
         copy.start()
-    levels = perturb_ref.shape[0]
-    weights = halves(spread(theirs_ref[theirs_ref.shape[0] - levels :, :]).T)
-    for place, values in ens_tiles(perturb_ref, theirs_ref, weights, own_ref):
+    for place, values in ens_tiles(perturb_ref, theirs_ref, (weights_ref[2], weights_ref[3]), own_ref):
         out_ref[place] = values
         copies.append(pltpu.make_async_copy(out_ref.at[place], out_hbm.at[place], sems.at[len(copies)]))
         copies[-1].start()
@@ -225,12 +228,7 @@
 
 
 def relabel(r, n, lev):
-    high, low = n // 2, n // 4
-    if low == 0:
-        return r
-    both = high | low
-    turned = (r & ~both) | ((r & low) << 1) | ((r & high) >> 1)
-    return r + (turned - r) * lev
+    return r ^ (((r & (n // 2)) >> 1) * lev)
 
 
 class Rows:
@@ -242,13 +240,12 @@
         self.total = at + 2 * n + EXTRA
 
 
-def static_kernel(band, pos_ref, lev_ref, counts_ref, static_ref, diag_ref, off_ref, obs_ref, innov_ref, src_ref, weight_ref, tgt_ref,
-                  *out_refs):
+def static_kernel(n, band, pos_ref, lev_ref, counts_ref, static_ref, diag_ref, off_ref, obs_ref, innov_ref, src_ref,
+                  weight_ref, tgt_ref, *out_refs):
     levels, cols = static_ref.shape
-    n = len(out_refs)
     cap = src_ref.shape[2]
     rows = Rows(levels, n)
-    peers = [pos_ref[0] ^ relabel(r, n, lev_ref[0]) for r in range(n)]
+    peers = [pos_ref[0] ^ r for r in range(n)]
     static, off, obs = static_ref[...], off_ref[...], obs_ref[...]
     lane = lax.broadcasted_iota(jnp.int32, (levels, cols), 1)
     left = jnp.where(lane == 0, 0.0, pltpu.roll(static, 1, 1))
@@ -266,46 +263,57 @@
     src = jnp.concatenate([src_ref[0, pl.ds(peer, 1), :] for peer in peers], axis=0).astype(F32)
     index = jnp.concatenate(tgts, axis=0).astype(F32) * float(band) + src
     factor = jnp.concatenate([factor_of(counts_ref, weight_ref, peer) for peer in peers], axis=0)
-    for r, out_ref in enumerate(out_refs):
-        picked = product(both, one_hot(tgts[r], cols))
-        out_ref[: 2 * levels, :] = picked[: 2 * levels] + picked[2 * levels :]
+    picks = []
+    for tgt in tgts:
+        picked = product(both, one_hot(tgt, cols))
+        picks.append(picked[: 2 * levels] + picked[2 * levels :])
+    *block_refs, give_ref = out_refs
+    low, high = n // 4, n // 2
+    first = lev_ref[0] == 0
+    for i in range(low):
+        here, there = picks[high + i], picks[high + low + i]
+        picks[high + i] = jnp.where(first, here, there)
+        give_ref[2 * levels * i : 2 * levels * (i + 1), :] = jnp.where(first, there, here)
+    give_ref[2 * levels * low :, :] = edge
+    for picked, out_ref in zip(picks, block_refs):
+        out_ref[: 2 * levels, :] = picked
         out_ref[rows.factor : rows.factor + n, :] = factor
         out_ref[rows.index : rows.index + n, :] = index
         out_ref[rows.edge :, :] = edge
 
 
-def blocks_kernel(groups, *refs):
-    sums = refs[:groups]
-    count = (len(refs) - groups - 1) // 2
-    rests = refs[groups : groups + count]
-    total_ref = refs[groups + count]
-    out_refs = refs[groups + count + 1 :]
+def blocks_kernel(groups, near, levels, lev_ref, *refs):
+    sums, refs = refs[:groups], refs[groups:]
+    count = (len(refs) - 2) // 2
+    rests, given_ref, total_ref, out_refs = refs[:count], refs[count], refs[count + 1], refs[count + 2 :]
     total = sum(ref[...] for ref in sums)
     cap = total_ref.shape[1]
-    total = jnp.concatenate([total[:, at : at + cap] for at in range(0, total.shape[1], cap)], axis=0)
-    total_ref[...] = total
-    for rest_ref, out_ref in zip(rests, out_refs):
-        out_ref[: total.shape[0], :] = total
-        out_ref[total.shape[0] :, :] = rest_ref[...]
+    own, other = (stack(part, cap) for part in (total[:levels], total[levels : 2 * levels]))
+    total_ref[...] = own
+    for rest_ref, out_ref in zip(rests[:near], out_refs[:near]):
+        out_ref[...] = jnp.concatenate([own, rest_ref[...]], axis=0)
+    first = lev_ref[0] == 0
+    for i, (rest_ref, out_ref) in enumerate(zip(rests[near:], out_refs[near:])):
+        mine = jnp.concatenate([own, rest_ref[: 2 * levels, :], rest_ref[-EXTRA:, :]], axis=0)
+        part = given_ref[2 * levels * i : 2 * levels * (i + 1), :]
+        theirs = jnp.concatenate([other, part, given_ref[-EXTRA:, :]], axis=0)
+        tables = rest_ref[2 * levels : -EXTRA, :]
+        out_ref[...] = jnp.concatenate([jnp.where(first, mine, theirs), tables, jnp.where(first, theirs, mine)], axis=0)
 
 
 class Block:
-    def __init__(self, refs, n, levels, band):
-        cap = refs[0].shape[1]
-        self.levels, self.parts, self.cap = levels, band // cap, cap
-        self.sums_ref, self.rest_ref = refs[0], refs[-1]
-        self.head = 0 if len(refs) == 2 else self.parts * levels
-        self.rows = Rows(levels, n)
-        words = self.rest(self.rows.index, n)
+    def __init__(self, sums, weight, base, tables, edge, lev, n, band):
+        self.levels, self.cap = weight.shape
+        self.stacked, self.weight, self.base, self.edge = sums, weight, base, edge
+        low, high = n // 4, n // 2
+        turned = [tables[at : at + size] for k in (0, n) for at, size in ((k, high), (k + high + low, low), (k + high, low))]
+        tables = jnp.where(lev == 1, jnp.concatenate(turned, axis=0), tables)
+        self.factor, words = tables[:n], tables[n:]
         self.tgt = jnp.floor((words + 0.5) * (1.0 / band))
         self.src = words - self.tgt * float(band)
-        self.factor = self.rest(self.rows.factor, n)
-
-    def rest(self, at, size):
-        return self.rest_ref[self.head + at : self.head + at + size, :]
 
     def sums(self):
-        parts = [self.sums_ref[i * self.levels : (i + 1) * self.levels, :] for i in range(self.parts)]
+        parts = [self.stacked[at : at + self.levels] for at in range(0, self.stacked.shape[0], self.levels)]
         return jnp.concatenate(halves(jnp.concatenate(parts, axis=1)), axis=0)
 
 
@@ -314,7 +322,7 @@
 
 
 def pick_source(block, r):
-    band = block.parts * block.cap
+    band = block.stacked.shape[0] // block.levels * block.cap
     column = lax.broadcasted_iota(jnp.int32, (band, block.cap), 0).astype(F32)
     return jnp.where(column == line(block.src, r), 1.0, 0.0).astype(BF16)
 
@@ -347,17 +355,28 @@
     return total[:levels] + total[levels:]
 
 
-def open_blocks(labels, refs, n, levels, band):
-    blocks = {0: Block(refs[:2], n, levels, band)}
-    refs = refs[2:]
-    for i, r in enumerate(labels[1:]):
-        blocks[r] = Block(refs[i : i + 1], n, levels, band)
-    return blocks, refs[len(labels) - 1 :]
-
-
-def stage_kernel(n, levels, band, cols, stages, *refs):
+def open_blocks(labels, refs, lev, n, levels, band):
+    blocks = {}
+    for r in labels:
+        head = band // refs[0].shape[1] * levels
+        if r == 0:
+            whole = jnp.concatenate([refs[0][...], refs[1][...]], axis=0)
+        else:
+            whole = refs[0][...]
+        refs = refs[1 + (r == 0) :]
+        if r >= n // 2:
+            size = (whole.shape[0] - 2 * n) // 2
+            part = jnp.where(lev == 0, whole[:size], whole[size + 2 * n :])
+            whole = jnp.concatenate([part[:-EXTRA], whole[size : size + 2 * n], part[-EXTRA:]], axis=0)
+        at = head + 2 * levels
+        weight, base = whole[head : head + levels], whole[head + levels : at]
+        blocks[r] = Block(whole[:head], weight, base, whole[at : at + 2 * n], whole[at + 2 * n :], lev, n, band)
+    return blocks, refs
+
+
+def stage_kernel(n, levels, band, cols, stages, lev_ref, *refs):
     known = sum(stages[:-1], [])
-    blocks, refs = open_blocks(known + stages[-1], refs, n, levels, band)
+    blocks, refs = open_blocks(known + stages[-1], refs, lev_ref[0], n, levels, band)
     old, refs = refs[: len(stages) - 1], refs[len(stages) - 1 :]
     if known:
         met_old, remap_old, slots_ref, met_ref, remap_ref = refs
@@ -378,27 +397,27 @@
     remap_ref[...] = landed + remap_old[...] if known else landed
 
 
-def shared_kernel(n, levels, band, cols, stages, pos_ref, lev_ref, mix_ref, *refs):
+def shared_kernel(n, levels, band, cols, stages, pos_ref, lev_ref, *refs):
     known = sum(stages[:-1], [])
-    blocks, refs = open_blocks(known + stages[-1], refs, n, levels, band)
+    blocks, refs = open_blocks(known + stages[-1], refs, lev_ref[0], n, levels, band)
     old, refs = refs[: len(stages) - 1], refs[len(stages) - 1 :]
     met_old, pick_ref, out_ref, slots_ref, tables_ref = refs
     me = pos_ref[0]
     for r, block in blocks.items():
         there = me ^ relabel(r, n, lev_ref[0])
         tables_ref[there, :n, :] = block.tgt
-        tables_ref[there, n:, :] = block.rest(block.rows.edge, EXTRA)
+        tables_ref[there, n:, :] = block.edge
     fill_slots(stages[-1], blocks, n, slots_ref)
     last = cols - 1.0
     total = jnp.zeros((levels, band), F32)
     for i, (d, block) in enumerate(blocks.items()):
-        value = met_at(d, block, stages[-1], slots_ref) + block.rest(levels, levels)
+        value = met_at(d, block, stages[-1], slots_ref) + block.base
         if d in known:
             value = value + met_old[i]
         else:
             for bands, ref in zip(stages, old):
                 value = value + met_at(d, block, bands, ref)
-        edge = block.rest(block.rows.edge, 1)
+        edge = line(block.edge, 0)
         own = line(block.tgt, d)
         there = me ^ relabel(d, n, lev_ref[0])
         before = tables_ref[jnp.maximum(there - 1, 0), n : n + 1, :]
@@ -407,9 +426,9 @@
         after = tables_ref[jnp.minimum(there + 1, n - 1), n : n + 1, :]
         near = jnp.where((own == last) & (there < n - 1), edge[:, 6 * levels : 6 * levels + 1], 0.0)
         value = value + row_as_column(after, levels, levels) * near
-        given = block.rest(0, levels) * value * line(blocks[0].factor, d)
+        given = block.weight * value * line(blocks[0].factor, d)
         total = total + select(given, pick_ref[d], ((1,), (1,)))
-    out_ref[...] = band_rows(total, mix_ref[...])
+    out_ref[...] = stack(total, out_ref.shape[1])
 
 
 def outputs_kernel(stages, pos_ref, lev_ref, *refs):
@@ -488,41 +507,51 @@
     lev = lax.axis_index("lev").astype(jnp.int32).reshape(1)
     pos = lax.axis_index("tile").astype(jnp.int32).reshape(1)
     other_control = lax.ppermute(control, "lev", swap)
+    other_perturb = lax.ppermute(perturb, "lev", swap)
     width = levels * SUB
-    level_mix, own_mix, given_mix = call(
+    sum_mix, ens_mix = call(
         mix_kernel,
-        (shape((2, width, 2 * width), BF16), shape((2, width, width), BF16), shape((levels, width), F32)),
-        [SMEM, VMEM],
+        (shape((4 * width, 2 * width), BF16), shape((4, width, width), BF16)),
+        [SMEM] + [VMEM] * 2,
         cost=pl.CostEstimate(flops=10**9, bytes_accessed=0, transcendentals=0),
-    )(lev, level_loc)
-    own_sum = call(sum_kernel, shape((levels, band_cols), F32), [VMEM] * 4)(perturb, control, other_control, level_mix)
+    )(lev, level_loc, lax.ppermute(level_loc, "lev", swap))
+    sums = call(sum_kernel, shape((2 * levels + SUB, band_cols), F32), [VMEM] * 5)(
+        perturb, other_perturb, control, other_control, sum_mix
+    )
     flat = shape((levels, tile_cols), F32)
-    mine_shape = shape((band_cols // width * levels + levels, width), F32)
+    mine_shape = shape((band_cols // cap * levels, cap), F32)
     diag, off = filter_diag.reshape(1, -1), filter_off.reshape(1, -1)
     if n * cap <= tile_cols and n >= 8 and lax.axis_size("lev") == 2 and n & (n - 1) == 0 and band_cols * tile_cols <= 2**20:
         rows = Rows(levels, n)
         stacked = band_cols // cap * levels
-        rests = call(functools.partial(static_kernel, band_cols), [shape((rows.total, cap), F32)] * n, [SMEM] * 3 + [VMEM] * 8)(
-            pos, lev, counts, static_control, diag, off, obs_weight, innovation, send_src, send_wt, recv_tgt
-        )
-        sums = [own_sum]
-        sums[0], other_perturb = lax.optimization_barrier((sums[0], lax.ppermute(perturb, "lev", swap)))
+        low, high = n // 4, n // 2
+        part = shape((rows.total, cap), F32)
+        sums, counts = lax.optimization_barrier((sums, counts))
+        *rests, give = call(
+            functools.partial(static_kernel, n, band_cols),
+            [part] * (high + low) + [shape((2 * levels * low + EXTRA, cap), F32)],
+            [SMEM] * 3 + [VMEM] * 8,
+        )(pos, lev, counts, static_control, diag, off, obs_weight, innovation, send_src, send_wt, recv_tgt)
+        given = lax.ppermute(give, "lev", swap)
+        sums = [sums]
         for k in range(1, groups):
             sums.append(lax.ppermute(sums[0], "grp", [(g, (g + k) % groups) for g in range(groups)]))
         total, *blocks = call(
-            functools.partial(blocks_kernel, groups),
-            [shape((stacked, cap), F32)] + [shape((stacked + rows.total, cap), F32)] * (n - 1),
-            [VMEM] * (groups + n - 1),
-        )(*sums, *rests[1:])
-        low, high = n // 4, n // 2
-        both_far = [high + low + i for i in range(low)]
-        mixed = [high + i for i in reversed(range(low))] + [low + i for i in reversed(range(low))]
-        stages = [[0] + both_far + mixed[: low // 2], mixed[low // 2 :], list(range(1, low))]
-        levs = lax.axis_size("lev")
+            functools.partial(blocks_kernel, groups, high - 1, levels),
+            [shape((stacked, cap), F32)]
+            + [shape((stacked + rows.total, cap), F32)] * (high - 1)
+            + [shape((2 * stacked + 4 * levels + 2 * n + 2 * EXTRA, cap), F32)] * low,
+            [SMEM] + [VMEM] * (groups + high + low),
+        )(lev, *sums, *rests[1:], given)
         arrived = {0: [total, rests[0]]}
-        for r in sum(stages, [])[1:]:
-            pairs = [(i * levs + v, (i ^ relabel(r, n, v)) * levs + v) for i in range(n) for v in range(levs)]
+        for r in range(high, high + low):
+            pairs = [(i * 2 + v, (i ^ relabel(r, n, v)) * 2 + v) for i in range(n) for v in range(2)]
             arrived[r] = [lax.ppermute(blocks[r - 1], ("tile", "lev"), pairs)]
+        for r in reversed(range(1, high)):
+            arrived[r] = [lax.ppermute(blocks[r - 1], "tile", [(i, i ^ r) for i in range(n)])]
+        for r in range(high, high + low):
+            arrived[r + low] = [lax.ppermute(arrived[r][0], "lev", swap)]
+        stages = [[0, high, high - 1], [*range(high + 1, n - 1), *range(2, high - 1)], [1, n - 1]]
         slots, carried, picks = [], [], []
         for count in range(1, len(stages)):
             labels = sum(stages[:count], [])
@@ -535,8 +564,9 @@
             new, *carried = call(
                 functools.partial(stage_kernel, n, levels, band_cols, tile_cols, stages[:count]),
                 outs,
-                [VMEM] * (len(refs) + len(slots) + len(carried)),
-            )(*refs, *slots, *carried)
+                [SMEM] + [VMEM] * (len(refs) + len(slots) + len(carried)),
+                cost=pl.CostEstimate(flops=10**9, bytes_accessed=0, transcendentals=0),
+            )(lev, *refs, *slots, *carried)
             slots.append(new)
             picks += carried[2:]
             carried = carried[:2]
@@ -545,20 +575,20 @@
         mine, new, tables = call(
             functools.partial(shared_kernel, n, levels, band_cols, tile_cols, stages),
             (mine_shape, shape((n, 2 * levels, len(stages[-1]) * cap), BF16), shape((n, n + EXTRA, cap), F32)),
-            [SMEM] * 2 + [VMEM] * (1 + len(refs)),
-        )(pos, lev, given_mix, *refs)
+            [SMEM] * 2 + [VMEM] * len(refs),
+            cost=pl.CostEstimate(flops=10**9, bytes_accessed=0, transcendentals=0),
+        )(pos, lev, *refs)
         slots.append(new)
         increment, grad_static = call(
             functools.partial(outputs_kernel, stages), (flat, flat), [SMEM] * 2 + [VMEM] * (len(slots) + 7)
         )(pos, lev, *slots, remap, tables, static_control, diag, off, obs_weight, innovation)
     else:
-        other_perturb = lax.ppermute(perturb, "lev", swap)
         payload = call(
             band_kernel,
             shape((groups, n, levels + EXTRA, cap), F32),
             [SMEM] + [VMEM] * 4,
             [pltpu.VMEM((2 * levels, band_cols), BF16)],
-        )(counts, own_sum, static_control, send_src, send_wt)
+        )(counts, sums, static_control, send_src, send_wt)
         arrived = lax.all_to_all(
             payload.reshape(groups * n, levels + EXTRA, cap), ("grp", "tile"), split_axis=0, concat_axis=0, tiled=True
         ).reshape(groups, n, levels + EXTRA, cap)
@@ -567,17 +597,17 @@
         )(pos, arrived, recv_tgt, static_control, diag, off, obs_weight, innovation)
         returned = lax.all_to_all(giving, "tile", split_axis=0, concat_axis=0, tiled=True)
         grad_static, mine = call(
-            functools.partial(adjoint_kernel, band_cols), (flat, mine_shape), [SMEM, SMEM] + [VMEM] * 5
-        )(pos, counts, returned, send_src, send_wt, partial, given_mix)
+            functools.partial(adjoint_kernel, band_cols), (flat, mine_shape), [SMEM, SMEM] + [VMEM] * 4
+        )(pos, counts, returned, send_src, send_wt, partial)
     theirs = lax.ppermute(mine, "lev", swap)
-    own = call(ens_own_kernel, shape(control.shape, F32), [VMEM] * 4)(perturb, mine, own_mix, control)
+    own = call(ens_own_kernel, shape(control.shape, F32), [VMEM] * 4)(perturb, mine, ens_mix, control)
     grad_ens, increment, grad_static = call(
         ens_kernel,
         (shape(control.shape, F32), flat, flat),
-        [VMEM] * 5,
+        [VMEM] * 6,
         [pltpu.VMEM(control.shape, F32), pltpu.SemaphoreType.DMA((2 + members // SUB,))],
         out=HBM,
-    )(other_perturb, theirs, own, increment, grad_static)
+    )(other_perturb, theirs, ens_mix, own, increment, grad_static)
     return (increment, grad_static, grad_ens)
 
 

time: 27.4 us -> 29.8 us (1.088)
  waiting for transfers between devices: 2 us -> 7.59 us
  starting transfers between devices: 16.4 us -> 12 us
  local copies, waits for them, and re-layouts: 1.39 us -> 2.23 us
    ppermute x7 -> x2, starting transfers between devices: 12.8 us -> 3.95 us  [body(): arrived[r] = [lax.ppermute(blocks[r - 1], ('tile', 'lev'), pairs)]]
    ppermute x1 -> x8, starting transfers between devices: 0.08 us -> 4.07 us  [the longest x3 3.49 us: body(): lax.ppermute(blocks[r - 1], 'tile', [(i, i ^ r) for i in range(n)])]
    ppermute x7 -> x2, waiting for transfers between devices: 0.66 us -> 4.44 us  [body(): arrived[r] = [lax.ppermute(blocks[r - 1], ('tile', 'lev'), pairs)]]
    ppermute x1 -> x8, waiting for transfers between devices: 0.01 us -> 3.14 us  [the longest x1 1.9 us: body(): lax.ppermute(level_loc, 'lev', swap)]
    ppermute x1, waiting for transfers between devices: 0.9 us -> 0.01 us  [body(): other_control = lax.ppermute(control, 'lev', swap)]
    unnamed x24, local copies, waits for them, and re-layouts: 1.39 us -> 2.23 us
    ppermute x1, starting transfers between devices: 0.01 us -> 0.52 us  [body(): theirs = lax.ppermute(mine, 'lev', swap)]
    ppermute x1, waiting for transfers between devices: 0.43 us -> 0.01 us  [body(): theirs = lax.ppermute(mine, 'lev', swap)]
  transfers between devices with their start and end apart: 11 -> 13, of which waited for: 4 -> 4; matrix products, arithmetic and copies ran while one was open for 0% -> 0% of each run, Pallas kernels for 17% -> 13%
where the time goes in v13:
time: 29.8 us; the launch traced here: 29.5 us
  starting transfers between devices  12 us (40%)
  waiting for transfers between devices  7.59 us (25%)
  Pallas kernels  6.95 us (23%)
  local copies, waits for them, and re-layouts  2.23 us (7%)
  between operations  0.8 us (3%)
    ppermute x2, waiting for transfers between devices, body(): arrived[r] = [lax.ppermute(blocks[r - 1], ('tile', 'lev'), pairs)]  4.44 us
    ppermute x2, starting transfers between devices, body(): arrived[r] = [lax.ppermute(blocks[r - 1], ('tile', 'lev'), pairs)]  3.95 us
    ppermute x3, starting transfers between devices, body(): lax.ppermute(blocks[r - 1], 'tile', [(i, i ^ r) for i in range(n)])  3.49 us
    ppermute x1, starting transfers between devices, body(): lax.ppermute(sums[0], 'grp', [(g, (g + k) % groups) for g in range(groups)])  2.92 us
    unnamed x24, local copies, waits for them, and re-layouts  2.23 us
    ppermute x1, waiting for transfers between devices, body(): lax.ppermute(level_loc, 'lev', swap)  1.9 us
    pallas_call x2, Pallas kernels, body(): call(functools.partial(stage_kernel, n, levels, band_cols, tile_cols, sta...  1.67 us
    ppermute x1, waiting for transfers between devices, body(): given = lax.ppermute(give, 'lev', swap)  1.2 us
  transfers between devices with their start and end apart: 13, of which 4 were waited for; matrix products, arithmetic and copies ran while one was open for 0% of the time, Pallas kernels for 13%

profile of v13, /device:TPU:0, one launch (start us, length us, event | category | flops | bytes accessed | tf_op | source)
XLA Modules:
  0.0 29.5 jit_solution(8137995965766875753)
XLA Ops:
  0.6 0.5 %collective-permute-start.1 = (f32[16,40,256]{2,1,0:T(8,128)}, f32[16,40,256]{2,1,0:T(8,128)S(1)}, u32[]{:S(2)}, u32[]{:S(2)}) collective-permute-start(f32[16,40,256]{2,1,0:T(8,128)} %control_ref.3), channel_id=1, source_target_pairs={{0,1},{1,0},{2,3},{3,2},{4,5},{5,4},{6,7},{7,6},{8,9},{9,8},{10,11... | collective-permute-start | bytes 1966088 | tf_op jit(solution)/shard_map/ppermute | solution.py:509
  1.1 0.1 collective-permute-start
  1.2 0.4 %collective-permute-start.2 = (f32[16,32]{1,0:T(8,128)}, f32[16,32]{1,0:T(8,128)S(1)}, u32[]{:S(2)}, u32[]{:S(2)}) collective-permute-start(f32[16,32]{1,0:T(8,128)} %loc_ref.1), channel_id=1, source_target_pairs={{0,1},{1,0},{2,3},{3,2},{4,5},{5,4},{6,7},{7,6},{8,9},{9,8},{10,11... | collective-permute-start | bytes 6152 | tf_op jit(solution)/shard_map/ppermute | solution.py:517
  1.7 1.9 %collective-permute-done.2.other_ref = f32[16,32]{1,0:T(8,128)S(1)} collective-permute-done((f32[16,32]{1,0:T(8,128)}, f32[16,32]{1,0:T(8,128)S(1)}, u32[]{:S(2)}, u32[]{:S(2)}) %collective-permute-start.2) | collective-permute-done | bytes 2080 | tf_op jit(solution)/shard_map/ppermute | solution.py:517
  3.6 0.7 %copy-done.11 = f32[16,32]{1,0:T(8,128)S(1)} copy-done((f32[16,32]{1,0:T(8,128)S(1)}, f32[16,32]{1,0:T(8,128)}, u32[]{:S(2)}) %copy-start.11) | copy-done | bytes 2072
  4.3 0.3 shard_map.139
  4.6 0.0 collective-permute-done.other_perturb_ref.perturb_ref
  4.6 0.0 collective-permute-done.1.other_ref
  4.6 0.8 %copy-done = f32[16,40,256]{2,1,0:T(8,128)S(1)} copy-done((f32[16,40,256]{2,1,0:T(8,128)S(1)}, f32[16,40,256]{2,1,0:T(8,128)}, u32[]{:S(2)}) %copy-start) | copy-done | bytes 655384
  5.3 0.1 copy-done.1
  5.4 0.0 copy-start.8
  5.5 0.0 copy-start.9
  5.5 0.8 %shard_map.140.refs_0_ = f32[40,256]{1,0:T(8,128)S(1)} custom-call(bf16[16,40,256]{2,1,0:T(8,128)(2,1)S(1)} %copy-done.1, bf16[16,40,256]{2,1,0:T(8,128)(2,1)S(1)} %collective-permute-done.other_perturb_ref.perturb_ref, f32[16,40,256]{2,1,0:T(8,128)S(1)} %copy-done, f32[16,40,256]{2,1,0:T(8,128)S(1)} %collective-permute-done.1.other_ref, ...), custom_call_target="tpu_custom_call" | custom-call | tf_op jit(solution)/shard_map/pallas_call | solution.py:518
  6.2 2.9 %collective-permute-start.3 = (f32[40,256]{1,0:T(8,128)S(1)}, f32[40,256]{1,0:T(8,128)S(1)}, u32[]{:S(2)}, u32[]{:S(2)}) collective-permute-start(f32[40,256]{1,0:T(8,128)S(1)} %shard_map.140.refs_0_), channel_id=1, source_target_pairs={{0,16},{16,0},{1,17},{17,1},{2,18},{18,2},{3,19},{19,3},{4,20},{20... | collective-permute-start | bytes 122888 | tf_op jit(solution)/shard_map/ppermute | solution.py:538
  9.2 0.0 copy-done.2
  9.2 0.0 copy-done.3
  9.2 0.0 copy-done.4
  9.2 0.0 copy-done.7
  9.2 0.0 copy-done.8
  9.2 0.0 copy-done.9
  9.2 0.6 %copy-done.6 = f32[1024]{0:T(1024)S(1)} copy-done((f32[1024]{0:T(1024)S(1)}, f32[1024]{0:T(1024)}, u32[]{:S(2)}) %copy-start.6) | copy-done | bytes 4120
  9.8 0.0 copy-done.5
  9.9 1.1 %shard_map.141 = (f32[56,128]{1,0:T(8,128)S(1)}, f32[56,128]{1,0:T(8,128)S(1)}, f32[56,128]{1,0:T(8,128)S(1)}, f32[56,128]{1,0:T(8,128)S(1)}, f32[56,128]{1,0:T(...) custom-call(s32[1]{0:T(128)} %bitcast.pos_ref, s32[1]{0:T(128)} %bitcast.1.lev_ref, s32[1,8]{1,0:T(1,128)S(1)} %copy-done.10, ...), custom_call_target="tpu_custom_call" | custom-call | tf_op jit(solution)/shard_map/pallas_call | solution.py:530
  11.0 0.1 collective-permute-start.4
  11.0 1.2 %collective-permute-done.4.refs_7_ = f32[72,128]{1,0:T(8,128)S(1)} collective-permute-done((f32[72,128]{1,0:T(8,128)S(1)}, f32[72,128]{1,0:T(8,128)S(1)}, u32[]{:S(2)}, u32[]{:S(2)}) %collective-permute-start.4) | collective-permute-done | bytes 36896 | tf_op jit(solution)/shard_map/ppermute | solution.py:535
  12.2 0.0 collective-permute-done.3.refs_1_
  12.3 2.7 %collective-permute-start.5 = (f32[160,128]{1,0:T(8,128)S(1)}, f32[160,128]{1,0:T(8,128)S(1)}, u32[]{:S(2)}, u32[]{:S(2)}) collective-permute-start(f32[160,128]{1,0:T(8,128)S(1)} %get-tuple-element.46), channel_id=1, source_target_pairs={{0,8},{1,13},{2,10},{3,15},{4,12},{5,9},{6,14},{7,11},{8,0},{9,5},... | collective-permute-start | bytes 245768 | tf_op jit(solution)/shard_map/ppermute | solution.py:549
  14.9 1.3 %collective-permute-start.7 = (f32[160,128]{1,0:T(8,128)S(1)}, f32[160,128]{1,0:T(8,128)S(1)}, u32[]{:S(2)}, u32[]{:S(2)}) collective-permute-start(f32[160,128]{1,0:T(8,128)S(1)} %get-tuple-element.48), channel_id=1, source_target_pairs={{0,10},{1,15},{2,8},{3,13},{4,14},{5,11},{6,12},{7,9},{8,2},{9,7},... | collective-permute-start | bytes 245768 | tf_op jit(solution)/shard_map/ppermute | solution.py:549
  16.2 1.5 %collective-permute-start.6 = (f32[88,128]{1,0:T(8,128)S(1)}, f32[88,128]{1,0:T(8,128)S(1)}, u32[]{:S(2)}, u32[]{:S(2)}) collective-permute-start(f32[88,128]{1,0:T(8,128)S(1)} %get-tuple-element.47), channel_id=1, source_target_pairs={{0,6},{2,4},{4,2},{6,0},{8,14},{10,12},{12,10},{14,8},{1,7},{3,5},... | collective-permute-start | bytes 135176 | tf_op jit(solution)/shard_map/ppermute | solution.py:551
  17.7 0.5 %collective-permute-start.9 = (f32[88,128]{1,0:T(8,128)S(1)}, f32[88,128]{1,0:T(8,128)S(1)}, u32[]{:S(2)}, u32[]{:S(2)}) collective-permute-start(f32[88,128]{1,0:T(8,128)S(1)} %get-tuple-element.49), channel_id=1, source_target_pairs={{0,4},{2,6},{4,0},{6,2},{8,12},{10,14},{12,8},{14,10},{1,5},{3,7},... | collective-permute-start | bytes 135176 | tf_op jit(solution)/shard_map/ppermute | solution.py:551
  18.2 1.5 %collective-permute-start.10 = (f32[88,128]{1,0:T(8,128)S(1)}, f32[88,128]{1,0:T(8,128)S(1)}, u32[]{:S(2)}, u32[]{:S(2)}) collective-permute-start(f32[88,128]{1,0:T(8,128)S(1)} %get-tuple-element.50), channel_id=1, source_target_pairs={{0,2},{2,0},{4,6},{6,4},{8,10},{10,8},{12,14},{14,12},{1,3},{3,1},... | collective-permute-start | bytes 135176 | tf_op jit(solution)/shard_map/ppermute | solution.py:551
  19.7 0.5 %collective-permute-done.5.refs_2_ = f32[160,128]{1,0:T(8,128)S(1)} collective-permute-done((f32[160,128]{1,0:T(8,128)S(1)}, f32[160,128]{1,0:T(8,128)S(1)}, u32[]{:S(2)}, u32[]{:S(2)}) %collective-permute-start.5) | collective-permute-done | bytes 81952 | tf_op jit(solution)/shard_map/ppermute | solution.py:549
  20.3 0.0 collective-permute-start.8
  20.3 3.9 %collective-permute-done.7.refs_4_ = f32[160,128]{1,0:T(8,128)S(1)} collective-permute-done((f32[160,128]{1,0:T(8,128)S(1)}, f32[160,128]{1,0:T(8,128)S(1)}, u32[]{:S(2)}, u32[]{:S(2)}) %collective-permute-start.7) | collective-permute-done | bytes 81952 | tf_op jit(solution)/shard_map/ppermute | solution.py:549
  24.2 0.0 collective-permute-start.11
  24.2 0.0 collective-permute-done.6.refs_3_
  24.2 0.7 %shard_map.143 = (bf16[8,32,384]{2,1,0:T(8,128)(2,1)S(1)}, f32[3,16,128]{2,1,0:T(8,128)S(1)}, f32[16,1024]{1,0:T(8,128)S(1)}, bf16[8,256,128]{2,1,0:T(8,128)(2,1)S(1)}) custom-call(s32[1]{0:T(128)} %bitcast.1.lev_ref, f32[32,128]{1,0:T(8,128)S(1)} %get-tuple-element.44.refs_0_, f32[56,128]{1,0:T(8,128)S(1)} %get-tuple-element.45.refs_1_, ...), custom_call_target="tpu_custom_call" | custom-call | flops 1000000000 | tf_op jit(solution)/shard_map/pallas_call | solution.py:564
  24.9 0.0 collective-permute-done.9.refs_6_
  24.9 0.0 collective-permute-done.8.refs_5_
  24.9 0.9 %shard_map.144 = (bf16[8,32,384]{2,1,0:T(8,128)(2,1)S(1)}, f32[6,16,128]{2,1,0:T(8,128)S(1)}, f32[16,1024]{1,0:T(8,128)S(1)}) custom-call(s32[1]{0:T(128)} %bitcast.1.lev_ref, f32[32,128]{1,0:T(8,128)S(1)} %get-tuple-element.44.refs_0_, f32[56,128]{1,0:T(8,128)S(1)} %get-tuple-element.45.refs_1_, f32[160,128]{1,0:T(8,128)S(1)} %collective-permute-done.5.refs_2_, ...), custom_call_target="tpu_custom_call" | custom-call | flops 1000000000 | tf_op jit(solution)/shard_map/pallas_call | solution.py:564
  25.9 0.0 collective-permute-done.10.refs_7_
  25.9 0.0 collective-permute-done.11.refs_8_
  25.9 1.1 %shard_map.145 = (f32[32,128]{1,0:T(8,128)S(1)}, bf16[8,32,256]{2,1,0:T(8,128)(2,1)S(1)}, f32[8,16,128]{2,1,0:T(8,128)S(1)}) custom-call(s32[1]{0:T(128)} %bitcast.pos_ref, s32[1]{0:T(128)} %bitcast.1.lev_ref, f32[32,128]{1,0:T(8,128)S(1)} %get-tuple-element.44.refs_0_, f32[56,128]{1,0:T(8,128)S(1)} %get-tuple-element.45.refs_1_, ...), custom_call_target="tpu_custom_call" | custom-call | flops 1000000000 | tf_op jit(solution)/shard_map/pallas_call | solution.py:575
  27.0 0.5 %collective-permute-start.12 = (f32[32,128]{1,0:T(8,128)S(1)}, f32[32,128]{1,0:T(8,128)S(1)}, u32[]{:S(2)}, u32[]{:S(2)}) collective-permute-start(f32[32,128]{1,0:T(8,128)S(1)} %get-tuple-element.57.mine_ref), channel_id=1, source_target_pairs={{0,1},{1,0},{2,3},{3,2},{4,5},{5,4},{6,7},{7,6},{8,9},{9,8},{10,11... | collective-permute-start | bytes 49160 | tf_op jit(solution)/shard_map/ppermute | solution.py:602
  27.5 0.4 %shard_map.146.own_ref = f32[16,40,256]{2,1,0:T(8,128)S(1)} custom-call(bf16[16,40,256]{2,1,0:T(8,128)(2,1)S(1)} %copy-done.1, f32[32,128]{1,0:T(8,128)S(1)} %get-tuple-element.57.mine_ref, bf16[4,128,128]{2,1,0:T(8,128)(2,1)S(1)} %get-tuple-element.58.weights_ref, f32[16,40,256]{2,1,0:T(8,128)S(1)} %copy-done), custom_call_target="tpu_custom_call" | custom-call | tf_op jit(solution)/shard_map/pallas_call | solution.py:603
  27.9 0.4 %shard_map.147 = (f32[16,1024]{1,0:T(8,128)S(1)}, f32[16,1024]{1,0:T(8,128)S(1)}) custom-call(s32[1]{0:T(128)} %bitcast.pos_ref, s32[1]{0:T(128)} %bitcast.1.lev_ref, bf16[8,32,384]{2,1,0:T(8,128)(2,1)S(1)} %get-tuple-element.51.refs_7_.refs_9_.refs_0_, bf16[8,32,384]{2,1,0:T(8,128)(2,1)S(1)} %get-tuple-element.54.refs_10_.refs_1_, ...), custom_call_target="tpu_custom_call" | custom-call | tf_op jit(solution)/shard_map/pallas_call | solution.py:582
  28.3 0.0 collective-permute-done.12.theirs_ref
  28.4 1.2 %shard_map.148 = (f32[16,40,256]{2,1,0:T(8,128)}, f32[16,1024]{1,0:T(8,128)}, f32[16,1024]{1,0:T(8,128)}) custom-call(bf16[16,40,256]{2,1,0:T(8,128)(2,1)S(1)} %collective-permute-done.other_perturb_ref.perturb_ref, f32[32,128]{1,0:T(8,128)S(1)} %collective-permute-done.12.theirs_ref, bf16[4,128,128]{2,1,0:T(8,128)(2,1)S(1)} %get-tuple-element.58.weights_ref, ...), custom_call_target="tpu_custom_call" | custom-call | tf_op jit(solution)/shard_map/pallas_call | solution.py:604
  (12 shorter events, 0.0 us)
Async XLA Ops:
  0.6 3.9 %collective-permute-start.1 = (f32[16,40,256]{2,1,0:T(8,128)}, f32[16,40,256]{2,1,0:T(8,128)S(1)}, u32[]{:S(2)}, u32[]{:S(2)}) collective-permute-start(f32[16,40,256]{2,1,0:T(8,128)} %control_ref.3), channel_id=1, source_target_pairs={{0,1},{1,0},{2,3},{3,2},{4,5},{5,4},{6,7},{7,6},{8,9},{9,8},{10,11... | collective-permute-start | bytes 1966088 | tf_op jit(solution)/shard_map/ppermute | solution.py:509
  1.1 3.4 %collective-permute-start = (bf16[16,40,256]{2,1,0:T(8,128)(2,1)}, bf16[16,40,256]{2,1,0:T(8,128)(2,1)S(1)}, u32[]{:S(2)}, u32[]{:S(2)}) collective-permute-start(bf16[16,40,256]{2,1,0:T(8,128)(2,1)} %perturb_ref.3), channel_id=1, source_target_pairs={{0,1},{1,0},{2,3},{3,2},{4,5},{5,4},{6,7},{7,6},{8,9},{9,8},{10,11... | collective-permute-start | bytes 983048 | tf_op jit(solution)/shard_map/ppermute | solution.py:510
  1.2 2.3 %collective-permute-start.2 = (f32[16,32]{1,0:T(8,128)}, f32[16,32]{1,0:T(8,128)S(1)}, u32[]{:S(2)}, u32[]{:S(2)}) collective-permute-start(f32[16,32]{1,0:T(8,128)} %loc_ref.1), channel_id=1, source_target_pairs={{0,1},{1,0},{2,3},{3,2},{4,5},{5,4},{6,7},{7,6},{8,9},{9,8},{10,11... | collective-permute-start | bytes 6152 | tf_op jit(solution)/shard_map/ppermute | solution.py:517
  3.6 0.7 %copy-start.11 = (f32[16,32]{1,0:T(8,128)S(1)}, f32[16,32]{1,0:T(8,128)}, u32[]{:S(2)}) copy-start(f32[16,32]{1,0:T(8,128)} %loc_ref.1) | copy-start | bytes 6148
  4.3 1.1 %copy-start = (f32[16,40,256]{2,1,0:T(8,128)S(1)}, f32[16,40,256]{2,1,0:T(8,128)}, u32[]{:S(2)}) copy-start(f32[16,40,256]{2,1,0:T(8,128)} %control_ref.3) | copy-start | bytes 1966084
  4.3 1.2 %copy-start.1 = (bf16[16,40,256]{2,1,0:T(8,128)(2,1)S(1)}, bf16[16,40,256]{2,1,0:T(8,128)(2,1)}, u32[]{:S(2)}) copy-start(bf16[16,40,256]{2,1,0:T(8,128)(2,1)} %perturb_ref.3) | copy-start | bytes 983044
  5.4 3.7 %copy-start.2 = (f32[16,1024]{1,0:T(8,128)S(1)}, f32[16,1024]{1,0:T(8,128)}, u32[]{:S(2)}) copy-start(f32[16,1024]{1,0:T(8,128)} %refs_5_.1) | copy-start | bytes 196612
  5.4 3.7 %copy-start.3 = (f32[16,1024]{1,0:T(8,128)S(1)}, f32[16,1024]{1,0:T(8,128)}, u32[]{:S(2)}) copy-start(f32[16,1024]{1,0:T(8,128)} %refs_8_.1) | copy-start | bytes 196612
  5.4 3.7 %copy-start.4 = (f32[16,1024]{1,0:T(8,128)S(1)}, f32[16,1024]{1,0:T(8,128)}, u32[]{:S(2)}) copy-start(f32[16,1024]{1,0:T(8,128)} %refs_9_.1) | copy-start | bytes 196612
  5.4 3.7 %copy-start.7 = (s32[1,8,128]{2,1,0:T(8,128)S(1)}, s32[1,8,128]{2,1,0:T(8,128)}, u32[]{:S(2)}) copy-start(s32[1,8,128]{2,1,0:T(8,128)} %src_ref.1) | copy-start | bytes 12292
  5.4 3.7 %copy-start.8 = (f32[1,8,128]{2,1,0:T(8,128)S(1)}, f32[1,8,128]{2,1,0:T(8,128)}, u32[]{:S(2)}) copy-start(f32[1,8,128]{2,1,0:T(8,128)} %weight_ref.1) | copy-start | bytes 12292
  5.5 3.7 %copy-start.9 = (s32[1,8,128]{2,1,0:T(8,128)S(1)}, s32[1,8,128]{2,1,0:T(8,128)}, u32[]{:S(2)}) copy-start(s32[1,8,128]{2,1,0:T(8,128)} %tgt_ref.1) | copy-start | bytes 12292
  6.2 6.0 %collective-permute-start.3 = (f32[40,256]{1,0:T(8,128)S(1)}, f32[40,256]{1,0:T(8,128)S(1)}, u32[]{:S(2)}, u32[]{:S(2)}) collective-permute-start(f32[40,256]{1,0:T(8,128)S(1)} %shard_map.140.refs_0_), channel_id=1, source_target_pairs={{0,16},{16,0},{1,17},{17,1},{2,18},{18,2},{3,19},{19,3},{4,20},{20... | collective-permute-start | bytes 122888 | tf_op jit(solution)/shard_map/ppermute | solution.py:538
  9.1 0.7 %copy-start.6 = (f32[1024]{0:T(1024)S(1)}, f32[1024]{0:T(1024)}, u32[]{:S(2)}) copy-start(f32[1024]{0:T(1024)} %param.17) | copy-start | bytes 12292
  9.2 0.7 %copy-start.5 = (f32[1024]{0:T(1024)S(1)}, f32[1024]{0:T(1024)}, u32[]{:S(2)}) copy-start(f32[1024]{0:T(1024)} %param.16) | copy-start | bytes 12292
  9.2 0.7 %copy-start.10 = (s32[1,8]{1,0:T(1,128)S(1)}, s32[1,8]{1,0:T(1,128)}, u32[]{:S(2)}) copy-start(s32[1,8]{1,0:T(1,128)} %counts_ref) | copy-start | bytes 100
  11.0 1.3 %collective-permute-start.4 = (f32[72,128]{1,0:T(8,128)S(1)}, f32[72,128]{1,0:T(8,128)S(1)}, u32[]{:S(2)}, u32[]{:S(2)}) collective-permute-start(f32[72,128]{1,0:T(8,128)S(1)} %get-tuple-element.43), channel_id=1, source_target_pairs={{0,1},{1,0},{2,3},{3,2},{4,5},{5,4},{6,7},{7,6},{8,9},{9,8},{10,11... | collective-permute-start | bytes 110600 | tf_op jit(solution)/shard_map/ppermute | solution.py:535
  12.3 8.0 %collective-permute-start.5 = (f32[160,128]{1,0:T(8,128)S(1)}, f32[160,128]{1,0:T(8,128)S(1)}, u32[]{:S(2)}, u32[]{:S(2)}) collective-permute-start(f32[160,128]{1,0:T(8,128)S(1)} %get-tuple-element.46), channel_id=1, source_target_pairs={{0,8},{1,13},{2,10},{3,15},{4,12},{5,9},{6,14},{7,11},{8,0},{9,5},... | collective-permute-start | bytes 245768 | tf_op jit(solution)/shard_map/ppermute | solution.py:549
  14.9 9.2 %collective-permute-start.7 = (f32[160,128]{1,0:T(8,128)S(1)}, f32[160,128]{1,0:T(8,128)S(1)}, u32[]{:S(2)}, u32[]{:S(2)}) collective-permute-start(f32[160,128]{1,0:T(8,128)S(1)} %get-tuple-element.48), channel_id=1, source_target_pairs={{0,10},{1,15},{2,8},{3,13},{4,14},{5,11},{6,12},{7,9},{8,2},{9,7},... | collective-permute-start | bytes 245768 | tf_op jit(solution)/shard_map/ppermute | solution.py:549
  16.2 7.9 %collective-permute-start.6 = (f32[88,128]{1,0:T(8,128)S(1)}, f32[88,128]{1,0:T(8,128)S(1)}, u32[]{:S(2)}, u32[]{:S(2)}) collective-permute-start(f32[88,128]{1,0:T(8,128)S(1)} %get-tuple-element.47), channel_id=1, source_target_pairs={{0,6},{2,4},{4,2},{6,0},{8,14},{10,12},{12,10},{14,8},{1,7},{3,5},... | collective-permute-start | bytes 135176 | tf_op jit(solution)/shard_map/ppermute | solution.py:551
  17.7 7.2 %collective-permute-start.9 = (f32[88,128]{1,0:T(8,128)S(1)}, f32[88,128]{1,0:T(8,128)S(1)}, u32[]{:S(2)}, u32[]{:S(2)}) collective-permute-start(f32[88,128]{1,0:T(8,128)S(1)} %get-tuple-element.49), channel_id=1, source_target_pairs={{0,4},{2,6},{4,0},{6,2},{8,12},{10,14},{12,8},{14,10},{1,5},{3,7},... | collective-permute-start | bytes 135176 | tf_op jit(solution)/shard_map/ppermute | solution.py:551
  18.2 7.6 %collective-permute-start.10 = (f32[88,128]{1,0:T(8,128)S(1)}, f32[88,128]{1,0:T(8,128)S(1)}, u32[]{:S(2)}, u32[]{:S(2)}) collective-permute-start(f32[88,128]{1,0:T(8,128)S(1)} %get-tuple-element.50), channel_id=1, source_target_pairs={{0,2},{2,0},{4,6},{6,4},{8,10},{10,8},{12,14},{14,12},{1,3},{3,1},... | collective-permute-start | bytes 135176 | tf_op jit(solution)/shard_map/ppermute | solution.py:551
  20.3 4.6 %collective-permute-start.8 = (f32[160,128]{1,0:T(8,128)S(1)}, f32[160,128]{1,0:T(8,128)S(1)}, u32[]{:S(2)}, u32[]{:S(2)}) collective-permute-start(f32[160,128]{1,0:T(8,128)S(1)} %collective-permute-done.5.refs_2_), channel_id=1, source_target_pairs={{0,1},{1,0},{2,3},{3,2},{4,5},{5,4},{6,7},{7,6},{8,9},{9,8},{10,11... | collective-permute-start | bytes 245768 | tf_op jit(solution)/shard_map/ppermute | solution.py:553
  24.2 1.7 %collective-permute-start.11 = (f32[160,128]{1,0:T(8,128)S(1)}, f32[160,128]{1,0:T(8,128)S(1)}, u32[]{:S(2)}, u32[]{:S(2)}) collective-permute-start(f32[160,128]{1,0:T(8,128)S(1)} %collective-permute-done.7.refs_4_), channel_id=1, source_target_pairs={{0,1},{1,0},{2,3},{3,2},{4,5},{5,4},{6,7},{7,6},{8,9},{9,8},{10,11... | collective-permute-start | bytes 245768 | tf_op jit(solution)/shard_map/ppermute | solution.py:553
  27.0 1.4 %collective-permute-start.12 = (f32[32,128]{1,0:T(8,128)S(1)}, f32[32,128]{1,0:T(8,128)S(1)}, u32[]{:S(2)}, u32[]{:S(2)}) collective-permute-start(f32[32,128]{1,0:T(8,128)S(1)} %get-tuple-element.57.mine_ref), channel_id=1, source_target_pairs={{0,1},{1,0},{2,3},{3,2},{4,5},{5,4},{6,7},{7,6},{8,9},{9,8},{10,11... | collective-permute-start | bytes 49160 | tf_op jit(solution)/shard_map/ppermute | solution.py:602

commit v14 on v12

--- a/solution.py
+++ b/solution.py
@@ -515,9 +515,9 @@
             [VMEM] * (groups + n - 1),
         )(*sums, *rests[1:])
         low, high = n // 4, n // 2
-        both_far = [high + low + i for i in range(low)]
-        mixed = [high + i for i in reversed(range(low))] + [low + i for i in reversed(range(low))]
-        stages = [[0] + both_far + mixed[: low // 2], mixed[low // 2 :], list(range(1, low))]
+        mixed = [r for i in reversed(range(low)) for r in (high + i, low + i)]
+        order = [high + low, mixed[0], *range(high + low + 1, n), *mixed[1:], *range(1, low)]
+        stages = [[0] + order[: high - 1], order[high - 1 : n - low], order[n - low :]]
         levs = lax.axis_size("lev")
         arrived = {0: [total, rests[0]]}
         for r in sum(stages, [])[1:]:

time: 27.4 us -> 27.8 us (1.015)
  waiting for transfers between devices: 2 us -> 3.51 us
  starting transfers between devices: 16.4 us -> 15.2 us
    ppermute x7, waiting for transfers between devices: 0.66 us -> 2.16 us  [body(): arrived[r] = [lax.ppermute(blocks[r - 1], ('tile', 'lev'), pairs)]]
    ppermute x7, starting transfers between devices: 12.8 us -> 11.7 us  [body(): arrived[r] = [lax.ppermute(blocks[r - 1], ('tile', 'lev'), pairs)]]
where the time goes in v14:
time: 27.8 us; the launch traced here: 27.6 us
  starting transfers between devices  15.2 us (55%)
  Pallas kernels  6.72 us (24%)
  waiting for transfers between devices  3.51 us (13%)
  local copies, waits for them, and re-layouts  1.39 us (5%)
  between operations  0.78 us (3%)
    ppermute x7, starting transfers between devices, body(): arrived[r] = [lax.ppermute(blocks[r - 1], ('tile', 'lev'), pairs)]  11.7 us
    ppermute x1, starting transfers between devices, body(): lax.ppermute(sums[0], 'grp', [(g, (g + k) % groups) for g in range(groups)])  2.97 us
    ppermute x7, waiting for transfers between devices, body(): arrived[r] = [lax.ppermute(blocks[r - 1], ('tile', 'lev'), pairs)]  2.16 us
    pallas_call x2, Pallas kernels, body(): call(functools.partial(stage_kernel, n, levels, band_cols, tile_cols, sta...  1.96 us
    unnamed x24, local copies, waits for them, and re-layouts  1.39 us
    pallas_call x1, Pallas kernels, body(): call(ens_kernel, (shape(control.shape, F32), flat, flat), [VMEM] * 5, [pl...  1.25 us
    pallas_call x1, Pallas kernels, body(): call(functools.partial(static_kernel, band_cols), [shape((rows.total, cap...  1.11 us
    ppermute x1, waiting for transfers between devices, body(): other_control = lax.ppermute(control, 'lev', swap)  0.9 us
  transfers between devices with their start and end apart: 11, of which 4 were waited for; matrix products, arithmetic and copies ran while one was open for 0% of the time, Pallas kernels for 17%

profile of v14, /device:TPU:0, one launch (start us, length us, event | category | flops | bytes accessed | tf_op | source)
XLA Modules:
  0.0 27.6 jit_solution(78809266751169908)
XLA Ops:
  0.6 0.5 %collective-permute-start = (f32[16,40,256]{2,1,0:T(8,128)}, f32[16,40,256]{2,1,0:T(8,128)S(1)}, u32[]{:S(2)}, u32[]{:S(2)}) collective-permute-start(f32[16,40,256]{2,1,0:T(8,128)} %control_ref.3), channel_id=1, source_target_pairs={{0,1},{1,0},{2,3},{3,2},{4,5},{5,4},{6,7},{7,6},{8,9},{9,8},{10,11... | collective-permute-start | bytes 1966088 | tf_op jit(solution)/shard_map/ppermute | solution.py:490
  1.1 0.1 collective-permute-start.1
  1.2 0.0 copy-start.11
  1.2 0.7 %copy-done.11 = f32[16,32]{1,0:T(8,128)S(1)} copy-done((f32[16,32]{1,0:T(8,128)S(1)}, f32[16,32]{1,0:T(8,128)}, u32[]{:S(2)}) %copy-start.11) | copy-done | bytes 2072
  1.9 0.0 copy-start
  1.9 0.2 shard_map.139
  2.2 0.9 %collective-permute-done.other_ref = f32[16,40,256]{2,1,0:T(8,128)S(1)} collective-permute-done((f32[16,40,256]{2,1,0:T(8,128)}, f32[16,40,256]{2,1,0:T(8,128)S(1)}, u32[]{:S(2)}, u32[]{:S(2)}) %collective-permute-start) | collective-permute-done | bytes 655392 | tf_op jit(solution)/shard_map/ppermute | solution.py:490
  3.1 0.0 copy-done
  3.1 0.0 copy-done.1
  3.1 0.0 copy-start.7
  3.1 0.0 copy-start.8
  3.1 0.0 copy-start.9
  3.1 0.5 %shard_map.140.refs_0_ = f32[16,256]{1,0:T(8,128)S(1)} custom-call(bf16[16,40,256]{2,1,0:T(8,128)(2,1)S(1)} %copy-done.1, f32[16,40,256]{2,1,0:T(8,128)S(1)} %copy-done, f32[16,40,256]{2,1,0:T(8,128)S(1)} %collective-permute-done.other_ref, bf16[2,128,256]{2,1,0:T(8,128)(2,1)S(1)} %get-tuple-element.39.mix_ref), custom_call_target="tpu_custom_call" | custom-call | tf_op jit(solution)/shard_map/pallas_call | solution.py:498
  3.6 0.0 collective-permute-done.1.perturb_ref
  3.7 3.0 %collective-permute-start.2 = (f32[16,256]{1,0:T(8,128)S(1)}, f32[16,256]{1,0:T(8,128)S(1)}, u32[]{:S(2)}, u32[]{:S(2)}) collective-permute-start(f32[16,256]{1,0:T(8,128)S(1)} %shard_map.140.refs_0_), channel_id=1, source_target_pairs={{0,16},{16,0},{1,17},{17,1},{2,18},{18,2},{3,19},{19,3},{4,20},{20... | collective-permute-start | bytes 49160 | tf_op jit(solution)/shard_map/ppermute | solution.py:511
  6.6 0.0 copy-done.2
  6.6 0.0 copy-done.3
  6.6 0.0 copy-done.4
  6.7 0.0 copy-done.7
  6.7 0.0 copy-done.8
  6.7 0.0 copy-done.9
  6.7 0.6 %copy-done.6 = f32[1024]{0:T(1024)S(1)} copy-done((f32[1024]{0:T(1024)S(1)}, f32[1024]{0:T(1024)}, u32[]{:S(2)}) %copy-start.6) | copy-done | bytes 4120
  7.3 0.0 copy-done.5
  7.3 0.0 copy-done.10
  7.3 1.1 %shard_map.141 = (f32[56,128]{1,0:T(8,128)S(1)}, f32[56,128]{1,0:T(8,128)S(1)}, f32[56,128]{1,0:T(8,128)S(1)}, f32[56,128]{1,0:T(8,128)S(1)}, f32[56,128]{1,0:T(...) custom-call(s32[1]{0:T(128)} %bitcast.1.pos_ref, s32[1]{0:T(128)} %bitcast.lev_ref, ...), custom_call_target="tpu_custom_call" | custom-call | tf_op jit(solution)/shard_map/pallas_call | solution.py:505
  8.4 0.0 collective-permute-done.2.refs_1_
  8.5 4.1 %collective-permute-start.3 = (f32[88,128]{1,0:T(8,128)S(1)}, f32[88,128]{1,0:T(8,128)S(1)}, u32[]{:S(2)}, u32[]{:S(2)}) collective-permute-start(f32[88,128]{1,0:T(8,128)S(1)} %get-tuple-element.52), channel_id=1, source_target_pairs={{0,12},{1,13},{2,14},{3,15},{4,8},{5,9},{6,10},{7,11},{8,4},{9,5},... | collective-permute-start | bytes 135176 | tf_op jit(solution)/shard_map/ppermute | solution.py:525
  12.6 0.4 %collective-permute-start.4 = (f32[88,128]{1,0:T(8,128)S(1)}, f32[88,128]{1,0:T(8,128)S(1)}, u32[]{:S(2)}, u32[]{:S(2)}) collective-permute-start(f32[88,128]{1,0:T(8,128)S(1)} %get-tuple-element.53), channel_id=1, source_target_pairs={{0,10},{1,7},{2,8},{3,5},{4,14},{5,3},{6,12},{7,1},{8,2},{9,15},{1... | collective-permute-start | bytes 135176 | tf_op jit(solution)/shard_map/ppermute | solution.py:525
  13.0 2.4 %collective-permute-start.5 = (f32[88,128]{1,0:T(8,128)S(1)}, f32[88,128]{1,0:T(8,128)S(1)}, u32[]{:S(2)}, u32[]{:S(2)}) collective-permute-start(f32[88,128]{1,0:T(8,128)S(1)} %get-tuple-element.54), channel_id=1, source_target_pairs={{0,14},{1,15},{2,12},{3,13},{4,10},{5,11},{6,8},{7,9},{8,6},{9,7},... | collective-permute-start | bytes 135176 | tf_op jit(solution)/shard_map/ppermute | solution.py:525
  15.4 2.5 %collective-permute-start.6 = (f32[88,128]{1,0:T(8,128)S(1)}, f32[88,128]{1,0:T(8,128)S(1)}, u32[]{:S(2)}, u32[]{:S(2)}) collective-permute-start(f32[88,128]{1,0:T(8,128)S(1)} %get-tuple-element.55), channel_id=1, source_target_pairs={{0,6},{1,11},{2,4},{3,9},{4,2},{5,15},{6,0},{7,13},{8,14},{9,3},{1... | collective-permute-start | bytes 135176 | tf_op jit(solution)/shard_map/ppermute | solution.py:525
  17.9 0.3 %collective-permute-start.7 = (f32[88,128]{1,0:T(8,128)S(1)}, f32[88,128]{1,0:T(8,128)S(1)}, u32[]{:S(2)}, u32[]{:S(2)}) collective-permute-start(f32[88,128]{1,0:T(8,128)S(1)} %get-tuple-element.56), channel_id=1, source_target_pairs={{0,8},{1,5},{2,10},{3,7},{4,12},{5,1},{6,14},{7,3},{8,0},{9,13},{1... | collective-permute-start | bytes 135176 | tf_op jit(solution)/shard_map/ppermute | solution.py:525
  18.2 0.0 collective-permute-done.3.refs_2_
  18.2 0.4 %collective-permute-start.8 = (f32[88,128]{1,0:T(8,128)S(1)}, f32[88,128]{1,0:T(8,128)S(1)}, u32[]{:S(2)}, u32[]{:S(2)}) collective-permute-start(f32[88,128]{1,0:T(8,128)S(1)} %get-tuple-element.57), channel_id=1, source_target_pairs={{0,4},{1,9},{2,6},{3,11},{4,0},{5,13},{6,2},{7,15},{8,12},{9,1},{1... | collective-permute-start | bytes 135176 | tf_op jit(solution)/shard_map/ppermute | solution.py:525
  18.7 1.3 %collective-permute-done.4.refs_3_ = f32[88,128]{1,0:T(8,128)S(1)} collective-permute-done((f32[88,128]{1,0:T(8,128)S(1)}, f32[88,128]{1,0:T(8,128)S(1)}, u32[]{:S(2)}, u32[]{:S(2)}) %collective-permute-start.4) | collective-permute-done | bytes 45088 | tf_op jit(solution)/shard_map/ppermute | solution.py:525
  20.0 1.4 %collective-permute-start.9 = (f32[88,128]{1,0:T(8,128)S(1)}, f32[88,128]{1,0:T(8,128)S(1)}, u32[]{:S(2)}, u32[]{:S(2)}) collective-permute-start(f32[88,128]{1,0:T(8,128)S(1)} %get-tuple-element.58), channel_id=1, source_target_pairs={{0,2},{1,3},{2,0},{3,1},{4,6},{5,7},{6,4},{7,5},{8,10},{9,11},{10,... | collective-permute-start | bytes 135176 | tf_op jit(solution)/shard_map/ppermute | solution.py:525
  21.4 0.0 collective-permute-done.5.refs_4_
  21.4 0.9 %shard_map.143 = (bf16[8,32,512]{2,1,0:T(8,128)(2,1)S(1)}, f32[4,16,128]{2,1,0:T(8,128)S(1)}, f32[16,1024]{1,0:T(8,128)S(1)}, bf16[8,256,128]{2,1,0:T(8,128)(2,1)S(1)}) custom-call(f32[32,128]{1,0:T(8,128)S(1)} %get-tuple-element.50.refs_0_, f32[56,128]{1,0:T(8,128)S(1)} %get-tuple-element.51.refs_1_, f32[88,128]{1,0:T(8,128)S(1)} %collective-permute-done.3.refs_2_, ...), custom_call_target="tpu_custom_call" | custom-call | tf_op jit(solution)/shard_map/pallas_call | solution.py:535
  22.4 0.0 collective-permute-done.6.refs_5_
  22.4 0.8 %collective-permute-done.7.refs_6_ = f32[88,128]{1,0:T(8,128)S(1)} collective-permute-done((f32[88,128]{1,0:T(8,128)S(1)}, f32[88,128]{1,0:T(8,128)S(1)}, u32[]{:S(2)}, u32[]{:S(2)}) %collective-permute-start.7) | collective-permute-done | bytes 45088 | tf_op jit(solution)/shard_map/ppermute | solution.py:525
  23.2 0.0 collective-permute-done.8.refs_7_
  23.2 1.0 %shard_map.144 = (bf16[8,32,384]{2,1,0:T(8,128)(2,1)S(1)}, f32[7,16,128]{2,1,0:T(8,128)S(1)}, f32[16,1024]{1,0:T(8,128)S(1)}) custom-call(f32[32,128]{1,0:T(8,128)S(1)} %get-tuple-element.50.refs_0_, f32[56,128]{1,0:T(8,128)S(1)} %get-tuple-element.51.refs_1_, f32[88,128]{1,0:T(8,128)S(1)} %collective-permute-done.3.refs_2_, ...), custom_call_target="tpu_custom_call" | custom-call | tf_op jit(solution)/shard_map/pallas_call | solution.py:535
  24.3 0.0 collective-permute-done.9.refs_8_
  24.3 0.9 %shard_map.145 = (f32[48,128]{1,0:T(8,128)S(1)}, bf16[8,32,128]{2,1,0:T(8,128)(2,1)S(1)}, f32[8,16,128]{2,1,0:T(8,128)S(1)}) custom-call(s32[1]{0:T(128)} %bitcast.1.pos_ref, s32[1]{0:T(128)} %bitcast.lev_ref, f32[16,128]{1,0:T(8,128)S(1)} %get-tuple-element.41.mix_ref, f32[32,128]{1,0:T(8,128)S(1)} %get-tuple-element.50.refs_0_, ...), custom_call_target="tpu_custom_call" | custom-call | tf_op jit(solution)/shard_map/pallas_call | solution.py:545
  25.2 0.0 collective-permute-start.10
  25.2 0.4 %shard_map.146.own_ref = f32[16,40,256]{2,1,0:T(8,128)S(1)} custom-call(bf16[16,40,256]{2,1,0:T(8,128)(2,1)S(1)} %copy-done.1, f32[48,128]{1,0:T(8,128)S(1)} %get-tuple-element.65.mine_ref, bf16[2,128,128]{2,1,0:T(8,128)(2,1)S(1)} %get-tuple-element.66.weights_ref, f32[16,40,256]{2,1,0:T(8,128)S(1)} %copy-done), custom_call_target="tpu_custom_call" | custom-call | tf_op jit(solution)/shard_map/pallas_call | solution.py:573
  25.6 0.3 %shard_map.147 = (f32[16,1024]{1,0:T(8,128)S(1)}, f32[16,1024]{1,0:T(8,128)S(1)}) custom-call(s32[1]{0:T(128)} %bitcast.1.pos_ref, s32[1]{0:T(128)} %bitcast.lev_ref, bf16[8,32,512]{2,1,0:T(8,128)(2,1)S(1)} %get-tuple-element.59.refs_8_.refs_9_.refs_0_, bf16[8,32,384]{2,1,0:T(8,128)(2,1)S(1)} %get-tuple-element.62.refs_10_.refs_1_, ...), custom_call_target="tpu_custom_call" | custom-call | tf_op jit(solution)/shard_map/pallas_call | solution.py:551
  25.9 0.4 %collective-permute-done.10.theirs_ref = f32[48,128]{1,0:T(8,128)S(1)} collective-permute-done((f32[48,128]{1,0:T(8,128)S(1)}, f32[48,128]{1,0:T(8,128)S(1)}, u32[]{:S(2)}, u32[]{:S(2)}) %collective-permute-start.10) | collective-permute-done | bytes 24608 | tf_op jit(solution)/shard_map/ppermute | solution.py:572
  26.4 1.2 %shard_map.148 = (f32[16,40,256]{2,1,0:T(8,128)}, f32[16,1024]{1,0:T(8,128)}, f32[16,1024]{1,0:T(8,128)}) custom-call(bf16[16,40,256]{2,1,0:T(8,128)(2,1)S(1)} %collective-permute-done.1.perturb_ref, f32[48,128]{1,0:T(8,128)S(1)} %collective-permute-done.10.theirs_ref, f32[16,40,256]{2,1,0:T(8,128)S(1)} %shard_map.146.own_ref, ...), custom_call_target="tpu_custom_call" | custom-call | tf_op jit(solution)/shard_map/pallas_call | solution.py:574
  (8 shorter events, 0.0 us)
Async XLA Ops:
  0.6 2.5 %collective-permute-start = (f32[16,40,256]{2,1,0:T(8,128)}, f32[16,40,256]{2,1,0:T(8,128)S(1)}, u32[]{:S(2)}, u32[]{:S(2)}) collective-permute-start(f32[16,40,256]{2,1,0:T(8,128)} %control_ref.3), channel_id=1, source_target_pairs={{0,1},{1,0},{2,3},{3,2},{4,5},{5,4},{6,7},{7,6},{8,9},{9,8},{10,11... | collective-permute-start | bytes 1966088 | tf_op jit(solution)/shard_map/ppermute | solution.py:490
  1.1 2.5 %collective-permute-start.1 = (bf16[16,40,256]{2,1,0:T(8,128)(2,1)}, bf16[16,40,256]{2,1,0:T(8,128)(2,1)S(1)}, u32[]{:S(2)}, u32[]{:S(2)}) collective-permute-start(bf16[16,40,256]{2,1,0:T(8,128)(2,1)} %perturb_ref.3), channel_id=1, source_target_pairs={{0,1},{1,0},{2,3},{3,2},{4,5},{5,4},{6,7},{7,6},{8,9},{9,8},{10,11... | collective-permute-start | bytes 983048 | tf_op jit(solution)/shard_map/ppermute | solution.py:509
  1.2 0.7 %copy-start.11 = (f32[16,32]{1,0:T(8,128)S(1)}, f32[16,32]{1,0:T(8,128)}, u32[]{:S(2)}) copy-start(f32[16,32]{1,0:T(8,128)} %loc_ref.1) | copy-start | bytes 6148
  1.9 1.2 %copy-start = (f32[16,40,256]{2,1,0:T(8,128)S(1)}, f32[16,40,256]{2,1,0:T(8,128)}, u32[]{:S(2)}) copy-start(f32[16,40,256]{2,1,0:T(8,128)} %control_ref.3) | copy-start | bytes 1966084
  1.9 1.2 %copy-start.1 = (bf16[16,40,256]{2,1,0:T(8,128)(2,1)S(1)}, bf16[16,40,256]{2,1,0:T(8,128)(2,1)}, u32[]{:S(2)}) copy-start(bf16[16,40,256]{2,1,0:T(8,128)(2,1)} %perturb_ref.3) | copy-start | bytes 983044
  3.1 3.5 %copy-start.2 = (f32[16,1024]{1,0:T(8,128)S(1)}, f32[16,1024]{1,0:T(8,128)}, u32[]{:S(2)}) copy-start(f32[16,1024]{1,0:T(8,128)} %refs_5_.1) | copy-start | bytes 196612
  3.1 3.5 %copy-start.3 = (f32[16,1024]{1,0:T(8,128)S(1)}, f32[16,1024]{1,0:T(8,128)}, u32[]{:S(2)}) copy-start(f32[16,1024]{1,0:T(8,128)} %refs_8_.1) | copy-start | bytes 196612
  3.1 3.5 %copy-start.4 = (f32[16,1024]{1,0:T(8,128)S(1)}, f32[16,1024]{1,0:T(8,128)}, u32[]{:S(2)}) copy-start(f32[16,1024]{1,0:T(8,128)} %refs_9_.1) | copy-start | bytes 196612
  3.1 3.5 %copy-start.7 = (s32[1,8,128]{2,1,0:T(8,128)S(1)}, s32[1,8,128]{2,1,0:T(8,128)}, u32[]{:S(2)}) copy-start(s32[1,8,128]{2,1,0:T(8,128)} %src_ref.1) | copy-start | bytes 12292
  3.1 3.5 %copy-start.8 = (f32[1,8,128]{2,1,0:T(8,128)S(1)}, f32[1,8,128]{2,1,0:T(8,128)}, u32[]{:S(2)}) copy-start(f32[1,8,128]{2,1,0:T(8,128)} %weight_ref.1) | copy-start | bytes 12292
  3.1 3.5 %copy-start.9 = (s32[1,8,128]{2,1,0:T(8,128)S(1)}, s32[1,8,128]{2,1,0:T(8,128)}, u32[]{:S(2)}) copy-start(s32[1,8,128]{2,1,0:T(8,128)} %tgt_ref.1) | copy-start | bytes 12292
  3.7 4.8 %collective-permute-start.2 = (f32[16,256]{1,0:T(8,128)S(1)}, f32[16,256]{1,0:T(8,128)S(1)}, u32[]{:S(2)}, u32[]{:S(2)}) collective-permute-start(f32[16,256]{1,0:T(8,128)S(1)} %shard_map.140.refs_0_), channel_id=1, source_target_pairs={{0,16},{16,0},{1,17},{17,1},{2,18},{18,2},{3,19},{19,3},{4,20},{20... | collective-permute-start | bytes 49160 | tf_op jit(solution)/shard_map/ppermute | solution.py:511
  6.6 0.7 %copy-start.6 = (f32[1024]{0:T(1024)S(1)}, f32[1024]{0:T(1024)}, u32[]{:S(2)}) copy-start(f32[1024]{0:T(1024)} %param.17) | copy-start | bytes 12292
  6.6 0.7 %copy-start.5 = (f32[1024]{0:T(1024)S(1)}, f32[1024]{0:T(1024)}, u32[]{:S(2)}) copy-start(f32[1024]{0:T(1024)} %param.16) | copy-start | bytes 12292
  6.6 0.7 %copy-start.10 = (s32[1,8]{1,0:T(1,128)S(1)}, s32[1,8]{1,0:T(1,128)}, u32[]{:S(2)}) copy-start(s32[1,8]{1,0:T(1,128)} %counts_ref.1) | copy-start | bytes 100
  8.5 9.8 %collective-permute-start.3 = (f32[88,128]{1,0:T(8,128)S(1)}, f32[88,128]{1,0:T(8,128)S(1)}, u32[]{:S(2)}, u32[]{:S(2)}) collective-permute-start(f32[88,128]{1,0:T(8,128)S(1)} %get-tuple-element.52), channel_id=1, source_target_pairs={{0,12},{1,13},{2,14},{3,15},{4,8},{5,9},{6,10},{7,11},{8,4},{9,5},... | collective-permute-start | bytes 135176 | tf_op jit(solution)/shard_map/ppermute | solution.py:525
  12.6 7.4 %collective-permute-start.4 = (f32[88,128]{1,0:T(8,128)S(1)}, f32[88,128]{1,0:T(8,128)S(1)}, u32[]{:S(2)}, u32[]{:S(2)}) collective-permute-start(f32[88,128]{1,0:T(8,128)S(1)} %get-tuple-element.53), channel_id=1, source_target_pairs={{0,10},{1,7},{2,8},{3,5},{4,14},{5,3},{6,12},{7,1},{8,2},{9,15},{1... | collective-permute-start | bytes 135176 | tf_op jit(solution)/shard_map/ppermute | solution.py:525
  13.0 8.5 %collective-permute-start.5 = (f32[88,128]{1,0:T(8,128)S(1)}, f32[88,128]{1,0:T(8,128)S(1)}, u32[]{:S(2)}, u32[]{:S(2)}) collective-permute-start(f32[88,128]{1,0:T(8,128)S(1)} %get-tuple-element.54), channel_id=1, source_target_pairs={{0,14},{1,15},{2,12},{3,13},{4,10},{5,11},{6,8},{7,9},{8,6},{9,7},... | collective-permute-start | bytes 135176 | tf_op jit(solution)/shard_map/ppermute | solution.py:525
  15.4 7.0 %collective-permute-start.6 = (f32[88,128]{1,0:T(8,128)S(1)}, f32[88,128]{1,0:T(8,128)S(1)}, u32[]{:S(2)}, u32[]{:S(2)}) collective-permute-start(f32[88,128]{1,0:T(8,128)S(1)} %get-tuple-element.55), channel_id=1, source_target_pairs={{0,6},{1,11},{2,4},{3,9},{4,2},{5,15},{6,0},{7,13},{8,14},{9,3},{1... | collective-permute-start | bytes 135176 | tf_op jit(solution)/shard_map/ppermute | solution.py:525
  17.9 5.3 %collective-permute-start.7 = (f32[88,128]{1,0:T(8,128)S(1)}, f32[88,128]{1,0:T(8,128)S(1)}, u32[]{:S(2)}, u32[]{:S(2)}) collective-permute-start(f32[88,128]{1,0:T(8,128)S(1)} %get-tuple-element.56), channel_id=1, source_target_pairs={{0,8},{1,5},{2,10},{3,7},{4,12},{5,1},{6,14},{7,3},{8,0},{9,13},{1... | collective-permute-start | bytes 135176 | tf_op jit(solution)/shard_map/ppermute | solution.py:525
  18.2 5.0 %collective-permute-start.8 = (f32[88,128]{1,0:T(8,128)S(1)}, f32[88,128]{1,0:T(8,128)S(1)}, u32[]{:S(2)}, u32[]{:S(2)}) collective-permute-start(f32[88,128]{1,0:T(8,128)S(1)} %get-tuple-element.57), channel_id=1, source_target_pairs={{0,4},{1,9},{2,6},{3,11},{4,0},{5,13},{6,2},{7,15},{8,12},{9,1},{1... | collective-permute-start | bytes 135176 | tf_op jit(solution)/shard_map/ppermute | solution.py:525
  20.0 4.3 %collective-permute-start.9 = (f32[88,128]{1,0:T(8,128)S(1)}, f32[88,128]{1,0:T(8,128)S(1)}, u32[]{:S(2)}, u32[]{:S(2)}) collective-permute-start(f32[88,128]{1,0:T(8,128)S(1)} %get-tuple-element.58), channel_id=1, source_target_pairs={{0,2},{1,3},{2,0},{3,1},{4,6},{5,7},{6,4},{7,5},{8,10},{9,11},{10,... | collective-permute-start | bytes 135176 | tf_op jit(solution)/shard_map/ppermute | solution.py:525
  25.2 1.2 %collective-permute-start.10 = (f32[48,128]{1,0:T(8,128)S(1)}, f32[48,128]{1,0:T(8,128)S(1)}, u32[]{:S(2)}, u32[]{:S(2)}) collective-permute-start(f32[48,128]{1,0:T(8,128)S(1)} %get-tuple-element.65.mine_ref), channel_id=1, source_target_pairs={{0,1},{1,0},{2,3},{3,2},{4,5},{5,4},{6,7},{7,6},{8,9},{9,8},{10,11... | collective-permute-start | bytes 73736 | tf_op jit(solution)/shard_map/ppermute | solution.py:572

commit v15 on v14

--- a/solution.py
+++ b/solution.py
@@ -274,38 +274,44 @@
         out_ref[rows.edge :, :] = edge
 
 
-def blocks_kernel(groups, *refs):
+def blocks_kernel(groups, levels, *refs):
     sums = refs[:groups]
     count = (len(refs) - groups - 1) // 2
     rests = refs[groups : groups + count]
-    total_ref = refs[groups + count]
-    out_refs = refs[groups + count + 1 :]
+    total_ref, *out_refs = refs[groups + count :]
     total = sum(ref[...] for ref in sums)
     cap = total_ref.shape[1]
     total = jnp.concatenate([total[:, at : at + cap] for at in range(0, total.shape[1], cap)], axis=0)
     total_ref[...] = total
-    for rest_ref, out_ref in zip(rests, out_refs):
+    for rest_ref, out_ref in zip(rests[:-1], out_refs[:-1]):
         out_ref[: total.shape[0], :] = total
         out_ref[total.shape[0] :, :] = rest_ref[...]
+    out_refs[-1][...] = jnp.concatenate([total, rests[-1][: 2 * levels, :], rests[-1][-EXTRA:, :]], axis=0)
+
+
+def pair_kernel(levels, total_ref, rest_ref, given_ref, out_ref):
+    head = total_ref.shape[0] + 2 * levels
+    out_ref[...] = jnp.concatenate(
+        [given_ref[:head, :], rest_ref[2 * levels : -EXTRA, :], given_ref[head:, :]]
+        + [total_ref[...], rest_ref[: 2 * levels, :], rest_ref[-EXTRA:, :]],
+        axis=0,
+    )
 
 
 class Block:
-    def __init__(self, refs, n, levels, band):
-        cap = refs[0].shape[1]
-        self.levels, self.parts, self.cap = levels, band // cap, cap
-        self.sums_ref, self.rest_ref = refs[0], refs[-1]
-        self.head = 0 if len(refs) == 2 else self.parts * levels
-        self.rows = Rows(levels, n)
-        words = self.rest(self.rows.index, n)
+    def __init__(self, sums, rest, n, levels, band):
+        self.levels, self.parts, self.cap = levels, sums.shape[0] // levels, sums.shape[1]
+        rows = Rows(levels, n)
+        self.stacked = sums
+        self.weight, self.base = rest[rows.weight], rest[rows.base]
+        self.factor = rest[rows.factor : rows.factor + n]
+        self.edge = rest[rows.edge :]
+        words = rest[rows.index : rows.index + n]
         self.tgt = jnp.floor((words + 0.5) * (1.0 / band))
         self.src = words - self.tgt * float(band)
-        self.factor = self.rest(self.rows.factor, n)
-
-    def rest(self, at, size):
-        return self.rest_ref[self.head + at : self.head + at + size, :]
 
     def sums(self):
-        parts = [self.sums_ref[i * self.levels : (i + 1) * self.levels, :] for i in range(self.parts)]
+        parts = [self.stacked[i * self.levels : (i + 1) * self.levels, :] for i in range(self.parts)]
         return jnp.concatenate(halves(jnp.concatenate(parts, axis=1)), axis=0)
 
 
@@ -347,17 +353,31 @@
     return total[:levels] + total[levels:]
 
 
-def open_blocks(labels, refs, n, levels, band):
-    blocks = {0: Block(refs[:2], n, levels, band)}
+def open_blocks(labels, refs, lev, n, levels, band):
+    blocks = {0: Block(refs[0][...], refs[1][...], n, levels, band)}
+    head, total = refs[0].shape[0], refs[1].shape[0]
     refs = refs[2:]
-    for i, r in enumerate(labels[1:]):
-        blocks[r] = Block(refs[i : i + 1], n, levels, band)
-    return blocks, refs[len(labels) - 1 :]
-
-
-def stage_kernel(n, levels, band, cols, stages, *refs):
+    for r in labels[1:]:
+        if r < n - 1:
+            blocks[r] = Block(refs[0][:head, :], refs[0][head:, :], n, levels, band)
+            refs = refs[1:]
+            continue
+        both = jnp.where(lev == 1, refs[0][...], refs[1][...])
+        refs = refs[2:]
+        first, second = both[: head + total], both[head + total :]
+        at = head + 2 * levels
+        tables = first[at : at + 2 * n]
+        turned = [tables[i + relabel(q, n, 1)][None] for i in (0, n) for q in range(n)]
+        tables = jnp.where(lev == 1, tables, jnp.concatenate(turned, axis=0))
+        first = jnp.concatenate([first[:at], first[at + 2 * n :]], axis=0)
+        mine = jnp.where(lev == 1, second, first)
+        blocks[r] = Block(mine[:head], jnp.concatenate([mine[head:at], tables, mine[at:]], axis=0), n, levels, band)
+    return blocks, refs
+
+
+def stage_kernel(n, levels, band, cols, stages, lev_ref, *refs):
     known = sum(stages[:-1], [])
-    blocks, refs = open_blocks(known + stages[-1], refs, n, levels, band)
+    blocks, refs = open_blocks(known + stages[-1], refs, lev_ref[0], n, levels, band)
     old, refs = refs[: len(stages) - 1], refs[len(stages) - 1 :]
     if known:
         met_old, remap_old, slots_ref, met_ref, remap_ref = refs
@@ -380,25 +400,25 @@
 
 def shared_kernel(n, levels, band, cols, stages, pos_ref, lev_ref, mix_ref, *refs):
     known = sum(stages[:-1], [])
-    blocks, refs = open_blocks(known + stages[-1], refs, n, levels, band)
+    blocks, refs = open_blocks(known + stages[-1], refs, lev_ref[0], n, levels, band)
     old, refs = refs[: len(stages) - 1], refs[len(stages) - 1 :]
     met_old, pick_ref, out_ref, slots_ref, tables_ref = refs
     me = pos_ref[0]
     for r, block in blocks.items():
         there = me ^ relabel(r, n, lev_ref[0])
         tables_ref[there, :n, :] = block.tgt
-        tables_ref[there, n:, :] = block.rest(block.rows.edge, EXTRA)
+        tables_ref[there, n:, :] = block.edge
     fill_slots(stages[-1], blocks, n, slots_ref)
     last = cols - 1.0
     total = jnp.zeros((levels, band), F32)
     for i, (d, block) in enumerate(blocks.items()):
-        value = met_at(d, block, stages[-1], slots_ref) + block.rest(levels, levels)
+        value = met_at(d, block, stages[-1], slots_ref) + block.base
         if d in known:
             value = value + met_old[i]
         else:
             for bands, ref in zip(stages, old):
                 value = value + met_at(d, block, bands, ref)
-        edge = block.rest(block.rows.edge, 1)
+        edge = line(block.edge, 0)
         own = line(block.tgt, d)
         there = me ^ relabel(d, n, lev_ref[0])
         before = tables_ref[jnp.maximum(there - 1, 0), n : n + 1, :]
@@ -407,7 +427,7 @@
         after = tables_ref[jnp.minimum(there + 1, n - 1), n : n + 1, :]
         near = jnp.where((own == last) & (there < n - 1), edge[:, 6 * levels : 6 * levels + 1], 0.0)
         value = value + row_as_column(after, levels, levels) * near
-        given = block.rest(0, levels) * value * line(blocks[0].factor, d)
+        given = block.weight * value * line(blocks[0].factor, d)
         total = total + select(given, pick_ref[d], ((1,), (1,)))
     out_ref[...] = band_rows(total, mix_ref[...])
 
@@ -509,20 +529,31 @@
         sums[0], other_perturb = lax.optimization_barrier((sums[0], lax.ppermute(perturb, "lev", swap)))
         for k in range(1, groups):
             sums.append(lax.ppermute(sums[0], "grp", [(g, (g + k) % groups) for g in range(groups)]))
-        total, *blocks = call(
-            functools.partial(blocks_kernel, groups),
-            [shape((stacked, cap), F32)] + [shape((stacked + rows.total, cap), F32)] * (n - 1),
+        low, high = n // 4, n // 2
+        order = [low, n - 1, *range(high + 1, n - 1), *range(low + 1, high), high, *range(1, low)]
+        stages = [[0, order[0], *order[2:4]], [n - 1, *order[4:-1]], order[-1:]]
+        direct = [r for r in order if r < n - 1]
+        total, *blocks, give = call(
+            functools.partial(blocks_kernel, groups, levels),
+            [shape((stacked, cap), F32)]
+            + [shape((stacked + rows.total, cap), F32)] * len(direct)
+            + [shape((stacked + 2 * levels + EXTRA, cap), F32)],
             [VMEM] * (groups + n - 1),
-        )(*sums, *rests[1:])
-        low, high = n // 4, n // 2
-        mixed = [r for i in reversed(range(low)) for r in (high + i, low + i)]
-        order = [high + low, mixed[0], *range(high + low + 1, n), *mixed[1:], *range(1, low)]
-        stages = [[0] + order[: high - 1], order[high - 1 : n - low], order[n - low :]]
-        levs = lax.axis_size("lev")
+        )(*sums, *[rests[r] for r in direct], rests[n - 1])
+        given = lax.ppermute(give, "lev", [(0, 1)])
+        pair = call(
+            functools.partial(pair_kernel, levels),
+            shape((2 * stacked + rows.total + 2 * levels + EXTRA, cap), F32),
+            [VMEM] * 3,
+        )(total, rests[n - 1], given)
+        blocks = dict(zip(direct, blocks)) | {n - 1: pair}
         arrived = {0: [total, rests[0]]}
-        for r in sum(stages, [])[1:]:
-            pairs = [(i * levs + v, (i ^ relabel(r, n, v)) * levs + v) for i in range(n) for v in range(levs)]
-            arrived[r] = [lax.ppermute(blocks[r - 1], ("tile", "lev"), pairs)]
+        for k, r in enumerate(order):
+            if k == 3:
+                arrived[order[0]][0], blocks[r] = lax.optimization_barrier((arrived[order[0]][0], blocks[r]))
+            pairs = [(i * 2 + v, (i ^ relabel(r, n, v)) * 2 + v) for i in range(n) for v in range(2) if v or r < n - 1]
+            arrived[r] = [lax.ppermute(blocks[r], ("tile", "lev"), pairs)]
+        arrived[n - 1].append(lax.ppermute(arrived[n - 1][0], "lev", [(1, 0)]))
         slots, carried, picks = [], [], []
         for count in range(1, len(stages)):
             labels = sum(stages[:count], [])
@@ -535,8 +566,9 @@
             new, *carried = call(
                 functools.partial(stage_kernel, n, levels, band_cols, tile_cols, stages[:count]),
                 outs,
-                [VMEM] * (len(refs) + len(slots) + len(carried)),
-            )(*refs, *slots, *carried)
+                [SMEM] + [VMEM] * (len(refs) + len(slots) + len(carried)),
+                cost=pl.CostEstimate(flops=10**9, bytes_accessed=0, transcendentals=0),
+            )(lev, *refs, *slots, *carried)
             slots.append(new)
             picks += carried[2:]
             carried = carried[:2]
@@ -546,6 +578,7 @@
             functools.partial(shared_kernel, n, levels, band_cols, tile_cols, stages),
             (mine_shape, shape((n, 2 * levels, len(stages[-1]) * cap), BF16), shape((n, n + EXTRA, cap), F32)),
             [SMEM] * 2 + [VMEM] * (1 + len(refs)),
+            cost=pl.CostEstimate(flops=10**9, bytes_accessed=0, transcendentals=0),
         )(pos, lev, given_mix, *refs)
         slots.append(new)
         increment, grad_static = call(

time: 27.8 us -> 29.9 us (1.076)
  starting transfers between devices: 15.2 us -> 18.5 us
  waiting for transfers between devices: 3.51 us -> 2.14 us
    ppermute x7 -> x9, starting transfers between devices: 11.7 us -> 14.8 us  [the longest x7 11.8 us: body(): arrived[r] = [lax.ppermute(blocks[r], ('tile', 'lev'), pairs)]]
    ppermute x7 -> x9, waiting for transfers between devices: 2.16 us -> 0.98 us  [the longest x1 0.72 us: body(): arrived[n - 1].append(lax.ppermute(arrived[n - 1][0], 'lev', [(1, 0)]))]
  transfers between devices with their start and end apart: 11 -> 13, of which waited for: 4 -> 4; matrix products, arithmetic and copies ran while one was open for 0% -> 0% of each run, Pallas kernels for 17% -> 15%
where the time goes in v15:
time: 29.9 us; the launch traced here: 29.6 us
  starting transfers between devices  18.5 us (62%)
  Pallas kernels  6.68 us (22%)
  waiting for transfers between devices  2.14 us (7%)
  local copies, waits for them, and re-layouts  1.39 us (5%)
  between operations  0.82 us (3%)
    ppermute x7, starting transfers between devices, body(): arrived[r] = [lax.ppermute(blocks[r], ('tile', 'lev'), pairs)]  11.8 us
    ppermute x1, starting transfers between devices, body(): lax.ppermute(sums[0], 'grp', [(g, (g + k) % groups) for g in range(groups)])  2.97 us
    pallas_call x2, Pallas kernels, body(): call(functools.partial(stage_kernel, n, levels, band_cols, tile_cols, sta...  1.94 us
    ppermute x1, starting transfers between devices, body(): given = lax.ppermute(give, 'lev', [(0, 1)])  1.72 us
    unnamed x24, local copies, waits for them, and re-layouts  1.39 us
    ppermute x1, starting transfers between devices, body(): arrived[n - 1].append(lax.ppermute(arrived[n - 1][0], 'lev', [(1, 0)]))  1.28 us
    pallas_call x1, Pallas kernels, body(): call(ens_kernel, (shape(control.shape, F32), flat, flat), [VMEM] * 5, [pl...  1.25 us
    pallas_call x1, Pallas kernels, body(): call(functools.partial(static_kernel, band_cols), [shape((rows.total, cap...  1.1 us
  transfers between devices with their start and end apart: 13, of which 4 were waited for; matrix products, arithmetic and copies ran while one was open for 0% of the time, Pallas kernels for 15%

profile of v15, /device:TPU:0, one launch (start us, length us, event | category | flops | bytes accessed | tf_op | source)
XLA Modules:
  0.0 29.6 jit_solution(4310937169176322906)
XLA Ops:
  0.6 0.5 %collective-permute-start = (f32[16,40,256]{2,1,0:T(8,128)}, f32[16,40,256]{2,1,0:T(8,128)S(1)}, u32[]{:S(2)}, u32[]{:S(2)}) collective-permute-start(f32[16,40,256]{2,1,0:T(8,128)} %control_ref.3), channel_id=1, source_target_pairs={{0,1},{1,0},{2,3},{3,2},{4,5},{5,4},{6,7},{7,6},{8,9},{9,8},{10,11... | collective-permute-start | bytes 1966088 | tf_op jit(solution)/shard_map/ppermute | solution.py:510
  1.1 0.1 collective-permute-start.1
  1.2 0.7 %copy-done.11 = f32[16,32]{1,0:T(8,128)S(1)} copy-done((f32[16,32]{1,0:T(8,128)S(1)}, f32[16,32]{1,0:T(8,128)}, u32[]{:S(2)}) %copy-start.11) | copy-done | bytes 2072
  1.9 0.2 shard_map.139
  2.2 0.9 %collective-permute-done.other_ref = f32[16,40,256]{2,1,0:T(8,128)S(1)} collective-permute-done((f32[16,40,256]{2,1,0:T(8,128)}, f32[16,40,256]{2,1,0:T(8,128)S(1)}, u32[]{:S(2)}, u32[]{:S(2)}) %collective-permute-start) | collective-permute-done | bytes 655392 | tf_op jit(solution)/shard_map/ppermute | solution.py:510
  3.1 0.0 copy-done
  3.1 0.0 copy-done.1
  3.1 0.0 copy-start.7
  3.1 0.0 copy-start.8
  3.1 0.0 copy-start.9
  3.1 0.5 %shard_map.140.refs_0_ = f32[16,256]{1,0:T(8,128)S(1)} custom-call(bf16[16,40,256]{2,1,0:T(8,128)(2,1)S(1)} %copy-done.1, f32[16,40,256]{2,1,0:T(8,128)S(1)} %copy-done, f32[16,40,256]{2,1,0:T(8,128)S(1)} %collective-permute-done.other_ref, bf16[2,128,256]{2,1,0:T(8,128)(2,1)S(1)} %get-tuple-element.41.mix_ref), custom_call_target="tpu_custom_call" | custom-call | tf_op jit(solution)/shard_map/pallas_call | solution.py:518
  3.6 0.0 collective-permute-done.1.perturb_ref
  3.7 3.0 %collective-permute-start.2 = (f32[16,256]{1,0:T(8,128)S(1)}, f32[16,256]{1,0:T(8,128)S(1)}, u32[]{:S(2)}, u32[]{:S(2)}) collective-permute-start(f32[16,256]{1,0:T(8,128)S(1)} %shard_map.140.refs_0_), channel_id=1, source_target_pairs={{0,16},{16,0},{1,17},{17,1},{2,18},{18,2},{3,19},{19,3},{4,20},{20... | collective-permute-start | bytes 49160 | tf_op jit(solution)/shard_map/ppermute | solution.py:531
  6.6 0.0 copy-done.2
  6.6 0.0 copy-done.3
  6.6 0.0 copy-done.4
  6.7 0.0 copy-done.7
  6.7 0.0 copy-done.8
  6.7 0.6 %copy-done.6 = f32[1024]{0:T(1024)S(1)} copy-done((f32[1024]{0:T(1024)S(1)}, f32[1024]{0:T(1024)}, u32[]{:S(2)}) %copy-start.6) | copy-done | bytes 4120
  7.3 0.0 copy-done.5
  7.3 1.1 %shard_map.141 = (f32[56,128]{1,0:T(8,128)S(1)}, f32[56,128]{1,0:T(8,128)S(1)}, f32[56,128]{1,0:T(8,128)S(1)}, f32[56,128]{1,0:T(8,128)S(1)}, f32[56,128]{1,0:T(...) custom-call(s32[1]{0:T(128)} %bitcast.1.pos_ref, s32[1]{0:T(128)} %bitcast.lev_ref, ...), custom_call_target="tpu_custom_call" | custom-call | tf_op jit(solution)/shard_map/pallas_call | solution.py:525
  8.4 0.0 collective-permute-done.2.refs_1_
  8.5 1.7 %collective-permute-start.6 = (f32[72,128]{1,0:T(8,128)S(1)}, f32[72,128]{1,0:T(8,128)S(1)}, u32[]{:S(2)}, u32[]{:S(2)}) collective-permute-start(f32[72,128]{1,0:T(8,128)S(1)} %get-tuple-element.59), channel_id=1, source_target_pairs={{0,1},{2,3},{4,5},{6,7},{8,9},{10,11},{12,13},{14,15},{16,17},{18,... | collective-permute-start | bytes 110600 | tf_op jit(solution)/shard_map/ppermute | solution.py:543
  10.2 1.6 %collective-permute-start.3 = (f32[88,128]{1,0:T(8,128)S(1)}, f32[88,128]{1,0:T(8,128)S(1)}, u32[]{:S(2)}, u32[]{:S(2)}) collective-permute-start(f32[88,128]{1,0:T(8,128)S(1)} %get-tuple-element.54), channel_id=1, source_target_pairs={{0,4},{1,9},{2,6},{3,11},{4,0},{5,13},{6,2},{7,15},{8,12},{9,1},{1... | collective-permute-start | bytes 135176 | tf_op jit(solution)/shard_map/ppermute | solution.py:555
  11.8 0.0 collective-permute-done.6.given_ref
  11.9 0.7 %collective-permute-start.7 = (f32[160,128]{1,0:T(8,128)S(1)}, f32[160,128]{1,0:T(8,128)S(1)}, u32[]{:S(2)}, u32[]{:S(2)}) collective-permute-start(f32[160,128]{1,0:T(8,128)S(1)} %shard_map.143), channel_id=1, source_target_pairs={{1,15},{3,13},{5,11},{7,9},{9,7},{11,5},{13,3},{15,1},{17,31},{19,... | collective-permute-start | bytes 245768 | tf_op jit(solution)/shard_map/ppermute | solution.py:555
  12.5 3.6 %collective-permute-start.4 = (f32[88,128]{1,0:T(8,128)S(1)}, f32[88,128]{1,0:T(8,128)S(1)}, u32[]{:S(2)}, u32[]{:S(2)}) collective-permute-start(f32[88,128]{1,0:T(8,128)S(1)} %get-tuple-element.57), channel_id=1, source_target_pairs={{0,10},{1,7},{2,8},{3,5},{4,14},{5,3},{6,12},{7,1},{8,2},{9,15},{1... | collective-permute-start | bytes 135176 | tf_op jit(solution)/shard_map/ppermute | solution.py:555
  16.2 0.0 collective-permute-done.3.refs_2_
  16.2 1.9 %collective-permute-start.5 = (f32[88,128]{1,0:T(8,128)S(1)}, f32[88,128]{1,0:T(8,128)S(1)}, u32[]{:S(2)}, u32[]{:S(2)}) collective-permute-start(f32[88,128]{1,0:T(8,128)S(1)} %get-tuple-element.58), channel_id=1, source_target_pairs={{0,12},{1,13},{2,14},{3,15},{4,8},{5,9},{6,10},{7,11},{8,4},{9,5},... | collective-permute-start | bytes 135176 | tf_op jit(solution)/shard_map/ppermute | solution.py:555
  18.1 0.3 %collective-permute-start.9 = (f32[88,128]{1,0:T(8,128)S(1)}, f32[88,128]{1,0:T(8,128)S(1)}, u32[]{:S(2)}, u32[]{:S(2)}) collective-permute-start(f32[88,128]{1,0:T(8,128)S(1)} %get-tuple-element.60), channel_id=1, source_target_pairs={{0,6},{1,11},{2,4},{3,9},{4,2},{5,15},{6,0},{7,13},{8,14},{9,3},{1... | collective-permute-start | bytes 135176 | tf_op jit(solution)/shard_map/ppermute | solution.py:555
  18.4 2.1 %collective-permute-start.10 = (f32[88,128]{1,0:T(8,128)S(1)}, f32[88,128]{1,0:T(8,128)S(1)}, u32[]{:S(2)}, u32[]{:S(2)}) collective-permute-start(f32[88,128]{1,0:T(8,128)S(1)} %get-tuple-element.61), channel_id=1, source_target_pairs={{0,8},{1,5},{2,10},{3,7},{4,12},{5,1},{6,14},{7,3},{8,0},{9,13},{1... | collective-permute-start | bytes 135176 | tf_op jit(solution)/shard_map/ppermute | solution.py:555
  20.5 0.0 collective-permute-done.4.refs_3_
  20.5 1.5 %collective-permute-start.11 = (f32[88,128]{1,0:T(8,128)S(1)}, f32[88,128]{1,0:T(8,128)S(1)}, u32[]{:S(2)}, u32[]{:S(2)}) collective-permute-start(f32[88,128]{1,0:T(8,128)S(1)} %get-tuple-element.62), channel_id=1, source_target_pairs={{0,2},{1,3},{2,0},{3,1},{4,6},{5,7},{6,4},{7,5},{8,10},{9,11},{10,... | collective-permute-start | bytes 135176 | tf_op jit(solution)/shard_map/ppermute | solution.py:555
  22.0 0.0 collective-permute-done.7.refs_5_
  22.0 1.3 %collective-permute-start.8 = (f32[160,128]{1,0:T(8,128)S(1)}, f32[160,128]{1,0:T(8,128)S(1)}, u32[]{:S(2)}, u32[]{:S(2)}) collective-permute-start(f32[160,128]{1,0:T(8,128)S(1)} %collective-permute-done.7.refs_5_), channel_id=1, source_target_pairs={{1,0},{3,2},{5,4},{7,6},{9,8},{11,10},{13,12},{15,14},{17,16},{19,... | collective-permute-start | bytes 245768 | tf_op jit(solution)/shard_map/ppermute | solution.py:556
  23.3 0.0 collective-permute-done.5.refs_4_
  23.3 0.9 %shard_map.144 = (bf16[8,32,512]{2,1,0:T(8,128)(2,1)S(1)}, f32[4,16,128]{2,1,0:T(8,128)S(1)}, f32[16,1024]{1,0:T(8,128)S(1)}, bf16[8,256,128]{2,1,0:T(8,128)(2,1)S(1)}) custom-call(s32[1]{0:T(128)} %bitcast.lev_ref, f32[32,128]{1,0:T(8,128)S(1)} %get-tuple-element.52.total_ref.refs_0_, f32[56,128]{1,0:T(8,128)S(1)} %get-tuple-element.53.refs_1_, ...), custom_call_target="tpu_custom_call" | custom-call | flops 1000000000 | tf_op jit(solution)/shard_map/pallas_call | solution.py:566
  24.2 0.0 collective-permute-done.9.refs_7_
  24.2 0.2 collective-permute-done.10.refs_8_
  24.5 0.7 %collective-permute-done.8.refs_6_ = f32[160,128]{1,0:T(8,128)S(1)} collective-permute-done((f32[160,128]{1,0:T(8,128)S(1)}, f32[160,128]{1,0:T(8,128)S(1)}, u32[]{:S(2)}, u32[]{:S(2)}) %collective-permute-start.8) | collective-permute-done | bytes 81952 | tf_op jit(solution)/shard_map/ppermute | solution.py:556
  25.2 1.0 %shard_map.145 = (bf16[8,32,384]{2,1,0:T(8,128)(2,1)S(1)}, f32[7,16,128]{2,1,0:T(8,128)S(1)}, f32[16,1024]{1,0:T(8,128)S(1)}) custom-call(s32[1]{0:T(128)} %bitcast.lev_ref, f32[32,128]{1,0:T(8,128)S(1)} %get-tuple-element.52.total_ref.refs_0_, f32[56,128]{1,0:T(8,128)S(1)} %get-tuple-element.53.refs_1_, f32[88,128]{1,0:T(8,128)S(1)} %collective-permute-done.3.refs_2_, ...), custom_call_target="tpu_custom_call" | custom-call | flops 1000000000 | tf_op jit(solution)/shard_map/pallas_call | solution.py:566
  26.2 0.0 collective-permute-done.11.refs_9_
  26.2 0.9 %shard_map.146 = (f32[48,128]{1,0:T(8,128)S(1)}, bf16[8,32,128]{2,1,0:T(8,128)(2,1)S(1)}, f32[8,16,128]{2,1,0:T(8,128)S(1)}) custom-call(s32[1]{0:T(128)} %bitcast.1.pos_ref, s32[1]{0:T(128)} %bitcast.lev_ref, f32[16,128]{1,0:T(8,128)S(1)} %get-tuple-element.43.mix_ref, f32[32,128]{1,0:T(8,128)S(1)} %get-tuple-element.52.total_ref.refs_0_, ...), custom_call_target="tpu_custom_call" | custom-call | flops 1000000000 | tf_op jit(solution)/shard_map/pallas_call | solution.py:577
  27.1 0.2 collective-permute-start.12
  27.3 0.4 %shard_map.147.own_ref = f32[16,40,256]{2,1,0:T(8,128)S(1)} custom-call(bf16[16,40,256]{2,1,0:T(8,128)(2,1)S(1)} %copy-done.1, f32[48,128]{1,0:T(8,128)S(1)} %get-tuple-element.69.mine_ref, bf16[2,128,128]{2,1,0:T(8,128)(2,1)S(1)} %get-tuple-element.70.weights_ref, f32[16,40,256]{2,1,0:T(8,128)S(1)} %copy-done), custom_call_target="tpu_custom_call" | custom-call | tf_op jit(solution)/shard_map/pallas_call | solution.py:606
  27.7 0.3 %shard_map.148 = (f32[16,1024]{1,0:T(8,128)S(1)}, f32[16,1024]{1,0:T(8,128)S(1)}) custom-call(s32[1]{0:T(128)} %bitcast.1.pos_ref, s32[1]{0:T(128)} %bitcast.lev_ref, bf16[8,32,512]{2,1,0:T(8,128)(2,1)S(1)} %get-tuple-element.63.refs_9_.refs_10_.refs_0_, bf16[8,32,384]{2,1,0:T(8,128)(2,1)S(1)} %get-tuple-element.66.refs_11_.refs_1_, ...), custom_call_target="tpu_custom_call" | custom-call | tf_op jit(solution)/shard_map/pallas_call | solution.py:584
  28.1 0.2 collective-permute-done.12.theirs_ref
  28.3 1.3 %shard_map.149 = (f32[16,40,256]{2,1,0:T(8,128)}, f32[16,1024]{1,0:T(8,128)}, f32[16,1024]{1,0:T(8,128)}) custom-call(bf16[16,40,256]{2,1,0:T(8,128)(2,1)S(1)} %collective-permute-done.1.perturb_ref, f32[48,128]{1,0:T(8,128)S(1)} %collective-permute-done.12.theirs_ref, f32[16,40,256]{2,1,0:T(8,128)S(1)} %shard_map.147.own_ref, ...), custom_call_target="tpu_custom_call" | custom-call | tf_op jit(solution)/shard_map/pallas_call | solution.py:607
  (13 shorter events, 0.1 us)
Async XLA Ops:
  0.6 2.5 %collective-permute-start = (f32[16,40,256]{2,1,0:T(8,128)}, f32[16,40,256]{2,1,0:T(8,128)S(1)}, u32[]{:S(2)}, u32[]{:S(2)}) collective-permute-start(f32[16,40,256]{2,1,0:T(8,128)} %control_ref.3), channel_id=1, source_target_pairs={{0,1},{1,0},{2,3},{3,2},{4,5},{5,4},{6,7},{7,6},{8,9},{9,8},{10,11... | collective-permute-start | bytes 1966088 | tf_op jit(solution)/shard_map/ppermute | solution.py:510
  1.1 2.5 %collective-permute-start.1 = (bf16[16,40,256]{2,1,0:T(8,128)(2,1)}, bf16[16,40,256]{2,1,0:T(8,128)(2,1)S(1)}, u32[]{:S(2)}, u32[]{:S(2)}) collective-permute-start(bf16[16,40,256]{2,1,0:T(8,128)(2,1)} %perturb_ref.3), channel_id=1, source_target_pairs={{0,1},{1,0},{2,3},{3,2},{4,5},{5,4},{6,7},{7,6},{8,9},{9,8},{10,11... | collective-permute-start | bytes 983048 | tf_op jit(solution)/shard_map/ppermute | solution.py:529
  1.2 0.7 %copy-start.11 = (f32[16,32]{1,0:T(8,128)S(1)}, f32[16,32]{1,0:T(8,128)}, u32[]{:S(2)}) copy-start(f32[16,32]{1,0:T(8,128)} %loc_ref.1) | copy-start | bytes 6148
  1.9 1.2 %copy-start = (f32[16,40,256]{2,1,0:T(8,128)S(1)}, f32[16,40,256]{2,1,0:T(8,128)}, u32[]{:S(2)}) copy-start(f32[16,40,256]{2,1,0:T(8,128)} %control_ref.3) | copy-start | bytes 1966084
  1.9 1.2 %copy-start.1 = (bf16[16,40,256]{2,1,0:T(8,128)(2,1)S(1)}, bf16[16,40,256]{2,1,0:T(8,128)(2,1)}, u32[]{:S(2)}) copy-start(bf16[16,40,256]{2,1,0:T(8,128)(2,1)} %perturb_ref.3) | copy-start | bytes 983044
  3.1 3.5 %copy-start.2 = (f32[16,1024]{1,0:T(8,128)S(1)}, f32[16,1024]{1,0:T(8,128)}, u32[]{:S(2)}) copy-start(f32[16,1024]{1,0:T(8,128)} %refs_5_.1) | copy-start | bytes 196612
  3.1 3.5 %copy-start.3 = (f32[16,1024]{1,0:T(8,128)S(1)}, f32[16,1024]{1,0:T(8,128)}, u32[]{:S(2)}) copy-start(f32[16,1024]{1,0:T(8,128)} %refs_8_.1) | copy-start | bytes 196612
  3.1 3.5 %copy-start.4 = (f32[16,1024]{1,0:T(8,128)S(1)}, f32[16,1024]{1,0:T(8,128)}, u32[]{:S(2)}) copy-start(f32[16,1024]{1,0:T(8,128)} %refs_9_.1) | copy-start | bytes 196612
  3.1 3.5 %copy-start.7 = (s32[1,8,128]{2,1,0:T(8,128)S(1)}, s32[1,8,128]{2,1,0:T(8,128)}, u32[]{:S(2)}) copy-start(s32[1,8,128]{2,1,0:T(8,128)} %src_ref.1) | copy-start | bytes 12292
  3.1 3.5 %copy-start.8 = (f32[1,8,128]{2,1,0:T(8,128)S(1)}, f32[1,8,128]{2,1,0:T(8,128)}, u32[]{:S(2)}) copy-start(f32[1,8,128]{2,1,0:T(8,128)} %weight_ref.1) | copy-start | bytes 12292
  3.1 3.5 %copy-start.9 = (s32[1,8,128]{2,1,0:T(8,128)S(1)}, s32[1,8,128]{2,1,0:T(8,128)}, u32[]{:S(2)}) copy-start(s32[1,8,128]{2,1,0:T(8,128)} %tgt_ref.1) | copy-start | bytes 12292
  3.7 4.8 %collective-permute-start.2 = (f32[16,256]{1,0:T(8,128)S(1)}, f32[16,256]{1,0:T(8,128)S(1)}, u32[]{:S(2)}, u32[]{:S(2)}) collective-permute-start(f32[16,256]{1,0:T(8,128)S(1)} %shard_map.140.refs_0_), channel_id=1, source_target_pairs={{0,16},{16,0},{1,17},{17,1},{2,18},{18,2},{3,19},{19,3},{4,20},{20... | collective-permute-start | bytes 49160 | tf_op jit(solution)/shard_map/ppermute | solution.py:531
  6.6 0.7 %copy-start.6 = (f32[1024]{0:T(1024)S(1)}, f32[1024]{0:T(1024)}, u32[]{:S(2)}) copy-start(f32[1024]{0:T(1024)} %param.17) | copy-start | bytes 12292
  6.6 0.7 %copy-start.5 = (f32[1024]{0:T(1024)S(1)}, f32[1024]{0:T(1024)}, u32[]{:S(2)}) copy-start(f32[1024]{0:T(1024)} %param.16) | copy-start | bytes 12292
  6.6 0.7 %copy-start.10 = (s32[1,8]{1,0:T(1,128)S(1)}, s32[1,8]{1,0:T(1,128)}, u32[]{:S(2)}) copy-start(s32[1,8]{1,0:T(1,128)} %counts_ref.1) | copy-start | bytes 100
  8.5 3.4 %collective-permute-start.6 = (f32[72,128]{1,0:T(8,128)S(1)}, f32[72,128]{1,0:T(8,128)S(1)}, u32[]{:S(2)}, u32[]{:S(2)}) collective-permute-start(f32[72,128]{1,0:T(8,128)S(1)} %get-tuple-element.59), channel_id=1, source_target_pairs={{0,1},{2,3},{4,5},{6,7},{8,9},{10,11},{12,13},{14,15},{16,17},{18,... | collective-permute-start | bytes 110600 | tf_op jit(solution)/shard_map/ppermute | solution.py:543
  10.2 5.9 %collective-permute-start.3 = (f32[88,128]{1,0:T(8,128)S(1)}, f32[88,128]{1,0:T(8,128)S(1)}, u32[]{:S(2)}, u32[]{:S(2)}) collective-permute-start(f32[88,128]{1,0:T(8,128)S(1)} %get-tuple-element.54), channel_id=1, source_target_pairs={{0,4},{1,9},{2,6},{3,11},{4,0},{5,13},{6,2},{7,15},{8,12},{9,1},{1... | collective-permute-start | bytes 135176 | tf_op jit(solution)/shard_map/ppermute | solution.py:555
  11.9 10.2 %collective-permute-start.7 = (f32[160,128]{1,0:T(8,128)S(1)}, f32[160,128]{1,0:T(8,128)S(1)}, u32[]{:S(2)}, u32[]{:S(2)}) collective-permute-start(f32[160,128]{1,0:T(8,128)S(1)} %shard_map.143), channel_id=1, source_target_pairs={{1,15},{3,13},{5,11},{7,9},{9,7},{11,5},{13,3},{15,1},{17,31},{19,... | collective-permute-start | bytes 245768 | tf_op jit(solution)/shard_map/ppermute | solution.py:555
  12.5 8.0 %collective-permute-start.4 = (f32[88,128]{1,0:T(8,128)S(1)}, f32[88,128]{1,0:T(8,128)S(1)}, u32[]{:S(2)}, u32[]{:S(2)}) collective-permute-start(f32[88,128]{1,0:T(8,128)S(1)} %get-tuple-element.57), channel_id=1, source_target_pairs={{0,10},{1,7},{2,8},{3,5},{4,14},{5,3},{6,12},{7,1},{8,2},{9,15},{1... | collective-permute-start | bytes 135176 | tf_op jit(solution)/shard_map/ppermute | solution.py:555
  16.2 7.2 %collective-permute-start.5 = (f32[88,128]{1,0:T(8,128)S(1)}, f32[88,128]{1,0:T(8,128)S(1)}, u32[]{:S(2)}, u32[]{:S(2)}) collective-permute-start(f32[88,128]{1,0:T(8,128)S(1)} %get-tuple-element.58), channel_id=1, source_target_pairs={{0,12},{1,13},{2,14},{3,15},{4,8},{5,9},{6,10},{7,11},{8,4},{9,5},... | collective-permute-start | bytes 135176 | tf_op jit(solution)/shard_map/ppermute | solution.py:555
  18.1 6.1 %collective-permute-start.9 = (f32[88,128]{1,0:T(8,128)S(1)}, f32[88,128]{1,0:T(8,128)S(1)}, u32[]{:S(2)}, u32[]{:S(2)}) collective-permute-start(f32[88,128]{1,0:T(8,128)S(1)} %get-tuple-element.60), channel_id=1, source_target_pairs={{0,6},{1,11},{2,4},{3,9},{4,2},{5,15},{6,0},{7,13},{8,14},{9,3},{1... | collective-permute-start | bytes 135176 | tf_op jit(solution)/shard_map/ppermute | solution.py:555
  18.4 6.0 %collective-permute-start.10 = (f32[88,128]{1,0:T(8,128)S(1)}, f32[88,128]{1,0:T(8,128)S(1)}, u32[]{:S(2)}, u32[]{:S(2)}) collective-permute-start(f32[88,128]{1,0:T(8,128)S(1)} %get-tuple-element.61), channel_id=1, source_target_pairs={{0,8},{1,5},{2,10},{3,7},{4,12},{5,1},{6,14},{7,3},{8,0},{9,13},{1... | collective-permute-start | bytes 135176 | tf_op jit(solution)/shard_map/ppermute | solution.py:555
  20.5 5.7 %collective-permute-start.11 = (f32[88,128]{1,0:T(8,128)S(1)}, f32[88,128]{1,0:T(8,128)S(1)}, u32[]{:S(2)}, u32[]{:S(2)}) collective-permute-start(f32[88,128]{1,0:T(8,128)S(1)} %get-tuple-element.62), channel_id=1, source_target_pairs={{0,2},{1,3},{2,0},{3,1},{4,6},{5,7},{6,4},{7,5},{8,10},{9,11},{10,... | collective-permute-start | bytes 135176 | tf_op jit(solution)/shard_map/ppermute | solution.py:555
  22.0 3.2 %collective-permute-start.8 = (f32[160,128]{1,0:T(8,128)S(1)}, f32[160,128]{1,0:T(8,128)S(1)}, u32[]{:S(2)}, u32[]{:S(2)}) collective-permute-start(f32[160,128]{1,0:T(8,128)S(1)} %collective-permute-done.7.refs_5_), channel_id=1, source_target_pairs={{1,0},{3,2},{5,4},{7,6},{9,8},{11,10},{13,12},{15,14},{17,16},{19,... | collective-permute-start | bytes 245768 | tf_op jit(solution)/shard_map/ppermute | solution.py:556
  27.1 1.2 %collective-permute-start.12 = (f32[48,128]{1,0:T(8,128)S(1)}, f32[48,128]{1,0:T(8,128)S(1)}, u32[]{:S(2)}, u32[]{:S(2)}) collective-permute-start(f32[48,128]{1,0:T(8,128)S(1)} %get-tuple-element.69.mine_ref), channel_id=1, source_target_pairs={{0,1},{1,0},{2,3},{3,2},{4,5},{5,4},{6,7},{7,6},{8,9},{9,8},{10,11... | collective-permute-start | bytes 73736 | tf_op jit(solution)/shard_map/ppermute | solution.py:605

commit v16 on v15

--- a/solution.py
+++ b/solution.py
@@ -540,7 +540,7 @@
             + [shape((stacked + 2 * levels + EXTRA, cap), F32)],
             [VMEM] * (groups + n - 1),
         )(*sums, *[rests[r] for r in direct], rests[n - 1])
-        given = lax.ppermute(give, "lev", [(0, 1)])
+        given = lax.ppermute(give, "lev", swap)
         pair = call(
             functools.partial(pair_kernel, levels),
             shape((2 * stacked + rows.total + 2 * levels + EXTRA, cap), F32),
@@ -551,9 +551,9 @@
         for k, r in enumerate(order):
             if k == 3:
                 arrived[order[0]][0], blocks[r] = lax.optimization_barrier((arrived[order[0]][0], blocks[r]))
-            pairs = [(i * 2 + v, (i ^ relabel(r, n, v)) * 2 + v) for i in range(n) for v in range(2) if v or r < n - 1]
+            pairs = [(i * 2 + v, (i ^ (relabel(r, n, v) * (v or r < n - 1))) * 2 + v) for i in range(n) for v in range(2)]
             arrived[r] = [lax.ppermute(blocks[r], ("tile", "lev"), pairs)]
-        arrived[n - 1].append(lax.ppermute(arrived[n - 1][0], "lev", [(1, 0)]))
+        arrived[n - 1].append(lax.ppermute(arrived[n - 1][0], "lev", swap))
         slots, carried, picks = [], [], []
         for count in range(1, len(stages)):
             labels = sum(stages[:count], [])

time: 29.9 us -> 28.1 us (0.940)
  waiting for transfers between devices: 2.14 us -> 1.05 us
  starting transfers between devices: 18.5 us -> 18 us
    ppermute x2, starting transfers between devices: 3 us -> 1.26 us  [the longest x1 1.19 us: body(): arrived[n - 1].append(lax.ppermute(arrived[n - 1][0], 'lev', swap))]
    ppermute x1, starting transfers between devices: 0.21 us -> 0.95 us  [body(): theirs = lax.ppermute(mine, 'lev', swap)]
    ppermute x2, waiting for transfers between devices: 0.73 us -> 0.02 us  [the longest x1 0.01 us: body(): arrived[n - 1].append(lax.ppermute(arrived[n - 1][0], 'lev', swap))]
    ppermute x7, starting transfers between devices: 11.8 us -> 12.2 us  [body(): arrived[r] = [lax.ppermute(blocks[r], ('tile', 'lev'), pairs)]]
  transfers between devices with their start and end apart: 13 -> 13, of which waited for: 4 -> 2; matrix products, arithmetic and copies ran while one was open for 0% -> 0% of each run, Pallas kernels for 15% -> 16%
where the time goes in v16:
time: 28.1 us; the launch traced here: 27.9 us
  starting transfers between devices  18 us (64%)
  Pallas kernels  6.67 us (24%)
  local copies, waits for them, and re-layouts  1.39 us (5%)
  waiting for transfers between devices  1.05 us (4%)
  between operations  0.81 us (3%)
    ppermute x7, starting transfers between devices, body(): arrived[r] = [lax.ppermute(blocks[r], ('tile', 'lev'), pairs)]  12.2 us
    ppermute x1, starting transfers between devices, body(): lax.ppermute(sums[0], 'grp', [(g, (g + k) % groups) for g in range(groups)])  2.97 us
    pallas_call x2, Pallas kernels, body(): call(functools.partial(stage_kernel, n, levels, band_cols, tile_cols, sta...  1.94 us
    unnamed x24, local copies, waits for them, and re-layouts  1.39 us
    pallas_call x1, Pallas kernels, body(): call(ens_kernel, (shape(control.shape, F32), flat, flat), [VMEM] * 5, [pl...  1.24 us
    ppermute x1, starting transfers between devices, body(): arrived[n - 1].append(lax.ppermute(arrived[n - 1][0], 'lev', swap))  1.19 us
    pallas_call x1, Pallas kernels, body(): call(functools.partial(static_kernel, band_cols), [shape((rows.total, cap...  1.1 us
    ppermute x1, starting transfers between devices, body(): theirs = lax.ppermute(mine, 'lev', swap)  0.95 us
  transfers between devices with their start and end apart: 13, of which 2 were waited for; matrix products, arithmetic and copies ran while one was open for 0% of the time, Pallas kernels for 16%

profile of v16, /device:TPU:0, one launch (start us, length us, event | category | flops | bytes accessed | tf_op | source)
XLA Modules:
  0.0 27.9 jit_solution(14324497412095040033)
XLA Ops:
  0.6 0.5 %collective-permute-start = (f32[16,40,256]{2,1,0:T(8,128)}, f32[16,40,256]{2,1,0:T(8,128)S(1)}, u32[]{:S(2)}, u32[]{:S(2)}) collective-permute-start(f32[16,40,256]{2,1,0:T(8,128)} %control_ref.3), channel_id=1, source_target_pairs={{0,1},{1,0},{2,3},{3,2},{4,5},{5,4},{6,7},{7,6},{8,9},{9,8},{10,11... | collective-permute-start | bytes 1966088 | tf_op jit(solution)/shard_map/ppermute | solution.py:510
  1.1 0.1 collective-permute-start.1
  1.2 0.7 %copy-done.11 = f32[16,32]{1,0:T(8,128)S(1)} copy-done((f32[16,32]{1,0:T(8,128)S(1)}, f32[16,32]{1,0:T(8,128)}, u32[]{:S(2)}) %copy-start.11) | copy-done | bytes 2072
  1.9 0.2 shard_map.139
  2.2 0.9 %collective-permute-done.other_ref = f32[16,40,256]{2,1,0:T(8,128)S(1)} collective-permute-done((f32[16,40,256]{2,1,0:T(8,128)}, f32[16,40,256]{2,1,0:T(8,128)S(1)}, u32[]{:S(2)}, u32[]{:S(2)}) %collective-permute-start) | collective-permute-done | bytes 655392 | tf_op jit(solution)/shard_map/ppermute | solution.py:510
  3.1 0.0 copy-done
  3.1 0.0 copy-done.1
  3.1 0.0 copy-start.7
  3.1 0.0 copy-start.8
  3.1 0.0 copy-start.9
  3.1 0.5 %shard_map.140.refs_0_ = f32[16,256]{1,0:T(8,128)S(1)} custom-call(bf16[16,40,256]{2,1,0:T(8,128)(2,1)S(1)} %copy-done.1, f32[16,40,256]{2,1,0:T(8,128)S(1)} %copy-done, f32[16,40,256]{2,1,0:T(8,128)S(1)} %collective-permute-done.other_ref, bf16[2,128,256]{2,1,0:T(8,128)(2,1)S(1)} %get-tuple-element.41.mix_ref), custom_call_target="tpu_custom_call" | custom-call | tf_op jit(solution)/shard_map/pallas_call | solution.py:518
  3.6 0.0 collective-permute-done.1.perturb_ref
  3.7 3.0 %collective-permute-start.2 = (f32[16,256]{1,0:T(8,128)S(1)}, f32[16,256]{1,0:T(8,128)S(1)}, u32[]{:S(2)}, u32[]{:S(2)}) collective-permute-start(f32[16,256]{1,0:T(8,128)S(1)} %shard_map.140.refs_0_), channel_id=1, source_target_pairs={{0,16},{16,0},{1,17},{17,1},{2,18},{18,2},{3,19},{19,3},{4,20},{20... | collective-permute-start | bytes 49160 | tf_op jit(solution)/shard_map/ppermute | solution.py:531
  6.6 0.0 copy-done.2
  6.6 0.0 copy-done.3
  6.6 0.0 copy-done.4
  6.7 0.0 copy-done.7
  6.7 0.0 copy-done.8
  6.7 0.6 %copy-done.6 = f32[1024]{0:T(1024)S(1)} copy-done((f32[1024]{0:T(1024)S(1)}, f32[1024]{0:T(1024)}, u32[]{:S(2)}) %copy-start.6) | copy-done | bytes 4120
  7.3 0.0 copy-done.5
  7.3 1.1 %shard_map.141 = (f32[56,128]{1,0:T(8,128)S(1)}, f32[56,128]{1,0:T(8,128)S(1)}, f32[56,128]{1,0:T(8,128)S(1)}, f32[56,128]{1,0:T(8,128)S(1)}, f32[56,128]{1,0:T(...) custom-call(s32[1]{0:T(128)} %bitcast.1.pos_ref, s32[1]{0:T(128)} %bitcast.lev_ref, ...), custom_call_target="tpu_custom_call" | custom-call | tf_op jit(solution)/shard_map/pallas_call | solution.py:525
  8.4 0.0 collective-permute-done.2.refs_1_
  8.5 0.1 collective-permute-start.6
  8.6 2.1 %collective-permute-start.3 = (f32[88,128]{1,0:T(8,128)S(1)}, f32[88,128]{1,0:T(8,128)S(1)}, u32[]{:S(2)}, u32[]{:S(2)}) collective-permute-start(f32[88,128]{1,0:T(8,128)S(1)} %get-tuple-element.54), channel_id=1, source_target_pairs={{0,4},{1,9},{2,6},{3,11},{4,0},{5,13},{6,2},{7,15},{8,12},{9,1},{1... | collective-permute-start | bytes 135176 | tf_op jit(solution)/shard_map/ppermute | solution.py:555
  10.6 0.0 collective-permute-done.6.given_ref
  10.6 0.7 %collective-permute-start.7 = (f32[160,128]{1,0:T(8,128)S(1)}, f32[160,128]{1,0:T(8,128)S(1)}, u32[]{:S(2)}, u32[]{:S(2)}) collective-permute-start(f32[160,128]{1,0:T(8,128)S(1)} %shard_map.143), channel_id=1, source_target_pairs={{0,0},{1,15},{2,2},{3,13},{4,4},{5,11},{6,6},{7,9},{8,8},{9,7},{10... | collective-permute-start | bytes 245768 | tf_op jit(solution)/shard_map/ppermute | solution.py:555
  11.3 3.6 %collective-permute-start.4 = (f32[88,128]{1,0:T(8,128)S(1)}, f32[88,128]{1,0:T(8,128)S(1)}, u32[]{:S(2)}, u32[]{:S(2)}) collective-permute-start(f32[88,128]{1,0:T(8,128)S(1)} %get-tuple-element.57), channel_id=1, source_target_pairs={{0,10},{1,7},{2,8},{3,5},{4,14},{5,3},{6,12},{7,1},{8,2},{9,15},{1... | collective-permute-start | bytes 135176 | tf_op jit(solution)/shard_map/ppermute | solution.py:555
  14.9 0.0 collective-permute-done.3.refs_2_
  14.9 1.8 %collective-permute-start.5 = (f32[88,128]{1,0:T(8,128)S(1)}, f32[88,128]{1,0:T(8,128)S(1)}, u32[]{:S(2)}, u32[]{:S(2)}) collective-permute-start(f32[88,128]{1,0:T(8,128)S(1)} %get-tuple-element.58), channel_id=1, source_target_pairs={{0,12},{1,13},{2,14},{3,15},{4,8},{5,9},{6,10},{7,11},{8,4},{9,5},... | collective-permute-start | bytes 135176 | tf_op jit(solution)/shard_map/ppermute | solution.py:555
  16.7 0.5 %collective-permute-start.9 = (f32[88,128]{1,0:T(8,128)S(1)}, f32[88,128]{1,0:T(8,128)S(1)}, u32[]{:S(2)}, u32[]{:S(2)}) collective-permute-start(f32[88,128]{1,0:T(8,128)S(1)} %get-tuple-element.60), channel_id=1, source_target_pairs={{0,6},{1,11},{2,4},{3,9},{4,2},{5,15},{6,0},{7,13},{8,14},{9,3},{1... | collective-permute-start | bytes 135176 | tf_op jit(solution)/shard_map/ppermute | solution.py:555
  17.2 2.1 %collective-permute-start.10 = (f32[88,128]{1,0:T(8,128)S(1)}, f32[88,128]{1,0:T(8,128)S(1)}, u32[]{:S(2)}, u32[]{:S(2)}) collective-permute-start(f32[88,128]{1,0:T(8,128)S(1)} %get-tuple-element.61), channel_id=1, source_target_pairs={{0,8},{1,5},{2,10},{3,7},{4,12},{5,1},{6,14},{7,3},{8,0},{9,13},{1... | collective-permute-start | bytes 135176 | tf_op jit(solution)/shard_map/ppermute | solution.py:555
  19.3 0.0 collective-permute-done.4.refs_3_
  19.3 1.5 %collective-permute-start.11 = (f32[88,128]{1,0:T(8,128)S(1)}, f32[88,128]{1,0:T(8,128)S(1)}, u32[]{:S(2)}, u32[]{:S(2)}) collective-permute-start(f32[88,128]{1,0:T(8,128)S(1)} %get-tuple-element.62), channel_id=1, source_target_pairs={{0,2},{1,3},{2,0},{3,1},{4,6},{5,7},{6,4},{7,5},{8,10},{9,11},{10,... | collective-permute-start | bytes 135176 | tf_op jit(solution)/shard_map/ppermute | solution.py:555
  20.8 0.0 collective-permute-done.7.refs_5_
  20.8 1.2 %collective-permute-start.8 = (f32[160,128]{1,0:T(8,128)S(1)}, f32[160,128]{1,0:T(8,128)S(1)}, u32[]{:S(2)}, u32[]{:S(2)}) collective-permute-start(f32[160,128]{1,0:T(8,128)S(1)} %collective-permute-done.7.refs_5_), channel_id=1, source_target_pairs={{0,1},{1,0},{2,3},{3,2},{4,5},{5,4},{6,7},{7,6},{8,9},{9,8},{10,11... | collective-permute-start | bytes 245768 | tf_op jit(solution)/shard_map/ppermute | solution.py:556
  22.0 0.0 collective-permute-done.5.refs_4_
  22.0 0.9 %shard_map.144 = (bf16[8,32,512]{2,1,0:T(8,128)(2,1)S(1)}, f32[4,16,128]{2,1,0:T(8,128)S(1)}, f32[16,1024]{1,0:T(8,128)S(1)}, bf16[8,256,128]{2,1,0:T(8,128)(2,1)S(1)}) custom-call(s32[1]{0:T(128)} %bitcast.lev_ref, f32[32,128]{1,0:T(8,128)S(1)} %get-tuple-element.52.total_ref.refs_0_, f32[56,128]{1,0:T(8,128)S(1)} %get-tuple-element.53.refs_1_, ...), custom_call_target="tpu_custom_call" | custom-call | flops 1000000000 | tf_op jit(solution)/shard_map/pallas_call | solution.py:566
  22.9 0.0 collective-permute-done.9.refs_7_
  22.9 0.0 collective-permute-done.10.refs_8_
  22.9 0.0 collective-permute-done.8.refs_6_
  22.9 1.1 %shard_map.145 = (bf16[8,32,384]{2,1,0:T(8,128)(2,1)S(1)}, f32[7,16,128]{2,1,0:T(8,128)S(1)}, f32[16,1024]{1,0:T(8,128)S(1)}) custom-call(s32[1]{0:T(128)} %bitcast.lev_ref, f32[32,128]{1,0:T(8,128)S(1)} %get-tuple-element.52.total_ref.refs_0_, f32[56,128]{1,0:T(8,128)S(1)} %get-tuple-element.53.refs_1_, f32[88,128]{1,0:T(8,128)S(1)} %collective-permute-done.3.refs_2_, ...), custom_call_target="tpu_custom_call" | custom-call | flops 1000000000 | tf_op jit(solution)/shard_map/pallas_call | solution.py:566
  23.9 0.0 collective-permute-done.11.refs_9_
  23.9 0.9 %shard_map.146 = (f32[48,128]{1,0:T(8,128)S(1)}, bf16[8,32,128]{2,1,0:T(8,128)(2,1)S(1)}, f32[8,16,128]{2,1,0:T(8,128)S(1)}) custom-call(s32[1]{0:T(128)} %bitcast.1.pos_ref, s32[1]{0:T(128)} %bitcast.lev_ref, f32[16,128]{1,0:T(8,128)S(1)} %get-tuple-element.43.mix_ref, f32[32,128]{1,0:T(8,128)S(1)} %get-tuple-element.52.total_ref.refs_0_, ...), custom_call_target="tpu_custom_call" | custom-call | flops 1000000000 | tf_op jit(solution)/shard_map/pallas_call | solution.py:577
  24.8 0.9 %collective-permute-start.12 = (f32[48,128]{1,0:T(8,128)S(1)}, f32[48,128]{1,0:T(8,128)S(1)}, u32[]{:S(2)}, u32[]{:S(2)}) collective-permute-start(f32[48,128]{1,0:T(8,128)S(1)} %get-tuple-element.69.mine_ref), channel_id=1, source_target_pairs={{0,1},{1,0},{2,3},{3,2},{4,5},{5,4},{6,7},{7,6},{8,9},{9,8},{10,11... | collective-permute-start | bytes 73736 | tf_op jit(solution)/shard_map/ppermute | solution.py:605
  25.8 0.4 %shard_map.147.own_ref = f32[16,40,256]{2,1,0:T(8,128)S(1)} custom-call(bf16[16,40,256]{2,1,0:T(8,128)(2,1)S(1)} %copy-done.1, f32[48,128]{1,0:T(8,128)S(1)} %get-tuple-element.69.mine_ref, bf16[2,128,128]{2,1,0:T(8,128)(2,1)S(1)} %get-tuple-element.70.weights_ref, f32[16,40,256]{2,1,0:T(8,128)S(1)} %copy-done), custom_call_target="tpu_custom_call" | custom-call | tf_op jit(solution)/shard_map/pallas_call | solution.py:606
  26.2 0.3 %shard_map.148 = (f32[16,1024]{1,0:T(8,128)S(1)}, f32[16,1024]{1,0:T(8,128)S(1)}) custom-call(s32[1]{0:T(128)} %bitcast.1.pos_ref, s32[1]{0:T(128)} %bitcast.lev_ref, bf16[8,32,512]{2,1,0:T(8,128)(2,1)S(1)} %get-tuple-element.63.refs_9_.refs_10_.refs_0_, bf16[8,32,384]{2,1,0:T(8,128)(2,1)S(1)} %get-tuple-element.66.refs_11_.refs_1_, ...), custom_call_target="tpu_custom_call" | custom-call | tf_op jit(solution)/shard_map/pallas_call | solution.py:584
  26.5 0.1 collective-permute-done.12.theirs_ref
  26.6 1.2 %shard_map.149 = (f32[16,40,256]{2,1,0:T(8,128)}, f32[16,1024]{1,0:T(8,128)}, f32[16,1024]{1,0:T(8,128)}) custom-call(bf16[16,40,256]{2,1,0:T(8,128)(2,1)S(1)} %collective-permute-done.1.perturb_ref, f32[48,128]{1,0:T(8,128)S(1)} %collective-permute-done.12.theirs_ref, f32[16,40,256]{2,1,0:T(8,128)S(1)} %shard_map.147.own_ref, ...), custom_call_target="tpu_custom_call" | custom-call | tf_op jit(solution)/shard_map/pallas_call | solution.py:607
  (13 shorter events, 0.1 us)
Async XLA Ops:
  0.6 2.5 %collective-permute-start = (f32[16,40,256]{2,1,0:T(8,128)}, f32[16,40,256]{2,1,0:T(8,128)S(1)}, u32[]{:S(2)}, u32[]{:S(2)}) collective-permute-start(f32[16,40,256]{2,1,0:T(8,128)} %control_ref.3), channel_id=1, source_target_pairs={{0,1},{1,0},{2,3},{3,2},{4,5},{5,4},{6,7},{7,6},{8,9},{9,8},{10,11... | collective-permute-start | bytes 1966088 | tf_op jit(solution)/shard_map/ppermute | solution.py:510
  1.1 2.5 %collective-permute-start.1 = (bf16[16,40,256]{2,1,0:T(8,128)(2,1)}, bf16[16,40,256]{2,1,0:T(8,128)(2,1)S(1)}, u32[]{:S(2)}, u32[]{:S(2)}) collective-permute-start(bf16[16,40,256]{2,1,0:T(8,128)(2,1)} %perturb_ref.3), channel_id=1, source_target_pairs={{0,1},{1,0},{2,3},{3,2},{4,5},{5,4},{6,7},{7,6},{8,9},{9,8},{10,11... | collective-permute-start | bytes 983048 | tf_op jit(solution)/shard_map/ppermute | solution.py:529
  1.2 0.7 %copy-start.11 = (f32[16,32]{1,0:T(8,128)S(1)}, f32[16,32]{1,0:T(8,128)}, u32[]{:S(2)}) copy-start(f32[16,32]{1,0:T(8,128)} %loc_ref.1) | copy-start | bytes 6148
  1.9 1.2 %copy-start = (f32[16,40,256]{2,1,0:T(8,128)S(1)}, f32[16,40,256]{2,1,0:T(8,128)}, u32[]{:S(2)}) copy-start(f32[16,40,256]{2,1,0:T(8,128)} %control_ref.3) | copy-start | bytes 1966084
  1.9 1.2 %copy-start.1 = (bf16[16,40,256]{2,1,0:T(8,128)(2,1)S(1)}, bf16[16,40,256]{2,1,0:T(8,128)(2,1)}, u32[]{:S(2)}) copy-start(bf16[16,40,256]{2,1,0:T(8,128)(2,1)} %perturb_ref.3) | copy-start | bytes 983044
  3.1 3.5 %copy-start.2 = (f32[16,1024]{1,0:T(8,128)S(1)}, f32[16,1024]{1,0:T(8,128)}, u32[]{:S(2)}) copy-start(f32[16,1024]{1,0:T(8,128)} %refs_5_.1) | copy-start | bytes 196612
  3.1 3.5 %copy-start.3 = (f32[16,1024]{1,0:T(8,128)S(1)}, f32[16,1024]{1,0:T(8,128)}, u32[]{:S(2)}) copy-start(f32[16,1024]{1,0:T(8,128)} %refs_8_.1) | copy-start | bytes 196612
  3.1 3.5 %copy-start.4 = (f32[16,1024]{1,0:T(8,128)S(1)}, f32[16,1024]{1,0:T(8,128)}, u32[]{:S(2)}) copy-start(f32[16,1024]{1,0:T(8,128)} %refs_9_.1) | copy-start | bytes 196612
  3.1 3.5 %copy-start.7 = (s32[1,8,128]{2,1,0:T(8,128)S(1)}, s32[1,8,128]{2,1,0:T(8,128)}, u32[]{:S(2)}) copy-start(s32[1,8,128]{2,1,0:T(8,128)} %src_ref.1) | copy-start | bytes 12292
  3.1 3.5 %copy-start.8 = (f32[1,8,128]{2,1,0:T(8,128)S(1)}, f32[1,8,128]{2,1,0:T(8,128)}, u32[]{:S(2)}) copy-start(f32[1,8,128]{2,1,0:T(8,128)} %weight_ref.1) | copy-start | bytes 12292
  3.1 3.5 %copy-start.9 = (s32[1,8,128]{2,1,0:T(8,128)S(1)}, s32[1,8,128]{2,1,0:T(8,128)}, u32[]{:S(2)}) copy-start(s32[1,8,128]{2,1,0:T(8,128)} %tgt_ref.1) | copy-start | bytes 12292
  3.7 4.8 %collective-permute-start.2 = (f32[16,256]{1,0:T(8,128)S(1)}, f32[16,256]{1,0:T(8,128)S(1)}, u32[]{:S(2)}, u32[]{:S(2)}) collective-permute-start(f32[16,256]{1,0:T(8,128)S(1)} %shard_map.140.refs_0_), channel_id=1, source_target_pairs={{0,16},{16,0},{1,17},{17,1},{2,18},{18,2},{3,19},{19,3},{4,20},{20... | collective-permute-start | bytes 49160 | tf_op jit(solution)/shard_map/ppermute | solution.py:531
  6.6 0.7 %copy-start.6 = (f32[1024]{0:T(1024)S(1)}, f32[1024]{0:T(1024)}, u32[]{:S(2)}) copy-start(f32[1024]{0:T(1024)} %param.17) | copy-start | bytes 12292
  6.6 0.7 %copy-start.5 = (f32[1024]{0:T(1024)S(1)}, f32[1024]{0:T(1024)}, u32[]{:S(2)}) copy-start(f32[1024]{0:T(1024)} %param.16) | copy-start | bytes 12292
  6.6 0.7 %copy-start.10 = (s32[1,8]{1,0:T(1,128)S(1)}, s32[1,8]{1,0:T(1,128)}, u32[]{:S(2)}) copy-start(s32[1,8]{1,0:T(1,128)} %counts_ref.1) | copy-start | bytes 100
  8.5 2.1 %collective-permute-start.6 = (f32[72,128]{1,0:T(8,128)S(1)}, f32[72,128]{1,0:T(8,128)S(1)}, u32[]{:S(2)}, u32[]{:S(2)}) collective-permute-start(f32[72,128]{1,0:T(8,128)S(1)} %get-tuple-element.59), channel_id=1, source_target_pairs={{0,1},{1,0},{2,3},{3,2},{4,5},{5,4},{6,7},{7,6},{8,9},{9,8},{10,11... | collective-permute-start | bytes 110600 | tf_op jit(solution)/shard_map/ppermute | solution.py:543
  8.6 6.4 %collective-permute-start.3 = (f32[88,128]{1,0:T(8,128)S(1)}, f32[88,128]{1,0:T(8,128)S(1)}, u32[]{:S(2)}, u32[]{:S(2)}) collective-permute-start(f32[88,128]{1,0:T(8,128)S(1)} %get-tuple-element.54), channel_id=1, source_target_pairs={{0,4},{1,9},{2,6},{3,11},{4,0},{5,13},{6,2},{7,15},{8,12},{9,1},{1... | collective-permute-start | bytes 135176 | tf_op jit(solution)/shard_map/ppermute | solution.py:555
  10.6 10.1 %collective-permute-start.7 = (f32[160,128]{1,0:T(8,128)S(1)}, f32[160,128]{1,0:T(8,128)S(1)}, u32[]{:S(2)}, u32[]{:S(2)}) collective-permute-start(f32[160,128]{1,0:T(8,128)S(1)} %shard_map.143), channel_id=1, source_target_pairs={{0,0},{1,15},{2,2},{3,13},{4,4},{5,11},{6,6},{7,9},{8,8},{9,7},{10... | collective-permute-start | bytes 245768 | tf_op jit(solution)/shard_map/ppermute | solution.py:555
  11.3 8.0 %collective-permute-start.4 = (f32[88,128]{1,0:T(8,128)S(1)}, f32[88,128]{1,0:T(8,128)S(1)}, u32[]{:S(2)}, u32[]{:S(2)}) collective-permute-start(f32[88,128]{1,0:T(8,128)S(1)} %get-tuple-element.57), channel_id=1, source_target_pairs={{0,10},{1,7},{2,8},{3,5},{4,14},{5,3},{6,12},{7,1},{8,2},{9,15},{1... | collective-permute-start | bytes 135176 | tf_op jit(solution)/shard_map/ppermute | solution.py:555
  14.9 7.1 %collective-permute-start.5 = (f32[88,128]{1,0:T(8,128)S(1)}, f32[88,128]{1,0:T(8,128)S(1)}, u32[]{:S(2)}, u32[]{:S(2)}) collective-permute-start(f32[88,128]{1,0:T(8,128)S(1)} %get-tuple-element.58), channel_id=1, source_target_pairs={{0,12},{1,13},{2,14},{3,15},{4,8},{5,9},{6,10},{7,11},{8,4},{9,5},... | collective-permute-start | bytes 135176 | tf_op jit(solution)/shard_map/ppermute | solution.py:555
  16.7 6.2 %collective-permute-start.9 = (f32[88,128]{1,0:T(8,128)S(1)}, f32[88,128]{1,0:T(8,128)S(1)}, u32[]{:S(2)}, u32[]{:S(2)}) collective-permute-start(f32[88,128]{1,0:T(8,128)S(1)} %get-tuple-element.60), channel_id=1, source_target_pairs={{0,6},{1,11},{2,4},{3,9},{4,2},{5,15},{6,0},{7,13},{8,14},{9,3},{1... | collective-permute-start | bytes 135176 | tf_op jit(solution)/shard_map/ppermute | solution.py:555
  17.2 5.7 %collective-permute-start.10 = (f32[88,128]{1,0:T(8,128)S(1)}, f32[88,128]{1,0:T(8,128)S(1)}, u32[]{:S(2)}, u32[]{:S(2)}) collective-permute-start(f32[88,128]{1,0:T(8,128)S(1)} %get-tuple-element.61), channel_id=1, source_target_pairs={{0,8},{1,5},{2,10},{3,7},{4,12},{5,1},{6,14},{7,3},{8,0},{9,13},{1... | collective-permute-start | bytes 135176 | tf_op jit(solution)/shard_map/ppermute | solution.py:555
  19.3 4.7 %collective-permute-start.11 = (f32[88,128]{1,0:T(8,128)S(1)}, f32[88,128]{1,0:T(8,128)S(1)}, u32[]{:S(2)}, u32[]{:S(2)}) collective-permute-start(f32[88,128]{1,0:T(8,128)S(1)} %get-tuple-element.62), channel_id=1, source_target_pairs={{0,2},{1,3},{2,0},{3,1},{4,6},{5,7},{6,4},{7,5},{8,10},{9,11},{10,... | collective-permute-start | bytes 135176 | tf_op jit(solution)/shard_map/ppermute | solution.py:555
  20.8 2.1 %collective-permute-start.8 = (f32[160,128]{1,0:T(8,128)S(1)}, f32[160,128]{1,0:T(8,128)S(1)}, u32[]{:S(2)}, u32[]{:S(2)}) collective-permute-start(f32[160,128]{1,0:T(8,128)S(1)} %collective-permute-done.7.refs_5_), channel_id=1, source_target_pairs={{0,1},{1,0},{2,3},{3,2},{4,5},{5,4},{6,7},{7,6},{8,9},{9,8},{10,11... | collective-permute-start | bytes 245768 | tf_op jit(solution)/shard_map/ppermute | solution.py:556
  24.8 1.8 %collective-permute-start.12 = (f32[48,128]{1,0:T(8,128)S(1)}, f32[48,128]{1,0:T(8,128)S(1)}, u32[]{:S(2)}, u32[]{:S(2)}) collective-permute-start(f32[48,128]{1,0:T(8,128)S(1)} %get-tuple-element.69.mine_ref), channel_id=1, source_target_pairs={{0,1},{1,0},{2,3},{3,2},{4,5},{5,4},{6,7},{7,6},{8,9},{9,8},{10,11... | collective-permute-start | bytes 73736 | tf_op jit(solution)/shard_map/ppermute | solution.py:605

commit v17 on v14

--- a/solution.py
+++ b/solution.py
@@ -517,7 +517,8 @@
         low, high = n // 4, n // 2
         mixed = [r for i in reversed(range(low)) for r in (high + i, low + i)]
         order = [high + low, mixed[0], *range(high + low + 1, n), *mixed[1:], *range(1, low)]
-        stages = [[0] + order[: high - 1], order[high - 1 : n - low], order[n - low :]]
+        late = [mixed[2 * low - 2], *order[n - low :]]
+        stages = [[0] + order[: high - 1], [r for r in order[high - 1 :] if r not in late], late]
         levs = lax.axis_size("lev")
         arrived = {0: [total, rests[0]]}
         for r in sum(stages, [])[1:]:

time: 27.8 us -> 27.8 us (level)
  starting transfers between devices: 15.2 us -> 15.6 us
  waiting for transfers between devices: 3.51 us -> 3.15 us
    ppermute x7, starting transfers between devices: 11.7 us -> 12 us  [body(): arrived[r] = [lax.ppermute(blocks[r - 1], ('tile', 'lev'), pairs)]]
    pallas_call x2, Pallas kernels: 1.96 us -> 1.61 us  [body(): call(functools.partial(stage_kernel, n, levels, band_cols, tile_cols, sta...]
    ppermute x7, waiting for transfers between devices: 2.16 us -> 1.88 us  [body(): arrived[r] = [lax.ppermute(blocks[r - 1], ('tile', 'lev'), pairs)]]
  transfers between devices with their start and end apart: 11 -> 11, of which waited for: 4 -> 4; matrix products, arithmetic and copies ran while one was open for 0% -> 0% of each run, Pallas kernels for 17% -> 16%
where the time goes in v17:
time: 27.8 us; the launch traced here: 27.6 us
  starting transfers between devices  15.6 us (56%)
  Pallas kernels  6.65 us (24%)
  waiting for transfers between devices  3.15 us (11%)
  local copies, waits for them, and re-layouts  1.39 us (5%)
  between operations  0.78 us (3%)
    ppermute x7, starting transfers between devices, body(): arrived[r] = [lax.ppermute(blocks[r - 1], ('tile', 'lev'), pairs)]  12 us
    ppermute x1, starting transfers between devices, body(): lax.ppermute(sums[0], 'grp', [(g, (g + k) % groups) for g in range(groups)])  2.97 us
    ppermute x7, waiting for transfers between devices, body(): arrived[r] = [lax.ppermute(blocks[r - 1], ('tile', 'lev'), pairs)]  1.88 us
    pallas_call x2, Pallas kernels, body(): call(functools.partial(stage_kernel, n, levels, band_cols, tile_cols, sta...  1.61 us
    unnamed x24, local copies, waits for them, and re-layouts  1.39 us
    pallas_call x1, Pallas kernels, body(): call(ens_kernel, (shape(control.shape, F32), flat, flat), [VMEM] * 5, [pl...  1.25 us
    pallas_call x1, Pallas kernels, body(): call(functools.partial(static_kernel, band_cols), [shape((rows.total, cap...  1.11 us
    pallas_call x1, Pallas kernels, body(): call(functools.partial(shared_kernel, n, levels, band_cols, tile_cols, st...  1.07 us
  transfers between devices with their start and end apart: 11, of which 4 were waited for; matrix products, arithmetic and copies ran while one was open for 0% of the time, Pallas kernels for 16%

profile of v17, /device:TPU:0, one launch (start us, length us, event | category | flops | bytes accessed | tf_op | source)
XLA Modules:
  0.0 27.6 jit_solution(10279971070821860112)
XLA Ops:
  0.6 0.5 %collective-permute-start = (f32[16,40,256]{2,1,0:T(8,128)}, f32[16,40,256]{2,1,0:T(8,128)S(1)}, u32[]{:S(2)}, u32[]{:S(2)}) collective-permute-start(f32[16,40,256]{2,1,0:T(8,128)} %control_ref.3), channel_id=1, source_target_pairs={{0,1},{1,0},{2,3},{3,2},{4,5},{5,4},{6,7},{7,6},{8,9},{9,8},{10,11... | collective-permute-start | bytes 1966088 | tf_op jit(solution)/shard_map/ppermute | solution.py:490
  1.1 0.1 collective-permute-start.1
  1.2 0.0 copy-start.11
  1.2 0.7 %copy-done.11 = f32[16,32]{1,0:T(8,128)S(1)} copy-done((f32[16,32]{1,0:T(8,128)S(1)}, f32[16,32]{1,0:T(8,128)}, u32[]{:S(2)}) %copy-start.11) | copy-done | bytes 2072
  1.9 0.0 copy-start
  1.9 0.2 shard_map.139
  2.2 0.9 %collective-permute-done.other_ref = f32[16,40,256]{2,1,0:T(8,128)S(1)} collective-permute-done((f32[16,40,256]{2,1,0:T(8,128)}, f32[16,40,256]{2,1,0:T(8,128)S(1)}, u32[]{:S(2)}, u32[]{:S(2)}) %collective-permute-start) | collective-permute-done | bytes 655392 | tf_op jit(solution)/shard_map/ppermute | solution.py:490
  3.1 0.0 copy-done
  3.1 0.0 copy-done.1
  3.1 0.0 copy-start.7
  3.1 0.0 copy-start.8
  3.1 0.0 copy-start.9
  3.1 0.5 %shard_map.140.refs_0_ = f32[16,256]{1,0:T(8,128)S(1)} custom-call(bf16[16,40,256]{2,1,0:T(8,128)(2,1)S(1)} %copy-done.1, f32[16,40,256]{2,1,0:T(8,128)S(1)} %copy-done, f32[16,40,256]{2,1,0:T(8,128)S(1)} %collective-permute-done.other_ref, bf16[2,128,256]{2,1,0:T(8,128)(2,1)S(1)} %get-tuple-element.39.mix_ref), custom_call_target="tpu_custom_call" | custom-call | tf_op jit(solution)/shard_map/pallas_call | solution.py:498
  3.6 0.0 collective-permute-done.1.perturb_ref
  3.7 3.0 %collective-permute-start.2 = (f32[16,256]{1,0:T(8,128)S(1)}, f32[16,256]{1,0:T(8,128)S(1)}, u32[]{:S(2)}, u32[]{:S(2)}) collective-permute-start(f32[16,256]{1,0:T(8,128)S(1)} %shard_map.140.refs_0_), channel_id=1, source_target_pairs={{0,16},{16,0},{1,17},{17,1},{2,18},{18,2},{3,19},{19,3},{4,20},{20... | collective-permute-start | bytes 49160 | tf_op jit(solution)/shard_map/ppermute | solution.py:511
  6.6 0.0 copy-done.2
  6.6 0.0 copy-done.3
  6.6 0.0 copy-done.4
  6.7 0.0 copy-done.7
  6.7 0.0 copy-done.8
  6.7 0.0 copy-done.9
  6.7 0.6 %copy-done.6 = f32[1024]{0:T(1024)S(1)} copy-done((f32[1024]{0:T(1024)S(1)}, f32[1024]{0:T(1024)}, u32[]{:S(2)}) %copy-start.6) | copy-done | bytes 4120
  7.3 0.0 copy-done.5
  7.3 0.0 copy-done.10
  7.3 1.1 %shard_map.141 = (f32[56,128]{1,0:T(8,128)S(1)}, f32[56,128]{1,0:T(8,128)S(1)}, f32[56,128]{1,0:T(8,128)S(1)}, f32[56,128]{1,0:T(8,128)S(1)}, f32[56,128]{1,0:T(...) custom-call(s32[1]{0:T(128)} %bitcast.1.pos_ref, s32[1]{0:T(128)} %bitcast.lev_ref, ...), custom_call_target="tpu_custom_call" | custom-call | tf_op jit(solution)/shard_map/pallas_call | solution.py:505
  8.4 0.0 collective-permute-done.2.refs_1_
  8.5 4.1 %collective-permute-start.3 = (f32[88,128]{1,0:T(8,128)S(1)}, f32[88,128]{1,0:T(8,128)S(1)}, u32[]{:S(2)}, u32[]{:S(2)}) collective-permute-start(f32[88,128]{1,0:T(8,128)S(1)} %get-tuple-element.52), channel_id=1, source_target_pairs={{0,12},{1,13},{2,14},{3,15},{4,8},{5,9},{6,10},{7,11},{8,4},{9,5},... | collective-permute-start | bytes 135176 | tf_op jit(solution)/shard_map/ppermute | solution.py:526
  12.6 0.4 %collective-permute-start.4 = (f32[88,128]{1,0:T(8,128)S(1)}, f32[88,128]{1,0:T(8,128)S(1)}, u32[]{:S(2)}, u32[]{:S(2)}) collective-permute-start(f32[88,128]{1,0:T(8,128)S(1)} %get-tuple-element.53), channel_id=1, source_target_pairs={{0,10},{1,7},{2,8},{3,5},{4,14},{5,3},{6,12},{7,1},{8,2},{9,15},{1... | collective-permute-start | bytes 135176 | tf_op jit(solution)/shard_map/ppermute | solution.py:526
  13.0 2.4 %collective-permute-start.5 = (f32[88,128]{1,0:T(8,128)S(1)}, f32[88,128]{1,0:T(8,128)S(1)}, u32[]{:S(2)}, u32[]{:S(2)}) collective-permute-start(f32[88,128]{1,0:T(8,128)S(1)} %get-tuple-element.54), channel_id=1, source_target_pairs={{0,14},{1,15},{2,12},{3,13},{4,10},{5,11},{6,8},{7,9},{8,6},{9,7},... | collective-permute-start | bytes 135176 | tf_op jit(solution)/shard_map/ppermute | solution.py:526
  15.4 2.5 %collective-permute-start.6 = (f32[88,128]{1,0:T(8,128)S(1)}, f32[88,128]{1,0:T(8,128)S(1)}, u32[]{:S(2)}, u32[]{:S(2)}) collective-permute-start(f32[88,128]{1,0:T(8,128)S(1)} %get-tuple-element.55), channel_id=1, source_target_pairs={{0,6},{1,11},{2,4},{3,9},{4,2},{5,15},{6,0},{7,13},{8,14},{9,3},{1... | collective-permute-start | bytes 135176 | tf_op jit(solution)/shard_map/ppermute | solution.py:526
  17.9 0.4 %collective-permute-start.7 = (f32[88,128]{1,0:T(8,128)S(1)}, f32[88,128]{1,0:T(8,128)S(1)}, u32[]{:S(2)}, u32[]{:S(2)}) collective-permute-start(f32[88,128]{1,0:T(8,128)S(1)} %get-tuple-element.56), channel_id=1, source_target_pairs={{0,4},{1,9},{2,6},{3,11},{4,0},{5,13},{6,2},{7,15},{8,12},{9,1},{1... | collective-permute-start | bytes 135176 | tf_op jit(solution)/shard_map/ppermute | solution.py:526
  18.4 0.0 collective-permute-done.3.refs_2_
  18.4 0.3 %collective-permute-start.8 = (f32[88,128]{1,0:T(8,128)S(1)}, f32[88,128]{1,0:T(8,128)S(1)}, u32[]{:S(2)}, u32[]{:S(2)}) collective-permute-start(f32[88,128]{1,0:T(8,128)S(1)} %get-tuple-element.57), channel_id=1, source_target_pairs={{0,8},{1,5},{2,10},{3,7},{4,12},{5,1},{6,14},{7,3},{8,0},{9,13},{1... | collective-permute-start | bytes 135176 | tf_op jit(solution)/shard_map/ppermute | solution.py:526
  18.7 1.3 %collective-permute-done.4.refs_3_ = f32[88,128]{1,0:T(8,128)S(1)} collective-permute-done((f32[88,128]{1,0:T(8,128)S(1)}, f32[88,128]{1,0:T(8,128)S(1)}, u32[]{:S(2)}, u32[]{:S(2)}) %collective-permute-start.4) | collective-permute-done | bytes 45088 | tf_op jit(solution)/shard_map/ppermute | solution.py:526
  20.0 1.8 %collective-permute-start.9 = (f32[88,128]{1,0:T(8,128)S(1)}, f32[88,128]{1,0:T(8,128)S(1)}, u32[]{:S(2)}, u32[]{:S(2)}) collective-permute-start(f32[88,128]{1,0:T(8,128)S(1)} %get-tuple-element.58), channel_id=1, source_target_pairs={{0,2},{1,3},{2,0},{3,1},{4,6},{5,7},{6,4},{7,5},{8,10},{9,11},{10,... | collective-permute-start | bytes 135176 | tf_op jit(solution)/shard_map/ppermute | solution.py:526
  21.8 0.0 collective-permute-done.5.refs_4_
  21.8 0.9 %shard_map.143 = (bf16[8,32,512]{2,1,0:T(8,128)(2,1)S(1)}, f32[4,16,128]{2,1,0:T(8,128)S(1)}, f32[16,1024]{1,0:T(8,128)S(1)}, bf16[8,256,128]{2,1,0:T(8,128)(2,1)S(1)}) custom-call(f32[32,128]{1,0:T(8,128)S(1)} %get-tuple-element.50.refs_0_, f32[56,128]{1,0:T(8,128)S(1)} %get-tuple-element.51.refs_1_, f32[88,128]{1,0:T(8,128)S(1)} %collective-permute-done.3.refs_2_, ...), custom_call_target="tpu_custom_call" | custom-call | tf_op jit(solution)/shard_map/pallas_call | solution.py:536
  22.8 0.0 collective-permute-done.6.refs_5_
  22.8 0.0 collective-permute-done.7.refs_6_
  22.8 0.7 %shard_map.144 = (bf16[8,32,256]{2,1,0:T(8,128)(2,1)S(1)}, f32[6,16,128]{2,1,0:T(8,128)S(1)}, f32[16,1024]{1,0:T(8,128)S(1)}) custom-call(f32[32,128]{1,0:T(8,128)S(1)} %get-tuple-element.50.refs_0_, f32[56,128]{1,0:T(8,128)S(1)} %get-tuple-element.51.refs_1_, f32[88,128]{1,0:T(8,128)S(1)} %collective-permute-done.3.refs_2_, ...), custom_call_target="tpu_custom_call" | custom-call | tf_op jit(solution)/shard_map/pallas_call | solution.py:536
  23.5 0.0 collective-permute-done.8.refs_7_
  23.5 0.6 %collective-permute-done.9.refs_8_ = f32[88,128]{1,0:T(8,128)S(1)} collective-permute-done((f32[88,128]{1,0:T(8,128)S(1)}, f32[88,128]{1,0:T(8,128)S(1)}, u32[]{:S(2)}, u32[]{:S(2)}) %collective-permute-start.9) | collective-permute-done | bytes 45088 | tf_op jit(solution)/shard_map/ppermute | solution.py:526
  24.0 1.1 %shard_map.145 = (f32[48,128]{1,0:T(8,128)S(1)}, bf16[8,32,256]{2,1,0:T(8,128)(2,1)S(1)}, f32[8,16,128]{2,1,0:T(8,128)S(1)}) custom-call(s32[1]{0:T(128)} %bitcast.1.pos_ref, s32[1]{0:T(128)} %bitcast.lev_ref, f32[16,128]{1,0:T(8,128)S(1)} %get-tuple-element.41.mix_ref, f32[32,128]{1,0:T(8,128)S(1)} %get-tuple-element.50.refs_0_, ...), custom_call_target="tpu_custom_call" | custom-call | tf_op jit(solution)/shard_map/pallas_call | solution.py:546
  25.1 0.0 collective-permute-start.10
  25.1 0.4 %shard_map.146.own_ref = f32[16,40,256]{2,1,0:T(8,128)S(1)} custom-call(bf16[16,40,256]{2,1,0:T(8,128)(2,1)S(1)} %copy-done.1, f32[48,128]{1,0:T(8,128)S(1)} %get-tuple-element.65.mine_ref, bf16[2,128,128]{2,1,0:T(8,128)(2,1)S(1)} %get-tuple-element.66.weights_ref, f32[16,40,256]{2,1,0:T(8,128)S(1)} %copy-done), custom_call_target="tpu_custom_call" | custom-call | tf_op jit(solution)/shard_map/pallas_call | solution.py:574
  25.6 0.4 %shard_map.147 = (f32[16,1024]{1,0:T(8,128)S(1)}, f32[16,1024]{1,0:T(8,128)S(1)}) custom-call(s32[1]{0:T(128)} %bitcast.1.pos_ref, s32[1]{0:T(128)} %bitcast.lev_ref, bf16[8,32,512]{2,1,0:T(8,128)(2,1)S(1)} %get-tuple-element.59.refs_7_.refs_9_.refs_0_, bf16[8,32,256]{2,1,0:T(8,128)(2,1)S(1)} %get-tuple-element.62.refs_10_.refs_1_, ...), custom_call_target="tpu_custom_call" | custom-call | tf_op jit(solution)/shard_map/pallas_call | solution.py:552
  26.0 0.4 %collective-permute-done.10.theirs_ref = f32[48,128]{1,0:T(8,128)S(1)} collective-permute-done((f32[48,128]{1,0:T(8,128)S(1)}, f32[48,128]{1,0:T(8,128)S(1)}, u32[]{:S(2)}, u32[]{:S(2)}) %collective-permute-start.10) | collective-permute-done | bytes 24608 | tf_op jit(solution)/shard_map/ppermute | solution.py:573
  26.3 1.3 %shard_map.148 = (f32[16,40,256]{2,1,0:T(8,128)}, f32[16,1024]{1,0:T(8,128)}, f32[16,1024]{1,0:T(8,128)}) custom-call(bf16[16,40,256]{2,1,0:T(8,128)(2,1)S(1)} %collective-permute-done.1.perturb_ref, f32[48,128]{1,0:T(8,128)S(1)} %collective-permute-done.10.theirs_ref, f32[16,40,256]{2,1,0:T(8,128)S(1)} %shard_map.146.own_ref, ...), custom_call_target="tpu_custom_call" | custom-call | tf_op jit(solution)/shard_map/pallas_call | solution.py:575
  (8 shorter events, 0.0 us)
Async XLA Ops:
  0.6 2.5 %collective-permute-start = (f32[16,40,256]{2,1,0:T(8,128)}, f32[16,40,256]{2,1,0:T(8,128)S(1)}, u32[]{:S(2)}, u32[]{:S(2)}) collective-permute-start(f32[16,40,256]{2,1,0:T(8,128)} %control_ref.3), channel_id=1, source_target_pairs={{0,1},{1,0},{2,3},{3,2},{4,5},{5,4},{6,7},{7,6},{8,9},{9,8},{10,11... | collective-permute-start | bytes 1966088 | tf_op jit(solution)/shard_map/ppermute | solution.py:490
  1.1 2.5 %collective-permute-start.1 = (bf16[16,40,256]{2,1,0:T(8,128)(2,1)}, bf16[16,40,256]{2,1,0:T(8,128)(2,1)S(1)}, u32[]{:S(2)}, u32[]{:S(2)}) collective-permute-start(bf16[16,40,256]{2,1,0:T(8,128)(2,1)} %perturb_ref.3), channel_id=1, source_target_pairs={{0,1},{1,0},{2,3},{3,2},{4,5},{5,4},{6,7},{7,6},{8,9},{9,8},{10,11... | collective-permute-start | bytes 983048 | tf_op jit(solution)/shard_map/ppermute | solution.py:509
  1.2 0.7 %copy-start.11 = (f32[16,32]{1,0:T(8,128)S(1)}, f32[16,32]{1,0:T(8,128)}, u32[]{:S(2)}) copy-start(f32[16,32]{1,0:T(8,128)} %loc_ref.1) | copy-start | bytes 6148
  1.9 1.2 %copy-start = (f32[16,40,256]{2,1,0:T(8,128)S(1)}, f32[16,40,256]{2,1,0:T(8,128)}, u32[]{:S(2)}) copy-start(f32[16,40,256]{2,1,0:T(8,128)} %control_ref.3) | copy-start | bytes 1966084
  1.9 1.2 %copy-start.1 = (bf16[16,40,256]{2,1,0:T(8,128)(2,1)S(1)}, bf16[16,40,256]{2,1,0:T(8,128)(2,1)}, u32[]{:S(2)}) copy-start(bf16[16,40,256]{2,1,0:T(8,128)(2,1)} %perturb_ref.3) | copy-start | bytes 983044
  3.1 3.5 %copy-start.2 = (f32[16,1024]{1,0:T(8,128)S(1)}, f32[16,1024]{1,0:T(8,128)}, u32[]{:S(2)}) copy-start(f32[16,1024]{1,0:T(8,128)} %refs_5_.1) | copy-start | bytes 196612
  3.1 3.5 %copy-start.3 = (f32[16,1024]{1,0:T(8,128)S(1)}, f32[16,1024]{1,0:T(8,128)}, u32[]{:S(2)}) copy-start(f32[16,1024]{1,0:T(8,128)} %refs_8_.1) | copy-start | bytes 196612
  3.1 3.5 %copy-start.4 = (f32[16,1024]{1,0:T(8,128)S(1)}, f32[16,1024]{1,0:T(8,128)}, u32[]{:S(2)}) copy-start(f32[16,1024]{1,0:T(8,128)} %refs_9_.1) | copy-start | bytes 196612
  3.1 3.5 %copy-start.7 = (s32[1,8,128]{2,1,0:T(8,128)S(1)}, s32[1,8,128]{2,1,0:T(8,128)}, u32[]{:S(2)}) copy-start(s32[1,8,128]{2,1,0:T(8,128)} %src_ref.1) | copy-start | bytes 12292
  3.1 3.5 %copy-start.8 = (f32[1,8,128]{2,1,0:T(8,128)S(1)}, f32[1,8,128]{2,1,0:T(8,128)}, u32[]{:S(2)}) copy-start(f32[1,8,128]{2,1,0:T(8,128)} %weight_ref.1) | copy-start | bytes 12292
  3.1 3.5 %copy-start.9 = (s32[1,8,128]{2,1,0:T(8,128)S(1)}, s32[1,8,128]{2,1,0:T(8,128)}, u32[]{:S(2)}) copy-start(s32[1,8,128]{2,1,0:T(8,128)} %tgt_ref.1) | copy-start | bytes 12292
  3.7 4.8 %collective-permute-start.2 = (f32[16,256]{1,0:T(8,128)S(1)}, f32[16,256]{1,0:T(8,128)S(1)}, u32[]{:S(2)}, u32[]{:S(2)}) collective-permute-start(f32[16,256]{1,0:T(8,128)S(1)} %shard_map.140.refs_0_), channel_id=1, source_target_pairs={{0,16},{16,0},{1,17},{17,1},{2,18},{18,2},{3,19},{19,3},{4,20},{20... | collective-permute-start | bytes 49160 | tf_op jit(solution)/shard_map/ppermute | solution.py:511
  6.6 0.7 %copy-start.6 = (f32[1024]{0:T(1024)S(1)}, f32[1024]{0:T(1024)}, u32[]{:S(2)}) copy-start(f32[1024]{0:T(1024)} %param.17) | copy-start | bytes 12292
  6.6 0.7 %copy-start.5 = (f32[1024]{0:T(1024)S(1)}, f32[1024]{0:T(1024)}, u32[]{:S(2)}) copy-start(f32[1024]{0:T(1024)} %param.16) | copy-start | bytes 12292
  6.6 0.7 %copy-start.10 = (s32[1,8]{1,0:T(1,128)S(1)}, s32[1,8]{1,0:T(1,128)}, u32[]{:S(2)}) copy-start(s32[1,8]{1,0:T(1,128)} %counts_ref.1) | copy-start | bytes 100
  8.5 9.9 %collective-permute-start.3 = (f32[88,128]{1,0:T(8,128)S(1)}, f32[88,128]{1,0:T(8,128)S(1)}, u32[]{:S(2)}, u32[]{:S(2)}) collective-permute-start(f32[88,128]{1,0:T(8,128)S(1)} %get-tuple-element.52), channel_id=1, source_target_pairs={{0,12},{1,13},{2,14},{3,15},{4,8},{5,9},{6,10},{7,11},{8,4},{9,5},... | collective-permute-start | bytes 135176 | tf_op jit(solution)/shard_map/ppermute | solution.py:526
  12.6 7.4 %collective-permute-start.4 = (f32[88,128]{1,0:T(8,128)S(1)}, f32[88,128]{1,0:T(8,128)S(1)}, u32[]{:S(2)}, u32[]{:S(2)}) collective-permute-start(f32[88,128]{1,0:T(8,128)S(1)} %get-tuple-element.53), channel_id=1, source_target_pairs={{0,10},{1,7},{2,8},{3,5},{4,14},{5,3},{6,12},{7,1},{8,2},{9,15},{1... | collective-permute-start | bytes 135176 | tf_op jit(solution)/shard_map/ppermute | solution.py:526
  13.0 8.9 %collective-permute-start.5 = (f32[88,128]{1,0:T(8,128)S(1)}, f32[88,128]{1,0:T(8,128)S(1)}, u32[]{:S(2)}, u32[]{:S(2)}) collective-permute-start(f32[88,128]{1,0:T(8,128)S(1)} %get-tuple-element.54), channel_id=1, source_target_pairs={{0,14},{1,15},{2,12},{3,13},{4,10},{5,11},{6,8},{7,9},{8,6},{9,7},... | collective-permute-start | bytes 135176 | tf_op jit(solution)/shard_map/ppermute | solution.py:526
  15.4 7.4 %collective-permute-start.6 = (f32[88,128]{1,0:T(8,128)S(1)}, f32[88,128]{1,0:T(8,128)S(1)}, u32[]{:S(2)}, u32[]{:S(2)}) collective-permute-start(f32[88,128]{1,0:T(8,128)S(1)} %get-tuple-element.55), channel_id=1, source_target_pairs={{0,6},{1,11},{2,4},{3,9},{4,2},{5,15},{6,0},{7,13},{8,14},{9,3},{1... | collective-permute-start | bytes 135176 | tf_op jit(solution)/shard_map/ppermute | solution.py:526
  17.9 4.8 %collective-permute-start.7 = (f32[88,128]{1,0:T(8,128)S(1)}, f32[88,128]{1,0:T(8,128)S(1)}, u32[]{:S(2)}, u32[]{:S(2)}) collective-permute-start(f32[88,128]{1,0:T(8,128)S(1)} %get-tuple-element.56), channel_id=1, source_target_pairs={{0,4},{1,9},{2,6},{3,11},{4,0},{5,13},{6,2},{7,15},{8,12},{9,1},{1... | collective-permute-start | bytes 135176 | tf_op jit(solution)/shard_map/ppermute | solution.py:526
  18.4 5.1 %collective-permute-start.8 = (f32[88,128]{1,0:T(8,128)S(1)}, f32[88,128]{1,0:T(8,128)S(1)}, u32[]{:S(2)}, u32[]{:S(2)}) collective-permute-start(f32[88,128]{1,0:T(8,128)S(1)} %get-tuple-element.57), channel_id=1, source_target_pairs={{0,8},{1,5},{2,10},{3,7},{4,12},{5,1},{6,14},{7,3},{8,0},{9,13},{1... | collective-permute-start | bytes 135176 | tf_op jit(solution)/shard_map/ppermute | solution.py:526
  20.0 4.0 %collective-permute-start.9 = (f32[88,128]{1,0:T(8,128)S(1)}, f32[88,128]{1,0:T(8,128)S(1)}, u32[]{:S(2)}, u32[]{:S(2)}) collective-permute-start(f32[88,128]{1,0:T(8,128)S(1)} %get-tuple-element.58), channel_id=1, source_target_pairs={{0,2},{1,3},{2,0},{3,1},{4,6},{5,7},{6,4},{7,5},{8,10},{9,11},{10,... | collective-permute-start | bytes 135176 | tf_op jit(solution)/shard_map/ppermute | solution.py:526
  25.1 1.2 %collective-permute-start.10 = (f32[48,128]{1,0:T(8,128)S(1)}, f32[48,128]{1,0:T(8,128)S(1)}, u32[]{:S(2)}, u32[]{:S(2)}) collective-permute-start(f32[48,128]{1,0:T(8,128)S(1)} %get-tuple-element.65.mine_ref), channel_id=1, source_target_pairs={{0,1},{1,0},{2,3},{3,2},{4,5},{5,4},{6,7},{7,6},{8,9},{9,8},{10,11... | collective-permute-start | bytes 73736 | tf_op jit(solution)/shard_map/ppermute | solution.py:573

commit v18 on v14

--- a/solution.py
+++ b/solution.py
@@ -517,7 +517,7 @@
         low, high = n // 4, n // 2
         mixed = [r for i in reversed(range(low)) for r in (high + i, low + i)]
         order = [high + low, mixed[0], *range(high + low + 1, n), *mixed[1:], *range(1, low)]
-        stages = [[0] + order[: high - 1], order[high - 1 : n - low], order[n - low :]]
+        stages = [[0] + order[: high - 1], order[high - 1 : high], order[high:]]
         levs = lax.axis_size("lev")
         arrived = {0: [total, rests[0]]}
         for r in sum(stages, [])[1:]:

time: 27.8 us -> 28.2 us (1.014)
    pallas_call x1, Pallas kernels: 0.89 us -> 1.51 us  [body(): call(functools.partial(shared_kernel, n, levels, band_cols, tile_cols, st...]
    pallas_call x2, Pallas kernels: 1.96 us -> 1.42 us  [body(): call(functools.partial(stage_kernel, n, levels, band_cols, tile_cols, sta...]
    ppermute x7, waiting for transfers between devices: 2.16 us -> 2.49 us  [body(): arrived[r] = [lax.ppermute(blocks[r - 1], ('tile', 'lev'), pairs)]]
  transfers between devices with their start and end apart: 11 -> 11, of which waited for: 4 -> 5; matrix products, arithmetic and copies ran while one was open for 0% -> 0% of each run, Pallas kernels for 17% -> 15%
where the time goes in v18:
time: 28.2 us; the launch traced here: 28 us
  starting transfers between devices  15.2 us (54%)
  Pallas kernels  6.96 us (25%)
  waiting for transfers between devices  3.68 us (13%)
  local copies, waits for them, and re-layouts  1.39 us (5%)
  between operations  0.78 us (3%)
    ppermute x7, starting transfers between devices, body(): arrived[r] = [lax.ppermute(blocks[r - 1], ('tile', 'lev'), pairs)]  11.6 us
    ppermute x1, starting transfers between devices, body(): lax.ppermute(sums[0], 'grp', [(g, (g + k) % groups) for g in range(groups)])  2.97 us
    ppermute x7, waiting for transfers between devices, body(): arrived[r] = [lax.ppermute(blocks[r - 1], ('tile', 'lev'), pairs)]  2.49 us
    pallas_call x1, Pallas kernels, body(): call(functools.partial(shared_kernel, n, levels, band_cols, tile_cols, st...  1.51 us
    pallas_call x2, Pallas kernels, body(): call(functools.partial(stage_kernel, n, levels, band_cols, tile_cols, sta...  1.42 us
    unnamed x24, local copies, waits for them, and re-layouts  1.39 us
    pallas_call x1, Pallas kernels, body(): call(ens_kernel, (shape(control.shape, F32), flat, flat), [VMEM] * 5, [pl...  1.25 us
    pallas_call x1, Pallas kernels, body(): call(functools.partial(static_kernel, band_cols), [shape((rows.total, cap...  1.1 us
  transfers between devices with their start and end apart: 11, of which 5 were waited for; matrix products, arithmetic and copies ran while one was open for 0% of the time, Pallas kernels for 15%

profile of v18, /device:TPU:0, one launch (start us, length us, event | category | flops | bytes accessed | tf_op | source)
XLA Modules:
  0.0 28.0 jit_solution(3873703725413859448)
XLA Ops:
  0.6 0.5 %collective-permute-start = (f32[16,40,256]{2,1,0:T(8,128)}, f32[16,40,256]{2,1,0:T(8,128)S(1)}, u32[]{:S(2)}, u32[]{:S(2)}) collective-permute-start(f32[16,40,256]{2,1,0:T(8,128)} %control_ref.3), channel_id=1, source_target_pairs={{0,1},{1,0},{2,3},{3,2},{4,5},{5,4},{6,7},{7,6},{8,9},{9,8},{10,11... | collective-permute-start | bytes 1966088 | tf_op jit(solution)/shard_map/ppermute | solution.py:490
  1.1 0.1 collective-permute-start.1
  1.2 0.0 copy-start.11
  1.2 0.7 %copy-done.11 = f32[16,32]{1,0:T(8,128)S(1)} copy-done((f32[16,32]{1,0:T(8,128)S(1)}, f32[16,32]{1,0:T(8,128)}, u32[]{:S(2)}) %copy-start.11) | copy-done | bytes 2072
  1.9 0.0 copy-start
  1.9 0.2 shard_map.139
  2.2 0.9 %collective-permute-done.other_ref = f32[16,40,256]{2,1,0:T(8,128)S(1)} collective-permute-done((f32[16,40,256]{2,1,0:T(8,128)}, f32[16,40,256]{2,1,0:T(8,128)S(1)}, u32[]{:S(2)}, u32[]{:S(2)}) %collective-permute-start) | collective-permute-done | bytes 655392 | tf_op jit(solution)/shard_map/ppermute | solution.py:490
  3.1 0.0 copy-done
  3.1 0.0 copy-done.1
  3.1 0.0 copy-start.7
  3.1 0.0 copy-start.8
  3.1 0.0 copy-start.9
  3.1 0.5 %shard_map.140.refs_0_ = f32[16,256]{1,0:T(8,128)S(1)} custom-call(bf16[16,40,256]{2,1,0:T(8,128)(2,1)S(1)} %copy-done.1, f32[16,40,256]{2,1,0:T(8,128)S(1)} %copy-done, f32[16,40,256]{2,1,0:T(8,128)S(1)} %collective-permute-done.other_ref, bf16[2,128,256]{2,1,0:T(8,128)(2,1)S(1)} %get-tuple-element.39.mix_ref), custom_call_target="tpu_custom_call" | custom-call | tf_op jit(solution)/shard_map/pallas_call | solution.py:498
  3.6 0.0 collective-permute-done.1.perturb_ref
  3.7 3.0 %collective-permute-start.2 = (f32[16,256]{1,0:T(8,128)S(1)}, f32[16,256]{1,0:T(8,128)S(1)}, u32[]{:S(2)}, u32[]{:S(2)}) collective-permute-start(f32[16,256]{1,0:T(8,128)S(1)} %shard_map.140.refs_0_), channel_id=1, source_target_pairs={{0,16},{16,0},{1,17},{17,1},{2,18},{18,2},{3,19},{19,3},{4,20},{20... | collective-permute-start | bytes 49160 | tf_op jit(solution)/shard_map/ppermute | solution.py:511
  6.6 0.0 copy-done.2
  6.6 0.0 copy-done.3
  6.6 0.0 copy-done.4
  6.7 0.0 copy-done.7
  6.7 0.0 copy-done.8
  6.7 0.0 copy-done.9
  6.7 0.6 %copy-done.6 = f32[1024]{0:T(1024)S(1)} copy-done((f32[1024]{0:T(1024)S(1)}, f32[1024]{0:T(1024)}, u32[]{:S(2)}) %copy-start.6) | copy-done | bytes 4120
  7.3 0.0 copy-done.5
  7.3 0.0 copy-done.10
  7.3 1.1 %shard_map.141 = (f32[56,128]{1,0:T(8,128)S(1)}, f32[56,128]{1,0:T(8,128)S(1)}, f32[56,128]{1,0:T(8,128)S(1)}, f32[56,128]{1,0:T(8,128)S(1)}, f32[56,128]{1,0:T(...) custom-call(s32[1]{0:T(128)} %bitcast.1.pos_ref, s32[1]{0:T(128)} %bitcast.lev_ref, ...), custom_call_target="tpu_custom_call" | custom-call | tf_op jit(solution)/shard_map/pallas_call | solution.py:505
  8.4 0.0 collective-permute-done.2.refs_1_
  8.5 4.1 %collective-permute-start.3 = (f32[88,128]{1,0:T(8,128)S(1)}, f32[88,128]{1,0:T(8,128)S(1)}, u32[]{:S(2)}, u32[]{:S(2)}) collective-permute-start(f32[88,128]{1,0:T(8,128)S(1)} %get-tuple-element.52), channel_id=1, source_target_pairs={{0,12},{1,13},{2,14},{3,15},{4,8},{5,9},{6,10},{7,11},{8,4},{9,5},... | collective-permute-start | bytes 135176 | tf_op jit(solution)/shard_map/ppermute | solution.py:525
  12.6 0.4 %collective-permute-start.4 = (f32[88,128]{1,0:T(8,128)S(1)}, f32[88,128]{1,0:T(8,128)S(1)}, u32[]{:S(2)}, u32[]{:S(2)}) collective-permute-start(f32[88,128]{1,0:T(8,128)S(1)} %get-tuple-element.53), channel_id=1, source_target_pairs={{0,10},{1,7},{2,8},{3,5},{4,14},{5,3},{6,12},{7,1},{8,2},{9,15},{1... | collective-permute-start | bytes 135176 | tf_op jit(solution)/shard_map/ppermute | solution.py:525
  13.0 2.4 %collective-permute-start.5 = (f32[88,128]{1,0:T(8,128)S(1)}, f32[88,128]{1,0:T(8,128)S(1)}, u32[]{:S(2)}, u32[]{:S(2)}) collective-permute-start(f32[88,128]{1,0:T(8,128)S(1)} %get-tuple-element.54), channel_id=1, source_target_pairs={{0,14},{1,15},{2,12},{3,13},{4,10},{5,11},{6,8},{7,9},{8,6},{9,7},... | collective-permute-start | bytes 135176 | tf_op jit(solution)/shard_map/ppermute | solution.py:525
  15.4 2.5 %collective-permute-start.6 = (f32[88,128]{1,0:T(8,128)S(1)}, f32[88,128]{1,0:T(8,128)S(1)}, u32[]{:S(2)}, u32[]{:S(2)}) collective-permute-start(f32[88,128]{1,0:T(8,128)S(1)} %get-tuple-element.55), channel_id=1, source_target_pairs={{0,6},{1,11},{2,4},{3,9},{4,2},{5,15},{6,0},{7,13},{8,14},{9,3},{1... | collective-permute-start | bytes 135176 | tf_op jit(solution)/shard_map/ppermute | solution.py:525
  17.9 0.3 %collective-permute-start.7 = (f32[88,128]{1,0:T(8,128)S(1)}, f32[88,128]{1,0:T(8,128)S(1)}, u32[]{:S(2)}, u32[]{:S(2)}) collective-permute-start(f32[88,128]{1,0:T(8,128)S(1)} %get-tuple-element.56), channel_id=1, source_target_pairs={{0,8},{1,5},{2,10},{3,7},{4,12},{5,1},{6,14},{7,3},{8,0},{9,13},{1... | collective-permute-start | bytes 135176 | tf_op jit(solution)/shard_map/ppermute | solution.py:525
  18.2 0.0 collective-permute-done.3.refs_2_
  18.2 0.4 %collective-permute-start.8 = (f32[88,128]{1,0:T(8,128)S(1)}, f32[88,128]{1,0:T(8,128)S(1)}, u32[]{:S(2)}, u32[]{:S(2)}) collective-permute-start(f32[88,128]{1,0:T(8,128)S(1)} %get-tuple-element.57), channel_id=1, source_target_pairs={{0,4},{1,9},{2,6},{3,11},{4,0},{5,13},{6,2},{7,15},{8,12},{9,1},{1... | collective-permute-start | bytes 135176 | tf_op jit(solution)/shard_map/ppermute | solution.py:525
  18.7 1.3 %collective-permute-done.4.refs_3_ = f32[88,128]{1,0:T(8,128)S(1)} collective-permute-done((f32[88,128]{1,0:T(8,128)S(1)}, f32[88,128]{1,0:T(8,128)S(1)}, u32[]{:S(2)}, u32[]{:S(2)}) %collective-permute-start.4) | collective-permute-done | bytes 45088 | tf_op jit(solution)/shard_map/ppermute | solution.py:525
  20.0 1.4 %collective-permute-start.9 = (f32[88,128]{1,0:T(8,128)S(1)}, f32[88,128]{1,0:T(8,128)S(1)}, u32[]{:S(2)}, u32[]{:S(2)}) collective-permute-start(f32[88,128]{1,0:T(8,128)S(1)} %get-tuple-element.58), channel_id=1, source_target_pairs={{0,2},{1,3},{2,0},{3,1},{4,6},{5,7},{6,4},{7,5},{8,10},{9,11},{10,... | collective-permute-start | bytes 135176 | tf_op jit(solution)/shard_map/ppermute | solution.py:525
  21.4 0.0 collective-permute-done.5.refs_4_
  21.4 0.9 %shard_map.143 = (bf16[8,32,512]{2,1,0:T(8,128)(2,1)S(1)}, f32[4,16,128]{2,1,0:T(8,128)S(1)}, f32[16,1024]{1,0:T(8,128)S(1)}, bf16[8,256,128]{2,1,0:T(8,128)(2,1)S(1)}) custom-call(f32[32,128]{1,0:T(8,128)S(1)} %get-tuple-element.50.refs_0_, f32[56,128]{1,0:T(8,128)S(1)} %get-tuple-element.51.refs_1_, f32[88,128]{1,0:T(8,128)S(1)} %collective-permute-done.3.refs_2_, ...), custom_call_target="tpu_custom_call" | custom-call | tf_op jit(solution)/shard_map/pallas_call | solution.py:535
  22.4 0.0 collective-permute-done.6.refs_5_
  22.4 0.5 %shard_map.144 = (bf16[8,32,128]{2,1,0:T(8,128)(2,1)S(1)}, f32[5,16,128]{2,1,0:T(8,128)S(1)}, f32[16,1024]{1,0:T(8,128)S(1)}) custom-call(f32[32,128]{1,0:T(8,128)S(1)} %get-tuple-element.50.refs_0_, f32[56,128]{1,0:T(8,128)S(1)} %get-tuple-element.51.refs_1_, f32[88,128]{1,0:T(8,128)S(1)} %collective-permute-done.3.refs_2_, ...), custom_call_target="tpu_custom_call" | custom-call | tf_op jit(solution)/shard_map/pallas_call | solution.py:535
  22.9 0.4 %collective-permute-done.7.refs_6_ = f32[88,128]{1,0:T(8,128)S(1)} collective-permute-done((f32[88,128]{1,0:T(8,128)S(1)}, f32[88,128]{1,0:T(8,128)S(1)}, u32[]{:S(2)}, u32[]{:S(2)}) %collective-permute-start.7) | collective-permute-done | bytes 45088 | tf_op jit(solution)/shard_map/ppermute | solution.py:525
  23.2 0.0 collective-permute-done.8.refs_7_
  23.2 0.8 %collective-permute-done.9.refs_8_ = f32[88,128]{1,0:T(8,128)S(1)} collective-permute-done((f32[88,128]{1,0:T(8,128)S(1)}, f32[88,128]{1,0:T(8,128)S(1)}, u32[]{:S(2)}, u32[]{:S(2)}) %collective-permute-start.9) | collective-permute-done | bytes 45088 | tf_op jit(solution)/shard_map/ppermute | solution.py:525
  24.0 1.5 %shard_map.145 = (f32[48,128]{1,0:T(8,128)S(1)}, bf16[8,32,384]{2,1,0:T(8,128)(2,1)S(1)}, f32[8,16,128]{2,1,0:T(8,128)S(1)}) custom-call(s32[1]{0:T(128)} %bitcast.1.pos_ref, s32[1]{0:T(128)} %bitcast.lev_ref, f32[16,128]{1,0:T(8,128)S(1)} %get-tuple-element.41.mix_ref, f32[32,128]{1,0:T(8,128)S(1)} %get-tuple-element.50.refs_0_, ...), custom_call_target="tpu_custom_call" | custom-call | tf_op jit(solution)/shard_map/pallas_call | solution.py:545
  25.6 0.0 collective-permute-start.10
  25.6 0.4 %shard_map.146.own_ref = f32[16,40,256]{2,1,0:T(8,128)S(1)} custom-call(bf16[16,40,256]{2,1,0:T(8,128)(2,1)S(1)} %copy-done.1, f32[48,128]{1,0:T(8,128)S(1)} %get-tuple-element.65.mine_ref, bf16[2,128,128]{2,1,0:T(8,128)(2,1)S(1)} %get-tuple-element.66.weights_ref, f32[16,40,256]{2,1,0:T(8,128)S(1)} %copy-done), custom_call_target="tpu_custom_call" | custom-call | tf_op jit(solution)/shard_map/pallas_call | solution.py:573
  26.0 0.5 %shard_map.147 = (f32[16,1024]{1,0:T(8,128)S(1)}, f32[16,1024]{1,0:T(8,128)S(1)}) custom-call(s32[1]{0:T(128)} %bitcast.1.pos_ref, s32[1]{0:T(128)} %bitcast.lev_ref, bf16[8,32,512]{2,1,0:T(8,128)(2,1)S(1)} %get-tuple-element.59.refs_6_.refs_9_.refs_0_, bf16[8,32,128]{2,1,0:T(8,128)(2,1)S(1)} %get-tuple-element.62.refs_10_.refs_1_, ...), custom_call_target="tpu_custom_call" | custom-call | tf_op jit(solution)/shard_map/pallas_call | solution.py:551
  26.5 0.3 %collective-permute-done.10.theirs_ref = f32[48,128]{1,0:T(8,128)S(1)} collective-permute-done((f32[48,128]{1,0:T(8,128)S(1)}, f32[48,128]{1,0:T(8,128)S(1)}, u32[]{:S(2)}, u32[]{:S(2)}) %collective-permute-start.10) | collective-permute-done | bytes 24608 | tf_op jit(solution)/shard_map/ppermute | solution.py:572
  26.8 1.2 %shard_map.148 = (f32[16,40,256]{2,1,0:T(8,128)}, f32[16,1024]{1,0:T(8,128)}, f32[16,1024]{1,0:T(8,128)}) custom-call(bf16[16,40,256]{2,1,0:T(8,128)(2,1)S(1)} %collective-permute-done.1.perturb_ref, f32[48,128]{1,0:T(8,128)S(1)} %collective-permute-done.10.theirs_ref, f32[16,40,256]{2,1,0:T(8,128)S(1)} %shard_map.146.own_ref, ...), custom_call_target="tpu_custom_call" | custom-call | tf_op jit(solution)/shard_map/pallas_call | solution.py:574
  (8 shorter events, 0.0 us)
Async XLA Ops:
  0.6 2.5 %collective-permute-start = (f32[16,40,256]{2,1,0:T(8,128)}, f32[16,40,256]{2,1,0:T(8,128)S(1)}, u32[]{:S(2)}, u32[]{:S(2)}) collective-permute-start(f32[16,40,256]{2,1,0:T(8,128)} %control_ref.3), channel_id=1, source_target_pairs={{0,1},{1,0},{2,3},{3,2},{4,5},{5,4},{6,7},{7,6},{8,9},{9,8},{10,11... | collective-permute-start | bytes 1966088 | tf_op jit(solution)/shard_map/ppermute | solution.py:490
  1.1 2.5 %collective-permute-start.1 = (bf16[16,40,256]{2,1,0:T(8,128)(2,1)}, bf16[16,40,256]{2,1,0:T(8,128)(2,1)S(1)}, u32[]{:S(2)}, u32[]{:S(2)}) collective-permute-start(bf16[16,40,256]{2,1,0:T(8,128)(2,1)} %perturb_ref.3), channel_id=1, source_target_pairs={{0,1},{1,0},{2,3},{3,2},{4,5},{5,4},{6,7},{7,6},{8,9},{9,8},{10,11... | collective-permute-start | bytes 983048 | tf_op jit(solution)/shard_map/ppermute | solution.py:509
  1.2 0.7 %copy-start.11 = (f32[16,32]{1,0:T(8,128)S(1)}, f32[16,32]{1,0:T(8,128)}, u32[]{:S(2)}) copy-start(f32[16,32]{1,0:T(8,128)} %loc_ref.1) | copy-start | bytes 6148
  1.9 1.2 %copy-start = (f32[16,40,256]{2,1,0:T(8,128)S(1)}, f32[16,40,256]{2,1,0:T(8,128)}, u32[]{:S(2)}) copy-start(f32[16,40,256]{2,1,0:T(8,128)} %control_ref.3) | copy-start | bytes 1966084
  1.9 1.2 %copy-start.1 = (bf16[16,40,256]{2,1,0:T(8,128)(2,1)S(1)}, bf16[16,40,256]{2,1,0:T(8,128)(2,1)}, u32[]{:S(2)}) copy-start(bf16[16,40,256]{2,1,0:T(8,128)(2,1)} %perturb_ref.3) | copy-start | bytes 983044
  3.1 3.5 %copy-start.2 = (f32[16,1024]{1,0:T(8,128)S(1)}, f32[16,1024]{1,0:T(8,128)}, u32[]{:S(2)}) copy-start(f32[16,1024]{1,0:T(8,128)} %refs_5_.1) | copy-start | bytes 196612
  3.1 3.5 %copy-start.3 = (f32[16,1024]{1,0:T(8,128)S(1)}, f32[16,1024]{1,0:T(8,128)}, u32[]{:S(2)}) copy-start(f32[16,1024]{1,0:T(8,128)} %refs_8_.1) | copy-start | bytes 196612
  3.1 3.5 %copy-start.4 = (f32[16,1024]{1,0:T(8,128)S(1)}, f32[16,1024]{1,0:T(8,128)}, u32[]{:S(2)}) copy-start(f32[16,1024]{1,0:T(8,128)} %refs_9_.1) | copy-start | bytes 196612
  3.1 3.5 %copy-start.7 = (s32[1,8,128]{2,1,0:T(8,128)S(1)}, s32[1,8,128]{2,1,0:T(8,128)}, u32[]{:S(2)}) copy-start(s32[1,8,128]{2,1,0:T(8,128)} %src_ref.1) | copy-start | bytes 12292
  3.1 3.5 %copy-start.8 = (f32[1,8,128]{2,1,0:T(8,128)S(1)}, f32[1,8,128]{2,1,0:T(8,128)}, u32[]{:S(2)}) copy-start(f32[1,8,128]{2,1,0:T(8,128)} %weight_ref.1) | copy-start | bytes 12292
  3.1 3.5 %copy-start.9 = (s32[1,8,128]{2,1,0:T(8,128)S(1)}, s32[1,8,128]{2,1,0:T(8,128)}, u32[]{:S(2)}) copy-start(s32[1,8,128]{2,1,0:T(8,128)} %tgt_ref.1) | copy-start | bytes 12292
  3.7 4.8 %collective-permute-start.2 = (f32[16,256]{1,0:T(8,128)S(1)}, f32[16,256]{1,0:T(8,128)S(1)}, u32[]{:S(2)}, u32[]{:S(2)}) collective-permute-start(f32[16,256]{1,0:T(8,128)S(1)} %shard_map.140.refs_0_), channel_id=1, source_target_pairs={{0,16},{16,0},{1,17},{17,1},{2,18},{18,2},{3,19},{19,3},{4,20},{20... | collective-permute-start | bytes 49160 | tf_op jit(solution)/shard_map/ppermute | solution.py:511
  6.6 0.7 %copy-start.6 = (f32[1024]{0:T(1024)S(1)}, f32[1024]{0:T(1024)}, u32[]{:S(2)}) copy-start(f32[1024]{0:T(1024)} %param.17) | copy-start | bytes 12292
  6.6 0.7 %copy-start.5 = (f32[1024]{0:T(1024)S(1)}, f32[1024]{0:T(1024)}, u32[]{:S(2)}) copy-start(f32[1024]{0:T(1024)} %param.16) | copy-start | bytes 12292
  6.6 0.7 %copy-start.10 = (s32[1,8]{1,0:T(1,128)S(1)}, s32[1,8]{1,0:T(1,128)}, u32[]{:S(2)}) copy-start(s32[1,8]{1,0:T(1,128)} %counts_ref.1) | copy-start | bytes 100
  8.5 9.8 %collective-permute-start.3 = (f32[88,128]{1,0:T(8,128)S(1)}, f32[88,128]{1,0:T(8,128)S(1)}, u32[]{:S(2)}, u32[]{:S(2)}) collective-permute-start(f32[88,128]{1,0:T(8,128)S(1)} %get-tuple-element.52), channel_id=1, source_target_pairs={{0,12},{1,13},{2,14},{3,15},{4,8},{5,9},{6,10},{7,11},{8,4},{9,5},... | collective-permute-start | bytes 135176 | tf_op jit(solution)/shard_map/ppermute | solution.py:525
  12.6 7.4 %collective-permute-start.4 = (f32[88,128]{1,0:T(8,128)S(1)}, f32[88,128]{1,0:T(8,128)S(1)}, u32[]{:S(2)}, u32[]{:S(2)}) collective-permute-start(f32[88,128]{1,0:T(8,128)S(1)} %get-tuple-element.53), channel_id=1, source_target_pairs={{0,10},{1,7},{2,8},{3,5},{4,14},{5,3},{6,12},{7,1},{8,2},{9,15},{1... | collective-permute-start | bytes 135176 | tf_op jit(solution)/shard_map/ppermute | solution.py:525
  13.0 8.5 %collective-permute-start.5 = (f32[88,128]{1,0:T(8,128)S(1)}, f32[88,128]{1,0:T(8,128)S(1)}, u32[]{:S(2)}, u32[]{:S(2)}) collective-permute-start(f32[88,128]{1,0:T(8,128)S(1)} %get-tuple-element.54), channel_id=1, source_target_pairs={{0,14},{1,15},{2,12},{3,13},{4,10},{5,11},{6,8},{7,9},{8,6},{9,7},... | collective-permute-start | bytes 135176 | tf_op jit(solution)/shard_map/ppermute | solution.py:525
  15.4 7.0 %collective-permute-start.6 = (f32[88,128]{1,0:T(8,128)S(1)}, f32[88,128]{1,0:T(8,128)S(1)}, u32[]{:S(2)}, u32[]{:S(2)}) collective-permute-start(f32[88,128]{1,0:T(8,128)S(1)} %get-tuple-element.55), channel_id=1, source_target_pairs={{0,6},{1,11},{2,4},{3,9},{4,2},{5,15},{6,0},{7,13},{8,14},{9,3},{1... | collective-permute-start | bytes 135176 | tf_op jit(solution)/shard_map/ppermute | solution.py:525
  17.9 5.3 %collective-permute-start.7 = (f32[88,128]{1,0:T(8,128)S(1)}, f32[88,128]{1,0:T(8,128)S(1)}, u32[]{:S(2)}, u32[]{:S(2)}) collective-permute-start(f32[88,128]{1,0:T(8,128)S(1)} %get-tuple-element.56), channel_id=1, source_target_pairs={{0,8},{1,5},{2,10},{3,7},{4,12},{5,1},{6,14},{7,3},{8,0},{9,13},{1... | collective-permute-start | bytes 135176 | tf_op jit(solution)/shard_map/ppermute | solution.py:525
  18.2 5.0 %collective-permute-start.8 = (f32[88,128]{1,0:T(8,128)S(1)}, f32[88,128]{1,0:T(8,128)S(1)}, u32[]{:S(2)}, u32[]{:S(2)}) collective-permute-start(f32[88,128]{1,0:T(8,128)S(1)} %get-tuple-element.57), channel_id=1, source_target_pairs={{0,4},{1,9},{2,6},{3,11},{4,0},{5,13},{6,2},{7,15},{8,12},{9,1},{1... | collective-permute-start | bytes 135176 | tf_op jit(solution)/shard_map/ppermute | solution.py:525
  20.0 4.0 %collective-permute-start.9 = (f32[88,128]{1,0:T(8,128)S(1)}, f32[88,128]{1,0:T(8,128)S(1)}, u32[]{:S(2)}, u32[]{:S(2)}) collective-permute-start(f32[88,128]{1,0:T(8,128)S(1)} %get-tuple-element.58), channel_id=1, source_target_pairs={{0,2},{1,3},{2,0},{3,1},{4,6},{5,7},{6,4},{7,5},{8,10},{9,11},{10,... | collective-permute-start | bytes 135176 | tf_op jit(solution)/shard_map/ppermute | solution.py:525
  25.6 1.2 %collective-permute-start.10 = (f32[48,128]{1,0:T(8,128)S(1)}, f32[48,128]{1,0:T(8,128)S(1)}, u32[]{:S(2)}, u32[]{:S(2)}) collective-permute-start(f32[48,128]{1,0:T(8,128)S(1)} %get-tuple-element.65.mine_ref), channel_id=1, source_target_pairs={{0,1},{1,0},{2,3},{3,2},{4,5},{5,4},{6,7},{7,6},{8,9},{9,8},{10,11... | collective-permute-start | bytes 73736 | tf_op jit(solution)/shard_map/ppermute | solution.py:572

commit v19 on v18

--- a/solution.py
+++ b/solution.py
@@ -224,15 +224,6 @@
         copy.wait()
 
 
-def relabel(r, n, lev):
-    high, low = n // 2, n // 4
-    if low == 0:
-        return r
-    both = high | low
-    turned = (r & ~both) | ((r & low) << 1) | ((r & high) >> 1)
-    return r + (turned - r) * lev
-
-
 class Rows:
     def __init__(self, levels, n):
         self.weight = slice(0, levels)
@@ -242,13 +233,13 @@
         self.total = at + 2 * n + EXTRA
 
 
-def static_kernel(band, pos_ref, lev_ref, counts_ref, static_ref, diag_ref, off_ref, obs_ref, innov_ref, src_ref, weight_ref, tgt_ref,
+def static_kernel(band, pos_ref, counts_ref, static_ref, diag_ref, off_ref, obs_ref, innov_ref, src_ref, weight_ref, tgt_ref,
                   *out_refs):
     levels, cols = static_ref.shape
     n = len(out_refs)
     cap = src_ref.shape[2]
     rows = Rows(levels, n)
-    peers = [pos_ref[0] ^ relabel(r, n, lev_ref[0]) for r in range(n)]
+    peers = [pos_ref[0] ^ r for r in range(n)]
     static, off, obs = static_ref[...], off_ref[...], obs_ref[...]
     lane = lax.broadcasted_iota(jnp.int32, (levels, cols), 1)
     left = jnp.where(lane == 0, 0.0, pltpu.roll(static, 1, 1))
@@ -274,27 +265,39 @@
         out_ref[rows.edge :, :] = edge
 
 
-def blocks_kernel(groups, *refs):
-    sums = refs[:groups]
-    count = (len(refs) - groups - 1) // 2
-    rests = refs[groups : groups + count]
-    total_ref = refs[groups + count]
-    out_refs = refs[groups + count + 1 :]
+def blocks_kernel(groups, levels, relayed, *refs):
+    sums, refs = refs[:groups], refs[groups:]
+    count = (len(refs) - 1 - relayed) // 2
+    rests, relays, total_ref, out_refs = refs[:count], refs[count : count + relayed], refs[count + relayed], refs[-count:]
     total = sum(ref[...] for ref in sums)
     cap = total_ref.shape[1]
     total = jnp.concatenate([total[:, at : at + cap] for at in range(0, total.shape[1], cap)], axis=0)
     total_ref[...] = total
-    for rest_ref, out_ref in zip(rests, out_refs):
-        out_ref[: total.shape[0], :] = total
-        out_ref[total.shape[0] :, :] = rest_ref[...]
+    for i, (rest_ref, out_ref) in enumerate(zip(rests, out_refs)):
+        parts = [total, rest_ref[...]]
+        if i == count - 1:
+            parts += [ref[: 2 * levels, :] for ref in relays]
+        out_ref[...] = jnp.concatenate(parts, axis=0)
+
+
+def relay_kernel(levels, stacked, got_ref, *refs):
+    count = len(refs) // 2
+    head = refs[0].shape[0]
+    for i, (block_ref, out_ref) in enumerate(zip(refs[:count], refs[count:])):
+        at = head + 2 * levels * i
+        out_ref[...] = jnp.concatenate(
+            [block_ref[...], got_ref[:stacked, :], got_ref[at : at + 2 * levels, :], got_ref[stacked + 2 * levels : head, :]],
+            axis=0,
+        )
 
 
 class Block:
-    def __init__(self, refs, n, levels, band):
+    def __init__(self, refs, n, levels, band, base=0):
         cap = refs[0].shape[1]
         self.levels, self.parts, self.cap = levels, band // cap, cap
         self.sums_ref, self.rest_ref = refs[0], refs[-1]
-        self.head = 0 if len(refs) == 2 else self.parts * levels
+        self.base = base
+        self.head = 0 if len(refs) == 2 else base + self.parts * levels
         self.rows = Rows(levels, n)
         words = self.rest(self.rows.index, n)
         self.tgt = jnp.floor((words + 0.5) * (1.0 / band))
@@ -305,7 +308,7 @@
         return self.rest_ref[self.head + at : self.head + at + size, :]
 
     def sums(self):
-        parts = [self.sums_ref[i * self.levels : (i + 1) * self.levels, :] for i in range(self.parts)]
+        parts = [self.sums_ref[self.base + i * self.levels : self.base + (i + 1) * self.levels, :] for i in range(self.parts)]
         return jnp.concatenate(halves(jnp.concatenate(parts, axis=1)), axis=0)
 
 
@@ -351,7 +354,8 @@
     blocks = {0: Block(refs[:2], n, levels, band)}
     refs = refs[2:]
     for i, r in enumerate(labels[1:]):
-        blocks[r] = Block(refs[i : i + 1], n, levels, band)
+        base = refs[i].shape[0] // 2 if r >= n // 2 + n // 4 else 0
+        blocks[r] = Block(refs[i : i + 1], n, levels, band, base)
     return blocks, refs[len(labels) - 1 :]
 
 
@@ -378,14 +382,14 @@
     remap_ref[...] = landed + remap_old[...] if known else landed
 
 
-def shared_kernel(n, levels, band, cols, stages, pos_ref, lev_ref, mix_ref, *refs):
+def shared_kernel(n, levels, band, cols, stages, pos_ref, mix_ref, *refs):
     known = sum(stages[:-1], [])
     blocks, refs = open_blocks(known + stages[-1], refs, n, levels, band)
     old, refs = refs[: len(stages) - 1], refs[len(stages) - 1 :]
     met_old, pick_ref, out_ref, slots_ref, tables_ref = refs
     me = pos_ref[0]
     for r, block in blocks.items():
-        there = me ^ relabel(r, n, lev_ref[0])
+        there = me ^ r
         tables_ref[there, :n, :] = block.tgt
         tables_ref[there, n:, :] = block.rest(block.rows.edge, EXTRA)
     fill_slots(stages[-1], blocks, n, slots_ref)
@@ -400,7 +404,7 @@
                 value = value + met_at(d, block, bands, ref)
         edge = block.rest(block.rows.edge, 1)
         own = line(block.tgt, d)
-        there = me ^ relabel(d, n, lev_ref[0])
+        there = me ^ d
         before = tables_ref[jnp.maximum(there - 1, 0), n : n + 1, :]
         near = jnp.where((own == 0.0) & (there > 0), edge[:, 6 * levels + 1 : 6 * levels + 2], 0.0)
         value = value + row_as_column(before, levels, 0) * near
@@ -412,7 +416,7 @@
     out_ref[...] = band_rows(total, mix_ref[...])
 
 
-def outputs_kernel(stages, pos_ref, lev_ref, *refs):
+def outputs_kernel(stages, pos_ref, *refs):
     slots_refs, refs = refs[: len(stages)], refs[len(stages) :]
     remap_ref, tables_ref, static_ref, diag_ref, off_ref, obs_ref, innov_ref, increment_ref, grad_ref = refs
     levels, cols = static_ref.shape
@@ -429,7 +433,7 @@
     def beside(there, exists, column, own_end, side):
         edge = tables_ref[there, n : n + 1, :]
         static_end, coupling, base = (row_as_column(edge, levels, (2 * i + side) * levels) for i in range(3))
-        far = relabel(me ^ there, n, lev_ref[0])
+        far = me ^ there
         landed = []
         for s, ref, place in given:
             values = ref[far, :levels, place].astype(F32) + ref[far, levels:, place].astype(F32)
@@ -502,27 +506,38 @@
     if n * cap <= tile_cols and n >= 8 and lax.axis_size("lev") == 2 and n & (n - 1) == 0 and band_cols * tile_cols <= 2**20:
         rows = Rows(levels, n)
         stacked = band_cols // cap * levels
-        rests = call(functools.partial(static_kernel, band_cols), [shape((rows.total, cap), F32)] * n, [SMEM] * 3 + [VMEM] * 8)(
-            pos, lev, counts, static_control, diag, off, obs_weight, innovation, send_src, send_wt, recv_tgt
+        rests = call(functools.partial(static_kernel, band_cols), [shape((rows.total, cap), F32)] * n, [SMEM] * 2 + [VMEM] * 8)(
+            pos, counts, static_control, diag, off, obs_weight, innovation, send_src, send_wt, recv_tgt
         )
         sums = [own_sum]
         sums[0], other_perturb = lax.optimization_barrier((sums[0], lax.ppermute(perturb, "lev", swap)))
         for k in range(1, groups):
             sums.append(lax.ppermute(sums[0], "grp", [(g, (g + k) % groups) for g in range(groups)]))
+        low, high = n // 4, n // 2
+        order = [high, *range(1, low), *range(high + 1, high + low), *reversed(range(low, high))]
+        stages = [[0] + order[: -low], *([r, r + high] for r in order[-low:])]
+        direct = order[::-1]
         total, *blocks = call(
-            functools.partial(blocks_kernel, groups),
-            [shape((stacked, cap), F32)] + [shape((stacked + rows.total, cap), F32)] * (n - 1),
-            [VMEM] * (groups + n - 1),
-        )(*sums, *rests[1:])
-        low, high = n // 4, n // 2
-        mixed = [r for i in reversed(range(low)) for r in (high + i, low + i)]
-        order = [high + low, mixed[0], *range(high + low + 1, n), *mixed[1:], *range(1, low)]
-        stages = [[0] + order[: high - 1], order[high - 1 : high], order[high:]]
-        levs = lax.axis_size("lev")
-        arrived = {0: [total, rests[0]]}
-        for r in sum(stages, [])[1:]:
-            pairs = [(i * levs + v, (i ^ relabel(r, n, v)) * levs + v) for i in range(n) for v in range(levs)]
-            arrived[r] = [lax.ppermute(blocks[r - 1], ("tile", "lev"), pairs)]
+            functools.partial(blocks_kernel, groups, levels, low),
+            [shape((stacked, cap), F32)]
+            + [shape((stacked + rows.total + (r == high) * 2 * levels * low, cap), F32) for r in direct],
+            [VMEM] * (groups + len(direct) + low),
+        )(*sums, *[rests[r] for r in direct], *rests[high + low :])
+        blocks = dict(zip(direct, blocks))
+
+        def to(r):
+            return lax.ppermute(blocks[r], "tile", [(i, i ^ r) for i in range(n)])
+
+        arrived = {0: [total, rests[0]]} | {r: [to(r)] for r in order[:-low]}
+        carriers = list(range(low, high))
+        joined = call(
+            functools.partial(relay_kernel, levels, stacked),
+            [shape((2 * (stacked + rows.total), cap), F32)] * low,
+            [VMEM] * (1 + low),
+        )(arrived[high][0], *[blocks[r] for r in carriers])
+        blocks |= dict(zip(carriers, joined))
+        for r in order[-low:]:
+            arrived[r] = arrived[r + high] = [to(r)]
         slots, carried, picks = [], [], []
         for count in range(1, len(stages)):
             labels = sum(stages[:count], [])
@@ -536,6 +551,7 @@
                 functools.partial(stage_kernel, n, levels, band_cols, tile_cols, stages[:count]),
                 outs,
                 [VMEM] * (len(refs) + len(slots) + len(carried)),
+                cost=pl.CostEstimate(flops=10**9, bytes_accessed=0, transcendentals=0),
             )(*refs, *slots, *carried)
             slots.append(new)
             picks += carried[2:]
@@ -545,12 +561,13 @@
         mine, new, tables = call(
             functools.partial(shared_kernel, n, levels, band_cols, tile_cols, stages),
             (mine_shape, shape((n, 2 * levels, len(stages[-1]) * cap), BF16), shape((n, n + EXTRA, cap), F32)),
-            [SMEM] * 2 + [VMEM] * (1 + len(refs)),
-        )(pos, lev, given_mix, *refs)
+            [SMEM] + [VMEM] * (1 + len(refs)),
+            cost=pl.CostEstimate(flops=10**9, bytes_accessed=0, transcendentals=0),
+        )(pos, given_mix, *refs)
         slots.append(new)
         increment, grad_static = call(
-            functools.partial(outputs_kernel, stages), (flat, flat), [SMEM] * 2 + [VMEM] * (len(slots) + 7)
-        )(pos, lev, *slots, remap, tables, static_control, diag, off, obs_weight, innovation)
+            functools.partial(outputs_kernel, stages), (flat, flat), [SMEM] + [VMEM] * (len(slots) + 7)
+        )(pos, *slots, remap, tables, static_control, diag, off, obs_weight, innovation)
     else:
         other_perturb = lax.ppermute(perturb, "lev", swap)
         payload = call(

time: 28.2 us -> 26.6 us (0.943)
  starting transfers between devices: 15.2 us -> 12 us
  waiting for transfers between devices: 3.68 us -> 5.56 us
  Pallas kernels: 6.96 us -> 6.67 us
    ppermute x7 -> x5, starting transfers between devices: 11.6 us -> 8.4 us  [to(): return lax.ppermute(blocks[r], 'tile', [(i, i ^ r) for i in range(n)])]
    ppermute x7 -> x5, waiting for transfers between devices: 2.49 us -> 4.31 us  [to(): return lax.ppermute(blocks[r], 'tile', [(i, i ^ r) for i in range(n)])]
    pallas_call x1, Pallas kernels: 1.51 us -> 1.04 us  [body(): call(functools.partial(shared_kernel, n, levels, band_cols, tile_cols, st...]
  transfers between devices with their start and end apart: 11 -> 9, of which waited for: 5 -> 6; matrix products, arithmetic and copies ran while one was open for 0% -> 0% of each run, Pallas kernels for 15% -> 17%
where the time goes in v19:
time: 26.6 us; the launch traced here: 26.4 us
  starting transfers between devices  12 us (45%)
  Pallas kernels  6.67 us (25%)
  waiting for transfers between devices  5.56 us (21%)
  local copies, waits for them, and re-layouts  1.39 us (5%)
  between operations  0.78 us (3%)
    ppermute x5, starting transfers between devices, to(): return lax.ppermute(blocks[r], 'tile', [(i, i ^ r) for i in range(n)])  8.4 us
    ppermute x5, waiting for transfers between devices, to(): return lax.ppermute(blocks[r], 'tile', [(i, i ^ r) for i in range(n)])  4.31 us
    ppermute x1, starting transfers between devices, body(): lax.ppermute(sums[0], 'grp', [(g, (g + k) % groups) for g in range(groups)])  2.97 us
    pallas_call x2, Pallas kernels, body(): call(functools.partial(stage_kernel, n, levels, band_cols, tile_cols, sta...  1.67 us
    unnamed x24, local copies, waits for them, and re-layouts  1.39 us
    pallas_call x1, Pallas kernels, body(): call(ens_kernel, (shape(control.shape, F32), flat, flat), [VMEM] * 5, [pl...  1.24 us
    pallas_call x1, Pallas kernels, body(): call(functools.partial(static_kernel, band_cols), [shape((rows.total, cap...  1.11 us
    pallas_call x1, Pallas kernels, body(): call(functools.partial(shared_kernel, n, levels, band_cols, tile_cols, st...  1.04 us
  transfers between devices with their start and end apart: 9, of which 6 were waited for; matrix products, arithmetic and copies ran while one was open for 0% of the time, Pallas kernels for 17%

profile of v19, /device:TPU:0, one launch (start us, length us, event | category | flops | bytes accessed | tf_op | source)
XLA Modules:
  0.0 26.4 jit_solution(14667568074472978941)
XLA Ops:
  0.6 0.5 %collective-permute-start = (f32[16,40,256]{2,1,0:T(8,128)}, f32[16,40,256]{2,1,0:T(8,128)S(1)}, u32[]{:S(2)}, u32[]{:S(2)}) collective-permute-start(f32[16,40,256]{2,1,0:T(8,128)} %control_ref.3), channel_id=1, source_target_pairs={{0,1},{1,0},{2,3},{3,2},{4,5},{5,4},{6,7},{7,6},{8,9},{9,8},{10,11... | collective-permute-start | bytes 1966088 | tf_op jit(solution)/shard_map/ppermute | solution.py:494
  1.1 0.1 collective-permute-start.1
  1.2 0.0 copy-start.11
  1.2 0.7 %copy-done.11 = f32[16,32]{1,0:T(8,128)S(1)} copy-done((f32[16,32]{1,0:T(8,128)S(1)}, f32[16,32]{1,0:T(8,128)}, u32[]{:S(2)}) %copy-start.11) | copy-done | bytes 2072
  1.9 0.0 copy-start
  1.9 0.0 copy-start.1
  1.9 0.2 shard_map.139
  2.2 0.9 %collective-permute-done.other_ref = f32[16,40,256]{2,1,0:T(8,128)S(1)} collective-permute-done((f32[16,40,256]{2,1,0:T(8,128)}, f32[16,40,256]{2,1,0:T(8,128)S(1)}, u32[]{:S(2)}, u32[]{:S(2)}) %collective-permute-start) | collective-permute-done | bytes 655392 | tf_op jit(solution)/shard_map/ppermute | solution.py:494
  3.1 0.0 copy-done
  3.1 0.0 copy-done.1
  3.1 0.0 copy-start.2
  3.1 0.0 copy-start.3
  3.1 0.0 copy-start.4
  3.1 0.0 copy-start.7
  3.1 0.0 copy-start.8
  3.1 0.0 copy-start.9
  3.1 0.5 %shard_map.140.refs_0_ = f32[16,256]{1,0:T(8,128)S(1)} custom-call(bf16[16,40,256]{2,1,0:T(8,128)(2,1)S(1)} %copy-done.1, f32[16,40,256]{2,1,0:T(8,128)S(1)} %copy-done, f32[16,40,256]{2,1,0:T(8,128)S(1)} %collective-permute-done.other_ref, bf16[2,128,256]{2,1,0:T(8,128)(2,1)S(1)} %get-tuple-element.39.mix_ref), custom_call_target="tpu_custom_call" | custom-call | tf_op jit(solution)/shard_map/pallas_call | solution.py:502
  3.6 0.0 collective-permute-done.1.perturb_ref
  3.7 3.0 %collective-permute-start.2 = (f32[16,256]{1,0:T(8,128)S(1)}, f32[16,256]{1,0:T(8,128)S(1)}, u32[]{:S(2)}, u32[]{:S(2)}) collective-permute-start(f32[16,256]{1,0:T(8,128)S(1)} %shard_map.140.refs_0_), channel_id=1, source_target_pairs={{0,16},{16,0},{1,17},{17,1},{2,18},{18,2},{3,19},{19,3},{4,20},{20... | collective-permute-start | bytes 49160 | tf_op jit(solution)/shard_map/ppermute | solution.py:515
  6.6 0.0 copy-done.2
  6.6 0.0 copy-done.3
  6.6 0.0 copy-done.4
  6.7 0.0 copy-done.7
  6.7 0.0 copy-done.8
  6.7 0.0 copy-done.9
  6.7 0.6 %copy-done.6 = f32[1024]{0:T(1024)S(1)} copy-done((f32[1024]{0:T(1024)S(1)}, f32[1024]{0:T(1024)}, u32[]{:S(2)}) %copy-start.6) | copy-done | bytes 4120
  7.3 0.0 copy-done.5
  7.3 0.0 copy-done.10
  7.3 1.1 %shard_map.141 = (f32[56,128]{1,0:T(8,128)S(1)}, f32[56,128]{1,0:T(8,128)S(1)}, f32[56,128]{1,0:T(8,128)S(1)}, f32[56,128]{1,0:T(8,128)S(1)}, f32[56,128]{1,0:T(...) custom-call(s32[1]{0:T(128)} %bitcast.1.pos_ref, s32[1,8]{1,0:T(1,128)S(1)} %copy-done.10, ...), custom_call_target="tpu_custom_call" | custom-call | tf_op jit(solution)/shard_map/pallas_call | solution.py:509
  8.4 0.0 collective-permute-done.2.refs_1_
  8.5 3.1 %collective-permute-start.3 = (f32[152,128]{1,0:T(8,128)S(1)}, f32[152,128]{1,0:T(8,128)S(1)}, u32[]{:S(2)}, u32[]{:S(2)}) collective-permute-start(f32[152,128]{1,0:T(8,128)S(1)} %get-tuple-element.52), channel_id=1, source_target_pairs={{0,8},{2,10},{4,12},{6,14},{8,0},{10,2},{12,4},{14,6},{1,9},{3,11}... | collective-permute-start | bytes 233480 | tf_op jit(solution)/shard_map/ppermute | solution.py:529
  11.5 1.5 %collective-permute-start.4 = (f32[88,128]{1,0:T(8,128)S(1)}, f32[88,128]{1,0:T(8,128)S(1)}, u32[]{:S(2)}, u32[]{:S(2)}) collective-permute-start(f32[88,128]{1,0:T(8,128)S(1)} %get-tuple-element.53), channel_id=1, source_target_pairs={{0,2},{2,0},{4,6},{6,4},{8,10},{10,8},{12,14},{14,12},{1,3},{3,1},... | collective-permute-start | bytes 135176 | tf_op jit(solution)/shard_map/ppermute | solution.py:529
  13.1 0.0 collective-permute-start.5
  13.1 1.5 %collective-permute-done.3.got_ref.refs_2_ = f32[152,128]{1,0:T(8,128)S(1)} collective-permute-done((f32[152,128]{1,0:T(8,128)S(1)}, f32[152,128]{1,0:T(8,128)S(1)}, u32[]{:S(2)}, u32[]{:S(2)}) %collective-permute-start.3) | collective-permute-done | bytes 77856 | tf_op jit(solution)/shard_map/ppermute | solution.py:529
  14.6 3.8 %collective-permute-start.6 = (f32[176,128]{1,0:T(8,128)S(1)}, f32[176,128]{1,0:T(8,128)S(1)}, u32[]{:S(2)}, u32[]{:S(2)}) collective-permute-start(f32[176,128]{1,0:T(8,128)S(1)} %get-tuple-element.57), channel_id=1, source_target_pairs={{0,6},{2,4},{4,2},{6,0},{8,14},{10,12},{12,10},{14,8},{1,7},{3,5},... | collective-permute-start | bytes 270344 | tf_op jit(solution)/shard_map/ppermute | solution.py:529
  18.4 0.0 collective-permute-start.7
  18.4 0.0 collective-permute-done.4.refs_3_
  18.4 0.7 %collective-permute-done.5.refs_4_ = f32[88,128]{1,0:T(8,128)S(1)} collective-permute-done((f32[88,128]{1,0:T(8,128)S(1)}, f32[88,128]{1,0:T(8,128)S(1)}, u32[]{:S(2)}, u32[]{:S(2)}) %collective-permute-start.5) | collective-permute-done | bytes 45088 | tf_op jit(solution)/shard_map/ppermute | solution.py:529
  19.0 1.0 %shard_map.144 = (bf16[8,32,512]{2,1,0:T(8,128)(2,1)S(1)}, f32[4,16,128]{2,1,0:T(8,128)S(1)}, f32[16,1024]{1,0:T(8,128)S(1)}, bf16[8,256,128]{2,1,0:T(8,128)(2,1)S(1)}) custom-call(f32[32,128]{1,0:T(8,128)S(1)} %get-tuple-element.50.refs_0_, f32[56,128]{1,0:T(8,128)S(1)} %get-tuple-element.51.refs_1_, f32[152,128]{1,0:T(8,128)S(1)} %collective-permute-done.3.got_ref.refs_2_, ...), custom_call_target="tpu_custom_call" | custom-call | flops 1000000000 | tf_op jit(solution)/shard_map/pallas_call | solution.py:550
  20.0 1.1 %collective-permute-done.6.refs_5_.refs_6_ = f32[176,128]{1,0:T(8,128)S(1)} collective-permute-done((f32[176,128]{1,0:T(8,128)S(1)}, f32[176,128]{1,0:T(8,128)S(1)}, u32[]{:S(2)}, u32[]{:S(2)}) %collective-permute-start.6) | collective-permute-done | bytes 90144 | tf_op jit(solution)/shard_map/ppermute | solution.py:529
  21.1 0.7 %shard_map.145 = (bf16[8,32,256]{2,1,0:T(8,128)(2,1)S(1)}, f32[6,16,128]{2,1,0:T(8,128)S(1)}, f32[16,1024]{1,0:T(8,128)S(1)}) custom-call(f32[32,128]{1,0:T(8,128)S(1)} %get-tuple-element.50.refs_0_, f32[56,128]{1,0:T(8,128)S(1)} %get-tuple-element.51.refs_1_, f32[152,128]{1,0:T(8,128)S(1)} %collective-permute-done.3.got_ref.refs_2_, ...), custom_call_target="tpu_custom_call" | custom-call | flops 1000000000 | tf_op jit(solution)/shard_map/pallas_call | solution.py:550
  21.8 1.1 %collective-permute-done.7.refs_7_.refs_8_ = f32[176,128]{1,0:T(8,128)S(1)} collective-permute-done((f32[176,128]{1,0:T(8,128)S(1)}, f32[176,128]{1,0:T(8,128)S(1)}, u32[]{:S(2)}, u32[]{:S(2)}) %collective-permute-start.7) | collective-permute-done | bytes 90144 | tf_op jit(solution)/shard_map/ppermute | solution.py:529
  22.9 1.0 %shard_map.146 = (f32[48,128]{1,0:T(8,128)S(1)}, bf16[8,32,256]{2,1,0:T(8,128)(2,1)S(1)}, f32[8,16,128]{2,1,0:T(8,128)S(1)}) custom-call(s32[1]{0:T(128)} %bitcast.1.pos_ref, f32[16,128]{1,0:T(8,128)S(1)} %get-tuple-element.41.mix_ref, f32[32,128]{1,0:T(8,128)S(1)} %get-tuple-element.50.refs_0_, f32[56,128]{1,0:T(8,128)S(1)} %get-tuple-element.51.refs_1_, ...), custom_call_target="tpu_custom_call" | custom-call | flops 1000000000 | tf_op jit(solution)/shard_map/pallas_call | solution.py:561
  23.9 0.0 collective-permute-start.8
  23.9 0.4 %shard_map.147.own_ref = f32[16,40,256]{2,1,0:T(8,128)S(1)} custom-call(bf16[16,40,256]{2,1,0:T(8,128)(2,1)S(1)} %copy-done.1, f32[48,128]{1,0:T(8,128)S(1)} %get-tuple-element.65.mine_ref, bf16[2,128,128]{2,1,0:T(8,128)(2,1)S(1)} %get-tuple-element.66.weights_ref, f32[16,40,256]{2,1,0:T(8,128)S(1)} %copy-done), custom_call_target="tpu_custom_call" | custom-call | tf_op jit(solution)/shard_map/pallas_call | solution.py:590
  24.4 0.4 %shard_map.148 = (f32[16,1024]{1,0:T(8,128)S(1)}, f32[16,1024]{1,0:T(8,128)S(1)}) custom-call(s32[1]{0:T(128)} %bitcast.1.pos_ref, bf16[8,32,512]{2,1,0:T(8,128)(2,1)S(1)} %get-tuple-element.59.refs_7_.refs_9_.refs_0_, bf16[8,32,256]{2,1,0:T(8,128)(2,1)S(1)} %get-tuple-element.62.refs_10_.refs_1_, bf16[8,32,256]{2,1,0:T(8,128)(2,1)S(1)} %get-tuple-element.67.refs_2_, ...), custom_call_target="tpu_custom_call" | custom-call | tf_op jit(solution)/shard_map/pallas_call | solution.py:568
  24.8 0.3 %collective-permute-done.8.theirs_ref = f32[48,128]{1,0:T(8,128)S(1)} collective-permute-done((f32[48,128]{1,0:T(8,128)S(1)}, f32[48,128]{1,0:T(8,128)S(1)}, u32[]{:S(2)}, u32[]{:S(2)}) %collective-permute-start.8) | collective-permute-done | bytes 24608 | tf_op jit(solution)/shard_map/ppermute | solution.py:589
  25.1 1.2 %shard_map.149 = (f32[16,40,256]{2,1,0:T(8,128)}, f32[16,1024]{1,0:T(8,128)}, f32[16,1024]{1,0:T(8,128)}) custom-call(bf16[16,40,256]{2,1,0:T(8,128)(2,1)S(1)} %collective-permute-done.1.perturb_ref, f32[48,128]{1,0:T(8,128)S(1)} %collective-permute-done.8.theirs_ref, f32[16,40,256]{2,1,0:T(8,128)S(1)} %shard_map.147.own_ref, ...), custom_call_target="tpu_custom_call" | custom-call | tf_op jit(solution)/shard_map/pallas_call | solution.py:591
  (5 shorter events, 0.0 us)
Async XLA Ops:
  0.6 2.5 %collective-permute-start = (f32[16,40,256]{2,1,0:T(8,128)}, f32[16,40,256]{2,1,0:T(8,128)S(1)}, u32[]{:S(2)}, u32[]{:S(2)}) collective-permute-start(f32[16,40,256]{2,1,0:T(8,128)} %control_ref.3), channel_id=1, source_target_pairs={{0,1},{1,0},{2,3},{3,2},{4,5},{5,4},{6,7},{7,6},{8,9},{9,8},{10,11... | collective-permute-start | bytes 1966088 | tf_op jit(solution)/shard_map/ppermute | solution.py:494
  1.1 2.5 %collective-permute-start.1 = (bf16[16,40,256]{2,1,0:T(8,128)(2,1)}, bf16[16,40,256]{2,1,0:T(8,128)(2,1)S(1)}, u32[]{:S(2)}, u32[]{:S(2)}) collective-permute-start(bf16[16,40,256]{2,1,0:T(8,128)(2,1)} %perturb_ref.3), channel_id=1, source_target_pairs={{0,1},{1,0},{2,3},{3,2},{4,5},{5,4},{6,7},{7,6},{8,9},{9,8},{10,11... | collective-permute-start | bytes 983048 | tf_op jit(solution)/shard_map/ppermute | solution.py:513
  1.2 0.7 %copy-start.11 = (f32[16,32]{1,0:T(8,128)S(1)}, f32[16,32]{1,0:T(8,128)}, u32[]{:S(2)}) copy-start(f32[16,32]{1,0:T(8,128)} %loc_ref.1) | copy-start | bytes 6148
  1.9 1.2 %copy-start = (f32[16,40,256]{2,1,0:T(8,128)S(1)}, f32[16,40,256]{2,1,0:T(8,128)}, u32[]{:S(2)}) copy-start(f32[16,40,256]{2,1,0:T(8,128)} %control_ref.3) | copy-start | bytes 1966084
  1.9 1.2 %copy-start.1 = (bf16[16,40,256]{2,1,0:T(8,128)(2,1)S(1)}, bf16[16,40,256]{2,1,0:T(8,128)(2,1)}, u32[]{:S(2)}) copy-start(bf16[16,40,256]{2,1,0:T(8,128)(2,1)} %perturb_ref.3) | copy-start | bytes 983044
  3.1 3.5 %copy-start.2 = (f32[16,1024]{1,0:T(8,128)S(1)}, f32[16,1024]{1,0:T(8,128)}, u32[]{:S(2)}) copy-start(f32[16,1024]{1,0:T(8,128)} %refs_5_.1) | copy-start | bytes 196612
  3.1 3.5 %copy-start.3 = (f32[16,1024]{1,0:T(8,128)S(1)}, f32[16,1024]{1,0:T(8,128)}, u32[]{:S(2)}) copy-start(f32[16,1024]{1,0:T(8,128)} %refs_8_.1) | copy-start | bytes 196612
  3.1 3.5 %copy-start.4 = (f32[16,1024]{1,0:T(8,128)S(1)}, f32[16,1024]{1,0:T(8,128)}, u32[]{:S(2)}) copy-start(f32[16,1024]{1,0:T(8,128)} %refs_9_.1) | copy-start | bytes 196612
  3.1 3.5 %copy-start.7 = (s32[1,8,128]{2,1,0:T(8,128)S(1)}, s32[1,8,128]{2,1,0:T(8,128)}, u32[]{:S(2)}) copy-start(s32[1,8,128]{2,1,0:T(8,128)} %src_ref.1) | copy-start | bytes 12292
  3.1 3.5 %copy-start.8 = (f32[1,8,128]{2,1,0:T(8,128)S(1)}, f32[1,8,128]{2,1,0:T(8,128)}, u32[]{:S(2)}) copy-start(f32[1,8,128]{2,1,0:T(8,128)} %weight_ref.1) | copy-start | bytes 12292
  3.1 3.5 %copy-start.9 = (s32[1,8,128]{2,1,0:T(8,128)S(1)}, s32[1,8,128]{2,1,0:T(8,128)}, u32[]{:S(2)}) copy-start(s32[1,8,128]{2,1,0:T(8,128)} %tgt_ref.1) | copy-start | bytes 12292
  3.7 4.8 %collective-permute-start.2 = (f32[16,256]{1,0:T(8,128)S(1)}, f32[16,256]{1,0:T(8,128)S(1)}, u32[]{:S(2)}, u32[]{:S(2)}) collective-permute-start(f32[16,256]{1,0:T(8,128)S(1)} %shard_map.140.refs_0_), channel_id=1, source_target_pairs={{0,16},{16,0},{1,17},{17,1},{2,18},{18,2},{3,19},{19,3},{4,20},{20... | collective-permute-start | bytes 49160 | tf_op jit(solution)/shard_map/ppermute | solution.py:515
  6.6 0.7 %copy-start.6 = (f32[1024]{0:T(1024)S(1)}, f32[1024]{0:T(1024)}, u32[]{:S(2)}) copy-start(f32[1024]{0:T(1024)} %param.17) | copy-start | bytes 12292
  6.6 0.7 %copy-start.5 = (f32[1024]{0:T(1024)S(1)}, f32[1024]{0:T(1024)}, u32[]{:S(2)}) copy-start(f32[1024]{0:T(1024)} %param.16) | copy-start | bytes 12292
  6.6 0.7 %copy-start.10 = (s32[1,8]{1,0:T(1,128)S(1)}, s32[1,8]{1,0:T(1,128)}, u32[]{:S(2)}) copy-start(s32[1,8]{1,0:T(1,128)} %counts_ref.1) | copy-start | bytes 100
  8.5 6.1 %collective-permute-start.3 = (f32[152,128]{1,0:T(8,128)S(1)}, f32[152,128]{1,0:T(8,128)S(1)}, u32[]{:S(2)}, u32[]{:S(2)}) collective-permute-start(f32[152,128]{1,0:T(8,128)S(1)} %get-tuple-element.52), channel_id=1, source_target_pairs={{0,8},{2,10},{4,12},{6,14},{8,0},{10,2},{12,4},{14,6},{1,9},{3,11}... | collective-permute-start | bytes 233480 | tf_op jit(solution)/shard_map/ppermute | solution.py:529
  11.5 6.8 %collective-permute-start.4 = (f32[88,128]{1,0:T(8,128)S(1)}, f32[88,128]{1,0:T(8,128)S(1)}, u32[]{:S(2)}, u32[]{:S(2)}) collective-permute-start(f32[88,128]{1,0:T(8,128)S(1)} %get-tuple-element.53), channel_id=1, source_target_pairs={{0,2},{2,0},{4,6},{6,4},{8,10},{10,8},{12,14},{14,12},{1,3},{3,1},... | collective-permute-start | bytes 135176 | tf_op jit(solution)/shard_map/ppermute | solution.py:529
  13.1 5.9 %collective-permute-start.5 = (f32[88,128]{1,0:T(8,128)S(1)}, f32[88,128]{1,0:T(8,128)S(1)}, u32[]{:S(2)}, u32[]{:S(2)}) collective-permute-start(f32[88,128]{1,0:T(8,128)S(1)} %get-tuple-element.54), channel_id=1, source_target_pairs={{0,10},{2,8},{4,14},{6,12},{8,2},{10,0},{12,6},{14,4},{1,11},{3,9}... | collective-permute-start | bytes 135176 | tf_op jit(solution)/shard_map/ppermute | solution.py:529
  14.6 6.5 %collective-permute-start.6 = (f32[176,128]{1,0:T(8,128)S(1)}, f32[176,128]{1,0:T(8,128)S(1)}, u32[]{:S(2)}, u32[]{:S(2)}) collective-permute-start(f32[176,128]{1,0:T(8,128)S(1)} %get-tuple-element.57), channel_id=1, source_target_pairs={{0,6},{2,4},{4,2},{6,0},{8,14},{10,12},{12,10},{14,8},{1,7},{3,5},... | collective-permute-start | bytes 270344 | tf_op jit(solution)/shard_map/ppermute | solution.py:529
  18.4 4.5 %collective-permute-start.7 = (f32[176,128]{1,0:T(8,128)S(1)}, f32[176,128]{1,0:T(8,128)S(1)}, u32[]{:S(2)}, u32[]{:S(2)}) collective-permute-start(f32[176,128]{1,0:T(8,128)S(1)} %get-tuple-element.58), channel_id=1, source_target_pairs={{0,4},{2,6},{4,0},{6,2},{8,12},{10,14},{12,8},{14,10},{1,5},{3,7},... | collective-permute-start | bytes 270344 | tf_op jit(solution)/shard_map/ppermute | solution.py:529
  23.9 1.2 %collective-permute-start.8 = (f32[48,128]{1,0:T(8,128)S(1)}, f32[48,128]{1,0:T(8,128)S(1)}, u32[]{:S(2)}, u32[]{:S(2)}) collective-permute-start(f32[48,128]{1,0:T(8,128)S(1)} %get-tuple-element.65.mine_ref), channel_id=1, source_target_pairs={{0,1},{1,0},{2,3},{3,2},{4,5},{5,4},{6,7},{7,6},{8,9},{9,8},{10,11... | collective-permute-start | bytes 73736 | tf_op jit(solution)/shard_map/ppermute | solution.py:589

commit v20 on v19

--- a/solution.py
+++ b/solution.py
@@ -280,24 +280,21 @@
         out_ref[...] = jnp.concatenate(parts, axis=0)
 
 
-def relay_kernel(levels, stacked, got_ref, *refs):
-    count = len(refs) // 2
-    head = refs[0].shape[0]
-    for i, (block_ref, out_ref) in enumerate(zip(refs[:count], refs[count:])):
+def relay_kernel(levels, stacked, got_ref, *out_refs):
+    head = got_ref.shape[0] - len(out_refs) * 2 * levels
+    for i, out_ref in enumerate(out_refs):
         at = head + 2 * levels * i
         out_ref[...] = jnp.concatenate(
-            [block_ref[...], got_ref[:stacked, :], got_ref[at : at + 2 * levels, :], got_ref[stacked + 2 * levels : head, :]],
-            axis=0,
+            [got_ref[:stacked, :], got_ref[at : at + 2 * levels, :], got_ref[stacked + 2 * levels : head, :]], axis=0
         )
 
 
 class Block:
-    def __init__(self, refs, n, levels, band, base=0):
+    def __init__(self, refs, n, levels, band):
         cap = refs[0].shape[1]
         self.levels, self.parts, self.cap = levels, band // cap, cap
         self.sums_ref, self.rest_ref = refs[0], refs[-1]
-        self.base = base
-        self.head = 0 if len(refs) == 2 else base + self.parts * levels
+        self.head = 0 if len(refs) == 2 else self.parts * levels
         self.rows = Rows(levels, n)
         words = self.rest(self.rows.index, n)
         self.tgt = jnp.floor((words + 0.5) * (1.0 / band))
@@ -308,7 +305,7 @@
         return self.rest_ref[self.head + at : self.head + at + size, :]
 
     def sums(self):
-        parts = [self.sums_ref[self.base + i * self.levels : self.base + (i + 1) * self.levels, :] for i in range(self.parts)]
+        parts = [self.sums_ref[i * self.levels : (i + 1) * self.levels, :] for i in range(self.parts)]
         return jnp.concatenate(halves(jnp.concatenate(parts, axis=1)), axis=0)
 
 
@@ -354,8 +351,7 @@
     blocks = {0: Block(refs[:2], n, levels, band)}
     refs = refs[2:]
     for i, r in enumerate(labels[1:]):
-        base = refs[i].shape[0] // 2 if r >= n // 2 + n // 4 else 0
-        blocks[r] = Block(refs[i : i + 1], n, levels, band, base)
+        blocks[r] = Block(refs[i : i + 1], n, levels, band)
     return blocks, refs[len(labels) - 1 :]
 
 
@@ -503,7 +499,7 @@
     flat = shape((levels, tile_cols), F32)
     mine_shape = shape((band_cols // width * levels + levels, width), F32)
     diag, off = filter_diag.reshape(1, -1), filter_off.reshape(1, -1)
-    if n * cap <= tile_cols and n >= 8 and lax.axis_size("lev") == 2 and n & (n - 1) == 0 and band_cols * tile_cols <= 2**20:
+    if n * cap <= tile_cols and n >= 4 and lax.axis_size("lev") == 2 and n & (n - 1) == 0 and band_cols * tile_cols <= 2**20:
         rows = Rows(levels, n)
         stacked = band_cols // cap * levels
         rests = call(functools.partial(static_kernel, band_cols), [shape((rows.total, cap), F32)] * n, [SMEM] * 2 + [VMEM] * 8)(
@@ -513,31 +509,27 @@
         sums[0], other_perturb = lax.optimization_barrier((sums[0], lax.ppermute(perturb, "lev", swap)))
         for k in range(1, groups):
             sums.append(lax.ppermute(sums[0], "grp", [(g, (g + k) % groups) for g in range(groups)]))
-        low, high = n // 4, n // 2
-        order = [high, *range(1, low), *range(high + 1, high + low), *reversed(range(low, high))]
-        stages = [[0] + order[: -low], *([r, r + high] for r in order[-low:])]
-        direct = order[::-1]
+        high = n // 2
+        near = list(range(1, high))
+        stages = [[0, *near], [high, *(r + high for r in reversed(near[1:]))], [high + 1]]
+        block = stacked + rows.total
         total, *blocks = call(
-            functools.partial(blocks_kernel, groups, levels, low),
+            functools.partial(blocks_kernel, groups, levels, high - 1),
             [shape((stacked, cap), F32)]
-            + [shape((stacked + rows.total + (r == high) * 2 * levels * low, cap), F32) for r in direct],
-            [VMEM] * (groups + len(direct) + low),
-        )(*sums, *[rests[r] for r in direct], *rests[high + low :])
-        blocks = dict(zip(direct, blocks))
-
-        def to(r):
-            return lax.ppermute(blocks[r], "tile", [(i, i ^ r) for i in range(n)])
-
-        arrived = {0: [total, rests[0]]} | {r: [to(r)] for r in order[:-low]}
-        carriers = list(range(low, high))
-        joined = call(
-            functools.partial(relay_kernel, levels, stacked),
-            [shape((2 * (stacked + rows.total), cap), F32)] * low,
-            [VMEM] * (1 + low),
-        )(arrived[high][0], *[blocks[r] for r in carriers])
-        blocks |= dict(zip(carriers, joined))
-        for r in order[-low:]:
-            arrived[r] = arrived[r + high] = [to(r)]
+            + [shape((block, cap), F32)] * (high - 1)
+            + [shape((block + 2 * levels * (high - 1), cap), F32)],
+            [VMEM] * (groups + n - 1),
+        )(*sums, *rests[1:])
+
+        def to(r, block):
+            return [lax.ppermute(block, "tile", [(i, i ^ r) for i in range(n)])]
+
+        arrived = {0: [total, rests[0]]} | {r: to(r, blocks[r - 1]) for r in (high, *near)}
+        passed = call(
+            functools.partial(relay_kernel, levels, stacked), [shape((block, cap), F32)] * (high - 1), [VMEM]
+        )(*arrived[high])
+        for r in reversed(near):
+            arrived[r + high] = to(r, passed[r - 1])
         slots, carried, picks = [], [], []
         for count in range(1, len(stages)):
             labels = sum(stages[:count], [])
@@ -551,7 +543,7 @@
                 functools.partial(stage_kernel, n, levels, band_cols, tile_cols, stages[:count]),
                 outs,
                 [VMEM] * (len(refs) + len(slots) + len(carried)),
-                cost=pl.CostEstimate(flops=10**9, bytes_accessed=0, transcendentals=0),
+                cost=pl.CostEstimate(flops=(10**9, 10**6)[count - 1], bytes_accessed=0, transcendentals=0),
             )(*refs, *slots, *carried)
             slots.append(new)
             picks += carried[2:]

time: 26.6 us -> 26.6 us (level)
  waiting for transfers between devices: 5.56 us -> 3.79 us
  starting transfers between devices: 12 us -> 13.7 us
    ppermute x5 -> x7, waiting for transfers between devices: 4.31 us -> 2.44 us  [to(): return [lax.ppermute(block, 'tile', [(i, i ^ r) for i in range(n)])]]
    ppermute x5 -> x7, starting transfers between devices: 8.4 us -> 10.2 us  [to(): return [lax.ppermute(block, 'tile', [(i, i ^ r) for i in range(n)])]]
  transfers between devices with their start and end apart: 9 -> 11, of which waited for: 6 -> 6; matrix products, arithmetic and copies ran while one was open for 0% -> 0% of each run, Pallas kernels for 17% -> 17%
where the time goes in v20:
time: 26.6 us; the launch traced here: 26.4 us
  starting transfers between devices  13.7 us (52%)
  Pallas kernels  6.65 us (25%)
  waiting for transfers between devices  3.79 us (14%)
  local copies, waits for them, and re-layouts  1.39 us (5%)
  between operations  0.79 us (3%)
    ppermute x7, starting transfers between devices, to(): return [lax.ppermute(block, 'tile', [(i, i ^ r) for i in range(n)])]  10.2 us
    ppermute x1, starting transfers between devices, body(): lax.ppermute(sums[0], 'grp', [(g, (g + k) % groups) for g in range(groups)])  2.97 us
    ppermute x7, waiting for transfers between devices, to(): return [lax.ppermute(block, 'tile', [(i, i ^ r) for i in range(n)])]  2.44 us
    pallas_call x2, Pallas kernels, body(): call(functools.partial(stage_kernel, n, levels, band_cols, tile_cols, sta...  1.9 us
    unnamed x24, local copies, waits for them, and re-layouts  1.39 us
    pallas_call x1, Pallas kernels, body(): call(ens_kernel, (shape(control.shape, F32), flat, flat), [VMEM] * 5, [pl...  1.25 us
    pallas_call x1, Pallas kernels, body(): call(functools.partial(static_kernel, band_cols), [shape((rows.total, cap...  1.11 us
    ppermute x1, waiting for transfers between devices, body(): other_control = lax.ppermute(control, 'lev', swap)  0.9 us
  transfers between devices with their start and end apart: 11, of which 6 were waited for; matrix products, arithmetic and copies ran while one was open for 0% of the time, Pallas kernels for 17%

profile of v20, /device:TPU:0, one launch (start us, length us, event | category | flops | bytes accessed | tf_op | source)
XLA Modules:
  0.0 26.4 jit_solution(10363623619713826030)
XLA Ops:
  0.6 0.5 %collective-permute-start = (f32[16,40,256]{2,1,0:T(8,128)}, f32[16,40,256]{2,1,0:T(8,128)S(1)}, u32[]{:S(2)}, u32[]{:S(2)}) collective-permute-start(f32[16,40,256]{2,1,0:T(8,128)} %control_ref.3), channel_id=1, source_target_pairs={{0,1},{1,0},{2,3},{3,2},{4,5},{5,4},{6,7},{7,6},{8,9},{9,8},{10,11... | collective-permute-start | bytes 1966088 | tf_op jit(solution)/shard_map/ppermute | solution.py:490
  1.1 0.1 collective-permute-start.1
  1.2 0.0 copy-start.11
  1.2 0.7 %copy-done.11 = f32[16,32]{1,0:T(8,128)S(1)} copy-done((f32[16,32]{1,0:T(8,128)S(1)}, f32[16,32]{1,0:T(8,128)}, u32[]{:S(2)}) %copy-start.11) | copy-done | bytes 2072
  1.9 0.0 copy-start
  1.9 0.2 shard_map.139
  2.2 0.9 %collective-permute-done.other_ref = f32[16,40,256]{2,1,0:T(8,128)S(1)} collective-permute-done((f32[16,40,256]{2,1,0:T(8,128)}, f32[16,40,256]{2,1,0:T(8,128)S(1)}, u32[]{:S(2)}, u32[]{:S(2)}) %collective-permute-start) | collective-permute-done | bytes 655392 | tf_op jit(solution)/shard_map/ppermute | solution.py:490
  3.1 0.0 copy-done
  3.1 0.0 copy-done.1
  3.1 0.0 copy-start.7
  3.1 0.0 copy-start.8
  3.1 0.0 copy-start.9
  3.1 0.5 %shard_map.140.refs_0_ = f32[16,256]{1,0:T(8,128)S(1)} custom-call(bf16[16,40,256]{2,1,0:T(8,128)(2,1)S(1)} %copy-done.1, f32[16,40,256]{2,1,0:T(8,128)S(1)} %copy-done, f32[16,40,256]{2,1,0:T(8,128)S(1)} %collective-permute-done.other_ref, bf16[2,128,256]{2,1,0:T(8,128)(2,1)S(1)} %get-tuple-element.39.mix_ref), custom_call_target="tpu_custom_call" | custom-call | tf_op jit(solution)/shard_map/pallas_call | solution.py:498
  3.6 0.0 collective-permute-done.1.perturb_ref
  3.7 3.0 %collective-permute-start.2 = (f32[16,256]{1,0:T(8,128)S(1)}, f32[16,256]{1,0:T(8,128)S(1)}, u32[]{:S(2)}, u32[]{:S(2)}) collective-permute-start(f32[16,256]{1,0:T(8,128)S(1)} %shard_map.140.refs_0_), channel_id=1, source_target_pairs={{0,16},{16,0},{1,17},{17,1},{2,18},{18,2},{3,19},{19,3},{4,20},{20... | collective-permute-start | bytes 49160 | tf_op jit(solution)/shard_map/ppermute | solution.py:511
  6.6 0.0 copy-done.2
  6.6 0.0 copy-done.3
  6.6 0.0 copy-done.4
  6.7 0.0 copy-done.7
  6.7 0.0 copy-done.8
  6.7 0.0 copy-done.9
  6.7 0.6 %copy-done.6 = f32[1024]{0:T(1024)S(1)} copy-done((f32[1024]{0:T(1024)S(1)}, f32[1024]{0:T(1024)}, u32[]{:S(2)}) %copy-start.6) | copy-done | bytes 4120
  7.3 0.0 copy-done.5
  7.3 0.0 copy-done.10
  7.3 1.1 %shard_map.141 = (f32[56,128]{1,0:T(8,128)S(1)}, f32[56,128]{1,0:T(8,128)S(1)}, f32[56,128]{1,0:T(8,128)S(1)}, f32[56,128]{1,0:T(8,128)S(1)}, f32[56,128]{1,0:T(...) custom-call(s32[1]{0:T(128)} %bitcast.1.pos_ref, s32[1,8]{1,0:T(1,128)S(1)} %copy-done.10, ...), custom_call_target="tpu_custom_call" | custom-call | tf_op jit(solution)/shard_map/pallas_call | solution.py:505
  8.4 0.0 collective-permute-done.2.refs_1_
  8.5 3.1 %collective-permute-start.6 = (f32[184,128]{1,0:T(8,128)S(1)}, f32[184,128]{1,0:T(8,128)S(1)}, u32[]{:S(2)}, u32[]{:S(2)}) collective-permute-start(f32[184,128]{1,0:T(8,128)S(1)} %get-tuple-element.55), channel_id=1, source_target_pairs={{0,8},{2,10},{4,12},{6,14},{8,0},{10,2},{12,4},{14,6},{1,9},{3,11}... | collective-permute-start | bytes 282632 | tf_op jit(solution)/shard_map/ppermute | solution.py:525
  11.5 1.5 %collective-permute-start.3 = (f32[88,128]{1,0:T(8,128)S(1)}, f32[88,128]{1,0:T(8,128)S(1)}, u32[]{:S(2)}, u32[]{:S(2)}) collective-permute-start(f32[88,128]{1,0:T(8,128)S(1)} %get-tuple-element.52), channel_id=1, source_target_pairs={{0,2},{2,0},{4,6},{6,4},{8,10},{10,8},{12,14},{14,12},{1,3},{3,1},... | collective-permute-start | bytes 135176 | tf_op jit(solution)/shard_map/ppermute | solution.py:525
  13.1 1.6 %collective-permute-start.4 = (f32[88,128]{1,0:T(8,128)S(1)}, f32[88,128]{1,0:T(8,128)S(1)}, u32[]{:S(2)}, u32[]{:S(2)}) collective-permute-start(f32[88,128]{1,0:T(8,128)S(1)} %get-tuple-element.53), channel_id=1, source_target_pairs={{0,4},{2,6},{4,0},{6,2},{8,12},{10,14},{12,8},{14,10},{1,5},{3,7},... | collective-permute-start | bytes 135176 | tf_op jit(solution)/shard_map/ppermute | solution.py:525
  14.6 0.4 %collective-permute-start.5 = (f32[88,128]{1,0:T(8,128)S(1)}, f32[88,128]{1,0:T(8,128)S(1)}, u32[]{:S(2)}, u32[]{:S(2)}) collective-permute-start(f32[88,128]{1,0:T(8,128)S(1)} %get-tuple-element.54), channel_id=1, source_target_pairs={{0,6},{2,4},{4,2},{6,0},{8,14},{10,12},{12,10},{14,8},{1,7},{3,5},... | collective-permute-start | bytes 135176 | tf_op jit(solution)/shard_map/ppermute | solution.py:525
  15.0 0.3 %collective-permute-done.6.got_ref.refs_5_ = f32[184,128]{1,0:T(8,128)S(1)} collective-permute-done((f32[184,128]{1,0:T(8,128)S(1)}, f32[184,128]{1,0:T(8,128)S(1)}, u32[]{:S(2)}, u32[]{:S(2)}) %collective-permute-start.6) | collective-permute-done | bytes 94240 | tf_op jit(solution)/shard_map/ppermute | solution.py:525
  15.4 2.3 %collective-permute-start.7 = (f32[88,128]{1,0:T(8,128)S(1)}, f32[88,128]{1,0:T(8,128)S(1)}, u32[]{:S(2)}, u32[]{:S(2)}) collective-permute-start(f32[88,128]{1,0:T(8,128)S(1)} %get-tuple-element.56), channel_id=1, source_target_pairs={{0,6},{2,4},{4,2},{6,0},{8,14},{10,12},{12,10},{14,8},{1,7},{3,5},... | collective-permute-start | bytes 135176 | tf_op jit(solution)/shard_map/ppermute | solution.py:525
  17.6 1.3 %collective-permute-start.8 = (f32[88,128]{1,0:T(8,128)S(1)}, f32[88,128]{1,0:T(8,128)S(1)}, u32[]{:S(2)}, u32[]{:S(2)}) collective-permute-start(f32[88,128]{1,0:T(8,128)S(1)} %get-tuple-element.57), channel_id=1, source_target_pairs={{0,4},{2,6},{4,0},{6,2},{8,12},{10,14},{12,8},{14,10},{1,5},{3,7},... | collective-permute-start | bytes 135176 | tf_op jit(solution)/shard_map/ppermute | solution.py:525
  19.0 0.0 collective-permute-done.3.refs_2_
  19.0 0.0 collective-permute-start.9
  19.0 0.0 collective-permute-done.4.refs_3_
  19.0 1.1 %collective-permute-done.5.refs_4_ = f32[88,128]{1,0:T(8,128)S(1)} collective-permute-done((f32[88,128]{1,0:T(8,128)S(1)}, f32[88,128]{1,0:T(8,128)S(1)}, u32[]{:S(2)}, u32[]{:S(2)}) %collective-permute-start.5) | collective-permute-done | bytes 45088 | tf_op jit(solution)/shard_map/ppermute | solution.py:525
  20.1 1.0 %shard_map.144 = (bf16[8,32,512]{2,1,0:T(8,128)(2,1)S(1)}, f32[4,16,128]{2,1,0:T(8,128)S(1)}, f32[16,1024]{1,0:T(8,128)S(1)}, bf16[8,256,128]{2,1,0:T(8,128)(2,1)S(1)}) custom-call(f32[32,128]{1,0:T(8,128)S(1)} %get-tuple-element.50.refs_0_, f32[56,128]{1,0:T(8,128)S(1)} %get-tuple-element.51.refs_1_, f32[88,128]{1,0:T(8,128)S(1)} %collective-permute-done.3.refs_2_, ...), custom_call_target="tpu_custom_call" | custom-call | flops 1000000000 | tf_op jit(solution)/shard_map/pallas_call | solution.py:542
  21.0 0.0 collective-permute-done.7.refs_6_
  21.0 0.7 %collective-permute-done.8.refs_7_ = f32[88,128]{1,0:T(8,128)S(1)} collective-permute-done((f32[88,128]{1,0:T(8,128)S(1)}, f32[88,128]{1,0:T(8,128)S(1)}, u32[]{:S(2)}, u32[]{:S(2)}) %collective-permute-start.8) | collective-permute-done | bytes 45088 | tf_op jit(solution)/shard_map/ppermute | solution.py:525
  21.7 0.9 %shard_map.145 = (bf16[8,32,384]{2,1,0:T(8,128)(2,1)S(1)}, f32[7,16,128]{2,1,0:T(8,128)S(1)}, f32[16,1024]{1,0:T(8,128)S(1)}) custom-call(f32[32,128]{1,0:T(8,128)S(1)} %get-tuple-element.50.refs_0_, f32[56,128]{1,0:T(8,128)S(1)} %get-tuple-element.51.refs_1_, f32[88,128]{1,0:T(8,128)S(1)} %collective-permute-done.3.refs_2_, ...), custom_call_target="tpu_custom_call" | custom-call | flops 1000000 | tf_op jit(solution)/shard_map/pallas_call | solution.py:542
  22.6 0.4 %collective-permute-done.9.refs_8_ = f32[88,128]{1,0:T(8,128)S(1)} collective-permute-done((f32[88,128]{1,0:T(8,128)S(1)}, f32[88,128]{1,0:T(8,128)S(1)}, u32[]{:S(2)}, u32[]{:S(2)}) %collective-permute-start.9) | collective-permute-done | bytes 45088 | tf_op jit(solution)/shard_map/ppermute | solution.py:525
  23.0 0.9 %shard_map.146 = (f32[48,128]{1,0:T(8,128)S(1)}, bf16[8,32,128]{2,1,0:T(8,128)(2,1)S(1)}, f32[8,16,128]{2,1,0:T(8,128)S(1)}) custom-call(s32[1]{0:T(128)} %bitcast.1.pos_ref, f32[16,128]{1,0:T(8,128)S(1)} %get-tuple-element.41.mix_ref, f32[32,128]{1,0:T(8,128)S(1)} %get-tuple-element.50.refs_0_, f32[56,128]{1,0:T(8,128)S(1)} %get-tuple-element.51.refs_1_, ...), custom_call_target="tpu_custom_call" | custom-call | flops 1000000000 | tf_op jit(solution)/shard_map/pallas_call | solution.py:553
  23.9 0.0 collective-permute-start.10
  23.9 0.4 %shard_map.147.own_ref = f32[16,40,256]{2,1,0:T(8,128)S(1)} custom-call(bf16[16,40,256]{2,1,0:T(8,128)(2,1)S(1)} %copy-done.1, f32[48,128]{1,0:T(8,128)S(1)} %get-tuple-element.65.mine_ref, bf16[2,128,128]{2,1,0:T(8,128)(2,1)S(1)} %get-tuple-element.66.weights_ref, f32[16,40,256]{2,1,0:T(8,128)S(1)} %copy-done), custom_call_target="tpu_custom_call" | custom-call | tf_op jit(solution)/shard_map/pallas_call | solution.py:582
  24.3 0.3 %shard_map.148 = (f32[16,1024]{1,0:T(8,128)S(1)}, f32[16,1024]{1,0:T(8,128)S(1)}) custom-call(s32[1]{0:T(128)} %bitcast.1.pos_ref, bf16[8,32,512]{2,1,0:T(8,128)(2,1)S(1)} %get-tuple-element.59.refs_8_.refs_9_.refs_0_, bf16[8,32,384]{2,1,0:T(8,128)(2,1)S(1)} %get-tuple-element.62.refs_10_.refs_1_, bf16[8,32,128]{2,1,0:T(8,128)(2,1)S(1)} %get-tuple-element.67.refs_2_, ...), custom_call_target="tpu_custom_call" | custom-call | tf_op jit(solution)/shard_map/pallas_call | solution.py:560
  24.7 0.4 %collective-permute-done.10.theirs_ref = f32[48,128]{1,0:T(8,128)S(1)} collective-permute-done((f32[48,128]{1,0:T(8,128)S(1)}, f32[48,128]{1,0:T(8,128)S(1)}, u32[]{:S(2)}, u32[]{:S(2)}) %collective-permute-start.10) | collective-permute-done | bytes 24608 | tf_op jit(solution)/shard_map/ppermute | solution.py:581
  25.1 1.3 %shard_map.149 = (f32[16,40,256]{2,1,0:T(8,128)}, f32[16,1024]{1,0:T(8,128)}, f32[16,1024]{1,0:T(8,128)}) custom-call(bf16[16,40,256]{2,1,0:T(8,128)(2,1)S(1)} %collective-permute-done.1.perturb_ref, f32[48,128]{1,0:T(8,128)S(1)} %collective-permute-done.10.theirs_ref, f32[16,40,256]{2,1,0:T(8,128)S(1)} %shard_map.147.own_ref, ...), custom_call_target="tpu_custom_call" | custom-call | tf_op jit(solution)/shard_map/pallas_call | solution.py:583
  (9 shorter events, 0.0 us)
Async XLA Ops:
  0.6 2.5 %collective-permute-start = (f32[16,40,256]{2,1,0:T(8,128)}, f32[16,40,256]{2,1,0:T(8,128)S(1)}, u32[]{:S(2)}, u32[]{:S(2)}) collective-permute-start(f32[16,40,256]{2,1,0:T(8,128)} %control_ref.3), channel_id=1, source_target_pairs={{0,1},{1,0},{2,3},{3,2},{4,5},{5,4},{6,7},{7,6},{8,9},{9,8},{10,11... | collective-permute-start | bytes 1966088 | tf_op jit(solution)/shard_map/ppermute | solution.py:490
  1.1 2.5 %collective-permute-start.1 = (bf16[16,40,256]{2,1,0:T(8,128)(2,1)}, bf16[16,40,256]{2,1,0:T(8,128)(2,1)S(1)}, u32[]{:S(2)}, u32[]{:S(2)}) collective-permute-start(bf16[16,40,256]{2,1,0:T(8,128)(2,1)} %perturb_ref.3), channel_id=1, source_target_pairs={{0,1},{1,0},{2,3},{3,2},{4,5},{5,4},{6,7},{7,6},{8,9},{9,8},{10,11... | collective-permute-start | bytes 983048 | tf_op jit(solution)/shard_map/ppermute | solution.py:509
  1.2 0.7 %copy-start.11 = (f32[16,32]{1,0:T(8,128)S(1)}, f32[16,32]{1,0:T(8,128)}, u32[]{:S(2)}) copy-start(f32[16,32]{1,0:T(8,128)} %loc_ref.1) | copy-start | bytes 6148
  1.9 1.2 %copy-start = (f32[16,40,256]{2,1,0:T(8,128)S(1)}, f32[16,40,256]{2,1,0:T(8,128)}, u32[]{:S(2)}) copy-start(f32[16,40,256]{2,1,0:T(8,128)} %control_ref.3) | copy-start | bytes 1966084
  1.9 1.2 %copy-start.1 = (bf16[16,40,256]{2,1,0:T(8,128)(2,1)S(1)}, bf16[16,40,256]{2,1,0:T(8,128)(2,1)}, u32[]{:S(2)}) copy-start(bf16[16,40,256]{2,1,0:T(8,128)(2,1)} %perturb_ref.3) | copy-start | bytes 983044
  3.1 3.5 %copy-start.2 = (f32[16,1024]{1,0:T(8,128)S(1)}, f32[16,1024]{1,0:T(8,128)}, u32[]{:S(2)}) copy-start(f32[16,1024]{1,0:T(8,128)} %refs_5_.1) | copy-start | bytes 196612
  3.1 3.5 %copy-start.3 = (f32[16,1024]{1,0:T(8,128)S(1)}, f32[16,1024]{1,0:T(8,128)}, u32[]{:S(2)}) copy-start(f32[16,1024]{1,0:T(8,128)} %refs_8_.1) | copy-start | bytes 196612
  3.1 3.5 %copy-start.4 = (f32[16,1024]{1,0:T(8,128)S(1)}, f32[16,1024]{1,0:T(8,128)}, u32[]{:S(2)}) copy-start(f32[16,1024]{1,0:T(8,128)} %refs_9_.1) | copy-start | bytes 196612
  3.1 3.5 %copy-start.7 = (s32[1,8,128]{2,1,0:T(8,128)S(1)}, s32[1,8,128]{2,1,0:T(8,128)}, u32[]{:S(2)}) copy-start(s32[1,8,128]{2,1,0:T(8,128)} %src_ref.1) | copy-start | bytes 12292
  3.1 3.5 %copy-start.8 = (f32[1,8,128]{2,1,0:T(8,128)S(1)}, f32[1,8,128]{2,1,0:T(8,128)}, u32[]{:S(2)}) copy-start(f32[1,8,128]{2,1,0:T(8,128)} %weight_ref.1) | copy-start | bytes 12292
  3.1 3.5 %copy-start.9 = (s32[1,8,128]{2,1,0:T(8,128)S(1)}, s32[1,8,128]{2,1,0:T(8,128)}, u32[]{:S(2)}) copy-start(s32[1,8,128]{2,1,0:T(8,128)} %tgt_ref.1) | copy-start | bytes 12292
  3.7 4.8 %collective-permute-start.2 = (f32[16,256]{1,0:T(8,128)S(1)}, f32[16,256]{1,0:T(8,128)S(1)}, u32[]{:S(2)}, u32[]{:S(2)}) collective-permute-start(f32[16,256]{1,0:T(8,128)S(1)} %shard_map.140.refs_0_), channel_id=1, source_target_pairs={{0,16},{16,0},{1,17},{17,1},{2,18},{18,2},{3,19},{19,3},{4,20},{20... | collective-permute-start | bytes 49160 | tf_op jit(solution)/shard_map/ppermute | solution.py:511
  6.6 0.7 %copy-start.6 = (f32[1024]{0:T(1024)S(1)}, f32[1024]{0:T(1024)}, u32[]{:S(2)}) copy-start(f32[1024]{0:T(1024)} %param.17) | copy-start | bytes 12292
  6.6 0.7 %copy-start.5 = (f32[1024]{0:T(1024)S(1)}, f32[1024]{0:T(1024)}, u32[]{:S(2)}) copy-start(f32[1024]{0:T(1024)} %param.16) | copy-start | bytes 12292
  6.6 0.7 %copy-start.10 = (s32[1,8]{1,0:T(1,128)S(1)}, s32[1,8]{1,0:T(1,128)}, u32[]{:S(2)}) copy-start(s32[1,8]{1,0:T(1,128)} %counts_ref.1) | copy-start | bytes 100
  8.5 6.9 %collective-permute-start.6 = (f32[184,128]{1,0:T(8,128)S(1)}, f32[184,128]{1,0:T(8,128)S(1)}, u32[]{:S(2)}, u32[]{:S(2)}) collective-permute-start(f32[184,128]{1,0:T(8,128)S(1)} %get-tuple-element.55), channel_id=1, source_target_pairs={{0,8},{2,10},{4,12},{6,14},{8,0},{10,2},{12,4},{14,6},{1,9},{3,11}... | collective-permute-start | bytes 282632 | tf_op jit(solution)/shard_map/ppermute | solution.py:525
  11.5 7.4 %collective-permute-start.3 = (f32[88,128]{1,0:T(8,128)S(1)}, f32[88,128]{1,0:T(8,128)S(1)}, u32[]{:S(2)}, u32[]{:S(2)}) collective-permute-start(f32[88,128]{1,0:T(8,128)S(1)} %get-tuple-element.52), channel_id=1, source_target_pairs={{0,2},{2,0},{4,6},{6,4},{8,10},{10,8},{12,14},{14,12},{1,3},{3,1},... | collective-permute-start | bytes 135176 | tf_op jit(solution)/shard_map/ppermute | solution.py:525
  13.1 5.9 %collective-permute-start.4 = (f32[88,128]{1,0:T(8,128)S(1)}, f32[88,128]{1,0:T(8,128)S(1)}, u32[]{:S(2)}, u32[]{:S(2)}) collective-permute-start(f32[88,128]{1,0:T(8,128)S(1)} %get-tuple-element.53), channel_id=1, source_target_pairs={{0,4},{2,6},{4,0},{6,2},{8,12},{10,14},{12,8},{14,10},{1,5},{3,7},... | collective-permute-start | bytes 135176 | tf_op jit(solution)/shard_map/ppermute | solution.py:525
  14.6 5.4 %collective-permute-start.5 = (f32[88,128]{1,0:T(8,128)S(1)}, f32[88,128]{1,0:T(8,128)S(1)}, u32[]{:S(2)}, u32[]{:S(2)}) collective-permute-start(f32[88,128]{1,0:T(8,128)S(1)} %get-tuple-element.54), channel_id=1, source_target_pairs={{0,6},{2,4},{4,2},{6,0},{8,14},{10,12},{12,10},{14,8},{1,7},{3,5},... | collective-permute-start | bytes 135176 | tf_op jit(solution)/shard_map/ppermute | solution.py:525
  15.4 5.7 %collective-permute-start.7 = (f32[88,128]{1,0:T(8,128)S(1)}, f32[88,128]{1,0:T(8,128)S(1)}, u32[]{:S(2)}, u32[]{:S(2)}) collective-permute-start(f32[88,128]{1,0:T(8,128)S(1)} %get-tuple-element.56), channel_id=1, source_target_pairs={{0,6},{2,4},{4,2},{6,0},{8,14},{10,12},{12,10},{14,8},{1,7},{3,5},... | collective-permute-start | bytes 135176 | tf_op jit(solution)/shard_map/ppermute | solution.py:525
  17.6 4.0 %collective-permute-start.8 = (f32[88,128]{1,0:T(8,128)S(1)}, f32[88,128]{1,0:T(8,128)S(1)}, u32[]{:S(2)}, u32[]{:S(2)}) collective-permute-start(f32[88,128]{1,0:T(8,128)S(1)} %get-tuple-element.57), channel_id=1, source_target_pairs={{0,4},{2,6},{4,0},{6,2},{8,12},{10,14},{12,8},{14,10},{1,5},{3,7},... | collective-permute-start | bytes 135176 | tf_op jit(solution)/shard_map/ppermute | solution.py:525
  19.0 4.0 %collective-permute-start.9 = (f32[88,128]{1,0:T(8,128)S(1)}, f32[88,128]{1,0:T(8,128)S(1)}, u32[]{:S(2)}, u32[]{:S(2)}) collective-permute-start(f32[88,128]{1,0:T(8,128)S(1)} %get-tuple-element.58), channel_id=1, source_target_pairs={{0,2},{2,0},{4,6},{6,4},{8,10},{10,8},{12,14},{14,12},{1,3},{3,1},... | collective-permute-start | bytes 135176 | tf_op jit(solution)/shard_map/ppermute | solution.py:525
  23.9 1.2 %collective-permute-start.10 = (f32[48,128]{1,0:T(8,128)S(1)}, f32[48,128]{1,0:T(8,128)S(1)}, u32[]{:S(2)}, u32[]{:S(2)}) collective-permute-start(f32[48,128]{1,0:T(8,128)S(1)} %get-tuple-element.65.mine_ref), channel_id=1, source_target_pairs={{0,1},{1,0},{2,3},{3,2},{4,5},{5,4},{6,7},{7,6},{8,9},{9,8},{10,11... | collective-permute-start | bytes 73736 | tf_op jit(solution)/shard_map/ppermute | solution.py:581

commit v21 on v20

--- a/solution.py
+++ b/solution.py
@@ -224,6 +224,13 @@
         copy.wait()
 
 
+def relabel(r, n, lev):
+    high, low = n // 2, n // 4
+    both = high | low
+    turned = (r & ~both) | ((r & low) << 1) | ((r & high) >> 1)
+    return r + (turned - r) * lev
+
+
 class Rows:
     def __init__(self, levels, n):
         self.weight = slice(0, levels)
@@ -233,13 +240,13 @@
         self.total = at + 2 * n + EXTRA
 
 
-def static_kernel(band, pos_ref, counts_ref, static_ref, diag_ref, off_ref, obs_ref, innov_ref, src_ref, weight_ref, tgt_ref,
+def static_kernel(band, pos_ref, lev_ref, counts_ref, static_ref, diag_ref, off_ref, obs_ref, innov_ref, src_ref, weight_ref, tgt_ref,
                   *out_refs):
     levels, cols = static_ref.shape
     n = len(out_refs)
     cap = src_ref.shape[2]
     rows = Rows(levels, n)
-    peers = [pos_ref[0] ^ r for r in range(n)]
+    peers = [pos_ref[0] ^ relabel(r, n, lev_ref[0]) for r in range(n)]
     static, off, obs = static_ref[...], off_ref[...], obs_ref[...]
     lane = lax.broadcasted_iota(jnp.int32, (levels, cols), 1)
     left = jnp.where(lane == 0, 0.0, pltpu.roll(static, 1, 1))
@@ -378,14 +385,14 @@
     remap_ref[...] = landed + remap_old[...] if known else landed
 
 
-def shared_kernel(n, levels, band, cols, stages, pos_ref, mix_ref, *refs):
+def shared_kernel(n, levels, band, cols, stages, pos_ref, lev_ref, mix_ref, *refs):
     known = sum(stages[:-1], [])
     blocks, refs = open_blocks(known + stages[-1], refs, n, levels, band)
     old, refs = refs[: len(stages) - 1], refs[len(stages) - 1 :]
     met_old, pick_ref, out_ref, slots_ref, tables_ref = refs
     me = pos_ref[0]
     for r, block in blocks.items():
-        there = me ^ r
+        there = me ^ relabel(r, n, lev_ref[0])
         tables_ref[there, :n, :] = block.tgt
         tables_ref[there, n:, :] = block.rest(block.rows.edge, EXTRA)
     fill_slots(stages[-1], blocks, n, slots_ref)
@@ -400,7 +407,7 @@
                 value = value + met_at(d, block, bands, ref)
         edge = block.rest(block.rows.edge, 1)
         own = line(block.tgt, d)
-        there = me ^ d
+        there = me ^ relabel(d, n, lev_ref[0])
         before = tables_ref[jnp.maximum(there - 1, 0), n : n + 1, :]
         near = jnp.where((own == 0.0) & (there > 0), edge[:, 6 * levels + 1 : 6 * levels + 2], 0.0)
         value = value + row_as_column(before, levels, 0) * near
@@ -412,7 +419,7 @@
     out_ref[...] = band_rows(total, mix_ref[...])
 
 
-def outputs_kernel(stages, pos_ref, *refs):
+def outputs_kernel(stages, pos_ref, lev_ref, *refs):
     slots_refs, refs = refs[: len(stages)], refs[len(stages) :]
     remap_ref, tables_ref, static_ref, diag_ref, off_ref, obs_ref, innov_ref, increment_ref, grad_ref = refs
     levels, cols = static_ref.shape
@@ -429,7 +436,7 @@
     def beside(there, exists, column, own_end, side):
         edge = tables_ref[there, n : n + 1, :]
         static_end, coupling, base = (row_as_column(edge, levels, (2 * i + side) * levels) for i in range(3))
-        far = me ^ there
+        far = relabel(me ^ there, n, lev_ref[0])
         landed = []
         for s, ref, place in given:
             values = ref[far, :levels, place].astype(F32) + ref[far, levels:, place].astype(F32)
@@ -502,8 +509,8 @@
     if n * cap <= tile_cols and n >= 4 and lax.axis_size("lev") == 2 and n & (n - 1) == 0 and band_cols * tile_cols <= 2**20:
         rows = Rows(levels, n)
         stacked = band_cols // cap * levels
-        rests = call(functools.partial(static_kernel, band_cols), [shape((rows.total, cap), F32)] * n, [SMEM] * 2 + [VMEM] * 8)(
-            pos, counts, static_control, diag, off, obs_weight, innovation, send_src, send_wt, recv_tgt
+        rests = call(functools.partial(static_kernel, band_cols), [shape((rows.total, cap), F32)] * n, [SMEM] * 3 + [VMEM] * 8)(
+            pos, lev, counts, static_control, diag, off, obs_weight, innovation, send_src, send_wt, recv_tgt
         )
         sums = [own_sum]
         sums[0], other_perturb = lax.optimization_barrier((sums[0], lax.ppermute(perturb, "lev", swap)))
@@ -522,7 +529,8 @@
         )(*sums, *rests[1:])
 
         def to(r, block):
-            return [lax.ppermute(block, "tile", [(i, i ^ r) for i in range(n)])]
+            pairs = [(i * 2 + v, (i ^ relabel(r, n, v)) * 2 + v) for i in range(n) for v in range(2)]
+            return [lax.ppermute(block, ("tile", "lev"), pairs)]
 
         arrived = {0: [total, rests[0]]} | {r: to(r, blocks[r - 1]) for r in (high, *near)}
         passed = call(
@@ -553,13 +561,13 @@
         mine, new, tables = call(
             functools.partial(shared_kernel, n, levels, band_cols, tile_cols, stages),
             (mine_shape, shape((n, 2 * levels, len(stages[-1]) * cap), BF16), shape((n, n + EXTRA, cap), F32)),
-            [SMEM] + [VMEM] * (1 + len(refs)),
+            [SMEM] * 2 + [VMEM] * (1 + len(refs)),
             cost=pl.CostEstimate(flops=10**9, bytes_accessed=0, transcendentals=0),
-        )(pos, given_mix, *refs)
+        )(pos, lev, given_mix, *refs)
         slots.append(new)
         increment, grad_static = call(
-            functools.partial(outputs_kernel, stages), (flat, flat), [SMEM] + [VMEM] * (len(slots) + 7)
-        )(pos, *slots, remap, tables, static_control, diag, off, obs_weight, innovation)
+            functools.partial(outputs_kernel, stages), (flat, flat), [SMEM] * 2 + [VMEM] * (len(slots) + 7)
+        )(pos, lev, *slots, remap, tables, static_control, diag, off, obs_weight, innovation)
     else:
         other_perturb = lax.ppermute(perturb, "lev", swap)
         payload = call(

time: 26.6 us -> 28.4 us (1.068)
  starting transfers between devices: 13.7 us -> 15.3 us
    ppermute x7, starting transfers between devices: 10.2 us -> 11.7 us  [to(): return [lax.ppermute(block, ('tile', 'lev'), pairs)]]
  transfers between devices with their start and end apart: 11 -> 11, of which waited for: 6 -> 4; matrix products, arithmetic and copies ran while one was open for 0% -> 0% of each run, Pallas kernels for 17% -> 16%
where the time goes in v21:
time: 28.4 us; the launch traced here: 27.9 us
  starting transfers between devices  15.3 us (54%)
  Pallas kernels  6.67 us (23%)
  waiting for transfers between devices  3.79 us (13%)
  local copies, waits for them, and re-layouts  1.39 us (5%)
  between operations  0.79 us (3%)
    ppermute x7, starting transfers between devices, to(): return [lax.ppermute(block, ('tile', 'lev'), pairs)]  11.7 us
    ppermute x1, starting transfers between devices, body(): lax.ppermute(sums[0], 'grp', [(g, (g + k) % groups) for g in range(groups)])  2.97 us
    ppermute x7, waiting for transfers between devices, to(): return [lax.ppermute(block, ('tile', 'lev'), pairs)]  2.45 us
    pallas_call x2, Pallas kernels, body(): call(functools.partial(stage_kernel, n, levels, band_cols, tile_cols, sta...  1.91 us
    unnamed x24, local copies, waits for them, and re-layouts  1.39 us
    pallas_call x1, Pallas kernels, body(): call(ens_kernel, (shape(control.shape, F32), flat, flat), [VMEM] * 5, [pl...  1.24 us
    pallas_call x1, Pallas kernels, body(): call(functools.partial(static_kernel, band_cols), [shape((rows.total, cap...  1.1 us
    ppermute x1, waiting for transfers between devices, body(): other_control = lax.ppermute(control, 'lev', swap)  0.9 us
  transfers between devices with their start and end apart: 11, of which 4 were waited for; matrix products, arithmetic and copies ran while one was open for 0% of the time, Pallas kernels for 16%

profile of v21, /device:TPU:0, one launch (start us, length us, event | category | flops | bytes accessed | tf_op | source)
XLA Modules:
  0.0 27.9 jit_solution(14422381450163123390)
XLA Ops:
  0.6 0.5 %collective-permute-start = (f32[16,40,256]{2,1,0:T(8,128)}, f32[16,40,256]{2,1,0:T(8,128)S(1)}, u32[]{:S(2)}, u32[]{:S(2)}) collective-permute-start(f32[16,40,256]{2,1,0:T(8,128)} %control_ref.3), channel_id=1, source_target_pairs={{0,1},{1,0},{2,3},{3,2},{4,5},{5,4},{6,7},{7,6},{8,9},{9,8},{10,11... | collective-permute-start | bytes 1966088 | tf_op jit(solution)/shard_map/ppermute | solution.py:497
  1.1 0.1 collective-permute-start.1
  1.2 0.0 copy-start.11
  1.2 0.7 %copy-done.11 = f32[16,32]{1,0:T(8,128)S(1)} copy-done((f32[16,32]{1,0:T(8,128)S(1)}, f32[16,32]{1,0:T(8,128)}, u32[]{:S(2)}) %copy-start.11) | copy-done | bytes 2072
  1.9 0.0 copy-start
  1.9 0.2 shard_map.139
  2.2 0.9 %collective-permute-done.other_ref = f32[16,40,256]{2,1,0:T(8,128)S(1)} collective-permute-done((f32[16,40,256]{2,1,0:T(8,128)}, f32[16,40,256]{2,1,0:T(8,128)S(1)}, u32[]{:S(2)}, u32[]{:S(2)}) %collective-permute-start) | collective-permute-done | bytes 655392 | tf_op jit(solution)/shard_map/ppermute | solution.py:497
  3.1 0.0 copy-done
  3.1 0.0 copy-done.1
  3.1 0.0 copy-start.7
  3.1 0.0 copy-start.8
  3.1 0.0 copy-start.9
  3.1 0.5 %shard_map.140.refs_0_ = f32[16,256]{1,0:T(8,128)S(1)} custom-call(bf16[16,40,256]{2,1,0:T(8,128)(2,1)S(1)} %copy-done.1, f32[16,40,256]{2,1,0:T(8,128)S(1)} %copy-done, f32[16,40,256]{2,1,0:T(8,128)S(1)} %collective-permute-done.other_ref, bf16[2,128,256]{2,1,0:T(8,128)(2,1)S(1)} %get-tuple-element.39.mix_ref), custom_call_target="tpu_custom_call" | custom-call | tf_op jit(solution)/shard_map/pallas_call | solution.py:505
  3.6 0.0 collective-permute-done.1.perturb_ref
  3.7 3.0 %collective-permute-start.2 = (f32[16,256]{1,0:T(8,128)S(1)}, f32[16,256]{1,0:T(8,128)S(1)}, u32[]{:S(2)}, u32[]{:S(2)}) collective-permute-start(f32[16,256]{1,0:T(8,128)S(1)} %shard_map.140.refs_0_), channel_id=1, source_target_pairs={{0,16},{16,0},{1,17},{17,1},{2,18},{18,2},{3,19},{19,3},{4,20},{20... | collective-permute-start | bytes 49160 | tf_op jit(solution)/shard_map/ppermute | solution.py:518
  6.6 0.0 copy-done.2
  6.6 0.0 copy-done.3
  6.6 0.0 copy-done.4
  6.7 0.0 copy-done.7
  6.7 0.0 copy-done.8
  6.7 0.0 copy-done.9
  6.7 0.6 %copy-done.6 = f32[1024]{0:T(1024)S(1)} copy-done((f32[1024]{0:T(1024)S(1)}, f32[1024]{0:T(1024)}, u32[]{:S(2)}) %copy-start.6) | copy-done | bytes 4120
  7.3 0.0 copy-done.5
  7.3 0.0 copy-done.10
  7.3 1.1 %shard_map.141 = (f32[56,128]{1,0:T(8,128)S(1)}, f32[56,128]{1,0:T(8,128)S(1)}, f32[56,128]{1,0:T(8,128)S(1)}, f32[56,128]{1,0:T(8,128)S(1)}, f32[56,128]{1,0:T(...) custom-call(s32[1]{0:T(128)} %bitcast.1.pos_ref, s32[1]{0:T(128)} %bitcast.lev_ref, ...), custom_call_target="tpu_custom_call" | custom-call | tf_op jit(solution)/shard_map/pallas_call | solution.py:512
  8.4 0.0 collective-permute-done.2.refs_1_
  8.5 3.1 %collective-permute-start.6 = (f32[184,128]{1,0:T(8,128)S(1)}, f32[184,128]{1,0:T(8,128)S(1)}, u32[]{:S(2)}, u32[]{:S(2)}) collective-permute-start(f32[184,128]{1,0:T(8,128)S(1)} %get-tuple-element.55), channel_id=1, source_target_pairs={{0,8},{1,5},{2,10},{3,7},{4,12},{5,1},{6,14},{7,3},{8,0},{9,13},{1... | collective-permute-start | bytes 282632 | tf_op jit(solution)/shard_map/ppermute | solution.py:533
  11.5 1.5 %collective-permute-start.3 = (f32[88,128]{1,0:T(8,128)S(1)}, f32[88,128]{1,0:T(8,128)S(1)}, u32[]{:S(2)}, u32[]{:S(2)}) collective-permute-start(f32[88,128]{1,0:T(8,128)S(1)} %get-tuple-element.52), channel_id=1, source_target_pairs={{0,2},{1,3},{2,0},{3,1},{4,6},{5,7},{6,4},{7,5},{8,10},{9,11},{10,... | collective-permute-start | bytes 135176 | tf_op jit(solution)/shard_map/ppermute | solution.py:533
  13.1 1.6 %collective-permute-start.4 = (f32[88,128]{1,0:T(8,128)S(1)}, f32[88,128]{1,0:T(8,128)S(1)}, u32[]{:S(2)}, u32[]{:S(2)}) collective-permute-start(f32[88,128]{1,0:T(8,128)S(1)} %get-tuple-element.53), channel_id=1, source_target_pairs={{0,4},{1,9},{2,6},{3,11},{4,0},{5,13},{6,2},{7,15},{8,12},{9,1},{1... | collective-permute-start | bytes 135176 | tf_op jit(solution)/shard_map/ppermute | solution.py:533
  14.6 0.4 %collective-permute-start.5 = (f32[88,128]{1,0:T(8,128)S(1)}, f32[88,128]{1,0:T(8,128)S(1)}, u32[]{:S(2)}, u32[]{:S(2)}) collective-permute-start(f32[88,128]{1,0:T(8,128)S(1)} %get-tuple-element.54), channel_id=1, source_target_pairs={{0,6},{1,11},{2,4},{3,9},{4,2},{5,15},{6,0},{7,13},{8,14},{9,3},{1... | collective-permute-start | bytes 135176 | tf_op jit(solution)/shard_map/ppermute | solution.py:533
  15.0 0.0 collective-permute-done.6.got_ref.refs_5_
  15.1 4.5 %collective-permute-start.7 = (f32[88,128]{1,0:T(8,128)S(1)}, f32[88,128]{1,0:T(8,128)S(1)}, u32[]{:S(2)}, u32[]{:S(2)}) collective-permute-start(f32[88,128]{1,0:T(8,128)S(1)} %get-tuple-element.56), channel_id=1, source_target_pairs={{0,6},{1,11},{2,4},{3,9},{4,2},{5,15},{6,0},{7,13},{8,14},{9,3},{1... | collective-permute-start | bytes 135176 | tf_op jit(solution)/shard_map/ppermute | solution.py:533
  19.6 0.0 collective-permute-start.8
  19.6 0.0 collective-permute-done.3.refs_2_
  19.6 0.6 %collective-permute-start.9 = (f32[88,128]{1,0:T(8,128)S(1)}, f32[88,128]{1,0:T(8,128)S(1)}, u32[]{:S(2)}, u32[]{:S(2)}) collective-permute-start(f32[88,128]{1,0:T(8,128)S(1)} %get-tuple-element.58), channel_id=1, source_target_pairs={{0,2},{1,3},{2,0},{3,1},{4,6},{5,7},{6,4},{7,5},{8,10},{9,11},{10,... | collective-permute-start | bytes 135176 | tf_op jit(solution)/shard_map/ppermute | solution.py:533
  20.2 0.0 collective-permute-done.4.refs_3_
  20.2 0.0 collective-permute-done.5.refs_4_
  20.3 1.0 %shard_map.144 = (bf16[8,32,512]{2,1,0:T(8,128)(2,1)S(1)}, f32[4,16,128]{2,1,0:T(8,128)S(1)}, f32[16,1024]{1,0:T(8,128)S(1)}, bf16[8,256,128]{2,1,0:T(8,128)(2,1)S(1)}) custom-call(f32[32,128]{1,0:T(8,128)S(1)} %get-tuple-element.50.refs_0_, f32[56,128]{1,0:T(8,128)S(1)} %get-tuple-element.51.refs_1_, f32[88,128]{1,0:T(8,128)S(1)} %collective-permute-done.3.refs_2_, ...), custom_call_target="tpu_custom_call" | custom-call | flops 1000000000 | tf_op jit(solution)/shard_map/pallas_call | solution.py:550
  21.2 0.4 %collective-permute-done.7.refs_6_ = f32[88,128]{1,0:T(8,128)S(1)} collective-permute-done((f32[88,128]{1,0:T(8,128)S(1)}, f32[88,128]{1,0:T(8,128)S(1)}, u32[]{:S(2)}, u32[]{:S(2)}) %collective-permute-start.7) | collective-permute-done | bytes 45088 | tf_op jit(solution)/shard_map/ppermute | solution.py:533
  21.6 2.0 %collective-permute-done.8.refs_7_ = f32[88,128]{1,0:T(8,128)S(1)} collective-permute-done((f32[88,128]{1,0:T(8,128)S(1)}, f32[88,128]{1,0:T(8,128)S(1)}, u32[]{:S(2)}, u32[]{:S(2)}) %collective-permute-start.8) | collective-permute-done | bytes 45088 | tf_op jit(solution)/shard_map/ppermute | solution.py:533
  23.6 1.0 %shard_map.145 = (bf16[8,32,384]{2,1,0:T(8,128)(2,1)S(1)}, f32[7,16,128]{2,1,0:T(8,128)S(1)}, f32[16,1024]{1,0:T(8,128)S(1)}) custom-call(f32[32,128]{1,0:T(8,128)S(1)} %get-tuple-element.50.refs_0_, f32[56,128]{1,0:T(8,128)S(1)} %get-tuple-element.51.refs_1_, f32[88,128]{1,0:T(8,128)S(1)} %collective-permute-done.3.refs_2_, ...), custom_call_target="tpu_custom_call" | custom-call | flops 1000000 | tf_op jit(solution)/shard_map/pallas_call | solution.py:550
  24.6 0.0 collective-permute-done.9.refs_8_
  24.6 0.9 %shard_map.146 = (f32[48,128]{1,0:T(8,128)S(1)}, bf16[8,32,128]{2,1,0:T(8,128)(2,1)S(1)}, f32[8,16,128]{2,1,0:T(8,128)S(1)}) custom-call(s32[1]{0:T(128)} %bitcast.1.pos_ref, s32[1]{0:T(128)} %bitcast.lev_ref, f32[16,128]{1,0:T(8,128)S(1)} %get-tuple-element.41.mix_ref, f32[32,128]{1,0:T(8,128)S(1)} %get-tuple-element.50.refs_0_, ...), custom_call_target="tpu_custom_call" | custom-call | flops 1000000000 | tf_op jit(solution)/shard_map/pallas_call | solution.py:561
  25.5 0.0 collective-permute-start.10
  25.5 0.4 %shard_map.147.own_ref = f32[16,40,256]{2,1,0:T(8,128)S(1)} custom-call(bf16[16,40,256]{2,1,0:T(8,128)(2,1)S(1)} %copy-done.1, f32[48,128]{1,0:T(8,128)S(1)} %get-tuple-element.65.mine_ref, bf16[2,128,128]{2,1,0:T(8,128)(2,1)S(1)} %get-tuple-element.66.weights_ref, f32[16,40,256]{2,1,0:T(8,128)S(1)} %copy-done), custom_call_target="tpu_custom_call" | custom-call | tf_op jit(solution)/shard_map/pallas_call | solution.py:590
  25.9 0.3 %shard_map.148 = (f32[16,1024]{1,0:T(8,128)S(1)}, f32[16,1024]{1,0:T(8,128)S(1)}) custom-call(s32[1]{0:T(128)} %bitcast.1.pos_ref, s32[1]{0:T(128)} %bitcast.lev_ref, bf16[8,32,512]{2,1,0:T(8,128)(2,1)S(1)} %get-tuple-element.59.refs_8_.refs_9_.refs_0_, bf16[8,32,384]{2,1,0:T(8,128)(2,1)S(1)} %get-tuple-element.62.refs_10_.refs_1_, ...), custom_call_target="tpu_custom_call" | custom-call | tf_op jit(solution)/shard_map/pallas_call | solution.py:568
  26.3 0.4 %collective-permute-done.10.theirs_ref = f32[48,128]{1,0:T(8,128)S(1)} collective-permute-done((f32[48,128]{1,0:T(8,128)S(1)}, f32[48,128]{1,0:T(8,128)S(1)}, u32[]{:S(2)}, u32[]{:S(2)}) %collective-permute-start.10) | collective-permute-done | bytes 24608 | tf_op jit(solution)/shard_map/ppermute | solution.py:589
  26.7 1.2 %shard_map.149 = (f32[16,40,256]{2,1,0:T(8,128)}, f32[16,1024]{1,0:T(8,128)}, f32[16,1024]{1,0:T(8,128)}) custom-call(bf16[16,40,256]{2,1,0:T(8,128)(2,1)S(1)} %collective-permute-done.1.perturb_ref, f32[48,128]{1,0:T(8,128)S(1)} %collective-permute-done.10.theirs_ref, f32[16,40,256]{2,1,0:T(8,128)S(1)} %shard_map.147.own_ref, ...), custom_call_target="tpu_custom_call" | custom-call | tf_op jit(solution)/shard_map/pallas_call | solution.py:591
  (9 shorter events, 0.0 us)
Async XLA Ops:
  0.6 2.5 %collective-permute-start = (f32[16,40,256]{2,1,0:T(8,128)}, f32[16,40,256]{2,1,0:T(8,128)S(1)}, u32[]{:S(2)}, u32[]{:S(2)}) collective-permute-start(f32[16,40,256]{2,1,0:T(8,128)} %control_ref.3), channel_id=1, source_target_pairs={{0,1},{1,0},{2,3},{3,2},{4,5},{5,4},{6,7},{7,6},{8,9},{9,8},{10,11... | collective-permute-start | bytes 1966088 | tf_op jit(solution)/shard_map/ppermute | solution.py:497
  1.1 2.5 %collective-permute-start.1 = (bf16[16,40,256]{2,1,0:T(8,128)(2,1)}, bf16[16,40,256]{2,1,0:T(8,128)(2,1)S(1)}, u32[]{:S(2)}, u32[]{:S(2)}) collective-permute-start(bf16[16,40,256]{2,1,0:T(8,128)(2,1)} %perturb_ref.3), channel_id=1, source_target_pairs={{0,1},{1,0},{2,3},{3,2},{4,5},{5,4},{6,7},{7,6},{8,9},{9,8},{10,11... | collective-permute-start | bytes 983048 | tf_op jit(solution)/shard_map/ppermute | solution.py:516
  1.2 0.7 %copy-start.11 = (f32[16,32]{1,0:T(8,128)S(1)}, f32[16,32]{1,0:T(8,128)}, u32[]{:S(2)}) copy-start(f32[16,32]{1,0:T(8,128)} %loc_ref.1) | copy-start | bytes 6148
  1.9 1.2 %copy-start = (f32[16,40,256]{2,1,0:T(8,128)S(1)}, f32[16,40,256]{2,1,0:T(8,128)}, u32[]{:S(2)}) copy-start(f32[16,40,256]{2,1,0:T(8,128)} %control_ref.3) | copy-start | bytes 1966084
  1.9 1.2 %copy-start.1 = (bf16[16,40,256]{2,1,0:T(8,128)(2,1)S(1)}, bf16[16,40,256]{2,1,0:T(8,128)(2,1)}, u32[]{:S(2)}) copy-start(bf16[16,40,256]{2,1,0:T(8,128)(2,1)} %perturb_ref.3) | copy-start | bytes 983044
  3.1 3.5 %copy-start.2 = (f32[16,1024]{1,0:T(8,128)S(1)}, f32[16,1024]{1,0:T(8,128)}, u32[]{:S(2)}) copy-start(f32[16,1024]{1,0:T(8,128)} %refs_5_.1) | copy-start | bytes 196612
  3.1 3.5 %copy-start.3 = (f32[16,1024]{1,0:T(8,128)S(1)}, f32[16,1024]{1,0:T(8,128)}, u32[]{:S(2)}) copy-start(f32[16,1024]{1,0:T(8,128)} %refs_8_.1) | copy-start | bytes 196612
  3.1 3.5 %copy-start.4 = (f32[16,1024]{1,0:T(8,128)S(1)}, f32[16,1024]{1,0:T(8,128)}, u32[]{:S(2)}) copy-start(f32[16,1024]{1,0:T(8,128)} %refs_9_.1) | copy-start | bytes 196612
  3.1 3.5 %copy-start.7 = (s32[1,8,128]{2,1,0:T(8,128)S(1)}, s32[1,8,128]{2,1,0:T(8,128)}, u32[]{:S(2)}) copy-start(s32[1,8,128]{2,1,0:T(8,128)} %src_ref.1) | copy-start | bytes 12292
  3.1 3.5 %copy-start.8 = (f32[1,8,128]{2,1,0:T(8,128)S(1)}, f32[1,8,128]{2,1,0:T(8,128)}, u32[]{:S(2)}) copy-start(f32[1,8,128]{2,1,0:T(8,128)} %weight_ref.1) | copy-start | bytes 12292
  3.1 3.5 %copy-start.9 = (s32[1,8,128]{2,1,0:T(8,128)S(1)}, s32[1,8,128]{2,1,0:T(8,128)}, u32[]{:S(2)}) copy-start(s32[1,8,128]{2,1,0:T(8,128)} %tgt_ref.1) | copy-start | bytes 12292
  3.7 4.8 %collective-permute-start.2 = (f32[16,256]{1,0:T(8,128)S(1)}, f32[16,256]{1,0:T(8,128)S(1)}, u32[]{:S(2)}, u32[]{:S(2)}) collective-permute-start(f32[16,256]{1,0:T(8,128)S(1)} %shard_map.140.refs_0_), channel_id=1, source_target_pairs={{0,16},{16,0},{1,17},{17,1},{2,18},{18,2},{3,19},{19,3},{4,20},{20... | collective-permute-start | bytes 49160 | tf_op jit(solution)/shard_map/ppermute | solution.py:518
  6.6 0.7 %copy-start.6 = (f32[1024]{0:T(1024)S(1)}, f32[1024]{0:T(1024)}, u32[]{:S(2)}) copy-start(f32[1024]{0:T(1024)} %param.17) | copy-start | bytes 12292
  6.6 0.7 %copy-start.5 = (f32[1024]{0:T(1024)S(1)}, f32[1024]{0:T(1024)}, u32[]{:S(2)}) copy-start(f32[1024]{0:T(1024)} %param.16) | copy-start | bytes 12292
  6.6 0.7 %copy-start.10 = (s32[1,8]{1,0:T(1,128)S(1)}, s32[1,8]{1,0:T(1,128)}, u32[]{:S(2)}) copy-start(s32[1,8]{1,0:T(1,128)} %counts_ref.1) | copy-start | bytes 100
  8.5 6.6 %collective-permute-start.6 = (f32[184,128]{1,0:T(8,128)S(1)}, f32[184,128]{1,0:T(8,128)S(1)}, u32[]{:S(2)}, u32[]{:S(2)}) collective-permute-start(f32[184,128]{1,0:T(8,128)S(1)} %get-tuple-element.55), channel_id=1, source_target_pairs={{0,8},{1,5},{2,10},{3,7},{4,12},{5,1},{6,14},{7,3},{8,0},{9,13},{1... | collective-permute-start | bytes 282632 | tf_op jit(solution)/shard_map/ppermute | solution.py:533
  11.5 8.1 %collective-permute-start.3 = (f32[88,128]{1,0:T(8,128)S(1)}, f32[88,128]{1,0:T(8,128)S(1)}, u32[]{:S(2)}, u32[]{:S(2)}) collective-permute-start(f32[88,128]{1,0:T(8,128)S(1)} %get-tuple-element.52), channel_id=1, source_target_pairs={{0,2},{1,3},{2,0},{3,1},{4,6},{5,7},{6,4},{7,5},{8,10},{9,11},{10,... | collective-permute-start | bytes 135176 | tf_op jit(solution)/shard_map/ppermute | solution.py:533
  13.1 7.2 %collective-permute-start.4 = (f32[88,128]{1,0:T(8,128)S(1)}, f32[88,128]{1,0:T(8,128)S(1)}, u32[]{:S(2)}, u32[]{:S(2)}) collective-permute-start(f32[88,128]{1,0:T(8,128)S(1)} %get-tuple-element.53), channel_id=1, source_target_pairs={{0,4},{1,9},{2,6},{3,11},{4,0},{5,13},{6,2},{7,15},{8,12},{9,1},{1... | collective-permute-start | bytes 135176 | tf_op jit(solution)/shard_map/ppermute | solution.py:533
  14.6 5.6 %collective-permute-start.5 = (f32[88,128]{1,0:T(8,128)S(1)}, f32[88,128]{1,0:T(8,128)S(1)}, u32[]{:S(2)}, u32[]{:S(2)}) collective-permute-start(f32[88,128]{1,0:T(8,128)S(1)} %get-tuple-element.54), channel_id=1, source_target_pairs={{0,6},{1,11},{2,4},{3,9},{4,2},{5,15},{6,0},{7,13},{8,14},{9,3},{1... | collective-permute-start | bytes 135176 | tf_op jit(solution)/shard_map/ppermute | solution.py:533
  15.1 6.6 %collective-permute-start.7 = (f32[88,128]{1,0:T(8,128)S(1)}, f32[88,128]{1,0:T(8,128)S(1)}, u32[]{:S(2)}, u32[]{:S(2)}) collective-permute-start(f32[88,128]{1,0:T(8,128)S(1)} %get-tuple-element.56), channel_id=1, source_target_pairs={{0,6},{1,11},{2,4},{3,9},{4,2},{5,15},{6,0},{7,13},{8,14},{9,3},{1... | collective-permute-start | bytes 135176 | tf_op jit(solution)/shard_map/ppermute | solution.py:533
  19.6 4.0 %collective-permute-start.8 = (f32[88,128]{1,0:T(8,128)S(1)}, f32[88,128]{1,0:T(8,128)S(1)}, u32[]{:S(2)}, u32[]{:S(2)}) collective-permute-start(f32[88,128]{1,0:T(8,128)S(1)} %get-tuple-element.57), channel_id=1, source_target_pairs={{0,4},{1,9},{2,6},{3,11},{4,0},{5,13},{6,2},{7,15},{8,12},{9,1},{1... | collective-permute-start | bytes 135176 | tf_op jit(solution)/shard_map/ppermute | solution.py:533
  19.6 5.0 %collective-permute-start.9 = (f32[88,128]{1,0:T(8,128)S(1)}, f32[88,128]{1,0:T(8,128)S(1)}, u32[]{:S(2)}, u32[]{:S(2)}) collective-permute-start(f32[88,128]{1,0:T(8,128)S(1)} %get-tuple-element.58), channel_id=1, source_target_pairs={{0,2},{1,3},{2,0},{3,1},{4,6},{5,7},{6,4},{7,5},{8,10},{9,11},{10,... | collective-permute-start | bytes 135176 | tf_op jit(solution)/shard_map/ppermute | solution.py:533
  25.5 1.2 %collective-permute-start.10 = (f32[48,128]{1,0:T(8,128)S(1)}, f32[48,128]{1,0:T(8,128)S(1)}, u32[]{:S(2)}, u32[]{:S(2)}) collective-permute-start(f32[48,128]{1,0:T(8,128)S(1)} %get-tuple-element.65.mine_ref), channel_id=1, source_target_pairs={{0,1},{1,0},{2,3},{3,2},{4,5},{5,4},{6,7},{7,6},{8,9},{9,8},{10,11... | collective-permute-start | bytes 73736 | tf_op jit(solution)/shard_map/ppermute | solution.py:589

commit v22 on v20

--- a/solution.py
+++ b/solution.py
@@ -280,21 +280,26 @@
         out_ref[...] = jnp.concatenate(parts, axis=0)
 
 
-def relay_kernel(levels, stacked, got_ref, *out_refs):
-    head = got_ref.shape[0] - len(out_refs) * 2 * levels
+def relay_kernel(levels, stacked, count, got_ref, *refs):
+    total = got_ref.shape[0]
+    own_refs, out_refs = refs[:count], refs[count:]
+    head = total - len(out_refs) * 2 * levels
+    alone = len(out_refs) - len(own_refs)
     for i, out_ref in enumerate(out_refs):
         at = head + 2 * levels * i
-        out_ref[...] = jnp.concatenate(
-            [got_ref[:stacked, :], got_ref[at : at + 2 * levels, :], got_ref[stacked + 2 * levels : head, :]], axis=0
-        )
+        parts = [got_ref[:stacked, :], got_ref[at : at + 2 * levels, :], got_ref[stacked + 2 * levels : head, :]]
+        if i >= alone:
+            parts = [own_refs[i - alone][...], *parts]
+        out_ref[...] = jnp.concatenate(parts, axis=0)
 
 
 class Block:
-    def __init__(self, refs, n, levels, band):
+    def __init__(self, refs, n, levels, band, base=0):
         cap = refs[0].shape[1]
         self.levels, self.parts, self.cap = levels, band // cap, cap
         self.sums_ref, self.rest_ref = refs[0], refs[-1]
-        self.head = 0 if len(refs) == 2 else self.parts * levels
+        self.base = base
+        self.head = 0 if len(refs) == 2 else base + self.parts * levels
         self.rows = Rows(levels, n)
         words = self.rest(self.rows.index, n)
         self.tgt = jnp.floor((words + 0.5) * (1.0 / band))
@@ -305,7 +310,8 @@
         return self.rest_ref[self.head + at : self.head + at + size, :]
 
     def sums(self):
-        parts = [self.sums_ref[i * self.levels : (i + 1) * self.levels, :] for i in range(self.parts)]
+        base = self.base
+        parts = [self.sums_ref[base + i * self.levels : base + (i + 1) * self.levels, :] for i in range(self.parts)]
         return jnp.concatenate(halves(jnp.concatenate(parts, axis=1)), axis=0)
 
 
@@ -351,7 +357,8 @@
     blocks = {0: Block(refs[:2], n, levels, band)}
     refs = refs[2:]
     for i, r in enumerate(labels[1:]):
-        blocks[r] = Block(refs[i : i + 1], n, levels, band)
+        base = refs[i].shape[0] // 2 if r >= n // 2 + n // 4 else 0
+        blocks[r] = Block(refs[i : i + 1], n, levels, band, base)
     return blocks, refs[len(labels) - 1 :]
 
 
@@ -509,9 +516,9 @@
         sums[0], other_perturb = lax.optimization_barrier((sums[0], lax.ppermute(perturb, "lev", swap)))
         for k in range(1, groups):
             sums.append(lax.ppermute(sums[0], "grp", [(g, (g + k) % groups) for g in range(groups)]))
-        high = n // 2
-        near = list(range(1, high))
-        stages = [[0, *near], [high, *(r + high for r in reversed(near[1:]))], [high + 1]]
+        low, high = n // 4, n // 2
+        pairs_of = [r for k in reversed(range(low + 1, high)) for r in (k, k + high)]
+        stages = [[0, *range(1, low), high], [r + high for r in range(1, low)] + pairs_of, [low, low + high]]
         block = stacked + rows.total
         total, *blocks = call(
             functools.partial(blocks_kernel, groups, levels, high - 1),
@@ -524,12 +531,16 @@
         def to(r, block):
             return [lax.ppermute(block, "tile", [(i, i ^ r) for i in range(n)])]
 
-        arrived = {0: [total, rests[0]]} | {r: to(r, blocks[r - 1]) for r in (high, *near)}
+        arrived = {0: [total, rests[0]]} | {r: to(r, blocks[r - 1]) for r in (high, *range(1, low))}
         passed = call(
-            functools.partial(relay_kernel, levels, stacked), [shape((block, cap), F32)] * (high - 1), [VMEM]
-        )(*arrived[high])
-        for r in reversed(near):
+            functools.partial(relay_kernel, levels, stacked, high - low),
+            [shape((block * (1 + (r >= low)), cap), F32) for r in range(1, high)],
+            [VMEM] * (1 + high - low),
+        )(*arrived[high], *blocks[low - 1 : high - 1])
+        for r in reversed(range(1, high)):
             arrived[r + high] = to(r, passed[r - 1])
+            if r >= low:
+                arrived[r] = arrived[r + high]
         slots, carried, picks = [], [], []
         for count in range(1, len(stages)):
             labels = sum(stages[:count], [])
@@ -543,7 +554,7 @@
                 functools.partial(stage_kernel, n, levels, band_cols, tile_cols, stages[:count]),
                 outs,
                 [VMEM] * (len(refs) + len(slots) + len(carried)),
-                cost=pl.CostEstimate(flops=(10**9, 10**6)[count - 1], bytes_accessed=0, transcendentals=0),
+                cost=pl.CostEstimate(flops=10**9 if count == 1 else 10**6, bytes_accessed=0, transcendentals=0),
             )(*refs, *slots, *carried)
             slots.append(new)
             picks += carried[2:]

time: 26.6 us -> 27.6 us (1.038)
  waiting for transfers between devices: 3.79 us -> 6.82 us
  starting transfers between devices: 13.7 us -> 11.7 us
    ppermute x7 -> x5, waiting for transfers between devices: 2.44 us -> 5.56 us  [to(): return [lax.ppermute(block, 'tile', [(i, i ^ r) for i in range(n)])]]
    ppermute x7 -> x5, starting transfers between devices: 10.2 us -> 8.13 us  [to(): return [lax.ppermute(block, 'tile', [(i, i ^ r) for i in range(n)])]]
    pallas_call x2, Pallas kernels: 1.9 us -> 1.62 us  [body(): call(functools.partial(stage_kernel, n, levels, band_cols, tile_cols, sta...]
  transfers between devices with their start and end apart: 11 -> 9, of which waited for: 6 -> 4; matrix products, arithmetic and copies ran while one was open for 0% -> 0% of each run, Pallas kernels for 17% -> 16%
where the time goes in v22:
time: 27.6 us; the launch traced here: 27.4 us
  starting transfers between devices  11.7 us (42%)
  waiting for transfers between devices  6.82 us (25%)
  Pallas kernels  6.68 us (24%)
  local copies, waits for them, and re-layouts  1.39 us (5%)
  between operations  0.79 us (3%)
    ppermute x5, starting transfers between devices, to(): return [lax.ppermute(block, 'tile', [(i, i ^ r) for i in range(n)])]  8.13 us
    ppermute x5, waiting for transfers between devices, to(): return [lax.ppermute(block, 'tile', [(i, i ^ r) for i in range(n)])]  5.56 us
    ppermute x1, starting transfers between devices, body(): lax.ppermute(sums[0], 'grp', [(g, (g + k) % groups) for g in range(groups)])  2.97 us
    pallas_call x2, Pallas kernels, body(): call(functools.partial(stage_kernel, n, levels, band_cols, tile_cols, sta...  1.62 us
    unnamed x24, local copies, waits for them, and re-layouts  1.39 us
    pallas_call x1, Pallas kernels, body(): call(ens_kernel, (shape(control.shape, F32), flat, flat), [VMEM] * 5, [pl...  1.24 us
    pallas_call x1, Pallas kernels, body(): call(functools.partial(static_kernel, band_cols), [shape((rows.total, cap...  1.11 us
    pallas_call x1, Pallas kernels, body(): call(functools.partial(shared_kernel, n, levels, band_cols, tile_cols, st...  1.09 us
  transfers between devices with their start and end apart: 9, of which 4 were waited for; matrix products, arithmetic and copies ran while one was open for 0% of the time, Pallas kernels for 16%

profile of v22, /device:TPU:0, one launch (start us, length us, event | category | flops | bytes accessed | tf_op | source)
XLA Modules:
  0.0 27.4 jit_solution(15140284204720141388)
XLA Ops:
  0.6 0.5 %collective-permute-start = (f32[16,40,256]{2,1,0:T(8,128)}, f32[16,40,256]{2,1,0:T(8,128)S(1)}, u32[]{:S(2)}, u32[]{:S(2)}) collective-permute-start(f32[16,40,256]{2,1,0:T(8,128)} %control_ref.3), channel_id=1, source_target_pairs={{0,1},{1,0},{2,3},{3,2},{4,5},{5,4},{6,7},{7,6},{8,9},{9,8},{10,11... | collective-permute-start | bytes 1966088 | tf_op jit(solution)/shard_map/ppermute | solution.py:497
  1.1 0.1 collective-permute-start.1
  1.2 0.0 copy-start.11
  1.2 0.7 %copy-done.11 = f32[16,32]{1,0:T(8,128)S(1)} copy-done((f32[16,32]{1,0:T(8,128)S(1)}, f32[16,32]{1,0:T(8,128)}, u32[]{:S(2)}) %copy-start.11) | copy-done | bytes 2072
  1.9 0.0 copy-start
  1.9 0.0 copy-start.1
  1.9 0.2 shard_map.139
  2.2 0.9 %collective-permute-done.other_ref = f32[16,40,256]{2,1,0:T(8,128)S(1)} collective-permute-done((f32[16,40,256]{2,1,0:T(8,128)}, f32[16,40,256]{2,1,0:T(8,128)S(1)}, u32[]{:S(2)}, u32[]{:S(2)}) %collective-permute-start) | collective-permute-done | bytes 655392 | tf_op jit(solution)/shard_map/ppermute | solution.py:497
  3.1 0.0 copy-done
  3.1 0.0 copy-done.1
  3.1 0.0 copy-start.2
  3.1 0.0 copy-start.3
  3.1 0.0 copy-start.4
  3.1 0.0 copy-start.7
  3.1 0.0 copy-start.8
  3.1 0.0 copy-start.9
  3.1 0.5 %shard_map.140.refs_0_ = f32[16,256]{1,0:T(8,128)S(1)} custom-call(bf16[16,40,256]{2,1,0:T(8,128)(2,1)S(1)} %copy-done.1, f32[16,40,256]{2,1,0:T(8,128)S(1)} %copy-done, f32[16,40,256]{2,1,0:T(8,128)S(1)} %collective-permute-done.other_ref, bf16[2,128,256]{2,1,0:T(8,128)(2,1)S(1)} %get-tuple-element.39.mix_ref), custom_call_target="tpu_custom_call" | custom-call | tf_op jit(solution)/shard_map/pallas_call | solution.py:505
  3.6 0.0 collective-permute-done.1.perturb_ref
  3.7 3.0 %collective-permute-start.2 = (f32[16,256]{1,0:T(8,128)S(1)}, f32[16,256]{1,0:T(8,128)S(1)}, u32[]{:S(2)}, u32[]{:S(2)}) collective-permute-start(f32[16,256]{1,0:T(8,128)S(1)} %shard_map.140.refs_0_), channel_id=1, source_target_pairs={{0,16},{16,0},{1,17},{17,1},{2,18},{18,2},{3,19},{19,3},{4,20},{20... | collective-permute-start | bytes 49160 | tf_op jit(solution)/shard_map/ppermute | solution.py:518
  6.6 0.0 copy-done.2
  6.6 0.0 copy-done.3
  6.6 0.0 copy-done.4
  6.7 0.0 copy-done.7
  6.7 0.0 copy-done.8
  6.7 0.0 copy-done.9
  6.7 0.6 %copy-done.6 = f32[1024]{0:T(1024)S(1)} copy-done((f32[1024]{0:T(1024)S(1)}, f32[1024]{0:T(1024)}, u32[]{:S(2)}) %copy-start.6) | copy-done | bytes 4120
  7.3 0.0 copy-done.5
  7.3 0.0 copy-done.10
  7.3 1.1 %shard_map.141 = (f32[56,128]{1,0:T(8,128)S(1)}, f32[56,128]{1,0:T(8,128)S(1)}, f32[56,128]{1,0:T(8,128)S(1)}, f32[56,128]{1,0:T(8,128)S(1)}, f32[56,128]{1,0:T(...) custom-call(s32[1]{0:T(128)} %bitcast.1.pos_ref, s32[1,8]{1,0:T(1,128)S(1)} %copy-done.10, ...), custom_call_target="tpu_custom_call" | custom-call | tf_op jit(solution)/shard_map/pallas_call | solution.py:512
  8.4 0.0 collective-permute-done.2.refs_1_
  8.5 3.1 %collective-permute-start.4 = (f32[184,128]{1,0:T(8,128)S(1)}, f32[184,128]{1,0:T(8,128)S(1)}, u32[]{:S(2)}, u32[]{:S(2)}) collective-permute-start(f32[184,128]{1,0:T(8,128)S(1)} %get-tuple-element.53), channel_id=1, source_target_pairs={{0,8},{2,10},{4,12},{6,14},{8,0},{10,2},{12,4},{14,6},{1,9},{3,11}... | collective-permute-start | bytes 282632 | tf_op jit(solution)/shard_map/ppermute | solution.py:532
  11.5 1.5 %collective-permute-start.3 = (f32[88,128]{1,0:T(8,128)S(1)}, f32[88,128]{1,0:T(8,128)S(1)}, u32[]{:S(2)}, u32[]{:S(2)}) collective-permute-start(f32[88,128]{1,0:T(8,128)S(1)} %get-tuple-element.52), channel_id=1, source_target_pairs={{0,2},{2,0},{4,6},{6,4},{8,10},{10,8},{12,14},{14,12},{1,3},{3,1},... | collective-permute-start | bytes 135176 | tf_op jit(solution)/shard_map/ppermute | solution.py:532
  13.1 2.8 %collective-permute-done.4.got_ref.refs_3_ = f32[184,128]{1,0:T(8,128)S(1)} collective-permute-done((f32[184,128]{1,0:T(8,128)S(1)}, f32[184,128]{1,0:T(8,128)S(1)}, u32[]{:S(2)}, u32[]{:S(2)}) %collective-permute-start.4) | collective-permute-done | bytes 94240 | tf_op jit(solution)/shard_map/ppermute | solution.py:532
  15.9 1.6 %collective-permute-start.5 = (f32[88,128]{1,0:T(8,128)S(1)}, f32[88,128]{1,0:T(8,128)S(1)}, u32[]{:S(2)}, u32[]{:S(2)}) collective-permute-start(f32[88,128]{1,0:T(8,128)S(1)} %get-tuple-element.56), channel_id=1, source_target_pairs={{0,2},{2,0},{4,6},{6,4},{8,10},{10,8},{12,14},{14,12},{1,3},{3,1},... | collective-permute-start | bytes 135176 | tf_op jit(solution)/shard_map/ppermute | solution.py:532
  17.5 0.6 %collective-permute-start.6 = (f32[176,128]{1,0:T(8,128)S(1)}, f32[176,128]{1,0:T(8,128)S(1)}, u32[]{:S(2)}, u32[]{:S(2)}) collective-permute-start(f32[176,128]{1,0:T(8,128)S(1)} %get-tuple-element.57), channel_id=1, source_target_pairs={{0,6},{2,4},{4,2},{6,0},{8,14},{10,12},{12,10},{14,8},{1,7},{3,5},... | collective-permute-start | bytes 270344 | tf_op jit(solution)/shard_map/ppermute | solution.py:532
  18.1 1.4 %collective-permute-start.7 = (f32[176,128]{1,0:T(8,128)S(1)}, f32[176,128]{1,0:T(8,128)S(1)}, u32[]{:S(2)}, u32[]{:S(2)}) collective-permute-start(f32[176,128]{1,0:T(8,128)S(1)} %get-tuple-element.58), channel_id=1, source_target_pairs={{0,4},{2,6},{4,0},{6,2},{8,12},{10,14},{12,8},{14,10},{1,5},{3,7},... | collective-permute-start | bytes 270344 | tf_op jit(solution)/shard_map/ppermute | solution.py:532
  19.5 0.0 collective-permute-done.3.refs_2_
  19.5 0.7 %shard_map.144 = (bf16[8,32,384]{2,1,0:T(8,128)(2,1)S(1)}, f32[3,16,128]{2,1,0:T(8,128)S(1)}, f32[16,1024]{1,0:T(8,128)S(1)}, bf16[8,256,128]{2,1,0:T(8,128)(2,1)S(1)}) custom-call(f32[32,128]{1,0:T(8,128)S(1)} %get-tuple-element.50.refs_0_, f32[56,128]{1,0:T(8,128)S(1)} %get-tuple-element.51.refs_1_, f32[88,128]{1,0:T(8,128)S(1)} %collective-permute-done.3.refs_2_, ...), custom_call_target="tpu_custom_call" | custom-call | flops 1000000000 | tf_op jit(solution)/shard_map/pallas_call | solution.py:553
  20.2 0.0 collective-permute-done.5.refs_4_
  20.2 2.7 %collective-permute-done.6.refs_5_.refs_6_ = f32[176,128]{1,0:T(8,128)S(1)} collective-permute-done((f32[176,128]{1,0:T(8,128)S(1)}, f32[176,128]{1,0:T(8,128)S(1)}, u32[]{:S(2)}, u32[]{:S(2)}) %collective-permute-start.6) | collective-permute-done | bytes 90144 | tf_op jit(solution)/shard_map/ppermute | solution.py:532
  22.9 0.9 %shard_map.145 = (bf16[8,32,384]{2,1,0:T(8,128)(2,1)S(1)}, f32[6,16,128]{2,1,0:T(8,128)S(1)}, f32[16,1024]{1,0:T(8,128)S(1)}) custom-call(f32[32,128]{1,0:T(8,128)S(1)} %get-tuple-element.50.refs_0_, f32[56,128]{1,0:T(8,128)S(1)} %get-tuple-element.51.refs_1_, f32[88,128]{1,0:T(8,128)S(1)} %collective-permute-done.3.refs_2_, ...), custom_call_target="tpu_custom_call" | custom-call | flops 1000000 | tf_op jit(solution)/shard_map/pallas_call | solution.py:553
  23.8 0.0 collective-permute-done.7.refs_7_.refs_8_
  23.8 1.1 %shard_map.146 = (f32[48,128]{1,0:T(8,128)S(1)}, bf16[8,32,256]{2,1,0:T(8,128)(2,1)S(1)}, f32[8,16,128]{2,1,0:T(8,128)S(1)}) custom-call(s32[1]{0:T(128)} %bitcast.1.pos_ref, f32[16,128]{1,0:T(8,128)S(1)} %get-tuple-element.41.mix_ref, f32[32,128]{1,0:T(8,128)S(1)} %get-tuple-element.50.refs_0_, f32[56,128]{1,0:T(8,128)S(1)} %get-tuple-element.51.refs_1_, ...), custom_call_target="tpu_custom_call" | custom-call | flops 1000000000 | tf_op jit(solution)/shard_map/pallas_call | solution.py:564
  24.9 0.0 collective-permute-start.8
  24.9 0.4 %shard_map.147.own_ref = f32[16,40,256]{2,1,0:T(8,128)S(1)} custom-call(bf16[16,40,256]{2,1,0:T(8,128)(2,1)S(1)} %copy-done.1, f32[48,128]{1,0:T(8,128)S(1)} %get-tuple-element.65.mine_ref, bf16[2,128,128]{2,1,0:T(8,128)(2,1)S(1)} %get-tuple-element.66.weights_ref, f32[16,40,256]{2,1,0:T(8,128)S(1)} %copy-done), custom_call_target="tpu_custom_call" | custom-call | tf_op jit(solution)/shard_map/pallas_call | solution.py:593
  25.4 0.4 %shard_map.148 = (f32[16,1024]{1,0:T(8,128)S(1)}, f32[16,1024]{1,0:T(8,128)S(1)}) custom-call(s32[1]{0:T(128)} %bitcast.1.pos_ref, bf16[8,32,384]{2,1,0:T(8,128)(2,1)S(1)} %get-tuple-element.59.refs_7_.refs_9_.refs_0_, bf16[8,32,384]{2,1,0:T(8,128)(2,1)S(1)} %get-tuple-element.62.refs_10_.refs_1_, bf16[8,32,256]{2,1,0:T(8,128)(2,1)S(1)} %get-tuple-element.67.refs_2_, ...), custom_call_target="tpu_custom_call" | custom-call | tf_op jit(solution)/shard_map/pallas_call | solution.py:571
  25.8 0.3 %collective-permute-done.8.theirs_ref = f32[48,128]{1,0:T(8,128)S(1)} collective-permute-done((f32[48,128]{1,0:T(8,128)S(1)}, f32[48,128]{1,0:T(8,128)S(1)}, u32[]{:S(2)}, u32[]{:S(2)}) %collective-permute-start.8) | collective-permute-done | bytes 24608 | tf_op jit(solution)/shard_map/ppermute | solution.py:592
  26.1 1.2 %shard_map.149 = (f32[16,40,256]{2,1,0:T(8,128)}, f32[16,1024]{1,0:T(8,128)}, f32[16,1024]{1,0:T(8,128)}) custom-call(bf16[16,40,256]{2,1,0:T(8,128)(2,1)S(1)} %collective-permute-done.1.perturb_ref, f32[48,128]{1,0:T(8,128)S(1)} %collective-permute-done.8.theirs_ref, f32[16,40,256]{2,1,0:T(8,128)S(1)} %shard_map.147.own_ref, ...), custom_call_target="tpu_custom_call" | custom-call | tf_op jit(solution)/shard_map/pallas_call | solution.py:594
  (5 shorter events, 0.0 us)
Async XLA Ops:
  0.6 2.5 %collective-permute-start = (f32[16,40,256]{2,1,0:T(8,128)}, f32[16,40,256]{2,1,0:T(8,128)S(1)}, u32[]{:S(2)}, u32[]{:S(2)}) collective-permute-start(f32[16,40,256]{2,1,0:T(8,128)} %control_ref.3), channel_id=1, source_target_pairs={{0,1},{1,0},{2,3},{3,2},{4,5},{5,4},{6,7},{7,6},{8,9},{9,8},{10,11... | collective-permute-start | bytes 1966088 | tf_op jit(solution)/shard_map/ppermute | solution.py:497
  1.1 2.5 %collective-permute-start.1 = (bf16[16,40,256]{2,1,0:T(8,128)(2,1)}, bf16[16,40,256]{2,1,0:T(8,128)(2,1)S(1)}, u32[]{:S(2)}, u32[]{:S(2)}) collective-permute-start(bf16[16,40,256]{2,1,0:T(8,128)(2,1)} %perturb_ref.3), channel_id=1, source_target_pairs={{0,1},{1,0},{2,3},{3,2},{4,5},{5,4},{6,7},{7,6},{8,9},{9,8},{10,11... | collective-permute-start | bytes 983048 | tf_op jit(solution)/shard_map/ppermute | solution.py:516
  1.2 0.7 %copy-start.11 = (f32[16,32]{1,0:T(8,128)S(1)}, f32[16,32]{1,0:T(8,128)}, u32[]{:S(2)}) copy-start(f32[16,32]{1,0:T(8,128)} %loc_ref.1) | copy-start | bytes 6148
  1.9 1.2 %copy-start = (f32[16,40,256]{2,1,0:T(8,128)S(1)}, f32[16,40,256]{2,1,0:T(8,128)}, u32[]{:S(2)}) copy-start(f32[16,40,256]{2,1,0:T(8,128)} %control_ref.3) | copy-start | bytes 1966084
  1.9 1.2 %copy-start.1 = (bf16[16,40,256]{2,1,0:T(8,128)(2,1)S(1)}, bf16[16,40,256]{2,1,0:T(8,128)(2,1)}, u32[]{:S(2)}) copy-start(bf16[16,40,256]{2,1,0:T(8,128)(2,1)} %perturb_ref.3) | copy-start | bytes 983044
  3.1 3.5 %copy-start.2 = (f32[16,1024]{1,0:T(8,128)S(1)}, f32[16,1024]{1,0:T(8,128)}, u32[]{:S(2)}) copy-start(f32[16,1024]{1,0:T(8,128)} %refs_5_.1) | copy-start | bytes 196612
  3.1 3.5 %copy-start.3 = (f32[16,1024]{1,0:T(8,128)S(1)}, f32[16,1024]{1,0:T(8,128)}, u32[]{:S(2)}) copy-start(f32[16,1024]{1,0:T(8,128)} %refs_8_.1) | copy-start | bytes 196612
  3.1 3.5 %copy-start.4 = (f32[16,1024]{1,0:T(8,128)S(1)}, f32[16,1024]{1,0:T(8,128)}, u32[]{:S(2)}) copy-start(f32[16,1024]{1,0:T(8,128)} %refs_9_.1) | copy-start | bytes 196612
  3.1 3.5 %copy-start.7 = (s32[1,8,128]{2,1,0:T(8,128)S(1)}, s32[1,8,128]{2,1,0:T(8,128)}, u32[]{:S(2)}) copy-start(s32[1,8,128]{2,1,0:T(8,128)} %src_ref.1) | copy-start | bytes 12292
  3.1 3.5 %copy-start.8 = (f32[1,8,128]{2,1,0:T(8,128)S(1)}, f32[1,8,128]{2,1,0:T(8,128)}, u32[]{:S(2)}) copy-start(f32[1,8,128]{2,1,0:T(8,128)} %weight_ref.1) | copy-start | bytes 12292
  3.1 3.5 %copy-start.9 = (s32[1,8,128]{2,1,0:T(8,128)S(1)}, s32[1,8,128]{2,1,0:T(8,128)}, u32[]{:S(2)}) copy-start(s32[1,8,128]{2,1,0:T(8,128)} %tgt_ref.1) | copy-start | bytes 12292
  3.7 4.8 %collective-permute-start.2 = (f32[16,256]{1,0:T(8,128)S(1)}, f32[16,256]{1,0:T(8,128)S(1)}, u32[]{:S(2)}, u32[]{:S(2)}) collective-permute-start(f32[16,256]{1,0:T(8,128)S(1)} %shard_map.140.refs_0_), channel_id=1, source_target_pairs={{0,16},{16,0},{1,17},{17,1},{2,18},{18,2},{3,19},{19,3},{4,20},{20... | collective-permute-start | bytes 49160 | tf_op jit(solution)/shard_map/ppermute | solution.py:518
  6.6 0.7 %copy-start.6 = (f32[1024]{0:T(1024)S(1)}, f32[1024]{0:T(1024)}, u32[]{:S(2)}) copy-start(f32[1024]{0:T(1024)} %param.17) | copy-start | bytes 12292
  6.6 0.7 %copy-start.5 = (f32[1024]{0:T(1024)S(1)}, f32[1024]{0:T(1024)}, u32[]{:S(2)}) copy-start(f32[1024]{0:T(1024)} %param.16) | copy-start | bytes 12292
  6.6 0.7 %copy-start.10 = (s32[1,8]{1,0:T(1,128)S(1)}, s32[1,8]{1,0:T(1,128)}, u32[]{:S(2)}) copy-start(s32[1,8]{1,0:T(1,128)} %counts_ref.1) | copy-start | bytes 100
  8.5 7.4 %collective-permute-start.4 = (f32[184,128]{1,0:T(8,128)S(1)}, f32[184,128]{1,0:T(8,128)S(1)}, u32[]{:S(2)}, u32[]{:S(2)}) collective-permute-start(f32[184,128]{1,0:T(8,128)S(1)} %get-tuple-element.53), channel_id=1, source_target_pairs={{0,8},{2,10},{4,12},{6,14},{8,0},{10,2},{12,4},{14,6},{1,9},{3,11}... | collective-permute-start | bytes 282632 | tf_op jit(solution)/shard_map/ppermute | solution.py:532
  11.5 7.9 %collective-permute-start.3 = (f32[88,128]{1,0:T(8,128)S(1)}, f32[88,128]{1,0:T(8,128)S(1)}, u32[]{:S(2)}, u32[]{:S(2)}) collective-permute-start(f32[88,128]{1,0:T(8,128)S(1)} %get-tuple-element.52), channel_id=1, source_target_pairs={{0,2},{2,0},{4,6},{6,4},{8,10},{10,8},{12,14},{14,12},{1,3},{3,1},... | collective-permute-start | bytes 135176 | tf_op jit(solution)/shard_map/ppermute | solution.py:532
  15.9 4.3 %collective-permute-start.5 = (f32[88,128]{1,0:T(8,128)S(1)}, f32[88,128]{1,0:T(8,128)S(1)}, u32[]{:S(2)}, u32[]{:S(2)}) collective-permute-start(f32[88,128]{1,0:T(8,128)S(1)} %get-tuple-element.56), channel_id=1, source_target_pairs={{0,2},{2,0},{4,6},{6,4},{8,10},{10,8},{12,14},{14,12},{1,3},{3,1},... | collective-permute-start | bytes 135176 | tf_op jit(solution)/shard_map/ppermute | solution.py:532
  17.5 5.4 %collective-permute-start.6 = (f32[176,128]{1,0:T(8,128)S(1)}, f32[176,128]{1,0:T(8,128)S(1)}, u32[]{:S(2)}, u32[]{:S(2)}) collective-permute-start(f32[176,128]{1,0:T(8,128)S(1)} %get-tuple-element.57), channel_id=1, source_target_pairs={{0,6},{2,4},{4,2},{6,0},{8,14},{10,12},{12,10},{14,8},{1,7},{3,5},... | collective-permute-start | bytes 270344 | tf_op jit(solution)/shard_map/ppermute | solution.py:532
  18.1 5.7 %collective-permute-start.7 = (f32[176,128]{1,0:T(8,128)S(1)}, f32[176,128]{1,0:T(8,128)S(1)}, u32[]{:S(2)}, u32[]{:S(2)}) collective-permute-start(f32[176,128]{1,0:T(8,128)S(1)} %get-tuple-element.58), channel_id=1, source_target_pairs={{0,4},{2,6},{4,0},{6,2},{8,12},{10,14},{12,8},{14,10},{1,5},{3,7},... | collective-permute-start | bytes 270344 | tf_op jit(solution)/shard_map/ppermute | solution.py:532
  24.9 1.2 %collective-permute-start.8 = (f32[48,128]{1,0:T(8,128)S(1)}, f32[48,128]{1,0:T(8,128)S(1)}, u32[]{:S(2)}, u32[]{:S(2)}) collective-permute-start(f32[48,128]{1,0:T(8,128)S(1)} %get-tuple-element.65.mine_ref), channel_id=1, source_target_pairs={{0,1},{1,0},{2,3},{3,2},{4,5},{5,4},{6,7},{7,6},{8,9},{9,8},{10,11... | collective-permute-start | bytes 73736 | tf_op jit(solution)/shard_map/ppermute | solution.py:592

commit v23 on v20

--- a/solution.py
+++ b/solution.py
@@ -511,7 +511,8 @@
             sums.append(lax.ppermute(sums[0], "grp", [(g, (g + k) % groups) for g in range(groups)]))
         high = n // 2
         near = list(range(1, high))
-        stages = [[0, *near], [high, *(r + high for r in reversed(near[1:]))], [high + 1]]
+        after = [near[0], *reversed(near[1:])]
+        stages = [[0, *near], [high, *(r + high for r in after[:-1])], [after[-1] + high]]
         block = stacked + rows.total
         total, *blocks = call(
             functools.partial(blocks_kernel, groups, levels, high - 1),
@@ -528,7 +529,7 @@
         passed = call(
             functools.partial(relay_kernel, levels, stacked), [shape((block, cap), F32)] * (high - 1), [VMEM]
         )(*arrived[high])
-        for r in reversed(near):
+        for r in after:
             arrived[r + high] = to(r, passed[r - 1])
         slots, carried, picks = [], [], []
         for count in range(1, len(stages)):

time: 26.6 us -> 27 us (1.015)
  waiting for transfers between devices: 3.79 us -> 4.1 us
    ppermute x7, waiting for transfers between devices: 2.44 us -> 2.76 us  [to(): return [lax.ppermute(block, 'tile', [(i, i ^ r) for i in range(n)])]]
  transfers between devices with their start and end apart: 11 -> 11, of which waited for: 6 -> 5; matrix products, arithmetic and copies ran while one was open for 0% -> 0% of each run, Pallas kernels for 17% -> 17%
where the time goes in v23:
time: 27 us; the launch traced here: 26.8 us
  starting transfers between devices  13.8 us (51%)
  Pallas kernels  6.68 us (25%)
  waiting for transfers between devices  4.1 us (15%)
  local copies, waits for them, and re-layouts  1.39 us (5%)
  between operations  0.79 us (3%)
    ppermute x7, starting transfers between devices, to(): return [lax.ppermute(block, 'tile', [(i, i ^ r) for i in range(n)])]  10.3 us
    ppermute x1, starting transfers between devices, body(): lax.ppermute(sums[0], 'grp', [(g, (g + k) % groups) for g in range(groups)])  2.97 us
    ppermute x7, waiting for transfers between devices, to(): return [lax.ppermute(block, 'tile', [(i, i ^ r) for i in range(n)])]  2.76 us
    pallas_call x2, Pallas kernels, body(): call(functools.partial(stage_kernel, n, levels, band_cols, tile_cols, sta...  1.9 us
    unnamed x24, local copies, waits for them, and re-layouts  1.39 us
    pallas_call x1, Pallas kernels, body(): call(ens_kernel, (shape(control.shape, F32), flat, flat), [VMEM] * 5, [pl...  1.24 us
    pallas_call x1, Pallas kernels, body(): call(functools.partial(static_kernel, band_cols), [shape((rows.total, cap...  1.11 us
    ppermute x1, waiting for transfers between devices, body(): other_control = lax.ppermute(control, 'lev', swap)  0.9 us
  transfers between devices with their start and end apart: 11, of which 5 were waited for; matrix products, arithmetic and copies ran while one was open for 0% of the time, Pallas kernels for 17%

profile of v23, /device:TPU:0, one launch (start us, length us, event | category | flops | bytes accessed | tf_op | source)
XLA Modules:
  0.0 26.8 jit_solution(15681022085876412324)
XLA Ops:
  0.6 0.5 %collective-permute-start = (f32[16,40,256]{2,1,0:T(8,128)}, f32[16,40,256]{2,1,0:T(8,128)S(1)}, u32[]{:S(2)}, u32[]{:S(2)}) collective-permute-start(f32[16,40,256]{2,1,0:T(8,128)} %control_ref.3), channel_id=1, source_target_pairs={{0,1},{1,0},{2,3},{3,2},{4,5},{5,4},{6,7},{7,6},{8,9},{9,8},{10,11... | collective-permute-start | bytes 1966088 | tf_op jit(solution)/shard_map/ppermute | solution.py:490
  1.1 0.1 collective-permute-start.1
  1.2 0.0 copy-start.11
  1.2 0.7 %copy-done.11 = f32[16,32]{1,0:T(8,128)S(1)} copy-done((f32[16,32]{1,0:T(8,128)S(1)}, f32[16,32]{1,0:T(8,128)}, u32[]{:S(2)}) %copy-start.11) | copy-done | bytes 2072
  1.9 0.0 copy-start
  1.9 0.2 shard_map.139
  2.2 0.9 %collective-permute-done.other_ref = f32[16,40,256]{2,1,0:T(8,128)S(1)} collective-permute-done((f32[16,40,256]{2,1,0:T(8,128)}, f32[16,40,256]{2,1,0:T(8,128)S(1)}, u32[]{:S(2)}, u32[]{:S(2)}) %collective-permute-start) | collective-permute-done | bytes 655392 | tf_op jit(solution)/shard_map/ppermute | solution.py:490
  3.1 0.0 copy-done
  3.1 0.0 copy-done.1
  3.1 0.0 copy-start.7
  3.1 0.0 copy-start.8
  3.1 0.0 copy-start.9
  3.1 0.5 %shard_map.140.refs_0_ = f32[16,256]{1,0:T(8,128)S(1)} custom-call(bf16[16,40,256]{2,1,0:T(8,128)(2,1)S(1)} %copy-done.1, f32[16,40,256]{2,1,0:T(8,128)S(1)} %copy-done, f32[16,40,256]{2,1,0:T(8,128)S(1)} %collective-permute-done.other_ref, bf16[2,128,256]{2,1,0:T(8,128)(2,1)S(1)} %get-tuple-element.39.mix_ref), custom_call_target="tpu_custom_call" | custom-call | tf_op jit(solution)/shard_map/pallas_call | solution.py:498
  3.6 0.0 collective-permute-done.1.perturb_ref
  3.7 3.0 %collective-permute-start.2 = (f32[16,256]{1,0:T(8,128)S(1)}, f32[16,256]{1,0:T(8,128)S(1)}, u32[]{:S(2)}, u32[]{:S(2)}) collective-permute-start(f32[16,256]{1,0:T(8,128)S(1)} %shard_map.140.refs_0_), channel_id=1, source_target_pairs={{0,16},{16,0},{1,17},{17,1},{2,18},{18,2},{3,19},{19,3},{4,20},{20... | collective-permute-start | bytes 49160 | tf_op jit(solution)/shard_map/ppermute | solution.py:511
  6.6 0.0 copy-done.2
  6.6 0.0 copy-done.3
  6.6 0.0 copy-done.4
  6.7 0.0 copy-done.7
  6.7 0.0 copy-done.8
  6.7 0.0 copy-done.9
  6.7 0.6 %copy-done.6 = f32[1024]{0:T(1024)S(1)} copy-done((f32[1024]{0:T(1024)S(1)}, f32[1024]{0:T(1024)}, u32[]{:S(2)}) %copy-start.6) | copy-done | bytes 4120
  7.3 0.0 copy-done.5
  7.3 0.0 copy-done.10
  7.3 1.1 %shard_map.141 = (f32[56,128]{1,0:T(8,128)S(1)}, f32[56,128]{1,0:T(8,128)S(1)}, f32[56,128]{1,0:T(8,128)S(1)}, f32[56,128]{1,0:T(8,128)S(1)}, f32[56,128]{1,0:T(...) custom-call(s32[1]{0:T(128)} %bitcast.1.pos_ref, s32[1,8]{1,0:T(1,128)S(1)} %copy-done.10, ...), custom_call_target="tpu_custom_call" | custom-call | tf_op jit(solution)/shard_map/pallas_call | solution.py:505
  8.4 0.0 collective-permute-done.2.refs_1_
  8.5 3.1 %collective-permute-start.6 = (f32[184,128]{1,0:T(8,128)S(1)}, f32[184,128]{1,0:T(8,128)S(1)}, u32[]{:S(2)}, u32[]{:S(2)}) collective-permute-start(f32[184,128]{1,0:T(8,128)S(1)} %get-tuple-element.55), channel_id=1, source_target_pairs={{0,8},{2,10},{4,12},{6,14},{8,0},{10,2},{12,4},{14,6},{1,9},{3,11}... | collective-permute-start | bytes 282632 | tf_op jit(solution)/shard_map/ppermute | solution.py:526
  11.5 1.5 %collective-permute-start.3 = (f32[88,128]{1,0:T(8,128)S(1)}, f32[88,128]{1,0:T(8,128)S(1)}, u32[]{:S(2)}, u32[]{:S(2)}) collective-permute-start(f32[88,128]{1,0:T(8,128)S(1)} %get-tuple-element.52), channel_id=1, source_target_pairs={{0,2},{2,0},{4,6},{6,4},{8,10},{10,8},{12,14},{14,12},{1,3},{3,1},... | collective-permute-start | bytes 135176 | tf_op jit(solution)/shard_map/ppermute | solution.py:526
  13.1 1.6 %collective-permute-start.4 = (f32[88,128]{1,0:T(8,128)S(1)}, f32[88,128]{1,0:T(8,128)S(1)}, u32[]{:S(2)}, u32[]{:S(2)}) collective-permute-start(f32[88,128]{1,0:T(8,128)S(1)} %get-tuple-element.53), channel_id=1, source_target_pairs={{0,4},{2,6},{4,0},{6,2},{8,12},{10,14},{12,8},{14,10},{1,5},{3,7},... | collective-permute-start | bytes 135176 | tf_op jit(solution)/shard_map/ppermute | solution.py:526
  14.6 0.4 %collective-permute-start.5 = (f32[88,128]{1,0:T(8,128)S(1)}, f32[88,128]{1,0:T(8,128)S(1)}, u32[]{:S(2)}, u32[]{:S(2)}) collective-permute-start(f32[88,128]{1,0:T(8,128)S(1)} %get-tuple-element.54), channel_id=1, source_target_pairs={{0,6},{2,4},{4,2},{6,0},{8,14},{10,12},{12,10},{14,8},{1,7},{3,5},... | collective-permute-start | bytes 135176 | tf_op jit(solution)/shard_map/ppermute | solution.py:526
  15.0 0.3 %collective-permute-done.6.got_ref.refs_5_ = f32[184,128]{1,0:T(8,128)S(1)} collective-permute-done((f32[184,128]{1,0:T(8,128)S(1)}, f32[184,128]{1,0:T(8,128)S(1)}, u32[]{:S(2)}, u32[]{:S(2)}) %collective-permute-start.6) | collective-permute-done | bytes 94240 | tf_op jit(solution)/shard_map/ppermute | solution.py:526
  15.4 2.2 %collective-permute-start.7 = (f32[88,128]{1,0:T(8,128)S(1)}, f32[88,128]{1,0:T(8,128)S(1)}, u32[]{:S(2)}, u32[]{:S(2)}) collective-permute-start(f32[88,128]{1,0:T(8,128)S(1)} %get-tuple-element.56), channel_id=1, source_target_pairs={{0,2},{2,0},{4,6},{6,4},{8,10},{10,8},{12,14},{14,12},{1,3},{3,1},... | collective-permute-start | bytes 135176 | tf_op jit(solution)/shard_map/ppermute | solution.py:526
  17.5 0.6 %collective-permute-start.8 = (f32[88,128]{1,0:T(8,128)S(1)}, f32[88,128]{1,0:T(8,128)S(1)}, u32[]{:S(2)}, u32[]{:S(2)}) collective-permute-start(f32[88,128]{1,0:T(8,128)S(1)} %get-tuple-element.57), channel_id=1, source_target_pairs={{0,6},{2,4},{4,2},{6,0},{8,14},{10,12},{12,10},{14,8},{1,7},{3,5},... | collective-permute-start | bytes 135176 | tf_op jit(solution)/shard_map/ppermute | solution.py:526
  18.2 0.0 collective-permute-done.3.refs_2_
  18.2 0.9 %collective-permute-start.9 = (f32[88,128]{1,0:T(8,128)S(1)}, f32[88,128]{1,0:T(8,128)S(1)}, u32[]{:S(2)}, u32[]{:S(2)}) collective-permute-start(f32[88,128]{1,0:T(8,128)S(1)} %get-tuple-element.58), channel_id=1, source_target_pairs={{0,4},{2,6},{4,0},{6,2},{8,12},{10,14},{12,8},{14,10},{1,5},{3,7},... | collective-permute-start | bytes 135176 | tf_op jit(solution)/shard_map/ppermute | solution.py:526
  19.1 0.0 collective-permute-done.4.refs_3_
  19.1 0.6 %collective-permute-done.5.refs_4_ = f32[88,128]{1,0:T(8,128)S(1)} collective-permute-done((f32[88,128]{1,0:T(8,128)S(1)}, f32[88,128]{1,0:T(8,128)S(1)}, u32[]{:S(2)}, u32[]{:S(2)}) %collective-permute-start.5) | collective-permute-done | bytes 45088 | tf_op jit(solution)/shard_map/ppermute | solution.py:526
  19.7 1.0 %shard_map.144 = (bf16[8,32,512]{2,1,0:T(8,128)(2,1)S(1)}, f32[4,16,128]{2,1,0:T(8,128)S(1)}, f32[16,1024]{1,0:T(8,128)S(1)}, bf16[8,256,128]{2,1,0:T(8,128)(2,1)S(1)}) custom-call(f32[32,128]{1,0:T(8,128)S(1)} %get-tuple-element.50.refs_0_, f32[56,128]{1,0:T(8,128)S(1)} %get-tuple-element.51.refs_1_, f32[88,128]{1,0:T(8,128)S(1)} %collective-permute-done.3.refs_2_, ...), custom_call_target="tpu_custom_call" | custom-call | flops 1000000000 | tf_op jit(solution)/shard_map/pallas_call | solution.py:543
  20.6 0.0 collective-permute-done.7.refs_6_
  20.6 1.8 %collective-permute-done.8.refs_7_ = f32[88,128]{1,0:T(8,128)S(1)} collective-permute-done((f32[88,128]{1,0:T(8,128)S(1)}, f32[88,128]{1,0:T(8,128)S(1)}, u32[]{:S(2)}, u32[]{:S(2)}) %collective-permute-start.8) | collective-permute-done | bytes 45088 | tf_op jit(solution)/shard_map/ppermute | solution.py:526
  22.5 0.9 %shard_map.145 = (bf16[8,32,384]{2,1,0:T(8,128)(2,1)S(1)}, f32[7,16,128]{2,1,0:T(8,128)S(1)}, f32[16,1024]{1,0:T(8,128)S(1)}) custom-call(f32[32,128]{1,0:T(8,128)S(1)} %get-tuple-element.50.refs_0_, f32[56,128]{1,0:T(8,128)S(1)} %get-tuple-element.51.refs_1_, f32[88,128]{1,0:T(8,128)S(1)} %collective-permute-done.3.refs_2_, ...), custom_call_target="tpu_custom_call" | custom-call | flops 1000000 | tf_op jit(solution)/shard_map/pallas_call | solution.py:543
  23.4 0.0 collective-permute-done.9.refs_8_
  23.4 0.9 %shard_map.146 = (f32[48,128]{1,0:T(8,128)S(1)}, bf16[8,32,128]{2,1,0:T(8,128)(2,1)S(1)}, f32[8,16,128]{2,1,0:T(8,128)S(1)}) custom-call(s32[1]{0:T(128)} %bitcast.1.pos_ref, f32[16,128]{1,0:T(8,128)S(1)} %get-tuple-element.41.mix_ref, f32[32,128]{1,0:T(8,128)S(1)} %get-tuple-element.50.refs_0_, f32[56,128]{1,0:T(8,128)S(1)} %get-tuple-element.51.refs_1_, ...), custom_call_target="tpu_custom_call" | custom-call | flops 1000000000 | tf_op jit(solution)/shard_map/pallas_call | solution.py:554
  24.3 0.0 collective-permute-start.10
  24.3 0.4 %shard_map.147.own_ref = f32[16,40,256]{2,1,0:T(8,128)S(1)} custom-call(bf16[16,40,256]{2,1,0:T(8,128)(2,1)S(1)} %copy-done.1, f32[48,128]{1,0:T(8,128)S(1)} %get-tuple-element.65.mine_ref, bf16[2,128,128]{2,1,0:T(8,128)(2,1)S(1)} %get-tuple-element.66.weights_ref, f32[16,40,256]{2,1,0:T(8,128)S(1)} %copy-done), custom_call_target="tpu_custom_call" | custom-call | tf_op jit(solution)/shard_map/pallas_call | solution.py:583
  24.8 0.3 %shard_map.148 = (f32[16,1024]{1,0:T(8,128)S(1)}, f32[16,1024]{1,0:T(8,128)S(1)}) custom-call(s32[1]{0:T(128)} %bitcast.1.pos_ref, bf16[8,32,512]{2,1,0:T(8,128)(2,1)S(1)} %get-tuple-element.59.refs_8_.refs_9_.refs_0_, bf16[8,32,384]{2,1,0:T(8,128)(2,1)S(1)} %get-tuple-element.62.refs_10_.refs_1_, bf16[8,32,128]{2,1,0:T(8,128)(2,1)S(1)} %get-tuple-element.67.refs_2_, ...), custom_call_target="tpu_custom_call" | custom-call | tf_op jit(solution)/shard_map/pallas_call | solution.py:561
  25.1 0.4 %collective-permute-done.10.theirs_ref = f32[48,128]{1,0:T(8,128)S(1)} collective-permute-done((f32[48,128]{1,0:T(8,128)S(1)}, f32[48,128]{1,0:T(8,128)S(1)}, u32[]{:S(2)}, u32[]{:S(2)}) %collective-permute-start.10) | collective-permute-done | bytes 24608 | tf_op jit(solution)/shard_map/ppermute | solution.py:582
  25.5 1.2 %shard_map.149 = (f32[16,40,256]{2,1,0:T(8,128)}, f32[16,1024]{1,0:T(8,128)}, f32[16,1024]{1,0:T(8,128)}) custom-call(bf16[16,40,256]{2,1,0:T(8,128)(2,1)S(1)} %collective-permute-done.1.perturb_ref, f32[48,128]{1,0:T(8,128)S(1)} %collective-permute-done.10.theirs_ref, f32[16,40,256]{2,1,0:T(8,128)S(1)} %shard_map.147.own_ref, ...), custom_call_target="tpu_custom_call" | custom-call | tf_op jit(solution)/shard_map/pallas_call | solution.py:584
  (9 shorter events, 0.0 us)
Async XLA Ops:
  0.6 2.5 %collective-permute-start = (f32[16,40,256]{2,1,0:T(8,128)}, f32[16,40,256]{2,1,0:T(8,128)S(1)}, u32[]{:S(2)}, u32[]{:S(2)}) collective-permute-start(f32[16,40,256]{2,1,0:T(8,128)} %control_ref.3), channel_id=1, source_target_pairs={{0,1},{1,0},{2,3},{3,2},{4,5},{5,4},{6,7},{7,6},{8,9},{9,8},{10,11... | collective-permute-start | bytes 1966088 | tf_op jit(solution)/shard_map/ppermute | solution.py:490
  1.1 2.5 %collective-permute-start.1 = (bf16[16,40,256]{2,1,0:T(8,128)(2,1)}, bf16[16,40,256]{2,1,0:T(8,128)(2,1)S(1)}, u32[]{:S(2)}, u32[]{:S(2)}) collective-permute-start(bf16[16,40,256]{2,1,0:T(8,128)(2,1)} %perturb_ref.3), channel_id=1, source_target_pairs={{0,1},{1,0},{2,3},{3,2},{4,5},{5,4},{6,7},{7,6},{8,9},{9,8},{10,11... | collective-permute-start | bytes 983048 | tf_op jit(solution)/shard_map/ppermute | solution.py:509
  1.2 0.7 %copy-start.11 = (f32[16,32]{1,0:T(8,128)S(1)}, f32[16,32]{1,0:T(8,128)}, u32[]{:S(2)}) copy-start(f32[16,32]{1,0:T(8,128)} %loc_ref.1) | copy-start | bytes 6148
  1.9 1.2 %copy-start = (f32[16,40,256]{2,1,0:T(8,128)S(1)}, f32[16,40,256]{2,1,0:T(8,128)}, u32[]{:S(2)}) copy-start(f32[16,40,256]{2,1,0:T(8,128)} %control_ref.3) | copy-start | bytes 1966084
  1.9 1.2 %copy-start.1 = (bf16[16,40,256]{2,1,0:T(8,128)(2,1)S(1)}, bf16[16,40,256]{2,1,0:T(8,128)(2,1)}, u32[]{:S(2)}) copy-start(bf16[16,40,256]{2,1,0:T(8,128)(2,1)} %perturb_ref.3) | copy-start | bytes 983044
  3.1 3.5 %copy-start.2 = (f32[16,1024]{1,0:T(8,128)S(1)}, f32[16,1024]{1,0:T(8,128)}, u32[]{:S(2)}) copy-start(f32[16,1024]{1,0:T(8,128)} %refs_5_.1) | copy-start | bytes 196612
  3.1 3.5 %copy-start.3 = (f32[16,1024]{1,0:T(8,128)S(1)}, f32[16,1024]{1,0:T(8,128)}, u32[]{:S(2)}) copy-start(f32[16,1024]{1,0:T(8,128)} %refs_8_.1) | copy-start | bytes 196612
  3.1 3.5 %copy-start.4 = (f32[16,1024]{1,0:T(8,128)S(1)}, f32[16,1024]{1,0:T(8,128)}, u32[]{:S(2)}) copy-start(f32[16,1024]{1,0:T(8,128)} %refs_9_.1) | copy-start | bytes 196612
  3.1 3.5 %copy-start.7 = (s32[1,8,128]{2,1,0:T(8,128)S(1)}, s32[1,8,128]{2,1,0:T(8,128)}, u32[]{:S(2)}) copy-start(s32[1,8,128]{2,1,0:T(8,128)} %src_ref.1) | copy-start | bytes 12292
  3.1 3.5 %copy-start.8 = (f32[1,8,128]{2,1,0:T(8,128)S(1)}, f32[1,8,128]{2,1,0:T(8,128)}, u32[]{:S(2)}) copy-start(f32[1,8,128]{2,1,0:T(8,128)} %weight_ref.1) | copy-start | bytes 12292
  3.1 3.5 %copy-start.9 = (s32[1,8,128]{2,1,0:T(8,128)S(1)}, s32[1,8,128]{2,1,0:T(8,128)}, u32[]{:S(2)}) copy-start(s32[1,8,128]{2,1,0:T(8,128)} %tgt_ref.1) | copy-start | bytes 12292
  3.7 4.8 %collective-permute-start.2 = (f32[16,256]{1,0:T(8,128)S(1)}, f32[16,256]{1,0:T(8,128)S(1)}, u32[]{:S(2)}, u32[]{:S(2)}) collective-permute-start(f32[16,256]{1,0:T(8,128)S(1)} %shard_map.140.refs_0_), channel_id=1, source_target_pairs={{0,16},{16,0},{1,17},{17,1},{2,18},{18,2},{3,19},{19,3},{4,20},{20... | collective-permute-start | bytes 49160 | tf_op jit(solution)/shard_map/ppermute | solution.py:511
  6.6 0.7 %copy-start.6 = (f32[1024]{0:T(1024)S(1)}, f32[1024]{0:T(1024)}, u32[]{:S(2)}) copy-start(f32[1024]{0:T(1024)} %param.17) | copy-start | bytes 12292
  6.6 0.7 %copy-start.5 = (f32[1024]{0:T(1024)S(1)}, f32[1024]{0:T(1024)}, u32[]{:S(2)}) copy-start(f32[1024]{0:T(1024)} %param.16) | copy-start | bytes 12292
  6.6 0.7 %copy-start.10 = (s32[1,8]{1,0:T(1,128)S(1)}, s32[1,8]{1,0:T(1,128)}, u32[]{:S(2)}) copy-start(s32[1,8]{1,0:T(1,128)} %counts_ref.1) | copy-start | bytes 100
  8.5 6.9 %collective-permute-start.6 = (f32[184,128]{1,0:T(8,128)S(1)}, f32[184,128]{1,0:T(8,128)S(1)}, u32[]{:S(2)}, u32[]{:S(2)}) collective-permute-start(f32[184,128]{1,0:T(8,128)S(1)} %get-tuple-element.55), channel_id=1, source_target_pairs={{0,8},{2,10},{4,12},{6,14},{8,0},{10,2},{12,4},{14,6},{1,9},{3,11}... | collective-permute-start | bytes 282632 | tf_op jit(solution)/shard_map/ppermute | solution.py:526
  11.5 6.6 %collective-permute-start.3 = (f32[88,128]{1,0:T(8,128)S(1)}, f32[88,128]{1,0:T(8,128)S(1)}, u32[]{:S(2)}, u32[]{:S(2)}) collective-permute-start(f32[88,128]{1,0:T(8,128)S(1)} %get-tuple-element.52), channel_id=1, source_target_pairs={{0,2},{2,0},{4,6},{6,4},{8,10},{10,8},{12,14},{14,12},{1,3},{3,1},... | collective-permute-start | bytes 135176 | tf_op jit(solution)/shard_map/ppermute | solution.py:526
  13.1 6.0 %collective-permute-start.4 = (f32[88,128]{1,0:T(8,128)S(1)}, f32[88,128]{1,0:T(8,128)S(1)}, u32[]{:S(2)}, u32[]{:S(2)}) collective-permute-start(f32[88,128]{1,0:T(8,128)S(1)} %get-tuple-element.53), channel_id=1, source_target_pairs={{0,4},{2,6},{4,0},{6,2},{8,12},{10,14},{12,8},{14,10},{1,5},{3,7},... | collective-permute-start | bytes 135176 | tf_op jit(solution)/shard_map/ppermute | solution.py:526
  14.6 5.0 %collective-permute-start.5 = (f32[88,128]{1,0:T(8,128)S(1)}, f32[88,128]{1,0:T(8,128)S(1)}, u32[]{:S(2)}, u32[]{:S(2)}) collective-permute-start(f32[88,128]{1,0:T(8,128)S(1)} %get-tuple-element.54), channel_id=1, source_target_pairs={{0,6},{2,4},{4,2},{6,0},{8,14},{10,12},{12,10},{14,8},{1,7},{3,5},... | collective-permute-start | bytes 135176 | tf_op jit(solution)/shard_map/ppermute | solution.py:526
  15.4 5.3 %collective-permute-start.7 = (f32[88,128]{1,0:T(8,128)S(1)}, f32[88,128]{1,0:T(8,128)S(1)}, u32[]{:S(2)}, u32[]{:S(2)}) collective-permute-start(f32[88,128]{1,0:T(8,128)S(1)} %get-tuple-element.56), channel_id=1, source_target_pairs={{0,2},{2,0},{4,6},{6,4},{8,10},{10,8},{12,14},{14,12},{1,3},{3,1},... | collective-permute-start | bytes 135176 | tf_op jit(solution)/shard_map/ppermute | solution.py:526
  17.5 4.9 %collective-permute-start.8 = (f32[88,128]{1,0:T(8,128)S(1)}, f32[88,128]{1,0:T(8,128)S(1)}, u32[]{:S(2)}, u32[]{:S(2)}) collective-permute-start(f32[88,128]{1,0:T(8,128)S(1)} %get-tuple-element.57), channel_id=1, source_target_pairs={{0,6},{2,4},{4,2},{6,0},{8,14},{10,12},{12,10},{14,8},{1,7},{3,5},... | collective-permute-start | bytes 135176 | tf_op jit(solution)/shard_map/ppermute | solution.py:526
  18.2 5.3 %collective-permute-start.9 = (f32[88,128]{1,0:T(8,128)S(1)}, f32[88,128]{1,0:T(8,128)S(1)}, u32[]{:S(2)}, u32[]{:S(2)}) collective-permute-start(f32[88,128]{1,0:T(8,128)S(1)} %get-tuple-element.58), channel_id=1, source_target_pairs={{0,4},{2,6},{4,0},{6,2},{8,12},{10,14},{12,8},{14,10},{1,5},{3,7},... | collective-permute-start | bytes 135176 | tf_op jit(solution)/shard_map/ppermute | solution.py:526
  24.3 1.2 %collective-permute-start.10 = (f32[48,128]{1,0:T(8,128)S(1)}, f32[48,128]{1,0:T(8,128)S(1)}, u32[]{:S(2)}, u32[]{:S(2)}) collective-permute-start(f32[48,128]{1,0:T(8,128)S(1)} %get-tuple-element.65.mine_ref), channel_id=1, source_target_pairs={{0,1},{1,0},{2,3},{3,2},{4,5},{5,4},{6,7},{7,6},{8,9},{9,8},{10,11... | collective-permute-start | bytes 73736 | tf_op jit(solution)/shard_map/ppermute | solution.py:582

commit v24 on v19

--- a/solution.py
+++ b/solution.py
@@ -218,8 +218,11 @@
     weights = halves(spread(theirs_ref[theirs_ref.shape[0] - levels :, :]).T)
     for place, values in ens_tiles(perturb_ref, theirs_ref, weights, own_ref):
         out_ref[place] = values
-        copies.append(pltpu.make_async_copy(out_ref.at[place], out_hbm.at[place], sems.at[len(copies)]))
-        copies[-1].start()
+        half = out_ref.shape[0] // 2
+        for part in (slice(0, half), slice(half, 2 * half)):
+            piece = (part, *place[1:])
+            copies.append(pltpu.make_async_copy(out_ref.at[piece], out_hbm.at[piece], sems.at[len(copies)]))
+            copies[-1].start()
     for copy in copies:
         copy.wait()
 
@@ -592,7 +595,7 @@
         ens_kernel,
         (shape(control.shape, F32), flat, flat),
         [VMEM] * 5,
-        [pltpu.VMEM(control.shape, F32), pltpu.SemaphoreType.DMA((2 + members // SUB,))],
+        [pltpu.VMEM(control.shape, F32), pltpu.SemaphoreType.DMA((2 + 2 * (members // SUB),))],
         out=HBM,
     )(other_perturb, theirs, own, increment, grad_static)
     return (increment, grad_static, grad_ens)

time: 26.6 us -> 26.6 us (level)
  no operation moved by 1% of the time
where the time goes in v24:
time: 26.6 us; the launch traced here: 26.4 us
  starting transfers between devices  12 us (45%)
  Pallas kernels  6.71 us (25%)
  waiting for transfers between devices  5.56 us (21%)
  local copies, waits for them, and re-layouts  1.39 us (5%)
  between operations  0.78 us (3%)
    ppermute x5, starting transfers between devices, to(): return lax.ppermute(blocks[r], 'tile', [(i, i ^ r) for i in range(n)])  8.4 us
    ppermute x5, waiting for transfers between devices, to(): return lax.ppermute(blocks[r], 'tile', [(i, i ^ r) for i in range(n)])  4.31 us
    ppermute x1, starting transfers between devices, body(): lax.ppermute(sums[0], 'grp', [(g, (g + k) % groups) for g in range(groups)])  2.97 us
    pallas_call x2, Pallas kernels, body(): call(functools.partial(stage_kernel, n, levels, band_cols, tile_cols, sta...  1.67 us
    unnamed x24, local copies, waits for them, and re-layouts  1.39 us
    pallas_call x1, Pallas kernels, body(): call(ens_kernel, (shape(control.shape, F32), flat, flat), [VMEM] * 5, [pl...  1.28 us
    pallas_call x1, Pallas kernels, body(): call(functools.partial(static_kernel, band_cols), [shape((rows.total, cap...  1.11 us
    pallas_call x1, Pallas kernels, body(): call(functools.partial(shared_kernel, n, levels, band_cols, tile_cols, st...  1.04 us
  transfers between devices with their start and end apart: 9, of which 6 were waited for; matrix products, arithmetic and copies ran while one was open for 0% of the time, Pallas kernels for 17%

profile of v24, /device:TPU:0, one launch (start us, length us, event | category | flops | bytes accessed | tf_op | source)
XLA Modules:
  0.0 26.4 jit_solution(8886407626403520203)
XLA Ops:
  0.6 0.5 %collective-permute-start = (f32[16,40,256]{2,1,0:T(8,128)}, f32[16,40,256]{2,1,0:T(8,128)S(1)}, u32[]{:S(2)}, u32[]{:S(2)}) collective-permute-start(f32[16,40,256]{2,1,0:T(8,128)} %control_ref.3), channel_id=1, source_target_pairs={{0,1},{1,0},{2,3},{3,2},{4,5},{5,4},{6,7},{7,6},{8,9},{9,8},{10,11... | collective-permute-start | bytes 1966088 | tf_op jit(solution)/shard_map/ppermute | solution.py:497
  1.1 0.1 collective-permute-start.1
  1.2 0.0 copy-start.11
  1.2 0.7 %copy-done.11 = f32[16,32]{1,0:T(8,128)S(1)} copy-done((f32[16,32]{1,0:T(8,128)S(1)}, f32[16,32]{1,0:T(8,128)}, u32[]{:S(2)}) %copy-start.11) | copy-done | bytes 2072
  1.9 0.0 copy-start
  1.9 0.0 copy-start.1
  1.9 0.2 shard_map.139
  2.2 0.9 %collective-permute-done.other_ref = f32[16,40,256]{2,1,0:T(8,128)S(1)} collective-permute-done((f32[16,40,256]{2,1,0:T(8,128)}, f32[16,40,256]{2,1,0:T(8,128)S(1)}, u32[]{:S(2)}, u32[]{:S(2)}) %collective-permute-start) | collective-permute-done | bytes 655392 | tf_op jit(solution)/shard_map/ppermute | solution.py:497
  3.1 0.0 copy-done
  3.1 0.0 copy-done.1
  3.1 0.0 copy-start.2
  3.1 0.0 copy-start.3
  3.1 0.0 copy-start.4
  3.1 0.0 copy-start.7
  3.1 0.0 copy-start.8
  3.1 0.0 copy-start.9
  3.1 0.5 %shard_map.140.refs_0_ = f32[16,256]{1,0:T(8,128)S(1)} custom-call(bf16[16,40,256]{2,1,0:T(8,128)(2,1)S(1)} %copy-done.1, f32[16,40,256]{2,1,0:T(8,128)S(1)} %copy-done, f32[16,40,256]{2,1,0:T(8,128)S(1)} %collective-permute-done.other_ref, bf16[2,128,256]{2,1,0:T(8,128)(2,1)S(1)} %get-tuple-element.39.mix_ref), custom_call_target="tpu_custom_call" | custom-call | tf_op jit(solution)/shard_map/pallas_call | solution.py:505
  3.6 0.0 collective-permute-done.1.perturb_ref
  3.7 3.0 %collective-permute-start.2 = (f32[16,256]{1,0:T(8,128)S(1)}, f32[16,256]{1,0:T(8,128)S(1)}, u32[]{:S(2)}, u32[]{:S(2)}) collective-permute-start(f32[16,256]{1,0:T(8,128)S(1)} %shard_map.140.refs_0_), channel_id=1, source_target_pairs={{0,16},{16,0},{1,17},{17,1},{2,18},{18,2},{3,19},{19,3},{4,20},{20... | collective-permute-start | bytes 49160 | tf_op jit(solution)/shard_map/ppermute | solution.py:518
  6.6 0.0 copy-done.2
  6.6 0.0 copy-done.3
  6.6 0.0 copy-done.4
  6.7 0.0 copy-done.7
  6.7 0.0 copy-done.8
  6.7 0.0 copy-done.9
  6.7 0.6 %copy-done.6 = f32[1024]{0:T(1024)S(1)} copy-done((f32[1024]{0:T(1024)S(1)}, f32[1024]{0:T(1024)}, u32[]{:S(2)}) %copy-start.6) | copy-done | bytes 4120
  7.3 0.0 copy-done.5
  7.3 0.0 copy-done.10
  7.3 1.1 %shard_map.141 = (f32[56,128]{1,0:T(8,128)S(1)}, f32[56,128]{1,0:T(8,128)S(1)}, f32[56,128]{1,0:T(8,128)S(1)}, f32[56,128]{1,0:T(8,128)S(1)}, f32[56,128]{1,0:T(...) custom-call(s32[1]{0:T(128)} %bitcast.1.pos_ref, s32[1,8]{1,0:T(1,128)S(1)} %copy-done.10, ...), custom_call_target="tpu_custom_call" | custom-call | tf_op jit(solution)/shard_map/pallas_call | solution.py:512
  8.4 0.0 collective-permute-done.2.refs_1_
  8.5 3.1 %collective-permute-start.3 = (f32[152,128]{1,0:T(8,128)S(1)}, f32[152,128]{1,0:T(8,128)S(1)}, u32[]{:S(2)}, u32[]{:S(2)}) collective-permute-start(f32[152,128]{1,0:T(8,128)S(1)} %get-tuple-element.52), channel_id=1, source_target_pairs={{0,8},{2,10},{4,12},{6,14},{8,0},{10,2},{12,4},{14,6},{1,9},{3,11}... | collective-permute-start | bytes 233480 | tf_op jit(solution)/shard_map/ppermute | solution.py:532
  11.5 1.5 %collective-permute-start.4 = (f32[88,128]{1,0:T(8,128)S(1)}, f32[88,128]{1,0:T(8,128)S(1)}, u32[]{:S(2)}, u32[]{:S(2)}) collective-permute-start(f32[88,128]{1,0:T(8,128)S(1)} %get-tuple-element.53), channel_id=1, source_target_pairs={{0,2},{2,0},{4,6},{6,4},{8,10},{10,8},{12,14},{14,12},{1,3},{3,1},... | collective-permute-start | bytes 135176 | tf_op jit(solution)/shard_map/ppermute | solution.py:532
  13.1 0.0 collective-permute-start.5
  13.1 1.5 %collective-permute-done.3.got_ref.refs_2_ = f32[152,128]{1,0:T(8,128)S(1)} collective-permute-done((f32[152,128]{1,0:T(8,128)S(1)}, f32[152,128]{1,0:T(8,128)S(1)}, u32[]{:S(2)}, u32[]{:S(2)}) %collective-permute-start.3) | collective-permute-done | bytes 77856 | tf_op jit(solution)/shard_map/ppermute | solution.py:532
  14.6 3.8 %collective-permute-start.6 = (f32[176,128]{1,0:T(8,128)S(1)}, f32[176,128]{1,0:T(8,128)S(1)}, u32[]{:S(2)}, u32[]{:S(2)}) collective-permute-start(f32[176,128]{1,0:T(8,128)S(1)} %get-tuple-element.57), channel_id=1, source_target_pairs={{0,6},{2,4},{4,2},{6,0},{8,14},{10,12},{12,10},{14,8},{1,7},{3,5},... | collective-permute-start | bytes 270344 | tf_op jit(solution)/shard_map/ppermute | solution.py:532
  18.4 0.0 collective-permute-start.7
  18.4 0.0 collective-permute-done.4.refs_3_
  18.4 0.7 %collective-permute-done.5.refs_4_ = f32[88,128]{1,0:T(8,128)S(1)} collective-permute-done((f32[88,128]{1,0:T(8,128)S(1)}, f32[88,128]{1,0:T(8,128)S(1)}, u32[]{:S(2)}, u32[]{:S(2)}) %collective-permute-start.5) | collective-permute-done | bytes 45088 | tf_op jit(solution)/shard_map/ppermute | solution.py:532
  19.0 1.0 %shard_map.144 = (bf16[8,32,512]{2,1,0:T(8,128)(2,1)S(1)}, f32[4,16,128]{2,1,0:T(8,128)S(1)}, f32[16,1024]{1,0:T(8,128)S(1)}, bf16[8,256,128]{2,1,0:T(8,128)(2,1)S(1)}) custom-call(f32[32,128]{1,0:T(8,128)S(1)} %get-tuple-element.50.refs_0_, f32[56,128]{1,0:T(8,128)S(1)} %get-tuple-element.51.refs_1_, f32[152,128]{1,0:T(8,128)S(1)} %collective-permute-done.3.got_ref.refs_2_, ...), custom_call_target="tpu_custom_call" | custom-call | flops 1000000000 | tf_op jit(solution)/shard_map/pallas_call | solution.py:553
  20.0 1.1 %collective-permute-done.6.refs_5_.refs_6_ = f32[176,128]{1,0:T(8,128)S(1)} collective-permute-done((f32[176,128]{1,0:T(8,128)S(1)}, f32[176,128]{1,0:T(8,128)S(1)}, u32[]{:S(2)}, u32[]{:S(2)}) %collective-permute-start.6) | collective-permute-done | bytes 90144 | tf_op jit(solution)/shard_map/ppermute | solution.py:532
  21.1 0.7 %shard_map.145 = (bf16[8,32,256]{2,1,0:T(8,128)(2,1)S(1)}, f32[6,16,128]{2,1,0:T(8,128)S(1)}, f32[16,1024]{1,0:T(8,128)S(1)}) custom-call(f32[32,128]{1,0:T(8,128)S(1)} %get-tuple-element.50.refs_0_, f32[56,128]{1,0:T(8,128)S(1)} %get-tuple-element.51.refs_1_, f32[152,128]{1,0:T(8,128)S(1)} %collective-permute-done.3.got_ref.refs_2_, ...), custom_call_target="tpu_custom_call" | custom-call | flops 1000000000 | tf_op jit(solution)/shard_map/pallas_call | solution.py:553
  21.8 1.1 %collective-permute-done.7.refs_7_.refs_8_ = f32[176,128]{1,0:T(8,128)S(1)} collective-permute-done((f32[176,128]{1,0:T(8,128)S(1)}, f32[176,128]{1,0:T(8,128)S(1)}, u32[]{:S(2)}, u32[]{:S(2)}) %collective-permute-start.7) | collective-permute-done | bytes 90144 | tf_op jit(solution)/shard_map/ppermute | solution.py:532
  22.9 1.0 %shard_map.146 = (f32[48,128]{1,0:T(8,128)S(1)}, bf16[8,32,256]{2,1,0:T(8,128)(2,1)S(1)}, f32[8,16,128]{2,1,0:T(8,128)S(1)}) custom-call(s32[1]{0:T(128)} %bitcast.1.pos_ref, f32[16,128]{1,0:T(8,128)S(1)} %get-tuple-element.41.mix_ref, f32[32,128]{1,0:T(8,128)S(1)} %get-tuple-element.50.refs_0_, f32[56,128]{1,0:T(8,128)S(1)} %get-tuple-element.51.refs_1_, ...), custom_call_target="tpu_custom_call" | custom-call | flops 1000000000 | tf_op jit(solution)/shard_map/pallas_call | solution.py:564
  23.9 0.0 collective-permute-start.8
  23.9 0.4 %shard_map.147.own_ref = f32[16,40,256]{2,1,0:T(8,128)S(1)} custom-call(bf16[16,40,256]{2,1,0:T(8,128)(2,1)S(1)} %copy-done.1, f32[48,128]{1,0:T(8,128)S(1)} %get-tuple-element.65.mine_ref, bf16[2,128,128]{2,1,0:T(8,128)(2,1)S(1)} %get-tuple-element.66.weights_ref, f32[16,40,256]{2,1,0:T(8,128)S(1)} %copy-done), custom_call_target="tpu_custom_call" | custom-call | tf_op jit(solution)/shard_map/pallas_call | solution.py:593
  24.4 0.4 %shard_map.148 = (f32[16,1024]{1,0:T(8,128)S(1)}, f32[16,1024]{1,0:T(8,128)S(1)}) custom-call(s32[1]{0:T(128)} %bitcast.1.pos_ref, bf16[8,32,512]{2,1,0:T(8,128)(2,1)S(1)} %get-tuple-element.59.refs_7_.refs_9_.refs_0_, bf16[8,32,256]{2,1,0:T(8,128)(2,1)S(1)} %get-tuple-element.62.refs_10_.refs_1_, bf16[8,32,256]{2,1,0:T(8,128)(2,1)S(1)} %get-tuple-element.67.refs_2_, ...), custom_call_target="tpu_custom_call" | custom-call | tf_op jit(solution)/shard_map/pallas_call | solution.py:571
  24.8 0.3 %collective-permute-done.8.theirs_ref = f32[48,128]{1,0:T(8,128)S(1)} collective-permute-done((f32[48,128]{1,0:T(8,128)S(1)}, f32[48,128]{1,0:T(8,128)S(1)}, u32[]{:S(2)}, u32[]{:S(2)}) %collective-permute-start.8) | collective-permute-done | bytes 24608 | tf_op jit(solution)/shard_map/ppermute | solution.py:592
  25.1 1.3 %shard_map.149 = (f32[16,40,256]{2,1,0:T(8,128)}, f32[16,1024]{1,0:T(8,128)}, f32[16,1024]{1,0:T(8,128)}) custom-call(bf16[16,40,256]{2,1,0:T(8,128)(2,1)S(1)} %collective-permute-done.1.perturb_ref, f32[48,128]{1,0:T(8,128)S(1)} %collective-permute-done.8.theirs_ref, f32[16,40,256]{2,1,0:T(8,128)S(1)} %shard_map.147.own_ref, ...), custom_call_target="tpu_custom_call" | custom-call | tf_op jit(solution)/shard_map/pallas_call | solution.py:594
  (5 shorter events, 0.0 us)
Async XLA Ops:
  0.6 2.5 %collective-permute-start = (f32[16,40,256]{2,1,0:T(8,128)}, f32[16,40,256]{2,1,0:T(8,128)S(1)}, u32[]{:S(2)}, u32[]{:S(2)}) collective-permute-start(f32[16,40,256]{2,1,0:T(8,128)} %control_ref.3), channel_id=1, source_target_pairs={{0,1},{1,0},{2,3},{3,2},{4,5},{5,4},{6,7},{7,6},{8,9},{9,8},{10,11... | collective-permute-start | bytes 1966088 | tf_op jit(solution)/shard_map/ppermute | solution.py:497
  1.1 2.5 %collective-permute-start.1 = (bf16[16,40,256]{2,1,0:T(8,128)(2,1)}, bf16[16,40,256]{2,1,0:T(8,128)(2,1)S(1)}, u32[]{:S(2)}, u32[]{:S(2)}) collective-permute-start(bf16[16,40,256]{2,1,0:T(8,128)(2,1)} %perturb_ref.3), channel_id=1, source_target_pairs={{0,1},{1,0},{2,3},{3,2},{4,5},{5,4},{6,7},{7,6},{8,9},{9,8},{10,11... | collective-permute-start | bytes 983048 | tf_op jit(solution)/shard_map/ppermute | solution.py:516
  1.2 0.7 %copy-start.11 = (f32[16,32]{1,0:T(8,128)S(1)}, f32[16,32]{1,0:T(8,128)}, u32[]{:S(2)}) copy-start(f32[16,32]{1,0:T(8,128)} %loc_ref.1) | copy-start | bytes 6148
  1.9 1.2 %copy-start = (f32[16,40,256]{2,1,0:T(8,128)S(1)}, f32[16,40,256]{2,1,0:T(8,128)}, u32[]{:S(2)}) copy-start(f32[16,40,256]{2,1,0:T(8,128)} %control_ref.3) | copy-start | bytes 1966084
  1.9 1.2 %copy-start.1 = (bf16[16,40,256]{2,1,0:T(8,128)(2,1)S(1)}, bf16[16,40,256]{2,1,0:T(8,128)(2,1)}, u32[]{:S(2)}) copy-start(bf16[16,40,256]{2,1,0:T(8,128)(2,1)} %perturb_ref.3) | copy-start | bytes 983044
  3.1 3.5 %copy-start.2 = (f32[16,1024]{1,0:T(8,128)S(1)}, f32[16,1024]{1,0:T(8,128)}, u32[]{:S(2)}) copy-start(f32[16,1024]{1,0:T(8,128)} %refs_5_.1) | copy-start | bytes 196612
  3.1 3.5 %copy-start.3 = (f32[16,1024]{1,0:T(8,128)S(1)}, f32[16,1024]{1,0:T(8,128)}, u32[]{:S(2)}) copy-start(f32[16,1024]{1,0:T(8,128)} %refs_8_.1) | copy-start | bytes 196612
  3.1 3.5 %copy-start.4 = (f32[16,1024]{1,0:T(8,128)S(1)}, f32[16,1024]{1,0:T(8,128)}, u32[]{:S(2)}) copy-start(f32[16,1024]{1,0:T(8,128)} %refs_9_.1) | copy-start | bytes 196612
  3.1 3.5 %copy-start.7 = (s32[1,8,128]{2,1,0:T(8,128)S(1)}, s32[1,8,128]{2,1,0:T(8,128)}, u32[]{:S(2)}) copy-start(s32[1,8,128]{2,1,0:T(8,128)} %src_ref.1) | copy-start | bytes 12292
  3.1 3.5 %copy-start.8 = (f32[1,8,128]{2,1,0:T(8,128)S(1)}, f32[1,8,128]{2,1,0:T(8,128)}, u32[]{:S(2)}) copy-start(f32[1,8,128]{2,1,0:T(8,128)} %weight_ref.1) | copy-start | bytes 12292
  3.1 3.5 %copy-start.9 = (s32[1,8,128]{2,1,0:T(8,128)S(1)}, s32[1,8,128]{2,1,0:T(8,128)}, u32[]{:S(2)}) copy-start(s32[1,8,128]{2,1,0:T(8,128)} %tgt_ref.1) | copy-start | bytes 12292
  3.7 4.8 %collective-permute-start.2 = (f32[16,256]{1,0:T(8,128)S(1)}, f32[16,256]{1,0:T(8,128)S(1)}, u32[]{:S(2)}, u32[]{:S(2)}) collective-permute-start(f32[16,256]{1,0:T(8,128)S(1)} %shard_map.140.refs_0_), channel_id=1, source_target_pairs={{0,16},{16,0},{1,17},{17,1},{2,18},{18,2},{3,19},{19,3},{4,20},{20... | collective-permute-start | bytes 49160 | tf_op jit(solution)/shard_map/ppermute | solution.py:518
  6.6 0.7 %copy-start.6 = (f32[1024]{0:T(1024)S(1)}, f32[1024]{0:T(1024)}, u32[]{:S(2)}) copy-start(f32[1024]{0:T(1024)} %param.17) | copy-start | bytes 12292
  6.6 0.7 %copy-start.5 = (f32[1024]{0:T(1024)S(1)}, f32[1024]{0:T(1024)}, u32[]{:S(2)}) copy-start(f32[1024]{0:T(1024)} %param.16) | copy-start | bytes 12292
  6.6 0.7 %copy-start.10 = (s32[1,8]{1,0:T(1,128)S(1)}, s32[1,8]{1,0:T(1,128)}, u32[]{:S(2)}) copy-start(s32[1,8]{1,0:T(1,128)} %counts_ref.1) | copy-start | bytes 100
  8.5 6.1 %collective-permute-start.3 = (f32[152,128]{1,0:T(8,128)S(1)}, f32[152,128]{1,0:T(8,128)S(1)}, u32[]{:S(2)}, u32[]{:S(2)}) collective-permute-start(f32[152,128]{1,0:T(8,128)S(1)} %get-tuple-element.52), channel_id=1, source_target_pairs={{0,8},{2,10},{4,12},{6,14},{8,0},{10,2},{12,4},{14,6},{1,9},{3,11}... | collective-permute-start | bytes 233480 | tf_op jit(solution)/shard_map/ppermute | solution.py:532
  11.5 6.8 %collective-permute-start.4 = (f32[88,128]{1,0:T(8,128)S(1)}, f32[88,128]{1,0:T(8,128)S(1)}, u32[]{:S(2)}, u32[]{:S(2)}) collective-permute-start(f32[88,128]{1,0:T(8,128)S(1)} %get-tuple-element.53), channel_id=1, source_target_pairs={{0,2},{2,0},{4,6},{6,4},{8,10},{10,8},{12,14},{14,12},{1,3},{3,1},... | collective-permute-start | bytes 135176 | tf_op jit(solution)/shard_map/ppermute | solution.py:532
  13.1 5.9 %collective-permute-start.5 = (f32[88,128]{1,0:T(8,128)S(1)}, f32[88,128]{1,0:T(8,128)S(1)}, u32[]{:S(2)}, u32[]{:S(2)}) collective-permute-start(f32[88,128]{1,0:T(8,128)S(1)} %get-tuple-element.54), channel_id=1, source_target_pairs={{0,10},{2,8},{4,14},{6,12},{8,2},{10,0},{12,6},{14,4},{1,11},{3,9}... | collective-permute-start | bytes 135176 | tf_op jit(solution)/shard_map/ppermute | solution.py:532
  14.6 6.5 %collective-permute-start.6 = (f32[176,128]{1,0:T(8,128)S(1)}, f32[176,128]{1,0:T(8,128)S(1)}, u32[]{:S(2)}, u32[]{:S(2)}) collective-permute-start(f32[176,128]{1,0:T(8,128)S(1)} %get-tuple-element.57), channel_id=1, source_target_pairs={{0,6},{2,4},{4,2},{6,0},{8,14},{10,12},{12,10},{14,8},{1,7},{3,5},... | collective-permute-start | bytes 270344 | tf_op jit(solution)/shard_map/ppermute | solution.py:532
  18.4 4.5 %collective-permute-start.7 = (f32[176,128]{1,0:T(8,128)S(1)}, f32[176,128]{1,0:T(8,128)S(1)}, u32[]{:S(2)}, u32[]{:S(2)}) collective-permute-start(f32[176,128]{1,0:T(8,128)S(1)} %get-tuple-element.58), channel_id=1, source_target_pairs={{0,4},{2,6},{4,0},{6,2},{8,12},{10,14},{12,8},{14,10},{1,5},{3,7},... | collective-permute-start | bytes 270344 | tf_op jit(solution)/shard_map/ppermute | solution.py:532
  23.9 1.2 %collective-permute-start.8 = (f32[48,128]{1,0:T(8,128)S(1)}, f32[48,128]{1,0:T(8,128)S(1)}, u32[]{:S(2)}, u32[]{:S(2)}) collective-permute-start(f32[48,128]{1,0:T(8,128)S(1)} %get-tuple-element.65.mine_ref), channel_id=1, source_target_pairs={{0,1},{1,0},{2,3},{3,2},{4,5},{5,4},{6,7},{7,6},{8,9},{9,8},{10,11... | collective-permute-start | bytes 73736 | tf_op jit(solution)/shard_map/ppermute | solution.py:592
